TPU v7x, 32 devices: a whole 2x2x4 slice. The times are simulated.
32 devices in a mesh: feat: 4 (over z), dom: 8 (over y, x, core).
Axes of the slice: x: 2, y: 2, z: 4, core: 2. Of those that a mesh axis runs over, the one named last changes fastest.
Arguments:
- features: bfloat16 [8, 512, 768], P('dom', None, 'feat'), may hold values from -6 to 6
- tiles: bfloat16 [8, 12, 128, 128], P('dom')
- tile_ids: int32 [8, 12, 2], P('dom'), may hold values from 0 to 3, as said below
- sources: int32 [8, 8, 4, 16], P('dom'), may hold values from 0 to 511
- targets: int32 [8, 8, 4, 16], P('dom'), may hold values from 0 to 127
- counts: int32 [8, 8, 4], P('dom'), may hold values from 0 to 16, as said below
- edge_weight: bfloat16 [8, 8, 4, 16], P('dom'), may hold values from 0.5 to 2
- self_one: bfloat16 [768, 1024], replicated, may hold values from -0.21875 to 0.21875
- neigh_one: bfloat16 [768, 1024], replicated, may hold values from -0.21875 to 0.21875
- self_out: bfloat16 [1024, 153], replicated, may hold values from -0.1875 to 0.1875
- neigh_out: bfloat16 [1024, 153], replicated, may hold values from -0.1875 to 0.1875
Outputs:
- hidden: bfloat16 [8, 512, 1024], P('dom', 'feat')
- logits: float32 [8, 153, 512], P('dom', None, 'feat')
Inputs may be any that keep to these rules, and one draw needn't show every extreme that they name: `tile_ids`: in each partition the 12 (row block, column block) pairs are distinct, and every row block appears in exactly 3 of them, in no fixed order. counts[e, e, g] is 0; in every draw some partition receives 16 live slots from every other partition in every group.
All inputs are finite; a program needn't handle non-finite values.
Results may differ from a plain program's by a relative error of at most 0.003.
Values may be sent and summed in bfloat16 or wider, within the bound.
No kernel may reach another device: no remote copies, remote signals or barrier semaphores. Data moves between devices by JAX's collectives and lax.ppermute only.
A program may use at most 64 MiB of HBM per device.

v0:
```python
import jax
import jax.numpy as jnp
from jax import lax
from jax.sharding import PartitionSpec as P

precise = lax.Precision.HIGHEST


def on_device(
    features,
    tiles,
    tile_ids,
    sources,
    targets,
    counts,
    edge_weight,
    self_one,
    neigh_one,
    self_out,
    neigh_out,
):
    feature_cols = features[0]
    tile_contents = tiles[0]
    tile_pairs = tile_ids[0]
    groups = lax.axis_size("feat")
    group_index = lax.axis_index("feat")
    part_nodes = feature_cols.shape[0]
    row_count = part_nodes // groups
    tile_side = tile_contents.shape[1]
    block_count = part_nodes // tile_side
    slots = sources.shape[3]
    owners = (
        tile_pairs[:, 0][:, None] == jnp.arange(block_count, dtype=jnp.int32)[None, :]
    ).astype(jnp.float32)
    slot_live = jnp.arange(slots, dtype=jnp.int32)[None, None, :] < counts[0][:, :, None]
    kept_weights = jnp.where(slot_live, edge_weight[0], jnp.zeros((), jnp.bfloat16))
    target_hits = targets[0][..., None] == jnp.arange(row_count, dtype=jnp.int32)
    edge_matrices = jnp.where(target_hits, kept_weights[..., None], jnp.zeros((), jnp.bfloat16))
    tile_rows = jnp.sum(tile_contents, axis=2, dtype=jnp.float32)
    local_degree = jnp.einsum("tb,ti->bi", owners, tile_rows, precision=precise).reshape(part_nodes)
    edge_degree = jnp.sum(edge_matrices, axis=(0, 2), dtype=jnp.float32).reshape(part_nodes)
    degree = local_degree + edge_degree
    col_blocks = feature_cols.reshape(block_count, tile_side, feature_cols.shape[1])
    picked = jnp.take(col_blocks, tile_pairs[:, 1], axis=0)
    products = jnp.einsum("tij,tjc->tic", tile_contents, picked, preferred_element_type=jnp.float32)
    local_term = jnp.einsum("tb,tic->bic", owners, products, precision=precise).reshape(
        part_nodes, feature_cols.shape[1]
    )
    outgoing = jnp.take(feature_cols, sources[0], axis=0)
    incoming = lax.all_to_all(outgoing, "dom", split_axis=0, concat_axis=0, tiled=True)
    edge_term = jnp.einsum(
        "dgsr,dgsc->grc", edge_matrices, incoming, preferred_element_type=jnp.float32
    )
    edge_term = edge_term.reshape(part_nodes, feature_cols.shape[1])
    neighbours = ((local_term + edge_term) / degree[:, None]).astype(jnp.bfloat16)
    feature_rows, neighbour_rows = (
        lax.all_to_all(feature_cols, "feat", split_axis=0, concat_axis=1, tiled=True),
        lax.all_to_all(neighbours, "feat", split_axis=0, concat_axis=1, tiled=True),
    )
    preact = jnp.dot(feature_rows, self_one, preferred_element_type=jnp.float32)
    preact = preact + jnp.dot(neighbour_rows, neigh_one, preferred_element_type=jnp.float32)
    hidden = jnp.maximum(preact, 0.0).astype(jnp.bfloat16)
    blocks_mine = row_count // tile_side
    first_block = group_index * blocks_mine
    row_pick = (
        tile_pairs[:, 0][:, None] == first_block + jnp.arange(blocks_mine, dtype=jnp.int32)[None, :]
    )
    col_pick = tile_pairs[:, 1][:, None] == jnp.arange(block_count, dtype=jnp.int32)[None, :]
    tile_positions = (row_pick[:, :, None] & col_pick[:, None, :]).astype(jnp.bfloat16)
    tile_band_rows = jnp.einsum(
        "mwr,mqy->wqry", tile_positions, tile_contents, preferred_element_type=jnp.float32
    )
    tile_band_rows = tile_band_rows.astype(jnp.bfloat16).reshape(row_count, part_nodes)
    group_mats = lax.dynamic_index_in_dim(edge_matrices, group_index, 1, keepdims=False)
    group_degree = lax.dynamic_slice_in_dim(degree, group_index * row_count, row_count)
    send_ids = lax.dynamic_index_in_dim(sources[0], group_index, 1, keepdims=False)
    own_term = lax.dot_general(
        self_out, hidden, (((0,), (1,)), ((), ())), preferred_element_type=jnp.float32
    )
    start_pick = jnp.zeros(send_ids.shape + (hidden.shape[1],), jnp.bfloat16)
    received = lax.all_gather(hidden, "feat", axis=0, tiled=True)
    chosen = start_pick
    piece_rows = received.shape[0]
    summed = jnp.dot(tile_band_rows, received, preferred_element_type=jnp.float32)
    inside = (send_ids >= 0) & (send_ids < piece_rows)
    picked_rows = jnp.take(received, jnp.clip(send_ids, 0, piece_rows - 1), axis=0)
    chosen = jnp.where(inside[..., None], picked_rows, chosen)
    summed, chosen = (summed, chosen)
    arrived = lax.all_to_all(chosen, "dom", split_axis=0, concat_axis=0, tiled=True)
    summed = summed + jnp.einsum(
        "dsr,dsc->rc", group_mats, arrived, preferred_element_type=jnp.float32
    )
    mean_two = summed / group_degree[:, None]
    logits = own_term + lax.dot_general(
        neigh_out.astype(jnp.float32), mean_two, (((0,), (1,)), ((), ())), precision=precise
    )
    return (hidden[None], logits[None])


def solution(mesh):
    placed = (
        P("dom", None, "feat"),
        P("dom", None, None, None),
        P("dom", None, None),
        P("dom", None, None, None),
        P("dom", None, None, None),
        P("dom", None, None),
        P("dom", None, None, None),
        P(),
        P(),
        P(),
        P(),
    )
    return jax.shard_map(
        on_device,
        mesh=mesh,
        in_specs=placed,
        out_specs=(P("dom", "feat", None), P("dom", None, "feat")),
        check_vma=False,
    )
```

profile of v0, /device:TPU:0, one launch (start us, length us, event | category | flops | bytes accessed | tf_op | source)
XLA Modules:
  0.0 99.0 jit_solution(5099712556406804035)
XLA Ops:
  7.2 0.0 copy-start
  7.2 0.8 compare_select_fusion
  8.0 0.7 compare_and_fusion
  8.8 1.1 %copy.53 = bf16[1,512,192]{2,1,0:T(8,128)(2,1)S(1)} copy(bf16[1,512,192]{1,2,0:T(8,128)(2,1)} %param.11) | data formatting | bytes 393216 | tf_op args[0]
  9.8 0.1 reshape.220
  9.9 0.0 copy-start.8
  9.9 0.0 copy-start.9
  10.0 0.0 copy-start.7
  10.0 2.0 %gather_fusion.1 = bf16[512,192]{1,0:T(8,128)(2,1)S(1)} fusion(bf16[512,192]{1,0:T(8,128)(2,1)S(1)} %bitcast.94, s32[1024]{0:T(1024)S(1)} %pad_clamp_fusion.1), kind=kCustom, calls=%fused_computation.1 | custom fusion | bytes 395264 | tf_op jit(solution)/shard_map/jit(_take)/gather | solution.py:49
  11.9 0.8 broadcast_select_fusion
  12.8 5.2 %all-to-all-start.1 = ((bf16[8,4,16,192]{3,2,1,0:T(8,128)(2,1)}), bf16[8,4,16,192]{3,2,1,0:T(8,128)(2,1)S(1)}, u32[]{:S(2)}, u32[]{:S(2)}) async-start(bf16[8,4,16,192]{3,2,1,0:T(8,128)(2,1)} %broadcast_select_fusion), calls=%async_computation.1 | async-start | bytes 524288 | tf_op jit(solution)/shard_map/all_to_all | solution.py:50
  18.0 0.1 all_to_all.32
  18.1 0.7 copy.47
  18.8 0.1 copy.51
  18.9 0.1 fusion.25
  19.0 0.2 convert_reduce_fusion
  19.2 1.6 %gather_fusion = bf16[12,128,192]{1,2,0:T(8,128)(2,1)S(1)} fusion(bf16[4,128,192]{1,2,0:T(8,128)(2,1)} %copy.47, s32[1024]{0:T(1024)S(1)} %pad_clamp_fusion.2), kind=kCustom, calls=%fused_computation | custom fusion | bytes 1179696 | tf_op jit(solution)/shard_map/jit(_take)/gather | solution.py:44
  20.8 1.5 %convolution_bitcast_fusion = f32[12,128,192]{1,2,0:T(8,128)} fusion(bf16[12,128,192]{1,2,0:T(8,128)(2,1)S(1)} %gather_fusion, pred[12]{0:T(512)(128)(4,1)S(1)} %get-tuple-element.11, bf16[1,12,128,128]{3,2,1,0:T(8,128)(2,1)S(1)} %copy-done.1), kind=kOutput, calls=%fused_computation.5 | convolution fusion | flops 75792384 | bytes 2162700 | tf_op jit(solution)/shard_map/tij,tjc->tic/dot_general | solution.py:45
  22.2 0.2 convert_reduce_fusion.1
  22.4 0.1 convolution_add_fusion.3
  22.6 2.3 %all-to-all-done.1 = bf16[8,4,16,192]{3,2,1,0:T(8,128)(2,1)S(1)} async-done(((bf16[8,4,16,192]{3,2,1,0:T(8,128)(2,1)}), bf16[8,4,16,192]{3,2,1,0:T(8,128)(2,1)S(1)}, u32[]{:S(2)}, u32[]{:S(2)}) %all-to-all-start.1) | async-done | bytes 196640 | tf_op jit(solution)/shard_map/all_to_all | solution.py:50
  24.9 4.9 %all-to-all-start = ((bf16[4,128,192]{1,2,0:T(8,128)(2,1)}), bf16[4,128,192]{1,2,0:T(8,128)(2,1)S(1)}, u32[]{:S(2)}, u32[]{:S(2)}) async-start(bf16[4,128,192]{1,2,0:T(8,128)(2,1)} %copy.47), calls=%async_computation | async-start | bytes 393216 | tf_op jit(solution)/shard_map/all_to_all | solution.py:57
  29.8 0.4 convolution_bitcast_fusion.2
  30.2 2.7 %fusion.11 = bf16[4,128,192]{1,0,2:T(4,128)(2,1)S(1)} fusion(f32[12,128,192]{1,2,0:T(8,128)} %convolution_bitcast_fusion, f32[4,128,192]{1,2,0:T(8,128)S(1)} %convolution_bitcast_fusion.2, f32[4,128]{1,0:T(4,128)S(1)} %convolution_add_fusion.3, s32[12]{0:T(128)S(1)} %get-tuple-element.14), kind=kOutput, calls=%fused_computation.15 | convolution fusion | flops 14450736 | bytes 1771568 | tf_op jit(solution)/shard_map/tb,tic->bic/dot_general | solution.py:46
  32.9 0.7 copy.56
  33.6 2.8 %all-to-all-done = bf16[4,128,192]{1,2,0:T(8,128)(2,1)S(1)} async-done(((bf16[4,128,192]{1,2,0:T(8,128)(2,1)}), bf16[4,128,192]{1,2,0:T(8,128)(2,1)S(1)}, u32[]{:S(2)}, u32[]{:S(2)}) %all-to-all-start) | async-done | bytes 196640 | tf_op jit(solution)/shard_map/all_to_all | solution.py:57
  36.4 3.4 %all-to-all-start.2 = ((bf16[4,128,192]{1,2,0:T(8,128)(2,1)}), bf16[4,128,192]{1,2,0:T(8,128)(2,1)S(1)}, u32[]{:S(2)}, u32[]{:S(2)}) async-start(bf16[4,128,192]{1,2,0:T(8,128)(2,1)} %copy.56), calls=%async_computation.2 | async-start | bytes 393216 | tf_op jit(solution)/shard_map/all_to_all | solution.py:58
  39.8 0.0 all-gather.2.cloned.1.call-start
  39.9 0.4 fusion.41
  40.3 5.7 %all-to-all-done.2 = bf16[4,128,192]{1,2,0:T(8,128)(2,1)S(1)} async-done(((bf16[4,128,192]{1,2,0:T(8,128)(2,1)}), bf16[4,128,192]{1,2,0:T(8,128)(2,1)S(1)}, u32[]{:S(2)}, u32[]{:S(2)}) %all-to-all-start.2) | async-done | bytes 196640 | tf_op jit(solution)/shard_map/all_to_all | solution.py:58
  46.0 2.5 %fusion.4 = bf16[128,1024]{1,0:T(8,128)(2,1)} fusion(f32[128,1024]{1,0:T(8,128)S(1)} %fusion.41, bf16[128,768]{0,1:T(8,128)(2,1)S(1)} %bitcast.100, bf16[768,1024]{1,0:T(8,128)(2,1)} %param.19), kind=kOutput, calls=%fused_computation.11 | convolution fusion | flops 201719808 | bytes 2555904 | tf_op jit(solution)/shard_map/dot_general | solution.py:61
  48.6 0.0 all-gather.2.cloned.1.call-update
  48.6 0.7 constant_dynamic-slice_fusion
  49.3 0.1 reshape.228
  49.4 0.1 dynamic_slice.13
  49.5 0.2 fusion.20
  49.7 1.0 convolution_convert_fusion
  50.7 24.9 %all-gather.2.cloned.1.call-done = bf16[512,1024]{1,0:T(8,128)(2,1)} async-done(((bf16[128,1024]{1,0:T(8,128)(2,1)}), bf16[512,1024]{1,0:T(8,128)(2,1)}) %all-gather.2.cloned.1.call-update) | async-done | bytes 1048592 | tf_op jit(solution)/shard_map/all_gather | solution.py:81
  75.6 2.4 %gather_fusion.2 = bf16[128,1024]{1,0:T(8,128)(2,1)S(1)} fusion(bf16[512,1024]{1,0:T(8,128)(2,1)} %all-gather.2.cloned.1.call-done, s32[1024]{0:T(1024)S(1)} %pad_clamp_fusion), kind=kCustom, calls=%fused_computation.2 | custom fusion | bytes 524800 | tf_op jit(solution)/shard_map/jit(_take)/gather | solution.py:86
  78.0 0.8 select_select_fusion
  78.8 3.7 %all-to-all-start.3 = ((bf16[8,16,1024]{2,1,0:T(8,128)(2,1)}), bf16[8,16,1024]{2,1,0:T(8,128)(2,1)S(1)}, u32[]{:S(2)}, u32[]{:S(2)}) async-start(bf16[8,16,1024]{2,1,0:T(8,128)(2,1)} %select_select_fusion), calls=%async_computation.3 | async-start | bytes 524288 | tf_op jit(solution)/shard_map/all_to_all | solution.py:89
  82.5 1.2 %fusion.42 = f32[128,153]{0,1:T(8,128)S(1)} fusion(bf16[128,1024]{1,0:T(8,128)(2,1)S(1)} %copy-done.3, bf16[1024,153]{0,1:T(8,128)(2,1)} %param.20), kind=kOutput, calls=%fused_computation.68 | convolution fusion | flops 40108032 | bytes 653824 | tf_op jit(solution)/shard_map/dot_general | solution.py:77
  83.7 5.7 %all-to-all-done.3 = bf16[8,16,1024]{2,1,0:T(8,128)(2,1)S(1)} async-done(((bf16[8,16,1024]{2,1,0:T(8,128)(2,1)}), bf16[8,16,1024]{2,1,0:T(8,128)(2,1)S(1)}, u32[]{:S(2)}, u32[]{:S(2)}) %all-to-all-start.3) | async-done | bytes 262176 | tf_op jit(solution)/shard_map/all_to_all | solution.py:89
  89.4 0.2 convolution_bitcast_fusion.1
  89.7 0.0 copy-start.5
  89.7 1.3 %fusion.2 = f32[128,1024]{1,0:T(8,128)S(1)} fusion(f32[128,1024]{1,0:T(8,128)S(1)} %convolution_bitcast_fusion.1, bf16[512,1024]{1,0:T(8,128)(2,1)S(1)} %copy-done.2, f32[128]{0:T(128)S(1)} %dynamic_slice.13, bf16[16,8,4,128]{3,2,1,0:T(4,128)(2,1)} %bitcast.101), kind=kOutput, calls=%fused_computation.7 | convolution fusion | flops 134479872 | bytes 2228736 | tf_op jit(solution)/shard_map/dot_general | solution.py:84
  91.0 0.5 fusion.14
  91.5 0.7 copy.59
  (25 shorter events, 0.1 us)
Async XLA Ops:
  7.2 32.7 %copy-start = (bf16[768,1024]{1,0:T(8,128)(2,1)S(1)}, bf16[768,1024]{1,0:T(8,128)(2,1)}, u32[]{:S(2)}) copy-start(bf16[768,1024]{1,0:T(8,128)(2,1)} %param.18) | copy-start | bytes 4718596
  9.9 8.0 %copy-start.4 = (bf16[1,512,192]{1,2,0:T(8,128)(2,1)S(1)}, bf16[1,512,192]{1,2,0:T(8,128)(2,1)}, u32[]{:S(2)}) copy-start(bf16[1,512,192]{1,2,0:T(8,128)(2,1)} %param.11) | copy-start | bytes 589828
  9.9 8.1 %copy-start.8 = (s32[1,12,2]{1,2,0:T(2,128)S(1)}, s32[1,12,2]{1,2,0:T(2,128)}, u32[]{:S(2)}) copy-start(s32[1,12,2]{1,2,0:T(2,128)} %param.13) | copy-start | bytes 292
  9.9 8.8 %copy-start.9 = (s32[1,8,4]{1,2,0:T(4,128)S(1)}, s32[1,8,4]{1,2,0:T(4,128)}, u32[]{:S(2)}) copy-start(s32[1,8,4]{1,2,0:T(4,128)} %param.16) | copy-start | bytes 388
  10.0 8.9 %copy-start.7 = (bf16[1,8,4,16]{3,2,1,0:T(4,128)(2,1)S(1)}, bf16[1,8,4,16]{3,2,1,0:T(4,128)(2,1)}, u32[]{:S(2)}) copy-start(bf16[1,8,4,16]{3,2,1,0:T(4,128)(2,1)} %param.17) | copy-start | bytes 3076
  10.0 9.0 %copy-start.6 = (s32[1,8,4,16]{3,2,1,0:T(4,128)S(1)}, s32[1,8,4,16]{3,2,1,0:T(4,128)}, u32[]{:S(2)}) copy-start(s32[1,8,4,16]{3,2,1,0:T(4,128)} %param.15) | copy-start | bytes 6148
  10.0 9.0 %copy-start.1 = (bf16[1,12,128,128]{3,2,1,0:T(8,128)(2,1)S(1)}, bf16[1,12,128,128]{3,2,1,0:T(8,128)(2,1)}, u32[]{:S(2)}) copy-start(bf16[1,12,128,128]{3,2,1,0:T(8,128)(2,1)} %param.12) | copy-start | bytes 1179652
  12.8 12.1 %all-to-all-start.1 = ((bf16[8,4,16,192]{3,2,1,0:T(8,128)(2,1)}), bf16[8,4,16,192]{3,2,1,0:T(8,128)(2,1)S(1)}, u32[]{:S(2)}, u32[]{:S(2)}) async-start(bf16[8,4,16,192]{3,2,1,0:T(8,128)(2,1)} %broadcast_select_fusion), calls=%async_computation.1 | async-start | bytes 524288 | tf_op jit(solution)/shard_map/all_to_all | solution.py:50
  24.9 11.5 %all-to-all-start = ((bf16[4,128,192]{1,2,0:T(8,128)(2,1)}), bf16[4,128,192]{1,2,0:T(8,128)(2,1)S(1)}, u32[]{:S(2)}, u32[]{:S(2)}) async-start(bf16[4,128,192]{1,2,0:T(8,128)(2,1)} %copy.47), calls=%async_computation | async-start | bytes 393216 | tf_op jit(solution)/shard_map/all_to_all | solution.py:57
  36.4 9.6 %all-to-all-start.2 = ((bf16[4,128,192]{1,2,0:T(8,128)(2,1)}), bf16[4,128,192]{1,2,0:T(8,128)(2,1)S(1)}, u32[]{:S(2)}, u32[]{:S(2)}) async-start(bf16[4,128,192]{1,2,0:T(8,128)(2,1)} %copy.56), calls=%async_computation.2 | async-start | bytes 393216 | tf_op jit(solution)/shard_map/all_to_all | solution.py:58
  39.8 35.8 %all-gather.2.cloned.1.call-start = ((), (), s32[]{:S(2)}) async-start(), calls=%async_computation.4 | async-start | bytes 1310720 | tf_op jit(solution)/shard_map/all_gather | solution.py:81
  50.7 31.8 %copy-start.3 = (bf16[128,1024]{1,0:T(8,128)(2,1)S(1)}, bf16[128,1024]{1,0:T(8,128)(2,1)}, u32[]{:S(2)}) copy-start(bf16[128,1024]{1,0:T(8,128)(2,1)} %fusion.4) | copy-start | bytes 786436
  78.0 11.7 %copy-start.2 = (bf16[512,1024]{1,0:T(8,128)(2,1)S(1)}, bf16[512,1024]{1,0:T(8,128)(2,1)}, u32[]{:S(2)}) copy-start(bf16[512,1024]{1,0:T(8,128)(2,1)} %all-gather.2.cloned.1.call-done) | copy-start | bytes 3145732
  78.8 10.6 %all-to-all-start.3 = ((bf16[8,16,1024]{2,1,0:T(8,128)(2,1)}), bf16[8,16,1024]{2,1,0:T(8,128)(2,1)S(1)}, u32[]{:S(2)}, u32[]{:S(2)}) async-start(bf16[8,16,1024]{2,1,0:T(8,128)(2,1)} %select_select_fusion), calls=%async_computation.3 | async-start | bytes 524288 | tf_op jit(solution)/shard_map/all_to_all | solution.py:89
  89.7 1.3 %copy-start.5 = (bf16[1024,153]{0,1:T(8,128)(2,1)S(1)}, bf16[1024,153]{0,1:T(8,128)(2,1)}, u32[]{:S(2)}) copy-start(bf16[1024,153]{0,1:T(8,128)(2,1)} %param.21) | copy-start | bytes 940036
Sparse Core Ops, SparseCore 0:
  48.7 26.8 all-gather.1
where the time goes:
time: 99.8 us; the launch traced here: 99 us
  waiting for transfers between devices  41.5 us (42%)
  starting transfers between devices  17.1 us (17%)
  between operations  14.3 us (14%)
  matrix products  11.8 us (12%)
  local copies, waits for them, and re-layouts  10.3 us (10%)
  other arithmetic  3.96 us (4%)
    all_gather x1, waiting for transfers between devices, on_device(): received = lax.all_gather(hidden, 'feat', axis=0, tiled=True)  24.9 us
    all_to_all x1, waiting for transfers between devices, on_device(): lax.all_to_all(neighbours, 'feat', split_axis=0, concat_axis=1, tiled=True)  5.75 us
    all_to_all x1, waiting for transfers between devices, on_device(): lax.all_to_all(chosen, 'dom', split_axis=0, concat_axis=0, tiled=True)  5.7 us
    all_to_all x1, starting transfers between devices, on_device(): lax.all_to_all(outgoing, 'dom', split_axis=0, concat_axis=0, tiled=True)  5.17 us
    all_to_all x1, starting transfers between devices, on_device(): lax.all_to_all(feature_cols, 'feat', split_axis=0, concat_axis=1, tiled=T...  4.87 us
    all_to_all x1, starting transfers between devices, on_device(): lax.all_to_all(chosen, 'dom', split_axis=0, concat_axis=0, tiled=True)  3.66 us
    all_to_all x1, starting transfers between devices, on_device(): lax.all_to_all(neighbours, 'feat', split_axis=0, concat_axis=1, tiled=True)  3.37 us
    all_to_all x1, waiting for transfers between devices, on_device(): lax.all_to_all(feature_cols, 'feat', split_axis=0, concat_axis=1, tiled=T...  2.83 us
  transfers between devices with their start and end apart: 5, of which 5 were waited for; matrix products, arithmetic and copies ran while one was open for 12% of the time, Pallas kernels for 0%

commit v1 on v0

v1 whole, which is shorter than its diff:
```python
import functools

import jax
import jax.numpy as jnp
from jax import lax
from jax.experimental import pallas as pl
from jax.experimental.pallas import tpu as pltpu
from jax.sharding import PartitionSpec as P

f32 = jnp.float32
bf16 = jnp.bfloat16
VM = pl.BlockSpec(memory_space=pltpu.VMEM)
SM = pl.BlockSpec(memory_space=pltpu.SMEM)


def call(kernel, out_shape, in_specs, scratch=(), cost=None, limit=24 << 20):
    return pl.pallas_call(
        kernel,
        out_shape=out_shape,
        in_specs=in_specs,
        out_specs=jax.tree.map(lambda _: VM, out_shape),
        scratch_shapes=list(scratch),
        cost_estimate=cost,
        compiler_params=pltpu.CompilerParams(vmem_limit_bytes=limit),
    )


def fill_hits(hits, sources_ref, first, chunk, offset):
    groups, slots = sources_ref.shape[1], sources_ref.shape[2]
    nodes = hits.shape[1]
    lane = lax.broadcasted_iota(jnp.int32, (slots, nodes), 1) + offset
    for e in range(chunk):
        columns = sources_ref[first + e].T
        for g in range(groups):
            row = (g * chunk + e) * slots
            hits[row : row + slots, :] = jnp.where(
                columns[:, g : g + 1] == lane, 1.0, 0.0
            ).astype(bf16)


def send_rows(hits, sources_ref, table, out_ref, chunk, offset):
    groups, parts, slots, width = out_ref.shape

    def step(i, _):
        first = i * chunk
        fill_hits(hits, sources_ref, first, chunk, offset)
        rows = jnp.dot(hits[...], table, preferred_element_type=f32).astype(bf16)
        rows = rows.reshape(groups, chunk, slots, width)
        out_ref[:, pl.ds(first, chunk), :, :] = rows
        return 0

    if parts == chunk:
        step(0, 0)
    else:
        lax.fori_loop(0, parts // chunk, step, 0)


def first_kernel(chunk, me_ref, ids_ref, sources_ref, features_ref, tiles_ref, *rest):
    groups, rows = len(rest) - 3, tiles_ref.shape[1]
    out_ref, locals_, sums, hits = rest[0], rest[1 : 1 + groups], rest[-2], rest[-1]
    send_rows(hits, sources_ref, features_ref[...], out_ref, chunk, 0)
    sums[...] = jnp.zeros_like(sums)

    def add(t, _):
        to = pl.multiple_of(ids_ref[t, 0] * rows, rows)
        at = pl.multiple_of(ids_ref[t, 1] * rows, rows)
        sums[pl.ds(to, rows), :] += jnp.dot(
            tiles_ref[t], features_ref[pl.ds(at, rows), :], preferred_element_type=f32
        )
        return 0

    lax.fori_loop(0, tiles_ref.shape[0], add, 0)
    for k in range(groups):
        group = lax.rem(me_ref[0] + k, groups)
        locals_[k][...] = sums[pl.ds(pl.multiple_of(group * rows, rows), rows), :].astype(bf16)


def graph_kernel(
    me_ref, ids_ref, tiles_ref, targets_ref, counts_ref, weight_ref, band_ref, edges_ref, degree_ref
):
    me = me_ref[0]
    parts, groups, slots = targets_ref.shape
    rows = band_ref.shape[1]
    band_ref[...] = jnp.zeros_like(band_ref)

    def place(t, _):
        @pl.when(ids_ref[t, 0] == me)
        def _():
            band_ref[ids_ref[t, 1]] = tiles_ref[t]

        return 0

    lax.fori_loop(0, tiles_ref.shape[0], place, 0)
    mine = lax.broadcasted_iota(jnp.int32, (parts, groups, slots), 1) == me
    target = jnp.sum(jnp.where(mine, targets_ref[...], 0), axis=1)
    weight = jnp.sum(jnp.where(mine, weight_ref[...].astype(f32), 0.0), axis=1)
    count_mine = lax.broadcasted_iota(jnp.int32, (parts, groups), 1) == me
    count = jnp.sum(jnp.where(count_mine, counts_ref[...], 0), axis=1, keepdims=True)
    live = lax.broadcasted_iota(jnp.int32, (parts, slots), 1) < count
    weight = jnp.where(live, weight, 0.0)
    target, weight = target.T, weight.T
    lane = lax.broadcasted_iota(jnp.int32, (slots, rows), 1)
    pieces = [
        jnp.where(target[:, d : d + 1] == lane, weight[:, d : d + 1], 0.0) for d in range(parts)
    ]
    edges = jnp.concatenate(pieces, axis=0).T
    edges_ref[...] = edges.astype(bf16)
    degree = jnp.sum(edges, axis=1, keepdims=True)
    for b in range(band_ref.shape[0]):
        degree = degree + jnp.sum(band_ref[b].astype(f32), axis=1, keepdims=True)
    degree_ref[...] = jnp.broadcast_to(degree, degree_ref.shape)


def blocks(me, groups, width):
    for k in range(groups):
        source = lax.rem(me + groups - k, groups)
        yield k, source, pl.ds(pl.multiple_of(source * width, width), width)


def self_kernel(me_ref, weight_ref, *rest):
    out_ref, parts = rest[-1], rest[:-1]
    total = None
    for k, _, span in blocks(me_ref[0], len(parts), parts[0].shape[1]):
        term = jnp.dot(parts[k][...], weight_ref[span, :], preferred_element_type=f32)
        total = term if total is None else total + term
    out_ref[...] = total


def hidden_kernel(
    groups,
    chunk,
    me_ref,
    weight_ref,
    out_weight_ref,
    sources_ref,
    own_ref,
    edges_ref,
    degree_ref,
    incoming_ref,
    *rest,
):
    locals_ = rest[:groups]
    hidden_ref, projected_ref, send_ref, hits = rest[groups:]
    rows, width = locals_[0].shape
    me = me_ref[0]
    total = own_ref[...]
    degree = degree_ref[:, :1]
    for k, source, span in blocks(me, groups, width):
        arrived = incoming_ref[source].reshape(edges_ref.shape[1], width)
        mean = jnp.dot(edges_ref[...], arrived, preferred_element_type=f32)
        mean = (mean + locals_[k][...].astype(f32)) / degree
        total = total + jnp.dot(
            mean.astype(bf16), weight_ref[span, :], preferred_element_type=f32
        )
    hidden = jnp.maximum(total, 0.0).astype(bf16)
    hidden_ref[...] = hidden
    projected = jnp.dot(hidden, out_weight_ref[...], preferred_element_type=f32).astype(bf16)
    projected_ref[...] = projected
    send_rows(hits, sources_ref, projected, send_ref, chunk, me * rows)


def own_kernel(hidden_ref, weight_ref, out_ref):
    out_ref[...] = jnp.dot(hidden_ref[...], weight_ref[...], preferred_element_type=f32)


def last_kernel(groups, me_ref, own_ref, band_ref, edges_ref, degree_ref, incoming_ref, *rest):
    projected, out_ref = rest[:groups], rest[groups]
    classes = own_ref.shape[1]
    total = jnp.zeros(own_ref.shape, f32)
    for k, source, _ in blocks(me_ref[0], groups, 1):
        total = total + jnp.dot(band_ref[source], projected[k][...], preferred_element_type=f32)
        arrived = incoming_ref[k].reshape(edges_ref.shape[1], classes)
        total = total + jnp.dot(edges_ref[...], arrived, preferred_element_type=f32)
    out_ref[...] = (own_ref[...] + total / degree_ref[:, :1]).T


def on_device(
    features,
    tiles,
    tile_ids,
    sources,
    targets,
    counts,
    edge_weight,
    self_one,
    neigh_one,
    self_out,
    neigh_out,
):
    feature_cols, tile_contents, tile_pairs = features[0], tiles[0], tile_ids[0]
    groups, parts = lax.axis_size("feat"), lax.axis_size("dom")
    me = lax.axis_index("feat")
    me_array = me.astype(jnp.int32).reshape(1)
    nodes, width = feature_cols.shape
    rows, side, slots = nodes // groups, tile_contents.shape[1], sources.shape[3]
    hid, classes = self_one.shape[1], self_out.shape[1]
    chunk = max(1, min(parts, 512 // (groups * slots)))
    both = ("feat", "dom")

    def shape(*dims, dtype=bf16):
        return jax.ShapeDtypeStruct(dims, dtype)

    def shift(value, k):
        return lax.ppermute(value, "feat", [(i, (i + k) % groups) for i in range(groups)])

    def cost(flops, size):
        return pl.CostEstimate(flops=flops, bytes_accessed=size, transcendentals=0)

    feature_blocks = [
        lax.dynamic_slice_in_dim(feature_cols, lax.rem(me + k, groups) * rows, rows)
        for k in range(groups)
    ]
    feature_blocks = feature_blocks[:1] + [
        shift(feature_blocks[k], k) for k in range(1, groups)
    ]
    sent, *local_blocks = call(
        functools.partial(first_kernel, chunk),
        (shape(groups, parts, slots, width),) + (shape(rows, width),) * groups,
        [SM, SM, VM, VM, VM],
        [pltpu.VMEM((nodes, width), f32), pltpu.VMEM((chunk * groups * slots, nodes), bf16)],
        cost(2 * nodes * nodes * width * 2, 1 << 20),
    )(me_array, tile_pairs, sources[0], feature_cols, tile_contents)
    sent = sent.reshape(groups * parts, slots, width)
    incoming = lax.all_to_all(sent, both, split_axis=0, concat_axis=0, tiled=True)
    incoming = incoming.reshape(groups, parts, slots, width)
    local_blocks = local_blocks[:1] + [shift(local_blocks[k], k) for k in range(1, groups)]
    band, edges, degree = call(
        graph_kernel,
        (shape(groups, rows, side), shape(rows, parts * slots), shape(rows, side, dtype=f32)),
        [SM, SM, VM, VM, VM, VM],
        (),
        cost(1 << 20, 2 << 20),
    )(me_array, tile_pairs, tile_contents, targets[0], counts[0], edge_weight[0])
    own = call(
        self_kernel,
        shape(rows, hid, dtype=f32),
        [SM] + [VM] * (1 + groups),
        (),
        cost(2 * rows * hid * groups * width, 2 << 20),
    )(me_array, self_one, *feature_blocks)
    hidden, projected, sent = call(
        functools.partial(hidden_kernel, groups, chunk),
        (shape(rows, hid), shape(rows, classes), shape(groups, parts, slots, classes)),
        [SM] + [VM] * (7 + groups),
        [pltpu.VMEM((chunk * groups * slots, rows), bf16)],
        cost(2 * rows * hid * groups * width, 3 << 20),
    )(me_array, neigh_one, neigh_out, sources[0], own, edges, degree, incoming, *local_blocks)
    sent = sent.reshape(groups * parts, slots, classes)
    incoming = lax.all_to_all(sent, both, split_axis=0, concat_axis=0, tiled=True)
    incoming = incoming.reshape(groups, parts, slots, classes)
    projected = [projected] + [shift(projected, k) for k in range(1, groups)]
    own = call(
        own_kernel, shape(rows, classes, dtype=f32), [VM, VM], (), cost(2 * rows * hid * classes, 1 << 20)
    )(hidden, self_out)
    logits = call(
        functools.partial(last_kernel, groups),
        shape(classes, rows, dtype=f32),
        [SM] + [VM] * (5 + groups),
        (),
        cost(2 * rows * nodes * classes * 2, 1 << 20),
    )(me_array, own, band, edges, degree, incoming, *projected)
    return hidden[None], logits[None]


def solution(mesh):
    placed = (
        P("dom", None, "feat"),
        P("dom", None, None, None),
        P("dom", None, None),
        P("dom", None, None, None),
        P("dom", None, None, None),
        P("dom", None, None),
        P("dom", None, None, None),
        P(),
        P(),
        P(),
        P(),
    )
    return jax.shard_map(
        on_device,
        mesh=mesh,
        in_specs=placed,
        out_specs=(P("dom", "feat", None), P("dom", None, "feat")),
        check_vma=False,
    )
```

time: 99.8 us -> 60.7 us (0.61)
  waiting for transfers between devices: 41.5 us -> 9.9 us
  between operations: 14.3 us -> 0.87 us
  matrix products: 11.8 us -> 0 us
  starting transfers between devices: 17.1 us -> 26.8 us
  Pallas kernels: 0 us -> 8.19 us
  local copies, waits for them, and re-layouts: 10.3 us -> 14.3 us
  other arithmetic: 3.96 us -> 0 us
    all_gather x1 -> x0, waiting for transfers between devices: 24.9 us -> none  [on_device(): received = lax.all_gather(hidden, 'feat', axis=0, tiled=True)]
    all_to_all x4 -> x2, waiting for transfers between devices: 16.6 us -> 0.01 us  [on_device(): lax.all_to_all(sent, both, split_axis=0, concat_axis=0, tiled=True)]
    ppermute x0 -> x9, starting transfers between devices: none -> 13.6 us  [shift(): lax.ppermute(value, 'feat', [(i, (i + k) % groups) for i in range(groups)])]
    dot_general x11 -> x0, matrix products: 11.8 us -> none  [the longest x1 2.71 us: on_device(): jnp.einsum('tb,tic->bic', owners, products, precision=precise)]
    ppermute x0 -> x9, waiting for transfers between devices: none -> 9.89 us  [shift(): lax.ppermute(value, 'feat', [(i, (i + k) % groups) for i in range(groups)])]
    unnamed x22 -> x34, local copies, waits for them, and re-layouts: 1.83 us -> 10.9 us
    pallas_call x0 -> x6, Pallas kernels: none -> 8.19 us  [the longest x1 3.66 us: on_device(): call(functools.partial(first_kernel, chunk), (shape(groups, parts, slots,...]
    gather x3 -> x0, local copies, waits for them, and re-layouts: 5.94 us -> none  [the longest x1 2.4 us: on_device(): jnp.take(received, jnp.clip(send_ids, 0, piece_rows - 1), axis=0)]
  transfers between devices with their start and end apart: 5 -> 11, of which waited for: 5 -> 4; matrix products, arithmetic and copies ran while one was open for 12% -> 7% of each run, Pallas kernels for 0% -> 3%
where the time goes in v1:
time: 60.7 us; the launch traced here: 60 us
  starting transfers between devices  26.8 us (44%)
  local copies, waits for them, and re-layouts  14.3 us (24%)
  waiting for transfers between devices  9.9 us (16%)
  Pallas kernels  8.19 us (13%)
  between operations  0.87 us (1%)
    ppermute x9, starting transfers between devices, shift(): lax.ppermute(value, 'feat', [(i, (i + k) % groups) for i in range(groups)])  13.6 us
    all_to_all x2, starting transfers between devices, on_device(): lax.all_to_all(sent, both, split_axis=0, concat_axis=0, tiled=True)  13.2 us
    unnamed x34, local copies, waits for them, and re-layouts  10.9 us
    ppermute x9, waiting for transfers between devices, shift(): lax.ppermute(value, 'feat', [(i, (i + k) % groups) for i in range(groups)])  9.89 us
    pallas_call x1, Pallas kernels, on_device(): call(functools.partial(first_kernel, chunk), (shape(groups, parts, slots,...  3.66 us
    dynamic_slice x5, local copies, waits for them, and re-layouts, on_device(): lax.dynamic_slice_in_dim(feature_cols, lax.rem(me + k, groups) * rows, rows)  2.57 us
    pallas_call x1, Pallas kernels, on_device(): call(functools.partial(hidden_kernel, groups, chunk), (shape(rows, hid),...  2.11 us
    pallas_call x1, Pallas kernels, on_device(): call(graph_kernel, (shape(groups, rows, side), shape(rows, parts * slots)...  1.42 us
  transfers between devices with their start and end apart: 11, of which 4 were waited for; matrix products, arithmetic and copies ran while one was open for 7% of the time, Pallas kernels for 3%

profile of v1, /device:TPU:0, one launch (start us, length us, event | category | flops | bytes accessed | tf_op | source)
XLA Modules:
  0.0 60.0 jit_solution(15570209237370413049)
XLA Ops:
  0.6 0.8 %copy.17.ids_ref = s32[12,2]{1,0:T(8,128)S(1)} copy(s32[12,2]{0,1:T(2,128)} %bitcast.32) | data formatting | bytes 192 | tf_op jit(solution)/shard_map/squeeze | solution.py:190
  1.4 1.1 %copy.19 = bf16[1,512,192]{2,1,0:T(8,128)(2,1)S(1)} copy(bf16[1,512,192]{1,2,0:T(8,128)(2,1)} %param.11) | data formatting | bytes 393216 | tf_op args[0]
  2.5 0.0 copy-start.2
  2.5 1.0 %copy-done.2 = bf16[1,12,128,128]{3,2,1,0:T(8,128)(2,1)S(1)} copy-done((bf16[1,12,128,128]{3,2,1,0:T(8,128)(2,1)S(1)}, bf16[1,12,128,128]{3,2,1,0:T(8,128)(2,1)}, u32[]{:S(2)}) %copy-start.2) | copy-done | bytes 393240
  3.5 0.7 %copy-done.9 = s32[1,8,4,16]{3,2,1,0:T(4,128)S(1)} copy-done((s32[1,8,4,16]{3,2,1,0:T(4,128)S(1)}, s32[1,8,4,16]{3,2,1,0:T(4,128)}, u32[]{:S(2)}) %copy-start.9) | copy-done | bytes 2072
  4.2 3.7 %shard_map.124 = (bf16[4,8,16,192]{3,2,1,0:T(8,128)(2,1)}, bf16[128,192]{1,0:T(8,128)(2,1)S(1)}, bf16[128,192]{1,0:T(8,128)(2,1)}, bf16[128,192]{1,0:T(8,128)(2,1)}, bf16[128,192]{1,0:T(8,128)(2,1)}) custom-call(s32[1]{0:T(128)} %bitcast.me_ref, s32[12,2]{1,0:T(8,128)S(1)} %copy.17.ids_ref, s32[8,4,16]{2,1,0:T(4,128)S(1)} %bitcast.26, ...), custom_call_target="tpu_custom_call" | custom-call | flops 201326592 | bytes 1048576 | tf_op jit(solution)/shard_map/pallas_call | solution.py:216
  7.9 7.3 %all-to-all-start = ((bf16[32,16,192]{2,1,0:T(8,128)(2,1)}), bf16[32,16,192]{2,1,0:T(8,128)(2,1)S(1)}, u32[]{:S(2)}, u32[]{:S(2)}) async-start(bf16[32,16,192]{2,1,0:T(8,128)(2,1)} %bitcast.12), calls=%async_computation | async-start | bytes 524288 | tf_op jit(solution)/shard_map/all_to_all | solution.py:224
  15.2 0.9 %constant_dynamic-slice_fusion = (bf16[1,128,192]{1,2,0:T(8,128)(2,1)S(1)}, bf16[1,128,192]{1,2,0:T(8,128)(2,1)S(1)}, bf16[1,128,192]{1,2,0:T(8,128)(2,1)S(1)}, bf16[1,128,192]{1,2,0:T(8,128)(2,1)S(1)}) fusion(bf16[1,512,192]{1,2,0:T(8,128)(2,1)} %param.11, s32[]{:T(128)S(6)} %select_n.15, s32[]{:T(128)S(6)} %select_n.14, s32[]{:T(128)S(6)} %select_n.13, ...), kind=kLoop, calls=%fused_computation | loop fusion | bytes 393232 | tf_op jit(solution)/shard_map/dynamic_slice | solution.py:210
  16.1 0.1 copy.14
  16.3 1.8 %collective-permute-start = (bf16[128,192]{1,0:T(8,128)(2,1)S(1)}, bf16[128,192]{1,0:T(8,128)(2,1)S(1)}, u32[]{:S(2)}, u32[]{:S(2)}) collective-permute-start(bf16[128,192]{1,0:T(8,128)(2,1)S(1)} %bitcast.30), channel_id=1, source_target_pairs={{0,8},{8,16},{16,24},{24,0},{1,9},{9,17},{17,25},{25,1},{2,10},{10... | collective-permute-start | bytes 147464 | tf_op jit(solution)/shard_map/ppermute | solution.py:204
  18.1 0.7 %copy.15 = bf16[1,128,192]{2,1,0:T(8,128)(2,1)} copy(bf16[1,128,192]{1,2,0:T(8,128)(2,1)S(1)} %get-tuple-element.27) | data formatting | bytes 98304 | tf_op jit(solution)/shard_map/dynamic_slice | solution.py:210
  18.8 2.4 %collective-permute-start.1 = (bf16[128,192]{1,0:T(8,128)(2,1)}, bf16[128,192]{1,0:T(8,128)(2,1)S(1)}, u32[]{:S(2)}, u32[]{:S(2)}) collective-permute-start(bf16[128,192]{1,0:T(8,128)(2,1)} %bitcast.4), channel_id=1, source_target_pairs={{0,16},{8,24},{16,0},{24,8},{1,17},{9,25},{17,1},{25,9},{2,18},{10... | collective-permute-start | bytes 147464 | tf_op jit(solution)/shard_map/ppermute | solution.py:204
  21.2 0.7 %copy.16 = bf16[1,128,192]{2,1,0:T(8,128)(2,1)} copy(bf16[1,128,192]{1,2,0:T(8,128)(2,1)S(1)} %get-tuple-element.26) | data formatting | bytes 98304 | tf_op jit(solution)/shard_map/dynamic_slice | solution.py:210
  22.0 1.4 %collective-permute-start.2 = (bf16[128,192]{1,0:T(8,128)(2,1)}, bf16[128,192]{1,0:T(8,128)(2,1)S(1)}, u32[]{:S(2)}, u32[]{:S(2)}) collective-permute-start(bf16[128,192]{1,0:T(8,128)(2,1)} %bitcast.5), channel_id=1, source_target_pairs={{0,24},{8,0},{16,8},{24,16},{1,25},{9,1},{17,9},{25,17},{2,26},{10... | collective-permute-start | bytes 147464 | tf_op jit(solution)/shard_map/ppermute | solution.py:204
  23.4 0.6 %collective-permute-start.3 = (bf16[128,192]{1,0:T(8,128)(2,1)}, bf16[128,192]{1,0:T(8,128)(2,1)S(1)}, u32[]{:S(2)}, u32[]{:S(2)}) collective-permute-start(bf16[128,192]{1,0:T(8,128)(2,1)} %get-tuple-element.17), channel_id=1, source_target_pairs={{0,8},{8,16},{16,24},{24,0},{1,9},{9,17},{17,25},{25,1},{2,10},{10... | collective-permute-start | bytes 147464 | tf_op jit(solution)/shard_map/ppermute | solution.py:204
  24.0 0.5 collective-permute-start.4
  24.5 1.5 %collective-permute-done.rest_1_ = bf16[128,192]{1,0:T(8,128)(2,1)S(1)} collective-permute-done((bf16[128,192]{1,0:T(8,128)(2,1)S(1)}, bf16[128,192]{1,0:T(8,128)(2,1)S(1)}, u32[]{:S(2)}, u32[]{:S(2)}) %collective-permute-start) | collective-permute-done | bytes 49184 | tf_op jit(solution)/shard_map/ppermute | solution.py:204
  26.0 1.2 %collective-permute-start.5 = (bf16[128,192]{1,0:T(8,128)(2,1)}, bf16[128,192]{1,0:T(8,128)(2,1)S(1)}, u32[]{:S(2)}, u32[]{:S(2)}) collective-permute-start(bf16[128,192]{1,0:T(8,128)(2,1)} %get-tuple-element.19), channel_id=1, source_target_pairs={{0,24},{8,0},{16,8},{24,16},{1,25},{9,1},{17,9},{25,17},{2,26},{10... | collective-permute-start | bytes 147464 | tf_op jit(solution)/shard_map/ppermute | solution.py:204
  27.2 0.1 copy.13
  27.3 0.1 copy.18.counts_ref
  27.4 1.2 %copy.21.out_weight_ref = bf16[1024,153]{1,0:T(8,128)(2,1)S(1)} copy(bf16[1024,153]{0,1:T(8,128)(2,1)} %param.21) | data formatting | bytes 626688 | tf_op args[10]
  28.6 0.0 copy-start.10
  28.6 0.0 copy-start.12
  28.6 0.7 %copy-done.12 = bf16[1,8,4,16]{3,2,1,0:T(4,128)(2,1)S(1)} copy-done((bf16[1,8,4,16]{3,2,1,0:T(4,128)(2,1)S(1)}, bf16[1,8,4,16]{3,2,1,0:T(4,128)(2,1)}, u32[]{:S(2)}) %copy-start.12) | copy-done | bytes 1048
  29.3 1.4 %shard_map.123 = (bf16[4,128,128]{2,1,0:T(8,128)(2,1)S(1)}, bf16[128,128]{1,0:T(8,128)(2,1)S(1)}, f32[128,128]{1,0:T(8,128)S(1)}) custom-call(s32[1]{0:T(128)} %bitcast.me_ref, s32[12,2]{1,0:T(8,128)S(1)} %copy.17.ids_ref, bf16[12,128,128]{2,1,0:T(8,128)(2,1)S(1)} %bitcast.21, s32[8,4,16]{2,1,0:T(4,128)S(1)} %bitcast.28, s32[8,4]{1,0:T(8,128)S(1)} %copy.18.counts_ref, ...), custom_call_target="tpu_custom_call" | custom-call | flops 1048576 | bytes 2097152 | tf_op jit(solution)/shard_map/pallas_call | solution.py:227
  30.7 1.3 %collective-permute-done.1.rest_2_ = bf16[128,192]{1,0:T(8,128)(2,1)S(1)} collective-permute-done((bf16[128,192]{1,0:T(8,128)(2,1)}, bf16[128,192]{1,0:T(8,128)(2,1)S(1)}, u32[]{:S(2)}, u32[]{:S(2)}) %collective-permute-start.1) | collective-permute-done | bytes 49184 | tf_op jit(solution)/shard_map/ppermute | solution.py:204
  32.1 0.6 %copy-done.5 = bf16[128,192]{1,0:T(8,128)(2,1)} copy-done((bf16[128,192]{1,0:T(8,128)(2,1)}, bf16[128,192]{1,0:T(8,128)(2,1)S(1)}, u32[]{:S(2)}) %copy-start.5) | copy-done | bytes 49176
  32.7 0.0 collective-permute-done.2.rest_3_
  32.7 0.6 %copy-done.7 = bf16[128,192]{1,0:T(8,128)(2,1)} copy-done((bf16[128,192]{1,0:T(8,128)(2,1)}, bf16[128,192]{1,0:T(8,128)(2,1)S(1)}, u32[]{:S(2)}) %copy-start.7) | copy-done | bytes 49176
  33.3 0.8 %copy-done.6 = bf16[128,192]{1,0:T(8,128)(2,1)S(1)} copy-done((bf16[128,192]{1,0:T(8,128)(2,1)S(1)}, bf16[128,192]{1,0:T(8,128)(2,1)}, u32[]{:S(2)}) %copy-start.6) | copy-done | bytes 49176
  34.2 0.8 %copy-done.8 = bf16[128,192]{1,0:T(8,128)(2,1)S(1)} copy-done((bf16[128,192]{1,0:T(8,128)(2,1)S(1)}, bf16[128,192]{1,0:T(8,128)(2,1)}, u32[]{:S(2)}) %copy-start.8) | copy-done | bytes 49176
  35.0 0.4 shard_map.122.own_ref
  35.5 0.0 collective-permute-done.3.rest_1_
  35.5 0.0 copy-start.1
  35.5 1.4 %copy-done.1 = bf16[768,1024]{1,0:T(8,128)(2,1)S(1)} copy-done((bf16[768,1024]{1,0:T(8,128)(2,1)S(1)}, bf16[768,1024]{1,0:T(8,128)(2,1)}, u32[]{:S(2)}) %copy-start.1) | copy-done | bytes 1572888
  36.9 2.1 %shard_map.125 = (bf16[128,1024]{1,0:T(8,128)(2,1)}, bf16[128,153]{1,0:T(8,128)(2,1)S(1)}, bf16[4,8,16,153]{3,2,1,0:T(8,128)(2,1)}) custom-call(s32[1]{0:T(128)} %bitcast.me_ref, bf16[768,1024]{1,0:T(8,128)(2,1)S(1)} %copy-done.1, bf16[1024,153]{1,0:T(8,128)(2,1)S(1)} %copy.21.out_weight_ref, s32[8,4,16]{2,1,0:T(4,128)S(1)} %bitcast.27, ...), custom_call_target="tpu_custom_call" | custom-call | flops 201326592 | bytes 3145728 | tf_op jit(solution)/shard_map/pallas_call | solution.py:241
  39.0 5.9 %all-to-all-start.1 = ((bf16[32,16,153]{2,1,0:T(8,128)(2,1)}), bf16[32,16,153]{2,1,0:T(8,128)(2,1)S(1)}, u32[]{:S(2)}, u32[]{:S(2)}) async-start(bf16[32,16,153]{2,1,0:T(8,128)(2,1)} %bitcast.15), calls=%async_computation.1 | async-start | bytes 524288 | tf_op jit(solution)/shard_map/all_to_all | solution.py:249
  44.9 1.8 %collective-permute-start.6 = (bf16[128,153]{1,0:T(8,128)(2,1)S(1)}, bf16[128,153]{1,0:T(8,128)(2,1)S(1)}, u32[]{:S(2)}, u32[]{:S(2)}) collective-permute-start(bf16[128,153]{1,0:T(8,128)(2,1)S(1)} %get-tuple-element.23.rest_0_), channel_id=1, source_target_pairs={{0,8},{8,16},{16,24},{24,0},{1,9},{9,17},{17,25},{25,1},{2,10},{10... | collective-permute-start | bytes 117512 | tf_op jit(solution)/shard_map/ppermute | solution.py:204
  46.7 2.4 %collective-permute-start.7 = (bf16[128,153]{1,0:T(8,128)(2,1)S(1)}, bf16[128,153]{1,0:T(8,128)(2,1)S(1)}, u32[]{:S(2)}, u32[]{:S(2)}) collective-permute-start(bf16[128,153]{1,0:T(8,128)(2,1)S(1)} %get-tuple-element.23.rest_0_), channel_id=1, source_target_pairs={{0,16},{8,24},{16,0},{24,8},{1,17},{9,25},{17,1},{25,9},{2,18},{10... | collective-permute-start | bytes 117512 | tf_op jit(solution)/shard_map/ppermute | solution.py:204
  49.1 1.4 %collective-permute-start.8 = (bf16[128,153]{1,0:T(8,128)(2,1)S(1)}, bf16[128,153]{1,0:T(8,128)(2,1)S(1)}, u32[]{:S(2)}, u32[]{:S(2)}) collective-permute-start(bf16[128,153]{1,0:T(8,128)(2,1)S(1)} %get-tuple-element.23.rest_0_), channel_id=1, source_target_pairs={{0,24},{8,0},{16,8},{24,16},{1,25},{9,1},{17,9},{25,17},{2,26},{10... | collective-permute-start | bytes 117512 | tf_op jit(solution)/shard_map/ppermute | solution.py:204
  50.6 0.2 copy.22.weight_ref
  50.8 0.0 copy-start.4
  50.8 0.9 %copy-done.4 = bf16[128,1024]{1,0:T(8,128)(2,1)S(1)} copy-done((bf16[128,1024]{1,0:T(8,128)(2,1)S(1)}, bf16[128,1024]{1,0:T(8,128)(2,1)}, u32[]{:S(2)}) %copy-start.4) | copy-done | bytes 262168
  51.7 0.2 shard_map.126.own_ref
  52.0 3.7 %collective-permute-done.6.rest_1_ = bf16[128,153]{1,0:T(8,128)(2,1)S(1)} collective-permute-done((bf16[128,153]{1,0:T(8,128)(2,1)S(1)}, bf16[128,153]{1,0:T(8,128)(2,1)S(1)}, u32[]{:S(2)}, u32[]{:S(2)}) %collective-permute-start.6) | collective-permute-done | bytes 39200 | tf_op jit(solution)/shard_map/ppermute | solution.py:204
  55.7 3.3 %collective-permute-done.7.rest_2_ = bf16[128,153]{1,0:T(8,128)(2,1)S(1)} collective-permute-done((bf16[128,153]{1,0:T(8,128)(2,1)S(1)}, bf16[128,153]{1,0:T(8,128)(2,1)S(1)}, u32[]{:S(2)}, u32[]{:S(2)}) %collective-permute-start.7) | collective-permute-done | bytes 39200 | tf_op jit(solution)/shard_map/ppermute | solution.py:204
  59.0 0.4 shard_map.127
  59.3 0.7 %copy.23 = f32[1,153,128]{2,0,1:T(1,128)} copy(f32[1,153,128]{2,1,0:T(8,128)S(1)} %bitcast.22) | data formatting | bytes 156672
  (21 shorter events, 0.0 us)
Async XLA Ops:
  0.6 26.7 %copy-start.14 = (s32[1,8,4]{1,2,0:T(4,128)S(1)}, s32[1,8,4]{1,2,0:T(4,128)}, u32[]{:S(2)}) copy-start(s32[1,8,4]{1,2,0:T(4,128)} %param.16) | copy-start | bytes 388
  1.4 27.2 %copy-start.3 = (bf16[1,12,128,128]{3,2,1,0:T(8,128)(2,1)S(1)}, bf16[1,12,128,128]{3,2,1,0:T(8,128)(2,1)}, u32[]{:S(2)}) copy-start(bf16[1,12,128,128]{3,2,1,0:T(8,128)(2,1)} %param.12) | copy-start | bytes 1179652
  1.4 27.2 %copy-start.11 = (s32[1,8,4,16]{3,2,1,0:T(4,128)S(1)}, s32[1,8,4,16]{3,2,1,0:T(4,128)}, u32[]{:S(2)}) copy-start(s32[1,8,4,16]{3,2,1,0:T(4,128)} %param.15) | copy-start | bytes 6148
  2.5 1.0 %copy-start.2 = (bf16[1,12,128,128]{3,2,1,0:T(8,128)(2,1)S(1)}, bf16[1,12,128,128]{3,2,1,0:T(8,128)(2,1)}, u32[]{:S(2)}) copy-start(bf16[1,12,128,128]{3,2,1,0:T(8,128)(2,1)} %param.12) | copy-start | bytes 1179652
  3.5 0.7 %copy-start.9 = (s32[1,8,4,16]{3,2,1,0:T(4,128)S(1)}, s32[1,8,4,16]{3,2,1,0:T(4,128)}, u32[]{:S(2)}) copy-start(s32[1,8,4,16]{3,2,1,0:T(4,128)} %param.14) | copy-start | bytes 6148
  7.9 25.4 %copy-start = (bf16[768,1024]{1,0:T(8,128)(2,1)S(1)}, bf16[768,1024]{1,0:T(8,128)(2,1)}, u32[]{:S(2)}) copy-start(bf16[768,1024]{1,0:T(8,128)(2,1)} %weight_ref.3) | copy-start | bytes 4718596
  7.9 27.6 %all-to-all-start = ((bf16[32,16,192]{2,1,0:T(8,128)(2,1)}), bf16[32,16,192]{2,1,0:T(8,128)(2,1)S(1)}, u32[]{:S(2)}, u32[]{:S(2)}) async-start(bf16[32,16,192]{2,1,0:T(8,128)(2,1)} %bitcast.12), calls=%async_computation | async-start | bytes 524288 | tf_op jit(solution)/shard_map/all_to_all | solution.py:224
  16.3 9.8 %collective-permute-start = (bf16[128,192]{1,0:T(8,128)(2,1)S(1)}, bf16[128,192]{1,0:T(8,128)(2,1)S(1)}, u32[]{:S(2)}, u32[]{:S(2)}) collective-permute-start(bf16[128,192]{1,0:T(8,128)(2,1)S(1)} %bitcast.30), channel_id=1, source_target_pairs={{0,8},{8,16},{16,24},{24,0},{1,9},{9,17},{17,25},{25,1},{2,10},{10... | collective-permute-start | bytes 147464 | tf_op jit(solution)/shard_map/ppermute | solution.py:204
  18.8 13.3 %collective-permute-start.1 = (bf16[128,192]{1,0:T(8,128)(2,1)}, bf16[128,192]{1,0:T(8,128)(2,1)S(1)}, u32[]{:S(2)}, u32[]{:S(2)}) collective-permute-start(bf16[128,192]{1,0:T(8,128)(2,1)} %bitcast.4), channel_id=1, source_target_pairs={{0,16},{8,24},{16,0},{24,8},{1,17},{9,25},{17,1},{25,9},{2,18},{10... | collective-permute-start | bytes 147464 | tf_op jit(solution)/shard_map/ppermute | solution.py:204
  22.0 10.8 %collective-permute-start.2 = (bf16[128,192]{1,0:T(8,128)(2,1)}, bf16[128,192]{1,0:T(8,128)(2,1)S(1)}, u32[]{:S(2)}, u32[]{:S(2)}) collective-permute-start(bf16[128,192]{1,0:T(8,128)(2,1)} %bitcast.5), channel_id=1, source_target_pairs={{0,24},{8,0},{16,8},{24,16},{1,25},{9,1},{17,9},{25,17},{2,26},{10... | collective-permute-start | bytes 147464 | tf_op jit(solution)/shard_map/ppermute | solution.py:204
  23.4 12.1 %collective-permute-start.3 = (bf16[128,192]{1,0:T(8,128)(2,1)}, bf16[128,192]{1,0:T(8,128)(2,1)S(1)}, u32[]{:S(2)}, u32[]{:S(2)}) collective-permute-start(bf16[128,192]{1,0:T(8,128)(2,1)} %get-tuple-element.17), channel_id=1, source_target_pairs={{0,8},{8,16},{16,24},{24,0},{1,9},{9,17},{17,25},{25,1},{2,10},{10... | collective-permute-start | bytes 147464 | tf_op jit(solution)/shard_map/ppermute | solution.py:204
  24.0 11.5 %collective-permute-start.4 = (bf16[128,192]{1,0:T(8,128)(2,1)}, bf16[128,192]{1,0:T(8,128)(2,1)S(1)}, u32[]{:S(2)}, u32[]{:S(2)}) collective-permute-start(bf16[128,192]{1,0:T(8,128)(2,1)} %get-tuple-element.18), channel_id=1, source_target_pairs={{0,16},{8,24},{16,0},{24,8},{1,17},{9,25},{17,1},{25,9},{2,18},{10... | collective-permute-start | bytes 147464 | tf_op jit(solution)/shard_map/ppermute | solution.py:204
  26.0 9.5 %collective-permute-start.5 = (bf16[128,192]{1,0:T(8,128)(2,1)}, bf16[128,192]{1,0:T(8,128)(2,1)S(1)}, u32[]{:S(2)}, u32[]{:S(2)}) collective-permute-start(bf16[128,192]{1,0:T(8,128)(2,1)} %get-tuple-element.19), channel_id=1, source_target_pairs={{0,24},{8,0},{16,8},{24,16},{1,25},{9,1},{17,9},{25,17},{2,26},{10... | collective-permute-start | bytes 147464 | tf_op jit(solution)/shard_map/ppermute | solution.py:204
  28.6 6.9 %copy-start.10 = (s32[1,8,4,16]{3,2,1,0:T(4,128)S(1)}, s32[1,8,4,16]{3,2,1,0:T(4,128)}, u32[]{:S(2)}) copy-start(s32[1,8,4,16]{3,2,1,0:T(4,128)} %param.14) | copy-start | bytes 6148
  28.6 0.7 %copy-start.12 = (bf16[1,8,4,16]{3,2,1,0:T(4,128)(2,1)S(1)}, bf16[1,8,4,16]{3,2,1,0:T(4,128)(2,1)}, u32[]{:S(2)}) copy-start(bf16[1,8,4,16]{3,2,1,0:T(4,128)(2,1)} %param.17) | copy-start | bytes 3076
  32.1 0.6 %copy-start.5 = (bf16[128,192]{1,0:T(8,128)(2,1)}, bf16[128,192]{1,0:T(8,128)(2,1)S(1)}, u32[]{:S(2)}) copy-start(bf16[128,192]{1,0:T(8,128)(2,1)S(1)} %collective-permute-done.1.rest_2_) | copy-start | bytes 147460
  32.7 0.6 %copy-start.7 = (bf16[128,192]{1,0:T(8,128)(2,1)}, bf16[128,192]{1,0:T(8,128)(2,1)S(1)}, u32[]{:S(2)}) copy-start(bf16[128,192]{1,0:T(8,128)(2,1)S(1)} %collective-permute-done.2.rest_3_) | copy-start | bytes 147460
  33.3 0.8 %copy-start.6 = (bf16[128,192]{1,0:T(8,128)(2,1)S(1)}, bf16[128,192]{1,0:T(8,128)(2,1)}, u32[]{:S(2)}) copy-start(bf16[128,192]{1,0:T(8,128)(2,1)} %copy-done.5) | copy-start | bytes 147460
  34.2 0.8 %copy-start.8 = (bf16[128,192]{1,0:T(8,128)(2,1)S(1)}, bf16[128,192]{1,0:T(8,128)(2,1)}, u32[]{:S(2)}) copy-start(bf16[128,192]{1,0:T(8,128)(2,1)} %copy-done.7) | copy-start | bytes 147460
  35.5 1.4 %copy-start.1 = (bf16[768,1024]{1,0:T(8,128)(2,1)S(1)}, bf16[768,1024]{1,0:T(8,128)(2,1)}, u32[]{:S(2)}) copy-start(bf16[768,1024]{1,0:T(8,128)(2,1)} %weight_ref.4) | copy-start | bytes 4718596
  36.9 13.6 %copy-start.13 = (bf16[1024,153]{0,1:T(8,128)(2,1)S(1)}, bf16[1024,153]{0,1:T(8,128)(2,1)}, u32[]{:S(2)}) copy-start(bf16[1024,153]{0,1:T(8,128)(2,1)} %param.20) | copy-start | bytes 940036
  39.0 19.9 %all-to-all-start.1 = ((bf16[32,16,153]{2,1,0:T(8,128)(2,1)}), bf16[32,16,153]{2,1,0:T(8,128)(2,1)S(1)}, u32[]{:S(2)}, u32[]{:S(2)}) async-start(bf16[32,16,153]{2,1,0:T(8,128)(2,1)} %bitcast.15), calls=%async_computation.1 | async-start | bytes 524288 | tf_op jit(solution)/shard_map/all_to_all | solution.py:249
  44.9 10.8 %collective-permute-start.6 = (bf16[128,153]{1,0:T(8,128)(2,1)S(1)}, bf16[128,153]{1,0:T(8,128)(2,1)S(1)}, u32[]{:S(2)}, u32[]{:S(2)}) collective-permute-start(bf16[128,153]{1,0:T(8,128)(2,1)S(1)} %get-tuple-element.23.rest_0_), channel_id=1, source_target_pairs={{0,8},{8,16},{16,24},{24,0},{1,9},{9,17},{17,25},{25,1},{2,10},{10... | collective-permute-start | bytes 117512 | tf_op jit(solution)/shard_map/ppermute | solution.py:204
  46.7 12.2 %collective-permute-start.7 = (bf16[128,153]{1,0:T(8,128)(2,1)S(1)}, bf16[128,153]{1,0:T(8,128)(2,1)S(1)}, u32[]{:S(2)}, u32[]{:S(2)}) collective-permute-start(bf16[128,153]{1,0:T(8,128)(2,1)S(1)} %get-tuple-element.23.rest_0_), channel_id=1, source_target_pairs={{0,16},{8,24},{16,0},{24,8},{1,17},{9,25},{17,1},{25,9},{2,18},{10... | collective-permute-start | bytes 117512 | tf_op jit(solution)/shard_map/ppermute | solution.py:204
  49.1 9.8 %collective-permute-start.8 = (bf16[128,153]{1,0:T(8,128)(2,1)S(1)}, bf16[128,153]{1,0:T(8,128)(2,1)S(1)}, u32[]{:S(2)}, u32[]{:S(2)}) collective-permute-start(bf16[128,153]{1,0:T(8,128)(2,1)S(1)} %get-tuple-element.23.rest_0_), channel_id=1, source_target_pairs={{0,24},{8,0},{16,8},{24,16},{1,25},{9,1},{17,9},{25,17},{2,26},{10... | collective-permute-start | bytes 117512 | tf_op jit(solution)/shard_map/ppermute | solution.py:204
  50.8 1.0 %copy-start.4 = (bf16[128,1024]{1,0:T(8,128)(2,1)S(1)}, bf16[128,1024]{1,0:T(8,128)(2,1)}, u32[]{:S(2)}) copy-start(bf16[128,1024]{1,0:T(8,128)(2,1)} %get-tuple-element.20.hidden_ref) | copy-start | bytes 786436

commit v2 on v0

v2 whole, which is shorter than its diff:
```python
import functools

import jax
import jax.numpy as jnp
from jax import lax
from jax.experimental import pallas as pl
from jax.experimental.pallas import tpu as pltpu
from jax.sharding import PartitionSpec as P

f32 = jnp.float32
bf16 = jnp.bfloat16
VM = pl.BlockSpec(memory_space=pltpu.VMEM)
SM = pl.BlockSpec(memory_space=pltpu.SMEM)
LAST = (((1,), (1,)), ((), ()))
FIRST = (((0,), (0,)), ((), ()))


def call(kernel, out_shape, in_specs, scratch=(), flops=0, size=0):
    return pl.pallas_call(
        kernel,
        out_shape=out_shape,
        in_specs=in_specs,
        out_specs=jax.tree.map(lambda _: VM, out_shape),
        scratch_shapes=list(scratch),
        cost_estimate=pl.CostEstimate(flops=flops, bytes_accessed=size, transcendentals=0),
        compiler_params=pltpu.CompilerParams(vmem_limit_bytes=24 << 20),
    )


def dot(left, right, dims):
    return lax.dot_general(left, right, dims, preferred_element_type=f32)


def behind(me, groups, k):
    return lax.rem(me + groups - k, groups)


def gather_kernel(chunk, me_ref, sources_ref, features_ref, out_ref, *rest):
    blocks, hits = rest[:-1], rest[-1]
    parts, groups, slots = sources_ref.shape
    nodes = hits.shape[1]
    rows = nodes // groups
    table = features_ref[...]
    lane = lax.broadcasted_iota(jnp.int32, (slots, nodes), 1)

    def step(i, _):
        for e in range(chunk):
            columns = sources_ref[i * chunk + e].T
            for g in range(groups):
                row = (e * groups + g) * slots
                hits[row : row + slots, :] = jnp.where(
                    columns[:, g : g + 1] == lane, 1.0, 0.0
                ).astype(bf16)
        picked = dot(hits[...], table, LAST).astype(bf16)
        out_ref[pl.ds(i * chunk, chunk)] = picked.reshape(chunk, groups * slots, -1)
        return 0

    if parts == chunk:
        step(0, 0)
    else:
        lax.fori_loop(0, parts // chunk, step, 0)
    for k in range(groups):
        group = lax.rem(me_ref[0] + k, groups)
        blocks[k][...] = features_ref[:, pl.ds(pl.multiple_of(group * rows, rows), rows)]


def local_kernel(
    me_ref,
    ids_ref,
    counts_ref,
    features_ref,
    tiles_ref,
    targets_ref,
    weight_ref,
    sums_ref,
    edges_ref,
    degree_ref,
    band_ref,
):
    me = me_ref[0]
    parts, groups, slots = targets_ref.shape
    rows = tiles_ref.shape[1]
    sums_ref[...] = jnp.zeros_like(sums_ref)
    degree_ref[...] = jnp.zeros_like(degree_ref)
    band_ref[...] = jnp.zeros_like(band_ref)
    ones = jnp.ones((degree_ref.shape[1], rows), bf16)

    def add(t, _):
        to, at = ids_ref[0, t], ids_ref[1, t]
        tile = tiles_ref[t]
        part = features_ref[:, pl.ds(pl.multiple_of(at * rows, rows), rows)]
        sums_ref[to] += dot(part, tile, LAST)
        degree_ref[to] += dot(ones, tile, LAST)

        @pl.when(to == me)
        def _():
            band_ref[at] = tile

        return 0

    lax.fori_loop(0, tiles_ref.shape[0], add, 0)
    lane = lax.broadcasted_iota(jnp.int32, (slots, rows), 1)
    slot = lax.broadcasted_iota(jnp.int32, (slots, rows), 0)

    def connect(d, _):
        target, weight = targets_ref[d].T, weight_ref[d].astype(f32).T
        for g in range(groups):
            hit = (target[:, g : g + 1] == lane) & (slot < counts_ref[g, d])
            values = jnp.where(hit, weight[:, g : g + 1], 0.0)
            edges_ref[g, d] = values.astype(bf16)
            degree_ref[g] += jnp.sum(values, axis=0, keepdims=True)
        return 0

    lax.fori_loop(0, parts, connect, 0)


def mean_kernel(me_ref, incoming_ref, sums_ref, edges_ref, degree_ref, *outs):
    groups, parts, slots, rows = edges_ref.shape
    width = incoming_ref.shape[2]
    for k in range(groups):
        group = lax.rem(me_ref[0] + k, groups)
        arrived = incoming_ref[:, pl.ds(pl.multiple_of(group * slots, slots), slots), :]
        arrived = arrived.reshape(parts * slots, width)
        total = sums_ref[group] + dot(arrived, edges_ref[group].reshape(parts * slots, rows), FIRST)
        outs[k][...] = (total / degree_ref[group][:1]).astype(bf16)


def self_kernel(me_ref, weight_ref, *rest):
    out_ref, parts = rest[-1], rest[:-1]
    width = parts[0].shape[0]
    total = None
    for k in range(len(parts)):
        source = behind(me_ref[0], len(parts), k)
        span = pl.ds(pl.multiple_of(source * width, width), width)
        term = dot(parts[k][...], weight_ref[span, :], FIRST)
        total = term if total is None else total + term
    out_ref[...] = total


def hidden_kernel(me_ref, weight_ref, out_weight_ref, own_ref, *rest):
    parts, hidden_ref, projected_ref = rest[:-2], rest[-2], rest[-1]
    width = parts[0].shape[0]
    total = own_ref[...]
    for k in range(len(parts)):
        source = behind(me_ref[0], len(parts), k)
        span = pl.ds(pl.multiple_of(source * width, width), width)
        total = total + dot(parts[k][...], weight_ref[span, :], FIRST)
    hidden = jnp.maximum(total, 0.0).astype(bf16)
    hidden_ref[...] = hidden
    projected_ref[...] = dot(out_weight_ref[...], hidden, LAST).astype(bf16)


def own_kernel(hidden_ref, weight_ref, out_ref):
    out_ref[...] = dot(weight_ref[...], hidden_ref[...], LAST)


def pick_kernel(me_ref, sources_ref, *rest):
    projected, out_ref = rest[:-1], rest[-1]
    parts, groups, slots = sources_ref.shape
    me, rows = me_ref[0], projected[0].shape[1]
    mine = lax.broadcasted_iota(jnp.int32, sources_ref.shape, 1) == me
    picks = jnp.sum(jnp.where(mine, sources_ref[...], 0), axis=1).T
    picks = jnp.concatenate(
        [jnp.broadcast_to(picks[:, e : e + 1], (slots, rows)) for e in range(parts)], axis=0
    )
    lane = lax.broadcasted_iota(jnp.int32, picks.shape, 1)
    total = None
    for k in range(groups):
        hits = jnp.where(picks == lane + behind(me, groups, k) * rows, 1.0, 0.0).astype(bf16)
        term = dot(hits, projected[k][...], LAST)
        total = term if total is None else total + term
    out_ref[...] = total.astype(bf16).reshape(out_ref.shape)


def near_kernel(me_ref, band_ref, *rest):
    projected, out_ref = rest[:-1], rest[-1]
    groups = len(projected)
    total = None
    for k in range(groups):
        term = dot(projected[k][...], band_ref[behind(me_ref[0], groups, k)], LAST)
        total = term if total is None else total + term
    out_ref[...] = total


def last_kernel(me_ref, own_ref, near_ref, edges_ref, degree_ref, incoming_ref, out_ref):
    groups, parts, slots, rows = edges_ref.shape
    me = me_ref[0]
    arrived = incoming_ref[...].reshape(parts * slots, -1)
    far = dot(arrived, edges_ref[me].reshape(parts * slots, rows), FIRST)
    total = own_ref[...] + (near_ref[...] + far) / degree_ref[me][:1]
    out_ref[...] = total.reshape(out_ref.shape)


def on_device(
    features,
    tiles,
    tile_ids,
    sources,
    targets,
    counts,
    edge_weight,
    self_one,
    neigh_one,
    self_out,
    neigh_out,
):
    feature_rows, tile_contents = features[0].T, tiles[0]
    groups, parts = lax.axis_size("feat"), lax.axis_size("dom")
    me = lax.axis_index("feat").astype(jnp.int32).reshape(1)
    width, nodes = feature_rows.shape
    rows, slots = nodes // groups, sources.shape[3]
    hid, classes = self_one.shape[1], self_out.shape[1]
    chunk = max(1, min(parts, 512 // (groups * slots)))

    def shape(*dims, dtype=bf16):
        return jax.ShapeDtypeStruct(dims, dtype)

    def shift(blocks):
        return [blocks[0]] + [
            lax.ppermute(blocks[k], "feat", [(i, (i + k) % groups) for i in range(groups)])
            for k in range(1, groups)
        ]

    def swap(value):
        return lax.all_to_all(value, "dom", split_axis=0, concat_axis=0, tiled=True)

    sent, *feature_blocks = call(
        functools.partial(gather_kernel, chunk),
        (shape(parts, groups * slots, width),) + (shape(width, rows),) * groups,
        [SM, VM, VM],
        [pltpu.VMEM((chunk * groups * slots, nodes), bf16)],
        2 * nodes * nodes * width,
        1 << 20,
    )(me, sources[0], feature_rows)
    incoming = swap(sent)
    feature_blocks = shift(feature_blocks)
    sums, edges, degree, band = call(
        local_kernel,
        (
            shape(groups, width, rows, dtype=f32),
            shape(groups, parts, slots, rows),
            shape(groups, 8, rows, dtype=f32),
            shape(groups, rows, rows),
        ),
        [SM, SM, SM, VM, VM, VM, VM],
        (),
        2 * nodes * nodes * width,
        1 << 20,
    )(
        me,
        tile_ids[0].T,
        counts[0].T,
        feature_rows,
        tile_contents,
        targets[0],
        edge_weight[0],
    )
    means = call(
        mean_kernel,
        (shape(width, rows),) * groups,
        [SM, VM, VM, VM, VM],
        (),
        2 * nodes * parts * slots * width,
        1 << 20,
    )(me, incoming, sums, edges, degree)
    means = shift(means)
    own = call(
        self_kernel,
        shape(rows, hid, dtype=f32),
        [SM] + [VM] * (1 + groups),
        (),
        2 * rows * hid * groups * width,
        2 << 20,
    )(me, self_one, *feature_blocks)
    hidden, projected = call(
        hidden_kernel,
        (shape(rows, hid), shape(classes, rows)),
        [SM] + [VM] * (3 + groups),
        (),
        2 * rows * hid * groups * width,
        2 << 20,
    )(me, neigh_one, neigh_out.T, own, *means)
    projected = shift([projected] * groups)
    sent = call(
        pick_kernel,
        shape(parts, slots, classes),
        [SM] + [VM] * (1 + groups),
        (),
        2 * parts * slots * nodes * classes,
        1 << 19,
    )(me, sources[0], *projected)
    incoming = swap(sent)
    own = call(
        own_kernel,
        shape(classes, rows, dtype=f32),
        [VM, VM],
        (),
        2 * rows * hid * classes,
        1 << 20,
    )(hidden, self_out.T)
    near = call(
        near_kernel,
        shape(classes, rows, dtype=f32),
        [SM] + [VM] * (1 + groups),
        (),
        2 * rows * nodes * classes,
        1 << 19,
    )(me, band, *projected)
    logits = call(
        last_kernel,
        shape(classes, 1, rows, dtype=f32),
        [SM] + [VM] * 5,
        (),
        2 * rows * parts * slots * classes,
        1 << 19,
    )(me, own, near, edges, degree, incoming)
    return hidden[None], logits.transpose(1, 0, 2)


def solution(mesh):
    placed = (
        P("dom", None, "feat"),
        P("dom", None, None, None),
        P("dom", None, None),
        P("dom", None, None, None),
        P("dom", None, None, None),
        P("dom", None, None),
        P("dom", None, None, None),
        P(),
        P(),
        P(),
        P(),
    )
    return jax.shard_map(
        on_device,
        mesh=mesh,
        in_specs=placed,
        out_specs=(P("dom", "feat", None), P("dom", None, "feat")),
        check_vma=False,
    )
```

time: 99.8 us -> 55.5 us (0.56)
  waiting for transfers between devices: 41.5 us -> 10 us
  between operations: 14.3 us -> 0.78 us
  matrix products: 11.8 us -> 0 us
  Pallas kernels: 0 us -> 10.5 us
  starting transfers between devices: 17.1 us -> 22.1 us
  other arithmetic: 3.96 us -> 0 us
  local copies, waits for them, and re-layouts: 10.3 us -> 11.3 us
    all_gather x1 -> x0, waiting for transfers between devices: 24.9 us -> none  [on_device(): received = lax.all_gather(hidden, 'feat', axis=0, tiled=True)]
    all_to_all x4 -> x2, waiting for transfers between devices: 16.6 us -> 3.58 us  [swap(): return lax.all_to_all(value, 'dom', split_axis=0, concat_axis=0, tiled=True)]
    ppermute x0 -> x9, starting transfers between devices: none -> 12.7 us  [shift(): lax.ppermute(blocks[k], 'feat', [(i, (i + k) % groups) for i in range(gro...]
    dot_general x11 -> x0, matrix products: 11.8 us -> none  [the longest x1 2.71 us: on_device(): jnp.einsum('tb,tic->bic', owners, products, precision=precise)]
    pallas_call x0 -> x9, Pallas kernels: none -> 10.5 us  [the longest x1 4.13 us: on_device(): call(local_kernel, (shape(groups, width, rows, dtype=f32), shape(groups,...]
    unnamed x22 -> x40, local copies, waits for them, and re-layouts: 1.83 us -> 11.3 us
    all_to_all x4 -> x2, starting transfers between devices: 17.1 us -> 9.38 us  [swap(): return lax.all_to_all(value, 'dom', split_axis=0, concat_axis=0, tiled=True)]
    ppermute x0 -> x9, waiting for transfers between devices: none -> 6.43 us  [shift(): lax.ppermute(blocks[k], 'feat', [(i, (i + k) % groups) for i in range(gro...]
  transfers between devices with their start and end apart: 5 -> 11, of which waited for: 5 -> 6; matrix products, arithmetic and copies ran while one was open for 12% -> 0% of each run, Pallas kernels for 0% -> 11%
where the time goes in v2:
time: 55.5 us; the launch traced here: 54.8 us
  starting transfers between devices  22.1 us (40%)
  local copies, waits for them, and re-layouts  11.3 us (20%)
  Pallas kernels  10.5 us (19%)
  waiting for transfers between devices  10 us (18%)
  between operations  0.78 us (1%)
    ppermute x9, starting transfers between devices, shift(): lax.ppermute(blocks[k], 'feat', [(i, (i + k) % groups) for i in range(gro...  12.7 us
    unnamed x40, local copies, waits for them, and re-layouts  11.3 us
    all_to_all x2, starting transfers between devices, swap(): return lax.all_to_all(value, 'dom', split_axis=0, concat_axis=0, tiled=True)  9.38 us
    ppermute x9, waiting for transfers between devices, shift(): lax.ppermute(blocks[k], 'feat', [(i, (i + k) % groups) for i in range(gro...  6.43 us
    pallas_call x1, Pallas kernels, on_device(): call(local_kernel, (shape(groups, width, rows, dtype=f32), shape(groups,...  4.13 us
    all_to_all x2, waiting for transfers between devices, swap(): return lax.all_to_all(value, 'dom', split_axis=0, concat_axis=0, tiled=True)  3.58 us
    pallas_call x1, Pallas kernels, on_device(): call(functools.partial(gather_kernel, chunk), (shape(parts, groups * slot...  1.33 us
    pallas_call x1, Pallas kernels, on_device(): call(self_kernel, shape(rows, hid, dtype=f32), [SM] + [VM] * (1 + groups)...  1.3 us
  transfers between devices with their start and end apart: 11, of which 6 were waited for; matrix products, arithmetic and copies ran while one was open for 0% of the time, Pallas kernels for 11%

profile of v2, /device:TPU:0, one launch (start us, length us, event | category | flops | bytes accessed | tf_op | source)
XLA Modules:
  0.0 54.8 jit_solution(7438338140121811202)
XLA Ops:
  0.6 0.0 copy-start.8
  0.7 1.0 %copy-done.8 = bf16[1,512,192]{1,2,0:T(8,128)(2,1)S(1)} copy-done((bf16[1,512,192]{1,2,0:T(8,128)(2,1)S(1)}, bf16[1,512,192]{1,2,0:T(8,128)(2,1)}, u32[]{:S(2)}) %copy-start.8) | copy-done | bytes 196632
  1.7 0.7 %copy-done.15 = s32[1,8,4,16]{3,2,1,0:T(4,128)S(1)} copy-done((s32[1,8,4,16]{3,2,1,0:T(4,128)S(1)}, s32[1,8,4,16]{3,2,1,0:T(4,128)}, u32[]{:S(2)}) %copy-start.15) | copy-done | bytes 2072
  2.4 1.3 %shard_map.122 = (bf16[8,64,192]{2,1,0:T(8,128)(2,1)}, bf16[192,128]{1,0:T(8,128)(2,1)S(1)}, bf16[192,128]{1,0:T(8,128)(2,1)}, bf16[192,128]{1,0:T(8,128)(2,1)}, bf16[192,128]{1,0:T(8,128)(2,1)}) custom-call(s32[1]{0:T(128)} %bitcast.me_ref, s32[8,4,16]{2,1,0:T(4,128)S(1)} %bitcast.25, bf16[192,512]{1,0:T(8,128)(2,1)S(1)} %bitcast.22), custom_call_target="tpu_custom_call" | custom-call | flops 100663296 | bytes 1048576 | tf_op jit(solution)/shard_map/pallas_call | solution.py:227
  3.7 0.6 %copy-done.12 = bf16[192,128]{1,0:T(8,128)(2,1)} copy-done((bf16[192,128]{1,0:T(8,128)(2,1)}, bf16[192,128]{1,0:T(8,128)(2,1)S(1)}, u32[]{:S(2)}) %copy-start.12) | copy-done | bytes 49176
  4.4 5.2 %all-to-all-start = ((bf16[8,64,192]{2,1,0:T(8,128)(2,1)}), bf16[8,64,192]{2,1,0:T(8,128)(2,1)S(1)}, u32[]{:S(2)}, u32[]{:S(2)}) async-start(bf16[8,64,192]{2,1,0:T(8,128)(2,1)} %get-tuple-element.21), calls=%async_computation | async-start | bytes 524288 | tf_op jit(solution)/shard_map/all_to_all | solution.py:225
  9.5 1.6 %collective-permute-start = (bf16[192,128]{1,0:T(8,128)(2,1)}, bf16[192,128]{1,0:T(8,128)(2,1)}, u32[]{:S(2)}, u32[]{:S(2)}) collective-permute-start(bf16[192,128]{1,0:T(8,128)(2,1)} %get-tuple-element.18), channel_id=1, source_target_pairs={{0,8},{8,16},{16,24},{24,0},{1,9},{9,17},{17,25},{25,1},{2,10},{10... | collective-permute-start | bytes 147464 | tf_op jit(solution)/shard_map/ppermute | solution.py:220
  11.1 2.6 %collective-permute-start.1 = (bf16[192,128]{1,0:T(8,128)(2,1)}, bf16[192,128]{1,0:T(8,128)(2,1)}, u32[]{:S(2)}, u32[]{:S(2)}) collective-permute-start(bf16[192,128]{1,0:T(8,128)(2,1)} %get-tuple-element.19), channel_id=1, source_target_pairs={{0,16},{8,24},{16,0},{24,8},{1,17},{9,25},{17,1},{25,9},{2,18},{10... | collective-permute-start | bytes 147464 | tf_op jit(solution)/shard_map/ppermute | solution.py:220
  13.7 1.3 %collective-permute-start.2 = (bf16[192,128]{1,0:T(8,128)(2,1)}, bf16[192,128]{1,0:T(8,128)(2,1)}, u32[]{:S(2)}, u32[]{:S(2)}) collective-permute-start(bf16[192,128]{1,0:T(8,128)(2,1)} %get-tuple-element.20), channel_id=1, source_target_pairs={{0,24},{8,0},{16,8},{24,16},{1,25},{9,1},{17,9},{25,17},{2,26},{10... | collective-permute-start | bytes 147464 | tf_op jit(solution)/shard_map/ppermute | solution.py:220
  15.0 1.0 %copy-done.2 = bf16[1,12,128,128]{3,2,1,0:T(8,128)(2,1)S(1)} copy-done((bf16[1,12,128,128]{3,2,1,0:T(8,128)(2,1)S(1)}, bf16[1,12,128,128]{3,2,1,0:T(8,128)(2,1)}, u32[]{:S(2)}) %copy-start.2) | copy-done | bytes 393240
  16.0 0.9 %copy-done.9 = bf16[1,512,192]{1,2,0:T(8,128)(2,1)S(1)} copy-done((bf16[1,512,192]{1,2,0:T(8,128)(2,1)S(1)}, bf16[1,512,192]{1,2,0:T(8,128)(2,1)}, u32[]{:S(2)}) %copy-start.9) | copy-done | bytes 196632
  17.0 0.7 %copy-done.14 = s32[1,8,4,16]{3,2,1,0:T(4,128)S(1)} copy-done((s32[1,8,4,16]{3,2,1,0:T(4,128)S(1)}, s32[1,8,4,16]{3,2,1,0:T(4,128)}, u32[]{:S(2)}) %copy-start.14) | copy-done | bytes 2072
  17.7 0.7 %copy-done.17 = bf16[1,8,4,16]{3,2,1,0:T(4,128)(2,1)S(1)} copy-done((bf16[1,8,4,16]{3,2,1,0:T(4,128)(2,1)S(1)}, bf16[1,8,4,16]{3,2,1,0:T(4,128)(2,1)}, u32[]{:S(2)}) %copy-start.17) | copy-done | bytes 1048
  18.4 0.7 %copy-done.18 = s32[1,8,4]{1,2,0:T(4,128)S(1)} copy-done((s32[1,8,4]{1,2,0:T(4,128)S(1)}, s32[1,8,4]{1,2,0:T(4,128)}, u32[]{:S(2)}) %copy-start.18) | copy-done | bytes 152
  19.1 0.7 %copy-done.19 = s32[1,12,2]{1,2,0:T(2,128)S(1)} copy-done((s32[1,12,2]{1,2,0:T(2,128)S(1)}, s32[1,12,2]{1,2,0:T(2,128)}, u32[]{:S(2)}) %copy-start.19) | copy-done | bytes 120
  19.7 4.1 %shard_map.124 = (f32[4,192,128]{2,1,0:T(8,128)S(1)}, bf16[4,8,16,128]{3,2,1,0:T(8,128)(2,1)S(1)}, f32[4,8,128]{2,1,0:T(8,128)S(1)}, bf16[4,128,128]{2,1,0:T(8,128)(2,1)S(1)}) custom-call(s32[1]{0:T(128)} %bitcast.me_ref, s32[2,12]{1,0:T(2,128)S(1)} %bitcast.29, s32[4,8]{1,0:T(4,128)S(1)} %bitcast.28, bf16[192,512]{1,0:T(8,128)(2,1)S(1)} %bitcast.23, ...), custom_call_target="tpu_custom_call" | custom-call | flops 100663296 | bytes 1048576 | tf_op jit(solution)/shard_map/pallas_call | solution.py:237
  23.9 0.7 %copy-done.3 = f32[4,192,128]{2,1,0:T(8,128)} copy-done((f32[4,192,128]{2,1,0:T(8,128)}, f32[4,192,128]{2,1,0:T(8,128)S(1)}, u32[]{:S(2)}) %copy-start.3) | copy-done | bytes 393240
  24.6 0.7 %copy-done.10 = bf16[4,128,128]{2,1,0:T(8,128)(2,1)} copy-done((bf16[4,128,128]{2,1,0:T(8,128)(2,1)}, bf16[4,128,128]{2,1,0:T(8,128)(2,1)S(1)}, u32[]{:S(2)}) %copy-start.10) | copy-done | bytes 131096
  25.3 0.0 all-to-all-done.incoming_ref
  25.3 1.1 %copy-done.4 = f32[4,192,128]{2,1,0:T(8,128)S(1)} copy-done((f32[4,192,128]{2,1,0:T(8,128)S(1)}, f32[4,192,128]{2,1,0:T(8,128)}, u32[]{:S(2)}) %copy-start.4) | copy-done | bytes 393240
  26.4 0.2 shard_map.125
  26.7 0.7 %collective-permute-start.3 = (bf16[192,128]{1,0:T(8,128)(2,1)S(1)}, bf16[192,128]{1,0:T(8,128)(2,1)S(1)}, u32[]{:S(2)}, u32[]{:S(2)}) collective-permute-start(bf16[192,128]{1,0:T(8,128)(2,1)S(1)} %get-tuple-element.26), channel_id=1, source_target_pairs={{0,8},{8,16},{16,24},{24,0},{1,9},{9,17},{17,25},{25,1},{2,10},{10... | collective-permute-start | bytes 147464 | tf_op jit(solution)/shard_map/ppermute | solution.py:220
  27.4 0.3 collective-permute-start.4
  27.7 0.0 collective-permute-done.rest_1_
  27.7 2.8 %collective-permute-start.5 = (bf16[192,128]{1,0:T(8,128)(2,1)S(1)}, bf16[192,128]{1,0:T(8,128)(2,1)S(1)}, u32[]{:S(2)}, u32[]{:S(2)}) collective-permute-start(bf16[192,128]{1,0:T(8,128)(2,1)S(1)} %get-tuple-element.28), channel_id=1, source_target_pairs={{0,24},{8,0},{16,8},{24,16},{1,25},{9,1},{17,9},{25,17},{2,26},{10... | collective-permute-start | bytes 147464 | tf_op jit(solution)/shard_map/ppermute | solution.py:220
  30.5 0.0 collective-permute-done.1.rest_2_
  30.6 0.8 %copy-done.13 = bf16[192,128]{1,0:T(8,128)(2,1)S(1)} copy-done((bf16[192,128]{1,0:T(8,128)(2,1)S(1)}, bf16[192,128]{1,0:T(8,128)(2,1)}, u32[]{:S(2)}) %copy-start.13) | copy-done | bytes 49176
  31.3 1.3 %shard_map.123.own_ref = f32[128,1024]{1,0:T(8,128)S(1)} custom-call(s32[1]{0:T(128)} %bitcast.me_ref, bf16[768,1024]{1,0:T(8,128)(2,1)S(1)} %copy-done, bf16[192,128]{1,0:T(8,128)(2,1)S(1)} %copy-done.13, bf16[192,128]{1,0:T(8,128)(2,1)} %collective-permute-done.rest_1_, bf16[192,128]{1,0:T(8,128)(2,1)} %collective-permute-done.1.rest_2_, ...), custom_call_target="tpu_custom_call" | custom-call | flops 201326592 | bytes 2097152 | tf_op jit(solution)/shard_map/pallas_call | solution.py:267
  32.7 0.0 copy-start.16
  32.7 0.0 copy-start.5
  32.7 0.2 collective-permute-done.3.rest_1_
  32.9 0.7 %collective-permute-done.4.rest_2_ = bf16[192,128]{1,0:T(8,128)(2,1)S(1)} collective-permute-done((bf16[192,128]{1,0:T(8,128)(2,1)S(1)}, bf16[192,128]{1,0:T(8,128)(2,1)S(1)}, u32[]{:S(2)}, u32[]{:S(2)}) %collective-permute-start.4) | collective-permute-done | bytes 49184 | tf_op jit(solution)/shard_map/ppermute | solution.py:220
  33.6 0.0 collective-permute-done.5.rest_3_
  33.7 1.2 %shard_map.126 = (bf16[128,1024]{1,0:T(8,128)(2,1)}, bf16[153,128]{1,0:T(8,128)(2,1)S(1)}) custom-call(s32[1]{0:T(128)} %bitcast.me_ref, bf16[768,1024]{1,0:T(8,128)(2,1)S(1)} %copy-done.1, bf16[153,1024]{1,0:T(8,128)(2,1)S(1)} %bitcast.20, f32[128,1024]{1,0:T(8,128)S(1)} %shard_map.123.own_ref, bf16[192,128]{1,0:T(8,128)(2,1)S(1)} %get-tuple-element.25.rest_0_, ...), custom_call_target="tpu_custom_call" | custom-call | flops 201326592 | bytes 2097152 | tf_op jit(solution)/shard_map/pallas_call | solution.py:275
  34.9 2.7 %collective-permute-start.8 = (bf16[153,128]{1,0:T(8,128)(2,1)S(1)}, bf16[153,128]{1,0:T(8,128)(2,1)S(1)}, u32[]{:S(2)}, u32[]{:S(2)}) collective-permute-start(bf16[153,128]{1,0:T(8,128)(2,1)S(1)} %get-tuple-element.31.rest_0_), channel_id=1, source_target_pairs={{0,24},{8,0},{16,8},{24,16},{1,25},{9,1},{17,9},{25,17},{2,26},{10... | collective-permute-start | bytes 117512 | tf_op jit(solution)/shard_map/ppermute | solution.py:220
  37.6 0.2 collective-permute-start.7
  37.9 0.3 collective-permute-start.6
  38.2 1.1 %collective-permute-done.8.rest_3_ = bf16[153,128]{1,0:T(8,128)(2,1)S(1)} collective-permute-done((bf16[153,128]{1,0:T(8,128)(2,1)S(1)}, bf16[153,128]{1,0:T(8,128)(2,1)S(1)}, u32[]{:S(2)}, u32[]{:S(2)}) %collective-permute-start.8) | collective-permute-done | bytes 39200 | tf_op jit(solution)/shard_map/ppermute | solution.py:220
  39.3 3.2 %collective-permute-done.7.rest_2_ = bf16[153,128]{1,0:T(8,128)(2,1)S(1)} collective-permute-done((bf16[153,128]{1,0:T(8,128)(2,1)S(1)}, bf16[153,128]{1,0:T(8,128)(2,1)S(1)}, u32[]{:S(2)}, u32[]{:S(2)}) %collective-permute-start.7) | collective-permute-done | bytes 39200 | tf_op jit(solution)/shard_map/ppermute | solution.py:220
  42.5 1.1 %collective-permute-done.6.rest_1_ = bf16[153,128]{1,0:T(8,128)(2,1)S(1)} collective-permute-done((bf16[153,128]{1,0:T(8,128)(2,1)S(1)}, bf16[153,128]{1,0:T(8,128)(2,1)S(1)}, u32[]{:S(2)}, u32[]{:S(2)}) %collective-permute-start.6) | collective-permute-done | bytes 39200 | tf_op jit(solution)/shard_map/ppermute | solution.py:220
  43.7 1.0 %shard_map.129 = bf16[8,16,153]{2,1,0:T(8,128)(2,1)} custom-call(s32[1]{0:T(128)} %bitcast.me_ref, s32[8,4,16]{2,1,0:T(4,128)S(1)} %bitcast.26, bf16[153,128]{1,0:T(8,128)(2,1)S(1)} %get-tuple-element.31.rest_0_, bf16[153,128]{1,0:T(8,128)(2,1)S(1)} %collective-permute-done.6.rest_1_, bf16[153,128]{1,0:T(8,128)(2,1)S(1)} %collective-permute-done.7.rest_2_, ...), custom_call_target="tpu_custom_call" | custom-call | flops 20054016 | bytes 524288 | tf_op jit(solution)/shard_map/pallas_call | solution.py:284
  44.7 4.2 %all-to-all-start.1 = ((bf16[8,16,153]{2,1,0:T(8,128)(2,1)}), bf16[8,16,153]{2,1,0:T(8,128)(2,1)S(1)}, u32[]{:S(2)}, u32[]{:S(2)}) async-start(bf16[8,16,153]{2,1,0:T(8,128)(2,1)} %shard_map.129), calls=%async_computation.1 | async-start | bytes 131072 | tf_op jit(solution)/shard_map/all_to_all | solution.py:225
  48.9 0.0 copy-start.7
  48.9 0.9 %copy-done.7 = bf16[128,1024]{1,0:T(8,128)(2,1)S(1)} copy-done((bf16[128,1024]{1,0:T(8,128)(2,1)S(1)}, bf16[128,1024]{1,0:T(8,128)(2,1)}, u32[]{:S(2)}) %copy-start.7) | copy-done | bytes 262168
  49.8 0.2 shard_map.127.own_ref
  50.1 0.2 shard_map.128.near_ref
  50.3 3.6 %all-to-all-done.1.incoming_ref = bf16[8,16,153]{2,1,0:T(8,128)(2,1)S(1)} async-done(((bf16[8,16,153]{2,1,0:T(8,128)(2,1)}), bf16[8,16,153]{2,1,0:T(8,128)(2,1)S(1)}, u32[]{:S(2)}, u32[]{:S(2)}) %all-to-all-start.1) | async-done | bytes 39200 | tf_op jit(solution)/shard_map/all_to_all | solution.py:225
  53.9 0.9 %shard_map.130 = f32[153,1,128]{2,1,0:T(1,128)} custom-call(s32[1]{0:T(128)} %bitcast.me_ref, f32[153,128]{1,0:T(8,128)S(1)} %shard_map.127.own_ref, f32[153,128]{1,0:T(8,128)S(1)} %shard_map.128.near_ref, bf16[4,8,16,128]{3,2,1,0:T(8,128)(2,1)S(1)} %get-tuple-element.23.edges_ref, f32[4,8,128]{2,1,0:T(8,128)S(1)} %get-tuple-element.24.degree_ref, ...), custom_call_target="tpu_custom_call" | custom-call | flops 5013504 | bytes 524288 | tf_op jit(solution)/shard_map/pallas_call | solution.py:309
  (23 shorter events, 0.0 us)
Async XLA Ops:
  0.6 29.9 %copy-start = (bf16[768,1024]{1,0:T(8,128)(2,1)S(1)}, bf16[768,1024]{1,0:T(8,128)(2,1)}, u32[]{:S(2)}) copy-start(bf16[768,1024]{1,0:T(8,128)(2,1)} %weight_ref.2) | copy-start | bytes 4718596
  0.6 1.0 %copy-start.8 = (bf16[1,512,192]{1,2,0:T(8,128)(2,1)S(1)}, bf16[1,512,192]{1,2,0:T(8,128)(2,1)}, u32[]{:S(2)}) copy-start(bf16[1,512,192]{1,2,0:T(8,128)(2,1)} %param.11) | copy-start | bytes 589828
  1.7 0.7 %copy-start.15 = (s32[1,8,4,16]{3,2,1,0:T(4,128)S(1)}, s32[1,8,4,16]{3,2,1,0:T(4,128)}, u32[]{:S(2)}) copy-start(s32[1,8,4,16]{3,2,1,0:T(4,128)} %param.14) | copy-start | bytes 6148
  3.7 0.6 %copy-start.12 = (bf16[192,128]{1,0:T(8,128)(2,1)}, bf16[192,128]{1,0:T(8,128)(2,1)S(1)}, u32[]{:S(2)}) copy-start(bf16[192,128]{1,0:T(8,128)(2,1)S(1)} %get-tuple-element.17.rest_0_) | copy-start | bytes 147460
  4.4 20.9 %all-to-all-start = ((bf16[8,64,192]{2,1,0:T(8,128)(2,1)}), bf16[8,64,192]{2,1,0:T(8,128)(2,1)S(1)}, u32[]{:S(2)}, u32[]{:S(2)}) async-start(bf16[8,64,192]{2,1,0:T(8,128)(2,1)} %get-tuple-element.21), calls=%async_computation | async-start | bytes 524288 | tf_op jit(solution)/shard_map/all_to_all | solution.py:225
  9.5 18.2 %collective-permute-start = (bf16[192,128]{1,0:T(8,128)(2,1)}, bf16[192,128]{1,0:T(8,128)(2,1)}, u32[]{:S(2)}, u32[]{:S(2)}) collective-permute-start(bf16[192,128]{1,0:T(8,128)(2,1)} %get-tuple-element.18), channel_id=1, source_target_pairs={{0,8},{8,16},{16,24},{24,0},{1,9},{9,17},{17,25},{25,1},{2,10},{10... | collective-permute-start | bytes 147464 | tf_op jit(solution)/shard_map/ppermute | solution.py:220
  11.1 19.4 %collective-permute-start.1 = (bf16[192,128]{1,0:T(8,128)(2,1)}, bf16[192,128]{1,0:T(8,128)(2,1)}, u32[]{:S(2)}, u32[]{:S(2)}) collective-permute-start(bf16[192,128]{1,0:T(8,128)(2,1)} %get-tuple-element.19), channel_id=1, source_target_pairs={{0,16},{8,24},{16,0},{24,8},{1,17},{9,25},{17,1},{25,9},{2,18},{10... | collective-permute-start | bytes 147464 | tf_op jit(solution)/shard_map/ppermute | solution.py:220
  13.7 16.8 %collective-permute-start.2 = (bf16[192,128]{1,0:T(8,128)(2,1)}, bf16[192,128]{1,0:T(8,128)(2,1)}, u32[]{:S(2)}, u32[]{:S(2)}) collective-permute-start(bf16[192,128]{1,0:T(8,128)(2,1)} %get-tuple-element.20), channel_id=1, source_target_pairs={{0,24},{8,0},{16,8},{24,16},{1,25},{9,1},{17,9},{25,17},{2,26},{10... | collective-permute-start | bytes 147464 | tf_op jit(solution)/shard_map/ppermute | solution.py:220
  15.0 1.0 %copy-start.2 = (bf16[1,12,128,128]{3,2,1,0:T(8,128)(2,1)S(1)}, bf16[1,12,128,128]{3,2,1,0:T(8,128)(2,1)}, u32[]{:S(2)}) copy-start(bf16[1,12,128,128]{3,2,1,0:T(8,128)(2,1)} %param.12) | copy-start | bytes 1179652
  16.0 0.9 %copy-start.9 = (bf16[1,512,192]{1,2,0:T(8,128)(2,1)S(1)}, bf16[1,512,192]{1,2,0:T(8,128)(2,1)}, u32[]{:S(2)}) copy-start(bf16[1,512,192]{1,2,0:T(8,128)(2,1)} %param.11) | copy-start | bytes 589828
  17.0 0.7 %copy-start.14 = (s32[1,8,4,16]{3,2,1,0:T(4,128)S(1)}, s32[1,8,4,16]{3,2,1,0:T(4,128)}, u32[]{:S(2)}) copy-start(s32[1,8,4,16]{3,2,1,0:T(4,128)} %param.15) | copy-start | bytes 6148
  17.7 0.7 %copy-start.17 = (bf16[1,8,4,16]{3,2,1,0:T(4,128)(2,1)S(1)}, bf16[1,8,4,16]{3,2,1,0:T(4,128)(2,1)}, u32[]{:S(2)}) copy-start(bf16[1,8,4,16]{3,2,1,0:T(4,128)(2,1)} %param.17) | copy-start | bytes 3076
  18.4 0.7 %copy-start.18 = (s32[1,8,4]{1,2,0:T(4,128)S(1)}, s32[1,8,4]{1,2,0:T(4,128)}, u32[]{:S(2)}) copy-start(s32[1,8,4]{1,2,0:T(4,128)} %param.16) | copy-start | bytes 388
  19.1 0.7 %copy-start.19 = (s32[1,12,2]{1,2,0:T(2,128)S(1)}, s32[1,12,2]{1,2,0:T(2,128)}, u32[]{:S(2)}) copy-start(s32[1,12,2]{1,2,0:T(2,128)} %param.13) | copy-start | bytes 292
  23.9 0.7 %copy-start.3 = (f32[4,192,128]{2,1,0:T(8,128)}, f32[4,192,128]{2,1,0:T(8,128)S(1)}, u32[]{:S(2)}) copy-start(f32[4,192,128]{2,1,0:T(8,128)S(1)} %get-tuple-element.22.sums_ref) | copy-start | bytes 1179652
  24.6 0.7 %copy-start.10 = (bf16[4,128,128]{2,1,0:T(8,128)(2,1)}, bf16[4,128,128]{2,1,0:T(8,128)(2,1)S(1)}, u32[]{:S(2)}) copy-start(bf16[4,128,128]{2,1,0:T(8,128)(2,1)S(1)} %get-tuple-element.30.band_ref) | copy-start | bytes 393220
  25.3 8.4 %copy-start.1 = (bf16[768,1024]{1,0:T(8,128)(2,1)S(1)}, bf16[768,1024]{1,0:T(8,128)(2,1)}, u32[]{:S(2)}) copy-start(bf16[768,1024]{1,0:T(8,128)(2,1)} %weight_ref.3) | copy-start | bytes 4718596
  25.3 1.1 %copy-start.4 = (f32[4,192,128]{2,1,0:T(8,128)S(1)}, f32[4,192,128]{2,1,0:T(8,128)}, u32[]{:S(2)}) copy-start(f32[4,192,128]{2,1,0:T(8,128)} %copy-done.3) | copy-start | bytes 1179652
  26.4 7.2 %copy-start.6 = (bf16[1024,153]{0,1:T(8,128)(2,1)S(1)}, bf16[1024,153]{0,1:T(8,128)(2,1)}, u32[]{:S(2)}) copy-start(bf16[1024,153]{0,1:T(8,128)(2,1)} %param.21) | copy-start | bytes 940036
  26.7 6.2 %collective-permute-start.3 = (bf16[192,128]{1,0:T(8,128)(2,1)S(1)}, bf16[192,128]{1,0:T(8,128)(2,1)S(1)}, u32[]{:S(2)}, u32[]{:S(2)}) collective-permute-start(bf16[192,128]{1,0:T(8,128)(2,1)S(1)} %get-tuple-element.26), channel_id=1, source_target_pairs={{0,8},{8,16},{16,24},{24,0},{1,9},{9,17},{17,25},{25,1},{2,10},{10... | collective-permute-start | bytes 147464 | tf_op jit(solution)/shard_map/ppermute | solution.py:220
  27.4 6.3 %collective-permute-start.4 = (bf16[192,128]{1,0:T(8,128)(2,1)S(1)}, bf16[192,128]{1,0:T(8,128)(2,1)S(1)}, u32[]{:S(2)}, u32[]{:S(2)}) collective-permute-start(bf16[192,128]{1,0:T(8,128)(2,1)S(1)} %get-tuple-element.27), channel_id=1, source_target_pairs={{0,16},{8,24},{16,0},{24,8},{1,17},{9,25},{17,1},{25,9},{2,18},{10... | collective-permute-start | bytes 147464 | tf_op jit(solution)/shard_map/ppermute | solution.py:220
  27.7 5.9 %collective-permute-start.5 = (bf16[192,128]{1,0:T(8,128)(2,1)S(1)}, bf16[192,128]{1,0:T(8,128)(2,1)S(1)}, u32[]{:S(2)}, u32[]{:S(2)}) collective-permute-start(bf16[192,128]{1,0:T(8,128)(2,1)S(1)} %get-tuple-element.28), channel_id=1, source_target_pairs={{0,24},{8,0},{16,8},{24,16},{1,25},{9,1},{17,9},{25,17},{2,26},{10... | collective-permute-start | bytes 147464 | tf_op jit(solution)/shard_map/ppermute | solution.py:220
  30.5 0.8 %copy-start.13 = (bf16[192,128]{1,0:T(8,128)(2,1)S(1)}, bf16[192,128]{1,0:T(8,128)(2,1)}, u32[]{:S(2)}) copy-start(bf16[192,128]{1,0:T(8,128)(2,1)} %copy-done.12) | copy-start | bytes 147460
  32.7 11.0 %copy-start.16 = (s32[1,8,4,16]{3,2,1,0:T(4,128)S(1)}, s32[1,8,4,16]{3,2,1,0:T(4,128)}, u32[]{:S(2)}) copy-start(s32[1,8,4,16]{3,2,1,0:T(4,128)} %param.14) | copy-start | bytes 6148
  32.7 16.2 %copy-start.5 = (bf16[1024,153]{0,1:T(8,128)(2,1)S(1)}, bf16[1024,153]{0,1:T(8,128)(2,1)}, u32[]{:S(2)}) copy-start(bf16[1024,153]{0,1:T(8,128)(2,1)} %param.20) | copy-start | bytes 940036
  33.7 16.4 %copy-start.11 = (bf16[4,128,128]{2,1,0:T(8,128)(2,1)S(1)}, bf16[4,128,128]{2,1,0:T(8,128)(2,1)}, u32[]{:S(2)}) copy-start(bf16[4,128,128]{2,1,0:T(8,128)(2,1)} %copy-done.10) | copy-start | bytes 393220
  34.9 4.4 %collective-permute-start.8 = (bf16[153,128]{1,0:T(8,128)(2,1)S(1)}, bf16[153,128]{1,0:T(8,128)(2,1)S(1)}, u32[]{:S(2)}, u32[]{:S(2)}) collective-permute-start(bf16[153,128]{1,0:T(8,128)(2,1)S(1)} %get-tuple-element.31.rest_0_), channel_id=1, source_target_pairs={{0,24},{8,0},{16,8},{24,16},{1,25},{9,1},{17,9},{25,17},{2,26},{10... | collective-permute-start | bytes 117512 | tf_op jit(solution)/shard_map/ppermute | solution.py:220
  37.6 4.9 %collective-permute-start.7 = (bf16[153,128]{1,0:T(8,128)(2,1)S(1)}, bf16[153,128]{1,0:T(8,128)(2,1)S(1)}, u32[]{:S(2)}, u32[]{:S(2)}) collective-permute-start(bf16[153,128]{1,0:T(8,128)(2,1)S(1)} %get-tuple-element.31.rest_0_), channel_id=1, source_target_pairs={{0,16},{8,24},{16,0},{24,8},{1,17},{9,25},{17,1},{25,9},{2,18},{10... | collective-permute-start | bytes 117512 | tf_op jit(solution)/shard_map/ppermute | solution.py:220
  37.9 5.8 %collective-permute-start.6 = (bf16[153,128]{1,0:T(8,128)(2,1)S(1)}, bf16[153,128]{1,0:T(8,128)(2,1)S(1)}, u32[]{:S(2)}, u32[]{:S(2)}) collective-permute-start(bf16[153,128]{1,0:T(8,128)(2,1)S(1)} %get-tuple-element.31.rest_0_), channel_id=1, source_target_pairs={{0,8},{8,16},{16,24},{24,0},{1,9},{9,17},{17,25},{25,1},{2,10},{10... | collective-permute-start | bytes 117512 | tf_op jit(solution)/shard_map/ppermute | solution.py:220
  44.7 9.2 %all-to-all-start.1 = ((bf16[8,16,153]{2,1,0:T(8,128)(2,1)}), bf16[8,16,153]{2,1,0:T(8,128)(2,1)S(1)}, u32[]{:S(2)}, u32[]{:S(2)}) async-start(bf16[8,16,153]{2,1,0:T(8,128)(2,1)} %shard_map.129), calls=%async_computation.1 | async-start | bytes 131072 | tf_op jit(solution)/shard_map/all_to_all | solution.py:225
  48.9 1.0 %copy-start.7 = (bf16[128,1024]{1,0:T(8,128)(2,1)S(1)}, bf16[128,1024]{1,0:T(8,128)(2,1)}, u32[]{:S(2)}) copy-start(bf16[128,1024]{1,0:T(8,128)(2,1)} %get-tuple-element.29.hidden_ref) | copy-start | bytes 786436

commit v3 on v2

v3 whole, which is shorter than its diff:
```python
import functools

import jax
import jax.numpy as jnp
from jax import lax
from jax.experimental import pallas as pl
from jax.experimental.pallas import tpu as pltpu
from jax.sharding import PartitionSpec as P

f32 = jnp.float32
bf16 = jnp.bfloat16
VM = pl.BlockSpec(memory_space=pltpu.VMEM)
SM = pl.BlockSpec(memory_space=pltpu.SMEM)
HB = pl.BlockSpec(memory_space=pltpu.HBM)
LAST = (((1,), (1,)), ((), ()))
FIRST = (((0,), (0,)), ((), ()))
EXTRA = 16


def call(kernel, out_shape, in_specs, scratch=(), flops=0, size=0, limit=4, out_specs=None):
    run = pl.pallas_call(
        kernel,
        out_shape=out_shape,
        in_specs=in_specs,
        out_specs=out_specs or jax.tree.map(lambda _: VM, out_shape),
        scratch_shapes=list(scratch),
        cost_estimate=pl.CostEstimate(flops=flops, bytes_accessed=size, transcendentals=0),
        compiler_params=pltpu.CompilerParams(vmem_limit_bytes=limit << 20),
    )

    def placed(*operands):
        return run(
            *(
                pltpu.with_memory_space_constraint(value, pltpu.HBM) if spec is HB else value
                for value, spec in zip(operands, in_specs)
            )
        )

    return placed


def dot(left, right, dims):
    return lax.dot_general(left, right, dims, preferred_element_type=f32)


def send_to(me, groups, k):
    return me ^ k if groups & (groups - 1) == 0 else (me + k) % groups


def ahead(me, groups, k):
    return me ^ k if groups & (groups - 1) == 0 else lax.rem(me + k, groups)


def behind(me, groups, k):
    return me ^ k if groups & (groups - 1) == 0 else lax.rem(me + groups - k, groups)


def fetch(sems, *pairs):
    copies = [pltpu.make_async_copy(a, b, sems.at[i]) for i, (a, b) in enumerate(pairs)]
    for copy in copies:
        copy.start()
    return copies


def columns_of(values):
    return values.reshape(-1, values.shape[-1]).T


def gather_kernel(chunk, me_ref, sources_hbm, features_hbm, out_ref, *rest):
    blocks, (sources_ref, features_ref, hits, sems) = rest[:-4], rest[-4:]
    parts, groups, slots = sources_ref.shape
    nodes = hits.shape[1]
    rows = nodes // groups
    for copy in fetch(sems, (sources_hbm, sources_ref), (features_hbm, features_ref)):
        copy.wait()
    lane = lax.broadcasted_iota(jnp.int32, (slots, nodes), 1)

    def step(i, _):
        columns = columns_of(sources_ref[pl.ds(i * chunk, chunk)])
        for n in range(chunk * groups):
            hits[n * slots : (n + 1) * slots, :] = jnp.where(
                columns[:, n : n + 1] == lane, 1.0, 0.0
            ).astype(bf16)
        picked = dot(hits[...], features_ref[...], LAST).astype(bf16)
        out_ref[pl.ds(i * chunk, chunk)] = picked.reshape(chunk, groups * slots, -1)
        return 0

    if parts == chunk:
        step(0, 0)
    else:
        lax.fori_loop(0, parts // chunk, step, 0)
    for k in range(1, groups):
        group = ahead(me_ref[0], groups, k)
        blocks[k - 1][...] = features_ref[:, pl.ds(pl.multiple_of(group * rows, rows), rows)]


def local_kernel(
    chunk,
    me_ref,
    ids_hbm,
    counts_hbm,
    features_hbm,
    tiles_hbm,
    targets_hbm,
    weight_hbm,
    sources_hbm,
    sums_ref,
    edges_ref,
    band_ref,
    hits_ref,
    ids_ref,
    counts_ref,
    features_ref,
    tiles_ref,
    targets_ref,
    weight_ref,
    sources_ref,
    bands,
    sems,
):
    me = me_ref[0]
    parts, groups, slots = targets_ref.shape
    rows = tiles_ref.shape[1]
    width = features_hbm.shape[0]
    copies = fetch(
        sems,
        (ids_hbm, ids_ref),
        (counts_hbm, counts_ref),
        (features_hbm, features_ref.at[pl.ds(0, width), :]),
        (tiles_hbm, tiles_ref),
        (targets_hbm, targets_ref),
        (weight_hbm, weight_ref),
        (sources_hbm, sources_ref),
    )
    extra = features_ref.shape[0] - width
    features_ref[width:, :] = jnp.ones((extra, features_ref.shape[1]), bf16)
    bands[...] = jnp.zeros_like(bands)
    for copy in copies:
        copy.wait()

    def place(t, _):
        at = pl.multiple_of(ids_ref[1, t] * rows, rows)
        bands[ids_ref[0, t], :, pl.ds(at, rows)] = tiles_ref[t]
        return 0

    lax.fori_loop(0, tiles_ref.shape[0], place, 0, unroll=tiles_ref.shape[0] <= 16)
    for g in range(groups):
        sums_ref[g] = dot(features_ref[...], bands[g], LAST)
    band_ref[...] = bands[me]
    lane = lax.broadcasted_iota(jnp.int32, (slots, rows), 1)
    slot = lax.broadcasted_iota(jnp.int32, (slots, rows), 0)

    def connect(i, _):
        first = i * chunk
        target = columns_of(targets_ref[pl.ds(first, chunk)])
        weight = columns_of(weight_ref[pl.ds(first, chunk)].astype(f32))
        for g in range(groups):
            degree = jnp.zeros((1, rows), f32)
            for e in range(chunk):
                n = e * groups + g
                hit = (target[:, n : n + 1] == lane) & (slot < counts_ref[g, first + e])
                values = jnp.where(hit, weight[:, n : n + 1], 0.0)
                edges_ref[g, first + e] = values.astype(bf16)
                degree = degree + jnp.sum(values, axis=0, keepdims=True)
            sums_ref[g, width : width + 1, :] += degree
        return 0

    if parts == chunk:
        connect(0, 0)
    else:
        lax.fori_loop(0, parts // chunk, connect, 0)
    mine = lax.broadcasted_iota(jnp.int32, sources_ref.shape, 1) == me
    picks = jnp.sum(jnp.where(mine, sources_ref[...], 0), axis=1).T
    lane = lax.broadcasted_iota(jnp.int32, (slots, hits_ref.shape[1]), 1)
    for e in range(parts):
        hits_ref[e * slots : (e + 1) * slots, :] = jnp.where(
            picks[:, e : e + 1] == lane, 1.0, 0.0
        ).astype(bf16)


def mean_kernel(me_ref, incoming_ref, sums_ref, edges_ref, *outs):
    groups, parts, slots, rows = edges_ref.shape
    width = incoming_ref.shape[2]
    for k in range(groups):
        group = ahead(me_ref[0], groups, k)
        arrived = incoming_ref[:, pl.ds(pl.multiple_of(group * slots, slots), slots), :]
        arrived = arrived.reshape(parts * slots, width)
        total = sums_ref[group, :width, :] + dot(
            arrived, edges_ref[group].reshape(parts * slots, rows), FIRST
        )
        outs[k][...] = (total / sums_ref[group, width : width + 1, :]).astype(bf16)


def self_kernel(me_ref, features_hbm, weight_ref, *rest):
    parts, (out_ref, own_ref, sem) = rest[:-3], rest[-3:]
    groups, (width, rows) = len(parts) + 1, own_ref.shape
    me = me_ref[0]
    own = pltpu.make_async_copy(
        features_hbm.at[:, pl.ds(pl.multiple_of(me * rows, rows), rows)], own_ref, sem
    )
    own.start()
    total = jnp.zeros(out_ref.shape, f32)
    for k in range(1, groups):
        span = pl.ds(pl.multiple_of(behind(me, groups, k) * width, width), width)
        total = total + dot(parts[k - 1][...], weight_ref[span, :], FIRST)
    own.wait()
    span = pl.ds(pl.multiple_of(me * width, width), width)
    out_ref[...] = total + dot(own_ref[...], weight_ref[span, :], FIRST)


def hidden_kernel(me_ref, weight_ref, out_weight_ref, own_ref, *rest):
    parts, hidden_ref, projected_ref = rest[:-2], rest[-2], rest[-1]
    width = parts[0].shape[0]
    total = own_ref[...]
    for k in range(len(parts)):
        source = behind(me_ref[0], len(parts), k)
        span = pl.ds(pl.multiple_of(source * width, width), width)
        total = total + dot(parts[k][...], weight_ref[span, :], FIRST)
    hidden = jnp.maximum(total, 0.0).astype(bf16)
    hidden_ref[...] = hidden
    projected_ref[...] = dot(out_weight_ref[...], hidden, LAST).astype(bf16)


def own_kernel(hidden_ref, weight_ref, out_ref, hidden_out, sem):
    copy = pltpu.make_async_copy(hidden_ref, hidden_out, sem)
    copy.start()
    out_ref[...] = dot(weight_ref[...], hidden_ref[...], LAST)
    copy.wait()


def pick_kernel(me_ref, hits_ref, *rest):
    projected, out_ref = rest[:-1], rest[-1]
    groups, rows = len(projected), projected[0].shape[1]
    total = None
    for k in range(groups):
        at = pl.multiple_of(behind(me_ref[0], groups, k) * rows, rows)
        term = dot(hits_ref[:, pl.ds(at, rows)], projected[k][...], LAST)
        total = term if total is None else total + term
    out_ref[...] = total.astype(bf16).reshape(out_ref.shape)


def near_kernel(me_ref, band_ref, *rest):
    projected, out_ref = rest[:-1], rest[-1]
    groups, rows = len(projected), projected[0].shape[1]
    total = None
    for k in range(groups):
        at = pl.multiple_of(behind(me_ref[0], groups, k) * rows, rows)
        term = dot(projected[k][...], band_ref[:, pl.ds(at, rows)], LAST)
        total = term if total is None else total + term
    out_ref[...] = total


def last_kernel(me_ref, own_ref, near_ref, edges_ref, sums_ref, incoming_ref, out_ref):
    groups, parts, slots, rows = edges_ref.shape
    me, width = me_ref[0], sums_ref.shape[1] - EXTRA
    arrived = incoming_ref[...].reshape(parts * slots, -1)
    far = dot(arrived, edges_ref[me].reshape(parts * slots, rows), FIRST)
    total = own_ref[...] + (near_ref[...] + far) / sums_ref[me, width : width + 1, :]
    out_ref[...] = total.reshape(out_ref.shape)


def on_device(
    features,
    tiles,
    tile_ids,
    sources,
    targets,
    counts,
    edge_weight,
    self_one,
    neigh_one,
    self_out,
    neigh_out,
):
    feature_rows, tile_contents = features[0].T, tiles[0]
    groups, parts = lax.axis_size("feat"), lax.axis_size("dom")
    me = lax.axis_index("feat").astype(jnp.int32).reshape(1)
    width, nodes = feature_rows.shape
    rows, slots = nodes // groups, sources.shape[3]
    hid, classes = self_one.shape[1], self_out.shape[1]
    chunk = max(1, min(parts, 512 // (groups * slots)))

    def shape(*dims, dtype=bf16):
        return jax.ShapeDtypeStruct(dims, dtype)

    def shift(blocks):
        return [
            lax.ppermute(
                block, "feat", [(i, send_to(i, groups, k)) for i in range(groups)]
            )
            for k, block in enumerate(blocks, 1)
        ]

    def swap(value):
        return lax.all_to_all(value, "dom", split_axis=0, concat_axis=0, tiled=True)

    sent, *feature_blocks = call(
        functools.partial(gather_kernel, chunk),
        (shape(parts, groups * slots, width),) + (shape(width, rows),) * (groups - 1),
        [SM, HB, HB],
        [
            pltpu.VMEM((parts, groups, slots), jnp.int32),
            pltpu.VMEM((width, nodes), bf16),
            pltpu.VMEM((chunk * groups * slots, nodes), bf16),
            pltpu.SemaphoreType.DMA((2,)),
        ],
        2 * nodes * nodes * width,
        1 << 20,
    )(me, sources[0], feature_rows)
    incoming = swap(sent)
    feature_blocks = shift(feature_blocks)
    sums, edges, band, hits = call(
        functools.partial(local_kernel, chunk),
        (
            shape(groups, width + EXTRA, rows, dtype=f32),
            shape(groups, parts, slots, rows),
            shape(rows, nodes),
            shape(parts * slots, nodes),
        ),
        [SM] + [HB] * 7,
        [
            pltpu.SMEM(tile_ids.shape[:0:-1], jnp.int32),
            pltpu.SMEM(counts.shape[:0:-1], jnp.int32),
            pltpu.VMEM((width + EXTRA, nodes), bf16),
            pltpu.VMEM(tile_contents.shape, bf16),
            pltpu.VMEM((parts, groups, slots), jnp.int32),
            pltpu.VMEM((parts, groups, slots), bf16),
            pltpu.VMEM((parts, groups, slots), jnp.int32),
            pltpu.VMEM((groups, rows, nodes), bf16),
            pltpu.SemaphoreType.DMA((7,)),
        ],
        2 * nodes * nodes * width,
        1 << 20,
        4 if groups <= 4 else 16,
    )(
        me,
        tile_ids[0].T,
        counts[0].T,
        feature_rows,
        tile_contents,
        targets[0],
        edge_weight[0],
        sources[0],
    )
    own_mean, *means = call(
        mean_kernel,
        (shape(width, rows),) * groups,
        [SM, VM, VM, VM],
        (),
        2 * nodes * parts * slots * width,
        1 << 20,
    )(me, incoming, sums, edges)
    means = shift(means)
    own = call(
        self_kernel,
        shape(rows, hid, dtype=f32),
        [SM, HB] + [VM] * groups,
        [pltpu.VMEM((width, rows), bf16), pltpu.SemaphoreType.DMA],
        2 * rows * hid * groups * width,
        2 << 20,
    )(me, feature_rows, self_one, *feature_blocks)
    hidden, projected = call(
        hidden_kernel,
        (shape(rows, hid), shape(classes, rows)),
        [SM] + [VM] * (3 + groups),
        (),
        2 * rows * hid * groups * width,
        2 << 20,
    )(me, neigh_one, neigh_out.T, own, own_mean, *means)
    projected = [projected] + shift([projected] * (groups - 1))
    sent = call(
        pick_kernel,
        shape(parts, slots, classes),
        [SM] + [VM] * (1 + groups),
        (),
        2 * parts * slots * nodes * classes,
        1 << 19,
    )(me, hits, *projected)
    incoming = swap(sent)
    own, hidden = call(
        own_kernel,
        (shape(classes, rows, dtype=f32), shape(rows, hid)),
        [VM, VM],
        [pltpu.SemaphoreType.DMA],
        2 * rows * hid * classes,
        1 << 20,
        out_specs=(VM, HB),
    )(hidden, self_out.T)
    near = call(
        near_kernel,
        shape(classes, rows, dtype=f32),
        [SM] + [VM] * (1 + groups),
        (),
        2 * rows * nodes * classes,
        1 << 19,
    )(me, band, *projected)
    logits = call(
        last_kernel,
        shape(classes, 1, rows, dtype=f32),
        [SM] + [VM] * 5,
        (),
        2 * rows * parts * slots * classes,
        1 << 19,
    )(me, own, near, edges, sums, incoming)
    return hidden[None], logits.transpose(1, 0, 2)


def solution(mesh):
    placed = (
        P("dom", None, "feat"),
        P("dom", None, None, None),
        P("dom", None, None),
        P("dom", None, None, None),
        P("dom", None, None, None),
        P("dom", None, None),
        P("dom", None, None, None),
        P(),
        P(),
        P(),
        P(),
    )
    return jax.shard_map(
        on_device,
        mesh=mesh,
        in_specs=placed,
        out_specs=(P("dom", "feat", None), P("dom", None, "feat")),
        check_vma=False,
    )
```

time: 55.5 us -> 43.1 us (0.78)
  local copies, waits for them, and re-layouts: 11.3 us -> 0.02 us
  Pallas kernels: 10.5 us -> 8.69 us
  waiting for transfers between devices: 10 us -> 11.4 us
    unnamed x40 -> x8, local copies, waits for them, and re-layouts: 11.3 us -> 0.02 us
    pallas_call x9, Pallas kernels: 10.5 us -> 8.69 us  [placed(): run(*(pltpu.with_memory_space_constraint(value, pltpu.HBM) if spec is HB...]
    all_to_all x2, waiting for transfers between devices: 3.58 us -> 4.95 us  [swap(): return lax.all_to_all(value, 'dom', split_axis=0, concat_axis=0, tiled=True)]
    all_to_all x2, starting transfers between devices: 9.38 us -> 8.55 us  [swap(): return lax.all_to_all(value, 'dom', split_axis=0, concat_axis=0, tiled=True)]
    ppermute x9, starting transfers between devices: 12.7 us -> 13.3 us  [shift(): lax.ppermute(block, 'feat', [(i, send_to(i, groups, k)) for i in range(gr...]
  transfers between devices with their start and end apart: 11 -> 11, of which waited for: 6 -> 6; matrix products, arithmetic and copies ran while one was open for 0% -> 0% of each run, Pallas kernels for 11% -> 9%
where the time goes in v3:
time: 43.1 us; the launch traced here: 42.7 us
  starting transfers between devices  21.8 us (51%)
  waiting for transfers between devices  11.4 us (26%)
  Pallas kernels  8.69 us (20%)
  between operations  0.73 us (2%)
    ppermute x9, starting transfers between devices, shift(): lax.ppermute(block, 'feat', [(i, send_to(i, groups, k)) for i in range(gr...  13.3 us
    pallas_call x9, Pallas kernels, placed(): run(*(pltpu.with_memory_space_constraint(value, pltpu.HBM) if spec is HB...  8.69 us
    all_to_all x2, starting transfers between devices, swap(): return lax.all_to_all(value, 'dom', split_axis=0, concat_axis=0, tiled=True)  8.55 us
    ppermute x9, waiting for transfers between devices, shift(): lax.ppermute(block, 'feat', [(i, send_to(i, groups, k)) for i in range(gr...  6.44 us
    all_to_all x2, waiting for transfers between devices, swap(): return lax.all_to_all(value, 'dom', split_axis=0, concat_axis=0, tiled=True)  4.95 us
  transfers between devices with their start and end apart: 11, of which 6 were waited for; matrix products, arithmetic and copies ran while one was open for 0% of the time, Pallas kernels for 9%

profile of v3, /device:TPU:0, one launch (start us, length us, event | category | flops | bytes accessed | tf_op | source)
XLA Modules:
  0.0 42.7 jit_solution(9449973917755763192)
XLA Ops:
  0.6 0.0 copy-start.1
  0.6 2.2 %shard_map.122 = (bf16[8,64,192]{2,1,0:T(8,128)(2,1)}, bf16[192,128]{1,0:T(8,128)(2,1)S(1)}, bf16[192,128]{1,0:T(8,128)(2,1)S(1)}, bf16[192,128]{1,0:T(8,128)(2,1)S(1)}) custom-call(s32[1]{0:T(128)} %bitcast.me_ref, s32[8,4,16]{2,1,0:T(4,128)} %bitcast.25, bf16[192,512]{1,0:T(8,128)(2,1)} %bitcast.20), custom_call_target="tpu_custom_call" | custom-call | flops 100663296 | bytes 1048576 | tf_op jit(solution)/shard_map/pallas_call | solution.py:32
  2.9 5.2 %all-to-all-start = ((bf16[8,64,192]{2,1,0:T(8,128)(2,1)}), bf16[8,64,192]{2,1,0:T(8,128)(2,1)S(1)}, u32[]{:S(2)}, u32[]{:S(2)}) async-start(bf16[8,64,192]{2,1,0:T(8,128)(2,1)} %get-tuple-element.21), calls=%async_computation | async-start | bytes 524288 | tf_op jit(solution)/shard_map/all_to_all | solution.py:295
  8.1 1.6 %collective-permute-start = (bf16[192,128]{1,0:T(8,128)(2,1)S(1)}, bf16[192,128]{1,0:T(8,128)(2,1)S(1)}, u32[]{:S(2)}, u32[]{:S(2)}) collective-permute-start(bf16[192,128]{1,0:T(8,128)(2,1)S(1)} %get-tuple-element.18), channel_id=1, source_target_pairs={{0,8},{8,0},{16,24},{24,16},{1,9},{9,1},{17,25},{25,17},{2,10},{10... | collective-permute-start | bytes 147464 | tf_op jit(solution)/shard_map/ppermute | solution.py:288
  9.6 2.6 %collective-permute-start.1 = (bf16[192,128]{1,0:T(8,128)(2,1)S(1)}, bf16[192,128]{1,0:T(8,128)(2,1)S(1)}, u32[]{:S(2)}, u32[]{:S(2)}) collective-permute-start(bf16[192,128]{1,0:T(8,128)(2,1)S(1)} %get-tuple-element.19), channel_id=1, source_target_pairs={{0,16},{8,24},{16,0},{24,8},{1,17},{9,25},{17,1},{25,9},{2,18},{10... | collective-permute-start | bytes 147464 | tf_op jit(solution)/shard_map/ppermute | solution.py:288
  12.2 0.2 collective-permute-start.2
  12.4 1.6 %shard_map.124 = (f32[4,208,128]{2,1,0:T(8,128)S(1)}, bf16[4,8,16,128]{3,2,1,0:T(8,128)(2,1)S(1)}, bf16[128,512]{1,0:T(8,128)(2,1)S(1)}, bf16[128,512]{1,0:T(8,128)(2,1)S(1)}) custom-call(s32[1]{0:T(128)} %bitcast.me_ref, s32[2,12]{1,0:T(2,128)} %bitcast.30, s32[4,8]{1,0:T(4,128)} %bitcast.29, bf16[192,512]{1,0:T(8,128)(2,1)} %bitcast.21, ...), custom_call_target="tpu_custom_call" | custom-call | flops 100663296 | bytes 1048576 | tf_op jit(solution)/shard_map/pallas_call | solution.py:32
  14.1 0.9 %all-to-all-done.incoming_ref = bf16[8,64,192]{2,1,0:T(8,128)(2,1)S(1)} async-done(((bf16[8,64,192]{2,1,0:T(8,128)(2,1)}), bf16[8,64,192]{2,1,0:T(8,128)(2,1)S(1)}, u32[]{:S(2)}, u32[]{:S(2)}) %all-to-all-start) | async-done | bytes 196640 | tf_op jit(solution)/shard_map/all_to_all | solution.py:295
  15.0 0.0 copy-start
  15.0 0.0 copy-start.3
  15.0 0.2 shard_map.125
  15.2 1.6 %collective-permute-start.3 = (bf16[192,128]{1,0:T(8,128)(2,1)S(1)}, bf16[192,128]{1,0:T(8,128)(2,1)S(1)}, u32[]{:S(2)}, u32[]{:S(2)}) collective-permute-start(bf16[192,128]{1,0:T(8,128)(2,1)S(1)} %get-tuple-element.25), channel_id=1, source_target_pairs={{0,8},{8,0},{16,24},{24,16},{1,9},{9,1},{17,25},{25,17},{2,10},{10... | collective-permute-start | bytes 147464 | tf_op jit(solution)/shard_map/ppermute | solution.py:288
  16.9 2.6 %collective-permute-start.4 = (bf16[192,128]{1,0:T(8,128)(2,1)S(1)}, bf16[192,128]{1,0:T(8,128)(2,1)S(1)}, u32[]{:S(2)}, u32[]{:S(2)}) collective-permute-start(bf16[192,128]{1,0:T(8,128)(2,1)S(1)} %get-tuple-element.26), channel_id=1, source_target_pairs={{0,16},{8,24},{16,0},{24,8},{1,17},{9,25},{17,1},{25,9},{2,18},{10... | collective-permute-start | bytes 147464 | tf_op jit(solution)/shard_map/ppermute | solution.py:288
  19.5 0.0 collective-permute-done.rest_0_
  19.5 0.2 collective-permute-start.5
  19.7 0.0 collective-permute-done.1.rest_1_
  19.7 0.0 collective-permute-done.2.rest_2_
  19.7 0.0 copy-done.1
  19.7 1.2 %shard_map.123.own_ref = f32[128,1024]{1,0:T(8,128)S(1)} custom-call(s32[1]{0:T(128)} %bitcast.me_ref, bf16[192,512]{1,0:T(8,128)(2,1)} %bitcast.22, bf16[768,1024]{1,0:T(8,128)(2,1)S(1)} %copy-done.1, bf16[192,128]{1,0:T(8,128)(2,1)S(1)} %collective-permute-done.rest_0_, bf16[192,128]{1,0:T(8,128)(2,1)S(1)} %collective-permute-done.1.rest_1_, ...), custom_call_target="tpu_custom_call" | custom-call | flops 201326592 | bytes 2097152 | tf_op jit(solution)/shard_map/pallas_call | solution.py:32
  20.9 0.0 copy-start.2
  21.0 0.0 collective-permute-done.3.rest_1_
  21.0 1.4 %collective-permute-done.4.rest_2_ = bf16[192,128]{1,0:T(8,128)(2,1)S(1)} collective-permute-done((bf16[192,128]{1,0:T(8,128)(2,1)S(1)}, bf16[192,128]{1,0:T(8,128)(2,1)S(1)}, u32[]{:S(2)}, u32[]{:S(2)}) %collective-permute-start.4) | collective-permute-done | bytes 49184 | tf_op jit(solution)/shard_map/ppermute | solution.py:288
  22.4 3.0 %collective-permute-done.5.rest_3_ = bf16[192,128]{1,0:T(8,128)(2,1)S(1)} collective-permute-done((bf16[192,128]{1,0:T(8,128)(2,1)S(1)}, bf16[192,128]{1,0:T(8,128)(2,1)S(1)}, u32[]{:S(2)}, u32[]{:S(2)}) %collective-permute-start.5) | collective-permute-done | bytes 49184 | tf_op jit(solution)/shard_map/ppermute | solution.py:288
  25.4 0.0 copy-done
  25.4 0.0 copy-done.3
  25.4 0.7 %shard_map.126 = (bf16[128,1024]{1,0:T(8,128)(2,1)S(1)}, bf16[153,128]{1,0:T(8,128)(2,1)S(1)}) custom-call(s32[1]{0:T(128)} %bitcast.me_ref, bf16[768,1024]{1,0:T(8,128)(2,1)S(1)} %copy-done, bf16[153,1024]{1,0:T(8,128)(2,1)S(1)} %bitcast.19, f32[128,1024]{1,0:T(8,128)S(1)} %shard_map.123.own_ref, bf16[192,128]{1,0:T(8,128)(2,1)S(1)} %get-tuple-element.24.rest_0_, ...), custom_call_target="tpu_custom_call" | custom-call | flops 201326592 | bytes 2097152 | tf_op jit(solution)/shard_map/pallas_call | solution.py:32
  26.1 0.7 %collective-permute-start.8 = (bf16[153,128]{1,0:T(8,128)(2,1)S(1)}, bf16[153,128]{1,0:T(8,128)(2,1)S(1)}, u32[]{:S(2)}, u32[]{:S(2)}) collective-permute-start(bf16[153,128]{1,0:T(8,128)(2,1)S(1)} %get-tuple-element.32.rest_0_), channel_id=1, source_target_pairs={{0,24},{8,16},{16,8},{24,0},{1,25},{9,17},{17,9},{25,1},{2,26},{10... | collective-permute-start | bytes 117512 | tf_op jit(solution)/shard_map/ppermute | solution.py:288
  26.7 0.0 collective-permute-start.7
  26.7 3.8 %collective-permute-start.6 = (bf16[153,128]{1,0:T(8,128)(2,1)S(1)}, bf16[153,128]{1,0:T(8,128)(2,1)S(1)}, u32[]{:S(2)}, u32[]{:S(2)}) collective-permute-start(bf16[153,128]{1,0:T(8,128)(2,1)S(1)} %get-tuple-element.32.rest_0_), channel_id=1, source_target_pairs={{0,8},{8,0},{16,24},{24,16},{1,9},{9,1},{17,25},{25,17},{2,10},{10... | collective-permute-start | bytes 117512 | tf_op jit(solution)/shard_map/ppermute | solution.py:288
  30.5 1.5 %collective-permute-done.8.rest_3_ = bf16[153,128]{1,0:T(8,128)(2,1)S(1)} collective-permute-done((bf16[153,128]{1,0:T(8,128)(2,1)S(1)}, bf16[153,128]{1,0:T(8,128)(2,1)S(1)}, u32[]{:S(2)}, u32[]{:S(2)}) %collective-permute-start.8) | collective-permute-done | bytes 39200 | tf_op jit(solution)/shard_map/ppermute | solution.py:288
  32.0 0.5 %collective-permute-done.7.rest_2_ = bf16[153,128]{1,0:T(8,128)(2,1)S(1)} collective-permute-done((bf16[153,128]{1,0:T(8,128)(2,1)S(1)}, bf16[153,128]{1,0:T(8,128)(2,1)S(1)}, u32[]{:S(2)}, u32[]{:S(2)}) %collective-permute-start.7) | collective-permute-done | bytes 39200 | tf_op jit(solution)/shard_map/ppermute | solution.py:288
  32.5 0.0 collective-permute-done.6.rest_1_
  32.5 0.9 %shard_map.129 = bf16[8,16,153]{2,1,0:T(8,128)(2,1)} custom-call(s32[1]{0:T(128)} %bitcast.me_ref, bf16[128,512]{1,0:T(8,128)(2,1)S(1)} %get-tuple-element.33.hits_ref, bf16[153,128]{1,0:T(8,128)(2,1)S(1)} %get-tuple-element.32.rest_0_, bf16[153,128]{1,0:T(8,128)(2,1)S(1)} %collective-permute-done.6.rest_1_, ...), custom_call_target="tpu_custom_call" | custom-call | flops 20054016 | bytes 524288 | tf_op jit(solution)/shard_map/pallas_call | solution.py:32
  33.4 3.4 %all-to-all-start.1 = ((bf16[8,16,153]{2,1,0:T(8,128)(2,1)}), bf16[8,16,153]{2,1,0:T(8,128)(2,1)S(1)}, u32[]{:S(2)}, u32[]{:S(2)}) async-start(bf16[8,16,153]{2,1,0:T(8,128)(2,1)} %shard_map.129), calls=%async_computation.1 | async-start | bytes 131072 | tf_op jit(solution)/shard_map/all_to_all | solution.py:295
  36.8 0.0 copy-done.2
  36.8 0.7 %shard_map.127 = (f32[153,128]{1,0:T(8,128)S(1)}, bf16[128,1024]{1,0:T(8,128)(2,1)}) custom-call(bf16[128,1024]{1,0:T(8,128)(2,1)S(1)} %get-tuple-element.28.hidden_ref, bf16[153,1024]{1,0:T(8,128)(2,1)S(1)} %bitcast.18), custom_call_target="tpu_custom_call" | custom-call | flops 40108032 | bytes 1048576 | tf_op jit(solution)/shard_map/pallas_call | solution.py:32
  37.5 0.2 shard_map.128.near_ref
  37.7 4.1 %all-to-all-done.1.incoming_ref = bf16[8,16,153]{2,1,0:T(8,128)(2,1)S(1)} async-done(((bf16[8,16,153]{2,1,0:T(8,128)(2,1)}), bf16[8,16,153]{2,1,0:T(8,128)(2,1)S(1)}, u32[]{:S(2)}, u32[]{:S(2)}) %all-to-all-start.1) | async-done | bytes 39200 | tf_op jit(solution)/shard_map/all_to_all | solution.py:295
  41.8 0.9 %shard_map.130 = f32[153,1,128]{2,1,0:T(1,128)} custom-call(s32[1]{0:T(128)} %bitcast.me_ref, f32[153,128]{1,0:T(8,128)S(1)} %get-tuple-element.30.own_ref, f32[153,128]{1,0:T(8,128)S(1)} %shard_map.128.near_ref, bf16[4,8,16,128]{3,2,1,0:T(8,128)(2,1)S(1)} %get-tuple-element.23.edges_ref, f32[4,208,128]{2,1,0:T(8,128)S(1)} %get-tuple-element.22.sums_ref, ...), custom_call_target="tpu_custom_call" | custom-call | flops 5013504 | bytes 524288 | tf_op jit(solution)/shard_map/pallas_call | solution.py:32
Async XLA Ops:
  0.6 19.1 %copy-start.1 = (bf16[768,1024]{1,0:T(8,128)(2,1)S(1)}, bf16[768,1024]{1,0:T(8,128)(2,1)}, u32[]{:S(2)}) copy-start(bf16[768,1024]{1,0:T(8,128)(2,1)} %weight_ref.2) | copy-start | bytes 4718596
  2.9 12.1 %all-to-all-start = ((bf16[8,64,192]{2,1,0:T(8,128)(2,1)}), bf16[8,64,192]{2,1,0:T(8,128)(2,1)S(1)}, u32[]{:S(2)}, u32[]{:S(2)}) async-start(bf16[8,64,192]{2,1,0:T(8,128)(2,1)} %get-tuple-element.21), calls=%async_computation | async-start | bytes 524288 | tf_op jit(solution)/shard_map/all_to_all | solution.py:295
  8.1 11.4 %collective-permute-start = (bf16[192,128]{1,0:T(8,128)(2,1)S(1)}, bf16[192,128]{1,0:T(8,128)(2,1)S(1)}, u32[]{:S(2)}, u32[]{:S(2)}) collective-permute-start(bf16[192,128]{1,0:T(8,128)(2,1)S(1)} %get-tuple-element.18), channel_id=1, source_target_pairs={{0,8},{8,0},{16,24},{24,16},{1,9},{9,1},{17,25},{25,17},{2,10},{10... | collective-permute-start | bytes 147464 | tf_op jit(solution)/shard_map/ppermute | solution.py:288
  9.6 10.1 %collective-permute-start.1 = (bf16[192,128]{1,0:T(8,128)(2,1)S(1)}, bf16[192,128]{1,0:T(8,128)(2,1)S(1)}, u32[]{:S(2)}, u32[]{:S(2)}) collective-permute-start(bf16[192,128]{1,0:T(8,128)(2,1)S(1)} %get-tuple-element.19), channel_id=1, source_target_pairs={{0,16},{8,24},{16,0},{24,8},{1,17},{9,25},{17,1},{25,9},{2,18},{10... | collective-permute-start | bytes 147464 | tf_op jit(solution)/shard_map/ppermute | solution.py:288
  12.2 7.5 %collective-permute-start.2 = (bf16[192,128]{1,0:T(8,128)(2,1)S(1)}, bf16[192,128]{1,0:T(8,128)(2,1)S(1)}, u32[]{:S(2)}, u32[]{:S(2)}) collective-permute-start(bf16[192,128]{1,0:T(8,128)(2,1)S(1)} %get-tuple-element.20), channel_id=1, source_target_pairs={{0,24},{8,16},{16,8},{24,0},{1,25},{9,17},{17,9},{25,1},{2,26},{10... | collective-permute-start | bytes 147464 | tf_op jit(solution)/shard_map/ppermute | solution.py:288
  15.0 10.4 %copy-start = (bf16[768,1024]{1,0:T(8,128)(2,1)S(1)}, bf16[768,1024]{1,0:T(8,128)(2,1)}, u32[]{:S(2)}) copy-start(bf16[768,1024]{1,0:T(8,128)(2,1)} %weight_ref.3) | copy-start | bytes 4718596
  15.0 10.4 %copy-start.3 = (bf16[1024,153]{0,1:T(8,128)(2,1)S(1)}, bf16[1024,153]{0,1:T(8,128)(2,1)}, u32[]{:S(2)}) copy-start(bf16[1024,153]{0,1:T(8,128)(2,1)} %param.21) | copy-start | bytes 940036
  15.2 5.7 %collective-permute-start.3 = (bf16[192,128]{1,0:T(8,128)(2,1)S(1)}, bf16[192,128]{1,0:T(8,128)(2,1)S(1)}, u32[]{:S(2)}, u32[]{:S(2)}) collective-permute-start(bf16[192,128]{1,0:T(8,128)(2,1)S(1)} %get-tuple-element.25), channel_id=1, source_target_pairs={{0,8},{8,0},{16,24},{24,16},{1,9},{9,1},{17,25},{25,17},{2,10},{10... | collective-permute-start | bytes 147464 | tf_op jit(solution)/shard_map/ppermute | solution.py:288
  16.9 5.5 %collective-permute-start.4 = (bf16[192,128]{1,0:T(8,128)(2,1)S(1)}, bf16[192,128]{1,0:T(8,128)(2,1)S(1)}, u32[]{:S(2)}, u32[]{:S(2)}) collective-permute-start(bf16[192,128]{1,0:T(8,128)(2,1)S(1)} %get-tuple-element.26), channel_id=1, source_target_pairs={{0,16},{8,24},{16,0},{24,8},{1,17},{9,25},{17,1},{25,9},{2,18},{10... | collective-permute-start | bytes 147464 | tf_op jit(solution)/shard_map/ppermute | solution.py:288
  19.5 5.9 %collective-permute-start.5 = (bf16[192,128]{1,0:T(8,128)(2,1)S(1)}, bf16[192,128]{1,0:T(8,128)(2,1)S(1)}, u32[]{:S(2)}, u32[]{:S(2)}) collective-permute-start(bf16[192,128]{1,0:T(8,128)(2,1)S(1)} %get-tuple-element.27), channel_id=1, source_target_pairs={{0,24},{8,16},{16,8},{24,0},{1,25},{9,17},{17,9},{25,1},{2,26},{10... | collective-permute-start | bytes 147464 | tf_op jit(solution)/shard_map/ppermute | solution.py:288
  20.9 15.9 %copy-start.2 = (bf16[1024,153]{0,1:T(8,128)(2,1)S(1)}, bf16[1024,153]{0,1:T(8,128)(2,1)}, u32[]{:S(2)}) copy-start(bf16[1024,153]{0,1:T(8,128)(2,1)} %param.20) | copy-start | bytes 940036
  26.1 6.0 %collective-permute-start.8 = (bf16[153,128]{1,0:T(8,128)(2,1)S(1)}, bf16[153,128]{1,0:T(8,128)(2,1)S(1)}, u32[]{:S(2)}, u32[]{:S(2)}) collective-permute-start(bf16[153,128]{1,0:T(8,128)(2,1)S(1)} %get-tuple-element.32.rest_0_), channel_id=1, source_target_pairs={{0,24},{8,16},{16,8},{24,0},{1,25},{9,17},{17,9},{25,1},{2,26},{10... | collective-permute-start | bytes 117512 | tf_op jit(solution)/shard_map/ppermute | solution.py:288
  26.7 5.8 %collective-permute-start.7 = (bf16[153,128]{1,0:T(8,128)(2,1)S(1)}, bf16[153,128]{1,0:T(8,128)(2,1)S(1)}, u32[]{:S(2)}, u32[]{:S(2)}) collective-permute-start(bf16[153,128]{1,0:T(8,128)(2,1)S(1)} %get-tuple-element.32.rest_0_), channel_id=1, source_target_pairs={{0,16},{8,24},{16,0},{24,8},{1,17},{9,25},{17,1},{25,9},{2,18},{10... | collective-permute-start | bytes 117512 | tf_op jit(solution)/shard_map/ppermute | solution.py:288
  26.7 5.8 %collective-permute-start.6 = (bf16[153,128]{1,0:T(8,128)(2,1)S(1)}, bf16[153,128]{1,0:T(8,128)(2,1)S(1)}, u32[]{:S(2)}, u32[]{:S(2)}) collective-permute-start(bf16[153,128]{1,0:T(8,128)(2,1)S(1)} %get-tuple-element.32.rest_0_), channel_id=1, source_target_pairs={{0,8},{8,0},{16,24},{24,16},{1,9},{9,1},{17,25},{25,17},{2,10},{10... | collective-permute-start | bytes 117512 | tf_op jit(solution)/shard_map/ppermute | solution.py:288
  33.4 8.4 %all-to-all-start.1 = ((bf16[8,16,153]{2,1,0:T(8,128)(2,1)}), bf16[8,16,153]{2,1,0:T(8,128)(2,1)S(1)}, u32[]{:S(2)}, u32[]{:S(2)}) async-start(bf16[8,16,153]{2,1,0:T(8,128)(2,1)} %shard_map.129), calls=%async_computation.1 | async-start | bytes 131072 | tf_op jit(solution)/shard_map/all_to_all | solution.py:295

commit v4 on v3

--- a/solution.py
+++ b/solution.py
@@ -43,16 +43,18 @@
     return lax.dot_general(left, right, dims, preferred_element_type=f32)
 
 
-def send_to(me, groups, k):
-    return me ^ k if groups & (groups - 1) == 0 else (me + k) % groups
+def step_of(groups, k):
+    return sorted(range(groups), key=lambda d: (d > 0, abs(2 * d - groups - 1)))[k]
 
 
 def ahead(me, groups, k):
-    return me ^ k if groups & (groups - 1) == 0 else lax.rem(me + k, groups)
+    step = step_of(groups, k)
+    return me ^ step if groups & (groups - 1) == 0 else (me + step) % groups
 
 
 def behind(me, groups, k):
-    return me ^ k if groups & (groups - 1) == 0 else lax.rem(me + groups - k, groups)
+    step = step_of(groups, k)
+    return me ^ step if groups & (groups - 1) == 0 else (me + groups - step) % groups
 
 
 def fetch(sems, *pairs):
@@ -71,24 +73,26 @@
     parts, groups, slots = sources_ref.shape
     nodes = hits.shape[1]
     rows = nodes // groups
-    for copy in fetch(sems, (sources_hbm, sources_ref), (features_hbm, features_ref)):
-        copy.wait()
+    indices, table = fetch(sems, (sources_hbm, sources_ref), (features_hbm, features_ref))
+    indices.wait()
     lane = lax.broadcasted_iota(jnp.int32, (slots, nodes), 1)
 
-    def step(i, _):
+    def step(i, last):
         columns = columns_of(sources_ref[pl.ds(i * chunk, chunk)])
         for n in range(chunk * groups):
             hits[n * slots : (n + 1) * slots, :] = jnp.where(
                 columns[:, n : n + 1] == lane, 1.0, 0.0
             ).astype(bf16)
+        if last:
+            table.wait()
         picked = dot(hits[...], features_ref[...], LAST).astype(bf16)
         out_ref[pl.ds(i * chunk, chunk)] = picked.reshape(chunk, groups * slots, -1)
-        return 0
 
     if parts == chunk:
-        step(0, 0)
+        step(0, True)
     else:
-        lax.fori_loop(0, parts // chunk, step, 0)
+        table.wait()
+        lax.fori_loop(0, parts // chunk, lambda i, _: step(i, False), None)
     for k in range(1, groups):
         group = ahead(me_ref[0], groups, k)
         blocks[k - 1][...] = features_ref[:, pl.ds(pl.multiple_of(group * rows, rows), rows)]
@@ -209,7 +213,8 @@
 
 
 def hidden_kernel(me_ref, weight_ref, out_weight_ref, own_ref, *rest):
-    parts, hidden_ref, projected_ref = rest[:-2], rest[-2], rest[-1]
+    groups = len(rest) // 2
+    parts, hidden_ref, copies = rest[:groups], rest[groups], rest[groups + 1 :]
     width = parts[0].shape[0]
     total = own_ref[...]
     for k in range(len(parts)):
@@ -218,7 +223,9 @@
         total = total + dot(parts[k][...], weight_ref[span, :], FIRST)
     hidden = jnp.maximum(total, 0.0).astype(bf16)
     hidden_ref[...] = hidden
-    projected_ref[...] = dot(out_weight_ref[...], hidden, LAST).astype(bf16)
+    projected = dot(out_weight_ref[...], hidden, LAST).astype(bf16)
+    for copy in copies:
+        copy[...] = projected
 
 
 def own_kernel(hidden_ref, weight_ref, out_ref, hidden_out, sem):
@@ -286,7 +293,7 @@
     def shift(blocks):
         return [
             lax.ppermute(
-                block, "feat", [(i, send_to(i, groups, k)) for i in range(groups)]
+                block, "feat", [(i, ahead(i, groups, k)) for i in range(groups)]
             )
             for k, block in enumerate(blocks, 1)
         ]
@@ -359,15 +366,15 @@
         2 * rows * hid * groups * width,
         2 << 20,
     )(me, feature_rows, self_one, *feature_blocks)
-    hidden, projected = call(
+    hidden, *projected = call(
         hidden_kernel,
-        (shape(rows, hid), shape(classes, rows)),
+        (shape(rows, hid),) + (shape(classes, rows),) * groups,
         [SM] + [VM] * (3 + groups),
         (),
         2 * rows * hid * groups * width,
         2 << 20,
     )(me, neigh_one, neigh_out.T, own, own_mean, *means)
-    projected = [projected] + shift([projected] * (groups - 1))
+    projected = projected[:1] + shift(projected[1:])
     sent = call(
         pick_kernel,
         shape(parts, slots, classes),

time: 43.1 us -> 42 us (0.974)
  starting transfers between devices: 21.8 us -> 20.5 us
    ppermute x9, starting transfers between devices: 13.3 us -> 12 us  [shift(): lax.ppermute(block, 'feat', [(i, ahead(i, groups, k)) for i in range(grou...]
  transfers between devices with their start and end apart: 11 -> 11, of which waited for: 6 -> 5; matrix products, arithmetic and copies ran while one was open for 0% -> 0% of each run, Pallas kernels for 9% -> 10%
where the time goes in v4:
time: 42 us; the launch traced here: 41.6 us
  starting transfers between devices  20.5 us (49%)
  waiting for transfers between devices  11.7 us (28%)
  Pallas kernels  8.62 us (21%)
  between operations  0.75 us (2%)
    ppermute x9, starting transfers between devices, shift(): lax.ppermute(block, 'feat', [(i, ahead(i, groups, k)) for i in range(grou...  12 us
    pallas_call x9, Pallas kernels, placed(): run(*(pltpu.with_memory_space_constraint(value, pltpu.HBM) if spec is HB...  8.62 us
    all_to_all x2, starting transfers between devices, swap(): return lax.all_to_all(value, 'dom', split_axis=0, concat_axis=0, tiled=True)  8.53 us
    ppermute x9, waiting for transfers between devices, shift(): lax.ppermute(block, 'feat', [(i, ahead(i, groups, k)) for i in range(grou...  6.62 us
    all_to_all x2, waiting for transfers between devices, swap(): return lax.all_to_all(value, 'dom', split_axis=0, concat_axis=0, tiled=True)  5.09 us
  transfers between devices with their start and end apart: 11, of which 5 were waited for; matrix products, arithmetic and copies ran while one was open for 0% of the time, Pallas kernels for 10%

profile of v4, /device:TPU:0, one launch (start us, length us, event | category | flops | bytes accessed | tf_op | source)
XLA Modules:
  0.0 41.6 jit_solution(820922616076603884)
XLA Ops:
  0.6 0.0 copy-start.1
  0.6 2.2 %shard_map.122 = (bf16[8,64,192]{2,1,0:T(8,128)(2,1)}, bf16[192,128]{1,0:T(8,128)(2,1)S(1)}, bf16[192,128]{1,0:T(8,128)(2,1)S(1)}, bf16[192,128]{1,0:T(8,128)(2,1)S(1)}) custom-call(s32[1]{0:T(128)} %bitcast.me_ref, s32[8,4,16]{2,1,0:T(4,128)} %bitcast.25, bf16[192,512]{1,0:T(8,128)(2,1)} %bitcast.20), custom_call_target="tpu_custom_call" | custom-call | flops 100663296 | bytes 1048576 | tf_op jit(solution)/shard_map/pallas_call | solution.py:32
  2.8 5.2 %all-to-all-start = ((bf16[8,64,192]{2,1,0:T(8,128)(2,1)}), bf16[8,64,192]{2,1,0:T(8,128)(2,1)S(1)}, u32[]{:S(2)}, u32[]{:S(2)}) async-start(bf16[8,64,192]{2,1,0:T(8,128)(2,1)} %get-tuple-element.24), calls=%async_computation | async-start | bytes 524288 | tf_op jit(solution)/shard_map/all_to_all | solution.py:302
  8.0 2.6 %collective-permute-start = (bf16[192,128]{1,0:T(8,128)(2,1)S(1)}, bf16[192,128]{1,0:T(8,128)(2,1)S(1)}, u32[]{:S(2)}, u32[]{:S(2)}) collective-permute-start(bf16[192,128]{1,0:T(8,128)(2,1)S(1)} %get-tuple-element.21), channel_id=1, source_target_pairs={{0,16},{8,24},{16,0},{24,8},{1,17},{9,25},{17,1},{25,9},{2,18},{10... | collective-permute-start | bytes 147464 | tf_op jit(solution)/shard_map/ppermute | solution.py:295
  10.6 1.3 %collective-permute-start.1 = (bf16[192,128]{1,0:T(8,128)(2,1)S(1)}, bf16[192,128]{1,0:T(8,128)(2,1)S(1)}, u32[]{:S(2)}, u32[]{:S(2)}) collective-permute-start(bf16[192,128]{1,0:T(8,128)(2,1)S(1)} %get-tuple-element.22), channel_id=1, source_target_pairs={{0,24},{8,16},{16,8},{24,0},{1,25},{9,17},{17,9},{25,1},{2,26},{10... | collective-permute-start | bytes 147464 | tf_op jit(solution)/shard_map/ppermute | solution.py:295
  11.9 0.2 collective-permute-start.2
  12.2 1.6 %shard_map.124 = (f32[4,208,128]{2,1,0:T(8,128)S(1)}, bf16[4,8,16,128]{3,2,1,0:T(8,128)(2,1)S(1)}, bf16[128,512]{1,0:T(8,128)(2,1)S(1)}, bf16[128,512]{1,0:T(8,128)(2,1)S(1)}) custom-call(s32[1]{0:T(128)} %bitcast.me_ref, s32[2,12]{1,0:T(2,128)} %bitcast.30, s32[4,8]{1,0:T(4,128)} %bitcast.29, bf16[192,512]{1,0:T(8,128)(2,1)} %bitcast.21, ...), custom_call_target="tpu_custom_call" | custom-call | flops 100663296 | bytes 1048576 | tf_op jit(solution)/shard_map/pallas_call | solution.py:32
  13.8 1.1 %all-to-all-done.incoming_ref = bf16[8,64,192]{2,1,0:T(8,128)(2,1)S(1)} async-done(((bf16[8,64,192]{2,1,0:T(8,128)(2,1)}), bf16[8,64,192]{2,1,0:T(8,128)(2,1)S(1)}, u32[]{:S(2)}, u32[]{:S(2)}) %all-to-all-start) | async-done | bytes 196640 | tf_op jit(solution)/shard_map/all_to_all | solution.py:302
  14.9 0.0 copy-start
  14.9 0.0 copy-start.3
  14.9 0.2 shard_map.125
  15.2 2.7 %collective-permute-start.3 = (bf16[192,128]{1,0:T(8,128)(2,1)S(1)}, bf16[192,128]{1,0:T(8,128)(2,1)S(1)}, u32[]{:S(2)}, u32[]{:S(2)}) collective-permute-start(bf16[192,128]{1,0:T(8,128)(2,1)S(1)} %get-tuple-element.28), channel_id=1, source_target_pairs={{0,16},{8,24},{16,0},{24,8},{1,17},{9,25},{17,1},{25,9},{2,18},{10... | collective-permute-start | bytes 147464 | tf_op jit(solution)/shard_map/ppermute | solution.py:295
  17.8 1.3 %collective-permute-start.4 = (bf16[192,128]{1,0:T(8,128)(2,1)S(1)}, bf16[192,128]{1,0:T(8,128)(2,1)S(1)}, u32[]{:S(2)}, u32[]{:S(2)}) collective-permute-start(bf16[192,128]{1,0:T(8,128)(2,1)S(1)} %get-tuple-element.29), channel_id=1, source_target_pairs={{0,24},{8,16},{16,8},{24,0},{1,25},{9,17},{17,9},{25,1},{2,26},{10... | collective-permute-start | bytes 147464 | tf_op jit(solution)/shard_map/ppermute | solution.py:295
  19.2 0.0 collective-permute-done.rest_0_
  19.2 0.2 collective-permute-start.5
  19.4 0.0 collective-permute-done.1.rest_1_
  19.4 0.0 collective-permute-done.2.rest_2_
  19.4 0.0 copy-done.1
  19.4 1.2 %shard_map.123.own_ref = f32[128,1024]{1,0:T(8,128)S(1)} custom-call(s32[1]{0:T(128)} %bitcast.me_ref, bf16[192,512]{1,0:T(8,128)(2,1)} %bitcast.22, bf16[768,1024]{1,0:T(8,128)(2,1)S(1)} %copy-done.1, bf16[192,128]{1,0:T(8,128)(2,1)S(1)} %collective-permute-done.rest_0_, bf16[192,128]{1,0:T(8,128)(2,1)S(1)} %collective-permute-done.1.rest_1_, ...), custom_call_target="tpu_custom_call" | custom-call | flops 201326592 | bytes 2097152 | tf_op jit(solution)/shard_map/pallas_call | solution.py:32
  20.7 0.0 copy-start.2
  20.7 0.0 collective-permute-done.3.rest_1_
  20.7 3.1 %collective-permute-done.4.rest_2_ = bf16[192,128]{1,0:T(8,128)(2,1)S(1)} collective-permute-done((bf16[192,128]{1,0:T(8,128)(2,1)S(1)}, bf16[192,128]{1,0:T(8,128)(2,1)S(1)}, u32[]{:S(2)}, u32[]{:S(2)}) %collective-permute-start.4) | collective-permute-done | bytes 49184 | tf_op jit(solution)/shard_map/ppermute | solution.py:295
  23.8 0.0 collective-permute-done.5.rest_3_
  23.8 0.0 copy-done
  23.8 0.0 copy-done.3
  23.8 0.7 %shard_map.126 = (bf16[128,1024]{1,0:T(8,128)(2,1)S(1)}, bf16[153,128]{1,0:T(8,128)(2,1)S(1)}, bf16[153,128]{1,0:T(8,128)(2,1)S(1)}, bf16[153,128]{1,0:T(8,128)(2,1)S(1)}, bf16[153,128]{1,0:T(8,128)(2,1)S(1)}) custom-call(s32[1]{0:T(128)} %bitcast.me_ref, bf16[768,1024]{1,0:T(8,128)(2,1)S(1)} %copy-done, bf16[153,1024]{1,0:T(8,128)(2,1)S(1)} %bitcast.19, ...), custom_call_target="tpu_custom_call" | custom-call | flops 201326592 | bytes 2097152 | tf_op jit(solution)/shard_map/pallas_call | solution.py:32
  24.5 1.2 %collective-permute-start.6 = (bf16[153,128]{1,0:T(8,128)(2,1)S(1)}, bf16[153,128]{1,0:T(8,128)(2,1)S(1)}, u32[]{:S(2)}, u32[]{:S(2)}) collective-permute-start(bf16[153,128]{1,0:T(8,128)(2,1)S(1)} %get-tuple-element.36), channel_id=1, source_target_pairs={{0,16},{8,24},{16,0},{24,8},{1,17},{9,25},{17,1},{25,9},{2,18},{10... | collective-permute-start | bytes 117512 | tf_op jit(solution)/shard_map/ppermute | solution.py:295
  25.7 1.2 %collective-permute-start.7 = (bf16[153,128]{1,0:T(8,128)(2,1)S(1)}, bf16[153,128]{1,0:T(8,128)(2,1)S(1)}, u32[]{:S(2)}, u32[]{:S(2)}) collective-permute-start(bf16[153,128]{1,0:T(8,128)(2,1)S(1)} %get-tuple-element.37), channel_id=1, source_target_pairs={{0,24},{8,16},{16,8},{24,0},{1,25},{9,17},{17,9},{25,1},{2,26},{10... | collective-permute-start | bytes 117512 | tf_op jit(solution)/shard_map/ppermute | solution.py:295
  26.9 1.1 %collective-permute-start.8 = (bf16[153,128]{1,0:T(8,128)(2,1)S(1)}, bf16[153,128]{1,0:T(8,128)(2,1)S(1)}, u32[]{:S(2)}, u32[]{:S(2)}) collective-permute-start(bf16[153,128]{1,0:T(8,128)(2,1)S(1)} %get-tuple-element.38), channel_id=1, source_target_pairs={{0,8},{8,0},{16,24},{24,16},{1,9},{9,1},{17,25},{25,17},{2,10},{10... | collective-permute-start | bytes 117512 | tf_op jit(solution)/shard_map/ppermute | solution.py:295
  28.1 1.6 %collective-permute-done.6.rest_1_ = bf16[153,128]{1,0:T(8,128)(2,1)S(1)} collective-permute-done((bf16[153,128]{1,0:T(8,128)(2,1)S(1)}, bf16[153,128]{1,0:T(8,128)(2,1)S(1)}, u32[]{:S(2)}, u32[]{:S(2)}) %collective-permute-start.6) | collective-permute-done | bytes 39200 | tf_op jit(solution)/shard_map/ppermute | solution.py:295
  29.6 1.9 %collective-permute-done.7.rest_2_ = bf16[153,128]{1,0:T(8,128)(2,1)S(1)} collective-permute-done((bf16[153,128]{1,0:T(8,128)(2,1)S(1)}, bf16[153,128]{1,0:T(8,128)(2,1)S(1)}, u32[]{:S(2)}, u32[]{:S(2)}) %collective-permute-start.7) | collective-permute-done | bytes 39200 | tf_op jit(solution)/shard_map/ppermute | solution.py:295
  31.5 0.0 collective-permute-done.8.rest_3_
  31.5 0.9 %shard_map.129 = bf16[8,16,153]{2,1,0:T(8,128)(2,1)} custom-call(s32[1]{0:T(128)} %bitcast.me_ref, bf16[128,512]{1,0:T(8,128)(2,1)S(1)} %get-tuple-element.39.hits_ref, bf16[153,128]{1,0:T(8,128)(2,1)S(1)} %get-tuple-element.35.rest_0_, bf16[153,128]{1,0:T(8,128)(2,1)S(1)} %collective-permute-done.6.rest_1_, ...), custom_call_target="tpu_custom_call" | custom-call | flops 20054016 | bytes 524288 | tf_op jit(solution)/shard_map/pallas_call | solution.py:32
  32.4 3.4 %all-to-all-start.1 = ((bf16[8,16,153]{2,1,0:T(8,128)(2,1)}), bf16[8,16,153]{2,1,0:T(8,128)(2,1)S(1)}, u32[]{:S(2)}, u32[]{:S(2)}) async-start(bf16[8,16,153]{2,1,0:T(8,128)(2,1)} %shard_map.129), calls=%async_computation.1 | async-start | bytes 131072 | tf_op jit(solution)/shard_map/all_to_all | solution.py:302
  35.8 0.0 copy-done.2
  35.8 0.7 %shard_map.127 = (f32[153,128]{1,0:T(8,128)S(1)}, bf16[128,1024]{1,0:T(8,128)(2,1)}) custom-call(bf16[128,1024]{1,0:T(8,128)(2,1)S(1)} %get-tuple-element.31.hidden_ref, bf16[153,1024]{1,0:T(8,128)(2,1)S(1)} %bitcast.18), custom_call_target="tpu_custom_call" | custom-call | flops 40108032 | bytes 1048576 | tf_op jit(solution)/shard_map/pallas_call | solution.py:32
  36.5 0.2 shard_map.128.near_ref
  36.8 4.0 %all-to-all-done.1.incoming_ref = bf16[8,16,153]{2,1,0:T(8,128)(2,1)S(1)} async-done(((bf16[8,16,153]{2,1,0:T(8,128)(2,1)}), bf16[8,16,153]{2,1,0:T(8,128)(2,1)S(1)}, u32[]{:S(2)}, u32[]{:S(2)}) %all-to-all-start.1) | async-done | bytes 39200 | tf_op jit(solution)/shard_map/all_to_all | solution.py:302
  40.7 0.9 %shard_map.130 = f32[153,1,128]{2,1,0:T(1,128)} custom-call(s32[1]{0:T(128)} %bitcast.me_ref, f32[153,128]{1,0:T(8,128)S(1)} %get-tuple-element.33.own_ref, f32[153,128]{1,0:T(8,128)S(1)} %shard_map.128.near_ref, bf16[4,8,16,128]{3,2,1,0:T(8,128)(2,1)S(1)} %get-tuple-element.26.edges_ref, f32[4,208,128]{2,1,0:T(8,128)S(1)} %get-tuple-element.25.sums_ref, ...), custom_call_target="tpu_custom_call" | custom-call | flops 5013504 | bytes 524288 | tf_op jit(solution)/shard_map/pallas_call | solution.py:32
Async XLA Ops:
  0.6 18.8 %copy-start.1 = (bf16[768,1024]{1,0:T(8,128)(2,1)S(1)}, bf16[768,1024]{1,0:T(8,128)(2,1)}, u32[]{:S(2)}) copy-start(bf16[768,1024]{1,0:T(8,128)(2,1)} %weight_ref.2) | copy-start | bytes 4718596
  2.8 12.1 %all-to-all-start = ((bf16[8,64,192]{2,1,0:T(8,128)(2,1)}), bf16[8,64,192]{2,1,0:T(8,128)(2,1)S(1)}, u32[]{:S(2)}, u32[]{:S(2)}) async-start(bf16[8,64,192]{2,1,0:T(8,128)(2,1)} %get-tuple-element.24), calls=%async_computation | async-start | bytes 524288 | tf_op jit(solution)/shard_map/all_to_all | solution.py:302
  8.0 11.2 %collective-permute-start = (bf16[192,128]{1,0:T(8,128)(2,1)S(1)}, bf16[192,128]{1,0:T(8,128)(2,1)S(1)}, u32[]{:S(2)}, u32[]{:S(2)}) collective-permute-start(bf16[192,128]{1,0:T(8,128)(2,1)S(1)} %get-tuple-element.21), channel_id=1, source_target_pairs={{0,16},{8,24},{16,0},{24,8},{1,17},{9,25},{17,1},{25,9},{2,18},{10... | collective-permute-start | bytes 147464 | tf_op jit(solution)/shard_map/ppermute | solution.py:295
  10.6 8.8 %collective-permute-start.1 = (bf16[192,128]{1,0:T(8,128)(2,1)S(1)}, bf16[192,128]{1,0:T(8,128)(2,1)S(1)}, u32[]{:S(2)}, u32[]{:S(2)}) collective-permute-start(bf16[192,128]{1,0:T(8,128)(2,1)S(1)} %get-tuple-element.22), channel_id=1, source_target_pairs={{0,24},{8,16},{16,8},{24,0},{1,25},{9,17},{17,9},{25,1},{2,26},{10... | collective-permute-start | bytes 147464 | tf_op jit(solution)/shard_map/ppermute | solution.py:295
  11.9 7.5 %collective-permute-start.2 = (bf16[192,128]{1,0:T(8,128)(2,1)S(1)}, bf16[192,128]{1,0:T(8,128)(2,1)S(1)}, u32[]{:S(2)}, u32[]{:S(2)}) collective-permute-start(bf16[192,128]{1,0:T(8,128)(2,1)S(1)} %get-tuple-element.23), channel_id=1, source_target_pairs={{0,8},{8,0},{16,24},{24,16},{1,9},{9,1},{17,25},{25,17},{2,10},{10... | collective-permute-start | bytes 147464 | tf_op jit(solution)/shard_map/ppermute | solution.py:295
  14.9 8.9 %copy-start = (bf16[768,1024]{1,0:T(8,128)(2,1)S(1)}, bf16[768,1024]{1,0:T(8,128)(2,1)}, u32[]{:S(2)}) copy-start(bf16[768,1024]{1,0:T(8,128)(2,1)} %weight_ref.3) | copy-start | bytes 4718596
  14.9 8.9 %copy-start.3 = (bf16[1024,153]{0,1:T(8,128)(2,1)S(1)}, bf16[1024,153]{0,1:T(8,128)(2,1)}, u32[]{:S(2)}) copy-start(bf16[1024,153]{0,1:T(8,128)(2,1)} %param.21) | copy-start | bytes 940036
  15.2 5.5 %collective-permute-start.3 = (bf16[192,128]{1,0:T(8,128)(2,1)S(1)}, bf16[192,128]{1,0:T(8,128)(2,1)S(1)}, u32[]{:S(2)}, u32[]{:S(2)}) collective-permute-start(bf16[192,128]{1,0:T(8,128)(2,1)S(1)} %get-tuple-element.28), channel_id=1, source_target_pairs={{0,16},{8,24},{16,0},{24,8},{1,17},{9,25},{17,1},{25,9},{2,18},{10... | collective-permute-start | bytes 147464 | tf_op jit(solution)/shard_map/ppermute | solution.py:295
  17.8 6.0 %collective-permute-start.4 = (bf16[192,128]{1,0:T(8,128)(2,1)S(1)}, bf16[192,128]{1,0:T(8,128)(2,1)S(1)}, u32[]{:S(2)}, u32[]{:S(2)}) collective-permute-start(bf16[192,128]{1,0:T(8,128)(2,1)S(1)} %get-tuple-element.29), channel_id=1, source_target_pairs={{0,24},{8,16},{16,8},{24,0},{1,25},{9,17},{17,9},{25,1},{2,26},{10... | collective-permute-start | bytes 147464 | tf_op jit(solution)/shard_map/ppermute | solution.py:295
  19.2 4.6 %collective-permute-start.5 = (bf16[192,128]{1,0:T(8,128)(2,1)S(1)}, bf16[192,128]{1,0:T(8,128)(2,1)S(1)}, u32[]{:S(2)}, u32[]{:S(2)}) collective-permute-start(bf16[192,128]{1,0:T(8,128)(2,1)S(1)} %get-tuple-element.30), channel_id=1, source_target_pairs={{0,8},{8,0},{16,24},{24,16},{1,9},{9,1},{17,25},{25,17},{2,10},{10... | collective-permute-start | bytes 147464 | tf_op jit(solution)/shard_map/ppermute | solution.py:295
  20.7 15.1 %copy-start.2 = (bf16[1024,153]{0,1:T(8,128)(2,1)S(1)}, bf16[1024,153]{0,1:T(8,128)(2,1)}, u32[]{:S(2)}) copy-start(bf16[1024,153]{0,1:T(8,128)(2,1)} %param.20) | copy-start | bytes 940036
  24.5 5.1 %collective-permute-start.6 = (bf16[153,128]{1,0:T(8,128)(2,1)S(1)}, bf16[153,128]{1,0:T(8,128)(2,1)S(1)}, u32[]{:S(2)}, u32[]{:S(2)}) collective-permute-start(bf16[153,128]{1,0:T(8,128)(2,1)S(1)} %get-tuple-element.36), channel_id=1, source_target_pairs={{0,16},{8,24},{16,0},{24,8},{1,17},{9,25},{17,1},{25,9},{2,18},{10... | collective-permute-start | bytes 117512 | tf_op jit(solution)/shard_map/ppermute | solution.py:295
  25.7 5.8 %collective-permute-start.7 = (bf16[153,128]{1,0:T(8,128)(2,1)S(1)}, bf16[153,128]{1,0:T(8,128)(2,1)S(1)}, u32[]{:S(2)}, u32[]{:S(2)}) collective-permute-start(bf16[153,128]{1,0:T(8,128)(2,1)S(1)} %get-tuple-element.37), channel_id=1, source_target_pairs={{0,24},{8,16},{16,8},{24,0},{1,25},{9,17},{17,9},{25,1},{2,26},{10... | collective-permute-start | bytes 117512 | tf_op jit(solution)/shard_map/ppermute | solution.py:295
  26.9 4.6 %collective-permute-start.8 = (bf16[153,128]{1,0:T(8,128)(2,1)S(1)}, bf16[153,128]{1,0:T(8,128)(2,1)S(1)}, u32[]{:S(2)}, u32[]{:S(2)}) collective-permute-start(bf16[153,128]{1,0:T(8,128)(2,1)S(1)} %get-tuple-element.38), channel_id=1, source_target_pairs={{0,8},{8,0},{16,24},{24,16},{1,9},{9,1},{17,25},{25,17},{2,10},{10... | collective-permute-start | bytes 117512 | tf_op jit(solution)/shard_map/ppermute | solution.py:295
  32.4 8.3 %all-to-all-start.1 = ((bf16[8,16,153]{2,1,0:T(8,128)(2,1)}), bf16[8,16,153]{2,1,0:T(8,128)(2,1)S(1)}, u32[]{:S(2)}, u32[]{:S(2)}) async-start(bf16[8,16,153]{2,1,0:T(8,128)(2,1)} %shard_map.129), calls=%async_computation.1 | async-start | bytes 131072 | tf_op jit(solution)/shard_map/all_to_all | solution.py:302

commit v5 on v4

--- a/solution.py
+++ b/solution.py
@@ -55,6 +55,14 @@
 def behind(me, groups, k):
     step = step_of(groups, k)
     return me ^ step if groups & (groups - 1) == 0 else (me + groups - step) % groups
+
+
+def step_to(a, b, count):
+    return a ^ b if count & (count - 1) == 0 else (b + count - a) % count
+
+
+def next_to(a, step, count):
+    return a ^ step if count & (count - 1) == 0 else (a + step) % count
 
 
 def fetch(sems, *pairs):
@@ -101,6 +109,7 @@
 def local_kernel(
     chunk,
     me_ref,
+    part_ref,
     ids_hbm,
     counts_hbm,
     features_hbm,
@@ -112,6 +121,7 @@
     edges_ref,
     band_ref,
     hits_ref,
+    far_ref,
     ids_ref,
     counts_ref,
     features_ref,
@@ -176,10 +186,15 @@
     mine = lax.broadcasted_iota(jnp.int32, sources_ref.shape, 1) == me
     picks = jnp.sum(jnp.where(mine, sources_ref[...], 0), axis=1).T
     lane = lax.broadcasted_iota(jnp.int32, (slots, hits_ref.shape[1]), 1)
-    for e in range(parts):
-        hits_ref[e * slots : (e + 1) * slots, :] = jnp.where(
-            picks[:, e : e + 1] == lane, 1.0, 0.0
+    chips, chip, core = parts // 2, part_ref[0] // 2, part_ref[0] % 2
+    for d in range(parts):
+        other = (d % 2) ^ core
+        to = other * chips + step_to(chip, d // 2, chips)
+        hits_ref[pl.ds(pl.multiple_of(to * slots, slots), slots), :] = jnp.where(
+            picks[:, d : d + 1] == lane, 1.0, 0.0
         ).astype(bf16)
+        at = step_to(d // 2, chip, chips) * 2 + other
+        far_ref[pl.ds(pl.multiple_of(at * slots, slots), slots), :] = edges_ref[me, d]
 
 
 def mean_kernel(me_ref, incoming_ref, sums_ref, edges_ref, *outs):
@@ -236,14 +251,23 @@
 
 
 def pick_kernel(me_ref, hits_ref, *rest):
-    projected, out_ref = rest[:-1], rest[-1]
+    projected, (mine_ref, mate_ref) = rest[:-2], rest[-2:]
     groups, rows = len(projected), projected[0].shape[1]
     total = None
     for k in range(groups):
         at = pl.multiple_of(behind(me_ref[0], groups, k) * rows, rows)
         term = dot(hits_ref[:, pl.ds(at, rows)], projected[k][...], LAST)
         total = term if total is None else total + term
-    out_ref[...] = total.astype(bf16).reshape(out_ref.shape)
+    total = total.astype(bf16)
+    half = total.shape[0] // 2
+    mine_ref[...] = total[:half].reshape(mine_ref.shape)
+    mate_ref[...] = total[half:].reshape(mate_ref.shape)
+
+
+def pair_kernel(mine_ref, got_ref, *outs):
+    for j, out in enumerate(outs):
+        out[0] = mine_ref[j]
+        out[1] = got_ref[j]
 
 
 def near_kernel(me_ref, band_ref, *rest):
@@ -257,12 +281,12 @@
     out_ref[...] = total
 
 
-def last_kernel(me_ref, own_ref, near_ref, edges_ref, sums_ref, incoming_ref, out_ref):
-    groups, parts, slots, rows = edges_ref.shape
-    me, width = me_ref[0], sums_ref.shape[1] - EXTRA
-    arrived = incoming_ref[...].reshape(parts * slots, -1)
-    far = dot(arrived, edges_ref[me].reshape(parts * slots, rows), FIRST)
-    total = own_ref[...] + (near_ref[...] + far) / sums_ref[me, width : width + 1, :]
+def last_kernel(me_ref, own_ref, near_ref, far_ref, sums_ref, *rest):
+    arrived, out_ref = rest[:-1], rest[-1]
+    width = sums_ref.shape[1] - EXTRA
+    arrived = jnp.concatenate([part[...].reshape(-1, part.shape[2]) for part in arrived], axis=0)
+    far = dot(arrived, far_ref[...], FIRST)
+    total = own_ref[...] + (near_ref[...] + far) / sums_ref[me_ref[0], width : width + 1, :]
     out_ref[...] = total.reshape(out_ref.shape)
 
 
@@ -282,6 +306,7 @@
     feature_rows, tile_contents = features[0].T, tiles[0]
     groups, parts = lax.axis_size("feat"), lax.axis_size("dom")
     me = lax.axis_index("feat").astype(jnp.int32).reshape(1)
+    part = lax.axis_index("dom").astype(jnp.int32).reshape(1)
     width, nodes = feature_rows.shape
     rows, slots = nodes // groups, sources.shape[3]
     hid, classes = self_one.shape[1], self_out.shape[1]
@@ -316,15 +341,16 @@
     )(me, sources[0], feature_rows)
     incoming = swap(sent)
     feature_blocks = shift(feature_blocks)
-    sums, edges, band, hits = call(
+    sums, edges, band, hits, far = call(
         functools.partial(local_kernel, chunk),
         (
             shape(groups, width + EXTRA, rows, dtype=f32),
             shape(groups, parts, slots, rows),
             shape(rows, nodes),
             shape(parts * slots, nodes),
+            shape(parts * slots, rows),
         ),
-        [SM] + [HB] * 7,
+        [SM, SM] + [HB] * 7,
         [
             pltpu.SMEM(tile_ids.shape[:0:-1], jnp.int32),
             pltpu.SMEM(counts.shape[:0:-1], jnp.int32),
@@ -341,6 +367,7 @@
         4 if groups <= 4 else 16,
     )(
         me,
+        part,
         tile_ids[0].T,
         counts[0].T,
         feature_rows,
@@ -375,15 +402,27 @@
         2 << 20,
     )(me, neigh_one, neigh_out.T, own, own_mean, *means)
     projected = projected[:1] + shift(projected[1:])
-    sent = call(
+    chips = parts // 2
+    mine, mate = call(
         pick_kernel,
-        shape(parts, slots, classes),
+        (shape(chips, slots, classes),) * 2,
         [SM] + [VM] * (1 + groups),
         (),
         2 * parts * slots * nodes * classes,
         1 << 19,
     )(me, hits, *projected)
-    incoming = swap(sent)
+    mate = lax.ppermute(mate, "dom", [(d, d ^ 1) for d in range(parts)])
+    arrived = call(
+        pair_kernel, (shape(2, slots, classes),) * chips, [VM, VM], (), 0, 1 << 19
+    )(mine, mate)
+    arrived = [arrived[0]] + [
+        lax.ppermute(
+            arrived[j],
+            "dom",
+            [(d, next_to(d // 2, j, chips) * 2 + d % 2) for d in range(parts)],
+        )
+        for j in range(1, chips)
+    ]
     own, hidden = call(
         own_kernel,
         (shape(classes, rows, dtype=f32), shape(rows, hid)),
@@ -404,11 +443,11 @@
     logits = call(
         last_kernel,
         shape(classes, 1, rows, dtype=f32),
-        [SM] + [VM] * 5,
+        [SM] + [VM] * (4 + chips),
         (),
         2 * rows * parts * slots * classes,
         1 << 19,
-    )(me, own, near, edges, sums, incoming)
+    )(me, own, near, far, sums, *arrived)
     return hidden[None], logits.transpose(1, 0, 2)
 
 

time: 42 us -> 41.4 us (0.986)
  Pallas kernels: 8.62 us -> 7.99 us
    all_to_all x2 -> x1, waiting for transfers between devices: 5.09 us -> 1.1 us  [swap(): return lax.all_to_all(value, 'dom', split_axis=0, concat_axis=0, tiled=True)]
    ppermute x0 -> x4, waiting for transfers between devices: none -> 3.87 us  [the longest x3 2.67 us: on_device(): lax.ppermute(arrived[j], 'dom', [(d, next_to(d // 2, j, chips) * 2 + d %...]
    ppermute x0 -> x4, starting transfers between devices: none -> 3.56 us  [the longest x3 3.49 us: on_device(): lax.ppermute(arrived[j], 'dom', [(d, next_to(d // 2, j, chips) * 2 + d %...]
    all_to_all x2 -> x1, starting transfers between devices: 8.53 us -> 5.18 us  [swap(): return lax.all_to_all(value, 'dom', split_axis=0, concat_axis=0, tiled=True)]
    pallas_call x9 -> x10, Pallas kernels: 8.62 us -> 7.99 us  [placed(): run(*(pltpu.with_memory_space_constraint(value, pltpu.HBM) if spec is HB...]
  transfers between devices with their start and end apart: 11 -> 14, of which waited for: 5 -> 7; matrix products, arithmetic and copies ran while one was open for 0% -> 0% of each run, Pallas kernels for 10% -> 10%
where the time goes in v5:
time: 41.4 us; the launch traced here: 41.1 us
  starting transfers between devices  20.7 us (50%)
  waiting for transfers between devices  11.6 us (28%)
  Pallas kernels  7.99 us (19%)
  between operations  0.76 us (2%)
    ppermute x9, starting transfers between devices, shift(): lax.ppermute(block, 'feat', [(i, ahead(i, groups, k)) for i in range(grou...  12 us
    pallas_call x10, Pallas kernels, placed(): run(*(pltpu.with_memory_space_constraint(value, pltpu.HBM) if spec is HB...  7.99 us
    ppermute x9, waiting for transfers between devices, shift(): lax.ppermute(block, 'feat', [(i, ahead(i, groups, k)) for i in range(grou...  6.62 us
    all_to_all x1, starting transfers between devices, swap(): return lax.all_to_all(value, 'dom', split_axis=0, concat_axis=0, tiled=True)  5.18 us
    ppermute x3, starting transfers between devices, on_device(): lax.ppermute(arrived[j], 'dom', [(d, next_to(d // 2, j, chips) * 2 + d %...  3.49 us
    ppermute x3, waiting for transfers between devices, on_device(): lax.ppermute(arrived[j], 'dom', [(d, next_to(d // 2, j, chips) * 2 + d %...  2.67 us
    ppermute x1, waiting for transfers between devices, on_device(): mate = lax.ppermute(mate, 'dom', [(d, d ^ 1) for d in range(parts)])  1.19 us
    all_to_all x1, waiting for transfers between devices, swap(): return lax.all_to_all(value, 'dom', split_axis=0, concat_axis=0, tiled=True)  1.1 us
  transfers between devices with their start and end apart: 14, of which 7 were waited for; matrix products, arithmetic and copies ran while one was open for 0% of the time, Pallas kernels for 10%

profile of v5, /device:TPU:0, one launch (start us, length us, event | category | flops | bytes accessed | tf_op | source)
XLA Modules:
  0.0 41.1 jit_solution(9283298462421795799)
XLA Ops:
  0.6 0.0 copy-start.1
  0.6 2.2 %shard_map.122 = (bf16[8,64,192]{2,1,0:T(8,128)(2,1)}, bf16[192,128]{1,0:T(8,128)(2,1)S(1)}, bf16[192,128]{1,0:T(8,128)(2,1)S(1)}, bf16[192,128]{1,0:T(8,128)(2,1)S(1)}) custom-call(s32[1]{0:T(128)} %bitcast.me_ref, s32[8,4,16]{2,1,0:T(4,128)} %bitcast.26, bf16[192,512]{1,0:T(8,128)(2,1)} %bitcast.21), custom_call_target="tpu_custom_call" | custom-call | flops 100663296 | bytes 1048576 | tf_op jit(solution)/shard_map/pallas_call | solution.py:32
  2.8 5.2 %all-to-all-start = ((bf16[8,64,192]{2,1,0:T(8,128)(2,1)}), bf16[8,64,192]{2,1,0:T(8,128)(2,1)S(1)}, u32[]{:S(2)}, u32[]{:S(2)}) async-start(bf16[8,64,192]{2,1,0:T(8,128)(2,1)} %get-tuple-element.31), calls=%async_computation | async-start | bytes 524288 | tf_op jit(solution)/shard_map/all_to_all | solution.py:327
  8.0 2.6 %collective-permute-start = (bf16[192,128]{1,0:T(8,128)(2,1)S(1)}, bf16[192,128]{1,0:T(8,128)(2,1)S(1)}, u32[]{:S(2)}, u32[]{:S(2)}) collective-permute-start(bf16[192,128]{1,0:T(8,128)(2,1)S(1)} %get-tuple-element.28), channel_id=1, source_target_pairs={{0,16},{8,24},{16,0},{24,8},{1,17},{9,25},{17,1},{25,9},{2,18},{10... | collective-permute-start | bytes 147464 | tf_op jit(solution)/shard_map/ppermute | solution.py:320
  10.6 1.3 %collective-permute-start.1 = (bf16[192,128]{1,0:T(8,128)(2,1)S(1)}, bf16[192,128]{1,0:T(8,128)(2,1)S(1)}, u32[]{:S(2)}, u32[]{:S(2)}) collective-permute-start(bf16[192,128]{1,0:T(8,128)(2,1)S(1)} %get-tuple-element.29), channel_id=1, source_target_pairs={{0,24},{8,16},{16,8},{24,0},{1,25},{9,17},{17,9},{25,1},{2,26},{10... | collective-permute-start | bytes 147464 | tf_op jit(solution)/shard_map/ppermute | solution.py:320
  11.9 0.2 collective-permute-start.2
  12.2 1.7 %shard_map.124 = (f32[4,208,128]{2,1,0:T(8,128)S(1)}, bf16[4,8,16,128]{3,2,1,0:T(8,128)(2,1)S(1)}, bf16[128,512]{1,0:T(8,128)(2,1)S(1)}, bf16[128,512]{1,0:T(8,128)(2,1)S(1)}, bf16[128,128]{1,0:T(8,128)(2,1)S(1)}) custom-call(s32[1]{0:T(128)} %bitcast.me_ref, s32[1]{0:T(128)} %bitcast.6.part_ref, s32[2,12]{1,0:T(2,128)} %bitcast.31, s32[4,8]{1,0:T(4,128)} %bitcast.30, ...), custom_call_target="tpu_custom_call" | custom-call | flops 100663296 | bytes 1048576 | tf_op jit(solution)/shard_map/pallas_call | solution.py:32
  13.8 1.1 %all-to-all-done.incoming_ref = bf16[8,64,192]{2,1,0:T(8,128)(2,1)S(1)} async-done(((bf16[8,64,192]{2,1,0:T(8,128)(2,1)}), bf16[8,64,192]{2,1,0:T(8,128)(2,1)S(1)}, u32[]{:S(2)}, u32[]{:S(2)}) %all-to-all-start) | async-done | bytes 196640 | tf_op jit(solution)/shard_map/all_to_all | solution.py:327
  14.9 0.0 copy-start
  14.9 0.0 copy-start.3
  14.9 0.2 shard_map.125
  15.2 2.7 %collective-permute-start.3 = (bf16[192,128]{1,0:T(8,128)(2,1)S(1)}, bf16[192,128]{1,0:T(8,128)(2,1)S(1)}, u32[]{:S(2)}, u32[]{:S(2)}) collective-permute-start(bf16[192,128]{1,0:T(8,128)(2,1)S(1)} %get-tuple-element.35), channel_id=1, source_target_pairs={{0,16},{8,24},{16,0},{24,8},{1,17},{9,25},{17,1},{25,9},{2,18},{10... | collective-permute-start | bytes 147464 | tf_op jit(solution)/shard_map/ppermute | solution.py:320
  17.8 1.4 %collective-permute-start.4 = (bf16[192,128]{1,0:T(8,128)(2,1)S(1)}, bf16[192,128]{1,0:T(8,128)(2,1)S(1)}, u32[]{:S(2)}, u32[]{:S(2)}) collective-permute-start(bf16[192,128]{1,0:T(8,128)(2,1)S(1)} %get-tuple-element.36), channel_id=1, source_target_pairs={{0,24},{8,16},{16,8},{24,0},{1,25},{9,17},{17,9},{25,1},{2,26},{10... | collective-permute-start | bytes 147464 | tf_op jit(solution)/shard_map/ppermute | solution.py:320
  19.2 0.0 collective-permute-done.rest_0_
  19.2 0.2 collective-permute-start.5
  19.4 0.0 collective-permute-done.1.rest_1_
  19.4 0.0 collective-permute-done.2.rest_2_
  19.4 0.0 copy-done.1
  19.4 1.2 %shard_map.123.own_ref = f32[128,1024]{1,0:T(8,128)S(1)} custom-call(s32[1]{0:T(128)} %bitcast.me_ref, bf16[192,512]{1,0:T(8,128)(2,1)} %bitcast.23, bf16[768,1024]{1,0:T(8,128)(2,1)S(1)} %copy-done.1, bf16[192,128]{1,0:T(8,128)(2,1)S(1)} %collective-permute-done.rest_0_, bf16[192,128]{1,0:T(8,128)(2,1)S(1)} %collective-permute-done.1.rest_1_, ...), custom_call_target="tpu_custom_call" | custom-call | flops 201326592 | bytes 2097152 | tf_op jit(solution)/shard_map/pallas_call | solution.py:32
  20.7 0.0 copy-start.2
  20.7 0.0 collective-permute-done.3.rest_1_
  20.7 3.1 %collective-permute-done.4.rest_2_ = bf16[192,128]{1,0:T(8,128)(2,1)S(1)} collective-permute-done((bf16[192,128]{1,0:T(8,128)(2,1)S(1)}, bf16[192,128]{1,0:T(8,128)(2,1)S(1)}, u32[]{:S(2)}, u32[]{:S(2)}) %collective-permute-start.4) | collective-permute-done | bytes 49184 | tf_op jit(solution)/shard_map/ppermute | solution.py:320
  23.8 0.0 collective-permute-done.5.rest_3_
  23.8 0.0 copy-done
  23.8 0.0 copy-done.3
  23.8 0.7 %shard_map.126 = (bf16[128,1024]{1,0:T(8,128)(2,1)S(1)}, bf16[153,128]{1,0:T(8,128)(2,1)S(1)}, bf16[153,128]{1,0:T(8,128)(2,1)S(1)}, bf16[153,128]{1,0:T(8,128)(2,1)S(1)}, bf16[153,128]{1,0:T(8,128)(2,1)S(1)}) custom-call(s32[1]{0:T(128)} %bitcast.me_ref, bf16[768,1024]{1,0:T(8,128)(2,1)S(1)} %copy-done, bf16[153,1024]{1,0:T(8,128)(2,1)S(1)} %bitcast.20, ...), custom_call_target="tpu_custom_call" | custom-call | flops 201326592 | bytes 2097152 | tf_op jit(solution)/shard_map/pallas_call | solution.py:32
  24.5 1.2 %collective-permute-start.6 = (bf16[153,128]{1,0:T(8,128)(2,1)S(1)}, bf16[153,128]{1,0:T(8,128)(2,1)S(1)}, u32[]{:S(2)}, u32[]{:S(2)}) collective-permute-start(bf16[153,128]{1,0:T(8,128)(2,1)S(1)} %get-tuple-element.43), channel_id=1, source_target_pairs={{0,16},{8,24},{16,0},{24,8},{1,17},{9,25},{17,1},{25,9},{2,18},{10... | collective-permute-start | bytes 117512 | tf_op jit(solution)/shard_map/ppermute | solution.py:320
  25.7 1.2 %collective-permute-start.7 = (bf16[153,128]{1,0:T(8,128)(2,1)S(1)}, bf16[153,128]{1,0:T(8,128)(2,1)S(1)}, u32[]{:S(2)}, u32[]{:S(2)}) collective-permute-start(bf16[153,128]{1,0:T(8,128)(2,1)S(1)} %get-tuple-element.44), channel_id=1, source_target_pairs={{0,24},{8,16},{16,8},{24,0},{1,25},{9,17},{17,9},{25,1},{2,26},{10... | collective-permute-start | bytes 117512 | tf_op jit(solution)/shard_map/ppermute | solution.py:320
  26.9 1.1 %collective-permute-start.8 = (bf16[153,128]{1,0:T(8,128)(2,1)S(1)}, bf16[153,128]{1,0:T(8,128)(2,1)S(1)}, u32[]{:S(2)}, u32[]{:S(2)}) collective-permute-start(bf16[153,128]{1,0:T(8,128)(2,1)S(1)} %get-tuple-element.45), channel_id=1, source_target_pairs={{0,8},{8,0},{16,24},{24,16},{1,9},{9,1},{17,25},{25,17},{2,10},{10... | collective-permute-start | bytes 117512 | tf_op jit(solution)/shard_map/ppermute | solution.py:320
  28.1 1.6 %collective-permute-done.6.rest_1_ = bf16[153,128]{1,0:T(8,128)(2,1)S(1)} collective-permute-done((bf16[153,128]{1,0:T(8,128)(2,1)S(1)}, bf16[153,128]{1,0:T(8,128)(2,1)S(1)}, u32[]{:S(2)}, u32[]{:S(2)}) %collective-permute-start.6) | collective-permute-done | bytes 39200 | tf_op jit(solution)/shard_map/ppermute | solution.py:320
  29.6 1.9 %collective-permute-done.7.rest_2_ = bf16[153,128]{1,0:T(8,128)(2,1)S(1)} collective-permute-done((bf16[153,128]{1,0:T(8,128)(2,1)S(1)}, bf16[153,128]{1,0:T(8,128)(2,1)S(1)}, u32[]{:S(2)}, u32[]{:S(2)}) %collective-permute-start.7) | collective-permute-done | bytes 39200 | tf_op jit(solution)/shard_map/ppermute | solution.py:320
  31.5 0.0 collective-permute-done.8.rest_3_
  31.5 0.3 shard_map.129
  31.8 0.1 collective-permute-start.9
  31.9 1.2 %collective-permute-done.9.got_ref = bf16[4,16,153]{2,1,0:T(8,128)(2,1)S(1)} collective-permute-done((bf16[4,16,153]{2,1,0:T(8,128)(2,1)S(1)}, bf16[4,16,153]{2,1,0:T(8,128)(2,1)S(1)}, u32[]{:S(2)}, u32[]{:S(2)}) %collective-permute-start.9) | collective-permute-done | bytes 19616 | tf_op jit(solution)/shard_map/ppermute | solution.py:414
  33.1 1.0 %collective-permute-start.10 = (bf16[2,16,153]{2,1,0:T(8,128)(2,1)S(1)}, bf16[2,16,153]{2,1,0:T(8,128)(2,1)S(1)}, u32[]{:S(2)}, u32[]{:S(2)}) collective-permute-start(bf16[2,16,153]{2,1,0:T(8,128)(2,1)S(1)} %get-tuple-element.51), channel_id=1, source_target_pairs={{0,2},{1,3},{2,0},{3,1},{4,6},{5,7},{6,4},{7,5},{8,10},{9,11},{10,... | collective-permute-start | bytes 29384 | tf_op jit(solution)/shard_map/ppermute | solution.py:419
  34.1 1.4 %collective-permute-start.11 = (bf16[2,16,153]{2,1,0:T(8,128)(2,1)S(1)}, bf16[2,16,153]{2,1,0:T(8,128)(2,1)S(1)}, u32[]{:S(2)}, u32[]{:S(2)}) collective-permute-start(bf16[2,16,153]{2,1,0:T(8,128)(2,1)S(1)} %get-tuple-element.52), channel_id=1, source_target_pairs={{0,4},{1,5},{2,6},{3,7},{4,0},{5,1},{6,2},{7,3},{8,12},{9,13},{10,... | collective-permute-start | bytes 29384 | tf_op jit(solution)/shard_map/ppermute | solution.py:419
  35.6 1.0 %collective-permute-start.12 = (bf16[2,16,153]{2,1,0:T(8,128)(2,1)S(1)}, bf16[2,16,153]{2,1,0:T(8,128)(2,1)S(1)}, u32[]{:S(2)}, u32[]{:S(2)}) collective-permute-start(bf16[2,16,153]{2,1,0:T(8,128)(2,1)S(1)} %get-tuple-element.53), channel_id=1, source_target_pairs={{0,6},{1,7},{2,4},{3,5},{4,2},{5,3},{6,0},{7,1},{8,14},{9,15},{10,... | collective-permute-start | bytes 29384 | tf_op jit(solution)/shard_map/ppermute | solution.py:419
  36.6 0.0 copy-done.2
  36.6 0.7 %shard_map.127 = (f32[153,128]{1,0:T(8,128)S(1)}, bf16[128,1024]{1,0:T(8,128)(2,1)}) custom-call(bf16[128,1024]{1,0:T(8,128)(2,1)S(1)} %get-tuple-element.38.hidden_ref, bf16[153,1024]{1,0:T(8,128)(2,1)S(1)} %bitcast.19), custom_call_target="tpu_custom_call" | custom-call | flops 40108032 | bytes 1048576 | tf_op jit(solution)/shard_map/pallas_call | solution.py:32
  37.3 0.2 shard_map.128.near_ref
  37.5 0.0 collective-permute-done.10.rest_1_
  37.5 0.3 collective-permute-done.11.rest_2_
  37.9 2.3 %collective-permute-done.12.rest_3_ = bf16[2,16,153]{2,1,0:T(8,128)(2,1)S(1)} collective-permute-done((bf16[2,16,153]{2,1,0:T(8,128)(2,1)S(1)}, bf16[2,16,153]{2,1,0:T(8,128)(2,1)S(1)}, u32[]{:S(2)}, u32[]{:S(2)}) %collective-permute-start.12) | collective-permute-done | bytes 9824 | tf_op jit(solution)/shard_map/ppermute | solution.py:419
  40.2 0.9 %shard_map.131 = f32[153,1,128]{2,1,0:T(1,128)} custom-call(s32[1]{0:T(128)} %bitcast.me_ref, f32[153,128]{1,0:T(8,128)S(1)} %get-tuple-element.40.own_ref, f32[153,128]{1,0:T(8,128)S(1)} %shard_map.128.near_ref, bf16[128,128]{1,0:T(8,128)(2,1)S(1)} %get-tuple-element.46.far_ref, f32[4,208,128]{2,1,0:T(8,128)S(1)} %get-tuple-element.32.sums_ref, ...), custom_call_target="tpu_custom_call" | custom-call | flops 5013504 | bytes 524288 | tf_op jit(solution)/shard_map/pallas_call | solution.py:32
  (1 shorter events, 0.0 us)
Async XLA Ops:
  0.6 18.8 %copy-start.1 = (bf16[768,1024]{1,0:T(8,128)(2,1)S(1)}, bf16[768,1024]{1,0:T(8,128)(2,1)}, u32[]{:S(2)}) copy-start(bf16[768,1024]{1,0:T(8,128)(2,1)} %weight_ref.2) | copy-start | bytes 4718596
  2.8 12.1 %all-to-all-start = ((bf16[8,64,192]{2,1,0:T(8,128)(2,1)}), bf16[8,64,192]{2,1,0:T(8,128)(2,1)S(1)}, u32[]{:S(2)}, u32[]{:S(2)}) async-start(bf16[8,64,192]{2,1,0:T(8,128)(2,1)} %get-tuple-element.31), calls=%async_computation | async-start | bytes 524288 | tf_op jit(solution)/shard_map/all_to_all | solution.py:327
  8.0 11.2 %collective-permute-start = (bf16[192,128]{1,0:T(8,128)(2,1)S(1)}, bf16[192,128]{1,0:T(8,128)(2,1)S(1)}, u32[]{:S(2)}, u32[]{:S(2)}) collective-permute-start(bf16[192,128]{1,0:T(8,128)(2,1)S(1)} %get-tuple-element.28), channel_id=1, source_target_pairs={{0,16},{8,24},{16,0},{24,8},{1,17},{9,25},{17,1},{25,9},{2,18},{10... | collective-permute-start | bytes 147464 | tf_op jit(solution)/shard_map/ppermute | solution.py:320
  10.6 8.8 %collective-permute-start.1 = (bf16[192,128]{1,0:T(8,128)(2,1)S(1)}, bf16[192,128]{1,0:T(8,128)(2,1)S(1)}, u32[]{:S(2)}, u32[]{:S(2)}) collective-permute-start(bf16[192,128]{1,0:T(8,128)(2,1)S(1)} %get-tuple-element.29), channel_id=1, source_target_pairs={{0,24},{8,16},{16,8},{24,0},{1,25},{9,17},{17,9},{25,1},{2,26},{10... | collective-permute-start | bytes 147464 | tf_op jit(solution)/shard_map/ppermute | solution.py:320
  11.9 7.5 %collective-permute-start.2 = (bf16[192,128]{1,0:T(8,128)(2,1)S(1)}, bf16[192,128]{1,0:T(8,128)(2,1)S(1)}, u32[]{:S(2)}, u32[]{:S(2)}) collective-permute-start(bf16[192,128]{1,0:T(8,128)(2,1)S(1)} %get-tuple-element.30), channel_id=1, source_target_pairs={{0,8},{8,0},{16,24},{24,16},{1,9},{9,1},{17,25},{25,17},{2,10},{10... | collective-permute-start | bytes 147464 | tf_op jit(solution)/shard_map/ppermute | solution.py:320
  14.9 8.9 %copy-start = (bf16[768,1024]{1,0:T(8,128)(2,1)S(1)}, bf16[768,1024]{1,0:T(8,128)(2,1)}, u32[]{:S(2)}) copy-start(bf16[768,1024]{1,0:T(8,128)(2,1)} %weight_ref.3) | copy-start | bytes 4718596
  14.9 8.9 %copy-start.3 = (bf16[1024,153]{0,1:T(8,128)(2,1)S(1)}, bf16[1024,153]{0,1:T(8,128)(2,1)}, u32[]{:S(2)}) copy-start(bf16[1024,153]{0,1:T(8,128)(2,1)} %param.21) | copy-start | bytes 940036
  15.2 5.5 %collective-permute-start.3 = (bf16[192,128]{1,0:T(8,128)(2,1)S(1)}, bf16[192,128]{1,0:T(8,128)(2,1)S(1)}, u32[]{:S(2)}, u32[]{:S(2)}) collective-permute-start(bf16[192,128]{1,0:T(8,128)(2,1)S(1)} %get-tuple-element.35), channel_id=1, source_target_pairs={{0,16},{8,24},{16,0},{24,8},{1,17},{9,25},{17,1},{25,9},{2,18},{10... | collective-permute-start | bytes 147464 | tf_op jit(solution)/shard_map/ppermute | solution.py:320
  17.8 6.0 %collective-permute-start.4 = (bf16[192,128]{1,0:T(8,128)(2,1)S(1)}, bf16[192,128]{1,0:T(8,128)(2,1)S(1)}, u32[]{:S(2)}, u32[]{:S(2)}) collective-permute-start(bf16[192,128]{1,0:T(8,128)(2,1)S(1)} %get-tuple-element.36), channel_id=1, source_target_pairs={{0,24},{8,16},{16,8},{24,0},{1,25},{9,17},{17,9},{25,1},{2,26},{10... | collective-permute-start | bytes 147464 | tf_op jit(solution)/shard_map/ppermute | solution.py:320
  19.2 4.6 %collective-permute-start.5 = (bf16[192,128]{1,0:T(8,128)(2,1)S(1)}, bf16[192,128]{1,0:T(8,128)(2,1)S(1)}, u32[]{:S(2)}, u32[]{:S(2)}) collective-permute-start(bf16[192,128]{1,0:T(8,128)(2,1)S(1)} %get-tuple-element.37), channel_id=1, source_target_pairs={{0,8},{8,0},{16,24},{24,16},{1,9},{9,1},{17,25},{25,17},{2,10},{10... | collective-permute-start | bytes 147464 | tf_op jit(solution)/shard_map/ppermute | solution.py:320
  20.7 15.9 %copy-start.2 = (bf16[1024,153]{0,1:T(8,128)(2,1)S(1)}, bf16[1024,153]{0,1:T(8,128)(2,1)}, u32[]{:S(2)}) copy-start(bf16[1024,153]{0,1:T(8,128)(2,1)} %param.20) | copy-start | bytes 940036
  24.5 5.1 %collective-permute-start.6 = (bf16[153,128]{1,0:T(8,128)(2,1)S(1)}, bf16[153,128]{1,0:T(8,128)(2,1)S(1)}, u32[]{:S(2)}, u32[]{:S(2)}) collective-permute-start(bf16[153,128]{1,0:T(8,128)(2,1)S(1)} %get-tuple-element.43), channel_id=1, source_target_pairs={{0,16},{8,24},{16,0},{24,8},{1,17},{9,25},{17,1},{25,9},{2,18},{10... | collective-permute-start | bytes 117512 | tf_op jit(solution)/shard_map/ppermute | solution.py:320
  25.7 5.8 %collective-permute-start.7 = (bf16[153,128]{1,0:T(8,128)(2,1)S(1)}, bf16[153,128]{1,0:T(8,128)(2,1)S(1)}, u32[]{:S(2)}, u32[]{:S(2)}) collective-permute-start(bf16[153,128]{1,0:T(8,128)(2,1)S(1)} %get-tuple-element.44), channel_id=1, source_target_pairs={{0,24},{8,16},{16,8},{24,0},{1,25},{9,17},{17,9},{25,1},{2,26},{10... | collective-permute-start | bytes 117512 | tf_op jit(solution)/shard_map/ppermute | solution.py:320
  26.9 4.6 %collective-permute-start.8 = (bf16[153,128]{1,0:T(8,128)(2,1)S(1)}, bf16[153,128]{1,0:T(8,128)(2,1)S(1)}, u32[]{:S(2)}, u32[]{:S(2)}) collective-permute-start(bf16[153,128]{1,0:T(8,128)(2,1)S(1)} %get-tuple-element.45), channel_id=1, source_target_pairs={{0,8},{8,0},{16,24},{24,16},{1,9},{9,1},{17,25},{25,17},{2,10},{10... | collective-permute-start | bytes 117512 | tf_op jit(solution)/shard_map/ppermute | solution.py:320
  31.8 1.3 %collective-permute-start.9 = (bf16[4,16,153]{2,1,0:T(8,128)(2,1)S(1)}, bf16[4,16,153]{2,1,0:T(8,128)(2,1)S(1)}, u32[]{:S(2)}, u32[]{:S(2)}) collective-permute-start(bf16[4,16,153]{2,1,0:T(8,128)(2,1)S(1)} %get-tuple-element.49), channel_id=1, source_target_pairs={{0,1},{1,0},{2,3},{3,2},{4,5},{5,4},{6,7},{7,6},{8,9},{9,8},{10,11... | collective-permute-start | bytes 58760 | tf_op jit(solution)/shard_map/ppermute | solution.py:414
  33.1 4.4 %collective-permute-start.10 = (bf16[2,16,153]{2,1,0:T(8,128)(2,1)S(1)}, bf16[2,16,153]{2,1,0:T(8,128)(2,1)S(1)}, u32[]{:S(2)}, u32[]{:S(2)}) collective-permute-start(bf16[2,16,153]{2,1,0:T(8,128)(2,1)S(1)} %get-tuple-element.51), channel_id=1, source_target_pairs={{0,2},{1,3},{2,0},{3,1},{4,6},{5,7},{6,4},{7,5},{8,10},{9,11},{10,... | collective-permute-start | bytes 29384 | tf_op jit(solution)/shard_map/ppermute | solution.py:419
  34.1 3.7 %collective-permute-start.11 = (bf16[2,16,153]{2,1,0:T(8,128)(2,1)S(1)}, bf16[2,16,153]{2,1,0:T(8,128)(2,1)S(1)}, u32[]{:S(2)}, u32[]{:S(2)}) collective-permute-start(bf16[2,16,153]{2,1,0:T(8,128)(2,1)S(1)} %get-tuple-element.52), channel_id=1, source_target_pairs={{0,4},{1,5},{2,6},{3,7},{4,0},{5,1},{6,2},{7,3},{8,12},{9,13},{10,... | collective-permute-start | bytes 29384 | tf_op jit(solution)/shard_map/ppermute | solution.py:419
  35.6 4.6 %collective-permute-start.12 = (bf16[2,16,153]{2,1,0:T(8,128)(2,1)S(1)}, bf16[2,16,153]{2,1,0:T(8,128)(2,1)S(1)}, u32[]{:S(2)}, u32[]{:S(2)}) collective-permute-start(bf16[2,16,153]{2,1,0:T(8,128)(2,1)S(1)} %get-tuple-element.53), channel_id=1, source_target_pairs={{0,6},{1,7},{2,4},{3,5},{4,2},{5,3},{6,0},{7,1},{8,14},{9,15},{10,... | collective-permute-start | bytes 29384 | tf_op jit(solution)/shard_map/ppermute | solution.py:419

commit v6 on v5

--- a/solution.py
+++ b/solution.py
@@ -44,7 +44,11 @@
 
 
 def step_of(groups, k):
-    return sorted(range(groups), key=lambda d: (d > 0, abs(2 * d - groups - 1)))[k]
+    return (groups - k) % groups
+
+
+def whole_lanes(count):
+    return -(-count // 128) * 128
 
 
 def ahead(me, groups, k):
@@ -58,10 +62,12 @@
 
 
 def step_to(a, b, count):
-    return a ^ b if count & (count - 1) == 0 else (b + count - a) % count
-
-
-def next_to(a, step, count):
+    step = a ^ b if count & (count - 1) == 0 else (b + count - a) % count
+    return (count - step) % count
+
+
+def next_to(a, j, count):
+    step = step_of(count, j)
     return a ^ step if count & (count - 1) == 0 else (a + step) % count
 
 
@@ -81,7 +87,12 @@
     parts, groups, slots = sources_ref.shape
     nodes = hits.shape[1]
     rows = nodes // groups
-    indices, table = fetch(sems, (sources_hbm, sources_ref), (features_hbm, features_ref))
+    width = features_hbm.shape[0]
+    indices, table = fetch(
+        sems, (sources_hbm, sources_ref), (features_hbm, features_ref.at[pl.ds(0, width), :])
+    )
+    if features_ref.shape[0] > width:
+        features_ref[width:, :] = jnp.zeros((features_ref.shape[0] - width, nodes), bf16)
     indices.wait()
     lane = lax.broadcasted_iota(jnp.int32, (slots, nodes), 1)
 
@@ -103,7 +114,7 @@
         lax.fori_loop(0, parts // chunk, lambda i, _: step(i, False), None)
     for k in range(1, groups):
         group = ahead(me_ref[0], groups, k)
-        blocks[k - 1][...] = features_ref[:, pl.ds(pl.multiple_of(group * rows, rows), rows)]
+        blocks[k - 1][...] = features_ref[:width, pl.ds(pl.multiple_of(group * rows, rows), rows)]
 
 
 def local_kernel(
@@ -199,14 +210,13 @@
 
 def mean_kernel(me_ref, incoming_ref, sums_ref, edges_ref, *outs):
     groups, parts, slots, rows = edges_ref.shape
-    width = incoming_ref.shape[2]
+    width = outs[0].shape[0]
     for k in range(groups):
         group = ahead(me_ref[0], groups, k)
         arrived = incoming_ref[:, pl.ds(pl.multiple_of(group * slots, slots), slots), :]
-        arrived = arrived.reshape(parts * slots, width)
-        total = sums_ref[group, :width, :] + dot(
-            arrived, edges_ref[group].reshape(parts * slots, rows), FIRST
-        )
+        arrived = arrived.reshape(parts * slots, -1)
+        far = dot(arrived, edges_ref[group].reshape(parts * slots, rows), FIRST)
+        total = sums_ref[group, :width, :] + far[:width]
         outs[k][...] = (total / sums_ref[group, width : width + 1, :]).astype(bf16)
 
 
@@ -258,7 +268,8 @@
         at = pl.multiple_of(behind(me_ref[0], groups, k) * rows, rows)
         term = dot(hits_ref[:, pl.ds(at, rows)], projected[k][...], LAST)
         total = term if total is None else total + term
-    total = total.astype(bf16)
+    gap = mine_ref.shape[2] - total.shape[1]
+    total = jnp.concatenate([total, jnp.zeros((total.shape[0], gap), f32)], axis=1).astype(bf16)
     half = total.shape[0] // 2
     mine_ref[...] = total[:half].reshape(mine_ref.shape)
     mate_ref[...] = total[half:].reshape(mate_ref.shape)
@@ -285,7 +296,7 @@
     arrived, out_ref = rest[:-1], rest[-1]
     width = sums_ref.shape[1] - EXTRA
     arrived = jnp.concatenate([part[...].reshape(-1, part.shape[2]) for part in arrived], axis=0)
-    far = dot(arrived, far_ref[...], FIRST)
+    far = dot(arrived, far_ref[...], FIRST)[: own_ref.shape[0]]
     total = own_ref[...] + (near_ref[...] + far) / sums_ref[me_ref[0], width : width + 1, :]
     out_ref[...] = total.reshape(out_ref.shape)
 
@@ -328,11 +339,12 @@
 
     sent, *feature_blocks = call(
         functools.partial(gather_kernel, chunk),
-        (shape(parts, groups * slots, width),) + (shape(width, rows),) * (groups - 1),
+        (shape(parts, groups * slots, whole_lanes(width)),)
+        + (shape(width, rows),) * (groups - 1),
         [SM, HB, HB],
         [
             pltpu.VMEM((parts, groups, slots), jnp.int32),
-            pltpu.VMEM((width, nodes), bf16),
+            pltpu.VMEM((whole_lanes(width), nodes), bf16),
             pltpu.VMEM((chunk * groups * slots, nodes), bf16),
             pltpu.SemaphoreType.DMA((2,)),
         ],
@@ -405,7 +417,7 @@
     chips = parts // 2
     mine, mate = call(
         pick_kernel,
-        (shape(chips, slots, classes),) * 2,
+        (shape(chips, slots, whole_lanes(classes)),) * 2,
         [SM] + [VM] * (1 + groups),
         (),
         2 * parts * slots * nodes * classes,
@@ -413,7 +425,7 @@
     )(me, hits, *projected)
     mate = lax.ppermute(mate, "dom", [(d, d ^ 1) for d in range(parts)])
     arrived = call(
-        pair_kernel, (shape(2, slots, classes),) * chips, [VM, VM], (), 0, 1 << 19
+        pair_kernel, (shape(2, slots, whole_lanes(classes)),) * chips, [VM, VM], (), 0, 1 << 19
     )(mine, mate)
     arrived = [arrived[0]] + [
         lax.ppermute(

time: 41.4 us -> 40.5 us (0.978)
  waiting for transfers between devices: 11.6 us -> 9.38 us
  starting transfers between devices: 20.7 us -> 22 us
    ppermute x9, starting transfers between devices: 12 us -> 13.3 us  [shift(): lax.ppermute(block, 'feat', [(i, ahead(i, groups, k)) for i in range(grou...]
    ppermute x9, waiting for transfers between devices: 6.62 us -> 5.37 us  [shift(): lax.ppermute(block, 'feat', [(i, ahead(i, groups, k)) for i in range(grou...]
    ppermute x3, waiting for transfers between devices: 2.67 us -> 1.92 us  [on_device(): lax.ppermute(arrived[j], 'dom', [(d, next_to(d // 2, j, chips) * 2 + d %...]
  transfers between devices with their start and end apart: 14 -> 14, of which waited for: 7 -> 10; matrix products, arithmetic and copies ran while one was open for 0% -> 0% of each run, Pallas kernels for 10% -> 10%
where the time goes in v6:
time: 40.5 us; the launch traced here: 40.2 us
  starting transfers between devices  22 us (54%)
  waiting for transfers between devices  9.38 us (23%)
  Pallas kernels  8.06 us (20%)
  between operations  0.74 us (2%)
    ppermute x9, starting transfers between devices, shift(): lax.ppermute(block, 'feat', [(i, ahead(i, groups, k)) for i in range(grou...  13.3 us
    pallas_call x10, Pallas kernels, placed(): run(*(pltpu.with_memory_space_constraint(value, pltpu.HBM) if spec is HB...  8.06 us
    ppermute x9, waiting for transfers between devices, shift(): lax.ppermute(block, 'feat', [(i, ahead(i, groups, k)) for i in range(grou...  5.37 us
    all_to_all x1, starting transfers between devices, swap(): return lax.all_to_all(value, 'dom', split_axis=0, concat_axis=0, tiled=True)  5.18 us
    ppermute x3, starting transfers between devices, on_device(): lax.ppermute(arrived[j], 'dom', [(d, next_to(d // 2, j, chips) * 2 + d %...  3.49 us
    ppermute x3, waiting for transfers between devices, on_device(): lax.ppermute(arrived[j], 'dom', [(d, next_to(d // 2, j, chips) * 2 + d %...  1.92 us
    ppermute x1, waiting for transfers between devices, on_device(): mate = lax.ppermute(mate, 'dom', [(d, d ^ 1) for d in range(parts)])  1.19 us
    all_to_all x1, waiting for transfers between devices, swap(): return lax.all_to_all(value, 'dom', split_axis=0, concat_axis=0, tiled=True)  0.89 us
  transfers between devices with their start and end apart: 14, of which 10 were waited for; matrix products, arithmetic and copies ran while one was open for 0% of the time, Pallas kernels for 10%

profile of v6, /device:TPU:0, one launch (start us, length us, event | category | flops | bytes accessed | tf_op | source)
XLA Modules:
  0.0 40.2 jit_solution(1263864313865389507)
XLA Ops:
  0.6 0.0 copy-start.1
  0.6 2.2 %shard_map.122 = (bf16[8,64,256]{2,1,0:T(8,128)(2,1)}, bf16[192,128]{1,0:T(8,128)(2,1)S(1)}, bf16[192,128]{1,0:T(8,128)(2,1)S(1)}, bf16[192,128]{1,0:T(8,128)(2,1)S(1)}) custom-call(s32[1]{0:T(128)} %bitcast.me_ref, s32[8,4,16]{2,1,0:T(4,128)} %bitcast.26, bf16[192,512]{1,0:T(8,128)(2,1)} %bitcast.21), custom_call_target="tpu_custom_call" | custom-call | flops 100663296 | bytes 1048576 | tf_op jit(solution)/shard_map/pallas_call | solution.py:32
  2.8 5.2 %all-to-all-start = ((bf16[8,64,256]{2,1,0:T(8,128)(2,1)}), bf16[8,64,256]{2,1,0:T(8,128)(2,1)S(1)}, u32[]{:S(2)}, u32[]{:S(2)}) async-start(bf16[8,64,256]{2,1,0:T(8,128)(2,1)} %get-tuple-element.31), calls=%async_computation | async-start | bytes 524288 | tf_op jit(solution)/shard_map/all_to_all | solution.py:338
  8.0 3.6 %collective-permute-start = (bf16[192,128]{1,0:T(8,128)(2,1)S(1)}, bf16[192,128]{1,0:T(8,128)(2,1)S(1)}, u32[]{:S(2)}, u32[]{:S(2)}) collective-permute-start(bf16[192,128]{1,0:T(8,128)(2,1)S(1)} %get-tuple-element.28), channel_id=1, source_target_pairs={{0,24},{8,16},{16,8},{24,0},{1,25},{9,17},{17,9},{25,1},{2,26},{10... | collective-permute-start | bytes 147464 | tf_op jit(solution)/shard_map/ppermute | solution.py:331
  11.6 0.0 collective-permute-start.1
  11.6 0.8 %collective-permute-start.2 = (bf16[192,128]{1,0:T(8,128)(2,1)S(1)}, bf16[192,128]{1,0:T(8,128)(2,1)S(1)}, u32[]{:S(2)}, u32[]{:S(2)}) collective-permute-start(bf16[192,128]{1,0:T(8,128)(2,1)S(1)} %get-tuple-element.30), channel_id=1, source_target_pairs={{0,8},{8,0},{16,24},{24,16},{1,9},{9,1},{17,25},{25,17},{2,10},{10... | collective-permute-start | bytes 147464 | tf_op jit(solution)/shard_map/ppermute | solution.py:331
  12.4 1.7 %shard_map.124 = (f32[4,208,128]{2,1,0:T(8,128)S(1)}, bf16[4,8,16,128]{3,2,1,0:T(8,128)(2,1)S(1)}, bf16[128,512]{1,0:T(8,128)(2,1)S(1)}, bf16[128,512]{1,0:T(8,128)(2,1)S(1)}, bf16[128,128]{1,0:T(8,128)(2,1)S(1)}) custom-call(s32[1]{0:T(128)} %bitcast.me_ref, s32[1]{0:T(128)} %bitcast.6.part_ref, s32[2,12]{1,0:T(2,128)} %bitcast.31, s32[4,8]{1,0:T(4,128)} %bitcast.30, ...), custom_call_target="tpu_custom_call" | custom-call | flops 100663296 | bytes 1048576 | tf_op jit(solution)/shard_map/pallas_call | solution.py:32
  14.1 0.9 %all-to-all-done.incoming_ref = bf16[8,64,256]{2,1,0:T(8,128)(2,1)S(1)} async-done(((bf16[8,64,256]{2,1,0:T(8,128)(2,1)}), bf16[8,64,256]{2,1,0:T(8,128)(2,1)S(1)}, u32[]{:S(2)}, u32[]{:S(2)}) %all-to-all-start) | async-done | bytes 262176 | tf_op jit(solution)/shard_map/all_to_all | solution.py:338
  14.9 0.0 copy-start
  14.9 0.0 copy-start.3
  14.9 0.3 shard_map.125
  15.2 3.7 %collective-permute-start.3 = (bf16[192,128]{1,0:T(8,128)(2,1)S(1)}, bf16[192,128]{1,0:T(8,128)(2,1)S(1)}, u32[]{:S(2)}, u32[]{:S(2)}) collective-permute-start(bf16[192,128]{1,0:T(8,128)(2,1)S(1)} %get-tuple-element.35), channel_id=1, source_target_pairs={{0,24},{8,16},{16,8},{24,0},{1,25},{9,17},{17,9},{25,1},{2,26},{10... | collective-permute-start | bytes 147464 | tf_op jit(solution)/shard_map/ppermute | solution.py:331
  18.9 0.0 collective-permute-start.4
  18.9 0.0 collective-permute-done.rest_0_
  18.9 0.8 %collective-permute-start.5 = (bf16[192,128]{1,0:T(8,128)(2,1)S(1)}, bf16[192,128]{1,0:T(8,128)(2,1)S(1)}, u32[]{:S(2)}, u32[]{:S(2)}) collective-permute-start(bf16[192,128]{1,0:T(8,128)(2,1)S(1)} %get-tuple-element.37), channel_id=1, source_target_pairs={{0,8},{8,0},{16,24},{24,16},{1,9},{9,1},{17,25},{25,17},{2,10},{10... | collective-permute-start | bytes 147464 | tf_op jit(solution)/shard_map/ppermute | solution.py:331
  19.7 0.0 collective-permute-done.1.rest_1_
  19.7 0.0 collective-permute-done.2.rest_2_
  19.7 0.0 copy-done.1
  19.7 1.2 %shard_map.123.own_ref = f32[128,1024]{1,0:T(8,128)S(1)} custom-call(s32[1]{0:T(128)} %bitcast.me_ref, bf16[192,512]{1,0:T(8,128)(2,1)} %bitcast.23, bf16[768,1024]{1,0:T(8,128)(2,1)S(1)} %copy-done.1, bf16[192,128]{1,0:T(8,128)(2,1)S(1)} %collective-permute-done.rest_0_, bf16[192,128]{1,0:T(8,128)(2,1)S(1)} %collective-permute-done.1.rest_1_, ...), custom_call_target="tpu_custom_call" | custom-call | flops 201326592 | bytes 2097152 | tf_op jit(solution)/shard_map/pallas_call | solution.py:32
  20.9 0.0 copy-start.2
  20.9 0.5 %collective-permute-done.3.rest_1_ = bf16[192,128]{1,0:T(8,128)(2,1)S(1)} collective-permute-done((bf16[192,128]{1,0:T(8,128)(2,1)S(1)}, bf16[192,128]{1,0:T(8,128)(2,1)S(1)}, u32[]{:S(2)}, u32[]{:S(2)}) %collective-permute-start.3) | collective-permute-done | bytes 49184 | tf_op jit(solution)/shard_map/ppermute | solution.py:331
  21.4 2.4 %collective-permute-done.4.rest_2_ = bf16[192,128]{1,0:T(8,128)(2,1)S(1)} collective-permute-done((bf16[192,128]{1,0:T(8,128)(2,1)S(1)}, bf16[192,128]{1,0:T(8,128)(2,1)S(1)}, u32[]{:S(2)}, u32[]{:S(2)}) %collective-permute-start.4) | collective-permute-done | bytes 49184 | tf_op jit(solution)/shard_map/ppermute | solution.py:331
  23.9 0.0 collective-permute-done.5.rest_3_
  23.9 0.0 copy-done
  23.9 0.0 copy-done.3
  23.9 0.7 %shard_map.126 = (bf16[128,1024]{1,0:T(8,128)(2,1)S(1)}, bf16[153,128]{1,0:T(8,128)(2,1)S(1)}, bf16[153,128]{1,0:T(8,128)(2,1)S(1)}, bf16[153,128]{1,0:T(8,128)(2,1)S(1)}, bf16[153,128]{1,0:T(8,128)(2,1)S(1)}) custom-call(s32[1]{0:T(128)} %bitcast.me_ref, bf16[768,1024]{1,0:T(8,128)(2,1)S(1)} %copy-done, bf16[153,1024]{1,0:T(8,128)(2,1)S(1)} %bitcast.20, ...), custom_call_target="tpu_custom_call" | custom-call | flops 201326592 | bytes 2097152 | tf_op jit(solution)/shard_map/pallas_call | solution.py:32
  24.6 1.7 %collective-permute-start.6 = (bf16[153,128]{1,0:T(8,128)(2,1)S(1)}, bf16[153,128]{1,0:T(8,128)(2,1)S(1)}, u32[]{:S(2)}, u32[]{:S(2)}) collective-permute-start(bf16[153,128]{1,0:T(8,128)(2,1)S(1)} %get-tuple-element.43), channel_id=1, source_target_pairs={{0,24},{8,16},{16,8},{24,0},{1,25},{9,17},{17,9},{25,1},{2,26},{10... | collective-permute-start | bytes 117512 | tf_op jit(solution)/shard_map/ppermute | solution.py:331
  26.3 0.5 %collective-permute-start.7 = (bf16[153,128]{1,0:T(8,128)(2,1)S(1)}, bf16[153,128]{1,0:T(8,128)(2,1)S(1)}, u32[]{:S(2)}, u32[]{:S(2)}) collective-permute-start(bf16[153,128]{1,0:T(8,128)(2,1)S(1)} %get-tuple-element.44), channel_id=1, source_target_pairs={{0,16},{8,24},{16,0},{24,8},{1,17},{9,25},{17,1},{25,9},{2,18},{10... | collective-permute-start | bytes 117512 | tf_op jit(solution)/shard_map/ppermute | solution.py:331
  26.7 2.3 %collective-permute-start.8 = (bf16[153,128]{1,0:T(8,128)(2,1)S(1)}, bf16[153,128]{1,0:T(8,128)(2,1)S(1)}, u32[]{:S(2)}, u32[]{:S(2)}) collective-permute-start(bf16[153,128]{1,0:T(8,128)(2,1)S(1)} %get-tuple-element.45), channel_id=1, source_target_pairs={{0,8},{8,0},{16,24},{24,16},{1,9},{9,1},{17,25},{25,17},{2,10},{10... | collective-permute-start | bytes 117512 | tf_op jit(solution)/shard_map/ppermute | solution.py:331
  29.0 1.4 %collective-permute-done.6.rest_1_ = bf16[153,128]{1,0:T(8,128)(2,1)S(1)} collective-permute-done((bf16[153,128]{1,0:T(8,128)(2,1)S(1)}, bf16[153,128]{1,0:T(8,128)(2,1)S(1)}, u32[]{:S(2)}, u32[]{:S(2)}) %collective-permute-start.6) | collective-permute-done | bytes 39200 | tf_op jit(solution)/shard_map/ppermute | solution.py:331
  30.4 0.8 %collective-permute-done.7.rest_2_ = bf16[153,128]{1,0:T(8,128)(2,1)S(1)} collective-permute-done((bf16[153,128]{1,0:T(8,128)(2,1)S(1)}, bf16[153,128]{1,0:T(8,128)(2,1)S(1)}, u32[]{:S(2)}, u32[]{:S(2)}) %collective-permute-start.7) | collective-permute-done | bytes 39200 | tf_op jit(solution)/shard_map/ppermute | solution.py:331
  31.3 0.2 collective-permute-done.8.rest_3_
  31.5 0.3 shard_map.129
  31.7 0.1 collective-permute-start.9
  31.8 1.2 %collective-permute-done.9.got_ref = bf16[4,16,256]{2,1,0:T(8,128)(2,1)S(1)} collective-permute-done((bf16[4,16,256]{2,1,0:T(8,128)(2,1)S(1)}, bf16[4,16,256]{2,1,0:T(8,128)(2,1)S(1)}, u32[]{:S(2)}, u32[]{:S(2)}) %collective-permute-start.9) | collective-permute-done | bytes 32800 | tf_op jit(solution)/shard_map/ppermute | solution.py:426
  33.0 2.1 %collective-permute-start.10 = (bf16[2,16,256]{2,1,0:T(8,128)(2,1)S(1)}, bf16[2,16,256]{2,1,0:T(8,128)(2,1)S(1)}, u32[]{:S(2)}, u32[]{:S(2)}) collective-permute-start(bf16[2,16,256]{2,1,0:T(8,128)(2,1)S(1)} %get-tuple-element.51), channel_id=1, source_target_pairs={{0,6},{1,7},{2,4},{3,5},{4,2},{5,3},{6,0},{7,1},{8,14},{9,15},{10,... | collective-permute-start | bytes 49160 | tf_op jit(solution)/shard_map/ppermute | solution.py:431
  35.1 0.5 %collective-permute-start.11 = (bf16[2,16,256]{2,1,0:T(8,128)(2,1)S(1)}, bf16[2,16,256]{2,1,0:T(8,128)(2,1)S(1)}, u32[]{:S(2)}, u32[]{:S(2)}) collective-permute-start(bf16[2,16,256]{2,1,0:T(8,128)(2,1)S(1)} %get-tuple-element.52), channel_id=1, source_target_pairs={{0,4},{1,5},{2,6},{3,7},{4,0},{5,1},{6,2},{7,3},{8,12},{9,13},{10,... | collective-permute-start | bytes 49160 | tf_op jit(solution)/shard_map/ppermute | solution.py:431
  35.6 0.9 %collective-permute-start.12 = (bf16[2,16,256]{2,1,0:T(8,128)(2,1)S(1)}, bf16[2,16,256]{2,1,0:T(8,128)(2,1)S(1)}, u32[]{:S(2)}, u32[]{:S(2)}) collective-permute-start(bf16[2,16,256]{2,1,0:T(8,128)(2,1)S(1)} %get-tuple-element.53), channel_id=1, source_target_pairs={{0,2},{1,3},{2,0},{3,1},{4,6},{5,7},{6,4},{7,5},{8,10},{9,11},{10,... | collective-permute-start | bytes 49160 | tf_op jit(solution)/shard_map/ppermute | solution.py:431
  36.5 0.0 copy-done.2
  36.5 0.7 %shard_map.127 = (f32[153,128]{1,0:T(8,128)S(1)}, bf16[128,1024]{1,0:T(8,128)(2,1)}) custom-call(bf16[128,1024]{1,0:T(8,128)(2,1)S(1)} %get-tuple-element.38.hidden_ref, bf16[153,1024]{1,0:T(8,128)(2,1)S(1)} %bitcast.19), custom_call_target="tpu_custom_call" | custom-call | flops 40108032 | bytes 1048576 | tf_op jit(solution)/shard_map/pallas_call | solution.py:32
  37.2 0.2 shard_map.128.near_ref
  37.4 0.2 collective-permute-done.10.rest_1_
  37.6 1.2 %collective-permute-done.11.rest_2_ = bf16[2,16,256]{2,1,0:T(8,128)(2,1)S(1)} collective-permute-done((bf16[2,16,256]{2,1,0:T(8,128)(2,1)S(1)}, bf16[2,16,256]{2,1,0:T(8,128)(2,1)S(1)}, u32[]{:S(2)}, u32[]{:S(2)}) %collective-permute-start.11) | collective-permute-done | bytes 16416 | tf_op jit(solution)/shard_map/ppermute | solution.py:431
  38.8 0.5 %collective-permute-done.12.rest_3_ = bf16[2,16,256]{2,1,0:T(8,128)(2,1)S(1)} collective-permute-done((bf16[2,16,256]{2,1,0:T(8,128)(2,1)S(1)}, bf16[2,16,256]{2,1,0:T(8,128)(2,1)S(1)}, u32[]{:S(2)}, u32[]{:S(2)}) %collective-permute-start.12) | collective-permute-done | bytes 16416 | tf_op jit(solution)/shard_map/ppermute | solution.py:431
  39.4 0.9 %shard_map.131 = f32[153,1,128]{2,1,0:T(1,128)} custom-call(s32[1]{0:T(128)} %bitcast.me_ref, f32[153,128]{1,0:T(8,128)S(1)} %get-tuple-element.40.own_ref, f32[153,128]{1,0:T(8,128)S(1)} %shard_map.128.near_ref, bf16[128,128]{1,0:T(8,128)(2,1)S(1)} %get-tuple-element.46.far_ref, f32[4,208,128]{2,1,0:T(8,128)S(1)} %get-tuple-element.32.sums_ref, ...), custom_call_target="tpu_custom_call" | custom-call | flops 5013504 | bytes 524288 | tf_op jit(solution)/shard_map/pallas_call | solution.py:32
  (1 shorter events, 0.0 us)
Async XLA Ops:
  0.6 19.1 %copy-start.1 = (bf16[768,1024]{1,0:T(8,128)(2,1)S(1)}, bf16[768,1024]{1,0:T(8,128)(2,1)}, u32[]{:S(2)}) copy-start(bf16[768,1024]{1,0:T(8,128)(2,1)} %weight_ref.2) | copy-start | bytes 4718596
  2.8 12.1 %all-to-all-start = ((bf16[8,64,256]{2,1,0:T(8,128)(2,1)}), bf16[8,64,256]{2,1,0:T(8,128)(2,1)S(1)}, u32[]{:S(2)}, u32[]{:S(2)}) async-start(bf16[8,64,256]{2,1,0:T(8,128)(2,1)} %get-tuple-element.31), calls=%async_computation | async-start | bytes 524288 | tf_op jit(solution)/shard_map/all_to_all | solution.py:338
  8.0 10.9 %collective-permute-start = (bf16[192,128]{1,0:T(8,128)(2,1)S(1)}, bf16[192,128]{1,0:T(8,128)(2,1)S(1)}, u32[]{:S(2)}, u32[]{:S(2)}) collective-permute-start(bf16[192,128]{1,0:T(8,128)(2,1)S(1)} %get-tuple-element.28), channel_id=1, source_target_pairs={{0,24},{8,16},{16,8},{24,0},{1,25},{9,17},{17,9},{25,1},{2,26},{10... | collective-permute-start | bytes 147464 | tf_op jit(solution)/shard_map/ppermute | solution.py:331
  11.6 8.1 %collective-permute-start.1 = (bf16[192,128]{1,0:T(8,128)(2,1)S(1)}, bf16[192,128]{1,0:T(8,128)(2,1)S(1)}, u32[]{:S(2)}, u32[]{:S(2)}) collective-permute-start(bf16[192,128]{1,0:T(8,128)(2,1)S(1)} %get-tuple-element.29), channel_id=1, source_target_pairs={{0,16},{8,24},{16,0},{24,8},{1,17},{9,25},{17,1},{25,9},{2,18},{10... | collective-permute-start | bytes 147464 | tf_op jit(solution)/shard_map/ppermute | solution.py:331
  11.6 8.1 %collective-permute-start.2 = (bf16[192,128]{1,0:T(8,128)(2,1)S(1)}, bf16[192,128]{1,0:T(8,128)(2,1)S(1)}, u32[]{:S(2)}, u32[]{:S(2)}) collective-permute-start(bf16[192,128]{1,0:T(8,128)(2,1)S(1)} %get-tuple-element.30), channel_id=1, source_target_pairs={{0,8},{8,0},{16,24},{24,16},{1,9},{9,1},{17,25},{25,17},{2,10},{10... | collective-permute-start | bytes 147464 | tf_op jit(solution)/shard_map/ppermute | solution.py:331
  14.9 8.9 %copy-start = (bf16[768,1024]{1,0:T(8,128)(2,1)S(1)}, bf16[768,1024]{1,0:T(8,128)(2,1)}, u32[]{:S(2)}) copy-start(bf16[768,1024]{1,0:T(8,128)(2,1)} %weight_ref.3) | copy-start | bytes 4718596
  14.9 8.9 %copy-start.3 = (bf16[1024,153]{0,1:T(8,128)(2,1)S(1)}, bf16[1024,153]{0,1:T(8,128)(2,1)}, u32[]{:S(2)}) copy-start(bf16[1024,153]{0,1:T(8,128)(2,1)} %param.21) | copy-start | bytes 940036
  15.2 6.2 %collective-permute-start.3 = (bf16[192,128]{1,0:T(8,128)(2,1)S(1)}, bf16[192,128]{1,0:T(8,128)(2,1)S(1)}, u32[]{:S(2)}, u32[]{:S(2)}) collective-permute-start(bf16[192,128]{1,0:T(8,128)(2,1)S(1)} %get-tuple-element.35), channel_id=1, source_target_pairs={{0,24},{8,16},{16,8},{24,0},{1,25},{9,17},{17,9},{25,1},{2,26},{10... | collective-permute-start | bytes 147464 | tf_op jit(solution)/shard_map/ppermute | solution.py:331
  18.9 5.0 %collective-permute-start.4 = (bf16[192,128]{1,0:T(8,128)(2,1)S(1)}, bf16[192,128]{1,0:T(8,128)(2,1)S(1)}, u32[]{:S(2)}, u32[]{:S(2)}) collective-permute-start(bf16[192,128]{1,0:T(8,128)(2,1)S(1)} %get-tuple-element.36), channel_id=1, source_target_pairs={{0,16},{8,24},{16,0},{24,8},{1,17},{9,25},{17,1},{25,9},{2,18},{10... | collective-permute-start | bytes 147464 | tf_op jit(solution)/shard_map/ppermute | solution.py:331
  18.9 5.0 %collective-permute-start.5 = (bf16[192,128]{1,0:T(8,128)(2,1)S(1)}, bf16[192,128]{1,0:T(8,128)(2,1)S(1)}, u32[]{:S(2)}, u32[]{:S(2)}) collective-permute-start(bf16[192,128]{1,0:T(8,128)(2,1)S(1)} %get-tuple-element.37), channel_id=1, source_target_pairs={{0,8},{8,0},{16,24},{24,16},{1,9},{9,1},{17,25},{25,17},{2,10},{10... | collective-permute-start | bytes 147464 | tf_op jit(solution)/shard_map/ppermute | solution.py:331
  20.9 15.6 %copy-start.2 = (bf16[1024,153]{0,1:T(8,128)(2,1)S(1)}, bf16[1024,153]{0,1:T(8,128)(2,1)}, u32[]{:S(2)}) copy-start(bf16[1024,153]{0,1:T(8,128)(2,1)} %param.20) | copy-start | bytes 940036
  24.6 5.9 %collective-permute-start.6 = (bf16[153,128]{1,0:T(8,128)(2,1)S(1)}, bf16[153,128]{1,0:T(8,128)(2,1)S(1)}, u32[]{:S(2)}, u32[]{:S(2)}) collective-permute-start(bf16[153,128]{1,0:T(8,128)(2,1)S(1)} %get-tuple-element.43), channel_id=1, source_target_pairs={{0,24},{8,16},{16,8},{24,0},{1,25},{9,17},{17,9},{25,1},{2,26},{10... | collective-permute-start | bytes 117512 | tf_op jit(solution)/shard_map/ppermute | solution.py:331
  26.3 5.0 %collective-permute-start.7 = (bf16[153,128]{1,0:T(8,128)(2,1)S(1)}, bf16[153,128]{1,0:T(8,128)(2,1)S(1)}, u32[]{:S(2)}, u32[]{:S(2)}) collective-permute-start(bf16[153,128]{1,0:T(8,128)(2,1)S(1)} %get-tuple-element.44), channel_id=1, source_target_pairs={{0,16},{8,24},{16,0},{24,8},{1,17},{9,25},{17,1},{25,9},{2,18},{10... | collective-permute-start | bytes 117512 | tf_op jit(solution)/shard_map/ppermute | solution.py:331
  26.7 4.7 %collective-permute-start.8 = (bf16[153,128]{1,0:T(8,128)(2,1)S(1)}, bf16[153,128]{1,0:T(8,128)(2,1)S(1)}, u32[]{:S(2)}, u32[]{:S(2)}) collective-permute-start(bf16[153,128]{1,0:T(8,128)(2,1)S(1)} %get-tuple-element.45), channel_id=1, source_target_pairs={{0,8},{8,0},{16,24},{24,16},{1,9},{9,1},{17,25},{25,17},{2,10},{10... | collective-permute-start | bytes 117512 | tf_op jit(solution)/shard_map/ppermute | solution.py:331
  31.7 1.3 %collective-permute-start.9 = (bf16[4,16,256]{2,1,0:T(8,128)(2,1)S(1)}, bf16[4,16,256]{2,1,0:T(8,128)(2,1)S(1)}, u32[]{:S(2)}, u32[]{:S(2)}) collective-permute-start(bf16[4,16,256]{2,1,0:T(8,128)(2,1)S(1)} %get-tuple-element.49), channel_id=1, source_target_pairs={{0,1},{1,0},{2,3},{3,2},{4,5},{5,4},{6,7},{7,6},{8,9},{9,8},{10,11... | collective-permute-start | bytes 98312 | tf_op jit(solution)/shard_map/ppermute | solution.py:426
  33.0 4.6 %collective-permute-start.10 = (bf16[2,16,256]{2,1,0:T(8,128)(2,1)S(1)}, bf16[2,16,256]{2,1,0:T(8,128)(2,1)S(1)}, u32[]{:S(2)}, u32[]{:S(2)}) collective-permute-start(bf16[2,16,256]{2,1,0:T(8,128)(2,1)S(1)} %get-tuple-element.51), channel_id=1, source_target_pairs={{0,6},{1,7},{2,4},{3,5},{4,2},{5,3},{6,0},{7,1},{8,14},{9,15},{10,... | collective-permute-start | bytes 49160 | tf_op jit(solution)/shard_map/ppermute | solution.py:431
  35.1 3.7 %collective-permute-start.11 = (bf16[2,16,256]{2,1,0:T(8,128)(2,1)S(1)}, bf16[2,16,256]{2,1,0:T(8,128)(2,1)S(1)}, u32[]{:S(2)}, u32[]{:S(2)}) collective-permute-start(bf16[2,16,256]{2,1,0:T(8,128)(2,1)S(1)} %get-tuple-element.52), channel_id=1, source_target_pairs={{0,4},{1,5},{2,6},{3,7},{4,0},{5,1},{6,2},{7,3},{8,12},{9,13},{10,... | collective-permute-start | bytes 49160 | tf_op jit(solution)/shard_map/ppermute | solution.py:431
  35.6 3.7 %collective-permute-start.12 = (bf16[2,16,256]{2,1,0:T(8,128)(2,1)S(1)}, bf16[2,16,256]{2,1,0:T(8,128)(2,1)S(1)}, u32[]{:S(2)}, u32[]{:S(2)}) collective-permute-start(bf16[2,16,256]{2,1,0:T(8,128)(2,1)S(1)} %get-tuple-element.53), channel_id=1, source_target_pairs={{0,2},{1,3},{2,0},{3,1},{4,6},{5,7},{6,4},{7,5},{8,10},{9,11},{10,... | collective-permute-start | bytes 49160 | tf_op jit(solution)/shard_map/ppermute | solution.py:431

commit v7 on v6

--- a/solution.py
+++ b/solution.py
@@ -51,14 +51,22 @@
     return -(-count // 128) * 128
 
 
-def ahead(me, groups, k):
-    step = step_of(groups, k)
+def hop(groups, k, core):
+    return k and groups - k + core * (1 if k > 1 else 2 - groups)
+
+
+def ahead(me, core, groups, k):
+    step = hop(groups, k, core)
     return me ^ step if groups & (groups - 1) == 0 else (me + step) % groups
 
 
-def behind(me, groups, k):
-    step = step_of(groups, k)
+def behind(me, core, groups, k):
+    step = hop(groups, k, core)
     return me ^ step if groups & (groups - 1) == 0 else (me + groups - step) % groups
+
+
+def place_of(me_ref):
+    return me_ref[0] // 2, me_ref[0] % 2
 
 
 def step_to(a, b, count):
@@ -113,7 +121,7 @@
         table.wait()
         lax.fori_loop(0, parts // chunk, lambda i, _: step(i, False), None)
     for k in range(1, groups):
-        group = ahead(me_ref[0], groups, k)
+        group = ahead(*place_of(me_ref), groups, k)
         blocks[k - 1][...] = features_ref[:width, pl.ds(pl.multiple_of(group * rows, rows), rows)]
 
 
@@ -143,7 +151,7 @@
     bands,
     sems,
 ):
-    me = me_ref[0]
+    me, core = place_of(me_ref)
     parts, groups, slots = targets_ref.shape
     rows = tiles_ref.shape[1]
     width = features_hbm.shape[0]
@@ -197,7 +205,7 @@
     mine = lax.broadcasted_iota(jnp.int32, sources_ref.shape, 1) == me
     picks = jnp.sum(jnp.where(mine, sources_ref[...], 0), axis=1).T
     lane = lax.broadcasted_iota(jnp.int32, (slots, hits_ref.shape[1]), 1)
-    chips, chip, core = parts // 2, part_ref[0] // 2, part_ref[0] % 2
+    chips, chip = parts // 2, part_ref[0] // 2
     for d in range(parts):
         other = (d % 2) ^ core
         to = other * chips + step_to(chip, d // 2, chips)
@@ -212,7 +220,7 @@
     groups, parts, slots, rows = edges_ref.shape
     width = outs[0].shape[0]
     for k in range(groups):
-        group = ahead(me_ref[0], groups, k)
+        group = ahead(*place_of(me_ref), groups, k)
         arrived = incoming_ref[:, pl.ds(pl.multiple_of(group * slots, slots), slots), :]
         arrived = arrived.reshape(parts * slots, -1)
         far = dot(arrived, edges_ref[group].reshape(parts * slots, rows), FIRST)
@@ -223,14 +231,14 @@
 def self_kernel(me_ref, features_hbm, weight_ref, *rest):
     parts, (out_ref, own_ref, sem) = rest[:-3], rest[-3:]
     groups, (width, rows) = len(parts) + 1, own_ref.shape
-    me = me_ref[0]
+    me, core = place_of(me_ref)
     own = pltpu.make_async_copy(
         features_hbm.at[:, pl.ds(pl.multiple_of(me * rows, rows), rows)], own_ref, sem
     )
     own.start()
     total = jnp.zeros(out_ref.shape, f32)
     for k in range(1, groups):
-        span = pl.ds(pl.multiple_of(behind(me, groups, k) * width, width), width)
+        span = pl.ds(pl.multiple_of(behind(me, core, groups, k) * width, width), width)
         total = total + dot(parts[k - 1][...], weight_ref[span, :], FIRST)
     own.wait()
     span = pl.ds(pl.multiple_of(me * width, width), width)
@@ -243,7 +251,7 @@
     width = parts[0].shape[0]
     total = own_ref[...]
     for k in range(len(parts)):
-        source = behind(me_ref[0], len(parts), k)
+        source = behind(*place_of(me_ref), len(parts), k)
         span = pl.ds(pl.multiple_of(source * width, width), width)
         total = total + dot(parts[k][...], weight_ref[span, :], FIRST)
     hidden = jnp.maximum(total, 0.0).astype(bf16)
@@ -265,7 +273,7 @@
     groups, rows = len(projected), projected[0].shape[1]
     total = None
     for k in range(groups):
-        at = pl.multiple_of(behind(me_ref[0], groups, k) * rows, rows)
+        at = pl.multiple_of(behind(*place_of(me_ref), groups, k) * rows, rows)
         term = dot(hits_ref[:, pl.ds(at, rows)], projected[k][...], LAST)
         total = term if total is None else total + term
     gap = mine_ref.shape[2] - total.shape[1]
@@ -286,7 +294,7 @@
     groups, rows = len(projected), projected[0].shape[1]
     total = None
     for k in range(groups):
-        at = pl.multiple_of(behind(me_ref[0], groups, k) * rows, rows)
+        at = pl.multiple_of(behind(*place_of(me_ref), groups, k) * rows, rows)
         term = dot(projected[k][...], band_ref[:, pl.ds(at, rows)], LAST)
         total = term if total is None else total + term
     out_ref[...] = total
@@ -297,7 +305,7 @@
     width = sums_ref.shape[1] - EXTRA
     arrived = jnp.concatenate([part[...].reshape(-1, part.shape[2]) for part in arrived], axis=0)
     far = dot(arrived, far_ref[...], FIRST)[: own_ref.shape[0]]
-    total = own_ref[...] + (near_ref[...] + far) / sums_ref[me_ref[0], width : width + 1, :]
+    total = own_ref[...] + (near_ref[...] + far) / sums_ref[me_ref[0] // 2, width : width + 1, :]
     out_ref[...] = total.reshape(out_ref.shape)
 
 
@@ -316,8 +324,9 @@
 ):
     feature_rows, tile_contents = features[0].T, tiles[0]
     groups, parts = lax.axis_size("feat"), lax.axis_size("dom")
-    me = lax.axis_index("feat").astype(jnp.int32).reshape(1)
-    part = lax.axis_index("dom").astype(jnp.int32).reshape(1)
+    part = lax.axis_index("dom").astype(jnp.int32)
+    me = (lax.axis_index("feat").astype(jnp.int32) * 2 + part % 2).reshape(1)
+    part = part.reshape(1)
     width, nodes = feature_rows.shape
     rows, slots = nodes // groups, sources.shape[3]
     hid, classes = self_one.shape[1], self_out.shape[1]
@@ -329,7 +338,13 @@
     def shift(blocks):
         return [
             lax.ppermute(
-                block, "feat", [(i, ahead(i, groups, k)) for i in range(groups)]
+                block,
+                ("feat", "dom"),
+                [
+                    (f * parts + d, ahead(f, d % 2, groups, k) * parts + d)
+                    for f in range(groups)
+                    for d in range(parts)
+                ],
             )
             for k, block in enumerate(blocks, 1)
         ]

time: 40.5 us -> 41.3 us (1.020)
  waiting for transfers between devices: 9.38 us -> 10.2 us
    ppermute x9, waiting for transfers between devices: 5.37 us -> 6.12 us  [shift(): lax.ppermute(block, ('feat', 'dom'), [(f * parts + d, ahead(f, d % 2, gro...]
  transfers between devices with their start and end apart: 14 -> 14, of which waited for: 10 -> 9; matrix products, arithmetic and copies ran while one was open for 0% -> 0% of each run, Pallas kernels for 10% -> 10%
where the time goes in v7:
time: 41.3 us; the launch traced here: 41 us
  starting transfers between devices  22 us (53%)
  waiting for transfers between devices  10.2 us (25%)
  Pallas kernels  8.02 us (19%)
  between operations  0.75 us (2%)
    ppermute x9, starting transfers between devices, shift(): lax.ppermute(block, ('feat', 'dom'), [(f * parts + d, ahead(f, d % 2, gro...  13.3 us
    pallas_call x10, Pallas kernels, placed(): run(*(pltpu.with_memory_space_constraint(value, pltpu.HBM) if spec is HB...  8.02 us
    ppermute x9, waiting for transfers between devices, shift(): lax.ppermute(block, ('feat', 'dom'), [(f * parts + d, ahead(f, d % 2, gro...  6.12 us
    all_to_all x1, starting transfers between devices, swap(): return lax.all_to_all(value, 'dom', split_axis=0, concat_axis=0, tiled=True)  5.18 us
    ppermute x3, starting transfers between devices, on_device(): lax.ppermute(arrived[j], 'dom', [(d, next_to(d // 2, j, chips) * 2 + d %...  3.49 us
    ppermute x3, waiting for transfers between devices, on_device(): lax.ppermute(arrived[j], 'dom', [(d, next_to(d // 2, j, chips) * 2 + d %...  2.01 us
    ppermute x1, waiting for transfers between devices, on_device(): mate = lax.ppermute(mate, 'dom', [(d, d ^ 1) for d in range(parts)])  1.19 us
    all_to_all x1, waiting for transfers between devices, swap(): return lax.all_to_all(value, 'dom', split_axis=0, concat_axis=0, tiled=True)  0.88 us
  transfers between devices with their start and end apart: 14, of which 9 were waited for; matrix products, arithmetic and copies ran while one was open for 0% of the time, Pallas kernels for 10%

profile of v7, /device:TPU:0, one launch (start us, length us, event | category | flops | bytes accessed | tf_op | source)
XLA Modules:
  0.0 41.0 jit_solution(16039821316288425131)
XLA Ops:
  0.6 0.0 copy-start.1
  0.7 2.2 %shard_map.122 = (bf16[8,64,256]{2,1,0:T(8,128)(2,1)}, bf16[192,128]{1,0:T(8,128)(2,1)S(1)}, bf16[192,128]{1,0:T(8,128)(2,1)S(1)}, bf16[192,128]{1,0:T(8,128)(2,1)S(1)}) custom-call(s32[1]{0:T(128)} %bitcast.me_ref, s32[8,4,16]{2,1,0:T(4,128)} %bitcast.26, bf16[192,512]{1,0:T(8,128)(2,1)} %bitcast.21), custom_call_target="tpu_custom_call" | custom-call | flops 100663296 | bytes 1048576 | tf_op jit(solution)/shard_map/pallas_call | solution.py:32
  2.8 5.2 %all-to-all-start = ((bf16[8,64,256]{2,1,0:T(8,128)(2,1)}), bf16[8,64,256]{2,1,0:T(8,128)(2,1)S(1)}, u32[]{:S(2)}, u32[]{:S(2)}) async-start(bf16[8,64,256]{2,1,0:T(8,128)(2,1)} %get-tuple-element.31), calls=%async_computation | async-start | bytes 524288 | tf_op jit(solution)/shard_map/all_to_all | solution.py:353
  8.0 3.6 %collective-permute-start = (bf16[192,128]{1,0:T(8,128)(2,1)S(1)}, bf16[192,128]{1,0:T(8,128)(2,1)S(1)}, u32[]{:S(2)}, u32[]{:S(2)}) collective-permute-start(bf16[192,128]{1,0:T(8,128)(2,1)S(1)} %get-tuple-element.28), channel_id=1, source_target_pairs={{0,24},{1,9},{2,26},{3,11},{4,28},{5,13},{6,30},{7,15},{8,16},{9,1... | collective-permute-start | bytes 147464 | tf_op jit(solution)/shard_map/ppermute | solution.py:340
  11.6 0.0 collective-permute-start.1
  11.6 0.8 %collective-permute-start.2 = (bf16[192,128]{1,0:T(8,128)(2,1)S(1)}, bf16[192,128]{1,0:T(8,128)(2,1)S(1)}, u32[]{:S(2)}, u32[]{:S(2)}) collective-permute-start(bf16[192,128]{1,0:T(8,128)(2,1)S(1)} %get-tuple-element.30), channel_id=1, source_target_pairs={{0,8},{1,17},{2,10},{3,19},{4,12},{5,21},{6,14},{7,23},{8,0},{9,25... | collective-permute-start | bytes 147464 | tf_op jit(solution)/shard_map/ppermute | solution.py:340
  12.4 1.7 %shard_map.124 = (f32[4,208,128]{2,1,0:T(8,128)S(1)}, bf16[4,8,16,128]{3,2,1,0:T(8,128)(2,1)S(1)}, bf16[128,512]{1,0:T(8,128)(2,1)S(1)}, bf16[128,512]{1,0:T(8,128)(2,1)S(1)}, bf16[128,128]{1,0:T(8,128)(2,1)S(1)}) custom-call(s32[1]{0:T(128)} %bitcast.me_ref, s32[1]{0:T(128)} %bitcast.6.part_ref, s32[2,12]{1,0:T(2,128)} %bitcast.31, s32[4,8]{1,0:T(4,128)} %bitcast.30, ...), custom_call_target="tpu_custom_call" | custom-call | flops 100663296 | bytes 1048576 | tf_op jit(solution)/shard_map/pallas_call | solution.py:32
  14.1 0.9 %all-to-all-done.incoming_ref = bf16[8,64,256]{2,1,0:T(8,128)(2,1)S(1)} async-done(((bf16[8,64,256]{2,1,0:T(8,128)(2,1)}), bf16[8,64,256]{2,1,0:T(8,128)(2,1)S(1)}, u32[]{:S(2)}, u32[]{:S(2)}) %all-to-all-start) | async-done | bytes 262176 | tf_op jit(solution)/shard_map/all_to_all | solution.py:353
  14.9 0.0 copy-start
  14.9 0.0 copy-start.3
  14.9 0.3 shard_map.125
  15.2 3.7 %collective-permute-start.3 = (bf16[192,128]{1,0:T(8,128)(2,1)S(1)}, bf16[192,128]{1,0:T(8,128)(2,1)S(1)}, u32[]{:S(2)}, u32[]{:S(2)}) collective-permute-start(bf16[192,128]{1,0:T(8,128)(2,1)S(1)} %get-tuple-element.35), channel_id=1, source_target_pairs={{0,24},{1,9},{2,26},{3,11},{4,28},{5,13},{6,30},{7,15},{8,16},{9,1... | collective-permute-start | bytes 147464 | tf_op jit(solution)/shard_map/ppermute | solution.py:340
  18.9 0.0 collective-permute-start.4
  18.9 0.0 collective-permute-done.rest_0_
  18.9 0.8 %collective-permute-start.5 = (bf16[192,128]{1,0:T(8,128)(2,1)S(1)}, bf16[192,128]{1,0:T(8,128)(2,1)S(1)}, u32[]{:S(2)}, u32[]{:S(2)}) collective-permute-start(bf16[192,128]{1,0:T(8,128)(2,1)S(1)} %get-tuple-element.37), channel_id=1, source_target_pairs={{0,8},{1,17},{2,10},{3,19},{4,12},{5,21},{6,14},{7,23},{8,0},{9,25... | collective-permute-start | bytes 147464 | tf_op jit(solution)/shard_map/ppermute | solution.py:340
  19.7 0.0 collective-permute-done.1.rest_1_
  19.7 0.0 collective-permute-done.2.rest_2_
  19.7 0.0 copy-done.1
  19.7 1.2 %shard_map.123.own_ref = f32[128,1024]{1,0:T(8,128)S(1)} custom-call(s32[1]{0:T(128)} %bitcast.me_ref, bf16[192,512]{1,0:T(8,128)(2,1)} %bitcast.23, bf16[768,1024]{1,0:T(8,128)(2,1)S(1)} %copy-done.1, bf16[192,128]{1,0:T(8,128)(2,1)S(1)} %collective-permute-done.rest_0_, bf16[192,128]{1,0:T(8,128)(2,1)S(1)} %collective-permute-done.1.rest_1_, ...), custom_call_target="tpu_custom_call" | custom-call | flops 201326592 | bytes 2097152 | tf_op jit(solution)/shard_map/pallas_call | solution.py:32
  20.9 0.0 copy-start.2
  20.9 0.4 collective-permute-done.3.rest_1_
  21.3 2.6 %collective-permute-done.4.rest_2_ = bf16[192,128]{1,0:T(8,128)(2,1)S(1)} collective-permute-done((bf16[192,128]{1,0:T(8,128)(2,1)S(1)}, bf16[192,128]{1,0:T(8,128)(2,1)S(1)}, u32[]{:S(2)}, u32[]{:S(2)}) %collective-permute-start.4) | collective-permute-done | bytes 49184 | tf_op jit(solution)/shard_map/ppermute | solution.py:340
  23.9 0.0 collective-permute-done.5.rest_3_
  23.9 0.0 copy-done
  23.9 0.0 copy-done.3
  23.9 0.7 %shard_map.126 = (bf16[128,1024]{1,0:T(8,128)(2,1)S(1)}, bf16[153,128]{1,0:T(8,128)(2,1)S(1)}, bf16[153,128]{1,0:T(8,128)(2,1)S(1)}, bf16[153,128]{1,0:T(8,128)(2,1)S(1)}, bf16[153,128]{1,0:T(8,128)(2,1)S(1)}) custom-call(s32[1]{0:T(128)} %bitcast.me_ref, bf16[768,1024]{1,0:T(8,128)(2,1)S(1)} %copy-done, bf16[153,1024]{1,0:T(8,128)(2,1)S(1)} %bitcast.20, ...), custom_call_target="tpu_custom_call" | custom-call | flops 201326592 | bytes 2097152 | tf_op jit(solution)/shard_map/pallas_call | solution.py:32
  24.6 2.3 %collective-permute-start.6 = (bf16[153,128]{1,0:T(8,128)(2,1)S(1)}, bf16[153,128]{1,0:T(8,128)(2,1)S(1)}, u32[]{:S(2)}, u32[]{:S(2)}) collective-permute-start(bf16[153,128]{1,0:T(8,128)(2,1)S(1)} %get-tuple-element.43), channel_id=1, source_target_pairs={{0,24},{1,9},{2,26},{3,11},{4,28},{5,13},{6,30},{7,15},{8,16},{9,1... | collective-permute-start | bytes 117512 | tf_op jit(solution)/shard_map/ppermute | solution.py:340
  26.8 0.0 collective-permute-start.7
  26.8 2.2 %collective-permute-start.8 = (bf16[153,128]{1,0:T(8,128)(2,1)S(1)}, bf16[153,128]{1,0:T(8,128)(2,1)S(1)}, u32[]{:S(2)}, u32[]{:S(2)}) collective-permute-start(bf16[153,128]{1,0:T(8,128)(2,1)S(1)} %get-tuple-element.45), channel_id=1, source_target_pairs={{0,8},{1,17},{2,10},{3,19},{4,12},{5,21},{6,14},{7,23},{8,0},{9,25... | collective-permute-start | bytes 117512 | tf_op jit(solution)/shard_map/ppermute | solution.py:340
  29.0 1.8 %collective-permute-done.6.rest_1_ = bf16[153,128]{1,0:T(8,128)(2,1)S(1)} collective-permute-done((bf16[153,128]{1,0:T(8,128)(2,1)S(1)}, bf16[153,128]{1,0:T(8,128)(2,1)S(1)}, u32[]{:S(2)}, u32[]{:S(2)}) %collective-permute-start.6) | collective-permute-done | bytes 39200 | tf_op jit(solution)/shard_map/ppermute | solution.py:340
  30.8 1.4 %collective-permute-done.7.rest_2_ = bf16[153,128]{1,0:T(8,128)(2,1)S(1)} collective-permute-done((bf16[153,128]{1,0:T(8,128)(2,1)S(1)}, bf16[153,128]{1,0:T(8,128)(2,1)S(1)}, u32[]{:S(2)}, u32[]{:S(2)}) %collective-permute-start.7) | collective-permute-done | bytes 39200 | tf_op jit(solution)/shard_map/ppermute | solution.py:340
  32.2 0.0 collective-permute-done.8.rest_3_
  32.2 0.2 shard_map.129
  32.4 0.1 collective-permute-start.9
  32.5 1.2 %collective-permute-done.9.got_ref = bf16[4,16,256]{2,1,0:T(8,128)(2,1)S(1)} collective-permute-done((bf16[4,16,256]{2,1,0:T(8,128)(2,1)S(1)}, bf16[4,16,256]{2,1,0:T(8,128)(2,1)S(1)}, u32[]{:S(2)}, u32[]{:S(2)}) %collective-permute-start.9) | collective-permute-done | bytes 32800 | tf_op jit(solution)/shard_map/ppermute | solution.py:441
  33.7 2.1 %collective-permute-start.10 = (bf16[2,16,256]{2,1,0:T(8,128)(2,1)S(1)}, bf16[2,16,256]{2,1,0:T(8,128)(2,1)S(1)}, u32[]{:S(2)}, u32[]{:S(2)}) collective-permute-start(bf16[2,16,256]{2,1,0:T(8,128)(2,1)S(1)} %get-tuple-element.51), channel_id=1, source_target_pairs={{0,6},{1,7},{2,4},{3,5},{4,2},{5,3},{6,0},{7,1},{8,14},{9,15},{10,... | collective-permute-start | bytes 49160 | tf_op jit(solution)/shard_map/ppermute | solution.py:446
  35.9 0.6 %collective-permute-start.11 = (bf16[2,16,256]{2,1,0:T(8,128)(2,1)S(1)}, bf16[2,16,256]{2,1,0:T(8,128)(2,1)S(1)}, u32[]{:S(2)}, u32[]{:S(2)}) collective-permute-start(bf16[2,16,256]{2,1,0:T(8,128)(2,1)S(1)} %get-tuple-element.52), channel_id=1, source_target_pairs={{0,4},{1,5},{2,6},{3,7},{4,0},{5,1},{6,2},{7,3},{8,12},{9,13},{10,... | collective-permute-start | bytes 49160 | tf_op jit(solution)/shard_map/ppermute | solution.py:446
  36.4 0.8 %collective-permute-start.12 = (bf16[2,16,256]{2,1,0:T(8,128)(2,1)S(1)}, bf16[2,16,256]{2,1,0:T(8,128)(2,1)S(1)}, u32[]{:S(2)}, u32[]{:S(2)}) collective-permute-start(bf16[2,16,256]{2,1,0:T(8,128)(2,1)S(1)} %get-tuple-element.53), channel_id=1, source_target_pairs={{0,2},{1,3},{2,0},{3,1},{4,6},{5,7},{6,4},{7,5},{8,10},{9,11},{10,... | collective-permute-start | bytes 49160 | tf_op jit(solution)/shard_map/ppermute | solution.py:446
  37.2 0.0 copy-done.2
  37.2 0.7 %shard_map.127 = (f32[153,128]{1,0:T(8,128)S(1)}, bf16[128,1024]{1,0:T(8,128)(2,1)}) custom-call(bf16[128,1024]{1,0:T(8,128)(2,1)S(1)} %get-tuple-element.38.hidden_ref, bf16[153,1024]{1,0:T(8,128)(2,1)S(1)} %bitcast.19), custom_call_target="tpu_custom_call" | custom-call | flops 40108032 | bytes 1048576 | tf_op jit(solution)/shard_map/pallas_call | solution.py:32
  37.9 0.2 shard_map.128.near_ref
  38.2 0.2 collective-permute-done.10.rest_1_
  38.3 1.2 %collective-permute-done.11.rest_2_ = bf16[2,16,256]{2,1,0:T(8,128)(2,1)S(1)} collective-permute-done((bf16[2,16,256]{2,1,0:T(8,128)(2,1)S(1)}, bf16[2,16,256]{2,1,0:T(8,128)(2,1)S(1)}, u32[]{:S(2)}, u32[]{:S(2)}) %collective-permute-start.11) | collective-permute-done | bytes 16416 | tf_op jit(solution)/shard_map/ppermute | solution.py:446
  39.6 0.6 %collective-permute-done.12.rest_3_ = bf16[2,16,256]{2,1,0:T(8,128)(2,1)S(1)} collective-permute-done((bf16[2,16,256]{2,1,0:T(8,128)(2,1)S(1)}, bf16[2,16,256]{2,1,0:T(8,128)(2,1)S(1)}, u32[]{:S(2)}, u32[]{:S(2)}) %collective-permute-start.12) | collective-permute-done | bytes 16416 | tf_op jit(solution)/shard_map/ppermute | solution.py:446
  40.2 0.9 %shard_map.131 = f32[153,1,128]{2,1,0:T(1,128)} custom-call(s32[1]{0:T(128)} %bitcast.me_ref, f32[153,128]{1,0:T(8,128)S(1)} %get-tuple-element.40.own_ref, f32[153,128]{1,0:T(8,128)S(1)} %shard_map.128.near_ref, bf16[128,128]{1,0:T(8,128)(2,1)S(1)} %get-tuple-element.46.far_ref, f32[4,208,128]{2,1,0:T(8,128)S(1)} %get-tuple-element.32.sums_ref, ...), custom_call_target="tpu_custom_call" | custom-call | flops 5013504 | bytes 524288 | tf_op jit(solution)/shard_map/pallas_call | solution.py:32
  (1 shorter events, 0.0 us)
Async XLA Ops:
  0.6 19.0 %copy-start.1 = (bf16[768,1024]{1,0:T(8,128)(2,1)S(1)}, bf16[768,1024]{1,0:T(8,128)(2,1)}, u32[]{:S(2)}) copy-start(bf16[768,1024]{1,0:T(8,128)(2,1)} %weight_ref.2) | copy-start | bytes 4718596
  2.8 12.1 %all-to-all-start = ((bf16[8,64,256]{2,1,0:T(8,128)(2,1)}), bf16[8,64,256]{2,1,0:T(8,128)(2,1)S(1)}, u32[]{:S(2)}, u32[]{:S(2)}) async-start(bf16[8,64,256]{2,1,0:T(8,128)(2,1)} %get-tuple-element.31), calls=%async_computation | async-start | bytes 524288 | tf_op jit(solution)/shard_map/all_to_all | solution.py:353
  8.0 10.9 %collective-permute-start = (bf16[192,128]{1,0:T(8,128)(2,1)S(1)}, bf16[192,128]{1,0:T(8,128)(2,1)S(1)}, u32[]{:S(2)}, u32[]{:S(2)}) collective-permute-start(bf16[192,128]{1,0:T(8,128)(2,1)S(1)} %get-tuple-element.28), channel_id=1, source_target_pairs={{0,24},{1,9},{2,26},{3,11},{4,28},{5,13},{6,30},{7,15},{8,16},{9,1... | collective-permute-start | bytes 147464 | tf_op jit(solution)/shard_map/ppermute | solution.py:340
  11.6 8.1 %collective-permute-start.1 = (bf16[192,128]{1,0:T(8,128)(2,1)S(1)}, bf16[192,128]{1,0:T(8,128)(2,1)S(1)}, u32[]{:S(2)}, u32[]{:S(2)}) collective-permute-start(bf16[192,128]{1,0:T(8,128)(2,1)S(1)} %get-tuple-element.29), channel_id=1, source_target_pairs={{0,16},{1,25},{2,18},{3,27},{4,20},{5,29},{6,22},{7,31},{8,24},{9,... | collective-permute-start | bytes 147464 | tf_op jit(solution)/shard_map/ppermute | solution.py:340
  11.6 8.1 %collective-permute-start.2 = (bf16[192,128]{1,0:T(8,128)(2,1)S(1)}, bf16[192,128]{1,0:T(8,128)(2,1)S(1)}, u32[]{:S(2)}, u32[]{:S(2)}) collective-permute-start(bf16[192,128]{1,0:T(8,128)(2,1)S(1)} %get-tuple-element.30), channel_id=1, source_target_pairs={{0,8},{1,17},{2,10},{3,19},{4,12},{5,21},{6,14},{7,23},{8,0},{9,25... | collective-permute-start | bytes 147464 | tf_op jit(solution)/shard_map/ppermute | solution.py:340
  14.9 8.9 %copy-start = (bf16[768,1024]{1,0:T(8,128)(2,1)S(1)}, bf16[768,1024]{1,0:T(8,128)(2,1)}, u32[]{:S(2)}) copy-start(bf16[768,1024]{1,0:T(8,128)(2,1)} %weight_ref.3) | copy-start | bytes 4718596
  14.9 8.9 %copy-start.3 = (bf16[1024,153]{0,1:T(8,128)(2,1)S(1)}, bf16[1024,153]{0,1:T(8,128)(2,1)}, u32[]{:S(2)}) copy-start(bf16[1024,153]{0,1:T(8,128)(2,1)} %param.21) | copy-start | bytes 940036
  15.2 6.1 %collective-permute-start.3 = (bf16[192,128]{1,0:T(8,128)(2,1)S(1)}, bf16[192,128]{1,0:T(8,128)(2,1)S(1)}, u32[]{:S(2)}, u32[]{:S(2)}) collective-permute-start(bf16[192,128]{1,0:T(8,128)(2,1)S(1)} %get-tuple-element.35), channel_id=1, source_target_pairs={{0,24},{1,9},{2,26},{3,11},{4,28},{5,13},{6,30},{7,15},{8,16},{9,1... | collective-permute-start | bytes 147464 | tf_op jit(solution)/shard_map/ppermute | solution.py:340
  18.9 5.0 %collective-permute-start.4 = (bf16[192,128]{1,0:T(8,128)(2,1)S(1)}, bf16[192,128]{1,0:T(8,128)(2,1)S(1)}, u32[]{:S(2)}, u32[]{:S(2)}) collective-permute-start(bf16[192,128]{1,0:T(8,128)(2,1)S(1)} %get-tuple-element.36), channel_id=1, source_target_pairs={{0,16},{1,25},{2,18},{3,27},{4,20},{5,29},{6,22},{7,31},{8,24},{9,... | collective-permute-start | bytes 147464 | tf_op jit(solution)/shard_map/ppermute | solution.py:340
  18.9 5.0 %collective-permute-start.5 = (bf16[192,128]{1,0:T(8,128)(2,1)S(1)}, bf16[192,128]{1,0:T(8,128)(2,1)S(1)}, u32[]{:S(2)}, u32[]{:S(2)}) collective-permute-start(bf16[192,128]{1,0:T(8,128)(2,1)S(1)} %get-tuple-element.37), channel_id=1, source_target_pairs={{0,8},{1,17},{2,10},{3,19},{4,12},{5,21},{6,14},{7,23},{8,0},{9,25... | collective-permute-start | bytes 147464 | tf_op jit(solution)/shard_map/ppermute | solution.py:340
  20.9 16.3 %copy-start.2 = (bf16[1024,153]{0,1:T(8,128)(2,1)S(1)}, bf16[1024,153]{0,1:T(8,128)(2,1)}, u32[]{:S(2)}) copy-start(bf16[1024,153]{0,1:T(8,128)(2,1)} %param.20) | copy-start | bytes 940036
  24.6 6.2 %collective-permute-start.6 = (bf16[153,128]{1,0:T(8,128)(2,1)S(1)}, bf16[153,128]{1,0:T(8,128)(2,1)S(1)}, u32[]{:S(2)}, u32[]{:S(2)}) collective-permute-start(bf16[153,128]{1,0:T(8,128)(2,1)S(1)} %get-tuple-element.43), channel_id=1, source_target_pairs={{0,24},{1,9},{2,26},{3,11},{4,28},{5,13},{6,30},{7,15},{8,16},{9,1... | collective-permute-start | bytes 117512 | tf_op jit(solution)/shard_map/ppermute | solution.py:340
  26.8 5.3 %collective-permute-start.7 = (bf16[153,128]{1,0:T(8,128)(2,1)S(1)}, bf16[153,128]{1,0:T(8,128)(2,1)S(1)}, u32[]{:S(2)}, u32[]{:S(2)}) collective-permute-start(bf16[153,128]{1,0:T(8,128)(2,1)S(1)} %get-tuple-element.44), channel_id=1, source_target_pairs={{0,16},{1,25},{2,18},{3,27},{4,20},{5,29},{6,22},{7,31},{8,24},{9,... | collective-permute-start | bytes 117512 | tf_op jit(solution)/shard_map/ppermute | solution.py:340
  26.8 5.3 %collective-permute-start.8 = (bf16[153,128]{1,0:T(8,128)(2,1)S(1)}, bf16[153,128]{1,0:T(8,128)(2,1)S(1)}, u32[]{:S(2)}, u32[]{:S(2)}) collective-permute-start(bf16[153,128]{1,0:T(8,128)(2,1)S(1)} %get-tuple-element.45), channel_id=1, source_target_pairs={{0,8},{1,17},{2,10},{3,19},{4,12},{5,21},{6,14},{7,23},{8,0},{9,25... | collective-permute-start | bytes 117512 | tf_op jit(solution)/shard_map/ppermute | solution.py:340
  32.4 1.3 %collective-permute-start.9 = (bf16[4,16,256]{2,1,0:T(8,128)(2,1)S(1)}, bf16[4,16,256]{2,1,0:T(8,128)(2,1)S(1)}, u32[]{:S(2)}, u32[]{:S(2)}) collective-permute-start(bf16[4,16,256]{2,1,0:T(8,128)(2,1)S(1)} %get-tuple-element.49), channel_id=1, source_target_pairs={{0,1},{1,0},{2,3},{3,2},{4,5},{5,4},{6,7},{7,6},{8,9},{9,8},{10,11... | collective-permute-start | bytes 98312 | tf_op jit(solution)/shard_map/ppermute | solution.py:441
  33.7 4.6 %collective-permute-start.10 = (bf16[2,16,256]{2,1,0:T(8,128)(2,1)S(1)}, bf16[2,16,256]{2,1,0:T(8,128)(2,1)S(1)}, u32[]{:S(2)}, u32[]{:S(2)}) collective-permute-start(bf16[2,16,256]{2,1,0:T(8,128)(2,1)S(1)} %get-tuple-element.51), channel_id=1, source_target_pairs={{0,6},{1,7},{2,4},{3,5},{4,2},{5,3},{6,0},{7,1},{8,14},{9,15},{10,... | collective-permute-start | bytes 49160 | tf_op jit(solution)/shard_map/ppermute | solution.py:446
  35.9 3.7 %collective-permute-start.11 = (bf16[2,16,256]{2,1,0:T(8,128)(2,1)S(1)}, bf16[2,16,256]{2,1,0:T(8,128)(2,1)S(1)}, u32[]{:S(2)}, u32[]{:S(2)}) collective-permute-start(bf16[2,16,256]{2,1,0:T(8,128)(2,1)S(1)} %get-tuple-element.52), channel_id=1, source_target_pairs={{0,4},{1,5},{2,6},{3,7},{4,0},{5,1},{6,2},{7,3},{8,12},{9,13},{10,... | collective-permute-start | bytes 49160 | tf_op jit(solution)/shard_map/ppermute | solution.py:446
  36.4 3.7 %collective-permute-start.12 = (bf16[2,16,256]{2,1,0:T(8,128)(2,1)S(1)}, bf16[2,16,256]{2,1,0:T(8,128)(2,1)S(1)}, u32[]{:S(2)}, u32[]{:S(2)}) collective-permute-start(bf16[2,16,256]{2,1,0:T(8,128)(2,1)S(1)} %get-tuple-element.53), channel_id=1, source_target_pairs={{0,2},{1,3},{2,0},{3,1},{4,6},{5,7},{6,4},{7,5},{8,10},{9,11},{10,... | collective-permute-start | bytes 49160 | tf_op jit(solution)/shard_map/ppermute | solution.py:446

commit v8 on v6

--- a/solution.py
+++ b/solution.py
@@ -82,12 +82,13 @@
     return values.reshape(-1, values.shape[-1]).T
 
 
-def gather_kernel(chunk, me_ref, sources_hbm, features_hbm, out_ref, *rest):
-    blocks, (sources_ref, features_ref, hits, sems) = rest[:-4], rest[-4:]
+def gather_kernel(chunk, me_ref, part_ref, sources_hbm, features_hbm, mine_ref, mate_ref, *rest):
+    blocks, (sources_ref, features_ref, order, hits, sems) = rest[:-5], rest[-5:]
     parts, groups, slots = sources_ref.shape
     nodes = hits.shape[1]
     rows = nodes // groups
     width = features_hbm.shape[0]
+    chips, chip, core = parts // 2, part_ref[0] // 2, part_ref[0] % 2
     indices, table = fetch(
         sems, (sources_hbm, sources_ref), (features_hbm, features_ref.at[pl.ds(0, width), :])
     )
@@ -96,8 +97,10 @@
     indices.wait()
     lane = lax.broadcasted_iota(jnp.int32, (slots, nodes), 1)
 
-    def step(i, last):
-        columns = columns_of(sources_ref[pl.ds(i * chunk, chunk)])
+    def step(i, out, other, last):
+        for j in range(chunk):
+            order[j] = sources_ref[next_to(chip, i * chunk + j, chips) * 2 + (core ^ other)]
+        columns = columns_of(order[...])
         for n in range(chunk * groups):
             hits[n * slots : (n + 1) * slots, :] = jnp.where(
                 columns[:, n : n + 1] == lane, 1.0, 0.0
@@ -105,13 +108,15 @@
         if last:
             table.wait()
         picked = dot(hits[...], features_ref[...], LAST).astype(bf16)
-        out_ref[pl.ds(i * chunk, chunk)] = picked.reshape(chunk, groups * slots, -1)
-
-    if parts == chunk:
-        step(0, True)
+        out[pl.ds(i * chunk, chunk)] = picked.reshape(chunk, groups * slots, -1)
+
+    if chips == chunk:
+        step(0, mate_ref, 1, True)
+        step(0, mine_ref, 0, False)
     else:
         table.wait()
-        lax.fori_loop(0, parts // chunk, lambda i, _: step(i, False), None)
+        for other, out in enumerate((mine_ref, mate_ref)):
+            lax.fori_loop(0, chips // chunk, lambda i, _: step(i, out, other, False), None)
     for k in range(1, groups):
         group = ahead(me_ref[0], groups, k)
         blocks[k - 1][...] = features_ref[:width, pl.ds(pl.multiple_of(group * rows, rows), rows)]
@@ -132,7 +137,6 @@
     edges_ref,
     band_ref,
     hits_ref,
-    far_ref,
     ids_ref,
     counts_ref,
     features_ref,
@@ -174,6 +178,7 @@
     band_ref[...] = bands[me]
     lane = lax.broadcasted_iota(jnp.int32, (slots, rows), 1)
     slot = lax.broadcasted_iota(jnp.int32, (slots, rows), 0)
+    chips, chip, core = parts // 2, part_ref[0] // 2, part_ref[0] % 2
 
     def connect(i, _):
         first = i * chunk
@@ -182,10 +187,11 @@
         for g in range(groups):
             degree = jnp.zeros((1, rows), f32)
             for e in range(chunk):
-                n = e * groups + g
+                n, d = e * groups + g, first + e
+                at = step_to(d // 2, chip, chips) * 2 + ((d % 2) ^ core)
                 hit = (target[:, n : n + 1] == lane) & (slot < counts_ref[g, first + e])
                 values = jnp.where(hit, weight[:, n : n + 1], 0.0)
-                edges_ref[g, first + e] = values.astype(bf16)
+                edges_ref[g, at] = values.astype(bf16)
                 degree = degree + jnp.sum(values, axis=0, keepdims=True)
             sums_ref[g, width : width + 1, :] += degree
         return 0
@@ -197,54 +203,59 @@
     mine = lax.broadcasted_iota(jnp.int32, sources_ref.shape, 1) == me
     picks = jnp.sum(jnp.where(mine, sources_ref[...], 0), axis=1).T
     lane = lax.broadcasted_iota(jnp.int32, (slots, hits_ref.shape[1]), 1)
-    chips, chip, core = parts // 2, part_ref[0] // 2, part_ref[0] % 2
     for d in range(parts):
         other = (d % 2) ^ core
         to = other * chips + step_to(chip, d // 2, chips)
         hits_ref[pl.ds(pl.multiple_of(to * slots, slots), slots), :] = jnp.where(
             picks[:, d : d + 1] == lane, 1.0, 0.0
         ).astype(bf16)
-        at = step_to(d // 2, chip, chips) * 2 + other
-        far_ref[pl.ds(pl.multiple_of(at * slots, slots), slots), :] = edges_ref[me, d]
-
-
-def mean_kernel(me_ref, incoming_ref, sums_ref, edges_ref, *outs):
+
+
+def mean_kernel(late, me_ref, sums_ref, edges_ref, *rest):
     groups, parts, slots, rows = edges_ref.shape
+    arrived, held, outs = rest[: parts // 2], rest[parts // 2 :][:late], rest[parts // 2 + late :]
     width = outs[0].shape[0]
     for k in range(groups):
         group = ahead(me_ref[0], groups, k)
-        arrived = incoming_ref[:, pl.ds(pl.multiple_of(group * slots, slots), slots), :]
-        arrived = arrived.reshape(parts * slots, -1)
-        far = dot(arrived, edges_ref[group].reshape(parts * slots, rows), FIRST)
+        span = pl.ds(pl.multiple_of(group * slots, slots), slots)
+        far = jnp.concatenate([x[:, span, :].reshape(2 * slots, -1) for x in arrived], axis=0)
+        far = dot(far, edges_ref[group].reshape(parts * slots, rows), FIRST)
         total = sums_ref[group, :width, :] + far[:width]
         outs[k][...] = (total / sums_ref[group, width : width + 1, :]).astype(bf16)
-
-
-def self_kernel(me_ref, features_hbm, weight_ref, *rest):
-    parts, (out_ref, own_ref, sem) = rest[:-3], rest[-3:]
-    groups, (width, rows) = len(parts) + 1, own_ref.shape
+    for block, out in zip(held, outs[groups:]):
+        out[...] = block[...]
+
+
+def rows_from(me, groups, k, width):
+    return pl.ds(pl.multiple_of(behind(me, groups, k) * width, width), width)
+
+
+def self_kernel(groups, me_ref, features_hbm, weight_ref, *rest):
+    early, (out_ref, own_ref, sem) = rest[:-3], rest[-3:]
+    width, rows = own_ref.shape
     me = me_ref[0]
     own = pltpu.make_async_copy(
         features_hbm.at[:, pl.ds(pl.multiple_of(me * rows, rows), rows)], own_ref, sem
     )
     own.start()
     total = jnp.zeros(out_ref.shape, f32)
-    for k in range(1, groups):
-        span = pl.ds(pl.multiple_of(behind(me, groups, k) * width, width), width)
-        total = total + dot(parts[k - 1][...], weight_ref[span, :], FIRST)
+    for k, block in enumerate(early, 1):
+        total = total + dot(block[...], weight_ref[rows_from(me, groups, k, width), :], FIRST)
     own.wait()
     span = pl.ds(pl.multiple_of(me * width, width), width)
     out_ref[...] = total + dot(own_ref[...], weight_ref[span, :], FIRST)
 
 
-def hidden_kernel(me_ref, weight_ref, out_weight_ref, own_ref, *rest):
-    groups = len(rest) // 2
-    parts, hidden_ref, copies = rest[:groups], rest[groups], rest[groups + 1 :]
+def hidden_kernel(groups, late, me_ref, self_weight_ref, weight_ref, out_weight_ref, own_ref, *rest):
+    held, parts, (hidden_ref, *copies) = rest[:late], rest[late:][:groups], rest[late + groups :]
     width = parts[0].shape[0]
+    me = me_ref[0]
     total = own_ref[...]
-    for k in range(len(parts)):
-        source = behind(me_ref[0], len(parts), k)
-        span = pl.ds(pl.multiple_of(source * width, width), width)
+    for k, block in enumerate(held, groups - late):
+        span = rows_from(me, groups, k, width)
+        total = total + dot(block[...], self_weight_ref[span, :], FIRST)
+    for k in range(groups):
+        span = rows_from(me, groups, k, width)
         total = total + dot(parts[k][...], weight_ref[span, :], FIRST)
     hidden = jnp.maximum(total, 0.0).astype(bf16)
     hidden_ref[...] = hidden
@@ -275,10 +286,15 @@
     mate_ref[...] = total[half:].reshape(mate_ref.shape)
 
 
-def pair_kernel(mine_ref, got_ref, *outs):
-    for j, out in enumerate(outs):
+def pair_kernel(after, mine_ref, got_ref, *rest):
+    del after
+    chips = mine_ref.shape[0]
+    held = (len(rest) - chips) // 2
+    for j, out in enumerate(rest[held : held + chips]):
         out[0] = mine_ref[j]
         out[1] = got_ref[j]
+    for block, out in zip(rest[:held], rest[held + chips :]):
+        out[...] = block[...]
 
 
 def near_kernel(me_ref, band_ref, *rest):
@@ -292,12 +308,14 @@
     out_ref[...] = total
 
 
-def last_kernel(me_ref, own_ref, near_ref, far_ref, sums_ref, *rest):
+def last_kernel(me_ref, own_ref, near_ref, edges_ref, sums_ref, *rest):
     arrived, out_ref = rest[:-1], rest[-1]
-    width = sums_ref.shape[1] - EXTRA
-    arrived = jnp.concatenate([part[...].reshape(-1, part.shape[2]) for part in arrived], axis=0)
-    far = dot(arrived, far_ref[...], FIRST)[: own_ref.shape[0]]
-    total = own_ref[...] + (near_ref[...] + far) / sums_ref[me_ref[0], width : width + 1, :]
+    groups, parts, slots, rows = edges_ref.shape
+    me, width = me_ref[0], sums_ref.shape[1] - EXTRA
+    arrived = jnp.concatenate([x[...].reshape(2 * slots, -1) for x in arrived], axis=0)
+    far = dot(arrived, edges_ref[me].reshape(parts * slots, rows), FIRST)
+    far = far[: own_ref.shape[0]]
+    total = own_ref[...] + (near_ref[...] + far) / sums_ref[me, width : width + 1, :]
     out_ref[...] = total.reshape(out_ref.shape)
 
 
@@ -321,46 +339,57 @@
     width, nodes = feature_rows.shape
     rows, slots = nodes // groups, sources.shape[3]
     hid, classes = self_one.shape[1], self_out.shape[1]
+    chips, late = parts // 2, 1
     chunk = max(1, min(parts, 512 // (groups * slots)))
 
     def shape(*dims, dtype=bf16):
         return jax.ShapeDtypeStruct(dims, dtype)
 
-    def shift(blocks):
+    def shift(blocks, first=1):
         return [
             lax.ppermute(
                 block, "feat", [(i, ahead(i, groups, k)) for i in range(groups)]
             )
-            for k, block in enumerate(blocks, 1)
+            for k, block in enumerate(blocks, first)
         ]
 
-    def swap(value):
-        return lax.all_to_all(value, "dom", split_axis=0, concat_axis=0, tiled=True)
-
-    sent, *feature_blocks = call(
-        functools.partial(gather_kernel, chunk),
-        (shape(parts, groups * slots, whole_lanes(width)),)
-        + (shape(width, rows),) * (groups - 1),
-        [SM, HB, HB],
+    def to_mate(value):
+        return lax.ppermute(value, "dom", [(d, d ^ 1) for d in range(parts)])
+
+    def to_chips(blocks):
+        return [blocks[0]] + [
+            lax.ppermute(
+                blocks[j],
+                "dom",
+                [(d, next_to(d // 2, j, chips) * 2 + d % 2) for d in range(parts)],
+            )
+            for j in range(1, chips)
+        ]
+
+    picked = min(chips, chunk)
+    lanes = whole_lanes(width)
+    mine, mate, *feature_blocks = call(
+        functools.partial(gather_kernel, picked),
+        (shape(chips, groups * slots, lanes),) * 2 + (shape(width, rows),) * (groups - 1),
+        [SM, SM, HB, HB],
         [
             pltpu.VMEM((parts, groups, slots), jnp.int32),
-            pltpu.VMEM((whole_lanes(width), nodes), bf16),
-            pltpu.VMEM((chunk * groups * slots, nodes), bf16),
+            pltpu.VMEM((lanes, nodes), bf16),
+            pltpu.VMEM((picked, groups, slots), jnp.int32),
+            pltpu.VMEM((picked * groups * slots, nodes), bf16),
             pltpu.SemaphoreType.DMA((2,)),
         ],
         2 * nodes * nodes * width,
         1 << 20,
-    )(me, sources[0], feature_rows)
-    incoming = swap(sent)
-    feature_blocks = shift(feature_blocks)
-    sums, edges, band, hits, far = call(
+    )(me, part, sources[0], feature_rows)
+    mate = to_mate(mate)
+    sums, edges, band, hits = call(
         functools.partial(local_kernel, chunk),
         (
             shape(groups, width + EXTRA, rows, dtype=f32),
             shape(groups, parts, slots, rows),
             shape(rows, nodes),
             shape(parts * slots, nodes),
-            shape(parts * slots, rows),
         ),
         [SM, SM] + [HB] * 7,
         [
@@ -388,33 +417,43 @@
         edge_weight[0],
         sources[0],
     )
-    own_mean, *means = call(
-        mean_kernel,
-        (shape(width, rows),) * groups,
-        [SM, VM, VM, VM],
+    paired = call(
+        pair_kernel,
+        (shape(2, groups * slots, lanes),) * chips + (shape(width, rows),) * (groups - 1 - late),
+        [VM] * (2 + groups - late),
+        (),
+        0,
+        1 << 20,
+    )(hits, mine, mate, *feature_blocks[: groups - 1 - late])
+    arrived = to_chips(paired[:chips])
+    early_blocks = shift(paired[chips:])
+    moved = call(
+        functools.partial(mean_kernel, late),
+        (shape(width, rows),) * (groups + late),
+        [SM] + [VM] * (2 + chips + late),
         (),
         2 * nodes * parts * slots * width,
         1 << 20,
-    )(me, incoming, sums, edges)
-    means = shift(means)
+    )(me, sums, edges, *arrived, *feature_blocks[groups - 1 - late :])
+    means = [moved[0]] + shift(moved[1:groups])
+    late_blocks = shift(moved[groups:], groups - late)
     own = call(
-        self_kernel,
+        functools.partial(self_kernel, groups),
         shape(rows, hid, dtype=f32),
-        [SM, HB] + [VM] * groups,
+        [SM, HB] + [VM] * (groups - late),
         [pltpu.VMEM((width, rows), bf16), pltpu.SemaphoreType.DMA],
         2 * rows * hid * groups * width,
         2 << 20,
-    )(me, feature_rows, self_one, *feature_blocks)
+    )(me, feature_rows, self_one, *early_blocks)
     hidden, *projected = call(
-        hidden_kernel,
+        functools.partial(hidden_kernel, groups, late),
         (shape(rows, hid),) + (shape(classes, rows),) * groups,
-        [SM] + [VM] * (3 + groups),
+        [SM] + [VM] * (4 + late + groups),
         (),
         2 * rows * hid * groups * width,
         2 << 20,
-    )(me, neigh_one, neigh_out.T, own, own_mean, *means)
+    )(me, self_one, neigh_one, neigh_out.T, own, *late_blocks, *means)
     projected = projected[:1] + shift(projected[1:])
-    chips = parts // 2
     mine, mate = call(
         pick_kernel,
         (shape(chips, slots, whole_lanes(classes)),) * 2,
@@ -423,18 +462,12 @@
         2 * parts * slots * nodes * classes,
         1 << 19,
     )(me, hits, *projected)
-    mate = lax.ppermute(mate, "dom", [(d, d ^ 1) for d in range(parts)])
-    arrived = call(
-        pair_kernel, (shape(2, slots, whole_lanes(classes)),) * chips, [VM, VM], (), 0, 1 << 19
-    )(mine, mate)
-    arrived = [arrived[0]] + [
-        lax.ppermute(
-            arrived[j],
-            "dom",
-            [(d, next_to(d // 2, j, chips) * 2 + d % 2) for d in range(parts)],
+    mate = to_mate(mate)
+    arrived = to_chips(
+        call(pair_kernel, (shape(2, slots, whole_lanes(classes)),) * chips, [VM] * 3, (), 0, 1 << 19)(
+            hits, mine, mate
         )
-        for j in range(1, chips)
-    ]
+    )
     own, hidden = call(
         own_kernel,
         (shape(classes, rows, dtype=f32), shape(rows, hid)),
@@ -459,7 +492,7 @@
         (),
         2 * rows * parts * slots * classes,
         1 << 19,
-    )(me, own, near, far, sums, *arrived)
+    )(me, own, near, edges, sums, *arrived)
     return hidden[None], logits.transpose(1, 0, 2)
 
 

time: 40.5 us -> 39.8 us (0.983)
  starting transfers between devices: 22 us -> 22.7 us
  Pallas kernels: 8.06 us -> 7.37 us
  waiting for transfers between devices: 9.38 us -> 8.75 us
    all_to_all x1 -> x0, starting transfers between devices: 5.18 us -> none  [swap(): return lax.all_to_all(value, 'dom', split_axis=0, concat_axis=0, tiled=True)]
    ppermute x4 -> x8, starting transfers between devices: 3.56 us -> 8.25 us  [the longest x6 7.66 us: to_chips(): lax.ppermute(blocks[j], 'dom', [(d, next_to(d // 2, j, chips) * 2 + d % 2...]
    ppermute x9, starting transfers between devices: 13.3 us -> 14.5 us  [shift(): lax.ppermute(block, 'feat', [(i, ahead(i, groups, k)) for i in range(grou...]
    all_to_all x1 -> x0, waiting for transfers between devices: 0.89 us -> none  [swap(): return lax.all_to_all(value, 'dom', split_axis=0, concat_axis=0, tiled=True)]
    pallas_call x10 -> x11, Pallas kernels: 8.06 us -> 7.37 us  [placed(): run(*(pltpu.with_memory_space_constraint(value, pltpu.HBM) if spec is HB...]
    ppermute x4 -> x8, waiting for transfers between devices: 3.12 us -> 3.59 us  [the longest x6 2.39 us: to_chips(): lax.ppermute(blocks[j], 'dom', [(d, next_to(d // 2, j, chips) * 2 + d % 2...]
  transfers between devices with their start and end apart: 14 -> 17, of which waited for: 10 -> 9; matrix products, arithmetic and copies ran while one was open for 0% -> 0% of each run, Pallas kernels for 10% -> 10%
where the time goes in v8:
time: 39.8 us; the launch traced here: 39.6 us
  starting transfers between devices  22.7 us (57%)
  waiting for transfers between devices  8.75 us (22%)
  Pallas kernels  7.37 us (19%)
  between operations  0.77 us (2%)
    ppermute x9, starting transfers between devices, shift(): lax.ppermute(block, 'feat', [(i, ahead(i, groups, k)) for i in range(grou...  14.5 us
    ppermute x6, starting transfers between devices, to_chips(): lax.ppermute(blocks[j], 'dom', [(d, next_to(d // 2, j, chips) * 2 + d % 2...  7.66 us
    pallas_call x11, Pallas kernels, placed(): run(*(pltpu.with_memory_space_constraint(value, pltpu.HBM) if spec is HB...  7.37 us
    ppermute x9, waiting for transfers between devices, shift(): lax.ppermute(block, 'feat', [(i, ahead(i, groups, k)) for i in range(grou...  5.16 us
    ppermute x6, waiting for transfers between devices, to_chips(): lax.ppermute(blocks[j], 'dom', [(d, next_to(d // 2, j, chips) * 2 + d % 2...  2.39 us
    ppermute x2, waiting for transfers between devices, to_mate(): return lax.ppermute(value, 'dom', [(d, d ^ 1) for d in range(parts)])  1.2 us
  transfers between devices with their start and end apart: 17, of which 9 were waited for; matrix products, arithmetic and copies ran while one was open for 0% of the time, Pallas kernels for 10%

profile of v8, /device:TPU:0, one launch (start us, length us, event | category | flops | bytes accessed | tf_op | source)
XLA Modules:
  0.0 39.6 jit_solution(9326613814752326925)
XLA Ops:
  0.6 0.0 copy-start
  0.6 1.5 %shard_map.123 = (bf16[4,64,256]{2,1,0:T(8,128)(2,1)S(1)}, bf16[4,64,256]{2,1,0:T(8,128)(2,1)S(1)}, bf16[192,128]{1,0:T(8,128)(2,1)S(1)}, bf16[192,128]{1,0:T(8,128)(2,1)S(1)}, bf16[192,128]{1,0:T(8,128)(2,1)S(1)}) custom-call(s32[1]{0:T(128)} %bitcast.me_ref, s32[1]{0:T(128)} %bitcast.4.part_ref, s32[8,4,16]{2,1,0:T(4,128)} %bitcast.27, ...), custom_call_target="tpu_custom_call" | custom-call | flops 100663296 | bytes 1048576 | tf_op jit(solution)/shard_map/pallas_call | solution.py:32
  2.2 0.5 %collective-permute-start = (bf16[4,64,256]{2,1,0:T(8,128)(2,1)S(1)}, bf16[4,64,256]{2,1,0:T(8,128)(2,1)S(1)}, u32[]{:S(2)}, u32[]{:S(2)}) collective-permute-start(bf16[4,64,256]{2,1,0:T(8,128)(2,1)S(1)} %get-tuple-element.37), channel_id=1, source_target_pairs={{0,1},{1,0},{2,3},{3,2},{4,5},{5,4},{6,7},{7,6},{8,9},{9,8},{10,11... | collective-permute-start | bytes 393224 | tf_op jit(solution)/shard_map/ppermute | solution.py:357
  2.7 1.7 %shard_map.122 = (f32[4,208,128]{2,1,0:T(8,128)S(1)}, bf16[4,8,16,128]{3,2,1,0:T(8,128)(2,1)S(1)}, bf16[128,512]{1,0:T(8,128)(2,1)S(1)}, bf16[128,512]{1,0:T(8,128)(2,1)S(1)}) custom-call(s32[1]{0:T(128)} %bitcast.me_ref, s32[1]{0:T(128)} %bitcast.4.part_ref, s32[2,12]{1,0:T(2,128)} %bitcast.31, s32[4,8]{1,0:T(4,128)} %bitcast.30, ...), custom_call_target="tpu_custom_call" | custom-call | flops 100663296 | bytes 1048576 | tf_op jit(solution)/shard_map/pallas_call | solution.py:32
  4.3 0.0 collective-permute-done.got_ref
  4.4 3.5 %collective-permute-start.3 = (bf16[2,64,256]{2,1,0:T(8,128)(2,1)S(1)}, bf16[2,64,256]{2,1,0:T(8,128)(2,1)S(1)}, u32[]{:S(2)}, u32[]{:S(2)}) collective-permute-start(bf16[2,64,256]{2,1,0:T(8,128)(2,1)S(1)} %get-tuple-element.45), channel_id=1, source_target_pairs={{0,6},{1,7},{2,4},{3,5},{4,2},{5,3},{6,0},{7,1},{8,14},{9,15},{10,... | collective-permute-start | bytes 196616 | tf_op jit(solution)/shard_map/ppermute | solution.py:361
  7.9 0.5 %collective-permute-start.4 = (bf16[2,64,256]{2,1,0:T(8,128)(2,1)S(1)}, bf16[2,64,256]{2,1,0:T(8,128)(2,1)S(1)}, u32[]{:S(2)}, u32[]{:S(2)}) collective-permute-start(bf16[2,64,256]{2,1,0:T(8,128)(2,1)S(1)} %get-tuple-element.46), channel_id=1, source_target_pairs={{0,4},{1,5},{2,6},{3,7},{4,0},{5,1},{6,2},{7,3},{8,12},{9,13},{10,... | collective-permute-start | bytes 196616 | tf_op jit(solution)/shard_map/ppermute | solution.py:361
  8.5 0.1 collective-permute-start.5
  8.6 4.0 %collective-permute-start.1 = (bf16[192,128]{1,0:T(8,128)(2,1)S(1)}, bf16[192,128]{1,0:T(8,128)(2,1)S(1)}, u32[]{:S(2)}, u32[]{:S(2)}) collective-permute-start(bf16[192,128]{1,0:T(8,128)(2,1)S(1)} %get-tuple-element.40), channel_id=1, source_target_pairs={{0,24},{8,16},{16,8},{24,0},{1,25},{9,17},{17,9},{25,1},{2,26},{10... | collective-permute-start | bytes 147464 | tf_op jit(solution)/shard_map/ppermute | solution.py:350
  12.6 0.0 collective-permute-start.2
  12.6 0.0 collective-permute-done.3.rest_1_
  12.6 0.0 collective-permute-done.4.rest_2_
  12.6 0.1 collective-permute-done.5.rest_3_
  12.7 0.3 shard_map.126
  13.0 1.6 %collective-permute-start.6 = (bf16[192,128]{1,0:T(8,128)(2,1)S(1)}, bf16[192,128]{1,0:T(8,128)(2,1)S(1)}, u32[]{:S(2)}, u32[]{:S(2)}) collective-permute-start(bf16[192,128]{1,0:T(8,128)(2,1)S(1)} %get-tuple-element.49), channel_id=1, source_target_pairs={{0,8},{8,0},{16,24},{24,16},{1,9},{9,1},{17,25},{25,17},{2,10},{10... | collective-permute-start | bytes 147464 | tf_op jit(solution)/shard_map/ppermute | solution.py:350
  14.6 2.7 %collective-permute-start.7 = (bf16[192,128]{1,0:T(8,128)(2,1)S(1)}, bf16[192,128]{1,0:T(8,128)(2,1)S(1)}, u32[]{:S(2)}, u32[]{:S(2)}) collective-permute-start(bf16[192,128]{1,0:T(8,128)(2,1)S(1)} %get-tuple-element.51), channel_id=1, source_target_pairs={{0,24},{8,16},{16,8},{24,0},{1,25},{9,17},{17,9},{25,1},{2,26},{10... | collective-permute-start | bytes 147464 | tf_op jit(solution)/shard_map/ppermute | solution.py:350
  17.3 0.0 collective-permute-start.8
  17.3 0.0 collective-permute-done.1.rest_0_
  17.3 1.7 %collective-permute-start.9 = (bf16[192,128]{1,0:T(8,128)(2,1)S(1)}, bf16[192,128]{1,0:T(8,128)(2,1)S(1)}, u32[]{:S(2)}, u32[]{:S(2)}) collective-permute-start(bf16[192,128]{1,0:T(8,128)(2,1)S(1)} %get-tuple-element.53), channel_id=1, source_target_pairs={{0,8},{8,0},{16,24},{24,16},{1,9},{9,1},{17,25},{25,17},{2,10},{10... | collective-permute-start | bytes 147464 | tf_op jit(solution)/shard_map/ppermute | solution.py:350
  19.0 0.0 collective-permute-done.2.rest_1_
  19.0 0.0 copy-done
  19.0 1.1 %shard_map.125.own_ref = f32[128,1024]{1,0:T(8,128)S(1)} custom-call(s32[1]{0:T(128)} %bitcast.me_ref, bf16[192,512]{1,0:T(8,128)(2,1)} %bitcast.23, bf16[768,1024]{1,0:T(8,128)(2,1)S(1)} %copy-done, bf16[192,128]{1,0:T(8,128)(2,1)S(1)} %collective-permute-done.1.rest_0_, bf16[192,128]{1,0:T(8,128)(2,1)S(1)} %collective-permute-done.2.rest_1_), custom_call_target="tpu_custom_call" | custom-call | flops 201326592 | bytes 2097152 | tf_op jit(solution)/shard_map/pallas_call | solution.py:32
  20.1 0.0 collective-permute-done.6.rest_0_
  20.1 0.4 collective-permute-done.7.rest_2_
  20.5 2.2 %collective-permute-done.8.rest_3_ = bf16[192,128]{1,0:T(8,128)(2,1)S(1)} collective-permute-done((bf16[192,128]{1,0:T(8,128)(2,1)S(1)}, bf16[192,128]{1,0:T(8,128)(2,1)S(1)}, u32[]{:S(2)}, u32[]{:S(2)}) %collective-permute-start.8) | collective-permute-done | bytes 49184 | tf_op jit(solution)/shard_map/ppermute | solution.py:350
  22.7 0.0 collective-permute-done.9.rest_4_
  22.7 0.0 copy-done.1
  22.7 0.0 copy-done.2
  22.7 0.0 copy-start.3
  22.7 0.8 %shard_map.127 = (bf16[128,1024]{1,0:T(8,128)(2,1)S(1)}, bf16[153,128]{1,0:T(8,128)(2,1)S(1)}, bf16[153,128]{1,0:T(8,128)(2,1)S(1)}, bf16[153,128]{1,0:T(8,128)(2,1)S(1)}, bf16[153,128]{1,0:T(8,128)(2,1)S(1)}) custom-call(s32[1]{0:T(128)} %bitcast.me_ref, bf16[768,1024]{1,0:T(8,128)(2,1)S(1)} %copy-done, bf16[768,1024]{1,0:T(8,128)(2,1)S(1)} %copy-done.1, ...), custom_call_target="tpu_custom_call" | custom-call | flops 201326592 | bytes 2097152 | tf_op jit(solution)/shard_map/pallas_call | solution.py:32
  23.5 2.0 %collective-permute-start.10 = (bf16[153,128]{1,0:T(8,128)(2,1)S(1)}, bf16[153,128]{1,0:T(8,128)(2,1)S(1)}, u32[]{:S(2)}, u32[]{:S(2)}) collective-permute-start(bf16[153,128]{1,0:T(8,128)(2,1)S(1)} %get-tuple-element.59), channel_id=1, source_target_pairs={{0,24},{8,16},{16,8},{24,0},{1,25},{9,17},{17,9},{25,1},{2,26},{10... | collective-permute-start | bytes 117512 | tf_op jit(solution)/shard_map/ppermute | solution.py:350
  25.5 0.0 collective-permute-start.11
  25.5 2.5 %collective-permute-start.12 = (bf16[153,128]{1,0:T(8,128)(2,1)S(1)}, bf16[153,128]{1,0:T(8,128)(2,1)S(1)}, u32[]{:S(2)}, u32[]{:S(2)}) collective-permute-start(bf16[153,128]{1,0:T(8,128)(2,1)S(1)} %get-tuple-element.61), channel_id=1, source_target_pairs={{0,8},{8,0},{16,24},{24,16},{1,9},{9,1},{17,25},{25,17},{2,10},{10... | collective-permute-start | bytes 117512 | tf_op jit(solution)/shard_map/ppermute | solution.py:350
  28.0 1.4 %collective-permute-done.10.rest_1_ = bf16[153,128]{1,0:T(8,128)(2,1)S(1)} collective-permute-done((bf16[153,128]{1,0:T(8,128)(2,1)S(1)}, bf16[153,128]{1,0:T(8,128)(2,1)S(1)}, u32[]{:S(2)}, u32[]{:S(2)}) %collective-permute-start.10) | collective-permute-done | bytes 39200 | tf_op jit(solution)/shard_map/ppermute | solution.py:350
  29.4 1.1 %collective-permute-done.11.rest_2_ = bf16[153,128]{1,0:T(8,128)(2,1)S(1)} collective-permute-done((bf16[153,128]{1,0:T(8,128)(2,1)S(1)}, bf16[153,128]{1,0:T(8,128)(2,1)S(1)}, u32[]{:S(2)}, u32[]{:S(2)}) %collective-permute-start.11) | collective-permute-done | bytes 39200 | tf_op jit(solution)/shard_map/ppermute | solution.py:350
  30.5 0.0 collective-permute-done.12.rest_3_
  30.5 0.3 shard_map.130
  30.8 0.1 collective-permute-start.13
  30.9 1.2 %collective-permute-done.13.got_ref = bf16[4,16,256]{2,1,0:T(8,128)(2,1)S(1)} collective-permute-done((bf16[4,16,256]{2,1,0:T(8,128)(2,1)S(1)}, bf16[4,16,256]{2,1,0:T(8,128)(2,1)S(1)}, u32[]{:S(2)}, u32[]{:S(2)}) %collective-permute-start.13) | collective-permute-done | bytes 32800 | tf_op jit(solution)/shard_map/ppermute | solution.py:357
  32.1 1.9 %collective-permute-start.14 = (bf16[2,16,256]{2,1,0:T(8,128)(2,1)S(1)}, bf16[2,16,256]{2,1,0:T(8,128)(2,1)S(1)}, u32[]{:S(2)}, u32[]{:S(2)}) collective-permute-start(bf16[2,16,256]{2,1,0:T(8,128)(2,1)S(1)} %get-tuple-element.65), channel_id=1, source_target_pairs={{0,6},{1,7},{2,4},{3,5},{4,2},{5,3},{6,0},{7,1},{8,14},{9,15},{10,... | collective-permute-start | bytes 49160 | tf_op jit(solution)/shard_map/ppermute | solution.py:361
  33.9 1.1 %collective-permute-start.15 = (bf16[2,16,256]{2,1,0:T(8,128)(2,1)S(1)}, bf16[2,16,256]{2,1,0:T(8,128)(2,1)S(1)}, u32[]{:S(2)}, u32[]{:S(2)}) collective-permute-start(bf16[2,16,256]{2,1,0:T(8,128)(2,1)S(1)} %get-tuple-element.66), channel_id=1, source_target_pairs={{0,4},{1,5},{2,6},{3,7},{4,0},{5,1},{6,2},{7,3},{8,12},{9,13},{10,... | collective-permute-start | bytes 49160 | tf_op jit(solution)/shard_map/ppermute | solution.py:361
  35.0 0.5 %collective-permute-start.16 = (bf16[2,16,256]{2,1,0:T(8,128)(2,1)S(1)}, bf16[2,16,256]{2,1,0:T(8,128)(2,1)S(1)}, u32[]{:S(2)}, u32[]{:S(2)}) collective-permute-start(bf16[2,16,256]{2,1,0:T(8,128)(2,1)S(1)} %get-tuple-element.67), channel_id=1, source_target_pairs={{0,2},{1,3},{2,0},{3,1},{4,6},{5,7},{6,4},{7,5},{8,10},{9,11},{10,... | collective-permute-start | bytes 49160 | tf_op jit(solution)/shard_map/ppermute | solution.py:361
  35.6 0.7 %shard_map.128 = (f32[153,128]{1,0:T(8,128)S(1)}, bf16[128,1024]{1,0:T(8,128)(2,1)}) custom-call(bf16[128,1024]{1,0:T(8,128)(2,1)S(1)} %get-tuple-element.54.hidden_ref, bf16[153,1024]{1,0:T(8,128)(2,1)S(1)} %bitcast.20), custom_call_target="tpu_custom_call" | custom-call | flops 40108032 | bytes 1048576 | tf_op jit(solution)/shard_map/pallas_call | solution.py:32
  36.3 0.2 shard_map.129.near_ref
  36.5 0.3 collective-permute-done.14.rest_1_
  36.8 0.9 %collective-permute-done.15.rest_2_ = bf16[2,16,256]{2,1,0:T(8,128)(2,1)S(1)} collective-permute-done((bf16[2,16,256]{2,1,0:T(8,128)(2,1)S(1)}, bf16[2,16,256]{2,1,0:T(8,128)(2,1)S(1)}, u32[]{:S(2)}, u32[]{:S(2)}) %collective-permute-start.15) | collective-permute-done | bytes 16416 | tf_op jit(solution)/shard_map/ppermute | solution.py:361
  37.7 1.1 %collective-permute-done.16.rest_3_ = bf16[2,16,256]{2,1,0:T(8,128)(2,1)S(1)} collective-permute-done((bf16[2,16,256]{2,1,0:T(8,128)(2,1)S(1)}, bf16[2,16,256]{2,1,0:T(8,128)(2,1)S(1)}, u32[]{:S(2)}, u32[]{:S(2)}) %collective-permute-start.16) | collective-permute-done | bytes 16416 | tf_op jit(solution)/shard_map/ppermute | solution.py:361
  38.7 0.9 %shard_map.132 = f32[153,1,128]{2,1,0:T(1,128)} custom-call(s32[1]{0:T(128)} %bitcast.me_ref, f32[153,128]{1,0:T(8,128)S(1)} %get-tuple-element.56.own_ref, f32[153,128]{1,0:T(8,128)S(1)} %shard_map.129.near_ref, bf16[4,8,16,128]{3,2,1,0:T(8,128)(2,1)S(1)} %get-tuple-element.43.edges_ref, f32[4,208,128]{2,1,0:T(8,128)S(1)} %get-tuple-element.42.sums_ref, ...), custom_call_target="tpu_custom_call" | custom-call | flops 5013504 | bytes 524288 | tf_op jit(solution)/shard_map/pallas_call | solution.py:32
  (5 shorter events, 0.0 us)
Async XLA Ops:
  0.6 18.4 %copy-start = (bf16[768,1024]{1,0:T(8,128)(2,1)S(1)}, bf16[768,1024]{1,0:T(8,128)(2,1)}, u32[]{:S(2)}) copy-start(bf16[768,1024]{1,0:T(8,128)(2,1)} %self_weight_ref.1) | copy-start | bytes 4718596
  2.2 2.2 %collective-permute-start = (bf16[4,64,256]{2,1,0:T(8,128)(2,1)S(1)}, bf16[4,64,256]{2,1,0:T(8,128)(2,1)S(1)}, u32[]{:S(2)}, u32[]{:S(2)}) collective-permute-start(bf16[4,64,256]{2,1,0:T(8,128)(2,1)S(1)} %get-tuple-element.37), channel_id=1, source_target_pairs={{0,1},{1,0},{2,3},{3,2},{4,5},{5,4},{6,7},{7,6},{8,9},{9,8},{10,11... | collective-permute-start | bytes 393224 | tf_op jit(solution)/shard_map/ppermute | solution.py:357
  4.4 8.2 %collective-permute-start.3 = (bf16[2,64,256]{2,1,0:T(8,128)(2,1)S(1)}, bf16[2,64,256]{2,1,0:T(8,128)(2,1)S(1)}, u32[]{:S(2)}, u32[]{:S(2)}) collective-permute-start(bf16[2,64,256]{2,1,0:T(8,128)(2,1)S(1)} %get-tuple-element.45), channel_id=1, source_target_pairs={{0,6},{1,7},{2,4},{3,5},{4,2},{5,3},{6,0},{7,1},{8,14},{9,15},{10,... | collective-permute-start | bytes 196616 | tf_op jit(solution)/shard_map/ppermute | solution.py:361
  7.9 4.7 %collective-permute-start.4 = (bf16[2,64,256]{2,1,0:T(8,128)(2,1)S(1)}, bf16[2,64,256]{2,1,0:T(8,128)(2,1)S(1)}, u32[]{:S(2)}, u32[]{:S(2)}) collective-permute-start(bf16[2,64,256]{2,1,0:T(8,128)(2,1)S(1)} %get-tuple-element.46), channel_id=1, source_target_pairs={{0,4},{1,5},{2,6},{3,7},{4,0},{5,1},{6,2},{7,3},{8,12},{9,13},{10,... | collective-permute-start | bytes 196616 | tf_op jit(solution)/shard_map/ppermute | solution.py:361
  8.5 4.3 %collective-permute-start.5 = (bf16[2,64,256]{2,1,0:T(8,128)(2,1)S(1)}, bf16[2,64,256]{2,1,0:T(8,128)(2,1)S(1)}, u32[]{:S(2)}, u32[]{:S(2)}) collective-permute-start(bf16[2,64,256]{2,1,0:T(8,128)(2,1)S(1)} %get-tuple-element.47), channel_id=1, source_target_pairs={{0,2},{1,3},{2,0},{3,1},{4,6},{5,7},{6,4},{7,5},{8,10},{9,11},{10,... | collective-permute-start | bytes 196616 | tf_op jit(solution)/shard_map/ppermute | solution.py:361
  8.6 8.8 %collective-permute-start.1 = (bf16[192,128]{1,0:T(8,128)(2,1)S(1)}, bf16[192,128]{1,0:T(8,128)(2,1)S(1)}, u32[]{:S(2)}, u32[]{:S(2)}) collective-permute-start(bf16[192,128]{1,0:T(8,128)(2,1)S(1)} %get-tuple-element.40), channel_id=1, source_target_pairs={{0,24},{8,16},{16,8},{24,0},{1,25},{9,17},{17,9},{25,1},{2,26},{10... | collective-permute-start | bytes 147464 | tf_op jit(solution)/shard_map/ppermute | solution.py:350
  12.6 6.4 %collective-permute-start.2 = (bf16[192,128]{1,0:T(8,128)(2,1)S(1)}, bf16[192,128]{1,0:T(8,128)(2,1)S(1)}, u32[]{:S(2)}, u32[]{:S(2)}) collective-permute-start(bf16[192,128]{1,0:T(8,128)(2,1)S(1)} %get-tuple-element.41), channel_id=1, source_target_pairs={{0,16},{8,24},{16,0},{24,8},{1,17},{9,25},{17,1},{25,9},{2,18},{10... | collective-permute-start | bytes 147464 | tf_op jit(solution)/shard_map/ppermute | solution.py:350
  12.7 10.0 %copy-start.1 = (bf16[768,1024]{1,0:T(8,128)(2,1)S(1)}, bf16[768,1024]{1,0:T(8,128)(2,1)}, u32[]{:S(2)}) copy-start(bf16[768,1024]{1,0:T(8,128)(2,1)} %weight_ref.3) | copy-start | bytes 4718596
  12.7 10.0 %copy-start.2 = (bf16[1024,153]{0,1:T(8,128)(2,1)S(1)}, bf16[1024,153]{0,1:T(8,128)(2,1)}, u32[]{:S(2)}) copy-start(bf16[1024,153]{0,1:T(8,128)(2,1)} %param.21) | copy-start | bytes 940036
  13.0 7.1 %collective-permute-start.6 = (bf16[192,128]{1,0:T(8,128)(2,1)S(1)}, bf16[192,128]{1,0:T(8,128)(2,1)S(1)}, u32[]{:S(2)}, u32[]{:S(2)}) collective-permute-start(bf16[192,128]{1,0:T(8,128)(2,1)S(1)} %get-tuple-element.49), channel_id=1, source_target_pairs={{0,8},{8,0},{16,24},{24,16},{1,9},{9,1},{17,25},{25,17},{2,10},{10... | collective-permute-start | bytes 147464 | tf_op jit(solution)/shard_map/ppermute | solution.py:350
  14.6 5.9 %collective-permute-start.7 = (bf16[192,128]{1,0:T(8,128)(2,1)S(1)}, bf16[192,128]{1,0:T(8,128)(2,1)S(1)}, u32[]{:S(2)}, u32[]{:S(2)}) collective-permute-start(bf16[192,128]{1,0:T(8,128)(2,1)S(1)} %get-tuple-element.51), channel_id=1, source_target_pairs={{0,24},{8,16},{16,8},{24,0},{1,25},{9,17},{17,9},{25,1},{2,26},{10... | collective-permute-start | bytes 147464 | tf_op jit(solution)/shard_map/ppermute | solution.py:350
  17.3 5.4 %collective-permute-start.8 = (bf16[192,128]{1,0:T(8,128)(2,1)S(1)}, bf16[192,128]{1,0:T(8,128)(2,1)S(1)}, u32[]{:S(2)}, u32[]{:S(2)}) collective-permute-start(bf16[192,128]{1,0:T(8,128)(2,1)S(1)} %get-tuple-element.52), channel_id=1, source_target_pairs={{0,16},{8,24},{16,0},{24,8},{1,17},{9,25},{17,1},{25,9},{2,18},{10... | collective-permute-start | bytes 147464 | tf_op jit(solution)/shard_map/ppermute | solution.py:350
  17.3 5.4 %collective-permute-start.9 = (bf16[192,128]{1,0:T(8,128)(2,1)S(1)}, bf16[192,128]{1,0:T(8,128)(2,1)S(1)}, u32[]{:S(2)}, u32[]{:S(2)}) collective-permute-start(bf16[192,128]{1,0:T(8,128)(2,1)S(1)} %get-tuple-element.53), channel_id=1, source_target_pairs={{0,8},{8,0},{16,24},{24,16},{1,9},{9,1},{17,25},{25,17},{2,10},{10... | collective-permute-start | bytes 147464 | tf_op jit(solution)/shard_map/ppermute | solution.py:350
  22.7 12.8 %copy-start.3 = (bf16[1024,153]{0,1:T(8,128)(2,1)S(1)}, bf16[1024,153]{0,1:T(8,128)(2,1)}, u32[]{:S(2)}) copy-start(bf16[1024,153]{0,1:T(8,128)(2,1)} %param.20) | copy-start | bytes 940036
  23.5 5.9 %collective-permute-start.10 = (bf16[153,128]{1,0:T(8,128)(2,1)S(1)}, bf16[153,128]{1,0:T(8,128)(2,1)S(1)}, u32[]{:S(2)}, u32[]{:S(2)}) collective-permute-start(bf16[153,128]{1,0:T(8,128)(2,1)S(1)} %get-tuple-element.59), channel_id=1, source_target_pairs={{0,24},{8,16},{16,8},{24,0},{1,25},{9,17},{17,9},{25,1},{2,26},{10... | collective-permute-start | bytes 117512 | tf_op jit(solution)/shard_map/ppermute | solution.py:350
  25.5 5.0 %collective-permute-start.11 = (bf16[153,128]{1,0:T(8,128)(2,1)S(1)}, bf16[153,128]{1,0:T(8,128)(2,1)S(1)}, u32[]{:S(2)}, u32[]{:S(2)}) collective-permute-start(bf16[153,128]{1,0:T(8,128)(2,1)S(1)} %get-tuple-element.60), channel_id=1, source_target_pairs={{0,16},{8,24},{16,0},{24,8},{1,17},{9,25},{17,1},{25,9},{2,18},{10... | collective-permute-start | bytes 117512 | tf_op jit(solution)/shard_map/ppermute | solution.py:350
  25.5 5.0 %collective-permute-start.12 = (bf16[153,128]{1,0:T(8,128)(2,1)S(1)}, bf16[153,128]{1,0:T(8,128)(2,1)S(1)}, u32[]{:S(2)}, u32[]{:S(2)}) collective-permute-start(bf16[153,128]{1,0:T(8,128)(2,1)S(1)} %get-tuple-element.61), channel_id=1, source_target_pairs={{0,8},{8,0},{16,24},{24,16},{1,9},{9,1},{17,25},{25,17},{2,10},{10... | collective-permute-start | bytes 117512 | tf_op jit(solution)/shard_map/ppermute | solution.py:350
  30.8 1.3 %collective-permute-start.13 = (bf16[4,16,256]{2,1,0:T(8,128)(2,1)S(1)}, bf16[4,16,256]{2,1,0:T(8,128)(2,1)S(1)}, u32[]{:S(2)}, u32[]{:S(2)}) collective-permute-start(bf16[4,16,256]{2,1,0:T(8,128)(2,1)S(1)} %get-tuple-element.63), channel_id=1, source_target_pairs={{0,1},{1,0},{2,3},{3,2},{4,5},{5,4},{6,7},{7,6},{8,9},{9,8},{10,11... | collective-permute-start | bytes 98312 | tf_op jit(solution)/shard_map/ppermute | solution.py:357
  32.1 4.7 %collective-permute-start.14 = (bf16[2,16,256]{2,1,0:T(8,128)(2,1)S(1)}, bf16[2,16,256]{2,1,0:T(8,128)(2,1)S(1)}, u32[]{:S(2)}, u32[]{:S(2)}) collective-permute-start(bf16[2,16,256]{2,1,0:T(8,128)(2,1)S(1)} %get-tuple-element.65), channel_id=1, source_target_pairs={{0,6},{1,7},{2,4},{3,5},{4,2},{5,3},{6,0},{7,1},{8,14},{9,15},{10,... | collective-permute-start | bytes 49160 | tf_op jit(solution)/shard_map/ppermute | solution.py:361
  33.9 3.7 %collective-permute-start.15 = (bf16[2,16,256]{2,1,0:T(8,128)(2,1)S(1)}, bf16[2,16,256]{2,1,0:T(8,128)(2,1)S(1)}, u32[]{:S(2)}, u32[]{:S(2)}) collective-permute-start(bf16[2,16,256]{2,1,0:T(8,128)(2,1)S(1)} %get-tuple-element.66), channel_id=1, source_target_pairs={{0,4},{1,5},{2,6},{3,7},{4,0},{5,1},{6,2},{7,3},{8,12},{9,13},{10,... | collective-permute-start | bytes 49160 | tf_op jit(solution)/shard_map/ppermute | solution.py:361
  35.0 3.7 %collective-permute-start.16 = (bf16[2,16,256]{2,1,0:T(8,128)(2,1)S(1)}, bf16[2,16,256]{2,1,0:T(8,128)(2,1)S(1)}, u32[]{:S(2)}, u32[]{:S(2)}) collective-permute-start(bf16[2,16,256]{2,1,0:T(8,128)(2,1)S(1)} %get-tuple-element.67), channel_id=1, source_target_pairs={{0,2},{1,3},{2,0},{3,1},{4,6},{5,7},{6,4},{7,5},{8,10},{9,11},{10,... | collective-permute-start | bytes 49160 | tf_op jit(solution)/shard_map/ppermute | solution.py:361

commit v9 on v8

--- a/solution.py
+++ b/solution.py
@@ -132,18 +132,15 @@
     tiles_hbm,
     targets_hbm,
     weight_hbm,
-    sources_hbm,
     sums_ref,
     edges_ref,
     band_ref,
-    hits_ref,
     ids_ref,
     counts_ref,
     features_ref,
     tiles_ref,
     targets_ref,
     weight_ref,
-    sources_ref,
     bands,
     sems,
 ):
@@ -159,7 +156,6 @@
         (tiles_hbm, tiles_ref),
         (targets_hbm, targets_ref),
         (weight_hbm, weight_ref),
-        (sources_hbm, sources_ref),
     )
     extra = features_ref.shape[0] - width
     features_ref[width:, :] = jnp.ones((extra, features_ref.shape[1]), bf16)
@@ -200,12 +196,20 @@
         connect(0, 0)
     else:
         lax.fori_loop(0, parts // chunk, connect, 0)
-    mine = lax.broadcasted_iota(jnp.int32, sources_ref.shape, 1) == me
+
+
+def hits_kernel(after, me_ref, part_ref, sources_hbm, hits_ref, sources_ref, sem):
+    del after
+    copy = pltpu.make_async_copy(sources_hbm, sources_ref, sem)
+    copy.start()
+    parts, groups, slots = sources_ref.shape
+    chips, chip, core = parts // 2, part_ref[0] // 2, part_ref[0] % 2
+    mine = lax.broadcasted_iota(jnp.int32, sources_ref.shape, 1) == me_ref[0]
+    copy.wait()
     picks = jnp.sum(jnp.where(mine, sources_ref[...], 0), axis=1).T
     lane = lax.broadcasted_iota(jnp.int32, (slots, hits_ref.shape[1]), 1)
     for d in range(parts):
-        other = (d % 2) ^ core
-        to = other * chips + step_to(chip, d // 2, chips)
+        to = ((d % 2) ^ core) * chips + step_to(chip, d // 2, chips)
         hits_ref[pl.ds(pl.multiple_of(to * slots, slots), slots), :] = jnp.where(
             picks[:, d : d + 1] == lane, 1.0, 0.0
         ).astype(bf16)
@@ -238,11 +242,11 @@
         features_hbm.at[:, pl.ds(pl.multiple_of(me * rows, rows), rows)], own_ref, sem
     )
     own.start()
+    span = pl.ds(pl.multiple_of(me * width, width), width)
     total = jnp.zeros(out_ref.shape, f32)
     for k, block in enumerate(early, 1):
         total = total + dot(block[...], weight_ref[rows_from(me, groups, k, width), :], FIRST)
     own.wait()
-    span = pl.ds(pl.multiple_of(me * width, width), width)
     out_ref[...] = total + dot(own_ref[...], weight_ref[span, :], FIRST)
 
 
@@ -254,9 +258,9 @@
     for k, block in enumerate(held, groups - late):
         span = rows_from(me, groups, k, width)
         total = total + dot(block[...], self_weight_ref[span, :], FIRST)
-    for k in range(groups):
+    for k, block in enumerate(parts):
         span = rows_from(me, groups, k, width)
-        total = total + dot(parts[k][...], weight_ref[span, :], FIRST)
+        total = total + dot(block[...], weight_ref[span, :], FIRST)
     hidden = jnp.maximum(total, 0.0).astype(bf16)
     hidden_ref[...] = hidden
     projected = dot(out_weight_ref[...], hidden, LAST).astype(bf16)
@@ -297,25 +301,26 @@
         out[...] = block[...]
 
 
-def near_kernel(me_ref, band_ref, *rest):
+def near_kernel(me_ref, own_ref, sums_ref, band_ref, *rest):
     projected, out_ref = rest[:-1], rest[-1]
     groups, rows = len(projected), projected[0].shape[1]
+    me, width = me_ref[0], sums_ref.shape[1] - EXTRA
     total = None
     for k in range(groups):
-        at = pl.multiple_of(behind(me_ref[0], groups, k) * rows, rows)
+        at = pl.multiple_of(behind(me, groups, k) * rows, rows)
         term = dot(projected[k][...], band_ref[:, pl.ds(at, rows)], LAST)
         total = term if total is None else total + term
-    out_ref[...] = total
-
-
-def last_kernel(me_ref, own_ref, near_ref, edges_ref, sums_ref, *rest):
+    out_ref[...] = own_ref[...] + total / sums_ref[me, width : width + 1, :]
+
+
+def last_kernel(me_ref, near_ref, edges_ref, sums_ref, *rest):
     arrived, out_ref = rest[:-1], rest[-1]
     groups, parts, slots, rows = edges_ref.shape
     me, width = me_ref[0], sums_ref.shape[1] - EXTRA
     arrived = jnp.concatenate([x[...].reshape(2 * slots, -1) for x in arrived], axis=0)
     far = dot(arrived, edges_ref[me].reshape(parts * slots, rows), FIRST)
-    far = far[: own_ref.shape[0]]
-    total = own_ref[...] + (near_ref[...] + far) / sums_ref[me, width : width + 1, :]
+    far = far[: near_ref.shape[0]]
+    total = near_ref[...] + far / sums_ref[me, width : width + 1, :]
     out_ref[...] = total.reshape(out_ref.shape)
 
 
@@ -339,7 +344,7 @@
     width, nodes = feature_rows.shape
     rows, slots = nodes // groups, sources.shape[3]
     hid, classes = self_one.shape[1], self_out.shape[1]
-    chips, late = parts // 2, 1
+    chips, late = parts // 2, 0
     chunk = max(1, min(parts, 512 // (groups * slots)))
 
     def shape(*dims, dtype=bf16):
@@ -383,15 +388,14 @@
         1 << 20,
     )(me, part, sources[0], feature_rows)
     mate = to_mate(mate)
-    sums, edges, band, hits = call(
+    sums, edges, band = call(
         functools.partial(local_kernel, chunk),
         (
             shape(groups, width + EXTRA, rows, dtype=f32),
             shape(groups, parts, slots, rows),
             shape(rows, nodes),
-            shape(parts * slots, nodes),
         ),
-        [SM, SM] + [HB] * 7,
+        [SM, SM] + [HB] * 6,
         [
             pltpu.SMEM(tile_ids.shape[:0:-1], jnp.int32),
             pltpu.SMEM(counts.shape[:0:-1], jnp.int32),
@@ -399,9 +403,8 @@
             pltpu.VMEM(tile_contents.shape, bf16),
             pltpu.VMEM((parts, groups, slots), jnp.int32),
             pltpu.VMEM((parts, groups, slots), bf16),
-            pltpu.VMEM((parts, groups, slots), jnp.int32),
             pltpu.VMEM((groups, rows, nodes), bf16),
-            pltpu.SemaphoreType.DMA((7,)),
+            pltpu.SemaphoreType.DMA((6,)),
         ],
         2 * nodes * nodes * width,
         1 << 20,
@@ -415,7 +418,6 @@
         tile_contents,
         targets[0],
         edge_weight[0],
-        sources[0],
     )
     paired = call(
         pair_kernel,
@@ -424,7 +426,7 @@
         (),
         0,
         1 << 20,
-    )(hits, mine, mate, *feature_blocks[: groups - 1 - late])
+    )(band, mine, mate, *feature_blocks[: groups - 1 - late])
     arrived = to_chips(paired[:chips])
     early_blocks = shift(paired[chips:])
     moved = call(
@@ -453,6 +455,14 @@
         2 * rows * hid * groups * width,
         2 << 20,
     )(me, self_one, neigh_one, neigh_out.T, own, *late_blocks, *means)
+    hits = call(
+        hits_kernel,
+        shape(parts * slots, nodes),
+        [VM, SM, SM, HB],
+        [pltpu.VMEM((parts, groups, slots), jnp.int32), pltpu.SemaphoreType.DMA],
+        0,
+        1 << 19,
+    )(projected[0], me, part, sources[0])
     projected = projected[:1] + shift(projected[1:])
     mine, mate = call(
         pick_kernel,
@@ -480,19 +490,19 @@
     near = call(
         near_kernel,
         shape(classes, rows, dtype=f32),
-        [SM] + [VM] * (1 + groups),
+        [SM] + [VM] * (3 + groups),
         (),
         2 * rows * nodes * classes,
         1 << 19,
-    )(me, band, *projected)
+    )(me, own, sums, band, *projected)
     logits = call(
         last_kernel,
         shape(classes, 1, rows, dtype=f32),
-        [SM] + [VM] * (4 + chips),
+        [SM] + [VM] * (3 + chips),
         (),
         2 * rows * parts * slots * classes,
         1 << 19,
-    )(me, own, near, edges, sums, *arrived)
+    )(me, near, edges, sums, *arrived)
     return hidden[None], logits.transpose(1, 0, 2)
 
 

time: 39.8 us -> 39.2 us (0.985)
  Pallas kernels: 7.37 us -> 8.32 us
  starting transfers between devices: 22.7 us -> 21.8 us
  waiting for transfers between devices: 8.75 us -> 8.04 us
    pallas_call x11 -> x12, Pallas kernels: 7.37 us -> 8.32 us  [placed(): run(*(pltpu.with_memory_space_constraint(value, pltpu.HBM) if spec is HB...]
    ppermute x9, starting transfers between devices: 14.5 us -> 13.6 us  [shift(): lax.ppermute(block, 'feat', [(i, ahead(i, groups, k)) for i in range(grou...]
    ppermute x9, waiting for transfers between devices: 5.16 us -> 4.6 us  [shift(): lax.ppermute(block, 'feat', [(i, ahead(i, groups, k)) for i in range(grou...]
  transfers between devices with their start and end apart: 17 -> 17, of which waited for: 9 -> 10; matrix products, arithmetic and copies ran while one was open for 0% -> 0% of each run, Pallas kernels for 10% -> 13%
where the time goes in v9:
time: 39.2 us; the launch traced here: 39 us
  starting transfers between devices  21.8 us (56%)
  Pallas kernels  8.32 us (21%)
  waiting for transfers between devices  8.04 us (21%)
  between operations  0.78 us (2%)
    ppermute x9, starting transfers between devices, shift(): lax.ppermute(block, 'feat', [(i, ahead(i, groups, k)) for i in range(grou...  13.6 us
    pallas_call x12, Pallas kernels, placed(): run(*(pltpu.with_memory_space_constraint(value, pltpu.HBM) if spec is HB...  8.32 us
    ppermute x6, starting transfers between devices, to_chips(): lax.ppermute(blocks[j], 'dom', [(d, next_to(d // 2, j, chips) * 2 + d % 2...  7.66 us
    ppermute x9, waiting for transfers between devices, shift(): lax.ppermute(block, 'feat', [(i, ahead(i, groups, k)) for i in range(grou...  4.6 us
    ppermute x6, waiting for transfers between devices, to_chips(): lax.ppermute(blocks[j], 'dom', [(d, next_to(d // 2, j, chips) * 2 + d % 2...  2.25 us
    ppermute x2, waiting for transfers between devices, to_mate(): return lax.ppermute(value, 'dom', [(d, d ^ 1) for d in range(parts)])  1.2 us
  transfers between devices with their start and end apart: 17, of which 10 were waited for; matrix products, arithmetic and copies ran while one was open for 0% of the time, Pallas kernels for 13%

profile of v9, /device:TPU:0, one launch (start us, length us, event | category | flops | bytes accessed | tf_op | source)
XLA Modules:
  0.0 39.0 jit_solution(6213639898534179914)
XLA Ops:
  0.6 0.0 copy-start
  0.6 1.5 %shard_map.123 = (bf16[4,64,256]{2,1,0:T(8,128)(2,1)S(1)}, bf16[4,64,256]{2,1,0:T(8,128)(2,1)S(1)}, bf16[192,128]{1,0:T(8,128)(2,1)S(1)}, bf16[192,128]{1,0:T(8,128)(2,1)S(1)}, bf16[192,128]{1,0:T(8,128)(2,1)S(1)}) custom-call(s32[1]{0:T(128)} %bitcast.me_ref, s32[1]{0:T(128)} %bitcast.4.part_ref, s32[8,4,16]{2,1,0:T(4,128)} %bitcast.27, ...), custom_call_target="tpu_custom_call" | custom-call | flops 100663296 | bytes 1048576 | tf_op jit(solution)/shard_map/pallas_call | solution.py:32
  2.2 0.5 %collective-permute-start = (bf16[4,64,256]{2,1,0:T(8,128)(2,1)S(1)}, bf16[4,64,256]{2,1,0:T(8,128)(2,1)S(1)}, u32[]{:S(2)}, u32[]{:S(2)}) collective-permute-start(bf16[4,64,256]{2,1,0:T(8,128)(2,1)S(1)} %get-tuple-element.36), channel_id=1, source_target_pairs={{0,1},{1,0},{2,3},{3,2},{4,5},{5,4},{6,7},{7,6},{8,9},{9,8},{10,11... | collective-permute-start | bytes 393224 | tf_op jit(solution)/shard_map/ppermute | solution.py:362
  2.7 1.6 %shard_map.122 = (f32[4,208,128]{2,1,0:T(8,128)S(1)}, bf16[4,8,16,128]{3,2,1,0:T(8,128)(2,1)S(1)}, bf16[128,512]{1,0:T(8,128)(2,1)S(1)}) custom-call(s32[1]{0:T(128)} %bitcast.me_ref, s32[1]{0:T(128)} %bitcast.4.part_ref, s32[2,12]{1,0:T(2,128)} %bitcast.31, s32[4,8]{1,0:T(4,128)} %bitcast.30, bf16[192,512]{1,0:T(8,128)(2,1)} %bitcast.22, ...), custom_call_target="tpu_custom_call" | custom-call | flops 100663296 | bytes 1048576 | tf_op jit(solution)/shard_map/pallas_call | solution.py:32
  4.3 0.0 collective-permute-done.got_ref
  4.4 3.5 %collective-permute-start.4 = (bf16[2,64,256]{2,1,0:T(8,128)(2,1)S(1)}, bf16[2,64,256]{2,1,0:T(8,128)(2,1)S(1)}, u32[]{:S(2)}, u32[]{:S(2)}) collective-permute-start(bf16[2,64,256]{2,1,0:T(8,128)(2,1)S(1)} %get-tuple-element.46), channel_id=1, source_target_pairs={{0,6},{1,7},{2,4},{3,5},{4,2},{5,3},{6,0},{7,1},{8,14},{9,15},{10,... | collective-permute-start | bytes 196616 | tf_op jit(solution)/shard_map/ppermute | solution.py:366
  7.9 0.5 %collective-permute-start.5 = (bf16[2,64,256]{2,1,0:T(8,128)(2,1)S(1)}, bf16[2,64,256]{2,1,0:T(8,128)(2,1)S(1)}, u32[]{:S(2)}, u32[]{:S(2)}) collective-permute-start(bf16[2,64,256]{2,1,0:T(8,128)(2,1)S(1)} %get-tuple-element.47), channel_id=1, source_target_pairs={{0,4},{1,5},{2,6},{3,7},{4,0},{5,1},{6,2},{7,3},{8,12},{9,13},{10,... | collective-permute-start | bytes 196616 | tf_op jit(solution)/shard_map/ppermute | solution.py:366
  8.4 0.1 collective-permute-start.6
  8.6 4.0 %collective-permute-start.1 = (bf16[192,128]{1,0:T(8,128)(2,1)S(1)}, bf16[192,128]{1,0:T(8,128)(2,1)S(1)}, u32[]{:S(2)}, u32[]{:S(2)}) collective-permute-start(bf16[192,128]{1,0:T(8,128)(2,1)S(1)} %get-tuple-element.40), channel_id=1, source_target_pairs={{0,24},{8,16},{16,8},{24,0},{1,25},{9,17},{17,9},{25,1},{2,26},{10... | collective-permute-start | bytes 147464 | tf_op jit(solution)/shard_map/ppermute | solution.py:355
  12.6 0.0 collective-permute-start.2
  12.6 0.0 collective-permute-done.4.rest_1_
  12.6 0.6 %collective-permute-start.3 = (bf16[192,128]{1,0:T(8,128)(2,1)S(1)}, bf16[192,128]{1,0:T(8,128)(2,1)S(1)}, u32[]{:S(2)}, u32[]{:S(2)}) collective-permute-start(bf16[192,128]{1,0:T(8,128)(2,1)S(1)} %get-tuple-element.42), channel_id=1, source_target_pairs={{0,8},{8,0},{16,24},{24,16},{1,9},{9,1},{17,25},{25,17},{2,10},{10... | collective-permute-start | bytes 147464 | tf_op jit(solution)/shard_map/ppermute | solution.py:355
  13.1 0.0 collective-permute-done.5.rest_2_
  13.1 0.0 collective-permute-done.6.rest_3_
  13.1 0.0 copy-start.2
  13.2 0.3 shard_map.126
  13.4 3.9 %collective-permute-start.7 = (bf16[192,128]{1,0:T(8,128)(2,1)S(1)}, bf16[192,128]{1,0:T(8,128)(2,1)S(1)}, u32[]{:S(2)}, u32[]{:S(2)}) collective-permute-start(bf16[192,128]{1,0:T(8,128)(2,1)S(1)} %get-tuple-element.50), channel_id=1, source_target_pairs={{0,24},{8,16},{16,8},{24,0},{1,25},{9,17},{17,9},{25,1},{2,26},{10... | collective-permute-start | bytes 147464 | tf_op jit(solution)/shard_map/ppermute | solution.py:355
  17.3 0.0 collective-permute-start.8
  17.3 0.0 collective-permute-done.1.rest_0_
  17.3 0.6 %collective-permute-start.9 = (bf16[192,128]{1,0:T(8,128)(2,1)S(1)}, bf16[192,128]{1,0:T(8,128)(2,1)S(1)}, u32[]{:S(2)}, u32[]{:S(2)}) collective-permute-start(bf16[192,128]{1,0:T(8,128)(2,1)S(1)} %get-tuple-element.52), channel_id=1, source_target_pairs={{0,8},{8,0},{16,24},{24,16},{1,9},{9,1},{17,25},{25,17},{2,10},{10... | collective-permute-start | bytes 147464 | tf_op jit(solution)/shard_map/ppermute | solution.py:355
  18.0 0.2 collective-permute-done.2.rest_1_
  18.1 0.0 collective-permute-done.3.rest_2_
  18.1 1.2 %shard_map.125.own_ref = f32[128,1024]{1,0:T(8,128)S(1)} custom-call(s32[1]{0:T(128)} %bitcast.me_ref, bf16[192,512]{1,0:T(8,128)(2,1)} %bitcast.23, bf16[768,1024]{1,0:T(8,128)(2,1)S(1)} %copy-done, bf16[192,128]{1,0:T(8,128)(2,1)S(1)} %collective-permute-done.1.rest_0_, bf16[192,128]{1,0:T(8,128)(2,1)S(1)} %collective-permute-done.2.rest_1_, ...), custom_call_target="tpu_custom_call" | custom-call | flops 201326592 | bytes 2097152 | tf_op jit(solution)/shard_map/pallas_call | solution.py:32
  19.3 0.4 %collective-permute-done.7.rest_1_ = bf16[192,128]{1,0:T(8,128)(2,1)S(1)} collective-permute-done((bf16[192,128]{1,0:T(8,128)(2,1)S(1)}, bf16[192,128]{1,0:T(8,128)(2,1)S(1)}, u32[]{:S(2)}, u32[]{:S(2)}) %collective-permute-start.7) | collective-permute-done | bytes 49184 | tf_op jit(solution)/shard_map/ppermute | solution.py:355
  19.8 2.6 %collective-permute-done.8.rest_2_ = bf16[192,128]{1,0:T(8,128)(2,1)S(1)} collective-permute-done((bf16[192,128]{1,0:T(8,128)(2,1)S(1)}, bf16[192,128]{1,0:T(8,128)(2,1)S(1)}, u32[]{:S(2)}, u32[]{:S(2)}) %collective-permute-start.8) | collective-permute-done | bytes 49184 | tf_op jit(solution)/shard_map/ppermute | solution.py:355
  22.3 0.0 collective-permute-done.9.rest_3_
  22.3 0.0 copy-done.2
  22.3 0.0 copy-start.3
  22.3 0.7 %shard_map.127 = (bf16[128,1024]{1,0:T(8,128)(2,1)S(1)}, bf16[153,128]{1,0:T(8,128)(2,1)S(1)}, bf16[153,128]{1,0:T(8,128)(2,1)S(1)}, bf16[153,128]{1,0:T(8,128)(2,1)S(1)}, bf16[153,128]{1,0:T(8,128)(2,1)S(1)}) custom-call(s32[1]{0:T(128)} %bitcast.me_ref, bf16[768,1024]{1,0:T(8,128)(2,1)S(1)} %copy-done, bf16[768,1024]{1,0:T(8,128)(2,1)S(1)} %copy-done.1, ...), custom_call_target="tpu_custom_call" | custom-call | flops 201326592 | bytes 2097152 | tf_op jit(solution)/shard_map/pallas_call | solution.py:32
  23.0 1.5 %collective-permute-start.10 = (bf16[153,128]{1,0:T(8,128)(2,1)S(1)}, bf16[153,128]{1,0:T(8,128)(2,1)S(1)}, u32[]{:S(2)}, u32[]{:S(2)}) collective-permute-start(bf16[153,128]{1,0:T(8,128)(2,1)S(1)} %get-tuple-element.57), channel_id=1, source_target_pairs={{0,24},{8,16},{16,8},{24,0},{1,25},{9,17},{17,9},{25,1},{2,26},{10... | collective-permute-start | bytes 117512 | tf_op jit(solution)/shard_map/ppermute | solution.py:355
  24.5 0.6 %collective-permute-start.11 = (bf16[153,128]{1,0:T(8,128)(2,1)S(1)}, bf16[153,128]{1,0:T(8,128)(2,1)S(1)}, u32[]{:S(2)}, u32[]{:S(2)}) collective-permute-start(bf16[153,128]{1,0:T(8,128)(2,1)S(1)} %get-tuple-element.58), channel_id=1, source_target_pairs={{0,16},{8,24},{16,0},{24,8},{1,17},{9,25},{17,1},{25,9},{2,18},{10... | collective-permute-start | bytes 117512 | tf_op jit(solution)/shard_map/ppermute | solution.py:355
  25.2 2.3 %collective-permute-start.12 = (bf16[153,128]{1,0:T(8,128)(2,1)S(1)}, bf16[153,128]{1,0:T(8,128)(2,1)S(1)}, u32[]{:S(2)}, u32[]{:S(2)}) collective-permute-start(bf16[153,128]{1,0:T(8,128)(2,1)S(1)} %get-tuple-element.59), channel_id=1, source_target_pairs={{0,8},{8,0},{16,24},{24,16},{1,9},{9,1},{17,25},{25,17},{2,10},{10... | collective-permute-start | bytes 117512 | tf_op jit(solution)/shard_map/ppermute | solution.py:355
  27.5 0.9 %shard_map.130.hits_ref.after = bf16[128,512]{1,0:T(8,128)(2,1)S(1)} custom-call(bf16[153,128]{1,0:T(8,128)(2,1)S(1)} %get-tuple-element.56.rest_0_.after, s32[1]{0:T(128)} %bitcast.me_ref, s32[1]{0:T(128)} %bitcast.4.part_ref, s32[8,4,16]{2,1,0:T(4,128)} %bitcast.28), custom_call_target="tpu_custom_call" | custom-call | bytes 524288 | tf_op jit(solution)/shard_map/pallas_call | solution.py:32
  28.4 0.5 %collective-permute-done.10.rest_1_ = bf16[153,128]{1,0:T(8,128)(2,1)S(1)} collective-permute-done((bf16[153,128]{1,0:T(8,128)(2,1)S(1)}, bf16[153,128]{1,0:T(8,128)(2,1)S(1)}, u32[]{:S(2)}, u32[]{:S(2)}) %collective-permute-start.10) | collective-permute-done | bytes 39200 | tf_op jit(solution)/shard_map/ppermute | solution.py:355
  28.9 0.6 %collective-permute-done.11.rest_2_ = bf16[153,128]{1,0:T(8,128)(2,1)S(1)} collective-permute-done((bf16[153,128]{1,0:T(8,128)(2,1)S(1)}, bf16[153,128]{1,0:T(8,128)(2,1)S(1)}, u32[]{:S(2)}, u32[]{:S(2)}) %collective-permute-start.11) | collective-permute-done | bytes 39200 | tf_op jit(solution)/shard_map/ppermute | solution.py:355
  29.5 0.4 %collective-permute-done.12.rest_3_ = bf16[153,128]{1,0:T(8,128)(2,1)S(1)} collective-permute-done((bf16[153,128]{1,0:T(8,128)(2,1)S(1)}, bf16[153,128]{1,0:T(8,128)(2,1)S(1)}, u32[]{:S(2)}, u32[]{:S(2)}) %collective-permute-start.12) | collective-permute-done | bytes 39200 | tf_op jit(solution)/shard_map/ppermute | solution.py:355
  29.9 0.3 shard_map.131
  30.1 0.1 collective-permute-start.13
  30.2 1.2 %collective-permute-done.13.got_ref = bf16[4,16,256]{2,1,0:T(8,128)(2,1)S(1)} collective-permute-done((bf16[4,16,256]{2,1,0:T(8,128)(2,1)S(1)}, bf16[4,16,256]{2,1,0:T(8,128)(2,1)S(1)}, u32[]{:S(2)}, u32[]{:S(2)}) %collective-permute-start.13) | collective-permute-done | bytes 32800 | tf_op jit(solution)/shard_map/ppermute | solution.py:362
  31.4 2.5 %collective-permute-start.14 = (bf16[2,16,256]{2,1,0:T(8,128)(2,1)S(1)}, bf16[2,16,256]{2,1,0:T(8,128)(2,1)S(1)}, u32[]{:S(2)}, u32[]{:S(2)}) collective-permute-start(bf16[2,16,256]{2,1,0:T(8,128)(2,1)S(1)} %get-tuple-element.63), channel_id=1, source_target_pairs={{0,6},{1,7},{2,4},{3,5},{4,2},{5,3},{6,0},{7,1},{8,14},{9,15},{10,... | collective-permute-start | bytes 49160 | tf_op jit(solution)/shard_map/ppermute | solution.py:366
  33.9 0.5 %collective-permute-start.15 = (bf16[2,16,256]{2,1,0:T(8,128)(2,1)S(1)}, bf16[2,16,256]{2,1,0:T(8,128)(2,1)S(1)}, u32[]{:S(2)}, u32[]{:S(2)}) collective-permute-start(bf16[2,16,256]{2,1,0:T(8,128)(2,1)S(1)} %get-tuple-element.64), channel_id=1, source_target_pairs={{0,4},{1,5},{2,6},{3,7},{4,0},{5,1},{6,2},{7,3},{8,12},{9,13},{10,... | collective-permute-start | bytes 49160 | tf_op jit(solution)/shard_map/ppermute | solution.py:366
  34.4 0.5 %collective-permute-start.16 = (bf16[2,16,256]{2,1,0:T(8,128)(2,1)S(1)}, bf16[2,16,256]{2,1,0:T(8,128)(2,1)S(1)}, u32[]{:S(2)}, u32[]{:S(2)}) collective-permute-start(bf16[2,16,256]{2,1,0:T(8,128)(2,1)S(1)} %get-tuple-element.65), channel_id=1, source_target_pairs={{0,2},{1,3},{2,0},{3,1},{4,6},{5,7},{6,4},{7,5},{8,10},{9,11},{10,... | collective-permute-start | bytes 49160 | tf_op jit(solution)/shard_map/ppermute | solution.py:366
  34.9 0.7 %shard_map.128 = (f32[153,128]{1,0:T(8,128)S(1)}, bf16[128,1024]{1,0:T(8,128)(2,1)}) custom-call(bf16[128,1024]{1,0:T(8,128)(2,1)S(1)} %get-tuple-element.53.hidden_ref, bf16[153,1024]{1,0:T(8,128)(2,1)S(1)} %bitcast.20), custom_call_target="tpu_custom_call" | custom-call | flops 40108032 | bytes 1048576 | tf_op jit(solution)/shard_map/pallas_call | solution.py:32
  35.6 0.2 shard_map.129.near_ref
  35.9 0.2 collective-permute-done.14.rest_1_
  36.0 1.6 %collective-permute-done.15.rest_2_ = bf16[2,16,256]{2,1,0:T(8,128)(2,1)S(1)} collective-permute-done((bf16[2,16,256]{2,1,0:T(8,128)(2,1)S(1)}, bf16[2,16,256]{2,1,0:T(8,128)(2,1)S(1)}, u32[]{:S(2)}, u32[]{:S(2)}) %collective-permute-start.15) | collective-permute-done | bytes 16416 | tf_op jit(solution)/shard_map/ppermute | solution.py:366
  37.6 0.5 %collective-permute-done.16.rest_3_ = bf16[2,16,256]{2,1,0:T(8,128)(2,1)S(1)} collective-permute-done((bf16[2,16,256]{2,1,0:T(8,128)(2,1)S(1)}, bf16[2,16,256]{2,1,0:T(8,128)(2,1)S(1)}, u32[]{:S(2)}, u32[]{:S(2)}) %collective-permute-start.16) | collective-permute-done | bytes 16416 | tf_op jit(solution)/shard_map/ppermute | solution.py:366
  38.1 0.9 %shard_map.133 = f32[153,1,128]{2,1,0:T(1,128)} custom-call(s32[1]{0:T(128)} %bitcast.me_ref, f32[153,128]{1,0:T(8,128)S(1)} %shard_map.129.near_ref, bf16[4,8,16,128]{3,2,1,0:T(8,128)(2,1)S(1)} %get-tuple-element.44.edges_ref, f32[4,208,128]{2,1,0:T(8,128)S(1)} %get-tuple-element.43.sums_ref, bf16[2,16,256]{2,1,0:T(8,128)(2,1)S(1)} %get-tuple-element.62.rest_0_, ...), custom_call_target="tpu_custom_call" | custom-call | flops 5013504 | bytes 524288 | tf_op jit(solution)/shard_map/pallas_call | solution.py:32
  (6 shorter events, 0.0 us)
Async XLA Ops:
  0.6 17.5 %copy-start = (bf16[768,1024]{1,0:T(8,128)(2,1)S(1)}, bf16[768,1024]{1,0:T(8,128)(2,1)}, u32[]{:S(2)}) copy-start(bf16[768,1024]{1,0:T(8,128)(2,1)} %self_weight_ref.1) | copy-start | bytes 4718596
  2.2 2.2 %collective-permute-start = (bf16[4,64,256]{2,1,0:T(8,128)(2,1)S(1)}, bf16[4,64,256]{2,1,0:T(8,128)(2,1)S(1)}, u32[]{:S(2)}, u32[]{:S(2)}) collective-permute-start(bf16[4,64,256]{2,1,0:T(8,128)(2,1)S(1)} %get-tuple-element.36), channel_id=1, source_target_pairs={{0,1},{1,0},{2,3},{3,2},{4,5},{5,4},{6,7},{7,6},{8,9},{9,8},{10,11... | collective-permute-start | bytes 393224 | tf_op jit(solution)/shard_map/ppermute | solution.py:362
  4.4 8.2 %collective-permute-start.4 = (bf16[2,64,256]{2,1,0:T(8,128)(2,1)S(1)}, bf16[2,64,256]{2,1,0:T(8,128)(2,1)S(1)}, u32[]{:S(2)}, u32[]{:S(2)}) collective-permute-start(bf16[2,64,256]{2,1,0:T(8,128)(2,1)S(1)} %get-tuple-element.46), channel_id=1, source_target_pairs={{0,6},{1,7},{2,4},{3,5},{4,2},{5,3},{6,0},{7,1},{8,14},{9,15},{10,... | collective-permute-start | bytes 196616 | tf_op jit(solution)/shard_map/ppermute | solution.py:366
  7.9 5.2 %collective-permute-start.5 = (bf16[2,64,256]{2,1,0:T(8,128)(2,1)S(1)}, bf16[2,64,256]{2,1,0:T(8,128)(2,1)S(1)}, u32[]{:S(2)}, u32[]{:S(2)}) collective-permute-start(bf16[2,64,256]{2,1,0:T(8,128)(2,1)S(1)} %get-tuple-element.47), channel_id=1, source_target_pairs={{0,4},{1,5},{2,6},{3,7},{4,0},{5,1},{6,2},{7,3},{8,12},{9,13},{10,... | collective-permute-start | bytes 196616 | tf_op jit(solution)/shard_map/ppermute | solution.py:366
  8.4 4.7 %collective-permute-start.6 = (bf16[2,64,256]{2,1,0:T(8,128)(2,1)S(1)}, bf16[2,64,256]{2,1,0:T(8,128)(2,1)S(1)}, u32[]{:S(2)}, u32[]{:S(2)}) collective-permute-start(bf16[2,64,256]{2,1,0:T(8,128)(2,1)S(1)} %get-tuple-element.48), channel_id=1, source_target_pairs={{0,2},{1,3},{2,0},{3,1},{4,6},{5,7},{6,4},{7,5},{8,10},{9,11},{10,... | collective-permute-start | bytes 196616 | tf_op jit(solution)/shard_map/ppermute | solution.py:366
  8.6 8.8 %collective-permute-start.1 = (bf16[192,128]{1,0:T(8,128)(2,1)S(1)}, bf16[192,128]{1,0:T(8,128)(2,1)S(1)}, u32[]{:S(2)}, u32[]{:S(2)}) collective-permute-start(bf16[192,128]{1,0:T(8,128)(2,1)S(1)} %get-tuple-element.40), channel_id=1, source_target_pairs={{0,24},{8,16},{16,8},{24,0},{1,25},{9,17},{17,9},{25,1},{2,26},{10... | collective-permute-start | bytes 147464 | tf_op jit(solution)/shard_map/ppermute | solution.py:355
  12.6 5.6 %collective-permute-start.2 = (bf16[192,128]{1,0:T(8,128)(2,1)S(1)}, bf16[192,128]{1,0:T(8,128)(2,1)S(1)}, u32[]{:S(2)}, u32[]{:S(2)}) collective-permute-start(bf16[192,128]{1,0:T(8,128)(2,1)S(1)} %get-tuple-element.41), channel_id=1, source_target_pairs={{0,16},{8,24},{16,0},{24,8},{1,17},{9,25},{17,1},{25,9},{2,18},{10... | collective-permute-start | bytes 147464 | tf_op jit(solution)/shard_map/ppermute | solution.py:355
  12.6 5.5 %collective-permute-start.3 = (bf16[192,128]{1,0:T(8,128)(2,1)S(1)}, bf16[192,128]{1,0:T(8,128)(2,1)S(1)}, u32[]{:S(2)}, u32[]{:S(2)}) collective-permute-start(bf16[192,128]{1,0:T(8,128)(2,1)S(1)} %get-tuple-element.42), channel_id=1, source_target_pairs={{0,8},{8,0},{16,24},{24,16},{1,9},{9,1},{17,25},{25,17},{2,10},{10... | collective-permute-start | bytes 147464 | tf_op jit(solution)/shard_map/ppermute | solution.py:355
  13.1 9.2 %copy-start.1 = (bf16[768,1024]{1,0:T(8,128)(2,1)S(1)}, bf16[768,1024]{1,0:T(8,128)(2,1)}, u32[]{:S(2)}) copy-start(bf16[768,1024]{1,0:T(8,128)(2,1)} %weight_ref.3) | copy-start | bytes 4718596
  13.1 9.2 %copy-start.2 = (bf16[1024,153]{0,1:T(8,128)(2,1)S(1)}, bf16[1024,153]{0,1:T(8,128)(2,1)}, u32[]{:S(2)}) copy-start(bf16[1024,153]{0,1:T(8,128)(2,1)} %param.21) | copy-start | bytes 940036
  13.4 6.3 %collective-permute-start.7 = (bf16[192,128]{1,0:T(8,128)(2,1)S(1)}, bf16[192,128]{1,0:T(8,128)(2,1)S(1)}, u32[]{:S(2)}, u32[]{:S(2)}) collective-permute-start(bf16[192,128]{1,0:T(8,128)(2,1)S(1)} %get-tuple-element.50), channel_id=1, source_target_pairs={{0,24},{8,16},{16,8},{24,0},{1,25},{9,17},{17,9},{25,1},{2,26},{10... | collective-permute-start | bytes 147464 | tf_op jit(solution)/shard_map/ppermute | solution.py:355
  17.3 5.0 %collective-permute-start.8 = (bf16[192,128]{1,0:T(8,128)(2,1)S(1)}, bf16[192,128]{1,0:T(8,128)(2,1)S(1)}, u32[]{:S(2)}, u32[]{:S(2)}) collective-permute-start(bf16[192,128]{1,0:T(8,128)(2,1)S(1)} %get-tuple-element.51), channel_id=1, source_target_pairs={{0,16},{8,24},{16,0},{24,8},{1,17},{9,25},{17,1},{25,9},{2,18},{10... | collective-permute-start | bytes 147464 | tf_op jit(solution)/shard_map/ppermute | solution.py:355
  17.3 5.0 %collective-permute-start.9 = (bf16[192,128]{1,0:T(8,128)(2,1)S(1)}, bf16[192,128]{1,0:T(8,128)(2,1)S(1)}, u32[]{:S(2)}, u32[]{:S(2)}) collective-permute-start(bf16[192,128]{1,0:T(8,128)(2,1)S(1)} %get-tuple-element.52), channel_id=1, source_target_pairs={{0,8},{8,0},{16,24},{24,16},{1,9},{9,1},{17,25},{25,17},{2,10},{10... | collective-permute-start | bytes 147464 | tf_op jit(solution)/shard_map/ppermute | solution.py:355
  22.3 12.6 %copy-start.3 = (bf16[1024,153]{0,1:T(8,128)(2,1)S(1)}, bf16[1024,153]{0,1:T(8,128)(2,1)}, u32[]{:S(2)}) copy-start(bf16[1024,153]{0,1:T(8,128)(2,1)} %param.20) | copy-start | bytes 940036
  23.0 5.9 %collective-permute-start.10 = (bf16[153,128]{1,0:T(8,128)(2,1)S(1)}, bf16[153,128]{1,0:T(8,128)(2,1)S(1)}, u32[]{:S(2)}, u32[]{:S(2)}) collective-permute-start(bf16[153,128]{1,0:T(8,128)(2,1)S(1)} %get-tuple-element.57), channel_id=1, source_target_pairs={{0,24},{8,16},{16,8},{24,0},{1,25},{9,17},{17,9},{25,1},{2,26},{10... | collective-permute-start | bytes 117512 | tf_op jit(solution)/shard_map/ppermute | solution.py:355
  24.5 4.9 %collective-permute-start.11 = (bf16[153,128]{1,0:T(8,128)(2,1)S(1)}, bf16[153,128]{1,0:T(8,128)(2,1)S(1)}, u32[]{:S(2)}, u32[]{:S(2)}) collective-permute-start(bf16[153,128]{1,0:T(8,128)(2,1)S(1)} %get-tuple-element.58), channel_id=1, source_target_pairs={{0,16},{8,24},{16,0},{24,8},{1,17},{9,25},{17,1},{25,9},{2,18},{10... | collective-permute-start | bytes 117512 | tf_op jit(solution)/shard_map/ppermute | solution.py:355
  25.2 4.7 %collective-permute-start.12 = (bf16[153,128]{1,0:T(8,128)(2,1)S(1)}, bf16[153,128]{1,0:T(8,128)(2,1)S(1)}, u32[]{:S(2)}, u32[]{:S(2)}) collective-permute-start(bf16[153,128]{1,0:T(8,128)(2,1)S(1)} %get-tuple-element.59), channel_id=1, source_target_pairs={{0,8},{8,0},{16,24},{24,16},{1,9},{9,1},{17,25},{25,17},{2,10},{10... | collective-permute-start | bytes 117512 | tf_op jit(solution)/shard_map/ppermute | solution.py:355
  30.1 1.3 %collective-permute-start.13 = (bf16[4,16,256]{2,1,0:T(8,128)(2,1)S(1)}, bf16[4,16,256]{2,1,0:T(8,128)(2,1)S(1)}, u32[]{:S(2)}, u32[]{:S(2)}) collective-permute-start(bf16[4,16,256]{2,1,0:T(8,128)(2,1)S(1)} %get-tuple-element.61), channel_id=1, source_target_pairs={{0,1},{1,0},{2,3},{3,2},{4,5},{5,4},{6,7},{7,6},{8,9},{9,8},{10,11... | collective-permute-start | bytes 98312 | tf_op jit(solution)/shard_map/ppermute | solution.py:362
  31.4 4.6 %collective-permute-start.14 = (bf16[2,16,256]{2,1,0:T(8,128)(2,1)S(1)}, bf16[2,16,256]{2,1,0:T(8,128)(2,1)S(1)}, u32[]{:S(2)}, u32[]{:S(2)}) collective-permute-start(bf16[2,16,256]{2,1,0:T(8,128)(2,1)S(1)} %get-tuple-element.63), channel_id=1, source_target_pairs={{0,6},{1,7},{2,4},{3,5},{4,2},{5,3},{6,0},{7,1},{8,14},{9,15},{10,... | collective-permute-start | bytes 49160 | tf_op jit(solution)/shard_map/ppermute | solution.py:366
  33.9 3.7 %collective-permute-start.15 = (bf16[2,16,256]{2,1,0:T(8,128)(2,1)S(1)}, bf16[2,16,256]{2,1,0:T(8,128)(2,1)S(1)}, u32[]{:S(2)}, u32[]{:S(2)}) collective-permute-start(bf16[2,16,256]{2,1,0:T(8,128)(2,1)S(1)} %get-tuple-element.64), channel_id=1, source_target_pairs={{0,4},{1,5},{2,6},{3,7},{4,0},{5,1},{6,2},{7,3},{8,12},{9,13},{10,... | collective-permute-start | bytes 49160 | tf_op jit(solution)/shard_map/ppermute | solution.py:366
  34.4 3.7 %collective-permute-start.16 = (bf16[2,16,256]{2,1,0:T(8,128)(2,1)S(1)}, bf16[2,16,256]{2,1,0:T(8,128)(2,1)S(1)}, u32[]{:S(2)}, u32[]{:S(2)}) collective-permute-start(bf16[2,16,256]{2,1,0:T(8,128)(2,1)S(1)} %get-tuple-element.65), channel_id=1, source_target_pairs={{0,2},{1,3},{2,0},{3,1},{4,6},{5,7},{6,4},{7,5},{8,10},{9,11},{10,... | collective-permute-start | bytes 49160 | tf_op jit(solution)/shard_map/ppermute | solution.py:366

commit v10 on v9

--- a/solution.py
+++ b/solution.py
@@ -59,6 +59,20 @@
 def behind(me, groups, k):
     step = step_of(groups, k)
     return me ^ step if groups & (groups - 1) == 0 else (me + groups - step) % groups
+
+
+def rounds_of(groups):
+    if groups == 4:
+        pairs = [[(0, 2)], [(0, 3), (1, 2)], [(1, 3)], [(0, 1), (2, 3)]]
+        return [dict(p + [(b, a) for a, b in p]) for p in pairs]
+    return [{i: ahead(i, groups, k) for i in range(groups)} for k in range(1, groups)]
+
+
+def look_up(table, me):
+    found = -1
+    for key, value in table.items():
+        found = jnp.where(me == key, value, found)
+    return found
 
 
 def step_to(a, b, count):
@@ -117,9 +131,9 @@
         table.wait()
         for other, out in enumerate((mine_ref, mate_ref)):
             lax.fori_loop(0, chips // chunk, lambda i, _: step(i, out, other, False), None)
-    for k in range(1, groups):
-        group = ahead(me_ref[0], groups, k)
-        blocks[k - 1][...] = features_ref[:width, pl.ds(pl.multiple_of(group * rows, rows), rows)]
+    for table, block in zip(rounds_of(groups), blocks):
+        group = jnp.maximum(look_up(table, me_ref[0]), 0)
+        block[...] = features_ref[:width, pl.ds(pl.multiple_of(group * rows, rows), rows)]
 
 
 def local_kernel(
@@ -215,9 +229,9 @@
         ).astype(bf16)
 
 
-def mean_kernel(late, me_ref, sums_ref, edges_ref, *rest):
+def mean_kernel(me_ref, sums_ref, edges_ref, *rest):
     groups, parts, slots, rows = edges_ref.shape
-    arrived, held, outs = rest[: parts // 2], rest[parts // 2 :][:late], rest[parts // 2 + late :]
+    arrived, outs = rest[: parts // 2], rest[parts // 2 :]
     width = outs[0].shape[0]
     for k in range(groups):
         group = ahead(me_ref[0], groups, k)
@@ -226,40 +240,36 @@
         far = dot(far, edges_ref[group].reshape(parts * slots, rows), FIRST)
         total = sums_ref[group, :width, :] + far[:width]
         outs[k][...] = (total / sums_ref[group, width : width + 1, :]).astype(bf16)
-    for block, out in zip(held, outs[groups:]):
-        out[...] = block[...]
-
-
-def rows_from(me, groups, k, width):
-    return pl.ds(pl.multiple_of(behind(me, groups, k) * width, width), width)
 
 
 def self_kernel(groups, me_ref, features_hbm, weight_ref, *rest):
-    early, (out_ref, own_ref, sem) = rest[:-3], rest[-3:]
+    blocks, (out_ref, own_ref, sem) = rest[:-3], rest[-3:]
     width, rows = own_ref.shape
     me = me_ref[0]
     own = pltpu.make_async_copy(
         features_hbm.at[:, pl.ds(pl.multiple_of(me * rows, rows), rows)], own_ref, sem
     )
     own.start()
-    span = pl.ds(pl.multiple_of(me * width, width), width)
-    total = jnp.zeros(out_ref.shape, f32)
-    for k, block in enumerate(early, 1):
-        total = total + dot(block[...], weight_ref[rows_from(me, groups, k, width), :], FIRST)
+    out_ref[...] = jnp.zeros_like(out_ref)
+
+    def add(block, source):
+        span = pl.ds(pl.multiple_of(source * width, width), width)
+        out_ref[...] += dot(block[...], weight_ref[span, :], FIRST)
+
+    for table, block in zip(rounds_of(groups), blocks):
+        source = look_up({b: a for a, b in table.items()}, me)
+        pl.when(source >= 0)(functools.partial(add, block, source))
     own.wait()
-    out_ref[...] = total + dot(own_ref[...], weight_ref[span, :], FIRST)
-
-
-def hidden_kernel(groups, late, me_ref, self_weight_ref, weight_ref, out_weight_ref, own_ref, *rest):
-    held, parts, (hidden_ref, *copies) = rest[:late], rest[late:][:groups], rest[late + groups :]
+    add(own_ref, me)
+
+
+def hidden_kernel(groups, me_ref, weight_ref, out_weight_ref, own_ref, *rest):
+    parts, (hidden_ref, *copies) = rest[:groups], rest[groups:]
     width = parts[0].shape[0]
-    me = me_ref[0]
     total = own_ref[...]
-    for k, block in enumerate(held, groups - late):
-        span = rows_from(me, groups, k, width)
-        total = total + dot(block[...], self_weight_ref[span, :], FIRST)
     for k, block in enumerate(parts):
-        span = rows_from(me, groups, k, width)
+        source = behind(me_ref[0], groups, k)
+        span = pl.ds(pl.multiple_of(source * width, width), width)
         total = total + dot(block[...], weight_ref[span, :], FIRST)
     hidden = jnp.maximum(total, 0.0).astype(bf16)
     hidden_ref[...] = hidden
@@ -344,18 +354,18 @@
     width, nodes = feature_rows.shape
     rows, slots = nodes // groups, sources.shape[3]
     hid, classes = self_one.shape[1], self_out.shape[1]
-    chips, late = parts // 2, 0
+    chips, rounds = parts // 2, rounds_of(groups)
     chunk = max(1, min(parts, 512 // (groups * slots)))
 
     def shape(*dims, dtype=bf16):
         return jax.ShapeDtypeStruct(dims, dtype)
 
-    def shift(blocks, first=1):
+    def shift(blocks):
         return [
             lax.ppermute(
                 block, "feat", [(i, ahead(i, groups, k)) for i in range(groups)]
             )
-            for k, block in enumerate(blocks, first)
+            for k, block in enumerate(blocks, 1)
         ]
 
     def to_mate(value):
@@ -375,7 +385,7 @@
     lanes = whole_lanes(width)
     mine, mate, *feature_blocks = call(
         functools.partial(gather_kernel, picked),
-        (shape(chips, groups * slots, lanes),) * 2 + (shape(width, rows),) * (groups - 1),
+        (shape(chips, groups * slots, lanes),) * 2 + (shape(width, rows),) * len(rounds),
         [SM, SM, HB, HB],
         [
             pltpu.VMEM((parts, groups, slots), jnp.int32),
@@ -421,40 +431,42 @@
     )
     paired = call(
         pair_kernel,
-        (shape(2, groups * slots, lanes),) * chips + (shape(width, rows),) * (groups - 1 - late),
-        [VM] * (2 + groups - late),
+        (shape(2, groups * slots, lanes),) * chips + (shape(width, rows),) * len(rounds),
+        [VM] * (3 + len(rounds)),
         (),
         0,
         1 << 20,
-    )(band, mine, mate, *feature_blocks[: groups - 1 - late])
+    )(band, mine, mate, *feature_blocks)
     arrived = to_chips(paired[:chips])
-    early_blocks = shift(paired[chips:])
-    moved = call(
-        functools.partial(mean_kernel, late),
-        (shape(width, rows),) * (groups + late),
-        [SM] + [VM] * (2 + chips + late),
+    feature_blocks = [
+        lax.ppermute(block, "feat", list(table.items()))
+        for table, block in zip(rounds, paired[chips:])
+    ]
+    means = call(
+        mean_kernel,
+        (shape(width, rows),) * groups,
+        [SM] + [VM] * (2 + chips),
         (),
         2 * nodes * parts * slots * width,
         1 << 20,
-    )(me, sums, edges, *arrived, *feature_blocks[groups - 1 - late :])
-    means = [moved[0]] + shift(moved[1:groups])
-    late_blocks = shift(moved[groups:], groups - late)
+    )(me, sums, edges, *arrived)
+    means = [means[0]] + shift(means[1:])
     own = call(
         functools.partial(self_kernel, groups),
         shape(rows, hid, dtype=f32),
-        [SM, HB] + [VM] * (groups - late),
+        [SM, HB] + [VM] * (1 + len(rounds)),
         [pltpu.VMEM((width, rows), bf16), pltpu.SemaphoreType.DMA],
         2 * rows * hid * groups * width,
         2 << 20,
-    )(me, feature_rows, self_one, *early_blocks)
+    )(me, feature_rows, self_one, *feature_blocks)
     hidden, *projected = call(
-        functools.partial(hidden_kernel, groups, late),
+        functools.partial(hidden_kernel, groups),
         (shape(rows, hid),) + (shape(classes, rows),) * groups,
-        [SM] + [VM] * (4 + late + groups),
+        [SM] + [VM] * (3 + groups),
         (),
         2 * rows * hid * groups * width,
         2 << 20,
-    )(me, self_one, neigh_one, neigh_out.T, own, *late_blocks, *means)
+    )(me, neigh_one, neigh_out.T, own, *means)
     hits = call(
         hits_kernel,
         shape(parts * slots, nodes),

time: 39.2 us -> 44.6 us (1.14)
  starting transfers between devices: 21.8 us -> 28.4 us
  waiting for transfers between devices: 8.04 us -> 6.81 us
    ppermute x0 -> x4, starting transfers between devices: none -> 11.3 us  [on_device(): lax.ppermute(block, 'feat', list(table.items()))]
    ppermute x9 -> x6, starting transfers between devices: 13.6 us -> 8.89 us  [shift(): lax.ppermute(block, 'feat', [(i, ahead(i, groups, k)) for i in range(grou...]
    ppermute x9 -> x6, waiting for transfers between devices: 4.6 us -> 3.35 us  [shift(): lax.ppermute(block, 'feat', [(i, ahead(i, groups, k)) for i in range(grou...]
  transfers between devices with their start and end apart: 17 -> 18, of which waited for: 10 -> 9; matrix products, arithmetic and copies ran while one was open for 0% -> 0% of each run, Pallas kernels for 13% -> 11%
where the time goes in v10:
time: 44.6 us; the launch traced here: 44.3 us
  starting transfers between devices  28.4 us (64%)
  Pallas kernels  8.19 us (18%)
  waiting for transfers between devices  6.81 us (15%)
  between operations  0.81 us (2%)
    ppermute x4, starting transfers between devices, on_device(): lax.ppermute(block, 'feat', list(table.items()))  11.3 us
    ppermute x6, starting transfers between devices, shift(): lax.ppermute(block, 'feat', [(i, ahead(i, groups, k)) for i in range(grou...  8.89 us
    pallas_call x12, Pallas kernels, placed(): run(*(pltpu.with_memory_space_constraint(value, pltpu.HBM) if spec is HB...  8.19 us
    ppermute x6, starting transfers between devices, to_chips(): lax.ppermute(blocks[j], 'dom', [(d, next_to(d // 2, j, chips) * 2 + d % 2...  7.65 us
    ppermute x6, waiting for transfers between devices, shift(): lax.ppermute(block, 'feat', [(i, ahead(i, groups, k)) for i in range(grou...  3.35 us
    ppermute x6, waiting for transfers between devices, to_chips(): lax.ppermute(blocks[j], 'dom', [(d, next_to(d // 2, j, chips) * 2 + d % 2...  2.26 us
    ppermute x2, waiting for transfers between devices, to_mate(): return lax.ppermute(value, 'dom', [(d, d ^ 1) for d in range(parts)])  1.2 us
  transfers between devices with their start and end apart: 18, of which 9 were waited for; matrix products, arithmetic and copies ran while one was open for 0% of the time, Pallas kernels for 11%

profile of v10, /device:TPU:0, one launch (start us, length us, event | category | flops | bytes accessed | tf_op | source)
XLA Modules:
  0.0 44.3 jit_solution(5295087008427025863)
XLA Ops:
  0.6 0.0 copy-start.1
  0.6 1.5 %shard_map.123 = (bf16[4,64,256]{2,1,0:T(8,128)(2,1)S(1)}, bf16[4,64,256]{2,1,0:T(8,128)(2,1)S(1)}, bf16[192,128]{1,0:T(8,128)(2,1)S(1)}, bf16[192,128]{1,0:T(8,...) custom-call(s32[1]{0:T(128)} %bitcast.me_ref, s32[1]{0:T(128)} %bitcast.4.part_ref, ...), custom_call_target="tpu_custom_call" | custom-call | flops 100663296 | bytes 1048576 | tf_op jit(solution)/shard_map/pallas_call | solution.py:32
  2.2 0.5 %collective-permute-start = (bf16[4,64,256]{2,1,0:T(8,128)(2,1)S(1)}, bf16[4,64,256]{2,1,0:T(8,128)(2,1)S(1)}, u32[]{:S(2)}, u32[]{:S(2)}) collective-permute-start(bf16[4,64,256]{2,1,0:T(8,128)(2,1)S(1)} %get-tuple-element.38), channel_id=1, source_target_pairs={{0,1},{1,0},{2,3},{3,2},{4,5},{5,4},{6,7},{7,6},{8,9},{9,8},{10,11... | collective-permute-start | bytes 393224 | tf_op jit(solution)/shard_map/ppermute | solution.py:372
  2.7 1.6 %shard_map.122 = (f32[4,208,128]{2,1,0:T(8,128)S(1)}, bf16[4,8,16,128]{3,2,1,0:T(8,128)(2,1)S(1)}, bf16[128,512]{1,0:T(8,128)(2,1)S(1)}) custom-call(s32[1]{0:T(128)} %bitcast.me_ref, s32[1]{0:T(128)} %bitcast.4.part_ref, s32[2,12]{1,0:T(2,128)} %bitcast.31, s32[4,8]{1,0:T(4,128)} %bitcast.30, bf16[192,512]{1,0:T(8,128)(2,1)} %bitcast.22, ...), custom_call_target="tpu_custom_call" | custom-call | flops 100663296 | bytes 1048576 | tf_op jit(solution)/shard_map/pallas_call | solution.py:32
  4.3 0.0 collective-permute-done.got_ref
  4.4 3.5 %collective-permute-start.5 = (bf16[2,64,256]{2,1,0:T(8,128)(2,1)S(1)}, bf16[2,64,256]{2,1,0:T(8,128)(2,1)S(1)}, u32[]{:S(2)}, u32[]{:S(2)}) collective-permute-start(bf16[2,64,256]{2,1,0:T(8,128)(2,1)S(1)} %get-tuple-element.50), channel_id=1, source_target_pairs={{0,6},{1,7},{2,4},{3,5},{4,2},{5,3},{6,0},{7,1},{8,14},{9,15},{10,... | collective-permute-start | bytes 196616 | tf_op jit(solution)/shard_map/ppermute | solution.py:376
  7.9 0.5 %collective-permute-start.6 = (bf16[2,64,256]{2,1,0:T(8,128)(2,1)S(1)}, bf16[2,64,256]{2,1,0:T(8,128)(2,1)S(1)}, u32[]{:S(2)}, u32[]{:S(2)}) collective-permute-start(bf16[2,64,256]{2,1,0:T(8,128)(2,1)S(1)} %get-tuple-element.51), channel_id=1, source_target_pairs={{0,4},{1,5},{2,6},{3,7},{4,0},{5,1},{6,2},{7,3},{8,12},{9,13},{10,... | collective-permute-start | bytes 196616 | tf_op jit(solution)/shard_map/ppermute | solution.py:376
  8.4 0.1 collective-permute-start.7
  8.6 4.9 %collective-permute-start.1 = (bf16[192,128]{1,0:T(8,128)(2,1)S(1)}, bf16[192,128]{1,0:T(8,128)(2,1)S(1)}, u32[]{:S(2)}, u32[]{:S(2)}) collective-permute-start(bf16[192,128]{1,0:T(8,128)(2,1)S(1)} %get-tuple-element.43), channel_id=1, source_target_pairs={{0,16},{16,0},{1,17},{17,1},{2,18},{18,2},{3,19},{19,3},{4,20},{20... | collective-permute-start | bytes 147464 | tf_op jit(solution)/shard_map/ppermute | solution.py:442
  13.5 0.1 collective-permute-start.2
  13.5 0.0 collective-permute-done.5.rest_1_
  13.5 0.7 %collective-permute-start.3 = (bf16[192,128]{1,0:T(8,128)(2,1)S(1)}, bf16[192,128]{1,0:T(8,128)(2,1)S(1)}, u32[]{:S(2)}, u32[]{:S(2)}) collective-permute-start(bf16[192,128]{1,0:T(8,128)(2,1)S(1)} %get-tuple-element.45), channel_id=1, source_target_pairs={{8,24},{24,8},{9,25},{25,9},{10,26},{26,10},{11,27},{27,11},{12,28... | collective-permute-start | bytes 147464 | tf_op jit(solution)/shard_map/ppermute | solution.py:442
  14.2 0.0 collective-permute-done.6.rest_2_
  14.2 5.7 %collective-permute-start.4 = (bf16[192,128]{1,0:T(8,128)(2,1)S(1)}, bf16[192,128]{1,0:T(8,128)(2,1)S(1)}, u32[]{:S(2)}, u32[]{:S(2)}) collective-permute-start(bf16[192,128]{1,0:T(8,128)(2,1)S(1)} %get-tuple-element.46), channel_id=1, source_target_pairs={{0,8},{16,24},{8,0},{24,16},{1,9},{17,25},{9,1},{25,17},{2,10},{18... | collective-permute-start | bytes 147464 | tf_op jit(solution)/shard_map/ppermute | solution.py:442
  19.9 0.0 collective-permute-done.7.rest_3_
  19.9 0.3 shard_map.126
  20.2 0.1 collective-permute-start.8
  20.2 0.0 collective-permute-done.1.rest_0_
  20.2 1.5 %collective-permute-start.9 = (bf16[192,128]{1,0:T(8,128)(2,1)S(1)}, bf16[192,128]{1,0:T(8,128)(2,1)S(1)}, u32[]{:S(2)}, u32[]{:S(2)}) collective-permute-start(bf16[192,128]{1,0:T(8,128)(2,1)S(1)} %get-tuple-element.55), channel_id=1, source_target_pairs={{0,16},{8,24},{16,0},{24,8},{1,17},{9,25},{17,1},{25,9},{2,18},{10... | collective-permute-start | bytes 147464 | tf_op jit(solution)/shard_map/ppermute | solution.py:365
  21.7 0.0 collective-permute-done.2.rest_1_
  21.7 2.9 %collective-permute-start.10 = (bf16[192,128]{1,0:T(8,128)(2,1)S(1)}, bf16[192,128]{1,0:T(8,128)(2,1)S(1)}, u32[]{:S(2)}, u32[]{:S(2)}) collective-permute-start(bf16[192,128]{1,0:T(8,128)(2,1)S(1)} %get-tuple-element.56), channel_id=1, source_target_pairs={{0,8},{8,0},{16,24},{24,16},{1,9},{9,1},{17,25},{25,17},{2,10},{10... | collective-permute-start | bytes 147464 | tf_op jit(solution)/shard_map/ppermute | solution.py:365
  24.6 0.0 collective-permute-done.3.rest_2_
  24.6 0.0 collective-permute-done.4.rest_3_
  24.6 0.0 copy-done.1
  24.6 1.1 %shard_map.125.own_ref = f32[128,1024]{1,0:T(8,128)S(1)} custom-call(s32[1]{0:T(128)} %bitcast.me_ref, bf16[192,512]{1,0:T(8,128)(2,1)} %bitcast.23, bf16[768,1024]{1,0:T(8,128)(2,1)S(1)} %copy-done.1, bf16[192,128]{1,0:T(8,128)(2,1)S(1)} %collective-permute-done.1.rest_0_, bf16[192,128]{1,0:T(8,128)(2,1)S(1)} %collective-permute-done.2.rest_1_, ...), custom_call_target="tpu_custom_call" | custom-call | flops 201326592 | bytes 2097152 | tf_op jit(solution)/shard_map/pallas_call | solution.py:32
  25.7 0.4 collective-permute-done.8.rest_1_
  26.1 0.0 collective-permute-done.9.rest_2_
  26.1 0.6 %collective-permute-done.10.rest_3_ = bf16[192,128]{1,0:T(8,128)(2,1)S(1)} collective-permute-done((bf16[192,128]{1,0:T(8,128)(2,1)S(1)}, bf16[192,128]{1,0:T(8,128)(2,1)S(1)}, u32[]{:S(2)}, u32[]{:S(2)}) %collective-permute-start.10) | collective-permute-done | bytes 49184 | tf_op jit(solution)/shard_map/ppermute | solution.py:365
  26.7 0.7 %shard_map.127 = (bf16[128,1024]{1,0:T(8,128)(2,1)S(1)}, bf16[153,128]{1,0:T(8,128)(2,1)S(1)}, bf16[153,128]{1,0:T(8,128)(2,1)S(1)}, bf16[153,128]{1,0:T(8,128)(2,1)S(1)}, bf16[153,128]{1,0:T(8,128)(2,1)S(1)}) custom-call(s32[1]{0:T(128)} %bitcast.me_ref, bf16[768,1024]{1,0:T(8,128)(2,1)S(1)} %copy-done, bf16[153,1024]{1,0:T(8,128)(2,1)S(1)} %bitcast.20, ...), custom_call_target="tpu_custom_call" | custom-call | flops 201326592 | bytes 2097152 | tf_op jit(solution)/shard_map/pallas_call | solution.py:32
  27.4 2.4 %collective-permute-start.11 = (bf16[153,128]{1,0:T(8,128)(2,1)S(1)}, bf16[153,128]{1,0:T(8,128)(2,1)S(1)}, u32[]{:S(2)}, u32[]{:S(2)}) collective-permute-start(bf16[153,128]{1,0:T(8,128)(2,1)S(1)} %get-tuple-element.61), channel_id=1, source_target_pairs={{0,24},{8,16},{16,8},{24,0},{1,25},{9,17},{17,9},{25,1},{2,26},{10... | collective-permute-start | bytes 117512 | tf_op jit(solution)/shard_map/ppermute | solution.py:365
  29.8 1.1 %collective-permute-start.12 = (bf16[153,128]{1,0:T(8,128)(2,1)S(1)}, bf16[153,128]{1,0:T(8,128)(2,1)S(1)}, u32[]{:S(2)}, u32[]{:S(2)}) collective-permute-start(bf16[153,128]{1,0:T(8,128)(2,1)S(1)} %get-tuple-element.62), channel_id=1, source_target_pairs={{0,16},{8,24},{16,0},{24,8},{1,17},{9,25},{17,1},{25,9},{2,18},{10... | collective-permute-start | bytes 117512 | tf_op jit(solution)/shard_map/ppermute | solution.py:365
  30.9 0.9 %collective-permute-start.13 = (bf16[153,128]{1,0:T(8,128)(2,1)S(1)}, bf16[153,128]{1,0:T(8,128)(2,1)S(1)}, u32[]{:S(2)}, u32[]{:S(2)}) collective-permute-start(bf16[153,128]{1,0:T(8,128)(2,1)S(1)} %get-tuple-element.63), channel_id=1, source_target_pairs={{0,8},{8,0},{16,24},{24,16},{1,9},{9,1},{17,25},{25,17},{2,10},{10... | collective-permute-start | bytes 117512 | tf_op jit(solution)/shard_map/ppermute | solution.py:365
  31.8 0.9 %shard_map.130.hits_ref.after = bf16[128,512]{1,0:T(8,128)(2,1)S(1)} custom-call(bf16[153,128]{1,0:T(8,128)(2,1)S(1)} %get-tuple-element.60.rest_0_.after, s32[1]{0:T(128)} %bitcast.me_ref, s32[1]{0:T(128)} %bitcast.4.part_ref, s32[8,4,16]{2,1,0:T(4,128)} %bitcast.28), custom_call_target="tpu_custom_call" | custom-call | bytes 524288 | tf_op jit(solution)/shard_map/pallas_call | solution.py:32
  32.7 0.6 %collective-permute-done.11.rest_1_ = bf16[153,128]{1,0:T(8,128)(2,1)S(1)} collective-permute-done((bf16[153,128]{1,0:T(8,128)(2,1)S(1)}, bf16[153,128]{1,0:T(8,128)(2,1)S(1)}, u32[]{:S(2)}, u32[]{:S(2)}) %collective-permute-start.11) | collective-permute-done | bytes 39200 | tf_op jit(solution)/shard_map/ppermute | solution.py:365
  33.3 1.4 %collective-permute-done.12.rest_2_ = bf16[153,128]{1,0:T(8,128)(2,1)S(1)} collective-permute-done((bf16[153,128]{1,0:T(8,128)(2,1)S(1)}, bf16[153,128]{1,0:T(8,128)(2,1)S(1)}, u32[]{:S(2)}, u32[]{:S(2)}) %collective-permute-start.12) | collective-permute-done | bytes 39200 | tf_op jit(solution)/shard_map/ppermute | solution.py:365
  34.7 0.4 collective-permute-done.13.rest_3_
  35.2 0.3 shard_map.131
  35.4 0.1 collective-permute-start.14
  35.5 1.2 %collective-permute-done.14.got_ref = bf16[4,16,256]{2,1,0:T(8,128)(2,1)S(1)} collective-permute-done((bf16[4,16,256]{2,1,0:T(8,128)(2,1)S(1)}, bf16[4,16,256]{2,1,0:T(8,128)(2,1)S(1)}, u32[]{:S(2)}, u32[]{:S(2)}) %collective-permute-start.14) | collective-permute-done | bytes 32800 | tf_op jit(solution)/shard_map/ppermute | solution.py:372
  36.7 2.5 %collective-permute-start.15 = (bf16[2,16,256]{2,1,0:T(8,128)(2,1)S(1)}, bf16[2,16,256]{2,1,0:T(8,128)(2,1)S(1)}, u32[]{:S(2)}, u32[]{:S(2)}) collective-permute-start(bf16[2,16,256]{2,1,0:T(8,128)(2,1)S(1)} %get-tuple-element.67), channel_id=1, source_target_pairs={{0,6},{1,7},{2,4},{3,5},{4,2},{5,3},{6,0},{7,1},{8,14},{9,15},{10,... | collective-permute-start | bytes 49160 | tf_op jit(solution)/shard_map/ppermute | solution.py:376
  39.2 0.5 %collective-permute-start.16 = (bf16[2,16,256]{2,1,0:T(8,128)(2,1)S(1)}, bf16[2,16,256]{2,1,0:T(8,128)(2,1)S(1)}, u32[]{:S(2)}, u32[]{:S(2)}) collective-permute-start(bf16[2,16,256]{2,1,0:T(8,128)(2,1)S(1)} %get-tuple-element.68), channel_id=1, source_target_pairs={{0,4},{1,5},{2,6},{3,7},{4,0},{5,1},{6,2},{7,3},{8,12},{9,13},{10,... | collective-permute-start | bytes 49160 | tf_op jit(solution)/shard_map/ppermute | solution.py:376
  39.6 0.5 %collective-permute-start.17 = (bf16[2,16,256]{2,1,0:T(8,128)(2,1)S(1)}, bf16[2,16,256]{2,1,0:T(8,128)(2,1)S(1)}, u32[]{:S(2)}, u32[]{:S(2)}) collective-permute-start(bf16[2,16,256]{2,1,0:T(8,128)(2,1)S(1)} %get-tuple-element.69), channel_id=1, source_target_pairs={{0,2},{1,3},{2,0},{3,1},{4,6},{5,7},{6,4},{7,5},{8,10},{9,11},{10,... | collective-permute-start | bytes 49160 | tf_op jit(solution)/shard_map/ppermute | solution.py:376
  40.2 0.7 %shard_map.128 = (f32[153,128]{1,0:T(8,128)S(1)}, bf16[128,1024]{1,0:T(8,128)(2,1)}) custom-call(bf16[128,1024]{1,0:T(8,128)(2,1)S(1)} %get-tuple-element.57.hidden_ref, bf16[153,1024]{1,0:T(8,128)(2,1)S(1)} %bitcast.19), custom_call_target="tpu_custom_call" | custom-call | flops 40108032 | bytes 1048576 | tf_op jit(solution)/shard_map/pallas_call | solution.py:32
  40.9 0.2 shard_map.129.near_ref
  41.1 0.2 collective-permute-done.15.rest_1_
  41.3 1.6 %collective-permute-done.16.rest_2_ = bf16[2,16,256]{2,1,0:T(8,128)(2,1)S(1)} collective-permute-done((bf16[2,16,256]{2,1,0:T(8,128)(2,1)S(1)}, bf16[2,16,256]{2,1,0:T(8,128)(2,1)S(1)}, u32[]{:S(2)}, u32[]{:S(2)}) %collective-permute-start.16) | collective-permute-done | bytes 16416 | tf_op jit(solution)/shard_map/ppermute | solution.py:376
  42.9 0.5 %collective-permute-done.17.rest_3_ = bf16[2,16,256]{2,1,0:T(8,128)(2,1)S(1)} collective-permute-done((bf16[2,16,256]{2,1,0:T(8,128)(2,1)S(1)}, bf16[2,16,256]{2,1,0:T(8,128)(2,1)S(1)}, u32[]{:S(2)}, u32[]{:S(2)}) %collective-permute-start.17) | collective-permute-done | bytes 16416 | tf_op jit(solution)/shard_map/ppermute | solution.py:376
  43.4 0.9 %shard_map.133 = f32[153,1,128]{2,1,0:T(1,128)} custom-call(s32[1]{0:T(128)} %bitcast.me_ref, f32[153,128]{1,0:T(8,128)S(1)} %shard_map.129.near_ref, bf16[4,8,16,128]{3,2,1,0:T(8,128)(2,1)S(1)} %get-tuple-element.48.edges_ref, f32[4,208,128]{2,1,0:T(8,128)S(1)} %get-tuple-element.47.sums_ref, bf16[2,16,256]{2,1,0:T(8,128)(2,1)S(1)} %get-tuple-element.66.rest_0_, ...), custom_call_target="tpu_custom_call" | custom-call | flops 5013504 | bytes 524288 | tf_op jit(solution)/shard_map/pallas_call | solution.py:32
  (8 shorter events, 0.1 us)
Async XLA Ops:
  0.6 24.0 %copy-start.1 = (bf16[768,1024]{1,0:T(8,128)(2,1)S(1)}, bf16[768,1024]{1,0:T(8,128)(2,1)}, u32[]{:S(2)}) copy-start(bf16[768,1024]{1,0:T(8,128)(2,1)} %weight_ref.2) | copy-start | bytes 4718596
  2.2 2.2 %collective-permute-start = (bf16[4,64,256]{2,1,0:T(8,128)(2,1)S(1)}, bf16[4,64,256]{2,1,0:T(8,128)(2,1)S(1)}, u32[]{:S(2)}, u32[]{:S(2)}) collective-permute-start(bf16[4,64,256]{2,1,0:T(8,128)(2,1)S(1)} %get-tuple-element.38), channel_id=1, source_target_pairs={{0,1},{1,0},{2,3},{3,2},{4,5},{5,4},{6,7},{7,6},{8,9},{9,8},{10,11... | collective-permute-start | bytes 393224 | tf_op jit(solution)/shard_map/ppermute | solution.py:372
  4.4 9.1 %collective-permute-start.5 = (bf16[2,64,256]{2,1,0:T(8,128)(2,1)S(1)}, bf16[2,64,256]{2,1,0:T(8,128)(2,1)S(1)}, u32[]{:S(2)}, u32[]{:S(2)}) collective-permute-start(bf16[2,64,256]{2,1,0:T(8,128)(2,1)S(1)} %get-tuple-element.50), channel_id=1, source_target_pairs={{0,6},{1,7},{2,4},{3,5},{4,2},{5,3},{6,0},{7,1},{8,14},{9,15},{10,... | collective-permute-start | bytes 196616 | tf_op jit(solution)/shard_map/ppermute | solution.py:376
  7.9 6.3 %collective-permute-start.6 = (bf16[2,64,256]{2,1,0:T(8,128)(2,1)S(1)}, bf16[2,64,256]{2,1,0:T(8,128)(2,1)S(1)}, u32[]{:S(2)}, u32[]{:S(2)}) collective-permute-start(bf16[2,64,256]{2,1,0:T(8,128)(2,1)S(1)} %get-tuple-element.51), channel_id=1, source_target_pairs={{0,4},{1,5},{2,6},{3,7},{4,0},{5,1},{6,2},{7,3},{8,12},{9,13},{10,... | collective-permute-start | bytes 196616 | tf_op jit(solution)/shard_map/ppermute | solution.py:376
  8.4 11.5 %collective-permute-start.7 = (bf16[2,64,256]{2,1,0:T(8,128)(2,1)S(1)}, bf16[2,64,256]{2,1,0:T(8,128)(2,1)S(1)}, u32[]{:S(2)}, u32[]{:S(2)}) collective-permute-start(bf16[2,64,256]{2,1,0:T(8,128)(2,1)S(1)} %get-tuple-element.52), channel_id=1, source_target_pairs={{0,2},{1,3},{2,0},{3,1},{4,6},{5,7},{6,4},{7,5},{8,10},{9,11},{10,... | collective-permute-start | bytes 196616 | tf_op jit(solution)/shard_map/ppermute | solution.py:376
  8.6 11.7 %collective-permute-start.1 = (bf16[192,128]{1,0:T(8,128)(2,1)S(1)}, bf16[192,128]{1,0:T(8,128)(2,1)S(1)}, u32[]{:S(2)}, u32[]{:S(2)}) collective-permute-start(bf16[192,128]{1,0:T(8,128)(2,1)S(1)} %get-tuple-element.43), channel_id=1, source_target_pairs={{0,16},{16,0},{1,17},{17,1},{2,18},{18,2},{3,19},{19,3},{4,20},{20... | collective-permute-start | bytes 147464 | tf_op jit(solution)/shard_map/ppermute | solution.py:442
  13.5 8.3 %collective-permute-start.2 = (bf16[192,128]{1,0:T(8,128)(2,1)S(1)}, bf16[192,128]{1,0:T(8,128)(2,1)S(1)}, u32[]{:S(2)}, u32[]{:S(2)}) collective-permute-start(bf16[192,128]{1,0:T(8,128)(2,1)S(1)} %get-tuple-element.44), channel_id=1, source_target_pairs={{0,24},{8,16},{24,0},{16,8},{1,25},{9,17},{25,1},{17,9},{2,26},{10... | collective-permute-start | bytes 147464 | tf_op jit(solution)/shard_map/ppermute | solution.py:442
  13.5 11.1 %collective-permute-start.3 = (bf16[192,128]{1,0:T(8,128)(2,1)S(1)}, bf16[192,128]{1,0:T(8,128)(2,1)S(1)}, u32[]{:S(2)}, u32[]{:S(2)}) collective-permute-start(bf16[192,128]{1,0:T(8,128)(2,1)S(1)} %get-tuple-element.45), channel_id=1, source_target_pairs={{8,24},{24,8},{9,25},{25,9},{10,26},{26,10},{11,27},{27,11},{12,28... | collective-permute-start | bytes 147464 | tf_op jit(solution)/shard_map/ppermute | solution.py:442
  14.2 10.4 %collective-permute-start.4 = (bf16[192,128]{1,0:T(8,128)(2,1)S(1)}, bf16[192,128]{1,0:T(8,128)(2,1)S(1)}, u32[]{:S(2)}, u32[]{:S(2)}) collective-permute-start(bf16[192,128]{1,0:T(8,128)(2,1)S(1)} %get-tuple-element.46), channel_id=1, source_target_pairs={{0,8},{16,24},{8,0},{24,16},{1,9},{17,25},{9,1},{25,17},{2,10},{18... | collective-permute-start | bytes 147464 | tf_op jit(solution)/shard_map/ppermute | solution.py:442
  19.9 6.8 %copy-start = (bf16[768,1024]{1,0:T(8,128)(2,1)S(1)}, bf16[768,1024]{1,0:T(8,128)(2,1)}, u32[]{:S(2)}) copy-start(bf16[768,1024]{1,0:T(8,128)(2,1)} %weight_ref.3) | copy-start | bytes 4718596
  19.9 6.8 %copy-start.3 = (bf16[1024,153]{0,1:T(8,128)(2,1)S(1)}, bf16[1024,153]{0,1:T(8,128)(2,1)}, u32[]{:S(2)}) copy-start(bf16[1024,153]{0,1:T(8,128)(2,1)} %param.21) | copy-start | bytes 940036
  20.2 6.0 %collective-permute-start.8 = (bf16[192,128]{1,0:T(8,128)(2,1)S(1)}, bf16[192,128]{1,0:T(8,128)(2,1)S(1)}, u32[]{:S(2)}, u32[]{:S(2)}) collective-permute-start(bf16[192,128]{1,0:T(8,128)(2,1)S(1)} %get-tuple-element.54), channel_id=1, source_target_pairs={{0,24},{8,16},{16,8},{24,0},{1,25},{9,17},{17,9},{25,1},{2,26},{10... | collective-permute-start | bytes 147464 | tf_op jit(solution)/shard_map/ppermute | solution.py:365
  20.2 5.9 %collective-permute-start.9 = (bf16[192,128]{1,0:T(8,128)(2,1)S(1)}, bf16[192,128]{1,0:T(8,128)(2,1)S(1)}, u32[]{:S(2)}, u32[]{:S(2)}) collective-permute-start(bf16[192,128]{1,0:T(8,128)(2,1)S(1)} %get-tuple-element.55), channel_id=1, source_target_pairs={{0,16},{8,24},{16,0},{24,8},{1,17},{9,25},{17,1},{25,9},{2,18},{10... | collective-permute-start | bytes 147464 | tf_op jit(solution)/shard_map/ppermute | solution.py:365
  21.7 4.9 %collective-permute-start.10 = (bf16[192,128]{1,0:T(8,128)(2,1)S(1)}, bf16[192,128]{1,0:T(8,128)(2,1)S(1)}, u32[]{:S(2)}, u32[]{:S(2)}) collective-permute-start(bf16[192,128]{1,0:T(8,128)(2,1)S(1)} %get-tuple-element.56), channel_id=1, source_target_pairs={{0,8},{8,0},{16,24},{24,16},{1,9},{9,1},{17,25},{25,17},{2,10},{10... | collective-permute-start | bytes 147464 | tf_op jit(solution)/shard_map/ppermute | solution.py:365
  26.7 13.5 %copy-start.2 = (bf16[1024,153]{0,1:T(8,128)(2,1)S(1)}, bf16[1024,153]{0,1:T(8,128)(2,1)}, u32[]{:S(2)}) copy-start(bf16[1024,153]{0,1:T(8,128)(2,1)} %param.20) | copy-start | bytes 940036
  27.4 6.0 %collective-permute-start.11 = (bf16[153,128]{1,0:T(8,128)(2,1)S(1)}, bf16[153,128]{1,0:T(8,128)(2,1)S(1)}, u32[]{:S(2)}, u32[]{:S(2)}) collective-permute-start(bf16[153,128]{1,0:T(8,128)(2,1)S(1)} %get-tuple-element.61), channel_id=1, source_target_pairs={{0,24},{8,16},{16,8},{24,0},{1,25},{9,17},{17,9},{25,1},{2,26},{10... | collective-permute-start | bytes 117512 | tf_op jit(solution)/shard_map/ppermute | solution.py:365
  29.8 4.9 %collective-permute-start.12 = (bf16[153,128]{1,0:T(8,128)(2,1)S(1)}, bf16[153,128]{1,0:T(8,128)(2,1)S(1)}, u32[]{:S(2)}, u32[]{:S(2)}) collective-permute-start(bf16[153,128]{1,0:T(8,128)(2,1)S(1)} %get-tuple-element.62), channel_id=1, source_target_pairs={{0,16},{8,24},{16,0},{24,8},{1,17},{9,25},{17,1},{25,9},{2,18},{10... | collective-permute-start | bytes 117512 | tf_op jit(solution)/shard_map/ppermute | solution.py:365
  30.9 4.2 %collective-permute-start.13 = (bf16[153,128]{1,0:T(8,128)(2,1)S(1)}, bf16[153,128]{1,0:T(8,128)(2,1)S(1)}, u32[]{:S(2)}, u32[]{:S(2)}) collective-permute-start(bf16[153,128]{1,0:T(8,128)(2,1)S(1)} %get-tuple-element.63), channel_id=1, source_target_pairs={{0,8},{8,0},{16,24},{24,16},{1,9},{9,1},{17,25},{25,17},{2,10},{10... | collective-permute-start | bytes 117512 | tf_op jit(solution)/shard_map/ppermute | solution.py:365
  35.4 1.3 %collective-permute-start.14 = (bf16[4,16,256]{2,1,0:T(8,128)(2,1)S(1)}, bf16[4,16,256]{2,1,0:T(8,128)(2,1)S(1)}, u32[]{:S(2)}, u32[]{:S(2)}) collective-permute-start(bf16[4,16,256]{2,1,0:T(8,128)(2,1)S(1)} %get-tuple-element.65), channel_id=1, source_target_pairs={{0,1},{1,0},{2,3},{3,2},{4,5},{5,4},{6,7},{7,6},{8,9},{9,8},{10,11... | collective-permute-start | bytes 98312 | tf_op jit(solution)/shard_map/ppermute | solution.py:372
  36.7 4.6 %collective-permute-start.15 = (bf16[2,16,256]{2,1,0:T(8,128)(2,1)S(1)}, bf16[2,16,256]{2,1,0:T(8,128)(2,1)S(1)}, u32[]{:S(2)}, u32[]{:S(2)}) collective-permute-start(bf16[2,16,256]{2,1,0:T(8,128)(2,1)S(1)} %get-tuple-element.67), channel_id=1, source_target_pairs={{0,6},{1,7},{2,4},{3,5},{4,2},{5,3},{6,0},{7,1},{8,14},{9,15},{10,... | collective-permute-start | bytes 49160 | tf_op jit(solution)/shard_map/ppermute | solution.py:376
  39.2 3.7 %collective-permute-start.16 = (bf16[2,16,256]{2,1,0:T(8,128)(2,1)S(1)}, bf16[2,16,256]{2,1,0:T(8,128)(2,1)S(1)}, u32[]{:S(2)}, u32[]{:S(2)}) collective-permute-start(bf16[2,16,256]{2,1,0:T(8,128)(2,1)S(1)} %get-tuple-element.68), channel_id=1, source_target_pairs={{0,4},{1,5},{2,6},{3,7},{4,0},{5,1},{6,2},{7,3},{8,12},{9,13},{10,... | collective-permute-start | bytes 49160 | tf_op jit(solution)/shard_map/ppermute | solution.py:376
  39.6 3.7 %collective-permute-start.17 = (bf16[2,16,256]{2,1,0:T(8,128)(2,1)S(1)}, bf16[2,16,256]{2,1,0:T(8,128)(2,1)S(1)}, u32[]{:S(2)}, u32[]{:S(2)}) collective-permute-start(bf16[2,16,256]{2,1,0:T(8,128)(2,1)S(1)} %get-tuple-element.69), channel_id=1, source_target_pairs={{0,2},{1,3},{2,0},{3,1},{4,6},{5,7},{6,4},{7,5},{8,10},{9,11},{10,... | collective-permute-start | bytes 49160 | tf_op jit(solution)/shard_map/ppermute | solution.py:376

commit v11 on v10

--- a/solution.py
+++ b/solution.py
@@ -61,20 +61,6 @@
     return me ^ step if groups & (groups - 1) == 0 else (me + groups - step) % groups
 
 
-def rounds_of(groups):
-    if groups == 4:
-        pairs = [[(0, 2)], [(0, 3), (1, 2)], [(1, 3)], [(0, 1), (2, 3)]]
-        return [dict(p + [(b, a) for a, b in p]) for p in pairs]
-    return [{i: ahead(i, groups, k) for i in range(groups)} for k in range(1, groups)]
-
-
-def look_up(table, me):
-    found = -1
-    for key, value in table.items():
-        found = jnp.where(me == key, value, found)
-    return found
-
-
 def step_to(a, b, count):
     step = a ^ b if count & (count - 1) == 0 else (b + count - a) % count
     return (count - step) % count
@@ -96,8 +82,20 @@
     return values.reshape(-1, values.shape[-1]).T
 
 
-def gather_kernel(chunk, me_ref, part_ref, sources_hbm, features_hbm, mine_ref, mate_ref, *rest):
-    blocks, (sources_ref, features_ref, order, hits, sems) = rest[:-5], rest[-5:]
+def gather_kernel(
+    chunk,
+    part_ref,
+    sources_hbm,
+    features_hbm,
+    mine_ref,
+    mate_ref,
+    blocks_ref,
+    sources_ref,
+    features_ref,
+    order,
+    hits,
+    sems,
+):
     parts, groups, slots = sources_ref.shape
     nodes = hits.shape[1]
     rows = nodes // groups
@@ -131,9 +129,8 @@
         table.wait()
         for other, out in enumerate((mine_ref, mate_ref)):
             lax.fori_loop(0, chips // chunk, lambda i, _: step(i, out, other, False), None)
-    for table, block in zip(rounds_of(groups), blocks):
-        group = jnp.maximum(look_up(table, me_ref[0]), 0)
-        block[...] = features_ref[:width, pl.ds(pl.multiple_of(group * rows, rows), rows)]
+    for g in range(groups):
+        blocks_ref[g] = features_ref[:width, g * rows : (g + 1) * rows]
 
 
 def local_kernel(
@@ -156,6 +153,7 @@
     targets_ref,
     weight_ref,
     bands,
+    degree_ref,
     sems,
 ):
     me = me_ref[0]
@@ -164,28 +162,19 @@
     width = features_hbm.shape[0]
     copies = fetch(
         sems,
+        (counts_hbm, counts_ref),
+        (targets_hbm, targets_ref),
+        (weight_hbm, weight_ref),
         (ids_hbm, ids_ref),
-        (counts_hbm, counts_ref),
         (features_hbm, features_ref.at[pl.ds(0, width), :]),
         (tiles_hbm, tiles_ref),
-        (targets_hbm, targets_ref),
-        (weight_hbm, weight_ref),
     )
     extra = features_ref.shape[0] - width
     features_ref[width:, :] = jnp.ones((extra, features_ref.shape[1]), bf16)
     bands[...] = jnp.zeros_like(bands)
-    for copy in copies:
+    degree_ref[...] = jnp.zeros_like(degree_ref)
+    for copy in copies[:3]:
         copy.wait()
-
-    def place(t, _):
-        at = pl.multiple_of(ids_ref[1, t] * rows, rows)
-        bands[ids_ref[0, t], :, pl.ds(at, rows)] = tiles_ref[t]
-        return 0
-
-    lax.fori_loop(0, tiles_ref.shape[0], place, 0, unroll=tiles_ref.shape[0] <= 16)
-    for g in range(groups):
-        sums_ref[g] = dot(features_ref[...], bands[g], LAST)
-    band_ref[...] = bands[me]
     lane = lax.broadcasted_iota(jnp.int32, (slots, rows), 1)
     slot = lax.broadcasted_iota(jnp.int32, (slots, rows), 0)
     chips, chip, core = parts // 2, part_ref[0] // 2, part_ref[0] % 2
@@ -203,13 +192,26 @@
                 values = jnp.where(hit, weight[:, n : n + 1], 0.0)
                 edges_ref[g, at] = values.astype(bf16)
                 degree = degree + jnp.sum(values, axis=0, keepdims=True)
-            sums_ref[g, width : width + 1, :] += degree
+            degree_ref[g] += degree
         return 0
 
     if parts == chunk:
         connect(0, 0)
     else:
         lax.fori_loop(0, parts // chunk, connect, 0)
+    for copy in copies[3:]:
+        copy.wait()
+
+    def place(t, _):
+        at = pl.multiple_of(ids_ref[1, t] * rows, rows)
+        bands[ids_ref[0, t], :, pl.ds(at, rows)] = tiles_ref[t]
+        return 0
+
+    lax.fori_loop(0, tiles_ref.shape[0], place, 0, unroll=tiles_ref.shape[0] <= 16)
+    for g in range(groups):
+        sums_ref[g] = dot(features_ref[...], bands[g], LAST)
+        sums_ref[g, width : width + 1, :] += degree_ref[g, :1]
+    band_ref[...] = bands[me]
 
 
 def hits_kernel(after, me_ref, part_ref, sources_hbm, hits_ref, sources_ref, sem):
@@ -242,25 +244,13 @@
         outs[k][...] = (total / sums_ref[group, width : width + 1, :]).astype(bf16)
 
 
-def self_kernel(groups, me_ref, features_hbm, weight_ref, *rest):
-    blocks, (out_ref, own_ref, sem) = rest[:-3], rest[-3:]
-    width, rows = own_ref.shape
-    me = me_ref[0]
-    own = pltpu.make_async_copy(
-        features_hbm.at[:, pl.ds(pl.multiple_of(me * rows, rows), rows)], own_ref, sem
-    )
-    own.start()
-    out_ref[...] = jnp.zeros_like(out_ref)
-
-    def add(block, source):
-        span = pl.ds(pl.multiple_of(source * width, width), width)
-        out_ref[...] += dot(block[...], weight_ref[span, :], FIRST)
-
-    for table, block in zip(rounds_of(groups), blocks):
-        source = look_up({b: a for a, b in table.items()}, me)
-        pl.when(source >= 0)(functools.partial(add, block, source))
-    own.wait()
-    add(own_ref, me)
+def self_kernel(weight_ref, blocks_ref, out_ref):
+    groups, width, _ = blocks_ref.shape
+    total = jnp.zeros(out_ref.shape, f32)
+    for g in range(groups):
+        weight = weight_ref[g * width : (g + 1) * width, :]
+        total = total + dot(blocks_ref[g], weight, FIRST)
+    out_ref[...] = total
 
 
 def hidden_kernel(groups, me_ref, weight_ref, out_weight_ref, own_ref, *rest):
@@ -354,7 +344,7 @@
     width, nodes = feature_rows.shape
     rows, slots = nodes // groups, sources.shape[3]
     hid, classes = self_one.shape[1], self_out.shape[1]
-    chips, rounds = parts // 2, rounds_of(groups)
+    chips = parts // 2
     chunk = max(1, min(parts, 512 // (groups * slots)))
 
     def shape(*dims, dtype=bf16):
@@ -383,10 +373,10 @@
 
     picked = min(chips, chunk)
     lanes = whole_lanes(width)
-    mine, mate, *feature_blocks = call(
+    mine, mate, feature_blocks = call(
         functools.partial(gather_kernel, picked),
-        (shape(chips, groups * slots, lanes),) * 2 + (shape(width, rows),) * len(rounds),
-        [SM, SM, HB, HB],
+        (shape(chips, groups * slots, lanes),) * 2 + (shape(groups, width, rows),),
+        [SM, HB, HB],
         [
             pltpu.VMEM((parts, groups, slots), jnp.int32),
             pltpu.VMEM((lanes, nodes), bf16),
@@ -396,7 +386,7 @@
         ],
         2 * nodes * nodes * width,
         1 << 20,
-    )(me, part, sources[0], feature_rows)
+    )(part, sources[0], feature_rows)
     mate = to_mate(mate)
     sums, edges, band = call(
         functools.partial(local_kernel, chunk),
@@ -414,6 +404,7 @@
             pltpu.VMEM((parts, groups, slots), jnp.int32),
             pltpu.VMEM((parts, groups, slots), bf16),
             pltpu.VMEM((groups, rows, nodes), bf16),
+            pltpu.VMEM((groups, 8, rows), f32),
             pltpu.SemaphoreType.DMA((6,)),
         ],
         2 * nodes * nodes * width,
@@ -429,19 +420,18 @@
         targets[0],
         edge_weight[0],
     )
-    paired = call(
+    *paired, feature_blocks = call(
         pair_kernel,
-        (shape(2, groups * slots, lanes),) * chips + (shape(width, rows),) * len(rounds),
-        [VM] * (3 + len(rounds)),
+        (shape(2, groups * slots, lanes),) * chips + (shape(groups, width, rows),),
+        [VM] * 4,
         (),
         0,
         1 << 20,
-    )(band, mine, mate, *feature_blocks)
-    arrived = to_chips(paired[:chips])
-    feature_blocks = [
-        lax.ppermute(block, "feat", list(table.items()))
-        for table, block in zip(rounds, paired[chips:])
-    ]
+    )(band, mine, mate, feature_blocks)
+    arrived = to_chips(paired)
+    feature_blocks = lax.all_to_all(
+        feature_blocks, "feat", split_axis=0, concat_axis=0, tiled=True
+    )
     means = call(
         mean_kernel,
         (shape(width, rows),) * groups,
@@ -452,13 +442,13 @@
     )(me, sums, edges, *arrived)
     means = [means[0]] + shift(means[1:])
     own = call(
-        functools.partial(self_kernel, groups),
+        self_kernel,
         shape(rows, hid, dtype=f32),
-        [SM, HB] + [VM] * (1 + len(rounds)),
-        [pltpu.VMEM((width, rows), bf16), pltpu.SemaphoreType.DMA],
+        [VM, VM],
+        (),
         2 * rows * hid * groups * width,
         2 << 20,
-    )(me, feature_rows, self_one, *feature_blocks)
+    )(self_one, feature_blocks)
     hidden, *projected = call(
         functools.partial(hidden_kernel, groups),
         (shape(rows, hid),) + (shape(classes, rows),) * groups,

time: 44.6 us -> 43.9 us (0.984)
  starting transfers between devices: 28.4 us -> 22.4 us
  waiting for transfers between devices: 6.81 us -> 12.2 us
    ppermute x4 -> x0, starting transfers between devices: 11.3 us -> none  [on_device(): lax.ppermute(block, 'feat', list(table.items()))]
    all_to_all x0 -> x1, starting transfers between devices: none -> 5.89 us  [on_device(): lax.all_to_all(feature_blocks, 'feat', split_axis=0, concat_axis=0, tiled...]
    ppermute x6, waiting for transfers between devices: 2.26 us -> 5.62 us  [to_chips(): lax.ppermute(blocks[j], 'dom', [(d, next_to(d // 2, j, chips) * 2 + d % 2...]
    ppermute x6, waiting for transfers between devices: 3.35 us -> 5.37 us  [shift(): lax.ppermute(block, 'feat', [(i, ahead(i, groups, k)) for i in range(grou...]
    ppermute x6, starting transfers between devices: 7.65 us -> 6.98 us  [to_chips(): lax.ppermute(blocks[j], 'dom', [(d, next_to(d // 2, j, chips) * 2 + d % 2...]
  transfers between devices with their start and end apart: 18 -> 15, of which waited for: 9 -> 12; matrix products, arithmetic and copies ran while one was open for 0% -> 0% of each run, Pallas kernels for 11% -> 10%
where the time goes in v11:
time: 43.9 us; the launch traced here: 43.6 us
  starting transfers between devices  22.4 us (51%)
  waiting for transfers between devices  12.2 us (28%)
  Pallas kernels  8.24 us (19%)
  between operations  0.75 us (2%)
    ppermute x6, starting transfers between devices, shift(): lax.ppermute(block, 'feat', [(i, ahead(i, groups, k)) for i in range(grou...  8.98 us
    pallas_call x12, Pallas kernels, placed(): run(*(pltpu.with_memory_space_constraint(value, pltpu.HBM) if spec is HB...  8.24 us
    ppermute x6, starting transfers between devices, to_chips(): lax.ppermute(blocks[j], 'dom', [(d, next_to(d // 2, j, chips) * 2 + d % 2...  6.98 us
    all_to_all x1, starting transfers between devices, on_device(): lax.all_to_all(feature_blocks, 'feat', split_axis=0, concat_axis=0, tiled...  5.89 us
    ppermute x6, waiting for transfers between devices, to_chips(): lax.ppermute(blocks[j], 'dom', [(d, next_to(d // 2, j, chips) * 2 + d % 2...  5.62 us
    ppermute x6, waiting for transfers between devices, shift(): lax.ppermute(block, 'feat', [(i, ahead(i, groups, k)) for i in range(grou...  5.37 us
    ppermute x2, waiting for transfers between devices, to_mate(): return lax.ppermute(value, 'dom', [(d, d ^ 1) for d in range(parts)])  1.2 us
  transfers between devices with their start and end apart: 15, of which 12 were waited for; matrix products, arithmetic and copies ran while one was open for 0% of the time, Pallas kernels for 10%

profile of v11, /device:TPU:0, one launch (start us, length us, event | category | flops | bytes accessed | tf_op | source)
XLA Modules:
  0.0 43.6 jit_solution(2782913887949998807)
XLA Ops:
  0.6 0.0 copy-start
  0.6 1.5 %shard_map.123 = (bf16[4,64,256]{2,1,0:T(8,128)(2,1)S(1)}, bf16[4,64,256]{2,1,0:T(8,128)(2,1)S(1)}, bf16[4,192,128]{2,1,0:T(8,128)(2,1)S(1)}) custom-call(s32[1]{0:T(128)} %bitcast.2.part_ref, s32[8,4,16]{2,1,0:T(4,128)} %bitcast.26, bf16[192,512]{1,0:T(8,128)(2,1)} %bitcast.22), custom_call_target="tpu_custom_call" | custom-call | flops 100663296 | bytes 1048576 | tf_op jit(solution)/shard_map/pallas_call | solution.py:32
  2.2 0.5 %collective-permute-start = (bf16[4,64,256]{2,1,0:T(8,128)(2,1)S(1)}, bf16[4,64,256]{2,1,0:T(8,128)(2,1)S(1)}, u32[]{:S(2)}, u32[]{:S(2)}) collective-permute-start(bf16[4,64,256]{2,1,0:T(8,128)(2,1)S(1)} %get-tuple-element.32), channel_id=1, source_target_pairs={{0,1},{1,0},{2,3},{3,2},{4,5},{5,4},{6,7},{7,6},{8,9},{9,8},{10,11... | collective-permute-start | bytes 393224 | tf_op jit(solution)/shard_map/ppermute | solution.py:362
  2.7 1.7 %shard_map.122 = (f32[4,208,128]{2,1,0:T(8,128)S(1)}, bf16[4,8,16,128]{3,2,1,0:T(8,128)(2,1)S(1)}, bf16[128,512]{1,0:T(8,128)(2,1)S(1)}) custom-call(s32[1]{0:T(128)} %bitcast.me_ref, s32[1]{0:T(128)} %bitcast.2.part_ref, s32[2,12]{1,0:T(2,128)} %bitcast.30, s32[4,8]{1,0:T(4,128)} %bitcast.29, bf16[192,512]{1,0:T(8,128)(2,1)} %bitcast.23, ...), custom_call_target="tpu_custom_call" | custom-call | flops 100663296 | bytes 1048576 | tf_op jit(solution)/shard_map/pallas_call | solution.py:32
  4.3 0.0 collective-permute-done.got_ref
  4.4 0.7 %shard_map.124 = (bf16[2,64,256]{2,1,0:T(8,128)(2,1)S(1)}, bf16[2,64,256]{2,1,0:T(8,128)(2,1)S(1)}, bf16[2,64,256]{2,1,0:T(8,128)(2,1)S(1)}, bf16[2,64,256]{2,1,0:T(8,128)(2,1)S(1)}, bf16[4,192,128]{2,1,0:T(8,128)(2,1)}) custom-call(bf16[128,512]{1,0:T(8,128)(2,1)S(1)} %get-tuple-element.30.after.band_ref, ...), custom_call_target="tpu_custom_call" | custom-call | bytes 1048576 | tf_op jit(solution)/shard_map/pallas_call | solution.py:32
  5.1 5.9 %all-to-all-start = ((bf16[4,192,128]{2,1,0:T(8,128)(2,1)}), bf16[4,192,128]{2,1,0:T(8,128)(2,1)S(1)}, u32[]{:S(2)}, u32[]{:S(2)}) async-start(bf16[4,192,128]{2,1,0:T(8,128)(2,1)} %get-tuple-element.34), calls=%async_computation | async-start | bytes 393216 | tf_op jit(solution)/shard_map/all_to_all | solution.py:432
  11.0 0.0 copy-start.3
  11.0 2.4 %collective-permute-start.1 = (bf16[2,64,256]{2,1,0:T(8,128)(2,1)S(1)}, bf16[2,64,256]{2,1,0:T(8,128)(2,1)S(1)}, u32[]{:S(2)}, u32[]{:S(2)}) collective-permute-start(bf16[2,64,256]{2,1,0:T(8,128)(2,1)S(1)} %get-tuple-element.38), channel_id=1, source_target_pairs={{0,6},{1,7},{2,4},{3,5},{4,2},{5,3},{6,0},{7,1},{8,14},{9,15},{10,... | collective-permute-start | bytes 196616 | tf_op jit(solution)/shard_map/ppermute | solution.py:366
  13.4 0.5 %collective-permute-start.2 = (bf16[2,64,256]{2,1,0:T(8,128)(2,1)S(1)}, bf16[2,64,256]{2,1,0:T(8,128)(2,1)S(1)}, u32[]{:S(2)}, u32[]{:S(2)}) collective-permute-start(bf16[2,64,256]{2,1,0:T(8,128)(2,1)S(1)} %get-tuple-element.39), channel_id=1, source_target_pairs={{0,4},{1,5},{2,6},{3,7},{4,0},{5,1},{6,2},{7,3},{8,12},{9,13},{10,... | collective-permute-start | bytes 196616 | tf_op jit(solution)/shard_map/ppermute | solution.py:366
  13.9 0.5 %collective-permute-start.3 = (bf16[2,64,256]{2,1,0:T(8,128)(2,1)S(1)}, bf16[2,64,256]{2,1,0:T(8,128)(2,1)S(1)}, u32[]{:S(2)}, u32[]{:S(2)}) collective-permute-start(bf16[2,64,256]{2,1,0:T(8,128)(2,1)S(1)} %get-tuple-element.40), channel_id=1, source_target_pairs={{0,2},{1,3},{2,0},{3,1},{4,6},{5,7},{6,4},{7,5},{8,10},{9,11},{10,... | collective-permute-start | bytes 196616 | tf_op jit(solution)/shard_map/ppermute | solution.py:366
  14.5 1.7 %collective-permute-done.1.rest_1_ = bf16[2,64,256]{2,1,0:T(8,128)(2,1)S(1)} collective-permute-done((bf16[2,64,256]{2,1,0:T(8,128)(2,1)S(1)}, bf16[2,64,256]{2,1,0:T(8,128)(2,1)S(1)}, u32[]{:S(2)}, u32[]{:S(2)}) %collective-permute-start.1) | collective-permute-done | bytes 65568 | tf_op jit(solution)/shard_map/ppermute | solution.py:366
  16.1 1.5 %collective-permute-done.2.rest_2_ = bf16[2,64,256]{2,1,0:T(8,128)(2,1)S(1)} collective-permute-done((bf16[2,64,256]{2,1,0:T(8,128)(2,1)S(1)}, bf16[2,64,256]{2,1,0:T(8,128)(2,1)S(1)}, u32[]{:S(2)}, u32[]{:S(2)}) %collective-permute-start.2) | collective-permute-done | bytes 65568 | tf_op jit(solution)/shard_map/ppermute | solution.py:366
  17.7 0.5 %collective-permute-done.3.rest_3_ = bf16[2,64,256]{2,1,0:T(8,128)(2,1)S(1)} collective-permute-done((bf16[2,64,256]{2,1,0:T(8,128)(2,1)S(1)}, bf16[2,64,256]{2,1,0:T(8,128)(2,1)S(1)}, u32[]{:S(2)}, u32[]{:S(2)}) %collective-permute-start.3) | collective-permute-done | bytes 65568 | tf_op jit(solution)/shard_map/ppermute | solution.py:366
  18.2 0.3 shard_map.126
  18.4 3.9 %collective-permute-start.4 = (bf16[192,128]{1,0:T(8,128)(2,1)S(1)}, bf16[192,128]{1,0:T(8,128)(2,1)S(1)}, u32[]{:S(2)}, u32[]{:S(2)}) collective-permute-start(bf16[192,128]{1,0:T(8,128)(2,1)S(1)} %get-tuple-element.42), channel_id=1, source_target_pairs={{0,24},{8,16},{16,8},{24,0},{1,25},{9,17},{17,9},{25,1},{2,26},{10... | collective-permute-start | bytes 147464 | tf_op jit(solution)/shard_map/ppermute | solution.py:355
  22.3 0.0 collective-permute-start.5
  22.3 0.6 %collective-permute-start.6 = (bf16[192,128]{1,0:T(8,128)(2,1)S(1)}, bf16[192,128]{1,0:T(8,128)(2,1)S(1)}, u32[]{:S(2)}, u32[]{:S(2)}) collective-permute-start(bf16[192,128]{1,0:T(8,128)(2,1)S(1)} %get-tuple-element.44), channel_id=1, source_target_pairs={{0,8},{8,0},{16,24},{24,16},{1,9},{9,1},{17,25},{25,17},{2,10},{10... | collective-permute-start | bytes 147464 | tf_op jit(solution)/shard_map/ppermute | solution.py:355
  23.0 0.0 all-to-all-done.blocks_ref
  23.0 0.0 copy-done
  23.0 0.5 %shard_map.125.own_ref = f32[128,1024]{1,0:T(8,128)S(1)} custom-call(bf16[768,1024]{1,0:T(8,128)(2,1)S(1)} %copy-done, bf16[4,192,128]{2,1,0:T(8,128)(2,1)S(1)} %all-to-all-done.blocks_ref), custom_call_target="tpu_custom_call" | custom-call | flops 201326592 | bytes 2097152 | tf_op jit(solution)/shard_map/pallas_call | solution.py:32
  23.4 1.0 %collective-permute-done.4.rest_1_ = bf16[192,128]{1,0:T(8,128)(2,1)S(1)} collective-permute-done((bf16[192,128]{1,0:T(8,128)(2,1)S(1)}, bf16[192,128]{1,0:T(8,128)(2,1)S(1)}, u32[]{:S(2)}, u32[]{:S(2)}) %collective-permute-start.4) | collective-permute-done | bytes 49184 | tf_op jit(solution)/shard_map/ppermute | solution.py:355
  24.4 2.9 %collective-permute-done.5.rest_2_ = bf16[192,128]{1,0:T(8,128)(2,1)S(1)} collective-permute-done((bf16[192,128]{1,0:T(8,128)(2,1)S(1)}, bf16[192,128]{1,0:T(8,128)(2,1)S(1)}, u32[]{:S(2)}, u32[]{:S(2)}) %collective-permute-start.5) | collective-permute-done | bytes 49184 | tf_op jit(solution)/shard_map/ppermute | solution.py:355
  27.3 0.0 collective-permute-done.6.rest_3_
  27.3 0.0 copy-done.3
  27.3 0.0 copy-done.1
  27.3 0.0 copy-start.2
  27.3 0.7 %shard_map.127 = (bf16[128,1024]{1,0:T(8,128)(2,1)S(1)}, bf16[153,128]{1,0:T(8,128)(2,1)S(1)}, bf16[153,128]{1,0:T(8,128)(2,1)S(1)}, bf16[153,128]{1,0:T(8,128)(2,1)S(1)}, bf16[153,128]{1,0:T(8,128)(2,1)S(1)}) custom-call(s32[1]{0:T(128)} %bitcast.me_ref, bf16[768,1024]{1,0:T(8,128)(2,1)S(1)} %copy-done.1, bf16[153,1024]{1,0:T(8,128)(2,1)S(1)} %bitcast.20, ...), custom_call_target="tpu_custom_call" | custom-call | flops 201326592 | bytes 2097152 | tf_op jit(solution)/shard_map/pallas_call | solution.py:32
  28.0 1.5 %collective-permute-start.7 = (bf16[153,128]{1,0:T(8,128)(2,1)S(1)}, bf16[153,128]{1,0:T(8,128)(2,1)S(1)}, u32[]{:S(2)}, u32[]{:S(2)}) collective-permute-start(bf16[153,128]{1,0:T(8,128)(2,1)S(1)} %get-tuple-element.49), channel_id=1, source_target_pairs={{0,24},{8,16},{16,8},{24,0},{1,25},{9,17},{17,9},{25,1},{2,26},{10... | collective-permute-start | bytes 117512 | tf_op jit(solution)/shard_map/ppermute | solution.py:355
  29.6 0.6 %collective-permute-start.8 = (bf16[153,128]{1,0:T(8,128)(2,1)S(1)}, bf16[153,128]{1,0:T(8,128)(2,1)S(1)}, u32[]{:S(2)}, u32[]{:S(2)}) collective-permute-start(bf16[153,128]{1,0:T(8,128)(2,1)S(1)} %get-tuple-element.50), channel_id=1, source_target_pairs={{0,16},{8,24},{16,0},{24,8},{1,17},{9,25},{17,1},{25,9},{2,18},{10... | collective-permute-start | bytes 117512 | tf_op jit(solution)/shard_map/ppermute | solution.py:355
  30.2 2.3 %collective-permute-start.9 = (bf16[153,128]{1,0:T(8,128)(2,1)S(1)}, bf16[153,128]{1,0:T(8,128)(2,1)S(1)}, u32[]{:S(2)}, u32[]{:S(2)}) collective-permute-start(bf16[153,128]{1,0:T(8,128)(2,1)S(1)} %get-tuple-element.51), channel_id=1, source_target_pairs={{0,8},{8,0},{16,24},{24,16},{1,9},{9,1},{17,25},{25,17},{2,10},{10... | collective-permute-start | bytes 117512 | tf_op jit(solution)/shard_map/ppermute | solution.py:355
  32.5 0.9 %shard_map.130.hits_ref.after = bf16[128,512]{1,0:T(8,128)(2,1)S(1)} custom-call(bf16[153,128]{1,0:T(8,128)(2,1)S(1)} %get-tuple-element.48.rest_0_.after, s32[1]{0:T(128)} %bitcast.me_ref, s32[1]{0:T(128)} %bitcast.2.part_ref, s32[8,4,16]{2,1,0:T(4,128)} %bitcast.27), custom_call_target="tpu_custom_call" | custom-call | bytes 524288 | tf_op jit(solution)/shard_map/pallas_call | solution.py:32
  33.4 0.5 %collective-permute-done.7.rest_1_ = bf16[153,128]{1,0:T(8,128)(2,1)S(1)} collective-permute-done((bf16[153,128]{1,0:T(8,128)(2,1)S(1)}, bf16[153,128]{1,0:T(8,128)(2,1)S(1)}, u32[]{:S(2)}, u32[]{:S(2)}) %collective-permute-start.7) | collective-permute-done | bytes 39200 | tf_op jit(solution)/shard_map/ppermute | solution.py:355
  33.9 0.6 %collective-permute-done.8.rest_2_ = bf16[153,128]{1,0:T(8,128)(2,1)S(1)} collective-permute-done((bf16[153,128]{1,0:T(8,128)(2,1)S(1)}, bf16[153,128]{1,0:T(8,128)(2,1)S(1)}, u32[]{:S(2)}, u32[]{:S(2)}) %collective-permute-start.8) | collective-permute-done | bytes 39200 | tf_op jit(solution)/shard_map/ppermute | solution.py:355
  34.5 0.4 collective-permute-done.9.rest_3_
  34.9 0.3 shard_map.131
  35.2 0.1 collective-permute-start.10
  35.2 1.2 %collective-permute-done.10.got_ref = bf16[4,16,256]{2,1,0:T(8,128)(2,1)S(1)} collective-permute-done((bf16[4,16,256]{2,1,0:T(8,128)(2,1)S(1)}, bf16[4,16,256]{2,1,0:T(8,128)(2,1)S(1)}, u32[]{:S(2)}, u32[]{:S(2)}) %collective-permute-start.10) | collective-permute-done | bytes 32800 | tf_op jit(solution)/shard_map/ppermute | solution.py:362
  36.4 1.5 %collective-permute-start.11 = (bf16[2,16,256]{2,1,0:T(8,128)(2,1)S(1)}, bf16[2,16,256]{2,1,0:T(8,128)(2,1)S(1)}, u32[]{:S(2)}, u32[]{:S(2)}) collective-permute-start(bf16[2,16,256]{2,1,0:T(8,128)(2,1)S(1)} %get-tuple-element.55), channel_id=1, source_target_pairs={{0,6},{1,7},{2,4},{3,5},{4,2},{5,3},{6,0},{7,1},{8,14},{9,15},{10,... | collective-permute-start | bytes 49160 | tf_op jit(solution)/shard_map/ppermute | solution.py:366
  37.9 1.1 %collective-permute-start.12 = (bf16[2,16,256]{2,1,0:T(8,128)(2,1)S(1)}, bf16[2,16,256]{2,1,0:T(8,128)(2,1)S(1)}, u32[]{:S(2)}, u32[]{:S(2)}) collective-permute-start(bf16[2,16,256]{2,1,0:T(8,128)(2,1)S(1)} %get-tuple-element.56), channel_id=1, source_target_pairs={{0,4},{1,5},{2,6},{3,7},{4,0},{5,1},{6,2},{7,3},{8,12},{9,13},{10,... | collective-permute-start | bytes 49160 | tf_op jit(solution)/shard_map/ppermute | solution.py:366
  39.0 0.9 %collective-permute-start.13 = (bf16[2,16,256]{2,1,0:T(8,128)(2,1)S(1)}, bf16[2,16,256]{2,1,0:T(8,128)(2,1)S(1)}, u32[]{:S(2)}, u32[]{:S(2)}) collective-permute-start(bf16[2,16,256]{2,1,0:T(8,128)(2,1)S(1)} %get-tuple-element.57), channel_id=1, source_target_pairs={{0,2},{1,3},{2,0},{3,1},{4,6},{5,7},{6,4},{7,5},{8,10},{9,11},{10,... | collective-permute-start | bytes 49160 | tf_op jit(solution)/shard_map/ppermute | solution.py:366
  39.9 0.0 copy-done.2
  39.9 0.7 %shard_map.128 = (f32[153,128]{1,0:T(8,128)S(1)}, bf16[128,1024]{1,0:T(8,128)(2,1)}) custom-call(bf16[128,1024]{1,0:T(8,128)(2,1)S(1)} %get-tuple-element.45.hidden_ref, bf16[153,1024]{1,0:T(8,128)(2,1)S(1)} %bitcast.19), custom_call_target="tpu_custom_call" | custom-call | flops 40108032 | bytes 1048576 | tf_op jit(solution)/shard_map/pallas_call | solution.py:32
  40.6 0.2 shard_map.129.near_ref
  40.9 0.2 collective-permute-done.11.rest_1_
  41.1 0.6 %collective-permute-done.12.rest_2_ = bf16[2,16,256]{2,1,0:T(8,128)(2,1)S(1)} collective-permute-done((bf16[2,16,256]{2,1,0:T(8,128)(2,1)S(1)}, bf16[2,16,256]{2,1,0:T(8,128)(2,1)S(1)}, u32[]{:S(2)}, u32[]{:S(2)}) %collective-permute-start.12) | collective-permute-done | bytes 16416 | tf_op jit(solution)/shard_map/ppermute | solution.py:366
  41.7 1.1 %collective-permute-done.13.rest_3_ = bf16[2,16,256]{2,1,0:T(8,128)(2,1)S(1)} collective-permute-done((bf16[2,16,256]{2,1,0:T(8,128)(2,1)S(1)}, bf16[2,16,256]{2,1,0:T(8,128)(2,1)S(1)}, u32[]{:S(2)}, u32[]{:S(2)}) %collective-permute-start.13) | collective-permute-done | bytes 16416 | tf_op jit(solution)/shard_map/ppermute | solution.py:366
  42.8 0.9 %shard_map.133 = f32[153,1,128]{2,1,0:T(1,128)} custom-call(s32[1]{0:T(128)} %bitcast.me_ref, f32[153,128]{1,0:T(8,128)S(1)} %shard_map.129.near_ref, bf16[4,8,16,128]{3,2,1,0:T(8,128)(2,1)S(1)} %get-tuple-element.36.edges_ref, f32[4,208,128]{2,1,0:T(8,128)S(1)} %get-tuple-element.35.sums_ref, bf16[2,16,256]{2,1,0:T(8,128)(2,1)S(1)} %get-tuple-element.54.rest_0_, ...), custom_call_target="tpu_custom_call" | custom-call | flops 5013504 | bytes 524288 | tf_op jit(solution)/shard_map/pallas_call | solution.py:32
  (2 shorter events, 0.0 us)
Async XLA Ops:
  0.6 22.4 %copy-start = (bf16[768,1024]{1,0:T(8,128)(2,1)S(1)}, bf16[768,1024]{1,0:T(8,128)(2,1)}, u32[]{:S(2)}) copy-start(bf16[768,1024]{1,0:T(8,128)(2,1)} %weight_ref.2) | copy-start | bytes 4718596
  2.2 2.2 %collective-permute-start = (bf16[4,64,256]{2,1,0:T(8,128)(2,1)S(1)}, bf16[4,64,256]{2,1,0:T(8,128)(2,1)S(1)}, u32[]{:S(2)}, u32[]{:S(2)}) collective-permute-start(bf16[4,64,256]{2,1,0:T(8,128)(2,1)S(1)} %get-tuple-element.32), channel_id=1, source_target_pairs={{0,1},{1,0},{2,3},{3,2},{4,5},{5,4},{6,7},{7,6},{8,9},{9,8},{10,11... | collective-permute-start | bytes 393224 | tf_op jit(solution)/shard_map/ppermute | solution.py:362
  5.1 17.9 %all-to-all-start = ((bf16[4,192,128]{2,1,0:T(8,128)(2,1)}), bf16[4,192,128]{2,1,0:T(8,128)(2,1)S(1)}, u32[]{:S(2)}, u32[]{:S(2)}) async-start(bf16[4,192,128]{2,1,0:T(8,128)(2,1)} %get-tuple-element.34), calls=%async_computation | async-start | bytes 393216 | tf_op jit(solution)/shard_map/all_to_all | solution.py:432
  11.0 16.4 %copy-start.3 = (bf16[1024,153]{0,1:T(8,128)(2,1)S(1)}, bf16[1024,153]{0,1:T(8,128)(2,1)}, u32[]{:S(2)}) copy-start(bf16[1024,153]{0,1:T(8,128)(2,1)} %param.21) | copy-start | bytes 940036
  11.0 5.2 %collective-permute-start.1 = (bf16[2,64,256]{2,1,0:T(8,128)(2,1)S(1)}, bf16[2,64,256]{2,1,0:T(8,128)(2,1)S(1)}, u32[]{:S(2)}, u32[]{:S(2)}) collective-permute-start(bf16[2,64,256]{2,1,0:T(8,128)(2,1)S(1)} %get-tuple-element.38), channel_id=1, source_target_pairs={{0,6},{1,7},{2,4},{3,5},{4,2},{5,3},{6,0},{7,1},{8,14},{9,15},{10,... | collective-permute-start | bytes 196616 | tf_op jit(solution)/shard_map/ppermute | solution.py:366
  13.4 4.3 %collective-permute-start.2 = (bf16[2,64,256]{2,1,0:T(8,128)(2,1)S(1)}, bf16[2,64,256]{2,1,0:T(8,128)(2,1)S(1)}, u32[]{:S(2)}, u32[]{:S(2)}) collective-permute-start(bf16[2,64,256]{2,1,0:T(8,128)(2,1)S(1)} %get-tuple-element.39), channel_id=1, source_target_pairs={{0,4},{1,5},{2,6},{3,7},{4,0},{5,1},{6,2},{7,3},{8,12},{9,13},{10,... | collective-permute-start | bytes 196616 | tf_op jit(solution)/shard_map/ppermute | solution.py:366
  13.9 4.3 %collective-permute-start.3 = (bf16[2,64,256]{2,1,0:T(8,128)(2,1)S(1)}, bf16[2,64,256]{2,1,0:T(8,128)(2,1)S(1)}, u32[]{:S(2)}, u32[]{:S(2)}) collective-permute-start(bf16[2,64,256]{2,1,0:T(8,128)(2,1)S(1)} %get-tuple-element.40), channel_id=1, source_target_pairs={{0,2},{1,3},{2,0},{3,1},{4,6},{5,7},{6,4},{7,5},{8,10},{9,11},{10,... | collective-permute-start | bytes 196616 | tf_op jit(solution)/shard_map/ppermute | solution.py:366
  18.4 6.0 %collective-permute-start.4 = (bf16[192,128]{1,0:T(8,128)(2,1)S(1)}, bf16[192,128]{1,0:T(8,128)(2,1)S(1)}, u32[]{:S(2)}, u32[]{:S(2)}) collective-permute-start(bf16[192,128]{1,0:T(8,128)(2,1)S(1)} %get-tuple-element.42), channel_id=1, source_target_pairs={{0,24},{8,16},{16,8},{24,0},{1,25},{9,17},{17,9},{25,1},{2,26},{10... | collective-permute-start | bytes 147464 | tf_op jit(solution)/shard_map/ppermute | solution.py:355
  22.3 5.0 %collective-permute-start.5 = (bf16[192,128]{1,0:T(8,128)(2,1)S(1)}, bf16[192,128]{1,0:T(8,128)(2,1)S(1)}, u32[]{:S(2)}, u32[]{:S(2)}) collective-permute-start(bf16[192,128]{1,0:T(8,128)(2,1)S(1)} %get-tuple-element.43), channel_id=1, source_target_pairs={{0,16},{8,24},{16,0},{24,8},{1,17},{9,25},{17,1},{25,9},{2,18},{10... | collective-permute-start | bytes 147464 | tf_op jit(solution)/shard_map/ppermute | solution.py:355
  22.3 5.0 %collective-permute-start.6 = (bf16[192,128]{1,0:T(8,128)(2,1)S(1)}, bf16[192,128]{1,0:T(8,128)(2,1)S(1)}, u32[]{:S(2)}, u32[]{:S(2)}) collective-permute-start(bf16[192,128]{1,0:T(8,128)(2,1)S(1)} %get-tuple-element.44), channel_id=1, source_target_pairs={{0,8},{8,0},{16,24},{24,16},{1,9},{9,1},{17,25},{25,17},{2,10},{10... | collective-permute-start | bytes 147464 | tf_op jit(solution)/shard_map/ppermute | solution.py:355
  23.0 4.3 %copy-start.1 = (bf16[768,1024]{1,0:T(8,128)(2,1)S(1)}, bf16[768,1024]{1,0:T(8,128)(2,1)}, u32[]{:S(2)}) copy-start(bf16[768,1024]{1,0:T(8,128)(2,1)} %weight_ref.3) | copy-start | bytes 4718596
  27.3 12.6 %copy-start.2 = (bf16[1024,153]{0,1:T(8,128)(2,1)S(1)}, bf16[1024,153]{0,1:T(8,128)(2,1)}, u32[]{:S(2)}) copy-start(bf16[1024,153]{0,1:T(8,128)(2,1)} %param.20) | copy-start | bytes 940036
  28.0 5.9 %collective-permute-start.7 = (bf16[153,128]{1,0:T(8,128)(2,1)S(1)}, bf16[153,128]{1,0:T(8,128)(2,1)S(1)}, u32[]{:S(2)}, u32[]{:S(2)}) collective-permute-start(bf16[153,128]{1,0:T(8,128)(2,1)S(1)} %get-tuple-element.49), channel_id=1, source_target_pairs={{0,24},{8,16},{16,8},{24,0},{1,25},{9,17},{17,9},{25,1},{2,26},{10... | collective-permute-start | bytes 117512 | tf_op jit(solution)/shard_map/ppermute | solution.py:355
  29.6 4.9 %collective-permute-start.8 = (bf16[153,128]{1,0:T(8,128)(2,1)S(1)}, bf16[153,128]{1,0:T(8,128)(2,1)S(1)}, u32[]{:S(2)}, u32[]{:S(2)}) collective-permute-start(bf16[153,128]{1,0:T(8,128)(2,1)S(1)} %get-tuple-element.50), channel_id=1, source_target_pairs={{0,16},{8,24},{16,0},{24,8},{1,17},{9,25},{17,1},{25,9},{2,18},{10... | collective-permute-start | bytes 117512 | tf_op jit(solution)/shard_map/ppermute | solution.py:355
  30.2 4.7 %collective-permute-start.9 = (bf16[153,128]{1,0:T(8,128)(2,1)S(1)}, bf16[153,128]{1,0:T(8,128)(2,1)S(1)}, u32[]{:S(2)}, u32[]{:S(2)}) collective-permute-start(bf16[153,128]{1,0:T(8,128)(2,1)S(1)} %get-tuple-element.51), channel_id=1, source_target_pairs={{0,8},{8,0},{16,24},{24,16},{1,9},{9,1},{17,25},{25,17},{2,10},{10... | collective-permute-start | bytes 117512 | tf_op jit(solution)/shard_map/ppermute | solution.py:355
  35.2 1.3 %collective-permute-start.10 = (bf16[4,16,256]{2,1,0:T(8,128)(2,1)S(1)}, bf16[4,16,256]{2,1,0:T(8,128)(2,1)S(1)}, u32[]{:S(2)}, u32[]{:S(2)}) collective-permute-start(bf16[4,16,256]{2,1,0:T(8,128)(2,1)S(1)} %get-tuple-element.53), channel_id=1, source_target_pairs={{0,1},{1,0},{2,3},{3,2},{4,5},{5,4},{6,7},{7,6},{8,9},{9,8},{10,11... | collective-permute-start | bytes 98312 | tf_op jit(solution)/shard_map/ppermute | solution.py:362
  36.4 4.6 %collective-permute-start.11 = (bf16[2,16,256]{2,1,0:T(8,128)(2,1)S(1)}, bf16[2,16,256]{2,1,0:T(8,128)(2,1)S(1)}, u32[]{:S(2)}, u32[]{:S(2)}) collective-permute-start(bf16[2,16,256]{2,1,0:T(8,128)(2,1)S(1)} %get-tuple-element.55), channel_id=1, source_target_pairs={{0,6},{1,7},{2,4},{3,5},{4,2},{5,3},{6,0},{7,1},{8,14},{9,15},{10,... | collective-permute-start | bytes 49160 | tf_op jit(solution)/shard_map/ppermute | solution.py:366
  37.9 3.7 %collective-permute-start.12 = (bf16[2,16,256]{2,1,0:T(8,128)(2,1)S(1)}, bf16[2,16,256]{2,1,0:T(8,128)(2,1)S(1)}, u32[]{:S(2)}, u32[]{:S(2)}) collective-permute-start(bf16[2,16,256]{2,1,0:T(8,128)(2,1)S(1)} %get-tuple-element.56), channel_id=1, source_target_pairs={{0,4},{1,5},{2,6},{3,7},{4,0},{5,1},{6,2},{7,3},{8,12},{9,13},{10,... | collective-permute-start | bytes 49160 | tf_op jit(solution)/shard_map/ppermute | solution.py:366
  39.0 3.7 %collective-permute-start.13 = (bf16[2,16,256]{2,1,0:T(8,128)(2,1)S(1)}, bf16[2,16,256]{2,1,0:T(8,128)(2,1)S(1)}, u32[]{:S(2)}, u32[]{:S(2)}) collective-permute-start(bf16[2,16,256]{2,1,0:T(8,128)(2,1)S(1)} %get-tuple-element.57), channel_id=1, source_target_pairs={{0,2},{1,3},{2,0},{3,1},{4,6},{5,7},{6,4},{7,5},{8,10},{9,11},{10,... | collective-permute-start | bytes 49160 | tf_op jit(solution)/shard_map/ppermute | solution.py:366

commit v12 on v10

--- a/solution.py
+++ b/solution.py
@@ -43,7 +43,9 @@
     return lax.dot_general(left, right, dims, preferred_element_type=f32)
 
 
-def step_of(groups, k):
+def step_of(groups, k, near=False):
+    if near and k:
+        return 1 if k == 1 else groups - k + 1
     return (groups - k) % groups
 
 
@@ -51,28 +53,14 @@
     return -(-count // 128) * 128
 
 
-def ahead(me, groups, k):
-    step = step_of(groups, k)
+def ahead(me, groups, k, near=False):
+    step = step_of(groups, k, near)
     return me ^ step if groups & (groups - 1) == 0 else (me + step) % groups
 
 
-def behind(me, groups, k):
-    step = step_of(groups, k)
+def behind(me, groups, k, near=False):
+    step = step_of(groups, k, near)
     return me ^ step if groups & (groups - 1) == 0 else (me + groups - step) % groups
-
-
-def rounds_of(groups):
-    if groups == 4:
-        pairs = [[(0, 2)], [(0, 3), (1, 2)], [(1, 3)], [(0, 1), (2, 3)]]
-        return [dict(p + [(b, a) for a, b in p]) for p in pairs]
-    return [{i: ahead(i, groups, k) for i in range(groups)} for k in range(1, groups)]
-
-
-def look_up(table, me):
-    found = -1
-    for key, value in table.items():
-        found = jnp.where(me == key, value, found)
-    return found
 
 
 def step_to(a, b, count):
@@ -131,9 +119,9 @@
         table.wait()
         for other, out in enumerate((mine_ref, mate_ref)):
             lax.fori_loop(0, chips // chunk, lambda i, _: step(i, out, other, False), None)
-    for table, block in zip(rounds_of(groups), blocks):
-        group = jnp.maximum(look_up(table, me_ref[0]), 0)
-        block[...] = features_ref[:width, pl.ds(pl.multiple_of(group * rows, rows), rows)]
+    for k in range(1, groups):
+        group = ahead(me_ref[0], groups, k, True)
+        blocks[k - 1][...] = features_ref[:width, pl.ds(pl.multiple_of(group * rows, rows), rows)]
 
 
 def local_kernel(
@@ -242,34 +230,34 @@
         outs[k][...] = (total / sums_ref[group, width : width + 1, :]).astype(bf16)
 
 
-def self_kernel(groups, me_ref, features_hbm, weight_ref, *rest):
+def rows_from(me, groups, k, width, near=False):
+    return pl.ds(pl.multiple_of(behind(me, groups, k, near) * width, width), width)
+
+
+def self_kernel(me_ref, features_hbm, weight_ref, *rest):
     blocks, (out_ref, own_ref, sem) = rest[:-3], rest[-3:]
-    width, rows = own_ref.shape
+    groups, (width, rows) = len(blocks) + 1, own_ref.shape
     me = me_ref[0]
     own = pltpu.make_async_copy(
         features_hbm.at[:, pl.ds(pl.multiple_of(me * rows, rows), rows)], own_ref, sem
     )
     own.start()
-    out_ref[...] = jnp.zeros_like(out_ref)
-
-    def add(block, source):
-        span = pl.ds(pl.multiple_of(source * width, width), width)
-        out_ref[...] += dot(block[...], weight_ref[span, :], FIRST)
-
-    for table, block in zip(rounds_of(groups), blocks):
-        source = look_up({b: a for a, b in table.items()}, me)
-        pl.when(source >= 0)(functools.partial(add, block, source))
+    total = jnp.zeros(out_ref.shape, f32)
+    for k, block in enumerate(blocks, 1):
+        span = rows_from(me, groups, k, width, True)
+        total = total + dot(block[...], weight_ref[span, :], FIRST)
     own.wait()
-    add(own_ref, me)
-
-
-def hidden_kernel(groups, me_ref, weight_ref, out_weight_ref, own_ref, *rest):
+    span = pl.ds(pl.multiple_of(me * width, width), width)
+    out_ref[...] = total + dot(own_ref[...], weight_ref[span, :], FIRST)
+
+
+def hidden_kernel(me_ref, weight_ref, out_weight_ref, own_ref, *rest):
+    groups = (len(rest) - 1) // 2
     parts, (hidden_ref, *copies) = rest[:groups], rest[groups:]
     width = parts[0].shape[0]
     total = own_ref[...]
     for k, block in enumerate(parts):
-        source = behind(me_ref[0], groups, k)
-        span = pl.ds(pl.multiple_of(source * width, width), width)
+        span = rows_from(me_ref[0], groups, k, width)
         total = total + dot(block[...], weight_ref[span, :], FIRST)
     hidden = jnp.maximum(total, 0.0).astype(bf16)
     hidden_ref[...] = hidden
@@ -354,17 +342,15 @@
     width, nodes = feature_rows.shape
     rows, slots = nodes // groups, sources.shape[3]
     hid, classes = self_one.shape[1], self_out.shape[1]
-    chips, rounds = parts // 2, rounds_of(groups)
+    chips = parts // 2
     chunk = max(1, min(parts, 512 // (groups * slots)))
 
     def shape(*dims, dtype=bf16):
         return jax.ShapeDtypeStruct(dims, dtype)
 
-    def shift(blocks):
+    def shift(blocks, near=False):
         return [
-            lax.ppermute(
-                block, "feat", [(i, ahead(i, groups, k)) for i in range(groups)]
-            )
+            lax.ppermute(block, "feat", [(i, ahead(i, groups, k, near)) for i in range(groups)])
             for k, block in enumerate(blocks, 1)
         ]
 
@@ -385,7 +371,7 @@
     lanes = whole_lanes(width)
     mine, mate, *feature_blocks = call(
         functools.partial(gather_kernel, picked),
-        (shape(chips, groups * slots, lanes),) * 2 + (shape(width, rows),) * len(rounds),
+        (shape(chips, groups * slots, lanes),) * 2 + (shape(width, rows),) * (groups - 1),
         [SM, SM, HB, HB],
         [
             pltpu.VMEM((parts, groups, slots), jnp.int32),
@@ -431,17 +417,14 @@
     )
     paired = call(
         pair_kernel,
-        (shape(2, groups * slots, lanes),) * chips + (shape(width, rows),) * len(rounds),
-        [VM] * (3 + len(rounds)),
+        (shape(2, groups * slots, lanes),) * chips + (shape(width, rows),) * (groups - 1),
+        [VM] * (2 + groups),
         (),
         0,
         1 << 20,
     )(band, mine, mate, *feature_blocks)
     arrived = to_chips(paired[:chips])
-    feature_blocks = [
-        lax.ppermute(block, "feat", list(table.items()))
-        for table, block in zip(rounds, paired[chips:])
-    ]
+    feature_blocks = shift(paired[chips:], near=True)
     means = call(
         mean_kernel,
         (shape(width, rows),) * groups,
@@ -452,15 +435,15 @@
     )(me, sums, edges, *arrived)
     means = [means[0]] + shift(means[1:])
     own = call(
-        functools.partial(self_kernel, groups),
+        self_kernel,
         shape(rows, hid, dtype=f32),
-        [SM, HB] + [VM] * (1 + len(rounds)),
+        [SM, HB] + [VM] * groups,
         [pltpu.VMEM((width, rows), bf16), pltpu.SemaphoreType.DMA],
         2 * rows * hid * groups * width,
         2 << 20,
     )(me, feature_rows, self_one, *feature_blocks)
     hidden, *projected = call(
-        functools.partial(hidden_kernel, groups),
+        hidden_kernel,
         (shape(rows, hid),) + (shape(classes, rows),) * groups,
         [SM] + [VM] * (3 + groups),
         (),

time: 44.6 us -> 39.9 us (0.89)
  starting transfers between devices: 28.4 us -> 22 us
  waiting for transfers between devices: 6.81 us -> 8.52 us
    ppermute x10 -> x9, starting transfers between devices: 20.2 us -> 13.8 us  [shift(): lax.ppermute(block, 'feat', [(i, ahead(i, groups, k, near)) for i in rang...]
    ppermute x10 -> x9, waiting for transfers between devices: 3.36 us -> 5.08 us  [shift(): lax.ppermute(block, 'feat', [(i, ahead(i, groups, k, near)) for i in rang...]
  transfers between devices with their start and end apart: 18 -> 17, of which waited for: 9 -> 8; matrix products, arithmetic and copies ran while one was open for 0% -> 0% of each run, Pallas kernels for 11% -> 12%
where the time goes in v12:
time: 39.9 us; the launch traced here: 39.7 us
  starting transfers between devices  22 us (55%)
  waiting for transfers between devices  8.52 us (21%)
  Pallas kernels  8.31 us (21%)
  between operations  0.78 us (2%)
    ppermute x9, starting transfers between devices, shift(): lax.ppermute(block, 'feat', [(i, ahead(i, groups, k, near)) for i in rang...  13.8 us
    pallas_call x12, Pallas kernels, placed(): run(*(pltpu.with_memory_space_constraint(value, pltpu.HBM) if spec is HB...  8.31 us
    ppermute x6, starting transfers between devices, to_chips(): lax.ppermute(blocks[j], 'dom', [(d, next_to(d // 2, j, chips) * 2 + d % 2...  7.66 us
    ppermute x9, waiting for transfers between devices, shift(): lax.ppermute(block, 'feat', [(i, ahead(i, groups, k, near)) for i in rang...  5.08 us
    ppermute x6, waiting for transfers between devices, to_chips(): lax.ppermute(blocks[j], 'dom', [(d, next_to(d // 2, j, chips) * 2 + d % 2...  2.25 us
    ppermute x2, waiting for transfers between devices, to_mate(): return lax.ppermute(value, 'dom', [(d, d ^ 1) for d in range(parts)])  1.2 us
  transfers between devices with their start and end apart: 17, of which 8 were waited for; matrix products, arithmetic and copies ran while one was open for 0% of the time, Pallas kernels for 12%

profile of v12, /device:TPU:0, one launch (start us, length us, event | category | flops | bytes accessed | tf_op | source)
XLA Modules:
  0.0 39.7 jit_solution(2896037841652869529)
XLA Ops:
  0.6 0.0 copy-start.1
  0.6 1.5 %shard_map.123 = (bf16[4,64,256]{2,1,0:T(8,128)(2,1)S(1)}, bf16[4,64,256]{2,1,0:T(8,128)(2,1)S(1)}, bf16[192,128]{1,0:T(8,128)(2,1)S(1)}, bf16[192,128]{1,0:T(8,128)(2,1)S(1)}, bf16[192,128]{1,0:T(8,128)(2,1)S(1)}) custom-call(s32[1]{0:T(128)} %bitcast.me_ref, s32[1]{0:T(128)} %bitcast.4.part_ref, s32[8,4,16]{2,1,0:T(4,128)} %bitcast.27, ...), custom_call_target="tpu_custom_call" | custom-call | flops 100663296 | bytes 1048576 | tf_op jit(solution)/shard_map/pallas_call | solution.py:32
  2.2 0.5 %collective-permute-start = (bf16[4,64,256]{2,1,0:T(8,128)(2,1)S(1)}, bf16[4,64,256]{2,1,0:T(8,128)(2,1)S(1)}, u32[]{:S(2)}, u32[]{:S(2)}) collective-permute-start(bf16[4,64,256]{2,1,0:T(8,128)(2,1)S(1)} %get-tuple-element.36), channel_id=1, source_target_pairs={{0,1},{1,0},{2,3},{3,2},{4,5},{5,4},{6,7},{7,6},{8,9},{9,8},{10,11... | collective-permute-start | bytes 393224 | tf_op jit(solution)/shard_map/ppermute | solution.py:358
  2.7 1.6 %shard_map.122 = (f32[4,208,128]{2,1,0:T(8,128)S(1)}, bf16[4,8,16,128]{3,2,1,0:T(8,128)(2,1)S(1)}, bf16[128,512]{1,0:T(8,128)(2,1)S(1)}) custom-call(s32[1]{0:T(128)} %bitcast.me_ref, s32[1]{0:T(128)} %bitcast.4.part_ref, s32[2,12]{1,0:T(2,128)} %bitcast.31, s32[4,8]{1,0:T(4,128)} %bitcast.30, bf16[192,512]{1,0:T(8,128)(2,1)} %bitcast.22, ...), custom_call_target="tpu_custom_call" | custom-call | flops 100663296 | bytes 1048576 | tf_op jit(solution)/shard_map/pallas_call | solution.py:32
  4.3 0.0 collective-permute-done.got_ref
  4.4 3.5 %collective-permute-start.4 = (bf16[2,64,256]{2,1,0:T(8,128)(2,1)S(1)}, bf16[2,64,256]{2,1,0:T(8,128)(2,1)S(1)}, u32[]{:S(2)}, u32[]{:S(2)}) collective-permute-start(bf16[2,64,256]{2,1,0:T(8,128)(2,1)S(1)} %get-tuple-element.46), channel_id=1, source_target_pairs={{0,6},{1,7},{2,4},{3,5},{4,2},{5,3},{6,0},{7,1},{8,14},{9,15},{10,... | collective-permute-start | bytes 196616 | tf_op jit(solution)/shard_map/ppermute | solution.py:362
  7.9 0.5 %collective-permute-start.5 = (bf16[2,64,256]{2,1,0:T(8,128)(2,1)S(1)}, bf16[2,64,256]{2,1,0:T(8,128)(2,1)S(1)}, u32[]{:S(2)}, u32[]{:S(2)}) collective-permute-start(bf16[2,64,256]{2,1,0:T(8,128)(2,1)S(1)} %get-tuple-element.47), channel_id=1, source_target_pairs={{0,4},{1,5},{2,6},{3,7},{4,0},{5,1},{6,2},{7,3},{8,12},{9,13},{10,... | collective-permute-start | bytes 196616 | tf_op jit(solution)/shard_map/ppermute | solution.py:362
  8.4 0.1 collective-permute-start.6
  8.6 2.0 %collective-permute-start.1 = (bf16[192,128]{1,0:T(8,128)(2,1)S(1)}, bf16[192,128]{1,0:T(8,128)(2,1)S(1)}, u32[]{:S(2)}, u32[]{:S(2)}) collective-permute-start(bf16[192,128]{1,0:T(8,128)(2,1)S(1)} %get-tuple-element.40), channel_id=1, source_target_pairs={{0,8},{8,0},{16,24},{24,16},{1,9},{9,1},{17,25},{25,17},{2,10},{10... | collective-permute-start | bytes 147464 | tf_op jit(solution)/shard_map/ppermute | solution.py:353
  10.5 2.5 %collective-permute-start.2 = (bf16[192,128]{1,0:T(8,128)(2,1)S(1)}, bf16[192,128]{1,0:T(8,128)(2,1)S(1)}, u32[]{:S(2)}, u32[]{:S(2)}) collective-permute-start(bf16[192,128]{1,0:T(8,128)(2,1)S(1)} %get-tuple-element.41), channel_id=1, source_target_pairs={{0,24},{8,16},{16,8},{24,0},{1,25},{9,17},{17,9},{25,1},{2,26},{10... | collective-permute-start | bytes 147464 | tf_op jit(solution)/shard_map/ppermute | solution.py:353
  13.0 0.0 collective-permute-done.4.rest_1_
  13.0 0.4 %collective-permute-start.3 = (bf16[192,128]{1,0:T(8,128)(2,1)S(1)}, bf16[192,128]{1,0:T(8,128)(2,1)S(1)}, u32[]{:S(2)}, u32[]{:S(2)}) collective-permute-start(bf16[192,128]{1,0:T(8,128)(2,1)S(1)} %get-tuple-element.42), channel_id=1, source_target_pairs={{0,16},{8,24},{16,0},{24,8},{1,17},{9,25},{17,1},{25,9},{2,18},{10... | collective-permute-start | bytes 147464 | tf_op jit(solution)/shard_map/ppermute | solution.py:353
  13.5 0.0 collective-permute-done.5.rest_2_
  13.5 0.0 collective-permute-done.6.rest_3_
  13.5 0.0 copy-start.3
  13.5 0.3 shard_map.126
  13.7 2.9 %collective-permute-start.7 = (bf16[192,128]{1,0:T(8,128)(2,1)S(1)}, bf16[192,128]{1,0:T(8,128)(2,1)S(1)}, u32[]{:S(2)}, u32[]{:S(2)}) collective-permute-start(bf16[192,128]{1,0:T(8,128)(2,1)S(1)} %get-tuple-element.50), channel_id=1, source_target_pairs={{0,24},{8,16},{16,8},{24,0},{1,25},{9,17},{17,9},{25,1},{2,26},{10... | collective-permute-start | bytes 147464 | tf_op jit(solution)/shard_map/ppermute | solution.py:353
  16.6 0.2 collective-permute-start.8
  16.9 0.0 collective-permute-done.1.rest_0_
  16.9 1.3 %collective-permute-start.9 = (bf16[192,128]{1,0:T(8,128)(2,1)S(1)}, bf16[192,128]{1,0:T(8,128)(2,1)S(1)}, u32[]{:S(2)}, u32[]{:S(2)}) collective-permute-start(bf16[192,128]{1,0:T(8,128)(2,1)S(1)} %get-tuple-element.52), channel_id=1, source_target_pairs={{0,8},{8,0},{16,24},{24,16},{1,9},{9,1},{17,25},{25,17},{2,10},{10... | collective-permute-start | bytes 147464 | tf_op jit(solution)/shard_map/ppermute | solution.py:353
  18.2 0.0 collective-permute-done.2.rest_1_
  18.2 2.5 %collective-permute-done.3.rest_2_ = bf16[192,128]{1,0:T(8,128)(2,1)S(1)} collective-permute-done((bf16[192,128]{1,0:T(8,128)(2,1)S(1)}, bf16[192,128]{1,0:T(8,128)(2,1)S(1)}, u32[]{:S(2)}, u32[]{:S(2)}) %collective-permute-start.3) | collective-permute-done | bytes 49184 | tf_op jit(solution)/shard_map/ppermute | solution.py:353
  20.7 0.0 copy-done.1
  20.7 1.2 %shard_map.125.own_ref = f32[128,1024]{1,0:T(8,128)S(1)} custom-call(s32[1]{0:T(128)} %bitcast.me_ref, bf16[192,512]{1,0:T(8,128)(2,1)} %bitcast.23, bf16[768,1024]{1,0:T(8,128)(2,1)S(1)} %copy-done.1, bf16[192,128]{1,0:T(8,128)(2,1)S(1)} %collective-permute-done.1.rest_0_, bf16[192,128]{1,0:T(8,128)(2,1)S(1)} %collective-permute-done.2.rest_1_, ...), custom_call_target="tpu_custom_call" | custom-call | flops 201326592 | bytes 2097152 | tf_op jit(solution)/shard_map/pallas_call | solution.py:32
  21.9 0.0 collective-permute-done.7.rest_1_
  22.0 0.5 %collective-permute-done.8.rest_2_ = bf16[192,128]{1,0:T(8,128)(2,1)S(1)} collective-permute-done((bf16[192,128]{1,0:T(8,128)(2,1)S(1)}, bf16[192,128]{1,0:T(8,128)(2,1)S(1)}, u32[]{:S(2)}, u32[]{:S(2)}) %collective-permute-start.8) | collective-permute-done | bytes 49184 | tf_op jit(solution)/shard_map/ppermute | solution.py:353
  22.4 0.0 collective-permute-done.9.rest_3_
  22.5 0.0 copy-start.2
  22.5 0.7 %shard_map.127 = (bf16[128,1024]{1,0:T(8,128)(2,1)S(1)}, bf16[153,128]{1,0:T(8,128)(2,1)S(1)}, bf16[153,128]{1,0:T(8,128)(2,1)S(1)}, bf16[153,128]{1,0:T(8,128)(2,1)S(1)}, bf16[153,128]{1,0:T(8,128)(2,1)S(1)}) custom-call(s32[1]{0:T(128)} %bitcast.me_ref, bf16[768,1024]{1,0:T(8,128)(2,1)S(1)} %copy-done, bf16[153,1024]{1,0:T(8,128)(2,1)S(1)} %bitcast.20, ...), custom_call_target="tpu_custom_call" | custom-call | flops 201326592 | bytes 2097152 | tf_op jit(solution)/shard_map/pallas_call | solution.py:32
  23.1 2.5 %collective-permute-start.10 = (bf16[153,128]{1,0:T(8,128)(2,1)S(1)}, bf16[153,128]{1,0:T(8,128)(2,1)S(1)}, u32[]{:S(2)}, u32[]{:S(2)}) collective-permute-start(bf16[153,128]{1,0:T(8,128)(2,1)S(1)} %get-tuple-element.57), channel_id=1, source_target_pairs={{0,24},{8,16},{16,8},{24,0},{1,25},{9,17},{17,9},{25,1},{2,26},{10... | collective-permute-start | bytes 117512 | tf_op jit(solution)/shard_map/ppermute | solution.py:353
  25.7 0.0 collective-permute-start.11
  25.7 1.9 %collective-permute-start.12 = (bf16[153,128]{1,0:T(8,128)(2,1)S(1)}, bf16[153,128]{1,0:T(8,128)(2,1)S(1)}, u32[]{:S(2)}, u32[]{:S(2)}) collective-permute-start(bf16[153,128]{1,0:T(8,128)(2,1)S(1)} %get-tuple-element.59), channel_id=1, source_target_pairs={{0,8},{8,0},{16,24},{24,16},{1,9},{9,1},{17,25},{25,17},{2,10},{10... | collective-permute-start | bytes 117512 | tf_op jit(solution)/shard_map/ppermute | solution.py:353
  27.6 0.9 %shard_map.130.hits_ref.after = bf16[128,512]{1,0:T(8,128)(2,1)S(1)} custom-call(bf16[153,128]{1,0:T(8,128)(2,1)S(1)} %get-tuple-element.56.rest_0_.after, s32[1]{0:T(128)} %bitcast.me_ref, s32[1]{0:T(128)} %bitcast.4.part_ref, s32[8,4,16]{2,1,0:T(4,128)} %bitcast.28), custom_call_target="tpu_custom_call" | custom-call | bytes 524288 | tf_op jit(solution)/shard_map/pallas_call | solution.py:32
  28.5 0.6 %collective-permute-done.10.rest_1_ = bf16[153,128]{1,0:T(8,128)(2,1)S(1)} collective-permute-done((bf16[153,128]{1,0:T(8,128)(2,1)S(1)}, bf16[153,128]{1,0:T(8,128)(2,1)S(1)}, u32[]{:S(2)}, u32[]{:S(2)}) %collective-permute-start.10) | collective-permute-done | bytes 39200 | tf_op jit(solution)/shard_map/ppermute | solution.py:353
  29.1 1.5 %collective-permute-done.11.rest_2_ = bf16[153,128]{1,0:T(8,128)(2,1)S(1)} collective-permute-done((bf16[153,128]{1,0:T(8,128)(2,1)S(1)}, bf16[153,128]{1,0:T(8,128)(2,1)S(1)}, u32[]{:S(2)}, u32[]{:S(2)}) %collective-permute-start.11) | collective-permute-done | bytes 39200 | tf_op jit(solution)/shard_map/ppermute | solution.py:353
  30.6 0.0 collective-permute-done.12.rest_3_
  30.6 0.3 shard_map.131
  30.9 0.1 collective-permute-start.13
  30.9 1.2 %collective-permute-done.13.got_ref = bf16[4,16,256]{2,1,0:T(8,128)(2,1)S(1)} collective-permute-done((bf16[4,16,256]{2,1,0:T(8,128)(2,1)S(1)}, bf16[4,16,256]{2,1,0:T(8,128)(2,1)S(1)}, u32[]{:S(2)}, u32[]{:S(2)}) %collective-permute-start.13) | collective-permute-done | bytes 32800 | tf_op jit(solution)/shard_map/ppermute | solution.py:358
  32.1 2.4 %collective-permute-start.14 = (bf16[2,16,256]{2,1,0:T(8,128)(2,1)S(1)}, bf16[2,16,256]{2,1,0:T(8,128)(2,1)S(1)}, u32[]{:S(2)}, u32[]{:S(2)}) collective-permute-start(bf16[2,16,256]{2,1,0:T(8,128)(2,1)S(1)} %get-tuple-element.63), channel_id=1, source_target_pairs={{0,6},{1,7},{2,4},{3,5},{4,2},{5,3},{6,0},{7,1},{8,14},{9,15},{10,... | collective-permute-start | bytes 49160 | tf_op jit(solution)/shard_map/ppermute | solution.py:362
  34.6 0.5 %collective-permute-start.15 = (bf16[2,16,256]{2,1,0:T(8,128)(2,1)S(1)}, bf16[2,16,256]{2,1,0:T(8,128)(2,1)S(1)}, u32[]{:S(2)}, u32[]{:S(2)}) collective-permute-start(bf16[2,16,256]{2,1,0:T(8,128)(2,1)S(1)} %get-tuple-element.64), channel_id=1, source_target_pairs={{0,4},{1,5},{2,6},{3,7},{4,0},{5,1},{6,2},{7,3},{8,12},{9,13},{10,... | collective-permute-start | bytes 49160 | tf_op jit(solution)/shard_map/ppermute | solution.py:362
  35.1 0.5 %collective-permute-start.16 = (bf16[2,16,256]{2,1,0:T(8,128)(2,1)S(1)}, bf16[2,16,256]{2,1,0:T(8,128)(2,1)S(1)}, u32[]{:S(2)}, u32[]{:S(2)}) collective-permute-start(bf16[2,16,256]{2,1,0:T(8,128)(2,1)S(1)} %get-tuple-element.65), channel_id=1, source_target_pairs={{0,2},{1,3},{2,0},{3,1},{4,6},{5,7},{6,4},{7,5},{8,10},{9,11},{10,... | collective-permute-start | bytes 49160 | tf_op jit(solution)/shard_map/ppermute | solution.py:362
  35.6 0.7 %shard_map.128 = (f32[153,128]{1,0:T(8,128)S(1)}, bf16[128,1024]{1,0:T(8,128)(2,1)}) custom-call(bf16[128,1024]{1,0:T(8,128)(2,1)S(1)} %get-tuple-element.53.hidden_ref, bf16[153,1024]{1,0:T(8,128)(2,1)S(1)} %bitcast.19), custom_call_target="tpu_custom_call" | custom-call | flops 40108032 | bytes 1048576 | tf_op jit(solution)/shard_map/pallas_call | solution.py:32
  36.3 0.2 shard_map.129.near_ref
  36.6 0.2 collective-permute-done.14.rest_1_
  36.8 1.5 %collective-permute-done.15.rest_2_ = bf16[2,16,256]{2,1,0:T(8,128)(2,1)S(1)} collective-permute-done((bf16[2,16,256]{2,1,0:T(8,128)(2,1)S(1)}, bf16[2,16,256]{2,1,0:T(8,128)(2,1)S(1)}, u32[]{:S(2)}, u32[]{:S(2)}) %collective-permute-start.15) | collective-permute-done | bytes 16416 | tf_op jit(solution)/shard_map/ppermute | solution.py:362
  38.3 0.5 %collective-permute-done.16.rest_3_ = bf16[2,16,256]{2,1,0:T(8,128)(2,1)S(1)} collective-permute-done((bf16[2,16,256]{2,1,0:T(8,128)(2,1)S(1)}, bf16[2,16,256]{2,1,0:T(8,128)(2,1)S(1)}, u32[]{:S(2)}, u32[]{:S(2)}) %collective-permute-start.16) | collective-permute-done | bytes 16416 | tf_op jit(solution)/shard_map/ppermute | solution.py:362
  38.8 0.9 %shard_map.133 = f32[153,1,128]{2,1,0:T(1,128)} custom-call(s32[1]{0:T(128)} %bitcast.me_ref, f32[153,128]{1,0:T(8,128)S(1)} %shard_map.129.near_ref, bf16[4,8,16,128]{3,2,1,0:T(8,128)(2,1)S(1)} %get-tuple-element.44.edges_ref, f32[4,208,128]{2,1,0:T(8,128)S(1)} %get-tuple-element.43.sums_ref, bf16[2,16,256]{2,1,0:T(8,128)(2,1)S(1)} %get-tuple-element.62.rest_0_, ...), custom_call_target="tpu_custom_call" | custom-call | flops 5013504 | bytes 524288 | tf_op jit(solution)/shard_map/pallas_call | solution.py:32
  (6 shorter events, 0.0 us)
Async XLA Ops:
  0.6 20.1 %copy-start.1 = (bf16[768,1024]{1,0:T(8,128)(2,1)S(1)}, bf16[768,1024]{1,0:T(8,128)(2,1)}, u32[]{:S(2)}) copy-start(bf16[768,1024]{1,0:T(8,128)(2,1)} %weight_ref.2) | copy-start | bytes 4718596
  2.2 2.2 %collective-permute-start = (bf16[4,64,256]{2,1,0:T(8,128)(2,1)S(1)}, bf16[4,64,256]{2,1,0:T(8,128)(2,1)S(1)}, u32[]{:S(2)}, u32[]{:S(2)}) collective-permute-start(bf16[4,64,256]{2,1,0:T(8,128)(2,1)S(1)} %get-tuple-element.36), channel_id=1, source_target_pairs={{0,1},{1,0},{2,3},{3,2},{4,5},{5,4},{6,7},{7,6},{8,9},{9,8},{10,11... | collective-permute-start | bytes 393224 | tf_op jit(solution)/shard_map/ppermute | solution.py:358
  4.4 8.6 %collective-permute-start.4 = (bf16[2,64,256]{2,1,0:T(8,128)(2,1)S(1)}, bf16[2,64,256]{2,1,0:T(8,128)(2,1)S(1)}, u32[]{:S(2)}, u32[]{:S(2)}) collective-permute-start(bf16[2,64,256]{2,1,0:T(8,128)(2,1)S(1)} %get-tuple-element.46), channel_id=1, source_target_pairs={{0,6},{1,7},{2,4},{3,5},{4,2},{5,3},{6,0},{7,1},{8,14},{9,15},{10,... | collective-permute-start | bytes 196616 | tf_op jit(solution)/shard_map/ppermute | solution.py:362
  7.9 5.5 %collective-permute-start.5 = (bf16[2,64,256]{2,1,0:T(8,128)(2,1)S(1)}, bf16[2,64,256]{2,1,0:T(8,128)(2,1)S(1)}, u32[]{:S(2)}, u32[]{:S(2)}) collective-permute-start(bf16[2,64,256]{2,1,0:T(8,128)(2,1)S(1)} %get-tuple-element.47), channel_id=1, source_target_pairs={{0,4},{1,5},{2,6},{3,7},{4,0},{5,1},{6,2},{7,3},{8,12},{9,13},{10,... | collective-permute-start | bytes 196616 | tf_op jit(solution)/shard_map/ppermute | solution.py:362
  8.4 5.0 %collective-permute-start.6 = (bf16[2,64,256]{2,1,0:T(8,128)(2,1)S(1)}, bf16[2,64,256]{2,1,0:T(8,128)(2,1)S(1)}, u32[]{:S(2)}, u32[]{:S(2)}) collective-permute-start(bf16[2,64,256]{2,1,0:T(8,128)(2,1)S(1)} %get-tuple-element.48), channel_id=1, source_target_pairs={{0,2},{1,3},{2,0},{3,1},{4,6},{5,7},{6,4},{7,5},{8,10},{9,11},{10,... | collective-permute-start | bytes 196616 | tf_op jit(solution)/shard_map/ppermute | solution.py:362
  8.6 8.3 %collective-permute-start.1 = (bf16[192,128]{1,0:T(8,128)(2,1)S(1)}, bf16[192,128]{1,0:T(8,128)(2,1)S(1)}, u32[]{:S(2)}, u32[]{:S(2)}) collective-permute-start(bf16[192,128]{1,0:T(8,128)(2,1)S(1)} %get-tuple-element.40), channel_id=1, source_target_pairs={{0,8},{8,0},{16,24},{24,16},{1,9},{9,1},{17,25},{25,17},{2,10},{10... | collective-permute-start | bytes 147464 | tf_op jit(solution)/shard_map/ppermute | solution.py:353
  10.5 7.7 %collective-permute-start.2 = (bf16[192,128]{1,0:T(8,128)(2,1)S(1)}, bf16[192,128]{1,0:T(8,128)(2,1)S(1)}, u32[]{:S(2)}, u32[]{:S(2)}) collective-permute-start(bf16[192,128]{1,0:T(8,128)(2,1)S(1)} %get-tuple-element.41), channel_id=1, source_target_pairs={{0,24},{8,16},{16,8},{24,0},{1,25},{9,17},{17,9},{25,1},{2,26},{10... | collective-permute-start | bytes 147464 | tf_op jit(solution)/shard_map/ppermute | solution.py:353
  13.0 7.7 %collective-permute-start.3 = (bf16[192,128]{1,0:T(8,128)(2,1)S(1)}, bf16[192,128]{1,0:T(8,128)(2,1)S(1)}, u32[]{:S(2)}, u32[]{:S(2)}) collective-permute-start(bf16[192,128]{1,0:T(8,128)(2,1)S(1)} %get-tuple-element.42), channel_id=1, source_target_pairs={{0,16},{8,24},{16,0},{24,8},{1,17},{9,25},{17,1},{25,9},{2,18},{10... | collective-permute-start | bytes 147464 | tf_op jit(solution)/shard_map/ppermute | solution.py:353
  13.5 9.0 %copy-start = (bf16[768,1024]{1,0:T(8,128)(2,1)S(1)}, bf16[768,1024]{1,0:T(8,128)(2,1)}, u32[]{:S(2)}) copy-start(bf16[768,1024]{1,0:T(8,128)(2,1)} %weight_ref.3) | copy-start | bytes 4718596
  13.5 9.0 %copy-start.3 = (bf16[1024,153]{0,1:T(8,128)(2,1)S(1)}, bf16[1024,153]{0,1:T(8,128)(2,1)}, u32[]{:S(2)}) copy-start(bf16[1024,153]{0,1:T(8,128)(2,1)} %param.21) | copy-start | bytes 940036
  13.7 8.2 %collective-permute-start.7 = (bf16[192,128]{1,0:T(8,128)(2,1)S(1)}, bf16[192,128]{1,0:T(8,128)(2,1)S(1)}, u32[]{:S(2)}, u32[]{:S(2)}) collective-permute-start(bf16[192,128]{1,0:T(8,128)(2,1)S(1)} %get-tuple-element.50), channel_id=1, source_target_pairs={{0,24},{8,16},{16,8},{24,0},{1,25},{9,17},{17,9},{25,1},{2,26},{10... | collective-permute-start | bytes 147464 | tf_op jit(solution)/shard_map/ppermute | solution.py:353
  16.6 5.8 %collective-permute-start.8 = (bf16[192,128]{1,0:T(8,128)(2,1)S(1)}, bf16[192,128]{1,0:T(8,128)(2,1)S(1)}, u32[]{:S(2)}, u32[]{:S(2)}) collective-permute-start(bf16[192,128]{1,0:T(8,128)(2,1)S(1)} %get-tuple-element.51), channel_id=1, source_target_pairs={{0,16},{8,24},{16,0},{24,8},{1,17},{9,25},{17,1},{25,9},{2,18},{10... | collective-permute-start | bytes 147464 | tf_op jit(solution)/shard_map/ppermute | solution.py:353
  16.9 5.6 %collective-permute-start.9 = (bf16[192,128]{1,0:T(8,128)(2,1)S(1)}, bf16[192,128]{1,0:T(8,128)(2,1)S(1)}, u32[]{:S(2)}, u32[]{:S(2)}) collective-permute-start(bf16[192,128]{1,0:T(8,128)(2,1)S(1)} %get-tuple-element.52), channel_id=1, source_target_pairs={{0,8},{8,0},{16,24},{24,16},{1,9},{9,1},{17,25},{25,17},{2,10},{10... | collective-permute-start | bytes 147464 | tf_op jit(solution)/shard_map/ppermute | solution.py:353
  22.5 13.2 %copy-start.2 = (bf16[1024,153]{0,1:T(8,128)(2,1)S(1)}, bf16[1024,153]{0,1:T(8,128)(2,1)}, u32[]{:S(2)}) copy-start(bf16[1024,153]{0,1:T(8,128)(2,1)} %param.20) | copy-start | bytes 940036
  23.1 5.9 %collective-permute-start.10 = (bf16[153,128]{1,0:T(8,128)(2,1)S(1)}, bf16[153,128]{1,0:T(8,128)(2,1)S(1)}, u32[]{:S(2)}, u32[]{:S(2)}) collective-permute-start(bf16[153,128]{1,0:T(8,128)(2,1)S(1)} %get-tuple-element.57), channel_id=1, source_target_pairs={{0,24},{8,16},{16,8},{24,0},{1,25},{9,17},{17,9},{25,1},{2,26},{10... | collective-permute-start | bytes 117512 | tf_op jit(solution)/shard_map/ppermute | solution.py:353
  25.7 4.9 %collective-permute-start.11 = (bf16[153,128]{1,0:T(8,128)(2,1)S(1)}, bf16[153,128]{1,0:T(8,128)(2,1)S(1)}, u32[]{:S(2)}, u32[]{:S(2)}) collective-permute-start(bf16[153,128]{1,0:T(8,128)(2,1)S(1)} %get-tuple-element.58), channel_id=1, source_target_pairs={{0,16},{8,24},{16,0},{24,8},{1,17},{9,25},{17,1},{25,9},{2,18},{10... | collective-permute-start | bytes 117512 | tf_op jit(solution)/shard_map/ppermute | solution.py:353
  25.7 4.9 %collective-permute-start.12 = (bf16[153,128]{1,0:T(8,128)(2,1)S(1)}, bf16[153,128]{1,0:T(8,128)(2,1)S(1)}, u32[]{:S(2)}, u32[]{:S(2)}) collective-permute-start(bf16[153,128]{1,0:T(8,128)(2,1)S(1)} %get-tuple-element.59), channel_id=1, source_target_pairs={{0,8},{8,0},{16,24},{24,16},{1,9},{9,1},{17,25},{25,17},{2,10},{10... | collective-permute-start | bytes 117512 | tf_op jit(solution)/shard_map/ppermute | solution.py:353
  30.9 1.3 %collective-permute-start.13 = (bf16[4,16,256]{2,1,0:T(8,128)(2,1)S(1)}, bf16[4,16,256]{2,1,0:T(8,128)(2,1)S(1)}, u32[]{:S(2)}, u32[]{:S(2)}) collective-permute-start(bf16[4,16,256]{2,1,0:T(8,128)(2,1)S(1)} %get-tuple-element.61), channel_id=1, source_target_pairs={{0,1},{1,0},{2,3},{3,2},{4,5},{5,4},{6,7},{7,6},{8,9},{9,8},{10,11... | collective-permute-start | bytes 98312 | tf_op jit(solution)/shard_map/ppermute | solution.py:358
  32.1 4.6 %collective-permute-start.14 = (bf16[2,16,256]{2,1,0:T(8,128)(2,1)S(1)}, bf16[2,16,256]{2,1,0:T(8,128)(2,1)S(1)}, u32[]{:S(2)}, u32[]{:S(2)}) collective-permute-start(bf16[2,16,256]{2,1,0:T(8,128)(2,1)S(1)} %get-tuple-element.63), channel_id=1, source_target_pairs={{0,6},{1,7},{2,4},{3,5},{4,2},{5,3},{6,0},{7,1},{8,14},{9,15},{10,... | collective-permute-start | bytes 49160 | tf_op jit(solution)/shard_map/ppermute | solution.py:362
  34.6 3.7 %collective-permute-start.15 = (bf16[2,16,256]{2,1,0:T(8,128)(2,1)S(1)}, bf16[2,16,256]{2,1,0:T(8,128)(2,1)S(1)}, u32[]{:S(2)}, u32[]{:S(2)}) collective-permute-start(bf16[2,16,256]{2,1,0:T(8,128)(2,1)S(1)} %get-tuple-element.64), channel_id=1, source_target_pairs={{0,4},{1,5},{2,6},{3,7},{4,0},{5,1},{6,2},{7,3},{8,12},{9,13},{10,... | collective-permute-start | bytes 49160 | tf_op jit(solution)/shard_map/ppermute | solution.py:362
  35.1 3.7 %collective-permute-start.16 = (bf16[2,16,256]{2,1,0:T(8,128)(2,1)S(1)}, bf16[2,16,256]{2,1,0:T(8,128)(2,1)S(1)}, u32[]{:S(2)}, u32[]{:S(2)}) collective-permute-start(bf16[2,16,256]{2,1,0:T(8,128)(2,1)S(1)} %get-tuple-element.65), channel_id=1, source_target_pairs={{0,2},{1,3},{2,0},{3,1},{4,6},{5,7},{6,4},{7,5},{8,10},{9,11},{10,... | collective-permute-start | bytes 49160 | tf_op jit(solution)/shard_map/ppermute | solution.py:362

commit v13 on v12

--- a/solution.py
+++ b/solution.py
@@ -44,8 +44,8 @@
 
 
 def step_of(groups, k, near=False):
-    if near and k:
-        return 1 if k == 1 else groups - k + 1
+    if near and groups > 2 and k in (1, 2):
+        return groups - 3 + k
     return (groups - k) % groups
 
 

time: 39.9 us -> 39.1 us (0.980)
  waiting for transfers between devices: 8.52 us -> 7.96 us
    ppermute x9, waiting for transfers between devices: 5.08 us -> 4.62 us  [shift(): lax.ppermute(block, 'feat', [(i, ahead(i, groups, k, near)) for i in rang...]
  transfers between devices with their start and end apart: 17 -> 17, of which waited for: 8 -> 9; matrix products, arithmetic and copies ran while one was open for 0% -> 0% of each run, Pallas kernels for 12% -> 13%
where the time goes in v13:
time: 39.1 us; the launch traced here: 38.8 us
  starting transfers between devices  21.7 us (55%)
  Pallas kernels  8.33 us (21%)
  waiting for transfers between devices  7.96 us (20%)
  between operations  0.78 us (2%)
    ppermute x9, starting transfers between devices, shift(): lax.ppermute(block, 'feat', [(i, ahead(i, groups, k, near)) for i in rang...  13.5 us
    pallas_call x12, Pallas kernels, placed(): run(*(pltpu.with_memory_space_constraint(value, pltpu.HBM) if spec is HB...  8.33 us
    ppermute x6, starting transfers between devices, to_chips(): lax.ppermute(blocks[j], 'dom', [(d, next_to(d // 2, j, chips) * 2 + d % 2...  7.66 us
    ppermute x9, waiting for transfers between devices, shift(): lax.ppermute(block, 'feat', [(i, ahead(i, groups, k, near)) for i in rang...  4.62 us
    ppermute x6, waiting for transfers between devices, to_chips(): lax.ppermute(blocks[j], 'dom', [(d, next_to(d // 2, j, chips) * 2 + d % 2...  2.15 us
    ppermute x2, waiting for transfers between devices, to_mate(): return lax.ppermute(value, 'dom', [(d, d ^ 1) for d in range(parts)])  1.2 us
  transfers between devices with their start and end apart: 17, of which 9 were waited for; matrix products, arithmetic and copies ran while one was open for 0% of the time, Pallas kernels for 13%

profile of v13, /device:TPU:0, one launch (start us, length us, event | category | flops | bytes accessed | tf_op | source)
XLA Modules:
  0.0 38.8 jit_solution(1821648426914963399)
XLA Ops:
  0.6 0.0 copy-start.1
  0.6 1.5 %shard_map.123 = (bf16[4,64,256]{2,1,0:T(8,128)(2,1)S(1)}, bf16[4,64,256]{2,1,0:T(8,128)(2,1)S(1)}, bf16[192,128]{1,0:T(8,128)(2,1)S(1)}, bf16[192,128]{1,0:T(8,128)(2,1)S(1)}, bf16[192,128]{1,0:T(8,128)(2,1)S(1)}) custom-call(s32[1]{0:T(128)} %bitcast.me_ref, s32[1]{0:T(128)} %bitcast.4.part_ref, s32[8,4,16]{2,1,0:T(4,128)} %bitcast.27, ...), custom_call_target="tpu_custom_call" | custom-call | flops 100663296 | bytes 1048576 | tf_op jit(solution)/shard_map/pallas_call | solution.py:32
  2.2 0.5 %collective-permute-start = (bf16[4,64,256]{2,1,0:T(8,128)(2,1)S(1)}, bf16[4,64,256]{2,1,0:T(8,128)(2,1)S(1)}, u32[]{:S(2)}, u32[]{:S(2)}) collective-permute-start(bf16[4,64,256]{2,1,0:T(8,128)(2,1)S(1)} %get-tuple-element.36), channel_id=1, source_target_pairs={{0,1},{1,0},{2,3},{3,2},{4,5},{5,4},{6,7},{7,6},{8,9},{9,8},{10,11... | collective-permute-start | bytes 393224 | tf_op jit(solution)/shard_map/ppermute | solution.py:358
  2.7 1.6 %shard_map.122 = (f32[4,208,128]{2,1,0:T(8,128)S(1)}, bf16[4,8,16,128]{3,2,1,0:T(8,128)(2,1)S(1)}, bf16[128,512]{1,0:T(8,128)(2,1)S(1)}) custom-call(s32[1]{0:T(128)} %bitcast.me_ref, s32[1]{0:T(128)} %bitcast.4.part_ref, s32[2,12]{1,0:T(2,128)} %bitcast.31, s32[4,8]{1,0:T(4,128)} %bitcast.30, bf16[192,512]{1,0:T(8,128)(2,1)} %bitcast.22, ...), custom_call_target="tpu_custom_call" | custom-call | flops 100663296 | bytes 1048576 | tf_op jit(solution)/shard_map/pallas_call | solution.py:32
  4.3 0.0 collective-permute-done.got_ref
  4.4 3.5 %collective-permute-start.4 = (bf16[2,64,256]{2,1,0:T(8,128)(2,1)S(1)}, bf16[2,64,256]{2,1,0:T(8,128)(2,1)S(1)}, u32[]{:S(2)}, u32[]{:S(2)}) collective-permute-start(bf16[2,64,256]{2,1,0:T(8,128)(2,1)S(1)} %get-tuple-element.46), channel_id=1, source_target_pairs={{0,6},{1,7},{2,4},{3,5},{4,2},{5,3},{6,0},{7,1},{8,14},{9,15},{10,... | collective-permute-start | bytes 196616 | tf_op jit(solution)/shard_map/ppermute | solution.py:362
  7.9 0.5 %collective-permute-start.5 = (bf16[2,64,256]{2,1,0:T(8,128)(2,1)S(1)}, bf16[2,64,256]{2,1,0:T(8,128)(2,1)S(1)}, u32[]{:S(2)}, u32[]{:S(2)}) collective-permute-start(bf16[2,64,256]{2,1,0:T(8,128)(2,1)S(1)} %get-tuple-element.47), channel_id=1, source_target_pairs={{0,4},{1,5},{2,6},{3,7},{4,0},{5,1},{6,2},{7,3},{8,12},{9,13},{10,... | collective-permute-start | bytes 196616 | tf_op jit(solution)/shard_map/ppermute | solution.py:362
  8.4 0.1 collective-permute-start.6
  8.6 3.0 %collective-permute-start.1 = (bf16[192,128]{1,0:T(8,128)(2,1)S(1)}, bf16[192,128]{1,0:T(8,128)(2,1)S(1)}, u32[]{:S(2)}, u32[]{:S(2)}) collective-permute-start(bf16[192,128]{1,0:T(8,128)(2,1)S(1)} %get-tuple-element.40), channel_id=1, source_target_pairs={{0,16},{8,24},{16,0},{24,8},{1,17},{9,25},{17,1},{25,9},{2,18},{10... | collective-permute-start | bytes 147464 | tf_op jit(solution)/shard_map/ppermute | solution.py:353
  11.5 1.3 %collective-permute-start.2 = (bf16[192,128]{1,0:T(8,128)(2,1)S(1)}, bf16[192,128]{1,0:T(8,128)(2,1)S(1)}, u32[]{:S(2)}, u32[]{:S(2)}) collective-permute-start(bf16[192,128]{1,0:T(8,128)(2,1)S(1)} %get-tuple-element.41), channel_id=1, source_target_pairs={{0,24},{8,16},{16,8},{24,0},{1,25},{9,17},{17,9},{25,1},{2,26},{10... | collective-permute-start | bytes 147464 | tf_op jit(solution)/shard_map/ppermute | solution.py:353
  12.9 0.0 collective-permute-done.4.rest_1_
  12.9 0.2 collective-permute-start.3
  13.1 0.0 collective-permute-done.5.rest_2_
  13.1 0.0 collective-permute-done.6.rest_3_
  13.1 0.0 copy-start.3
  13.2 0.3 shard_map.126
  13.4 3.2 %collective-permute-start.7 = (bf16[192,128]{1,0:T(8,128)(2,1)S(1)}, bf16[192,128]{1,0:T(8,128)(2,1)S(1)}, u32[]{:S(2)}, u32[]{:S(2)}) collective-permute-start(bf16[192,128]{1,0:T(8,128)(2,1)S(1)} %get-tuple-element.50), channel_id=1, source_target_pairs={{0,24},{8,16},{16,8},{24,0},{1,25},{9,17},{17,9},{25,1},{2,26},{10... | collective-permute-start | bytes 147464 | tf_op jit(solution)/shard_map/ppermute | solution.py:353
  16.6 0.1 collective-permute-start.8
  16.7 0.0 collective-permute-done.1.rest_0_
  16.7 1.1 %collective-permute-start.9 = (bf16[192,128]{1,0:T(8,128)(2,1)S(1)}, bf16[192,128]{1,0:T(8,128)(2,1)S(1)}, u32[]{:S(2)}, u32[]{:S(2)}) collective-permute-start(bf16[192,128]{1,0:T(8,128)(2,1)S(1)} %get-tuple-element.52), channel_id=1, source_target_pairs={{0,8},{8,0},{16,24},{24,16},{1,9},{9,1},{17,25},{25,17},{2,10},{10... | collective-permute-start | bytes 147464 | tf_op jit(solution)/shard_map/ppermute | solution.py:353
  17.9 0.1 collective-permute-done.2.rest_1_
  18.0 0.0 collective-permute-done.3.rest_2_
  18.0 0.0 copy-done.1
  18.0 1.2 %shard_map.125.own_ref = f32[128,1024]{1,0:T(8,128)S(1)} custom-call(s32[1]{0:T(128)} %bitcast.me_ref, bf16[192,512]{1,0:T(8,128)(2,1)} %bitcast.23, bf16[768,1024]{1,0:T(8,128)(2,1)S(1)} %copy-done.1, bf16[192,128]{1,0:T(8,128)(2,1)S(1)} %collective-permute-done.1.rest_0_, bf16[192,128]{1,0:T(8,128)(2,1)S(1)} %collective-permute-done.2.rest_1_, ...), custom_call_target="tpu_custom_call" | custom-call | flops 201326592 | bytes 2097152 | tf_op jit(solution)/shard_map/pallas_call | solution.py:32
  19.2 0.4 collective-permute-done.7.rest_1_
  19.6 2.2 %collective-permute-done.8.rest_2_ = bf16[192,128]{1,0:T(8,128)(2,1)S(1)} collective-permute-done((bf16[192,128]{1,0:T(8,128)(2,1)S(1)}, bf16[192,128]{1,0:T(8,128)(2,1)S(1)}, u32[]{:S(2)}, u32[]{:S(2)}) %collective-permute-start.8) | collective-permute-done | bytes 49184 | tf_op jit(solution)/shard_map/ppermute | solution.py:353
  21.8 0.0 collective-permute-done.9.rest_3_
  21.8 0.0 copy-start.2
  21.8 0.7 %shard_map.127 = (bf16[128,1024]{1,0:T(8,128)(2,1)S(1)}, bf16[153,128]{1,0:T(8,128)(2,1)S(1)}, bf16[153,128]{1,0:T(8,128)(2,1)S(1)}, bf16[153,128]{1,0:T(8,128)(2,1)S(1)}, bf16[153,128]{1,0:T(8,128)(2,1)S(1)}) custom-call(s32[1]{0:T(128)} %bitcast.me_ref, bf16[768,1024]{1,0:T(8,128)(2,1)S(1)} %copy-done, bf16[153,1024]{1,0:T(8,128)(2,1)S(1)} %bitcast.20, ...), custom_call_target="tpu_custom_call" | custom-call | flops 201326592 | bytes 2097152 | tf_op jit(solution)/shard_map/pallas_call | solution.py:32
  22.5 2.4 %collective-permute-start.10 = (bf16[153,128]{1,0:T(8,128)(2,1)S(1)}, bf16[153,128]{1,0:T(8,128)(2,1)S(1)}, u32[]{:S(2)}, u32[]{:S(2)}) collective-permute-start(bf16[153,128]{1,0:T(8,128)(2,1)S(1)} %get-tuple-element.57), channel_id=1, source_target_pairs={{0,24},{8,16},{16,8},{24,0},{1,25},{9,17},{17,9},{25,1},{2,26},{10... | collective-permute-start | bytes 117512 | tf_op jit(solution)/shard_map/ppermute | solution.py:353
  24.9 0.0 collective-permute-start.11
  24.9 2.1 %collective-permute-start.12 = (bf16[153,128]{1,0:T(8,128)(2,1)S(1)}, bf16[153,128]{1,0:T(8,128)(2,1)S(1)}, u32[]{:S(2)}, u32[]{:S(2)}) collective-permute-start(bf16[153,128]{1,0:T(8,128)(2,1)S(1)} %get-tuple-element.59), channel_id=1, source_target_pairs={{0,8},{8,0},{16,24},{24,16},{1,9},{9,1},{17,25},{25,17},{2,10},{10... | collective-permute-start | bytes 117512 | tf_op jit(solution)/shard_map/ppermute | solution.py:353
  27.0 0.9 %shard_map.130.hits_ref.after = bf16[128,512]{1,0:T(8,128)(2,1)S(1)} custom-call(bf16[153,128]{1,0:T(8,128)(2,1)S(1)} %get-tuple-element.56.rest_0_.after, s32[1]{0:T(128)} %bitcast.me_ref, s32[1]{0:T(128)} %bitcast.4.part_ref, s32[8,4,16]{2,1,0:T(4,128)} %bitcast.28), custom_call_target="tpu_custom_call" | custom-call | bytes 524288 | tf_op jit(solution)/shard_map/pallas_call | solution.py:32
  27.9 0.6 %collective-permute-done.10.rest_1_ = bf16[153,128]{1,0:T(8,128)(2,1)S(1)} collective-permute-done((bf16[153,128]{1,0:T(8,128)(2,1)S(1)}, bf16[153,128]{1,0:T(8,128)(2,1)S(1)}, u32[]{:S(2)}, u32[]{:S(2)}) %collective-permute-start.10) | collective-permute-done | bytes 39200 | tf_op jit(solution)/shard_map/ppermute | solution.py:353
  28.5 1.3 %collective-permute-done.11.rest_2_ = bf16[153,128]{1,0:T(8,128)(2,1)S(1)} collective-permute-done((bf16[153,128]{1,0:T(8,128)(2,1)S(1)}, bf16[153,128]{1,0:T(8,128)(2,1)S(1)}, u32[]{:S(2)}, u32[]{:S(2)}) %collective-permute-start.11) | collective-permute-done | bytes 39200 | tf_op jit(solution)/shard_map/ppermute | solution.py:353
  29.8 0.0 collective-permute-done.12.rest_3_
  29.8 0.3 shard_map.131
  30.1 0.1 collective-permute-start.13
  30.2 1.2 %collective-permute-done.13.got_ref = bf16[4,16,256]{2,1,0:T(8,128)(2,1)S(1)} collective-permute-done((bf16[4,16,256]{2,1,0:T(8,128)(2,1)S(1)}, bf16[4,16,256]{2,1,0:T(8,128)(2,1)S(1)}, u32[]{:S(2)}, u32[]{:S(2)}) %collective-permute-start.13) | collective-permute-done | bytes 32800 | tf_op jit(solution)/shard_map/ppermute | solution.py:358
  31.4 2.5 %collective-permute-start.14 = (bf16[2,16,256]{2,1,0:T(8,128)(2,1)S(1)}, bf16[2,16,256]{2,1,0:T(8,128)(2,1)S(1)}, u32[]{:S(2)}, u32[]{:S(2)}) collective-permute-start(bf16[2,16,256]{2,1,0:T(8,128)(2,1)S(1)} %get-tuple-element.63), channel_id=1, source_target_pairs={{0,6},{1,7},{2,4},{3,5},{4,2},{5,3},{6,0},{7,1},{8,14},{9,15},{10,... | collective-permute-start | bytes 49160 | tf_op jit(solution)/shard_map/ppermute | solution.py:362
  33.9 0.3 collective-permute-start.15
  34.2 0.6 %collective-permute-start.16 = (bf16[2,16,256]{2,1,0:T(8,128)(2,1)S(1)}, bf16[2,16,256]{2,1,0:T(8,128)(2,1)S(1)}, u32[]{:S(2)}, u32[]{:S(2)}) collective-permute-start(bf16[2,16,256]{2,1,0:T(8,128)(2,1)S(1)} %get-tuple-element.65), channel_id=1, source_target_pairs={{0,2},{1,3},{2,0},{3,1},{4,6},{5,7},{6,4},{7,5},{8,10},{9,11},{10,... | collective-permute-start | bytes 49160 | tf_op jit(solution)/shard_map/ppermute | solution.py:362
  34.9 0.7 %shard_map.128 = (f32[153,128]{1,0:T(8,128)S(1)}, bf16[128,1024]{1,0:T(8,128)(2,1)}) custom-call(bf16[128,1024]{1,0:T(8,128)(2,1)S(1)} %get-tuple-element.53.hidden_ref, bf16[153,1024]{1,0:T(8,128)(2,1)S(1)} %bitcast.19), custom_call_target="tpu_custom_call" | custom-call | flops 40108032 | bytes 1048576 | tf_op jit(solution)/shard_map/pallas_call | solution.py:32
  35.6 0.2 shard_map.129.near_ref
  35.8 0.2 collective-permute-done.14.rest_1_
  36.0 1.6 %collective-permute-done.15.rest_2_ = bf16[2,16,256]{2,1,0:T(8,128)(2,1)S(1)} collective-permute-done((bf16[2,16,256]{2,1,0:T(8,128)(2,1)S(1)}, bf16[2,16,256]{2,1,0:T(8,128)(2,1)S(1)}, u32[]{:S(2)}, u32[]{:S(2)}) %collective-permute-start.15) | collective-permute-done | bytes 16416 | tf_op jit(solution)/shard_map/ppermute | solution.py:362
  37.6 0.3 collective-permute-done.16.rest_3_
  38.0 0.9 %shard_map.133 = f32[153,1,128]{2,1,0:T(1,128)} custom-call(s32[1]{0:T(128)} %bitcast.me_ref, f32[153,128]{1,0:T(8,128)S(1)} %shard_map.129.near_ref, bf16[4,8,16,128]{3,2,1,0:T(8,128)(2,1)S(1)} %get-tuple-element.44.edges_ref, f32[4,208,128]{2,1,0:T(8,128)S(1)} %get-tuple-element.43.sums_ref, bf16[2,16,256]{2,1,0:T(8,128)(2,1)S(1)} %get-tuple-element.62.rest_0_, ...), custom_call_target="tpu_custom_call" | custom-call | flops 5013504 | bytes 524288 | tf_op jit(solution)/shard_map/pallas_call | solution.py:32
  (6 shorter events, 0.0 us)
Async XLA Ops:
  0.6 17.4 %copy-start.1 = (bf16[768,1024]{1,0:T(8,128)(2,1)S(1)}, bf16[768,1024]{1,0:T(8,128)(2,1)}, u32[]{:S(2)}) copy-start(bf16[768,1024]{1,0:T(8,128)(2,1)} %weight_ref.2) | copy-start | bytes 4718596
  2.2 2.2 %collective-permute-start = (bf16[4,64,256]{2,1,0:T(8,128)(2,1)S(1)}, bf16[4,64,256]{2,1,0:T(8,128)(2,1)S(1)}, u32[]{:S(2)}, u32[]{:S(2)}) collective-permute-start(bf16[4,64,256]{2,1,0:T(8,128)(2,1)S(1)} %get-tuple-element.36), channel_id=1, source_target_pairs={{0,1},{1,0},{2,3},{3,2},{4,5},{5,4},{6,7},{7,6},{8,9},{9,8},{10,11... | collective-permute-start | bytes 393224 | tf_op jit(solution)/shard_map/ppermute | solution.py:358
  4.4 8.5 %collective-permute-start.4 = (bf16[2,64,256]{2,1,0:T(8,128)(2,1)S(1)}, bf16[2,64,256]{2,1,0:T(8,128)(2,1)S(1)}, u32[]{:S(2)}, u32[]{:S(2)}) collective-permute-start(bf16[2,64,256]{2,1,0:T(8,128)(2,1)S(1)} %get-tuple-element.46), channel_id=1, source_target_pairs={{0,6},{1,7},{2,4},{3,5},{4,2},{5,3},{6,0},{7,1},{8,14},{9,15},{10,... | collective-permute-start | bytes 196616 | tf_op jit(solution)/shard_map/ppermute | solution.py:362
  7.9 5.2 %collective-permute-start.5 = (bf16[2,64,256]{2,1,0:T(8,128)(2,1)S(1)}, bf16[2,64,256]{2,1,0:T(8,128)(2,1)S(1)}, u32[]{:S(2)}, u32[]{:S(2)}) collective-permute-start(bf16[2,64,256]{2,1,0:T(8,128)(2,1)S(1)} %get-tuple-element.47), channel_id=1, source_target_pairs={{0,4},{1,5},{2,6},{3,7},{4,0},{5,1},{6,2},{7,3},{8,12},{9,13},{10,... | collective-permute-start | bytes 196616 | tf_op jit(solution)/shard_map/ppermute | solution.py:362
  8.4 4.7 %collective-permute-start.6 = (bf16[2,64,256]{2,1,0:T(8,128)(2,1)S(1)}, bf16[2,64,256]{2,1,0:T(8,128)(2,1)S(1)}, u32[]{:S(2)}, u32[]{:S(2)}) collective-permute-start(bf16[2,64,256]{2,1,0:T(8,128)(2,1)S(1)} %get-tuple-element.48), channel_id=1, source_target_pairs={{0,2},{1,3},{2,0},{3,1},{4,6},{5,7},{6,4},{7,5},{8,10},{9,11},{10,... | collective-permute-start | bytes 196616 | tf_op jit(solution)/shard_map/ppermute | solution.py:362
  8.6 8.2 %collective-permute-start.1 = (bf16[192,128]{1,0:T(8,128)(2,1)S(1)}, bf16[192,128]{1,0:T(8,128)(2,1)S(1)}, u32[]{:S(2)}, u32[]{:S(2)}) collective-permute-start(bf16[192,128]{1,0:T(8,128)(2,1)S(1)} %get-tuple-element.40), channel_id=1, source_target_pairs={{0,16},{8,24},{16,0},{24,8},{1,17},{9,25},{17,1},{25,9},{2,18},{10... | collective-permute-start | bytes 147464 | tf_op jit(solution)/shard_map/ppermute | solution.py:353
  11.5 6.5 %collective-permute-start.2 = (bf16[192,128]{1,0:T(8,128)(2,1)S(1)}, bf16[192,128]{1,0:T(8,128)(2,1)S(1)}, u32[]{:S(2)}, u32[]{:S(2)}) collective-permute-start(bf16[192,128]{1,0:T(8,128)(2,1)S(1)} %get-tuple-element.41), channel_id=1, source_target_pairs={{0,24},{8,16},{16,8},{24,0},{1,25},{9,17},{17,9},{25,1},{2,26},{10... | collective-permute-start | bytes 147464 | tf_op jit(solution)/shard_map/ppermute | solution.py:353
  12.9 5.1 %collective-permute-start.3 = (bf16[192,128]{1,0:T(8,128)(2,1)S(1)}, bf16[192,128]{1,0:T(8,128)(2,1)S(1)}, u32[]{:S(2)}, u32[]{:S(2)}) collective-permute-start(bf16[192,128]{1,0:T(8,128)(2,1)S(1)} %get-tuple-element.42), channel_id=1, source_target_pairs={{0,8},{8,0},{16,24},{24,16},{1,9},{9,1},{17,25},{25,17},{2,10},{10... | collective-permute-start | bytes 147464 | tf_op jit(solution)/shard_map/ppermute | solution.py:353
  13.1 8.7 %copy-start = (bf16[768,1024]{1,0:T(8,128)(2,1)S(1)}, bf16[768,1024]{1,0:T(8,128)(2,1)}, u32[]{:S(2)}) copy-start(bf16[768,1024]{1,0:T(8,128)(2,1)} %weight_ref.3) | copy-start | bytes 4718596
  13.1 8.7 %copy-start.3 = (bf16[1024,153]{0,1:T(8,128)(2,1)S(1)}, bf16[1024,153]{0,1:T(8,128)(2,1)}, u32[]{:S(2)}) copy-start(bf16[1024,153]{0,1:T(8,128)(2,1)} %param.21) | copy-start | bytes 940036
  13.4 6.2 %collective-permute-start.7 = (bf16[192,128]{1,0:T(8,128)(2,1)S(1)}, bf16[192,128]{1,0:T(8,128)(2,1)S(1)}, u32[]{:S(2)}, u32[]{:S(2)}) collective-permute-start(bf16[192,128]{1,0:T(8,128)(2,1)S(1)} %get-tuple-element.50), channel_id=1, source_target_pairs={{0,24},{8,16},{16,8},{24,0},{1,25},{9,17},{17,9},{25,1},{2,26},{10... | collective-permute-start | bytes 147464 | tf_op jit(solution)/shard_map/ppermute | solution.py:353
  16.6 5.2 %collective-permute-start.8 = (bf16[192,128]{1,0:T(8,128)(2,1)S(1)}, bf16[192,128]{1,0:T(8,128)(2,1)S(1)}, u32[]{:S(2)}, u32[]{:S(2)}) collective-permute-start(bf16[192,128]{1,0:T(8,128)(2,1)S(1)} %get-tuple-element.51), channel_id=1, source_target_pairs={{0,16},{8,24},{16,0},{24,8},{1,17},{9,25},{17,1},{25,9},{2,18},{10... | collective-permute-start | bytes 147464 | tf_op jit(solution)/shard_map/ppermute | solution.py:353
  16.7 5.1 %collective-permute-start.9 = (bf16[192,128]{1,0:T(8,128)(2,1)S(1)}, bf16[192,128]{1,0:T(8,128)(2,1)S(1)}, u32[]{:S(2)}, u32[]{:S(2)}) collective-permute-start(bf16[192,128]{1,0:T(8,128)(2,1)S(1)} %get-tuple-element.52), channel_id=1, source_target_pairs={{0,8},{8,0},{16,24},{24,16},{1,9},{9,1},{17,25},{25,17},{2,10},{10... | collective-permute-start | bytes 147464 | tf_op jit(solution)/shard_map/ppermute | solution.py:353
  21.8 13.0 %copy-start.2 = (bf16[1024,153]{0,1:T(8,128)(2,1)S(1)}, bf16[1024,153]{0,1:T(8,128)(2,1)}, u32[]{:S(2)}) copy-start(bf16[1024,153]{0,1:T(8,128)(2,1)} %param.20) | copy-start | bytes 940036
  22.5 6.0 %collective-permute-start.10 = (bf16[153,128]{1,0:T(8,128)(2,1)S(1)}, bf16[153,128]{1,0:T(8,128)(2,1)S(1)}, u32[]{:S(2)}, u32[]{:S(2)}) collective-permute-start(bf16[153,128]{1,0:T(8,128)(2,1)S(1)} %get-tuple-element.57), channel_id=1, source_target_pairs={{0,24},{8,16},{16,8},{24,0},{1,25},{9,17},{17,9},{25,1},{2,26},{10... | collective-permute-start | bytes 117512 | tf_op jit(solution)/shard_map/ppermute | solution.py:353
  24.9 4.9 %collective-permute-start.11 = (bf16[153,128]{1,0:T(8,128)(2,1)S(1)}, bf16[153,128]{1,0:T(8,128)(2,1)S(1)}, u32[]{:S(2)}, u32[]{:S(2)}) collective-permute-start(bf16[153,128]{1,0:T(8,128)(2,1)S(1)} %get-tuple-element.58), channel_id=1, source_target_pairs={{0,16},{8,24},{16,0},{24,8},{1,17},{9,25},{17,1},{25,9},{2,18},{10... | collective-permute-start | bytes 117512 | tf_op jit(solution)/shard_map/ppermute | solution.py:353
  24.9 4.9 %collective-permute-start.12 = (bf16[153,128]{1,0:T(8,128)(2,1)S(1)}, bf16[153,128]{1,0:T(8,128)(2,1)S(1)}, u32[]{:S(2)}, u32[]{:S(2)}) collective-permute-start(bf16[153,128]{1,0:T(8,128)(2,1)S(1)} %get-tuple-element.59), channel_id=1, source_target_pairs={{0,8},{8,0},{16,24},{24,16},{1,9},{9,1},{17,25},{25,17},{2,10},{10... | collective-permute-start | bytes 117512 | tf_op jit(solution)/shard_map/ppermute | solution.py:353
  30.1 1.3 %collective-permute-start.13 = (bf16[4,16,256]{2,1,0:T(8,128)(2,1)S(1)}, bf16[4,16,256]{2,1,0:T(8,128)(2,1)S(1)}, u32[]{:S(2)}, u32[]{:S(2)}) collective-permute-start(bf16[4,16,256]{2,1,0:T(8,128)(2,1)S(1)} %get-tuple-element.61), channel_id=1, source_target_pairs={{0,1},{1,0},{2,3},{3,2},{4,5},{5,4},{6,7},{7,6},{8,9},{9,8},{10,11... | collective-permute-start | bytes 98312 | tf_op jit(solution)/shard_map/ppermute | solution.py:358
  31.4 4.6 %collective-permute-start.14 = (bf16[2,16,256]{2,1,0:T(8,128)(2,1)S(1)}, bf16[2,16,256]{2,1,0:T(8,128)(2,1)S(1)}, u32[]{:S(2)}, u32[]{:S(2)}) collective-permute-start(bf16[2,16,256]{2,1,0:T(8,128)(2,1)S(1)} %get-tuple-element.63), channel_id=1, source_target_pairs={{0,6},{1,7},{2,4},{3,5},{4,2},{5,3},{6,0},{7,1},{8,14},{9,15},{10,... | collective-permute-start | bytes 49160 | tf_op jit(solution)/shard_map/ppermute | solution.py:362
  33.9 3.7 %collective-permute-start.15 = (bf16[2,16,256]{2,1,0:T(8,128)(2,1)S(1)}, bf16[2,16,256]{2,1,0:T(8,128)(2,1)S(1)}, u32[]{:S(2)}, u32[]{:S(2)}) collective-permute-start(bf16[2,16,256]{2,1,0:T(8,128)(2,1)S(1)} %get-tuple-element.64), channel_id=1, source_target_pairs={{0,4},{1,5},{2,6},{3,7},{4,0},{5,1},{6,2},{7,3},{8,12},{9,13},{10,... | collective-permute-start | bytes 49160 | tf_op jit(solution)/shard_map/ppermute | solution.py:362
  34.2 3.7 %collective-permute-start.16 = (bf16[2,16,256]{2,1,0:T(8,128)(2,1)S(1)}, bf16[2,16,256]{2,1,0:T(8,128)(2,1)S(1)}, u32[]{:S(2)}, u32[]{:S(2)}) collective-permute-start(bf16[2,16,256]{2,1,0:T(8,128)(2,1)S(1)} %get-tuple-element.65), channel_id=1, source_target_pairs={{0,2},{1,3},{2,0},{3,1},{4,6},{5,7},{6,4},{7,5},{8,10},{9,11},{10,... | collective-permute-start | bytes 49160 | tf_op jit(solution)/shard_map/ppermute | solution.py:362

commit v14 on v13

--- a/solution.py
+++ b/solution.py
@@ -84,18 +84,49 @@
     return values.reshape(-1, values.shape[-1]).T
 
 
-def gather_kernel(chunk, me_ref, part_ref, sources_hbm, features_hbm, mine_ref, mate_ref, *rest):
-    blocks, (sources_ref, features_ref, order, hits, sems) = rest[:-5], rest[-5:]
+def gather_kernel(
+    chunk,
+    me_ref,
+    part_ref,
+    sources_hbm,
+    ids_hbm,
+    features_hbm,
+    tiles_hbm,
+    mine_ref,
+    mate_ref,
+    table_ref,
+    bands_ref,
+    *rest,
+):
+    blocks, (sources_ref, ids_ref, order, hits, sems, tile_sems) = rest[:-6], rest[-6:]
     parts, groups, slots = sources_ref.shape
-    nodes = hits.shape[1]
-    rows = nodes // groups
-    width = features_hbm.shape[0]
+    tiles, rows = tiles_hbm.shape[:2]
+    width, nodes = features_hbm.shape
+    lanes = mine_ref.shape[2]
     chips, chip, core = parts // 2, part_ref[0] // 2, part_ref[0] % 2
-    indices, table = fetch(
-        sems, (sources_hbm, sources_ref), (features_hbm, features_ref.at[pl.ds(0, width), :])
-    )
-    if features_ref.shape[0] > width:
-        features_ref[width:, :] = jnp.zeros((features_ref.shape[0] - width, nodes), bf16)
+    indices, ids, table = fetch(
+        sems,
+        (sources_hbm, sources_ref),
+        (ids_hbm, ids_ref),
+        (features_hbm, table_ref.at[pl.ds(0, width), :]),
+    )
+    table_ref[width : width + EXTRA, :] = jnp.ones((EXTRA, nodes), bf16)
+    if table_ref.shape[0] > width + EXTRA:
+        table_ref[width + EXTRA :, :] = jnp.zeros(
+            (table_ref.shape[0] - width - EXTRA, nodes), bf16
+        )
+    bands_ref[...] = jnp.zeros_like(bands_ref)
+
+    def tile_copy(t):
+        at = pl.multiple_of(ids_ref[1, t] * rows, rows)
+        to = bands_ref.at[ids_ref[0, t], :, pl.ds(at, rows)]
+        return pltpu.make_async_copy(tiles_hbm.at[t], to, tile_sems.at[t])
+
+    def each_tile(run):
+        lax.fori_loop(0, tiles, lambda t, _: run(tile_copy(t)), None, unroll=tiles <= 16)
+
+    ids.wait()
+    each_tile(lambda copy: copy.start())
     indices.wait()
     lane = lax.broadcasted_iota(jnp.int32, (slots, nodes), 1)
 
@@ -109,7 +140,7 @@
             ).astype(bf16)
         if last:
             table.wait()
-        picked = dot(hits[...], features_ref[...], LAST).astype(bf16)
+        picked = dot(hits[...], table_ref[:lanes, :], LAST).astype(bf16)
         out[pl.ds(i * chunk, chunk)] = picked.reshape(chunk, groups * slots, -1)
 
     if chips == chunk:
@@ -121,62 +152,41 @@
             lax.fori_loop(0, chips // chunk, lambda i, _: step(i, out, other, False), None)
     for k in range(1, groups):
         group = ahead(me_ref[0], groups, k, True)
-        blocks[k - 1][...] = features_ref[:width, pl.ds(pl.multiple_of(group * rows, rows), rows)]
+        blocks[k - 1][...] = table_ref[:width, pl.ds(pl.multiple_of(group * rows, rows), rows)]
+    each_tile(lambda copy: copy.wait())
 
 
 def local_kernel(
     chunk,
     me_ref,
     part_ref,
-    ids_hbm,
+    table_ref,
+    bands_ref,
     counts_hbm,
-    features_hbm,
-    tiles_hbm,
     targets_hbm,
     weight_hbm,
     sums_ref,
     edges_ref,
     band_ref,
-    ids_ref,
     counts_ref,
-    features_ref,
-    tiles_ref,
     targets_ref,
     weight_ref,
-    bands,
     sems,
 ):
-    me = me_ref[0]
     parts, groups, slots = targets_ref.shape
-    rows = tiles_ref.shape[1]
-    width = features_hbm.shape[0]
+    rows = edges_ref.shape[3]
+    high = sums_ref.shape[1]
     copies = fetch(
-        sems,
-        (ids_hbm, ids_ref),
-        (counts_hbm, counts_ref),
-        (features_hbm, features_ref.at[pl.ds(0, width), :]),
-        (tiles_hbm, tiles_ref),
-        (targets_hbm, targets_ref),
-        (weight_hbm, weight_ref),
-    )
-    extra = features_ref.shape[0] - width
-    features_ref[width:, :] = jnp.ones((extra, features_ref.shape[1]), bf16)
-    bands[...] = jnp.zeros_like(bands)
-    for copy in copies:
-        copy.wait()
-
-    def place(t, _):
-        at = pl.multiple_of(ids_ref[1, t] * rows, rows)
-        bands[ids_ref[0, t], :, pl.ds(at, rows)] = tiles_ref[t]
-        return 0
-
-    lax.fori_loop(0, tiles_ref.shape[0], place, 0, unroll=tiles_ref.shape[0] <= 16)
+        sems, (counts_hbm, counts_ref), (targets_hbm, targets_ref), (weight_hbm, weight_ref)
+    )
     for g in range(groups):
-        sums_ref[g] = dot(features_ref[...], bands[g], LAST)
-    band_ref[...] = bands[me]
+        sums_ref[g] = dot(table_ref[:high, :], bands_ref[g], LAST)
+    band_ref[...] = bands_ref[me_ref[0]]
     lane = lax.broadcasted_iota(jnp.int32, (slots, rows), 1)
     slot = lax.broadcasted_iota(jnp.int32, (slots, rows), 0)
     chips, chip, core = parts // 2, part_ref[0] // 2, part_ref[0] % 2
+    for copy in copies:
+        copy.wait()
 
     def connect(i, _):
         first = i * chunk
@@ -187,11 +197,11 @@
             for e in range(chunk):
                 n, d = e * groups + g, first + e
                 at = step_to(d // 2, chip, chips) * 2 + ((d % 2) ^ core)
-                hit = (target[:, n : n + 1] == lane) & (slot < counts_ref[g, first + e])
+                hit = (target[:, n : n + 1] == lane) & (slot < counts_ref[g, d])
                 values = jnp.where(hit, weight[:, n : n + 1], 0.0)
                 edges_ref[g, at] = values.astype(bf16)
                 degree = degree + jnp.sum(values, axis=0, keepdims=True)
-            sums_ref[g, width : width + 1, :] += degree
+            sums_ref[g, high - EXTRA : high - EXTRA + 1, :] += degree
         return 0
 
     if parts == chunk:
@@ -251,14 +261,21 @@
     out_ref[...] = total + dot(own_ref[...], weight_ref[span, :], FIRST)
 
 
-def hidden_kernel(me_ref, weight_ref, out_weight_ref, own_ref, *rest):
-    groups = (len(rest) - 1) // 2
-    parts, (hidden_ref, *copies) = rest[:groups], rest[groups:]
-    width = parts[0].shape[0]
-    total = own_ref[...]
-    for k, block in enumerate(parts):
-        span = rows_from(me_ref[0], groups, k, width)
-        total = total + dot(block[...], weight_ref[span, :], FIRST)
+def add_blocks(total, me, groups, first, blocks, weight_ref):
+    width = blocks[0].shape[0]
+    for k, block in enumerate(blocks, first):
+        total = total + dot(block[...], weight_ref[rows_from(me, groups, k, width), :], FIRST)
+    return total
+
+
+def early_kernel(groups, me_ref, weight_ref, own_ref, *rest):
+    blocks, out_ref = rest[:-1], rest[-1]
+    out_ref[...] = add_blocks(own_ref[...], me_ref[0], groups, 0, blocks, weight_ref)
+
+
+def hidden_kernel(groups, me_ref, weight_ref, out_weight_ref, early_ref, *rest):
+    blocks, (hidden_ref, *copies) = rest[: groups - 2], rest[groups - 2 :]
+    total = add_blocks(early_ref[...], me_ref[0], groups, 2, blocks, weight_ref)
     hidden = jnp.maximum(total, 0.0).astype(bf16)
     hidden_ref[...] = hidden
     projected = dot(out_weight_ref[...], hidden, LAST).astype(bf16)
@@ -369,20 +386,25 @@
 
     picked = min(chips, chunk)
     lanes = whole_lanes(width)
-    mine, mate, *feature_blocks = call(
+    table_rows = max(lanes, width + EXTRA)
+    mine, mate, table, bands, *feature_blocks = call(
         functools.partial(gather_kernel, picked),
-        (shape(chips, groups * slots, lanes),) * 2 + (shape(width, rows),) * (groups - 1),
-        [SM, SM, HB, HB],
+        (shape(chips, groups * slots, lanes),) * 2
+        + (shape(table_rows, nodes), shape(groups, rows, nodes))
+        + (shape(width, rows),) * (groups - 1),
+        [SM, SM, HB, HB, HB, HB],
         [
             pltpu.VMEM((parts, groups, slots), jnp.int32),
-            pltpu.VMEM((lanes, nodes), bf16),
+            pltpu.SMEM(tile_ids.shape[:0:-1], jnp.int32),
             pltpu.VMEM((picked, groups, slots), jnp.int32),
             pltpu.VMEM((picked * groups * slots, nodes), bf16),
-            pltpu.SemaphoreType.DMA((2,)),
+            pltpu.SemaphoreType.DMA((3,)),
+            pltpu.SemaphoreType.DMA((tile_contents.shape[0],)),
         ],
         2 * nodes * nodes * width,
         1 << 20,
-    )(me, part, sources[0], feature_rows)
+        4 if groups <= 4 else 16,
+    )(me, part, sources[0], tile_ids[0].T, feature_rows, tile_contents)
     mate = to_mate(mate)
     sums, edges, band = call(
         functools.partial(local_kernel, chunk),
@@ -391,30 +413,17 @@
             shape(groups, parts, slots, rows),
             shape(rows, nodes),
         ),
-        [SM, SM] + [HB] * 6,
+        [SM, SM, VM, VM] + [HB] * 3,
         [
-            pltpu.SMEM(tile_ids.shape[:0:-1], jnp.int32),
             pltpu.SMEM(counts.shape[:0:-1], jnp.int32),
-            pltpu.VMEM((width + EXTRA, nodes), bf16),
-            pltpu.VMEM(tile_contents.shape, bf16),
             pltpu.VMEM((parts, groups, slots), jnp.int32),
             pltpu.VMEM((parts, groups, slots), bf16),
-            pltpu.VMEM((groups, rows, nodes), bf16),
-            pltpu.SemaphoreType.DMA((6,)),
+            pltpu.SemaphoreType.DMA((3,)),
         ],
         2 * nodes * nodes * width,
         1 << 20,
         4 if groups <= 4 else 16,
-    )(
-        me,
-        part,
-        tile_ids[0].T,
-        counts[0].T,
-        feature_rows,
-        tile_contents,
-        targets[0],
-        edge_weight[0],
-    )
+    )(me, part, table, bands, counts[0].T, targets[0], edge_weight[0])
     paired = call(
         pair_kernel,
         (shape(2, groups * slots, lanes),) * chips + (shape(width, rows),) * (groups - 1),
@@ -442,14 +451,22 @@
         2 * rows * hid * groups * width,
         2 << 20,
     )(me, feature_rows, self_one, *feature_blocks)
+    early = call(
+        functools.partial(early_kernel, groups),
+        shape(rows, hid, dtype=f32),
+        [SM] + [VM] * 4,
+        (),
+        rows * hid * groups * width,
+        2 << 20,
+    )(me, neigh_one, own, *means[:2])
     hidden, *projected = call(
-        hidden_kernel,
+        functools.partial(hidden_kernel, groups),
         (shape(rows, hid),) + (shape(classes, rows),) * groups,
-        [SM] + [VM] * (3 + groups),
-        (),
-        2 * rows * hid * groups * width,
+        [SM] + [VM] * (1 + groups),
+        (),
+        rows * hid * groups * width,
         2 << 20,
-    )(me, neigh_one, neigh_out.T, own, *means)
+    )(me, neigh_one, neigh_out.T, early, *means[2:])
     hits = call(
         hits_kernel,
         shape(parts * slots, nodes),

time: 39.1 us -> 39.1 us (level)
    pallas_call x12 -> x13, Pallas kernels: 8.33 us -> 8.56 us  [placed(): run(*(pltpu.with_memory_space_constraint(value, pltpu.HBM) if spec is HB...]
where the time goes in v14:
time: 39.1 us; the launch traced here: 38.7 us
  starting transfers between devices  21.7 us (55%)
  Pallas kernels  8.56 us (22%)
  waiting for transfers between devices  7.63 us (20%)
  between operations  0.78 us (2%)
    ppermute x9, starting transfers between devices, shift(): lax.ppermute(block, 'feat', [(i, ahead(i, groups, k, near)) for i in rang...  13.5 us
    pallas_call x13, Pallas kernels, placed(): run(*(pltpu.with_memory_space_constraint(value, pltpu.HBM) if spec is HB...  8.56 us
    ppermute x6, starting transfers between devices, to_chips(): lax.ppermute(blocks[j], 'dom', [(d, next_to(d // 2, j, chips) * 2 + d % 2...  7.68 us
    ppermute x9, waiting for transfers between devices, shift(): lax.ppermute(block, 'feat', [(i, ahead(i, groups, k, near)) for i in rang...  4.26 us
    ppermute x6, waiting for transfers between devices, to_chips(): lax.ppermute(blocks[j], 'dom', [(d, next_to(d // 2, j, chips) * 2 + d % 2...  2.18 us
    ppermute x2, waiting for transfers between devices, to_mate(): return lax.ppermute(value, 'dom', [(d, d ^ 1) for d in range(parts)])  1.2 us
  transfers between devices with their start and end apart: 17, of which 9 were waited for; matrix products, arithmetic and copies ran while one was open for 0% of the time, Pallas kernels for 13%

profile of v14, /device:TPU:0, one launch (start us, length us, event | category | flops | bytes accessed | tf_op | source)
XLA Modules:
  0.0 38.7 jit_solution(2058675796387802274)
XLA Ops:
  0.6 0.0 copy-start.1
  0.6 1.9 %shard_map.122 = (bf16[4,64,256]{2,1,0:T(8,128)(2,1)S(1)}, bf16[4,64,256]{2,1,0:T(8,128)(2,1)S(1)}, bf16[256,512]{1,0:T(8,128)(2,1)S(1)}, bf16[4,128,512]{2,1,0:...) custom-call(s32[1]{0:T(128)} %bitcast.me_ref, ...), custom_call_target="tpu_custom_call" | custom-call | flops 100663296 | bytes 1048576 | tf_op jit(solution)/shard_map/pallas_call | solution.py:32
  2.6 0.5 %collective-permute-start = (bf16[4,64,256]{2,1,0:T(8,128)(2,1)S(1)}, bf16[4,64,256]{2,1,0:T(8,128)(2,1)S(1)}, u32[]{:S(2)}, u32[]{:S(2)}) collective-permute-start(bf16[4,64,256]{2,1,0:T(8,128)(2,1)S(1)} %get-tuple-element.40), channel_id=1, source_target_pairs={{0,1},{1,0},{2,3},{3,2},{4,5},{5,4},{6,7},{7,6},{8,9},{9,8},{10,11... | collective-permute-start | bytes 393224 | tf_op jit(solution)/shard_map/ppermute | solution.py:375
  3.1 1.3 %shard_map.123 = (f32[4,208,128]{2,1,0:T(8,128)S(1)}, bf16[4,8,16,128]{3,2,1,0:T(8,128)(2,1)S(1)}, bf16[128,512]{1,0:T(8,128)(2,1)S(1)}) custom-call(s32[1]{0:T(128)} %bitcast.me_ref, s32[1]{0:T(128)} %bitcast.4.part_ref, bf16[256,512]{1,0:T(8,128)(2,1)S(1)} %get-tuple-element.36.table_ref, bf16[4,128,512]{2,1,0:T(8,128)(2,1)S(1)} %get-tuple-element.37.bands_ref, ...), custom_call_target="tpu_custom_call" | custom-call | flops 100663296 | bytes 1048576 | tf_op jit(solution)/shard_map/pallas_call | solution.py:32
  4.4 0.0 collective-permute-done.got_ref
  4.4 3.5 %collective-permute-start.4 = (bf16[2,64,256]{2,1,0:T(8,128)(2,1)S(1)}, bf16[2,64,256]{2,1,0:T(8,128)(2,1)S(1)}, u32[]{:S(2)}, u32[]{:S(2)}) collective-permute-start(bf16[2,64,256]{2,1,0:T(8,128)(2,1)S(1)} %get-tuple-element.50), channel_id=1, source_target_pairs={{0,6},{1,7},{2,4},{3,5},{4,2},{5,3},{6,0},{7,1},{8,14},{9,15},{10,... | collective-permute-start | bytes 196616 | tf_op jit(solution)/shard_map/ppermute | solution.py:379
  8.0 0.5 %collective-permute-start.5 = (bf16[2,64,256]{2,1,0:T(8,128)(2,1)S(1)}, bf16[2,64,256]{2,1,0:T(8,128)(2,1)S(1)}, u32[]{:S(2)}, u32[]{:S(2)}) collective-permute-start(bf16[2,64,256]{2,1,0:T(8,128)(2,1)S(1)} %get-tuple-element.51), channel_id=1, source_target_pairs={{0,4},{1,5},{2,6},{3,7},{4,0},{5,1},{6,2},{7,3},{8,12},{9,13},{10,... | collective-permute-start | bytes 196616 | tf_op jit(solution)/shard_map/ppermute | solution.py:379
  8.5 0.1 collective-permute-start.6
  8.6 3.0 %collective-permute-start.1 = (bf16[192,128]{1,0:T(8,128)(2,1)S(1)}, bf16[192,128]{1,0:T(8,128)(2,1)S(1)}, u32[]{:S(2)}, u32[]{:S(2)}) collective-permute-start(bf16[192,128]{1,0:T(8,128)(2,1)S(1)} %get-tuple-element.44), channel_id=1, source_target_pairs={{0,16},{8,24},{16,0},{24,8},{1,17},{9,25},{17,1},{25,9},{2,18},{10... | collective-permute-start | bytes 147464 | tf_op jit(solution)/shard_map/ppermute | solution.py:370
  11.6 1.3 %collective-permute-start.2 = (bf16[192,128]{1,0:T(8,128)(2,1)S(1)}, bf16[192,128]{1,0:T(8,128)(2,1)S(1)}, u32[]{:S(2)}, u32[]{:S(2)}) collective-permute-start(bf16[192,128]{1,0:T(8,128)(2,1)S(1)} %get-tuple-element.45), channel_id=1, source_target_pairs={{0,24},{8,16},{16,8},{24,0},{1,25},{9,17},{17,9},{25,1},{2,26},{10... | collective-permute-start | bytes 147464 | tf_op jit(solution)/shard_map/ppermute | solution.py:370
  13.0 0.0 collective-permute-done.4.rest_1_
  13.0 0.2 collective-permute-start.3
  13.2 0.0 collective-permute-done.5.rest_2_
  13.2 0.0 collective-permute-done.6.rest_3_
  13.2 0.3 shard_map.126
  13.5 3.2 %collective-permute-start.7 = (bf16[192,128]{1,0:T(8,128)(2,1)S(1)}, bf16[192,128]{1,0:T(8,128)(2,1)S(1)}, u32[]{:S(2)}, u32[]{:S(2)}) collective-permute-start(bf16[192,128]{1,0:T(8,128)(2,1)S(1)} %get-tuple-element.54), channel_id=1, source_target_pairs={{0,24},{8,16},{16,8},{24,0},{1,25},{9,17},{17,9},{25,1},{2,26},{10... | collective-permute-start | bytes 147464 | tf_op jit(solution)/shard_map/ppermute | solution.py:370
  16.7 0.1 collective-permute-start.8
  16.8 0.0 collective-permute-done.1.rest_0_
  16.8 1.1 %collective-permute-start.9 = (bf16[192,128]{1,0:T(8,128)(2,1)S(1)}, bf16[192,128]{1,0:T(8,128)(2,1)S(1)}, u32[]{:S(2)}, u32[]{:S(2)}) collective-permute-start(bf16[192,128]{1,0:T(8,128)(2,1)S(1)} %get-tuple-element.56), channel_id=1, source_target_pairs={{0,8},{8,0},{16,24},{24,16},{1,9},{9,1},{17,25},{25,17},{2,10},{10... | collective-permute-start | bytes 147464 | tf_op jit(solution)/shard_map/ppermute | solution.py:370
  17.9 0.2 collective-permute-done.2.rest_1_
  18.1 0.0 collective-permute-done.3.rest_2_
  18.1 1.2 %shard_map.125.own_ref = f32[128,1024]{1,0:T(8,128)S(1)} custom-call(s32[1]{0:T(128)} %bitcast.me_ref, bf16[192,512]{1,0:T(8,128)(2,1)} %bitcast.22, bf16[768,1024]{1,0:T(8,128)(2,1)S(1)} %copy-done.1, bf16[192,128]{1,0:T(8,128)(2,1)S(1)} %collective-permute-done.1.rest_0_, bf16[192,128]{1,0:T(8,128)(2,1)S(1)} %collective-permute-done.2.rest_1_, ...), custom_call_target="tpu_custom_call" | custom-call | flops 201326592 | bytes 2097152 | tf_op jit(solution)/shard_map/pallas_call | solution.py:32
  19.3 0.0 copy-start.3
  19.3 0.3 collective-permute-done.7.rest_1_
  19.7 0.0 copy-done
  19.7 0.3 shard_map.127.early_ref
  20.0 1.9 %collective-permute-done.8.rest_0_ = bf16[192,128]{1,0:T(8,128)(2,1)S(1)} collective-permute-done((bf16[192,128]{1,0:T(8,128)(2,1)S(1)}, bf16[192,128]{1,0:T(8,128)(2,1)S(1)}, u32[]{:S(2)}, u32[]{:S(2)}) %collective-permute-start.8) | collective-permute-done | bytes 49184 | tf_op jit(solution)/shard_map/ppermute | solution.py:370
  21.9 0.0 collective-permute-done.9.rest_1_
  21.9 0.5 %shard_map.128 = (bf16[128,1024]{1,0:T(8,128)(2,1)S(1)}, bf16[153,128]{1,0:T(8,128)(2,1)S(1)}, bf16[153,128]{1,0:T(8,128)(2,1)S(1)}, bf16[153,128]{1,0:T(8,128)(2,1)S(1)}, bf16[153,128]{1,0:T(8,128)(2,1)S(1)}) custom-call(s32[1]{0:T(128)} %bitcast.me_ref, bf16[768,1024]{1,0:T(8,128)(2,1)S(1)} %copy-done, bf16[153,1024]{1,0:T(8,128)(2,1)S(1)} %bitcast.20, ...), custom_call_target="tpu_custom_call" | custom-call | flops 100663296 | bytes 2097152 | tf_op jit(solution)/shard_map/pallas_call | solution.py:32
  22.4 2.4 %collective-permute-start.10 = (bf16[153,128]{1,0:T(8,128)(2,1)S(1)}, bf16[153,128]{1,0:T(8,128)(2,1)S(1)}, u32[]{:S(2)}, u32[]{:S(2)}) collective-permute-start(bf16[153,128]{1,0:T(8,128)(2,1)S(1)} %get-tuple-element.61), channel_id=1, source_target_pairs={{0,24},{8,16},{16,8},{24,0},{1,25},{9,17},{17,9},{25,1},{2,26},{10... | collective-permute-start | bytes 117512 | tf_op jit(solution)/shard_map/ppermute | solution.py:370
  24.8 0.0 collective-permute-start.11
  24.8 2.1 %collective-permute-start.12 = (bf16[153,128]{1,0:T(8,128)(2,1)S(1)}, bf16[153,128]{1,0:T(8,128)(2,1)S(1)}, u32[]{:S(2)}, u32[]{:S(2)}) collective-permute-start(bf16[153,128]{1,0:T(8,128)(2,1)S(1)} %get-tuple-element.63), channel_id=1, source_target_pairs={{0,8},{8,0},{16,24},{24,16},{1,9},{9,1},{17,25},{25,17},{2,10},{10... | collective-permute-start | bytes 117512 | tf_op jit(solution)/shard_map/ppermute | solution.py:370
  26.9 0.9 %shard_map.131.hits_ref.after = bf16[128,512]{1,0:T(8,128)(2,1)S(1)} custom-call(bf16[153,128]{1,0:T(8,128)(2,1)S(1)} %get-tuple-element.60.rest_0_.after, s32[1]{0:T(128)} %bitcast.me_ref, s32[1]{0:T(128)} %bitcast.4.part_ref, s32[8,4,16]{2,1,0:T(4,128)} %bitcast.26), custom_call_target="tpu_custom_call" | custom-call | bytes 524288 | tf_op jit(solution)/shard_map/pallas_call | solution.py:32
  27.8 0.7 %collective-permute-done.10.rest_1_ = bf16[153,128]{1,0:T(8,128)(2,1)S(1)} collective-permute-done((bf16[153,128]{1,0:T(8,128)(2,1)S(1)}, bf16[153,128]{1,0:T(8,128)(2,1)S(1)}, u32[]{:S(2)}, u32[]{:S(2)}) %collective-permute-start.10) | collective-permute-done | bytes 39200 | tf_op jit(solution)/shard_map/ppermute | solution.py:370
  28.5 1.2 %collective-permute-done.11.rest_2_ = bf16[153,128]{1,0:T(8,128)(2,1)S(1)} collective-permute-done((bf16[153,128]{1,0:T(8,128)(2,1)S(1)}, bf16[153,128]{1,0:T(8,128)(2,1)S(1)}, u32[]{:S(2)}, u32[]{:S(2)}) %collective-permute-start.11) | collective-permute-done | bytes 39200 | tf_op jit(solution)/shard_map/ppermute | solution.py:370
  29.7 0.0 collective-permute-done.12.rest_3_
  29.7 0.3 shard_map.132
  30.0 0.1 collective-permute-start.13
  30.0 1.2 %collective-permute-done.13.got_ref = bf16[4,16,256]{2,1,0:T(8,128)(2,1)S(1)} collective-permute-done((bf16[4,16,256]{2,1,0:T(8,128)(2,1)S(1)}, bf16[4,16,256]{2,1,0:T(8,128)(2,1)S(1)}, u32[]{:S(2)}, u32[]{:S(2)}) %collective-permute-start.13) | collective-permute-done | bytes 32800 | tf_op jit(solution)/shard_map/ppermute | solution.py:375
  31.2 2.5 %collective-permute-start.14 = (bf16[2,16,256]{2,1,0:T(8,128)(2,1)S(1)}, bf16[2,16,256]{2,1,0:T(8,128)(2,1)S(1)}, u32[]{:S(2)}, u32[]{:S(2)}) collective-permute-start(bf16[2,16,256]{2,1,0:T(8,128)(2,1)S(1)} %get-tuple-element.67), channel_id=1, source_target_pairs={{0,6},{1,7},{2,4},{3,5},{4,2},{5,3},{6,0},{7,1},{8,14},{9,15},{10,... | collective-permute-start | bytes 49160 | tf_op jit(solution)/shard_map/ppermute | solution.py:379
  33.8 0.3 collective-permute-start.15
  34.1 0.6 %collective-permute-start.16 = (bf16[2,16,256]{2,1,0:T(8,128)(2,1)S(1)}, bf16[2,16,256]{2,1,0:T(8,128)(2,1)S(1)}, u32[]{:S(2)}, u32[]{:S(2)}) collective-permute-start(bf16[2,16,256]{2,1,0:T(8,128)(2,1)S(1)} %get-tuple-element.69), channel_id=1, source_target_pairs={{0,2},{1,3},{2,0},{3,1},{4,6},{5,7},{6,4},{7,5},{8,10},{9,11},{10,... | collective-permute-start | bytes 49160 | tf_op jit(solution)/shard_map/ppermute | solution.py:379
  34.7 0.7 %shard_map.129 = (f32[153,128]{1,0:T(8,128)S(1)}, bf16[128,1024]{1,0:T(8,128)(2,1)}) custom-call(bf16[128,1024]{1,0:T(8,128)(2,1)S(1)} %get-tuple-element.57.hidden_ref, bf16[153,1024]{1,0:T(8,128)(2,1)S(1)} %bitcast.19), custom_call_target="tpu_custom_call" | custom-call | flops 40108032 | bytes 1048576 | tf_op jit(solution)/shard_map/pallas_call | solution.py:32
  35.5 0.2 shard_map.130.near_ref
  35.7 0.2 collective-permute-done.14.rest_1_
  35.9 1.6 %collective-permute-done.15.rest_2_ = bf16[2,16,256]{2,1,0:T(8,128)(2,1)S(1)} collective-permute-done((bf16[2,16,256]{2,1,0:T(8,128)(2,1)S(1)}, bf16[2,16,256]{2,1,0:T(8,128)(2,1)S(1)}, u32[]{:S(2)}, u32[]{:S(2)}) %collective-permute-start.15) | collective-permute-done | bytes 16416 | tf_op jit(solution)/shard_map/ppermute | solution.py:379
  37.5 0.3 collective-permute-done.16.rest_3_
  37.9 0.9 %shard_map.134 = f32[153,1,128]{2,1,0:T(1,128)} custom-call(s32[1]{0:T(128)} %bitcast.me_ref, f32[153,128]{1,0:T(8,128)S(1)} %shard_map.130.near_ref, bf16[4,8,16,128]{3,2,1,0:T(8,128)(2,1)S(1)} %get-tuple-element.48.edges_ref, f32[4,208,128]{2,1,0:T(8,128)S(1)} %get-tuple-element.47.sums_ref, bf16[2,16,256]{2,1,0:T(8,128)(2,1)S(1)} %get-tuple-element.66.rest_0_, ...), custom_call_target="tpu_custom_call" | custom-call | flops 5013504 | bytes 524288 | tf_op jit(solution)/shard_map/pallas_call | solution.py:32
  (7 shorter events, 0.0 us)
Async XLA Ops:
  0.6 17.5 %copy-start.1 = (bf16[768,1024]{1,0:T(8,128)(2,1)S(1)}, bf16[768,1024]{1,0:T(8,128)(2,1)}, u32[]{:S(2)}) copy-start(bf16[768,1024]{1,0:T(8,128)(2,1)} %weight_ref.3) | copy-start | bytes 4718596
  2.6 1.8 %collective-permute-start = (bf16[4,64,256]{2,1,0:T(8,128)(2,1)S(1)}, bf16[4,64,256]{2,1,0:T(8,128)(2,1)S(1)}, u32[]{:S(2)}, u32[]{:S(2)}) collective-permute-start(bf16[4,64,256]{2,1,0:T(8,128)(2,1)S(1)} %get-tuple-element.40), channel_id=1, source_target_pairs={{0,1},{1,0},{2,3},{3,2},{4,5},{5,4},{6,7},{7,6},{8,9},{9,8},{10,11... | collective-permute-start | bytes 393224 | tf_op jit(solution)/shard_map/ppermute | solution.py:375
  4.4 8.5 %collective-permute-start.4 = (bf16[2,64,256]{2,1,0:T(8,128)(2,1)S(1)}, bf16[2,64,256]{2,1,0:T(8,128)(2,1)S(1)}, u32[]{:S(2)}, u32[]{:S(2)}) collective-permute-start(bf16[2,64,256]{2,1,0:T(8,128)(2,1)S(1)} %get-tuple-element.50), channel_id=1, source_target_pairs={{0,6},{1,7},{2,4},{3,5},{4,2},{5,3},{6,0},{7,1},{8,14},{9,15},{10,... | collective-permute-start | bytes 196616 | tf_op jit(solution)/shard_map/ppermute | solution.py:379
  8.0 5.2 %collective-permute-start.5 = (bf16[2,64,256]{2,1,0:T(8,128)(2,1)S(1)}, bf16[2,64,256]{2,1,0:T(8,128)(2,1)S(1)}, u32[]{:S(2)}, u32[]{:S(2)}) collective-permute-start(bf16[2,64,256]{2,1,0:T(8,128)(2,1)S(1)} %get-tuple-element.51), channel_id=1, source_target_pairs={{0,4},{1,5},{2,6},{3,7},{4,0},{5,1},{6,2},{7,3},{8,12},{9,13},{10,... | collective-permute-start | bytes 196616 | tf_op jit(solution)/shard_map/ppermute | solution.py:379
  8.5 4.7 %collective-permute-start.6 = (bf16[2,64,256]{2,1,0:T(8,128)(2,1)S(1)}, bf16[2,64,256]{2,1,0:T(8,128)(2,1)S(1)}, u32[]{:S(2)}, u32[]{:S(2)}) collective-permute-start(bf16[2,64,256]{2,1,0:T(8,128)(2,1)S(1)} %get-tuple-element.52), channel_id=1, source_target_pairs={{0,2},{1,3},{2,0},{3,1},{4,6},{5,7},{6,4},{7,5},{8,10},{9,11},{10,... | collective-permute-start | bytes 196616 | tf_op jit(solution)/shard_map/ppermute | solution.py:379
  8.6 8.2 %collective-permute-start.1 = (bf16[192,128]{1,0:T(8,128)(2,1)S(1)}, bf16[192,128]{1,0:T(8,128)(2,1)S(1)}, u32[]{:S(2)}, u32[]{:S(2)}) collective-permute-start(bf16[192,128]{1,0:T(8,128)(2,1)S(1)} %get-tuple-element.44), channel_id=1, source_target_pairs={{0,16},{8,24},{16,0},{24,8},{1,17},{9,25},{17,1},{25,9},{2,18},{10... | collective-permute-start | bytes 147464 | tf_op jit(solution)/shard_map/ppermute | solution.py:370
  11.6 6.5 %collective-permute-start.2 = (bf16[192,128]{1,0:T(8,128)(2,1)S(1)}, bf16[192,128]{1,0:T(8,128)(2,1)S(1)}, u32[]{:S(2)}, u32[]{:S(2)}) collective-permute-start(bf16[192,128]{1,0:T(8,128)(2,1)S(1)} %get-tuple-element.45), channel_id=1, source_target_pairs={{0,24},{8,16},{16,8},{24,0},{1,25},{9,17},{17,9},{25,1},{2,26},{10... | collective-permute-start | bytes 147464 | tf_op jit(solution)/shard_map/ppermute | solution.py:370
  13.0 5.1 %collective-permute-start.3 = (bf16[192,128]{1,0:T(8,128)(2,1)S(1)}, bf16[192,128]{1,0:T(8,128)(2,1)S(1)}, u32[]{:S(2)}, u32[]{:S(2)}) collective-permute-start(bf16[192,128]{1,0:T(8,128)(2,1)S(1)} %get-tuple-element.46), channel_id=1, source_target_pairs={{0,8},{8,0},{16,24},{24,16},{1,9},{9,1},{17,25},{25,17},{2,10},{10... | collective-permute-start | bytes 147464 | tf_op jit(solution)/shard_map/ppermute | solution.py:370
  13.2 6.5 %copy-start = (bf16[768,1024]{1,0:T(8,128)(2,1)S(1)}, bf16[768,1024]{1,0:T(8,128)(2,1)}, u32[]{:S(2)}) copy-start(bf16[768,1024]{1,0:T(8,128)(2,1)} %weight_ref.5) | copy-start | bytes 4718596
  13.5 6.2 %collective-permute-start.7 = (bf16[192,128]{1,0:T(8,128)(2,1)S(1)}, bf16[192,128]{1,0:T(8,128)(2,1)S(1)}, u32[]{:S(2)}, u32[]{:S(2)}) collective-permute-start(bf16[192,128]{1,0:T(8,128)(2,1)S(1)} %get-tuple-element.54), channel_id=1, source_target_pairs={{0,24},{8,16},{16,8},{24,0},{1,25},{9,17},{17,9},{25,1},{2,26},{10... | collective-permute-start | bytes 147464 | tf_op jit(solution)/shard_map/ppermute | solution.py:370
  16.7 5.2 %collective-permute-start.8 = (bf16[192,128]{1,0:T(8,128)(2,1)S(1)}, bf16[192,128]{1,0:T(8,128)(2,1)S(1)}, u32[]{:S(2)}, u32[]{:S(2)}) collective-permute-start(bf16[192,128]{1,0:T(8,128)(2,1)S(1)} %get-tuple-element.55), channel_id=1, source_target_pairs={{0,16},{8,24},{16,0},{24,8},{1,17},{9,25},{17,1},{25,9},{2,18},{10... | collective-permute-start | bytes 147464 | tf_op jit(solution)/shard_map/ppermute | solution.py:370
  16.8 5.1 %collective-permute-start.9 = (bf16[192,128]{1,0:T(8,128)(2,1)S(1)}, bf16[192,128]{1,0:T(8,128)(2,1)S(1)}, u32[]{:S(2)}, u32[]{:S(2)}) collective-permute-start(bf16[192,128]{1,0:T(8,128)(2,1)S(1)} %get-tuple-element.56), channel_id=1, source_target_pairs={{0,8},{8,0},{16,24},{24,16},{1,9},{9,1},{17,25},{25,17},{2,10},{10... | collective-permute-start | bytes 147464 | tf_op jit(solution)/shard_map/ppermute | solution.py:370
  19.3 2.5 %copy-start.3 = (bf16[1024,153]{0,1:T(8,128)(2,1)S(1)}, bf16[1024,153]{0,1:T(8,128)(2,1)}, u32[]{:S(2)}) copy-start(bf16[1024,153]{0,1:T(8,128)(2,1)} %param.21) | copy-start | bytes 940036
  21.9 12.9 %copy-start.2 = (bf16[1024,153]{0,1:T(8,128)(2,1)S(1)}, bf16[1024,153]{0,1:T(8,128)(2,1)}, u32[]{:S(2)}) copy-start(bf16[1024,153]{0,1:T(8,128)(2,1)} %param.20) | copy-start | bytes 940036
  22.4 6.0 %collective-permute-start.10 = (bf16[153,128]{1,0:T(8,128)(2,1)S(1)}, bf16[153,128]{1,0:T(8,128)(2,1)S(1)}, u32[]{:S(2)}, u32[]{:S(2)}) collective-permute-start(bf16[153,128]{1,0:T(8,128)(2,1)S(1)} %get-tuple-element.61), channel_id=1, source_target_pairs={{0,24},{8,16},{16,8},{24,0},{1,25},{9,17},{17,9},{25,1},{2,26},{10... | collective-permute-start | bytes 117512 | tf_op jit(solution)/shard_map/ppermute | solution.py:370
  24.8 4.9 %collective-permute-start.11 = (bf16[153,128]{1,0:T(8,128)(2,1)S(1)}, bf16[153,128]{1,0:T(8,128)(2,1)S(1)}, u32[]{:S(2)}, u32[]{:S(2)}) collective-permute-start(bf16[153,128]{1,0:T(8,128)(2,1)S(1)} %get-tuple-element.62), channel_id=1, source_target_pairs={{0,16},{8,24},{16,0},{24,8},{1,17},{9,25},{17,1},{25,9},{2,18},{10... | collective-permute-start | bytes 117512 | tf_op jit(solution)/shard_map/ppermute | solution.py:370
  24.8 4.9 %collective-permute-start.12 = (bf16[153,128]{1,0:T(8,128)(2,1)S(1)}, bf16[153,128]{1,0:T(8,128)(2,1)S(1)}, u32[]{:S(2)}, u32[]{:S(2)}) collective-permute-start(bf16[153,128]{1,0:T(8,128)(2,1)S(1)} %get-tuple-element.63), channel_id=1, source_target_pairs={{0,8},{8,0},{16,24},{24,16},{1,9},{9,1},{17,25},{25,17},{2,10},{10... | collective-permute-start | bytes 117512 | tf_op jit(solution)/shard_map/ppermute | solution.py:370
  30.0 1.3 %collective-permute-start.13 = (bf16[4,16,256]{2,1,0:T(8,128)(2,1)S(1)}, bf16[4,16,256]{2,1,0:T(8,128)(2,1)S(1)}, u32[]{:S(2)}, u32[]{:S(2)}) collective-permute-start(bf16[4,16,256]{2,1,0:T(8,128)(2,1)S(1)} %get-tuple-element.65), channel_id=1, source_target_pairs={{0,1},{1,0},{2,3},{3,2},{4,5},{5,4},{6,7},{7,6},{8,9},{9,8},{10,11... | collective-permute-start | bytes 98312 | tf_op jit(solution)/shard_map/ppermute | solution.py:375
  31.2 4.6 %collective-permute-start.14 = (bf16[2,16,256]{2,1,0:T(8,128)(2,1)S(1)}, bf16[2,16,256]{2,1,0:T(8,128)(2,1)S(1)}, u32[]{:S(2)}, u32[]{:S(2)}) collective-permute-start(bf16[2,16,256]{2,1,0:T(8,128)(2,1)S(1)} %get-tuple-element.67), channel_id=1, source_target_pairs={{0,6},{1,7},{2,4},{3,5},{4,2},{5,3},{6,0},{7,1},{8,14},{9,15},{10,... | collective-permute-start | bytes 49160 | tf_op jit(solution)/shard_map/ppermute | solution.py:379
  33.8 3.7 %collective-permute-start.15 = (bf16[2,16,256]{2,1,0:T(8,128)(2,1)S(1)}, bf16[2,16,256]{2,1,0:T(8,128)(2,1)S(1)}, u32[]{:S(2)}, u32[]{:S(2)}) collective-permute-start(bf16[2,16,256]{2,1,0:T(8,128)(2,1)S(1)} %get-tuple-element.68), channel_id=1, source_target_pairs={{0,4},{1,5},{2,6},{3,7},{4,0},{5,1},{6,2},{7,3},{8,12},{9,13},{10,... | collective-permute-start | bytes 49160 | tf_op jit(solution)/shard_map/ppermute | solution.py:379
  34.1 3.7 %collective-permute-start.16 = (bf16[2,16,256]{2,1,0:T(8,128)(2,1)S(1)}, bf16[2,16,256]{2,1,0:T(8,128)(2,1)S(1)}, u32[]{:S(2)}, u32[]{:S(2)}) collective-permute-start(bf16[2,16,256]{2,1,0:T(8,128)(2,1)S(1)} %get-tuple-element.69), channel_id=1, source_target_pairs={{0,2},{1,3},{2,0},{3,1},{4,6},{5,7},{6,4},{7,5},{8,10},{9,11},{10,... | collective-permute-start | bytes 49160 | tf_op jit(solution)/shard_map/ppermute | solution.py:379

commit v15 on v14

--- a/solution.py
+++ b/solution.py
@@ -15,6 +15,7 @@
 LAST = (((1,), (1,)), ((), ()))
 FIRST = (((0,), (0,)), ((), ()))
 EXTRA = 16
+PASSED = 5
 
 
 def call(kernel, out_shape, in_specs, scratch=(), flops=0, size=0, limit=4, out_specs=None):
@@ -89,44 +90,28 @@
     me_ref,
     part_ref,
     sources_hbm,
-    ids_hbm,
     features_hbm,
-    tiles_hbm,
-    mine_ref,
-    mate_ref,
-    table_ref,
-    bands_ref,
     *rest,
 ):
-    blocks, (sources_ref, ids_ref, order, hits, sems, tile_sems) = rest[:-6], rest[-6:]
+    extras, (mine_ref, mate_ref, table_ref, *outs) = rest[:PASSED], rest[PASSED:]
+    passed, blocks = outs[:PASSED], outs[PASSED:-4]
+    sources_ref, order, hits, sems = outs[-4:]
     parts, groups, slots = sources_ref.shape
-    tiles, rows = tiles_hbm.shape[:2]
     width, nodes = features_hbm.shape
+    rows = nodes // groups
     lanes = mine_ref.shape[2]
     chips, chip, core = parts // 2, part_ref[0] // 2, part_ref[0] % 2
-    indices, ids, table = fetch(
+    indices, table, *others = fetch(
         sems,
         (sources_hbm, sources_ref),
-        (ids_hbm, ids_ref),
         (features_hbm, table_ref.at[pl.ds(0, width), :]),
+        *zip(extras, passed),
     )
     table_ref[width : width + EXTRA, :] = jnp.ones((EXTRA, nodes), bf16)
     if table_ref.shape[0] > width + EXTRA:
         table_ref[width + EXTRA :, :] = jnp.zeros(
             (table_ref.shape[0] - width - EXTRA, nodes), bf16
         )
-    bands_ref[...] = jnp.zeros_like(bands_ref)
-
-    def tile_copy(t):
-        at = pl.multiple_of(ids_ref[1, t] * rows, rows)
-        to = bands_ref.at[ids_ref[0, t], :, pl.ds(at, rows)]
-        return pltpu.make_async_copy(tiles_hbm.at[t], to, tile_sems.at[t])
-
-    def each_tile(run):
-        lax.fori_loop(0, tiles, lambda t, _: run(tile_copy(t)), None, unroll=tiles <= 16)
-
-    ids.wait()
-    each_tile(lambda copy: copy.start())
     indices.wait()
     lane = lax.broadcasted_iota(jnp.int32, (slots, nodes), 1)
 
@@ -153,7 +138,8 @@
     for k in range(1, groups):
         group = ahead(me_ref[0], groups, k, True)
         blocks[k - 1][...] = table_ref[:width, pl.ds(pl.multiple_of(group * rows, rows), rows)]
-    each_tile(lambda copy: copy.wait())
+    for copy in others:
+        copy.wait()
 
 
 def local_kernel(
@@ -161,32 +147,39 @@
     me_ref,
     part_ref,
     table_ref,
-    bands_ref,
-    counts_hbm,
-    targets_hbm,
-    weight_hbm,
+    tiles_ref,
+    targets_ref,
+    weight_ref,
+    ids_vmem,
+    counts_vmem,
     sums_ref,
     edges_ref,
     band_ref,
+    ids_ref,
     counts_ref,
-    targets_ref,
-    weight_ref,
+    bands_ref,
     sems,
 ):
     parts, groups, slots = targets_ref.shape
     rows = edges_ref.shape[3]
     high = sums_ref.shape[1]
-    copies = fetch(
-        sems, (counts_hbm, counts_ref), (targets_hbm, targets_ref), (weight_hbm, weight_ref)
-    )
+    copies = fetch(sems, (ids_vmem, ids_ref), (counts_vmem, counts_ref))
+    bands_ref[...] = jnp.zeros_like(bands_ref)
+    for copy in copies:
+        copy.wait()
+
+    def place(t, _):
+        at = pl.multiple_of(ids_ref[1, t] * rows, rows)
+        bands_ref[ids_ref[0, t], :, pl.ds(at, rows)] = tiles_ref[t]
+        return 0
+
+    lax.fori_loop(0, tiles_ref.shape[0], place, 0, unroll=tiles_ref.shape[0] <= 16)
     for g in range(groups):
         sums_ref[g] = dot(table_ref[:high, :], bands_ref[g], LAST)
     band_ref[...] = bands_ref[me_ref[0]]
     lane = lax.broadcasted_iota(jnp.int32, (slots, rows), 1)
     slot = lax.broadcasted_iota(jnp.int32, (slots, rows), 0)
     chips, chip, core = parts // 2, part_ref[0] // 2, part_ref[0] % 2
-    for copy in copies:
-        copy.wait()
 
     def connect(i, _):
         first = i * chunk
@@ -387,24 +380,24 @@
     picked = min(chips, chunk)
     lanes = whole_lanes(width)
     table_rows = max(lanes, width + EXTRA)
-    mine, mate, table, bands, *feature_blocks = call(
+    extras = (tile_contents, targets[0], edge_weight[0], tile_ids[0].T, counts[0].T)
+    mine, mate, table, *rest = call(
         functools.partial(gather_kernel, picked),
         (shape(chips, groups * slots, lanes),) * 2
-        + (shape(table_rows, nodes), shape(groups, rows, nodes))
+        + (shape(table_rows, nodes),)
+        + tuple(shape(*value.shape, dtype=value.dtype) for value in extras)
         + (shape(width, rows),) * (groups - 1),
-        [SM, SM, HB, HB, HB, HB],
+        [SM, SM, HB, HB] + [HB] * PASSED,
         [
             pltpu.VMEM((parts, groups, slots), jnp.int32),
-            pltpu.SMEM(tile_ids.shape[:0:-1], jnp.int32),
             pltpu.VMEM((picked, groups, slots), jnp.int32),
             pltpu.VMEM((picked * groups * slots, nodes), bf16),
-            pltpu.SemaphoreType.DMA((3,)),
-            pltpu.SemaphoreType.DMA((tile_contents.shape[0],)),
+            pltpu.SemaphoreType.DMA((2 + PASSED,)),
         ],
         2 * nodes * nodes * width,
         1 << 20,
-        4 if groups <= 4 else 16,
-    )(me, part, sources[0], tile_ids[0].T, feature_rows, tile_contents)
+    )(me, part, sources[0], feature_rows, *extras)
+    passed, feature_blocks = rest[:PASSED], rest[PASSED:]
     mate = to_mate(mate)
     sums, edges, band = call(
         functools.partial(local_kernel, chunk),
@@ -413,17 +406,17 @@
             shape(groups, parts, slots, rows),
             shape(rows, nodes),
         ),
-        [SM, SM, VM, VM] + [HB] * 3,
+        [SM, SM, VM] + [VM] * PASSED,
         [
+            pltpu.SMEM(tile_ids.shape[:0:-1], jnp.int32),
             pltpu.SMEM(counts.shape[:0:-1], jnp.int32),
-            pltpu.VMEM((parts, groups, slots), jnp.int32),
-            pltpu.VMEM((parts, groups, slots), bf16),
-            pltpu.SemaphoreType.DMA((3,)),
+            pltpu.VMEM((groups, rows, nodes), bf16),
+            pltpu.SemaphoreType.DMA((2,)),
         ],
         2 * nodes * nodes * width,
         1 << 20,
         4 if groups <= 4 else 16,
-    )(me, part, table, bands, counts[0].T, targets[0], edge_weight[0])
+    )(me, part, table, *passed)
     paired = call(
         pair_kernel,
         (shape(2, groups * slots, lanes),) * chips + (shape(width, rows),) * (groups - 1),

time: 39.1 us -> 38.4 us (0.982)
  Pallas kernels: 8.56 us -> 7.99 us
    pallas_call x13, Pallas kernels: 8.56 us -> 7.99 us  [placed(): run(*(pltpu.with_memory_space_constraint(value, pltpu.HBM) if spec is HB...]
  transfers between devices with their start and end apart: 17 -> 17, of which waited for: 9 -> 9; matrix products, arithmetic and copies ran while one was open for 0% -> 0% of each run, Pallas kernels for 13% -> 12%
where the time goes in v15:
time: 38.4 us; the launch traced here: 38.2 us
  starting transfers between devices  22 us (57%)
  Pallas kernels  7.99 us (21%)
  waiting for transfers between devices  7.45 us (19%)
  between operations  0.79 us (2%)
    ppermute x9, starting transfers between devices, shift(): lax.ppermute(block, 'feat', [(i, ahead(i, groups, k, near)) for i in rang...  13.5 us
    pallas_call x13, Pallas kernels, placed(): run(*(pltpu.with_memory_space_constraint(value, pltpu.HBM) if spec is HB...  7.99 us
    ppermute x6, starting transfers between devices, to_chips(): lax.ppermute(blocks[j], 'dom', [(d, next_to(d // 2, j, chips) * 2 + d % 2...  7.89 us
    ppermute x9, waiting for transfers between devices, shift(): lax.ppermute(block, 'feat', [(i, ahead(i, groups, k, near)) for i in rang...  4.22 us
    ppermute x6, waiting for transfers between devices, to_chips(): lax.ppermute(blocks[j], 'dom', [(d, next_to(d // 2, j, chips) * 2 + d % 2...  2.04 us
    ppermute x2, waiting for transfers between devices, to_mate(): return lax.ppermute(value, 'dom', [(d, d ^ 1) for d in range(parts)])  1.2 us
  transfers between devices with their start and end apart: 17, of which 9 were waited for; matrix products, arithmetic and copies ran while one was open for 0% of the time, Pallas kernels for 12%

profile of v15, /device:TPU:0, one launch (start us, length us, event | category | flops | bytes accessed | tf_op | source)
XLA Modules:
  0.0 38.2 jit_solution(4059890437047603319)
XLA Ops:
  0.6 0.0 copy-start.1
  0.6 1.6 %shard_map.122 = (bf16[4,64,256]{2,1,0:T(8,128)(2,1)S(1)}, bf16[4,64,256]{2,1,0:T(8,128)(2,1)S(1)}, bf16[256,512]{1,0:T(8,128)(2,1)S(1)}, bf16[12,128,128]{2,1,0...) custom-call(s32[1]{0:T(128)} %bitcast.me_ref, ...), custom_call_target="tpu_custom_call" | custom-call | flops 100663296 | bytes 1048576 | tf_op jit(solution)/shard_map/pallas_call | solution.py:33
  2.2 0.5 %collective-permute-start = (bf16[4,64,256]{2,1,0:T(8,128)(2,1)S(1)}, bf16[4,64,256]{2,1,0:T(8,128)(2,1)S(1)}, u32[]{:S(2)}, u32[]{:S(2)}) collective-permute-start(bf16[4,64,256]{2,1,0:T(8,128)(2,1)S(1)} %get-tuple-element.48), channel_id=1, source_target_pairs={{0,1},{1,0},{2,3},{3,2},{4,5},{5,4},{6,7},{7,6},{8,9},{9,8},{10,11... | collective-permute-start | bytes 393224 | tf_op jit(solution)/shard_map/ppermute | solution.py:368
  2.7 1.1 %shard_map.123 = (f32[4,208,128]{2,1,0:T(8,128)S(1)}, bf16[4,8,16,128]{3,2,1,0:T(8,128)(2,1)S(1)}, bf16[128,512]{1,0:T(8,128)(2,1)S(1)}) custom-call(s32[1]{0:T(128)} %bitcast.me_ref, s32[1]{0:T(128)} %bitcast.4.part_ref, bf16[256,512]{1,0:T(8,128)(2,1)S(1)} %get-tuple-element.40.table_ref, bf16[12,128,128]{2,1,0:T(8,128)(2,1)S(1)} %get-tuple-element.41.tiles_ref, ...), custom_call_target="tpu_custom_call" | custom-call | flops 100663296 | bytes 1048576 | tf_op jit(solution)/shard_map/pallas_call | solution.py:33
  3.8 0.0 collective-permute-done.got_ref
  3.9 3.8 %collective-permute-start.4 = (bf16[2,64,256]{2,1,0:T(8,128)(2,1)S(1)}, bf16[2,64,256]{2,1,0:T(8,128)(2,1)S(1)}, u32[]{:S(2)}, u32[]{:S(2)}) collective-permute-start(bf16[2,64,256]{2,1,0:T(8,128)(2,1)S(1)} %get-tuple-element.58), channel_id=1, source_target_pairs={{0,6},{1,7},{2,4},{3,5},{4,2},{5,3},{6,0},{7,1},{8,14},{9,15},{10,... | collective-permute-start | bytes 196616 | tf_op jit(solution)/shard_map/ppermute | solution.py:372
  7.6 0.5 %collective-permute-start.5 = (bf16[2,64,256]{2,1,0:T(8,128)(2,1)S(1)}, bf16[2,64,256]{2,1,0:T(8,128)(2,1)S(1)}, u32[]{:S(2)}, u32[]{:S(2)}) collective-permute-start(bf16[2,64,256]{2,1,0:T(8,128)(2,1)S(1)} %get-tuple-element.59), channel_id=1, source_target_pairs={{0,4},{1,5},{2,6},{3,7},{4,0},{5,1},{6,2},{7,3},{8,12},{9,13},{10,... | collective-permute-start | bytes 196616 | tf_op jit(solution)/shard_map/ppermute | solution.py:372
  8.1 0.1 collective-permute-start.6
  8.3 3.0 %collective-permute-start.1 = (bf16[192,128]{1,0:T(8,128)(2,1)S(1)}, bf16[192,128]{1,0:T(8,128)(2,1)S(1)}, u32[]{:S(2)}, u32[]{:S(2)}) collective-permute-start(bf16[192,128]{1,0:T(8,128)(2,1)S(1)} %get-tuple-element.52), channel_id=1, source_target_pairs={{0,16},{8,24},{16,0},{24,8},{1,17},{9,25},{17,1},{25,9},{2,18},{10... | collective-permute-start | bytes 147464 | tf_op jit(solution)/shard_map/ppermute | solution.py:363
  11.3 1.3 %collective-permute-start.2 = (bf16[192,128]{1,0:T(8,128)(2,1)S(1)}, bf16[192,128]{1,0:T(8,128)(2,1)S(1)}, u32[]{:S(2)}, u32[]{:S(2)}) collective-permute-start(bf16[192,128]{1,0:T(8,128)(2,1)S(1)} %get-tuple-element.53), channel_id=1, source_target_pairs={{0,24},{8,16},{16,8},{24,0},{1,25},{9,17},{17,9},{25,1},{2,26},{10... | collective-permute-start | bytes 147464 | tf_op jit(solution)/shard_map/ppermute | solution.py:363
  12.6 0.0 collective-permute-done.4.rest_1_
  12.6 0.2 collective-permute-start.3
  12.8 0.0 collective-permute-done.5.rest_2_
  12.9 0.0 collective-permute-done.6.rest_3_
  12.9 0.3 shard_map.126
  13.1 3.2 %collective-permute-start.7 = (bf16[192,128]{1,0:T(8,128)(2,1)S(1)}, bf16[192,128]{1,0:T(8,128)(2,1)S(1)}, u32[]{:S(2)}, u32[]{:S(2)}) collective-permute-start(bf16[192,128]{1,0:T(8,128)(2,1)S(1)} %get-tuple-element.62), channel_id=1, source_target_pairs={{0,24},{8,16},{16,8},{24,0},{1,25},{9,17},{17,9},{25,1},{2,26},{10... | collective-permute-start | bytes 147464 | tf_op jit(solution)/shard_map/ppermute | solution.py:363
  16.3 0.1 collective-permute-start.8
  16.5 0.0 collective-permute-done.1.rest_0_
  16.5 1.1 %collective-permute-start.9 = (bf16[192,128]{1,0:T(8,128)(2,1)S(1)}, bf16[192,128]{1,0:T(8,128)(2,1)S(1)}, u32[]{:S(2)}, u32[]{:S(2)}) collective-permute-start(bf16[192,128]{1,0:T(8,128)(2,1)S(1)} %get-tuple-element.64), channel_id=1, source_target_pairs={{0,8},{8,0},{16,24},{24,16},{1,9},{9,1},{17,25},{25,17},{2,10},{10... | collective-permute-start | bytes 147464 | tf_op jit(solution)/shard_map/ppermute | solution.py:363
  17.6 0.1 collective-permute-done.2.rest_1_
  17.7 0.2 collective-permute-done.3.rest_2_
  17.9 0.0 copy-done.1
  17.9 1.2 %shard_map.125.own_ref = f32[128,1024]{1,0:T(8,128)S(1)} custom-call(s32[1]{0:T(128)} %bitcast.me_ref, bf16[192,512]{1,0:T(8,128)(2,1)} %bitcast.22, bf16[768,1024]{1,0:T(8,128)(2,1)S(1)} %copy-done.1, bf16[192,128]{1,0:T(8,128)(2,1)S(1)} %collective-permute-done.1.rest_0_, bf16[192,128]{1,0:T(8,128)(2,1)S(1)} %collective-permute-done.2.rest_1_, ...), custom_call_target="tpu_custom_call" | custom-call | flops 201326592 | bytes 2097152 | tf_op jit(solution)/shard_map/pallas_call | solution.py:33
  19.1 0.0 copy-start.3
  19.1 0.0 collective-permute-done.7.rest_1_
  19.1 0.3 shard_map.127.early_ref
  19.5 2.1 %collective-permute-done.8.rest_0_ = bf16[192,128]{1,0:T(8,128)(2,1)S(1)} collective-permute-done((bf16[192,128]{1,0:T(8,128)(2,1)S(1)}, bf16[192,128]{1,0:T(8,128)(2,1)S(1)}, u32[]{:S(2)}, u32[]{:S(2)}) %collective-permute-start.8) | collective-permute-done | bytes 49184 | tf_op jit(solution)/shard_map/ppermute | solution.py:363
  21.5 0.0 collective-permute-done.9.rest_1_
  21.5 0.5 %shard_map.128 = (bf16[128,1024]{1,0:T(8,128)(2,1)S(1)}, bf16[153,128]{1,0:T(8,128)(2,1)S(1)}, bf16[153,128]{1,0:T(8,128)(2,1)S(1)}, bf16[153,128]{1,0:T(8,128)(2,1)S(1)}, bf16[153,128]{1,0:T(8,128)(2,1)S(1)}) custom-call(s32[1]{0:T(128)} %bitcast.me_ref, bf16[768,1024]{1,0:T(8,128)(2,1)S(1)} %copy-done, bf16[153,1024]{1,0:T(8,128)(2,1)S(1)} %bitcast.20, ...), custom_call_target="tpu_custom_call" | custom-call | flops 100663296 | bytes 2097152 | tf_op jit(solution)/shard_map/pallas_call | solution.py:33
  22.1 2.1 %collective-permute-start.10 = (bf16[153,128]{1,0:T(8,128)(2,1)S(1)}, bf16[153,128]{1,0:T(8,128)(2,1)S(1)}, u32[]{:S(2)}, u32[]{:S(2)}) collective-permute-start(bf16[153,128]{1,0:T(8,128)(2,1)S(1)} %get-tuple-element.69), channel_id=1, source_target_pairs={{0,24},{8,16},{16,8},{24,0},{1,25},{9,17},{17,9},{25,1},{2,26},{10... | collective-permute-start | bytes 117512 | tf_op jit(solution)/shard_map/ppermute | solution.py:363
  24.2 0.0 collective-permute-start.11
  24.2 2.4 %collective-permute-start.12 = (bf16[153,128]{1,0:T(8,128)(2,1)S(1)}, bf16[153,128]{1,0:T(8,128)(2,1)S(1)}, u32[]{:S(2)}, u32[]{:S(2)}) collective-permute-start(bf16[153,128]{1,0:T(8,128)(2,1)S(1)} %get-tuple-element.71), channel_id=1, source_target_pairs={{0,8},{8,0},{16,24},{24,16},{1,9},{9,1},{17,25},{25,17},{2,10},{10... | collective-permute-start | bytes 117512 | tf_op jit(solution)/shard_map/ppermute | solution.py:363
  26.5 0.9 %shard_map.131.hits_ref.after = bf16[128,512]{1,0:T(8,128)(2,1)S(1)} custom-call(bf16[153,128]{1,0:T(8,128)(2,1)S(1)} %get-tuple-element.68.rest_0_.after, s32[1]{0:T(128)} %bitcast.me_ref, s32[1]{0:T(128)} %bitcast.4.part_ref, s32[8,4,16]{2,1,0:T(4,128)} %bitcast.26), custom_call_target="tpu_custom_call" | custom-call | bytes 524288 | tf_op jit(solution)/shard_map/pallas_call | solution.py:33
  27.5 0.5 %collective-permute-done.10.rest_1_ = bf16[153,128]{1,0:T(8,128)(2,1)S(1)} collective-permute-done((bf16[153,128]{1,0:T(8,128)(2,1)S(1)}, bf16[153,128]{1,0:T(8,128)(2,1)S(1)}, u32[]{:S(2)}, u32[]{:S(2)}) %collective-permute-start.10) | collective-permute-done | bytes 39200 | tf_op jit(solution)/shard_map/ppermute | solution.py:363
  27.9 1.4 %collective-permute-done.11.rest_2_ = bf16[153,128]{1,0:T(8,128)(2,1)S(1)} collective-permute-done((bf16[153,128]{1,0:T(8,128)(2,1)S(1)}, bf16[153,128]{1,0:T(8,128)(2,1)S(1)}, u32[]{:S(2)}, u32[]{:S(2)}) %collective-permute-start.11) | collective-permute-done | bytes 39200 | tf_op jit(solution)/shard_map/ppermute | solution.py:363
  29.3 0.0 collective-permute-done.12.rest_3_
  29.3 0.3 shard_map.132
  29.6 0.1 collective-permute-start.13
  29.7 1.2 %collective-permute-done.13.got_ref = bf16[4,16,256]{2,1,0:T(8,128)(2,1)S(1)} collective-permute-done((bf16[4,16,256]{2,1,0:T(8,128)(2,1)S(1)}, bf16[4,16,256]{2,1,0:T(8,128)(2,1)S(1)}, u32[]{:S(2)}, u32[]{:S(2)}) %collective-permute-start.13) | collective-permute-done | bytes 32800 | tf_op jit(solution)/shard_map/ppermute | solution.py:368
  30.9 2.4 %collective-permute-start.14 = (bf16[2,16,256]{2,1,0:T(8,128)(2,1)S(1)}, bf16[2,16,256]{2,1,0:T(8,128)(2,1)S(1)}, u32[]{:S(2)}, u32[]{:S(2)}) collective-permute-start(bf16[2,16,256]{2,1,0:T(8,128)(2,1)S(1)} %get-tuple-element.75), channel_id=1, source_target_pairs={{0,6},{1,7},{2,4},{3,5},{4,2},{5,3},{6,0},{7,1},{8,14},{9,15},{10,... | collective-permute-start | bytes 49160 | tf_op jit(solution)/shard_map/ppermute | solution.py:372
  33.3 0.3 collective-permute-start.15
  33.6 0.8 %collective-permute-start.16 = (bf16[2,16,256]{2,1,0:T(8,128)(2,1)S(1)}, bf16[2,16,256]{2,1,0:T(8,128)(2,1)S(1)}, u32[]{:S(2)}, u32[]{:S(2)}) collective-permute-start(bf16[2,16,256]{2,1,0:T(8,128)(2,1)S(1)} %get-tuple-element.77), channel_id=1, source_target_pairs={{0,2},{1,3},{2,0},{3,1},{4,6},{5,7},{6,4},{7,5},{8,10},{9,11},{10,... | collective-permute-start | bytes 49160 | tf_op jit(solution)/shard_map/ppermute | solution.py:372
  34.4 0.7 %shard_map.129 = (f32[153,128]{1,0:T(8,128)S(1)}, bf16[128,1024]{1,0:T(8,128)(2,1)}) custom-call(bf16[128,1024]{1,0:T(8,128)(2,1)S(1)} %get-tuple-element.65.hidden_ref, bf16[153,1024]{1,0:T(8,128)(2,1)S(1)} %bitcast.19), custom_call_target="tpu_custom_call" | custom-call | flops 40108032 | bytes 1048576 | tf_op jit(solution)/shard_map/pallas_call | solution.py:33
  35.1 0.2 shard_map.130.near_ref
  35.3 0.2 collective-permute-done.14.rest_1_
  35.5 1.5 %collective-permute-done.15.rest_2_ = bf16[2,16,256]{2,1,0:T(8,128)(2,1)S(1)} collective-permute-done((bf16[2,16,256]{2,1,0:T(8,128)(2,1)S(1)}, bf16[2,16,256]{2,1,0:T(8,128)(2,1)S(1)}, u32[]{:S(2)}, u32[]{:S(2)}) %collective-permute-start.15) | collective-permute-done | bytes 16416 | tf_op jit(solution)/shard_map/ppermute | solution.py:372
  37.0 0.3 collective-permute-done.16.rest_3_
  37.3 0.9 %shard_map.134 = f32[153,1,128]{2,1,0:T(1,128)} custom-call(s32[1]{0:T(128)} %bitcast.me_ref, f32[153,128]{1,0:T(8,128)S(1)} %shard_map.130.near_ref, bf16[4,8,16,128]{3,2,1,0:T(8,128)(2,1)S(1)} %get-tuple-element.56.edges_ref, f32[4,208,128]{2,1,0:T(8,128)S(1)} %get-tuple-element.55.sums_ref, bf16[2,16,256]{2,1,0:T(8,128)(2,1)S(1)} %get-tuple-element.74.rest_0_, ...), custom_call_target="tpu_custom_call" | custom-call | flops 5013504 | bytes 524288 | tf_op jit(solution)/shard_map/pallas_call | solution.py:33
  (7 shorter events, 0.0 us)
Async XLA Ops:
  0.6 17.2 %copy-start.1 = (bf16[768,1024]{1,0:T(8,128)(2,1)S(1)}, bf16[768,1024]{1,0:T(8,128)(2,1)}, u32[]{:S(2)}) copy-start(bf16[768,1024]{1,0:T(8,128)(2,1)} %weight_ref.3) | copy-start | bytes 4718596
  2.2 1.6 %collective-permute-start = (bf16[4,64,256]{2,1,0:T(8,128)(2,1)S(1)}, bf16[4,64,256]{2,1,0:T(8,128)(2,1)S(1)}, u32[]{:S(2)}, u32[]{:S(2)}) collective-permute-start(bf16[4,64,256]{2,1,0:T(8,128)(2,1)S(1)} %get-tuple-element.48), channel_id=1, source_target_pairs={{0,1},{1,0},{2,3},{3,2},{4,5},{5,4},{6,7},{7,6},{8,9},{9,8},{10,11... | collective-permute-start | bytes 393224 | tf_op jit(solution)/shard_map/ppermute | solution.py:368
  3.9 8.7 %collective-permute-start.4 = (bf16[2,64,256]{2,1,0:T(8,128)(2,1)S(1)}, bf16[2,64,256]{2,1,0:T(8,128)(2,1)S(1)}, u32[]{:S(2)}, u32[]{:S(2)}) collective-permute-start(bf16[2,64,256]{2,1,0:T(8,128)(2,1)S(1)} %get-tuple-element.58), channel_id=1, source_target_pairs={{0,6},{1,7},{2,4},{3,5},{4,2},{5,3},{6,0},{7,1},{8,14},{9,15},{10,... | collective-permute-start | bytes 196616 | tf_op jit(solution)/shard_map/ppermute | solution.py:372
  7.6 5.2 %collective-permute-start.5 = (bf16[2,64,256]{2,1,0:T(8,128)(2,1)S(1)}, bf16[2,64,256]{2,1,0:T(8,128)(2,1)S(1)}, u32[]{:S(2)}, u32[]{:S(2)}) collective-permute-start(bf16[2,64,256]{2,1,0:T(8,128)(2,1)S(1)} %get-tuple-element.59), channel_id=1, source_target_pairs={{0,4},{1,5},{2,6},{3,7},{4,0},{5,1},{6,2},{7,3},{8,12},{9,13},{10,... | collective-permute-start | bytes 196616 | tf_op jit(solution)/shard_map/ppermute | solution.py:372
  8.1 4.7 %collective-permute-start.6 = (bf16[2,64,256]{2,1,0:T(8,128)(2,1)S(1)}, bf16[2,64,256]{2,1,0:T(8,128)(2,1)S(1)}, u32[]{:S(2)}, u32[]{:S(2)}) collective-permute-start(bf16[2,64,256]{2,1,0:T(8,128)(2,1)S(1)} %get-tuple-element.60), channel_id=1, source_target_pairs={{0,2},{1,3},{2,0},{3,1},{4,6},{5,7},{6,4},{7,5},{8,10},{9,11},{10,... | collective-permute-start | bytes 196616 | tf_op jit(solution)/shard_map/ppermute | solution.py:372
  8.3 8.2 %collective-permute-start.1 = (bf16[192,128]{1,0:T(8,128)(2,1)S(1)}, bf16[192,128]{1,0:T(8,128)(2,1)S(1)}, u32[]{:S(2)}, u32[]{:S(2)}) collective-permute-start(bf16[192,128]{1,0:T(8,128)(2,1)S(1)} %get-tuple-element.52), channel_id=1, source_target_pairs={{0,16},{8,24},{16,0},{24,8},{1,17},{9,25},{17,1},{25,9},{2,18},{10... | collective-permute-start | bytes 147464 | tf_op jit(solution)/shard_map/ppermute | solution.py:363
  11.3 6.4 %collective-permute-start.2 = (bf16[192,128]{1,0:T(8,128)(2,1)S(1)}, bf16[192,128]{1,0:T(8,128)(2,1)S(1)}, u32[]{:S(2)}, u32[]{:S(2)}) collective-permute-start(bf16[192,128]{1,0:T(8,128)(2,1)S(1)} %get-tuple-element.53), channel_id=1, source_target_pairs={{0,24},{8,16},{16,8},{24,0},{1,25},{9,17},{17,9},{25,1},{2,26},{10... | collective-permute-start | bytes 147464 | tf_op jit(solution)/shard_map/ppermute | solution.py:363
  12.6 5.3 %collective-permute-start.3 = (bf16[192,128]{1,0:T(8,128)(2,1)S(1)}, bf16[192,128]{1,0:T(8,128)(2,1)S(1)}, u32[]{:S(2)}, u32[]{:S(2)}) collective-permute-start(bf16[192,128]{1,0:T(8,128)(2,1)S(1)} %get-tuple-element.54), channel_id=1, source_target_pairs={{0,8},{8,0},{16,24},{24,16},{1,9},{9,1},{17,25},{25,17},{2,10},{10... | collective-permute-start | bytes 147464 | tf_op jit(solution)/shard_map/ppermute | solution.py:363
  12.9 6.3 %copy-start = (bf16[768,1024]{1,0:T(8,128)(2,1)S(1)}, bf16[768,1024]{1,0:T(8,128)(2,1)}, u32[]{:S(2)}) copy-start(bf16[768,1024]{1,0:T(8,128)(2,1)} %weight_ref.5) | copy-start | bytes 4718596
  13.1 6.0 %collective-permute-start.7 = (bf16[192,128]{1,0:T(8,128)(2,1)S(1)}, bf16[192,128]{1,0:T(8,128)(2,1)S(1)}, u32[]{:S(2)}, u32[]{:S(2)}) collective-permute-start(bf16[192,128]{1,0:T(8,128)(2,1)S(1)} %get-tuple-element.62), channel_id=1, source_target_pairs={{0,24},{8,16},{16,8},{24,0},{1,25},{9,17},{17,9},{25,1},{2,26},{10... | collective-permute-start | bytes 147464 | tf_op jit(solution)/shard_map/ppermute | solution.py:363
  16.3 5.2 %collective-permute-start.8 = (bf16[192,128]{1,0:T(8,128)(2,1)S(1)}, bf16[192,128]{1,0:T(8,128)(2,1)S(1)}, u32[]{:S(2)}, u32[]{:S(2)}) collective-permute-start(bf16[192,128]{1,0:T(8,128)(2,1)S(1)} %get-tuple-element.63), channel_id=1, source_target_pairs={{0,16},{8,24},{16,0},{24,8},{1,17},{9,25},{17,1},{25,9},{2,18},{10... | collective-permute-start | bytes 147464 | tf_op jit(solution)/shard_map/ppermute | solution.py:363
  16.5 5.1 %collective-permute-start.9 = (bf16[192,128]{1,0:T(8,128)(2,1)S(1)}, bf16[192,128]{1,0:T(8,128)(2,1)S(1)}, u32[]{:S(2)}, u32[]{:S(2)}) collective-permute-start(bf16[192,128]{1,0:T(8,128)(2,1)S(1)} %get-tuple-element.64), channel_id=1, source_target_pairs={{0,8},{8,0},{16,24},{24,16},{1,9},{9,1},{17,25},{25,17},{2,10},{10... | collective-permute-start | bytes 147464 | tf_op jit(solution)/shard_map/ppermute | solution.py:363
  19.1 2.4 %copy-start.3 = (bf16[1024,153]{0,1:T(8,128)(2,1)S(1)}, bf16[1024,153]{0,1:T(8,128)(2,1)}, u32[]{:S(2)}) copy-start(bf16[1024,153]{0,1:T(8,128)(2,1)} %param.21) | copy-start | bytes 940036
  21.5 12.8 %copy-start.2 = (bf16[1024,153]{0,1:T(8,128)(2,1)S(1)}, bf16[1024,153]{0,1:T(8,128)(2,1)}, u32[]{:S(2)}) copy-start(bf16[1024,153]{0,1:T(8,128)(2,1)} %param.20) | copy-start | bytes 940036
  22.1 5.9 %collective-permute-start.10 = (bf16[153,128]{1,0:T(8,128)(2,1)S(1)}, bf16[153,128]{1,0:T(8,128)(2,1)S(1)}, u32[]{:S(2)}, u32[]{:S(2)}) collective-permute-start(bf16[153,128]{1,0:T(8,128)(2,1)S(1)} %get-tuple-element.69), channel_id=1, source_target_pairs={{0,24},{8,16},{16,8},{24,0},{1,25},{9,17},{17,9},{25,1},{2,26},{10... | collective-permute-start | bytes 117512 | tf_op jit(solution)/shard_map/ppermute | solution.py:363
  24.2 5.1 %collective-permute-start.11 = (bf16[153,128]{1,0:T(8,128)(2,1)S(1)}, bf16[153,128]{1,0:T(8,128)(2,1)S(1)}, u32[]{:S(2)}, u32[]{:S(2)}) collective-permute-start(bf16[153,128]{1,0:T(8,128)(2,1)S(1)} %get-tuple-element.70), channel_id=1, source_target_pairs={{0,16},{8,24},{16,0},{24,8},{1,17},{9,25},{17,1},{25,9},{2,18},{10... | collective-permute-start | bytes 117512 | tf_op jit(solution)/shard_map/ppermute | solution.py:363
  24.2 5.1 %collective-permute-start.12 = (bf16[153,128]{1,0:T(8,128)(2,1)S(1)}, bf16[153,128]{1,0:T(8,128)(2,1)S(1)}, u32[]{:S(2)}, u32[]{:S(2)}) collective-permute-start(bf16[153,128]{1,0:T(8,128)(2,1)S(1)} %get-tuple-element.71), channel_id=1, source_target_pairs={{0,8},{8,0},{16,24},{24,16},{1,9},{9,1},{17,25},{25,17},{2,10},{10... | collective-permute-start | bytes 117512 | tf_op jit(solution)/shard_map/ppermute | solution.py:363
  29.6 1.3 %collective-permute-start.13 = (bf16[4,16,256]{2,1,0:T(8,128)(2,1)S(1)}, bf16[4,16,256]{2,1,0:T(8,128)(2,1)S(1)}, u32[]{:S(2)}, u32[]{:S(2)}) collective-permute-start(bf16[4,16,256]{2,1,0:T(8,128)(2,1)S(1)} %get-tuple-element.73), channel_id=1, source_target_pairs={{0,1},{1,0},{2,3},{3,2},{4,5},{5,4},{6,7},{7,6},{8,9},{9,8},{10,11... | collective-permute-start | bytes 98312 | tf_op jit(solution)/shard_map/ppermute | solution.py:368
  30.9 4.6 %collective-permute-start.14 = (bf16[2,16,256]{2,1,0:T(8,128)(2,1)S(1)}, bf16[2,16,256]{2,1,0:T(8,128)(2,1)S(1)}, u32[]{:S(2)}, u32[]{:S(2)}) collective-permute-start(bf16[2,16,256]{2,1,0:T(8,128)(2,1)S(1)} %get-tuple-element.75), channel_id=1, source_target_pairs={{0,6},{1,7},{2,4},{3,5},{4,2},{5,3},{6,0},{7,1},{8,14},{9,15},{10,... | collective-permute-start | bytes 49160 | tf_op jit(solution)/shard_map/ppermute | solution.py:372
  33.3 3.7 %collective-permute-start.15 = (bf16[2,16,256]{2,1,0:T(8,128)(2,1)S(1)}, bf16[2,16,256]{2,1,0:T(8,128)(2,1)S(1)}, u32[]{:S(2)}, u32[]{:S(2)}) collective-permute-start(bf16[2,16,256]{2,1,0:T(8,128)(2,1)S(1)} %get-tuple-element.76), channel_id=1, source_target_pairs={{0,4},{1,5},{2,6},{3,7},{4,0},{5,1},{6,2},{7,3},{8,12},{9,13},{10,... | collective-permute-start | bytes 49160 | tf_op jit(solution)/shard_map/ppermute | solution.py:372
  33.6 3.7 %collective-permute-start.16 = (bf16[2,16,256]{2,1,0:T(8,128)(2,1)S(1)}, bf16[2,16,256]{2,1,0:T(8,128)(2,1)S(1)}, u32[]{:S(2)}, u32[]{:S(2)}) collective-permute-start(bf16[2,16,256]{2,1,0:T(8,128)(2,1)S(1)} %get-tuple-element.77), channel_id=1, source_target_pairs={{0,2},{1,3},{2,0},{3,1},{4,6},{5,7},{6,4},{7,5},{8,10},{9,11},{10,... | collective-permute-start | bytes 49160 | tf_op jit(solution)/shard_map/ppermute | solution.py:372

commit v16 on v15

--- a/solution.py
+++ b/solution.py
@@ -85,22 +85,37 @@
     return values.reshape(-1, values.shape[-1]).T
 
 
-def gather_kernel(
-    chunk,
-    me_ref,
-    part_ref,
-    sources_hbm,
-    features_hbm,
-    *rest,
-):
-    extras, (mine_ref, mate_ref, table_ref, *outs) = rest[:PASSED], rest[PASSED:]
-    passed, blocks = outs[:PASSED], outs[PASSED:-4]
-    sources_ref, order, hits, sems = outs[-4:]
-    parts, groups, slots = sources_ref.shape
+def pick_rows(chunk, other, part_ref, sources_ref, table_ref, out_ref, order, hits, ready):
+    chips, lanes = out_ref.shape[0], out_ref.shape[2]
+    _, groups, slots = sources_ref.shape
+    nodes = table_ref.shape[1]
+    chip, core = part_ref[0] // 2, part_ref[0] % 2
+    lane = lax.broadcasted_iota(jnp.int32, (slots, nodes), 1)
+
+    def step(i, last):
+        for j in range(chunk):
+            order[j] = sources_ref[next_to(chip, i * chunk + j, chips) * 2 + (core ^ other)]
+        columns = columns_of(order[...])
+        for n in range(chunk * groups):
+            hits[n * slots : (n + 1) * slots, :] = jnp.where(
+                columns[:, n : n + 1] == lane, 1.0, 0.0
+            ).astype(bf16)
+        if last:
+            ready()
+        picked = dot(hits[...], table_ref[:lanes, :], LAST).astype(bf16)
+        out_ref[pl.ds(i * chunk, chunk)] = picked.reshape(chunk, groups * slots, -1)
+
+    if chips == chunk:
+        step(0, True)
+    else:
+        ready()
+        lax.fori_loop(0, chips // chunk, lambda i, _: step(i, False), None)
+
+
+def gather_kernel(chunk, part_ref, sources_hbm, features_hbm, *rest):
+    extras, (mate_ref, table_ref, sources_ref, *rest) = rest[:PASSED], rest[PASSED:]
+    passed, (order, hits, sems) = rest[:PASSED], rest[PASSED:]
     width, nodes = features_hbm.shape
-    rows = nodes // groups
-    lanes = mine_ref.shape[2]
-    chips, chip, core = parts // 2, part_ref[0] // 2, part_ref[0] % 2
     indices, table, *others = fetch(
         sems,
         (sources_hbm, sources_ref),
@@ -113,31 +128,7 @@
             (table_ref.shape[0] - width - EXTRA, nodes), bf16
         )
     indices.wait()
-    lane = lax.broadcasted_iota(jnp.int32, (slots, nodes), 1)
-
-    def step(i, out, other, last):
-        for j in range(chunk):
-            order[j] = sources_ref[next_to(chip, i * chunk + j, chips) * 2 + (core ^ other)]
-        columns = columns_of(order[...])
-        for n in range(chunk * groups):
-            hits[n * slots : (n + 1) * slots, :] = jnp.where(
-                columns[:, n : n + 1] == lane, 1.0, 0.0
-            ).astype(bf16)
-        if last:
-            table.wait()
-        picked = dot(hits[...], table_ref[:lanes, :], LAST).astype(bf16)
-        out[pl.ds(i * chunk, chunk)] = picked.reshape(chunk, groups * slots, -1)
-
-    if chips == chunk:
-        step(0, mate_ref, 1, True)
-        step(0, mine_ref, 0, False)
-    else:
-        table.wait()
-        for other, out in enumerate((mine_ref, mate_ref)):
-            lax.fori_loop(0, chips // chunk, lambda i, _: step(i, out, other, False), None)
-    for k in range(1, groups):
-        group = ahead(me_ref[0], groups, k, True)
-        blocks[k - 1][...] = table_ref[:width, pl.ds(pl.multiple_of(group * rows, rows), rows)]
+    pick_rows(chunk, 1, part_ref, sources_ref, table_ref, mate_ref, order, hits, table.wait)
     for copy in others:
         copy.wait()
 
@@ -147,6 +138,7 @@
     me_ref,
     part_ref,
     table_ref,
+    sources_ref,
     tiles_ref,
     targets_ref,
     weight_ref,
@@ -155,16 +147,21 @@
     sums_ref,
     edges_ref,
     band_ref,
-    ids_ref,
-    counts_ref,
-    bands_ref,
-    sems,
+    mine_ref,
+    *rest,
 ):
+    blocks, (ids_ref, counts_ref, bands_ref, order, hits, sems) = rest[:-6], rest[-6:]
     parts, groups, slots = targets_ref.shape
     rows = edges_ref.shape[3]
     high = sums_ref.shape[1]
+    width = high - EXTRA
     copies = fetch(sems, (ids_vmem, ids_ref), (counts_vmem, counts_ref))
     bands_ref[...] = jnp.zeros_like(bands_ref)
+    picked = order.shape[0]
+    pick_rows(picked, 0, part_ref, sources_ref, table_ref, mine_ref, order, hits, lambda: None)
+    for k in range(1, groups):
+        group = ahead(me_ref[0], groups, k, True)
+        blocks[k - 1][...] = table_ref[:width, pl.ds(pl.multiple_of(group * rows, rows), rows)]
     for copy in copies:
         copy.wait()
 
@@ -194,7 +191,7 @@
                 values = jnp.where(hit, weight[:, n : n + 1], 0.0)
                 edges_ref[g, at] = values.astype(bf16)
                 degree = degree + jnp.sum(values, axis=0, keepdims=True)
-            sums_ref[g, high - EXTRA : high - EXTRA + 1, :] += degree
+            sums_ref[g, width : width + 1, :] += degree
         return 0
 
     if parts == chunk:
@@ -237,21 +234,22 @@
     return pl.ds(pl.multiple_of(behind(me, groups, k, near) * width, width), width)
 
 
-def self_kernel(me_ref, features_hbm, weight_ref, *rest):
-    blocks, (out_ref, own_ref, sem) = rest[:-3], rest[-3:]
+def self_kernel(me_ref, features_hbm, weight_hbm, *rest):
+    blocks, (out_ref, own_ref, weight_ref, sems) = rest[:-4], rest[-4:]
     groups, (width, rows) = len(blocks) + 1, own_ref.shape
     me = me_ref[0]
-    own = pltpu.make_async_copy(
-        features_hbm.at[:, pl.ds(pl.multiple_of(me * rows, rows), rows)], own_ref, sem
+    spans = [rows_from(me, groups, k, width, True) for k in range(groups)]
+    own, *weights = fetch(
+        sems,
+        (features_hbm.at[:, pl.ds(pl.multiple_of(me * rows, rows), rows)], own_ref),
+        *[(weight_hbm.at[span, :], weight_ref.at[span, :]) for span in spans],
     )
-    own.start()
+    own.wait()
     total = jnp.zeros(out_ref.shape, f32)
-    for k, block in enumerate(blocks, 1):
-        span = rows_from(me, groups, k, width, True)
+    for block, span, weight in zip((own_ref, *blocks), spans, weights):
+        weight.wait()
         total = total + dot(block[...], weight_ref[span, :], FIRST)
-    own.wait()
-    span = pl.ds(pl.multiple_of(me * width, width), width)
-    out_ref[...] = total + dot(own_ref[...], weight_ref[span, :], FIRST)
+    out_ref[...] = total
 
 
 def add_blocks(total, me, groups, first, blocks, weight_ref):
@@ -381,38 +379,41 @@
     lanes = whole_lanes(width)
     table_rows = max(lanes, width + EXTRA)
     extras = (tile_contents, targets[0], edge_weight[0], tile_ids[0].T, counts[0].T)
-    mine, mate, table, *rest = call(
+    picking = [
+        pltpu.VMEM((picked, groups, slots), jnp.int32),
+        pltpu.VMEM((picked * groups * slots, nodes), bf16),
+    ]
+    mate, table, *passed = call(
         functools.partial(gather_kernel, picked),
-        (shape(chips, groups * slots, lanes),) * 2
-        + (shape(table_rows, nodes),)
-        + tuple(shape(*value.shape, dtype=value.dtype) for value in extras)
-        + (shape(width, rows),) * (groups - 1),
-        [SM, SM, HB, HB] + [HB] * PASSED,
-        [
-            pltpu.VMEM((parts, groups, slots), jnp.int32),
-            pltpu.VMEM((picked, groups, slots), jnp.int32),
-            pltpu.VMEM((picked * groups * slots, nodes), bf16),
-            pltpu.SemaphoreType.DMA((2 + PASSED,)),
-        ],
+        (
+            shape(chips, groups * slots, lanes),
+            shape(table_rows, nodes),
+            shape(parts, groups, slots, dtype=jnp.int32),
+        )
+        + tuple(shape(*value.shape, dtype=value.dtype) for value in extras),
+        [SM, HB, HB] + [HB] * PASSED,
+        picking + [pltpu.SemaphoreType.DMA((2 + PASSED,))],
         2 * nodes * nodes * width,
         1 << 20,
-    )(me, part, sources[0], feature_rows, *extras)
-    passed, feature_blocks = rest[:PASSED], rest[PASSED:]
+    )(part, sources[0], feature_rows, *extras)
     mate = to_mate(mate)
-    sums, edges, band = call(
+    sums, edges, band, mine, *feature_blocks = call(
         functools.partial(local_kernel, chunk),
         (
             shape(groups, width + EXTRA, rows, dtype=f32),
             shape(groups, parts, slots, rows),
             shape(rows, nodes),
-        ),
-        [SM, SM, VM] + [VM] * PASSED,
+            shape(chips, groups * slots, lanes),
+        )
+        + (shape(width, rows),) * (groups - 1),
+        [SM, SM, VM, VM] + [VM] * PASSED,
         [
             pltpu.SMEM(tile_ids.shape[:0:-1], jnp.int32),
             pltpu.SMEM(counts.shape[:0:-1], jnp.int32),
             pltpu.VMEM((groups, rows, nodes), bf16),
-            pltpu.SemaphoreType.DMA((2,)),
-        ],
+        ]
+        + picking
+        + [pltpu.SemaphoreType.DMA((2,))],
         2 * nodes * nodes * width,
         1 << 20,
         4 if groups <= 4 else 16,
@@ -439,8 +440,12 @@
     own = call(
         self_kernel,
         shape(rows, hid, dtype=f32),
-        [SM, HB] + [VM] * groups,
-        [pltpu.VMEM((width, rows), bf16), pltpu.SemaphoreType.DMA],
+        [SM, HB, HB] + [VM] * (groups - 1),
+        [
+            pltpu.VMEM((width, rows), bf16),
+            pltpu.VMEM(self_one.shape, bf16),
+            pltpu.SemaphoreType.DMA((1 + groups,)),
+        ],
         2 * rows * hid * groups * width,
         2 << 20,
     )(me, feature_rows, self_one, *feature_blocks)

time: 38.4 us -> 38.2 us (level)
  waiting for transfers between devices: 7.45 us -> 6.93 us
  Pallas kernels: 7.99 us -> 8.39 us
    ppermute x9, waiting for transfers between devices: 4.22 us -> 3.63 us  [shift(): lax.ppermute(block, 'feat', [(i, ahead(i, groups, k, near)) for i in rang...]
    pallas_call x13, Pallas kernels: 7.99 us -> 8.39 us  [placed(): run(*(pltpu.with_memory_space_constraint(value, pltpu.HBM) if spec is HB...]
  transfers between devices with their start and end apart: 17 -> 17, of which waited for: 9 -> 8; matrix products, arithmetic and copies ran while one was open for 0% -> 0% of each run, Pallas kernels for 12% -> 14%
where the time goes in v16:
time: 38.2 us; the launch traced here: 38 us
  starting transfers between devices  21.9 us (57%)
  Pallas kernels  8.39 us (22%)
  waiting for transfers between devices  6.93 us (18%)
  between operations  0.78 us (2%)
    ppermute x9, starting transfers between devices, shift(): lax.ppermute(block, 'feat', [(i, ahead(i, groups, k, near)) for i in rang...  13.5 us
    pallas_call x13, Pallas kernels, placed(): run(*(pltpu.with_memory_space_constraint(value, pltpu.HBM) if spec is HB...  8.39 us
    ppermute x6, starting transfers between devices, to_chips(): lax.ppermute(blocks[j], 'dom', [(d, next_to(d // 2, j, chips) * 2 + d % 2...  7.8 us
    ppermute x9, waiting for transfers between devices, shift(): lax.ppermute(block, 'feat', [(i, ahead(i, groups, k, near)) for i in rang...  3.63 us
    ppermute x6, waiting for transfers between devices, to_chips(): lax.ppermute(blocks[j], 'dom', [(d, next_to(d // 2, j, chips) * 2 + d % 2...  2.11 us
    ppermute x2, waiting for transfers between devices, to_mate(): return lax.ppermute(value, 'dom', [(d, d ^ 1) for d in range(parts)])  1.2 us
  transfers between devices with their start and end apart: 17, of which 8 were waited for; matrix products, arithmetic and copies ran while one was open for 0% of the time, Pallas kernels for 14%

profile of v16, /device:TPU:0, one launch (start us, length us, event | category | flops | bytes accessed | tf_op | source)
XLA Modules:
  0.0 38.0 jit_solution(16715327883395008458)
XLA Ops:
  0.6 1.3 %shard_map.122 = (bf16[4,64,256]{2,1,0:T(8,128)(2,1)S(1)}, bf16[256,512]{1,0:T(8,128)(2,1)S(1)}, s32[8,4,16]{2,1,0:T(4,128)S(1)}, bf16[12,128,128]{2,1,0:T(8,128...) custom-call(s32[1]{0:T(128)} %bitcast.4.part_ref, ...), custom_call_target="tpu_custom_call" | custom-call | flops 100663296 | bytes 1048576 | tf_op jit(solution)/shard_map/pallas_call | solution.py:33
  1.9 0.5 %collective-permute-start = (bf16[4,64,256]{2,1,0:T(8,128)(2,1)S(1)}, bf16[4,64,256]{2,1,0:T(8,128)(2,1)S(1)}, u32[]{:S(2)}, u32[]{:S(2)}) collective-permute-start(bf16[4,64,256]{2,1,0:T(8,128)(2,1)S(1)} %get-tuple-element.50), channel_id=1, source_target_pairs={{0,1},{1,0},{2,3},{3,2},{4,5},{5,4},{6,7},{7,6},{8,9},{9,8},{10,11... | collective-permute-start | bytes 393224 | tf_op jit(solution)/shard_map/ppermute | solution.py:366
  2.5 1.2 %shard_map.123 = (f32[4,208,128]{2,1,0:T(8,128)S(1)}, bf16[4,8,16,128]{3,2,1,0:T(8,128)(2,1)S(1)}, bf16[128,512]{1,0:T(8,128)(2,1)S(1)}, bf16[4,64,256]{2,1,0:T(...) custom-call(s32[1]{0:T(128)} %bitcast.me_ref, ...), custom_call_target="tpu_custom_call" | custom-call | flops 100663296 | bytes 1048576 | tf_op jit(solution)/shard_map/pallas_call | solution.py:33
  3.6 0.0 collective-permute-done.got_ref
  3.7 3.7 %collective-permute-start.4 = (bf16[2,64,256]{2,1,0:T(8,128)(2,1)S(1)}, bf16[2,64,256]{2,1,0:T(8,128)(2,1)S(1)}, u32[]{:S(2)}, u32[]{:S(2)}) collective-permute-start(bf16[2,64,256]{2,1,0:T(8,128)(2,1)S(1)} %get-tuple-element.60), channel_id=1, source_target_pairs={{0,6},{1,7},{2,4},{3,5},{4,2},{5,3},{6,0},{7,1},{8,14},{9,15},{10,... | collective-permute-start | bytes 196616 | tf_op jit(solution)/shard_map/ppermute | solution.py:370
  7.4 0.5 %collective-permute-start.5 = (bf16[2,64,256]{2,1,0:T(8,128)(2,1)S(1)}, bf16[2,64,256]{2,1,0:T(8,128)(2,1)S(1)}, u32[]{:S(2)}, u32[]{:S(2)}) collective-permute-start(bf16[2,64,256]{2,1,0:T(8,128)(2,1)S(1)} %get-tuple-element.61), channel_id=1, source_target_pairs={{0,4},{1,5},{2,6},{3,7},{4,0},{5,1},{6,2},{7,3},{8,12},{9,13},{10,... | collective-permute-start | bytes 196616 | tf_op jit(solution)/shard_map/ppermute | solution.py:370
  7.9 0.1 collective-permute-start.6
  8.0 3.0 %collective-permute-start.1 = (bf16[192,128]{1,0:T(8,128)(2,1)S(1)}, bf16[192,128]{1,0:T(8,128)(2,1)S(1)}, u32[]{:S(2)}, u32[]{:S(2)}) collective-permute-start(bf16[192,128]{1,0:T(8,128)(2,1)S(1)} %get-tuple-element.54), channel_id=1, source_target_pairs={{0,16},{8,24},{16,0},{24,8},{1,17},{9,25},{17,1},{25,9},{2,18},{10... | collective-permute-start | bytes 147464 | tf_op jit(solution)/shard_map/ppermute | solution.py:361
  11.0 1.3 %collective-permute-start.2 = (bf16[192,128]{1,0:T(8,128)(2,1)S(1)}, bf16[192,128]{1,0:T(8,128)(2,1)S(1)}, u32[]{:S(2)}, u32[]{:S(2)}) collective-permute-start(bf16[192,128]{1,0:T(8,128)(2,1)S(1)} %get-tuple-element.55), channel_id=1, source_target_pairs={{0,24},{8,16},{16,8},{24,0},{1,25},{9,17},{17,9},{25,1},{2,26},{10... | collective-permute-start | bytes 147464 | tf_op jit(solution)/shard_map/ppermute | solution.py:361
  12.3 0.0 collective-permute-done.4.rest_1_
  12.3 0.2 collective-permute-start.3
  12.6 0.0 collective-permute-done.5.rest_2_
  12.6 0.0 collective-permute-done.6.rest_3_
  12.6 0.3 shard_map.126
  12.8 3.2 %collective-permute-start.7 = (bf16[192,128]{1,0:T(8,128)(2,1)S(1)}, bf16[192,128]{1,0:T(8,128)(2,1)S(1)}, u32[]{:S(2)}, u32[]{:S(2)}) collective-permute-start(bf16[192,128]{1,0:T(8,128)(2,1)S(1)} %get-tuple-element.64), channel_id=1, source_target_pairs={{0,24},{8,16},{16,8},{24,0},{1,25},{9,17},{17,9},{25,1},{2,26},{10... | collective-permute-start | bytes 147464 | tf_op jit(solution)/shard_map/ppermute | solution.py:361
  16.1 0.1 collective-permute-start.8
  16.2 0.0 collective-permute-done.1.rest_0_
  16.2 1.1 %collective-permute-start.9 = (bf16[192,128]{1,0:T(8,128)(2,1)S(1)}, bf16[192,128]{1,0:T(8,128)(2,1)S(1)}, u32[]{:S(2)}, u32[]{:S(2)}) collective-permute-start(bf16[192,128]{1,0:T(8,128)(2,1)S(1)} %get-tuple-element.66), channel_id=1, source_target_pairs={{0,8},{8,0},{16,24},{24,16},{1,9},{9,1},{17,25},{25,17},{2,10},{10... | collective-permute-start | bytes 147464 | tf_op jit(solution)/shard_map/ppermute | solution.py:361
  17.3 0.2 collective-permute-done.2.rest_1_
  17.5 0.0 collective-permute-done.3.rest_2_
  17.5 1.8 %shard_map.125.own_ref = f32[128,1024]{1,0:T(8,128)S(1)} custom-call(s32[1]{0:T(128)} %bitcast.me_ref, bf16[192,512]{1,0:T(8,128)(2,1)} %bitcast.22, bf16[768,1024]{1,0:T(8,128)(2,1)} %weight_hbm.1, bf16[192,128]{1,0:T(8,128)(2,1)S(1)} %collective-permute-done.1.rest_0_, bf16[192,128]{1,0:T(8,128)(2,1)S(1)} %collective-permute-done.2.rest_1_, ...), custom_call_target="tpu_custom_call" | custom-call | flops 201326592 | bytes 2097152 | tf_op jit(solution)/shard_map/pallas_call | solution.py:33
  19.3 0.0 copy-start.2
  19.3 0.0 collective-permute-done.7.rest_1_
  19.3 0.0 copy-done
  19.3 0.3 shard_map.127.early_ref
  19.6 1.6 %collective-permute-done.8.rest_0_ = bf16[192,128]{1,0:T(8,128)(2,1)S(1)} collective-permute-done((bf16[192,128]{1,0:T(8,128)(2,1)S(1)}, bf16[192,128]{1,0:T(8,128)(2,1)S(1)}, u32[]{:S(2)}, u32[]{:S(2)}) %collective-permute-start.8) | collective-permute-done | bytes 49184 | tf_op jit(solution)/shard_map/ppermute | solution.py:361
  21.2 0.0 collective-permute-done.9.rest_1_
  21.2 0.6 %shard_map.128 = (bf16[128,1024]{1,0:T(8,128)(2,1)S(1)}, bf16[153,128]{1,0:T(8,128)(2,1)S(1)}, bf16[153,128]{1,0:T(8,128)(2,1)S(1)}, bf16[153,128]{1,0:T(8,128)(2,1)S(1)}, bf16[153,128]{1,0:T(8,128)(2,1)S(1)}) custom-call(s32[1]{0:T(128)} %bitcast.me_ref, bf16[768,1024]{1,0:T(8,128)(2,1)S(1)} %copy-done, bf16[153,1024]{1,0:T(8,128)(2,1)S(1)} %bitcast.20, ...), custom_call_target="tpu_custom_call" | custom-call | flops 100663296 | bytes 2097152 | tf_op jit(solution)/shard_map/pallas_call | solution.py:33
  21.8 2.2 %collective-permute-start.10 = (bf16[153,128]{1,0:T(8,128)(2,1)S(1)}, bf16[153,128]{1,0:T(8,128)(2,1)S(1)}, u32[]{:S(2)}, u32[]{:S(2)}) collective-permute-start(bf16[153,128]{1,0:T(8,128)(2,1)S(1)} %get-tuple-element.71), channel_id=1, source_target_pairs={{0,24},{8,16},{16,8},{24,0},{1,25},{9,17},{17,9},{25,1},{2,26},{10... | collective-permute-start | bytes 117512 | tf_op jit(solution)/shard_map/ppermute | solution.py:361
  24.0 0.0 collective-permute-start.11
  24.0 2.3 %collective-permute-start.12 = (bf16[153,128]{1,0:T(8,128)(2,1)S(1)}, bf16[153,128]{1,0:T(8,128)(2,1)S(1)}, u32[]{:S(2)}, u32[]{:S(2)}) collective-permute-start(bf16[153,128]{1,0:T(8,128)(2,1)S(1)} %get-tuple-element.73), channel_id=1, source_target_pairs={{0,8},{8,0},{16,24},{24,16},{1,9},{9,1},{17,25},{25,17},{2,10},{10... | collective-permute-start | bytes 117512 | tf_op jit(solution)/shard_map/ppermute | solution.py:361
  26.3 0.9 %shard_map.131.hits_ref.after = bf16[128,512]{1,0:T(8,128)(2,1)S(1)} custom-call(bf16[153,128]{1,0:T(8,128)(2,1)S(1)} %get-tuple-element.70.rest_0_.after, s32[1]{0:T(128)} %bitcast.me_ref, s32[1]{0:T(128)} %bitcast.4.part_ref, s32[8,4,16]{2,1,0:T(4,128)} %bitcast.26), custom_call_target="tpu_custom_call" | custom-call | bytes 524288 | tf_op jit(solution)/shard_map/pallas_call | solution.py:33
  27.2 0.7 %collective-permute-done.10.rest_1_ = bf16[153,128]{1,0:T(8,128)(2,1)S(1)} collective-permute-done((bf16[153,128]{1,0:T(8,128)(2,1)S(1)}, bf16[153,128]{1,0:T(8,128)(2,1)S(1)}, u32[]{:S(2)}, u32[]{:S(2)}) %collective-permute-start.10) | collective-permute-done | bytes 39200 | tf_op jit(solution)/shard_map/ppermute | solution.py:361
  27.9 1.1 %collective-permute-done.11.rest_2_ = bf16[153,128]{1,0:T(8,128)(2,1)S(1)} collective-permute-done((bf16[153,128]{1,0:T(8,128)(2,1)S(1)}, bf16[153,128]{1,0:T(8,128)(2,1)S(1)}, u32[]{:S(2)}, u32[]{:S(2)}) %collective-permute-start.11) | collective-permute-done | bytes 39200 | tf_op jit(solution)/shard_map/ppermute | solution.py:361
  29.0 0.0 collective-permute-done.12.rest_3_
  29.0 0.3 shard_map.132
  29.3 0.1 collective-permute-start.13
  29.4 1.2 %collective-permute-done.13.got_ref = bf16[4,16,256]{2,1,0:T(8,128)(2,1)S(1)} collective-permute-done((bf16[4,16,256]{2,1,0:T(8,128)(2,1)S(1)}, bf16[4,16,256]{2,1,0:T(8,128)(2,1)S(1)}, u32[]{:S(2)}, u32[]{:S(2)}) %collective-permute-start.13) | collective-permute-done | bytes 32800 | tf_op jit(solution)/shard_map/ppermute | solution.py:366
  30.6 2.4 %collective-permute-start.14 = (bf16[2,16,256]{2,1,0:T(8,128)(2,1)S(1)}, bf16[2,16,256]{2,1,0:T(8,128)(2,1)S(1)}, u32[]{:S(2)}, u32[]{:S(2)}) collective-permute-start(bf16[2,16,256]{2,1,0:T(8,128)(2,1)S(1)} %get-tuple-element.77), channel_id=1, source_target_pairs={{0,6},{1,7},{2,4},{3,5},{4,2},{5,3},{6,0},{7,1},{8,14},{9,15},{10,... | collective-permute-start | bytes 49160 | tf_op jit(solution)/shard_map/ppermute | solution.py:370
  33.0 0.4 collective-permute-start.15
  33.4 0.7 %collective-permute-start.16 = (bf16[2,16,256]{2,1,0:T(8,128)(2,1)S(1)}, bf16[2,16,256]{2,1,0:T(8,128)(2,1)S(1)}, u32[]{:S(2)}, u32[]{:S(2)}) collective-permute-start(bf16[2,16,256]{2,1,0:T(8,128)(2,1)S(1)} %get-tuple-element.79), channel_id=1, source_target_pairs={{0,2},{1,3},{2,0},{3,1},{4,6},{5,7},{6,4},{7,5},{8,10},{9,11},{10,... | collective-permute-start | bytes 49160 | tf_op jit(solution)/shard_map/ppermute | solution.py:370
  34.1 0.0 copy-done.1
  34.1 0.7 %shard_map.129 = (f32[153,128]{1,0:T(8,128)S(1)}, bf16[128,1024]{1,0:T(8,128)(2,1)}) custom-call(bf16[128,1024]{1,0:T(8,128)(2,1)S(1)} %get-tuple-element.67.hidden_ref, bf16[153,1024]{1,0:T(8,128)(2,1)S(1)} %bitcast.19), custom_call_target="tpu_custom_call" | custom-call | flops 40108032 | bytes 1048576 | tf_op jit(solution)/shard_map/pallas_call | solution.py:33
  34.8 0.2 shard_map.130.near_ref
  35.0 0.2 collective-permute-done.14.rest_1_
  35.2 1.5 %collective-permute-done.15.rest_2_ = bf16[2,16,256]{2,1,0:T(8,128)(2,1)S(1)} collective-permute-done((bf16[2,16,256]{2,1,0:T(8,128)(2,1)S(1)}, bf16[2,16,256]{2,1,0:T(8,128)(2,1)S(1)}, u32[]{:S(2)}, u32[]{:S(2)}) %collective-permute-start.15) | collective-permute-done | bytes 16416 | tf_op jit(solution)/shard_map/ppermute | solution.py:370
  36.7 0.4 collective-permute-done.16.rest_3_
  37.1 0.9 %shard_map.134 = f32[153,1,128]{2,1,0:T(1,128)} custom-call(s32[1]{0:T(128)} %bitcast.me_ref, f32[153,128]{1,0:T(8,128)S(1)} %shard_map.130.near_ref, bf16[4,8,16,128]{3,2,1,0:T(8,128)(2,1)S(1)} %get-tuple-element.58.edges_ref, f32[4,208,128]{2,1,0:T(8,128)S(1)} %get-tuple-element.57.sums_ref, bf16[2,16,256]{2,1,0:T(8,128)(2,1)S(1)} %get-tuple-element.76.rest_0_, ...), custom_call_target="tpu_custom_call" | custom-call | flops 5013504 | bytes 524288 | tf_op jit(solution)/shard_map/pallas_call | solution.py:33
  (5 shorter events, 0.0 us)
Async XLA Ops:
  1.9 1.7 %collective-permute-start = (bf16[4,64,256]{2,1,0:T(8,128)(2,1)S(1)}, bf16[4,64,256]{2,1,0:T(8,128)(2,1)S(1)}, u32[]{:S(2)}, u32[]{:S(2)}) collective-permute-start(bf16[4,64,256]{2,1,0:T(8,128)(2,1)S(1)} %get-tuple-element.50), channel_id=1, source_target_pairs={{0,1},{1,0},{2,3},{3,2},{4,5},{5,4},{6,7},{7,6},{8,9},{9,8},{10,11... | collective-permute-start | bytes 393224 | tf_op jit(solution)/shard_map/ppermute | solution.py:366
  3.7 8.7 %collective-permute-start.4 = (bf16[2,64,256]{2,1,0:T(8,128)(2,1)S(1)}, bf16[2,64,256]{2,1,0:T(8,128)(2,1)S(1)}, u32[]{:S(2)}, u32[]{:S(2)}) collective-permute-start(bf16[2,64,256]{2,1,0:T(8,128)(2,1)S(1)} %get-tuple-element.60), channel_id=1, source_target_pairs={{0,6},{1,7},{2,4},{3,5},{4,2},{5,3},{6,0},{7,1},{8,14},{9,15},{10,... | collective-permute-start | bytes 196616 | tf_op jit(solution)/shard_map/ppermute | solution.py:370
  7.4 5.2 %collective-permute-start.5 = (bf16[2,64,256]{2,1,0:T(8,128)(2,1)S(1)}, bf16[2,64,256]{2,1,0:T(8,128)(2,1)S(1)}, u32[]{:S(2)}, u32[]{:S(2)}) collective-permute-start(bf16[2,64,256]{2,1,0:T(8,128)(2,1)S(1)} %get-tuple-element.61), channel_id=1, source_target_pairs={{0,4},{1,5},{2,6},{3,7},{4,0},{5,1},{6,2},{7,3},{8,12},{9,13},{10,... | collective-permute-start | bytes 196616 | tf_op jit(solution)/shard_map/ppermute | solution.py:370
  7.9 4.7 %collective-permute-start.6 = (bf16[2,64,256]{2,1,0:T(8,128)(2,1)S(1)}, bf16[2,64,256]{2,1,0:T(8,128)(2,1)S(1)}, u32[]{:S(2)}, u32[]{:S(2)}) collective-permute-start(bf16[2,64,256]{2,1,0:T(8,128)(2,1)S(1)} %get-tuple-element.62), channel_id=1, source_target_pairs={{0,2},{1,3},{2,0},{3,1},{4,6},{5,7},{6,4},{7,5},{8,10},{9,11},{10,... | collective-permute-start | bytes 196616 | tf_op jit(solution)/shard_map/ppermute | solution.py:370
  8.0 8.2 %collective-permute-start.1 = (bf16[192,128]{1,0:T(8,128)(2,1)S(1)}, bf16[192,128]{1,0:T(8,128)(2,1)S(1)}, u32[]{:S(2)}, u32[]{:S(2)}) collective-permute-start(bf16[192,128]{1,0:T(8,128)(2,1)S(1)} %get-tuple-element.54), channel_id=1, source_target_pairs={{0,16},{8,24},{16,0},{24,8},{1,17},{9,25},{17,1},{25,9},{2,18},{10... | collective-permute-start | bytes 147464 | tf_op jit(solution)/shard_map/ppermute | solution.py:361
  11.0 6.5 %collective-permute-start.2 = (bf16[192,128]{1,0:T(8,128)(2,1)S(1)}, bf16[192,128]{1,0:T(8,128)(2,1)S(1)}, u32[]{:S(2)}, u32[]{:S(2)}) collective-permute-start(bf16[192,128]{1,0:T(8,128)(2,1)S(1)} %get-tuple-element.55), channel_id=1, source_target_pairs={{0,24},{8,16},{16,8},{24,0},{1,25},{9,17},{17,9},{25,1},{2,26},{10... | collective-permute-start | bytes 147464 | tf_op jit(solution)/shard_map/ppermute | solution.py:361
  12.3 5.1 %collective-permute-start.3 = (bf16[192,128]{1,0:T(8,128)(2,1)S(1)}, bf16[192,128]{1,0:T(8,128)(2,1)S(1)}, u32[]{:S(2)}, u32[]{:S(2)}) collective-permute-start(bf16[192,128]{1,0:T(8,128)(2,1)S(1)} %get-tuple-element.56), channel_id=1, source_target_pairs={{0,8},{8,0},{16,24},{24,16},{1,9},{9,1},{17,25},{25,17},{2,10},{10... | collective-permute-start | bytes 147464 | tf_op jit(solution)/shard_map/ppermute | solution.py:361
  12.6 6.7 %copy-start = (bf16[768,1024]{1,0:T(8,128)(2,1)S(1)}, bf16[768,1024]{1,0:T(8,128)(2,1)}, u32[]{:S(2)}) copy-start(bf16[768,1024]{1,0:T(8,128)(2,1)} %weight_ref.3) | copy-start | bytes 4718596
  12.8 6.4 %collective-permute-start.7 = (bf16[192,128]{1,0:T(8,128)(2,1)S(1)}, bf16[192,128]{1,0:T(8,128)(2,1)S(1)}, u32[]{:S(2)}, u32[]{:S(2)}) collective-permute-start(bf16[192,128]{1,0:T(8,128)(2,1)S(1)} %get-tuple-element.64), channel_id=1, source_target_pairs={{0,24},{8,16},{16,8},{24,0},{1,25},{9,17},{17,9},{25,1},{2,26},{10... | collective-permute-start | bytes 147464 | tf_op jit(solution)/shard_map/ppermute | solution.py:361
  16.1 5.2 %collective-permute-start.8 = (bf16[192,128]{1,0:T(8,128)(2,1)S(1)}, bf16[192,128]{1,0:T(8,128)(2,1)S(1)}, u32[]{:S(2)}, u32[]{:S(2)}) collective-permute-start(bf16[192,128]{1,0:T(8,128)(2,1)S(1)} %get-tuple-element.65), channel_id=1, source_target_pairs={{0,16},{8,24},{16,0},{24,8},{1,17},{9,25},{17,1},{25,9},{2,18},{10... | collective-permute-start | bytes 147464 | tf_op jit(solution)/shard_map/ppermute | solution.py:361
  16.2 5.1 %collective-permute-start.9 = (bf16[192,128]{1,0:T(8,128)(2,1)S(1)}, bf16[192,128]{1,0:T(8,128)(2,1)S(1)}, u32[]{:S(2)}, u32[]{:S(2)}) collective-permute-start(bf16[192,128]{1,0:T(8,128)(2,1)S(1)} %get-tuple-element.66), channel_id=1, source_target_pairs={{0,8},{8,0},{16,24},{24,16},{1,9},{9,1},{17,25},{25,17},{2,10},{10... | collective-permute-start | bytes 147464 | tf_op jit(solution)/shard_map/ppermute | solution.py:361
  19.3 2.0 %copy-start.2 = (bf16[1024,153]{0,1:T(8,128)(2,1)S(1)}, bf16[1024,153]{0,1:T(8,128)(2,1)}, u32[]{:S(2)}) copy-start(bf16[1024,153]{0,1:T(8,128)(2,1)} %param.21) | copy-start | bytes 940036
  21.2 12.8 %copy-start.1 = (bf16[1024,153]{0,1:T(8,128)(2,1)S(1)}, bf16[1024,153]{0,1:T(8,128)(2,1)}, u32[]{:S(2)}) copy-start(bf16[1024,153]{0,1:T(8,128)(2,1)} %param.20) | copy-start | bytes 940036
  21.8 6.1 %collective-permute-start.10 = (bf16[153,128]{1,0:T(8,128)(2,1)S(1)}, bf16[153,128]{1,0:T(8,128)(2,1)S(1)}, u32[]{:S(2)}, u32[]{:S(2)}) collective-permute-start(bf16[153,128]{1,0:T(8,128)(2,1)S(1)} %get-tuple-element.71), channel_id=1, source_target_pairs={{0,24},{8,16},{16,8},{24,0},{1,25},{9,17},{17,9},{25,1},{2,26},{10... | collective-permute-start | bytes 117512 | tf_op jit(solution)/shard_map/ppermute | solution.py:361
  24.0 5.0 %collective-permute-start.11 = (bf16[153,128]{1,0:T(8,128)(2,1)S(1)}, bf16[153,128]{1,0:T(8,128)(2,1)S(1)}, u32[]{:S(2)}, u32[]{:S(2)}) collective-permute-start(bf16[153,128]{1,0:T(8,128)(2,1)S(1)} %get-tuple-element.72), channel_id=1, source_target_pairs={{0,16},{8,24},{16,0},{24,8},{1,17},{9,25},{17,1},{25,9},{2,18},{10... | collective-permute-start | bytes 117512 | tf_op jit(solution)/shard_map/ppermute | solution.py:361
  24.0 5.0 %collective-permute-start.12 = (bf16[153,128]{1,0:T(8,128)(2,1)S(1)}, bf16[153,128]{1,0:T(8,128)(2,1)S(1)}, u32[]{:S(2)}, u32[]{:S(2)}) collective-permute-start(bf16[153,128]{1,0:T(8,128)(2,1)S(1)} %get-tuple-element.73), channel_id=1, source_target_pairs={{0,8},{8,0},{16,24},{24,16},{1,9},{9,1},{17,25},{25,17},{2,10},{10... | collective-permute-start | bytes 117512 | tf_op jit(solution)/shard_map/ppermute | solution.py:361
  29.3 1.3 %collective-permute-start.13 = (bf16[4,16,256]{2,1,0:T(8,128)(2,1)S(1)}, bf16[4,16,256]{2,1,0:T(8,128)(2,1)S(1)}, u32[]{:S(2)}, u32[]{:S(2)}) collective-permute-start(bf16[4,16,256]{2,1,0:T(8,128)(2,1)S(1)} %get-tuple-element.75), channel_id=1, source_target_pairs={{0,1},{1,0},{2,3},{3,2},{4,5},{5,4},{6,7},{7,6},{8,9},{9,8},{10,11... | collective-permute-start | bytes 98312 | tf_op jit(solution)/shard_map/ppermute | solution.py:366
  30.6 4.6 %collective-permute-start.14 = (bf16[2,16,256]{2,1,0:T(8,128)(2,1)S(1)}, bf16[2,16,256]{2,1,0:T(8,128)(2,1)S(1)}, u32[]{:S(2)}, u32[]{:S(2)}) collective-permute-start(bf16[2,16,256]{2,1,0:T(8,128)(2,1)S(1)} %get-tuple-element.77), channel_id=1, source_target_pairs={{0,6},{1,7},{2,4},{3,5},{4,2},{5,3},{6,0},{7,1},{8,14},{9,15},{10,... | collective-permute-start | bytes 49160 | tf_op jit(solution)/shard_map/ppermute | solution.py:370
  33.0 3.7 %collective-permute-start.15 = (bf16[2,16,256]{2,1,0:T(8,128)(2,1)S(1)}, bf16[2,16,256]{2,1,0:T(8,128)(2,1)S(1)}, u32[]{:S(2)}, u32[]{:S(2)}) collective-permute-start(bf16[2,16,256]{2,1,0:T(8,128)(2,1)S(1)} %get-tuple-element.78), channel_id=1, source_target_pairs={{0,4},{1,5},{2,6},{3,7},{4,0},{5,1},{6,2},{7,3},{8,12},{9,13},{10,... | collective-permute-start | bytes 49160 | tf_op jit(solution)/shard_map/ppermute | solution.py:370
  33.4 3.7 %collective-permute-start.16 = (bf16[2,16,256]{2,1,0:T(8,128)(2,1)S(1)}, bf16[2,16,256]{2,1,0:T(8,128)(2,1)S(1)}, u32[]{:S(2)}, u32[]{:S(2)}) collective-permute-start(bf16[2,16,256]{2,1,0:T(8,128)(2,1)S(1)} %get-tuple-element.79), channel_id=1, source_target_pairs={{0,2},{1,3},{2,0},{3,1},{4,6},{5,7},{6,4},{7,5},{8,10},{9,11},{10,... | collective-permute-start | bytes 49160 | tf_op jit(solution)/shard_map/ppermute | solution.py:370

commit v17 on v16

--- a/solution.py
+++ b/solution.py
@@ -217,17 +217,18 @@
         ).astype(bf16)
 
 
-def mean_kernel(me_ref, sums_ref, edges_ref, *rest):
+def mean_kernel(me_ref, sums_ref, edges_ref, held_ref, *rest):
     groups, parts, slots, rows = edges_ref.shape
     arrived, outs = rest[: parts // 2], rest[parts // 2 :]
-    width = outs[0].shape[0]
+    width = held_ref.shape[0]
     for k in range(groups):
         group = ahead(me_ref[0], groups, k)
         span = pl.ds(pl.multiple_of(group * slots, slots), slots)
         far = jnp.concatenate([x[:, span, :].reshape(2 * slots, -1) for x in arrived], axis=0)
         far = dot(far, edges_ref[group].reshape(parts * slots, rows), FIRST)
         total = sums_ref[group, :width, :] + far[:width]
-        outs[k][...] = (total / sums_ref[group, width : width + 1, :]).astype(bf16)
+        outs[k][:width, :] = (total / sums_ref[group, width : width + 1, :]).astype(bf16)
+    outs[groups - 1][width:, :] = held_ref[...]
 
 
 def rows_from(me, groups, k, width, near=False):
@@ -235,14 +236,15 @@
 
 
 def self_kernel(me_ref, features_hbm, weight_hbm, *rest):
-    blocks, (out_ref, own_ref, weight_ref, sems) = rest[:-4], rest[-4:]
-    groups, (width, rows) = len(blocks) + 1, own_ref.shape
+    blocks, (out_ref, near_ref, own_ref, weight_ref, sems) = rest[:-5], rest[-5:]
+    groups, (width, rows) = len(blocks) + 2, own_ref.shape
     me = me_ref[0]
     spans = [rows_from(me, groups, k, width, True) for k in range(groups)]
-    own, *weights = fetch(
+    own, *weights, near = fetch(
         sems,
         (features_hbm.at[:, pl.ds(pl.multiple_of(me * rows, rows), rows)], own_ref),
-        *[(weight_hbm.at[span, :], weight_ref.at[span, :]) for span in spans],
+        *[(weight_hbm.at[span, :], weight_ref.at[span, :]) for span in spans[:-1]],
+        (weight_hbm.at[spans[-1], :], near_ref),
     )
     own.wait()
     total = jnp.zeros(out_ref.shape, f32)
@@ -250,23 +252,27 @@
         weight.wait()
         total = total + dot(block[...], weight_ref[span, :], FIRST)
     out_ref[...] = total
-
-
-def add_blocks(total, me, groups, first, blocks, weight_ref):
-    width = blocks[0].shape[0]
+    near.wait()
+
+
+def add_blocks(total, me, groups, first, blocks, weight_ref, width):
     for k, block in enumerate(blocks, first):
-        total = total + dot(block[...], weight_ref[rows_from(me, groups, k, width), :], FIRST)
+        span = rows_from(me, groups, k, width)
+        total = total + dot(block[:width, :], weight_ref[span, :], FIRST)
     return total
 
 
 def early_kernel(groups, me_ref, weight_ref, own_ref, *rest):
     blocks, out_ref = rest[:-1], rest[-1]
-    out_ref[...] = add_blocks(own_ref[...], me_ref[0], groups, 0, blocks, weight_ref)
-
-
-def hidden_kernel(groups, me_ref, weight_ref, out_weight_ref, early_ref, *rest):
+    width = blocks[0].shape[0]
+    out_ref[...] = add_blocks(own_ref[...], me_ref[0], groups, 0, blocks, weight_ref, width)
+
+
+def hidden_kernel(groups, me_ref, weight_ref, near_ref, out_weight_ref, early_ref, *rest):
     blocks, (hidden_ref, *copies) = rest[: groups - 2], rest[groups - 2 :]
-    total = add_blocks(early_ref[...], me_ref[0], groups, 2, blocks, weight_ref)
+    width = near_ref.shape[0]
+    total = add_blocks(early_ref[...], me_ref[0], groups, 2, blocks, weight_ref, width)
+    total = total + dot(blocks[-1][width:, :], near_ref[...], FIRST)
     hidden = jnp.maximum(total, 0.0).astype(bf16)
     hidden_ref[...] = hidden
     projected = dot(out_weight_ref[...], hidden, LAST).astype(bf16)
@@ -418,10 +424,11 @@
         1 << 20,
         4 if groups <= 4 else 16,
     )(me, part, table, *passed)
+    *feature_blocks, near_block = feature_blocks
     paired = call(
         pair_kernel,
-        (shape(2, groups * slots, lanes),) * chips + (shape(width, rows),) * (groups - 1),
-        [VM] * (2 + groups),
+        (shape(2, groups * slots, lanes),) * chips + (shape(width, rows),) * (groups - 2),
+        [VM] * (1 + groups),
         (),
         0,
         1 << 20,
@@ -430,24 +437,24 @@
     feature_blocks = shift(paired[chips:], near=True)
     means = call(
         mean_kernel,
-        (shape(width, rows),) * groups,
-        [SM] + [VM] * (2 + chips),
+        (shape(width, rows),) * (groups - 1) + (shape(2 * width, rows),),
+        [SM] + [VM] * (3 + chips),
         (),
         2 * nodes * parts * slots * width,
         1 << 20,
-    )(me, sums, edges, *arrived)
+    )(me, sums, edges, near_block, *arrived)
     means = [means[0]] + shift(means[1:])
-    own = call(
+    own, near_weight = call(
         self_kernel,
-        shape(rows, hid, dtype=f32),
-        [SM, HB, HB] + [VM] * (groups - 1),
+        (shape(rows, hid, dtype=f32), shape(width, hid)),
+        [SM, HB, HB] + [VM] * (groups - 2),
         [
             pltpu.VMEM((width, rows), bf16),
             pltpu.VMEM(self_one.shape, bf16),
             pltpu.SemaphoreType.DMA((1 + groups,)),
         ],
-        2 * rows * hid * groups * width,
-        2 << 20,
+        100 * rows * hid * groups * width,
+        100 << 20,
     )(me, feature_rows, self_one, *feature_blocks)
     early = call(
         functools.partial(early_kernel, groups),
@@ -460,11 +467,11 @@
     hidden, *projected = call(
         functools.partial(hidden_kernel, groups),
         (shape(rows, hid),) + (shape(classes, rows),) * groups,
-        [SM] + [VM] * (1 + groups),
+        [SM] + [VM] * (2 + groups),
         (),
         rows * hid * groups * width,
         2 << 20,
-    )(me, neigh_one, neigh_out.T, early, *means[2:])
+    )(me, neigh_one, near_weight, neigh_out.T, early, *means[2:])
     hits = call(
         hits_kernel,
         shape(parts * slots, nodes),

time: 38.2 us -> 38.9 us (1.018)
  waiting for transfers between devices: 6.93 us -> 7.91 us
    ppermute x9 -> x8, waiting for transfers between devices: 3.63 us -> 4.56 us  [shift(): lax.ppermute(block, 'feat', [(i, ahead(i, groups, k, near)) for i in rang...]
    ppermute x9 -> x8, starting transfers between devices: 13.5 us -> 13.2 us  [shift(): lax.ppermute(block, 'feat', [(i, ahead(i, groups, k, near)) for i in rang...]
  transfers between devices with their start and end apart: 17 -> 16, of which waited for: 8 -> 9; matrix products, arithmetic and copies ran while one was open for 0% -> 0% of each run, Pallas kernels for 14% -> 14%
where the time goes in v17:
time: 38.9 us; the launch traced here: 38.6 us
  starting transfers between devices  21.6 us (56%)
  Pallas kernels  8.3 us (21%)
  waiting for transfers between devices  7.91 us (20%)
  between operations  0.78 us (2%)
    ppermute x8, starting transfers between devices, shift(): lax.ppermute(block, 'feat', [(i, ahead(i, groups, k, near)) for i in rang...  13.2 us
    pallas_call x13, Pallas kernels, placed(): run(*(pltpu.with_memory_space_constraint(value, pltpu.HBM) if spec is HB...  8.3 us
    ppermute x6, starting transfers between devices, to_chips(): lax.ppermute(blocks[j], 'dom', [(d, next_to(d // 2, j, chips) * 2 + d % 2...  7.8 us
    ppermute x8, waiting for transfers between devices, shift(): lax.ppermute(block, 'feat', [(i, ahead(i, groups, k, near)) for i in rang...  4.56 us
    ppermute x6, waiting for transfers between devices, to_chips(): lax.ppermute(blocks[j], 'dom', [(d, next_to(d // 2, j, chips) * 2 + d % 2...  2.15 us
    ppermute x2, waiting for transfers between devices, to_mate(): return lax.ppermute(value, 'dom', [(d, d ^ 1) for d in range(parts)])  1.2 us
  transfers between devices with their start and end apart: 16, of which 9 were waited for; matrix products, arithmetic and copies ran while one was open for 0% of the time, Pallas kernels for 14%

profile of v17, /device:TPU:0, one launch (start us, length us, event | category | flops | bytes accessed | tf_op | source)
XLA Modules:
  0.0 38.6 jit_solution(8924788323923529420)
XLA Ops:
  0.6 1.3 %shard_map.122 = (bf16[4,64,256]{2,1,0:T(8,128)(2,1)S(1)}, bf16[256,512]{1,0:T(8,128)(2,1)S(1)}, s32[8,4,16]{2,1,0:T(4,128)S(1)}, bf16[12,128,128]{2,1,0:T(8,128...) custom-call(s32[1]{0:T(128)} %bitcast.3.part_ref, ...), custom_call_target="tpu_custom_call" | custom-call | flops 100663296 | bytes 1048576 | tf_op jit(solution)/shard_map/pallas_call | solution.py:33
  1.9 0.5 %collective-permute-start = (bf16[4,64,256]{2,1,0:T(8,128)(2,1)S(1)}, bf16[4,64,256]{2,1,0:T(8,128)(2,1)S(1)}, u32[]{:S(2)}, u32[]{:S(2)}) collective-permute-start(bf16[4,64,256]{2,1,0:T(8,128)(2,1)S(1)} %get-tuple-element.51), channel_id=1, source_target_pairs={{0,1},{1,0},{2,3},{3,2},{4,5},{5,4},{6,7},{7,6},{8,9},{9,8},{10,11... | collective-permute-start | bytes 393224 | tf_op jit(solution)/shard_map/ppermute | solution.py:372
  2.5 1.2 %shard_map.123 = (f32[4,208,128]{2,1,0:T(8,128)S(1)}, bf16[4,8,16,128]{3,2,1,0:T(8,128)(2,1)S(1)}, bf16[128,512]{1,0:T(8,128)(2,1)S(1)}, bf16[4,64,256]{2,1,0:T(...) custom-call(s32[1]{0:T(128)} %bitcast.me_ref, ...), custom_call_target="tpu_custom_call" | custom-call | flops 100663296 | bytes 1048576 | tf_op jit(solution)/shard_map/pallas_call | solution.py:33
  3.6 0.0 collective-permute-done.got_ref
  3.7 3.7 %collective-permute-start.3 = (bf16[2,64,256]{2,1,0:T(8,128)(2,1)S(1)}, bf16[2,64,256]{2,1,0:T(8,128)(2,1)S(1)}, u32[]{:S(2)}, u32[]{:S(2)}) collective-permute-start(bf16[2,64,256]{2,1,0:T(8,128)(2,1)S(1)} %get-tuple-element.62), channel_id=1, source_target_pairs={{0,6},{1,7},{2,4},{3,5},{4,2},{5,3},{6,0},{7,1},{8,14},{9,15},{10,... | collective-permute-start | bytes 196616 | tf_op jit(solution)/shard_map/ppermute | solution.py:376
  7.3 0.5 %collective-permute-start.4 = (bf16[2,64,256]{2,1,0:T(8,128)(2,1)S(1)}, bf16[2,64,256]{2,1,0:T(8,128)(2,1)S(1)}, u32[]{:S(2)}, u32[]{:S(2)}) collective-permute-start(bf16[2,64,256]{2,1,0:T(8,128)(2,1)S(1)} %get-tuple-element.63), channel_id=1, source_target_pairs={{0,4},{1,5},{2,6},{3,7},{4,0},{5,1},{6,2},{7,3},{8,12},{9,13},{10,... | collective-permute-start | bytes 196616 | tf_op jit(solution)/shard_map/ppermute | solution.py:376
  7.9 0.1 collective-permute-start.5
  8.0 3.0 %collective-permute-start.1 = (bf16[192,128]{1,0:T(8,128)(2,1)S(1)}, bf16[192,128]{1,0:T(8,128)(2,1)S(1)}, u32[]{:S(2)}, u32[]{:S(2)}) collective-permute-start(bf16[192,128]{1,0:T(8,128)(2,1)S(1)} %get-tuple-element.54), channel_id=1, source_target_pairs={{0,16},{8,24},{16,0},{24,8},{1,17},{9,25},{17,1},{25,9},{2,18},{10... | collective-permute-start | bytes 147464 | tf_op jit(solution)/shard_map/ppermute | solution.py:367
  11.0 1.3 %collective-permute-start.2 = (bf16[192,128]{1,0:T(8,128)(2,1)S(1)}, bf16[192,128]{1,0:T(8,128)(2,1)S(1)}, u32[]{:S(2)}, u32[]{:S(2)}) collective-permute-start(bf16[192,128]{1,0:T(8,128)(2,1)S(1)} %get-tuple-element.55), channel_id=1, source_target_pairs={{0,24},{8,16},{16,8},{24,0},{1,25},{9,17},{17,9},{25,1},{2,26},{10... | collective-permute-start | bytes 147464 | tf_op jit(solution)/shard_map/ppermute | solution.py:367
  12.3 0.0 collective-permute-done.3.rest_1_
  12.3 0.0 collective-permute-done.4.rest_2_
  12.3 0.0 collective-permute-done.5.rest_3_
  12.3 0.3 shard_map.126
  12.6 3.4 %collective-permute-start.6 = (bf16[192,128]{1,0:T(8,128)(2,1)S(1)}, bf16[192,128]{1,0:T(8,128)(2,1)S(1)}, u32[]{:S(2)}, u32[]{:S(2)}) collective-permute-start(bf16[192,128]{1,0:T(8,128)(2,1)S(1)} %get-tuple-element.66), channel_id=1, source_target_pairs={{0,24},{8,16},{16,8},{24,0},{1,25},{9,17},{17,9},{25,1},{2,26},{10... | collective-permute-start | bytes 147464 | tf_op jit(solution)/shard_map/ppermute | solution.py:367
  16.1 0.0 collective-permute-start.7
  16.1 0.0 copy-start
  16.1 1.0 %collective-permute-start.8 = (bf16[384,128]{1,0:T(8,128)(2,1)S(1)}, bf16[384,128]{1,0:T(8,128)(2,1)S(1)}, u32[]{:S(2)}, u32[]{:S(2)}) collective-permute-start(bf16[384,128]{1,0:T(8,128)(2,1)S(1)} %get-tuple-element.68), channel_id=1, source_target_pairs={{0,8},{8,0},{16,24},{24,16},{1,9},{9,1},{17,25},{25,17},{2,10},{10... | collective-permute-start | bytes 294920 | tf_op jit(solution)/shard_map/ppermute | solution.py:367
  17.1 0.0 collective-permute-done.1.rest_0_
  17.1 0.1 collective-permute-done.2.rest_1_
  17.2 1.7 %shard_map.125 = (f32[128,1024]{1,0:T(8,128)S(1)}, bf16[192,1024]{1,0:T(8,128)(2,1)S(1)}) custom-call(s32[1]{0:T(128)} %bitcast.me_ref, bf16[192,512]{1,0:T(8,128)(2,1)} %bitcast.23, bf16[768,1024]{1,0:T(8,128)(2,1)} %weight_hbm.1, bf16[192,128]{1,0:T(8,128)(2,1)S(1)} %collective-permute-done.1.rest_0_, bf16[192,128]{1,0:T(8,128)(2,1)S(1)} %collective-permute-done.2.rest_1_), custom_call_target="tpu_custom_call" | custom-call | flops 10066329600 | bytes 104857600 | tf_op jit(solution)/shard_map/pallas_call | solution.py:33
  18.8 0.0 copy-start.1
  18.8 0.0 collective-permute-done.6.rest_1_
  18.9 0.0 copy-done
  18.9 0.3 shard_map.127.early_ref
  19.2 2.0 %collective-permute-done.7.rest_0_ = bf16[192,128]{1,0:T(8,128)(2,1)S(1)} collective-permute-done((bf16[192,128]{1,0:T(8,128)(2,1)S(1)}, bf16[192,128]{1,0:T(8,128)(2,1)S(1)}, u32[]{:S(2)}, u32[]{:S(2)}) %collective-permute-start.7) | collective-permute-done | bytes 49184 | tf_op jit(solution)/shard_map/ppermute | solution.py:367
  21.2 0.1 collective-permute-done.8.rest_1_
  21.3 0.0 copy-done.1
  21.3 0.6 %shard_map.128 = (bf16[128,1024]{1,0:T(8,128)(2,1)S(1)}, bf16[153,128]{1,0:T(8,128)(2,1)S(1)}, bf16[153,128]{1,0:T(8,128)(2,1)S(1)}, bf16[153,128]{1,0:T(8,128)(2,1)S(1)}, bf16[153,128]{1,0:T(8,128)(2,1)S(1)}) custom-call(s32[1]{0:T(128)} %bitcast.me_ref, bf16[768,1024]{1,0:T(8,128)(2,1)S(1)} %copy-done, bf16[192,1024]{1,0:T(8,128)(2,1)S(1)} %get-tuple-element.56.near_ref, ...), custom_call_target="tpu_custom_call" | custom-call | flops 100663296 | bytes 2097152 | tf_op jit(solution)/shard_map/pallas_call | solution.py:33
  21.9 2.6 %collective-permute-start.9 = (bf16[153,128]{1,0:T(8,128)(2,1)S(1)}, bf16[153,128]{1,0:T(8,128)(2,1)S(1)}, u32[]{:S(2)}, u32[]{:S(2)}) collective-permute-start(bf16[153,128]{1,0:T(8,128)(2,1)S(1)} %get-tuple-element.73), channel_id=1, source_target_pairs={{0,24},{8,16},{16,8},{24,0},{1,25},{9,17},{17,9},{25,1},{2,26},{10... | collective-permute-start | bytes 117512 | tf_op jit(solution)/shard_map/ppermute | solution.py:367
  24.4 0.0 collective-permute-start.10
  24.4 1.9 %collective-permute-start.11 = (bf16[153,128]{1,0:T(8,128)(2,1)S(1)}, bf16[153,128]{1,0:T(8,128)(2,1)S(1)}, u32[]{:S(2)}, u32[]{:S(2)}) collective-permute-start(bf16[153,128]{1,0:T(8,128)(2,1)S(1)} %get-tuple-element.75), channel_id=1, source_target_pairs={{0,8},{8,0},{16,24},{24,16},{1,9},{9,1},{17,25},{25,17},{2,10},{10... | collective-permute-start | bytes 117512 | tf_op jit(solution)/shard_map/ppermute | solution.py:367
  26.3 0.9 %shard_map.131.hits_ref.after = bf16[128,512]{1,0:T(8,128)(2,1)S(1)} custom-call(bf16[153,128]{1,0:T(8,128)(2,1)S(1)} %get-tuple-element.72.rest_0_.after, s32[1]{0:T(128)} %bitcast.me_ref, s32[1]{0:T(128)} %bitcast.3.part_ref, s32[8,4,16]{2,1,0:T(4,128)} %bitcast.26), custom_call_target="tpu_custom_call" | custom-call | bytes 524288 | tf_op jit(solution)/shard_map/pallas_call | solution.py:33
  27.2 0.5 %collective-permute-done.9.rest_1_ = bf16[153,128]{1,0:T(8,128)(2,1)S(1)} collective-permute-done((bf16[153,128]{1,0:T(8,128)(2,1)S(1)}, bf16[153,128]{1,0:T(8,128)(2,1)S(1)}, u32[]{:S(2)}, u32[]{:S(2)}) %collective-permute-start.9) | collective-permute-done | bytes 39200 | tf_op jit(solution)/shard_map/ppermute | solution.py:367
  27.7 1.9 %collective-permute-done.10.rest_2_ = bf16[153,128]{1,0:T(8,128)(2,1)S(1)} collective-permute-done((bf16[153,128]{1,0:T(8,128)(2,1)S(1)}, bf16[153,128]{1,0:T(8,128)(2,1)S(1)}, u32[]{:S(2)}, u32[]{:S(2)}) %collective-permute-start.10) | collective-permute-done | bytes 39200 | tf_op jit(solution)/shard_map/ppermute | solution.py:367
  29.6 0.0 collective-permute-done.11.rest_3_
  29.6 0.3 shard_map.132
  29.9 0.1 collective-permute-start.12
  30.0 1.2 %collective-permute-done.12.got_ref = bf16[4,16,256]{2,1,0:T(8,128)(2,1)S(1)} collective-permute-done((bf16[4,16,256]{2,1,0:T(8,128)(2,1)S(1)}, bf16[4,16,256]{2,1,0:T(8,128)(2,1)S(1)}, u32[]{:S(2)}, u32[]{:S(2)}) %collective-permute-start.12) | collective-permute-done | bytes 32800 | tf_op jit(solution)/shard_map/ppermute | solution.py:372
  31.2 1.8 %collective-permute-start.13 = (bf16[2,16,256]{2,1,0:T(8,128)(2,1)S(1)}, bf16[2,16,256]{2,1,0:T(8,128)(2,1)S(1)}, u32[]{:S(2)}, u32[]{:S(2)}) collective-permute-start(bf16[2,16,256]{2,1,0:T(8,128)(2,1)S(1)} %get-tuple-element.79), channel_id=1, source_target_pairs={{0,6},{1,7},{2,4},{3,5},{4,2},{5,3},{6,0},{7,1},{8,14},{9,15},{10,... | collective-permute-start | bytes 49160 | tf_op jit(solution)/shard_map/ppermute | solution.py:376
  33.0 1.1 %collective-permute-start.14 = (bf16[2,16,256]{2,1,0:T(8,128)(2,1)S(1)}, bf16[2,16,256]{2,1,0:T(8,128)(2,1)S(1)}, u32[]{:S(2)}, u32[]{:S(2)}) collective-permute-start(bf16[2,16,256]{2,1,0:T(8,128)(2,1)S(1)} %get-tuple-element.80), channel_id=1, source_target_pairs={{0,4},{1,5},{2,6},{3,7},{4,0},{5,1},{6,2},{7,3},{8,12},{9,13},{10,... | collective-permute-start | bytes 49160 | tf_op jit(solution)/shard_map/ppermute | solution.py:376
  34.0 0.6 %collective-permute-start.15 = (bf16[2,16,256]{2,1,0:T(8,128)(2,1)S(1)}, bf16[2,16,256]{2,1,0:T(8,128)(2,1)S(1)}, u32[]{:S(2)}, u32[]{:S(2)}) collective-permute-start(bf16[2,16,256]{2,1,0:T(8,128)(2,1)S(1)} %get-tuple-element.81), channel_id=1, source_target_pairs={{0,2},{1,3},{2,0},{3,1},{4,6},{5,7},{6,4},{7,5},{8,10},{9,11},{10,... | collective-permute-start | bytes 49160 | tf_op jit(solution)/shard_map/ppermute | solution.py:376
  34.7 0.0 copy-done.2
  34.7 0.7 %shard_map.129 = (f32[153,128]{1,0:T(8,128)S(1)}, bf16[128,1024]{1,0:T(8,128)(2,1)}) custom-call(bf16[128,1024]{1,0:T(8,128)(2,1)S(1)} %get-tuple-element.69.hidden_ref, bf16[153,1024]{1,0:T(8,128)(2,1)S(1)} %bitcast.20), custom_call_target="tpu_custom_call" | custom-call | flops 40108032 | bytes 1048576 | tf_op jit(solution)/shard_map/pallas_call | solution.py:33
  35.4 0.2 shard_map.130.near_ref
  35.6 0.2 collective-permute-done.13.rest_1_
  35.8 0.9 %collective-permute-done.14.rest_2_ = bf16[2,16,256]{2,1,0:T(8,128)(2,1)S(1)} collective-permute-done((bf16[2,16,256]{2,1,0:T(8,128)(2,1)S(1)}, bf16[2,16,256]{2,1,0:T(8,128)(2,1)S(1)}, u32[]{:S(2)}, u32[]{:S(2)}) %collective-permute-start.14) | collective-permute-done | bytes 16416 | tf_op jit(solution)/shard_map/ppermute | solution.py:376
  36.7 1.1 %collective-permute-done.15.rest_3_ = bf16[2,16,256]{2,1,0:T(8,128)(2,1)S(1)} collective-permute-done((bf16[2,16,256]{2,1,0:T(8,128)(2,1)S(1)}, bf16[2,16,256]{2,1,0:T(8,128)(2,1)S(1)}, u32[]{:S(2)}, u32[]{:S(2)}) %collective-permute-start.15) | collective-permute-done | bytes 16416 | tf_op jit(solution)/shard_map/ppermute | solution.py:376
  37.8 0.9 %shard_map.134 = f32[153,1,128]{2,1,0:T(1,128)} custom-call(s32[1]{0:T(128)} %bitcast.me_ref, f32[153,128]{1,0:T(8,128)S(1)} %shard_map.130.near_ref, bf16[4,8,16,128]{3,2,1,0:T(8,128)(2,1)S(1)} %get-tuple-element.59.edges_ref, f32[4,208,128]{2,1,0:T(8,128)S(1)} %get-tuple-element.58.sums_ref, bf16[2,16,256]{2,1,0:T(8,128)(2,1)S(1)} %get-tuple-element.78.rest_0_, ...), custom_call_target="tpu_custom_call" | custom-call | flops 5013504 | bytes 524288 | tf_op jit(solution)/shard_map/pallas_call | solution.py:33
  (3 shorter events, 0.0 us)
Async XLA Ops:
  1.9 1.7 %collective-permute-start = (bf16[4,64,256]{2,1,0:T(8,128)(2,1)S(1)}, bf16[4,64,256]{2,1,0:T(8,128)(2,1)S(1)}, u32[]{:S(2)}, u32[]{:S(2)}) collective-permute-start(bf16[4,64,256]{2,1,0:T(8,128)(2,1)S(1)} %get-tuple-element.51), channel_id=1, source_target_pairs={{0,1},{1,0},{2,3},{3,2},{4,5},{5,4},{6,7},{7,6},{8,9},{9,8},{10,11... | collective-permute-start | bytes 393224 | tf_op jit(solution)/shard_map/ppermute | solution.py:372
  3.7 8.7 %collective-permute-start.3 = (bf16[2,64,256]{2,1,0:T(8,128)(2,1)S(1)}, bf16[2,64,256]{2,1,0:T(8,128)(2,1)S(1)}, u32[]{:S(2)}, u32[]{:S(2)}) collective-permute-start(bf16[2,64,256]{2,1,0:T(8,128)(2,1)S(1)} %get-tuple-element.62), channel_id=1, source_target_pairs={{0,6},{1,7},{2,4},{3,5},{4,2},{5,3},{6,0},{7,1},{8,14},{9,15},{10,... | collective-permute-start | bytes 196616 | tf_op jit(solution)/shard_map/ppermute | solution.py:376
  7.3 5.0 %collective-permute-start.4 = (bf16[2,64,256]{2,1,0:T(8,128)(2,1)S(1)}, bf16[2,64,256]{2,1,0:T(8,128)(2,1)S(1)}, u32[]{:S(2)}, u32[]{:S(2)}) collective-permute-start(bf16[2,64,256]{2,1,0:T(8,128)(2,1)S(1)} %get-tuple-element.63), channel_id=1, source_target_pairs={{0,4},{1,5},{2,6},{3,7},{4,0},{5,1},{6,2},{7,3},{8,12},{9,13},{10,... | collective-permute-start | bytes 196616 | tf_op jit(solution)/shard_map/ppermute | solution.py:376
  7.9 4.5 %collective-permute-start.5 = (bf16[2,64,256]{2,1,0:T(8,128)(2,1)S(1)}, bf16[2,64,256]{2,1,0:T(8,128)(2,1)S(1)}, u32[]{:S(2)}, u32[]{:S(2)}) collective-permute-start(bf16[2,64,256]{2,1,0:T(8,128)(2,1)S(1)} %get-tuple-element.64), channel_id=1, source_target_pairs={{0,2},{1,3},{2,0},{3,1},{4,6},{5,7},{6,4},{7,5},{8,10},{9,11},{10,... | collective-permute-start | bytes 196616 | tf_op jit(solution)/shard_map/ppermute | solution.py:376
  8.0 9.1 %collective-permute-start.1 = (bf16[192,128]{1,0:T(8,128)(2,1)S(1)}, bf16[192,128]{1,0:T(8,128)(2,1)S(1)}, u32[]{:S(2)}, u32[]{:S(2)}) collective-permute-start(bf16[192,128]{1,0:T(8,128)(2,1)S(1)} %get-tuple-element.54), channel_id=1, source_target_pairs={{0,16},{8,24},{16,0},{24,8},{1,17},{9,25},{17,1},{25,9},{2,18},{10... | collective-permute-start | bytes 147464 | tf_op jit(solution)/shard_map/ppermute | solution.py:367
  11.0 6.2 %collective-permute-start.2 = (bf16[192,128]{1,0:T(8,128)(2,1)S(1)}, bf16[192,128]{1,0:T(8,128)(2,1)S(1)}, u32[]{:S(2)}, u32[]{:S(2)}) collective-permute-start(bf16[192,128]{1,0:T(8,128)(2,1)S(1)} %get-tuple-element.55), channel_id=1, source_target_pairs={{0,24},{8,16},{16,8},{24,0},{1,25},{9,17},{17,9},{25,1},{2,26},{10... | collective-permute-start | bytes 147464 | tf_op jit(solution)/shard_map/ppermute | solution.py:367
  12.6 6.2 %collective-permute-start.6 = (bf16[192,128]{1,0:T(8,128)(2,1)S(1)}, bf16[192,128]{1,0:T(8,128)(2,1)S(1)}, u32[]{:S(2)}, u32[]{:S(2)}) collective-permute-start(bf16[192,128]{1,0:T(8,128)(2,1)S(1)} %get-tuple-element.66), channel_id=1, source_target_pairs={{0,24},{8,16},{16,8},{24,0},{1,25},{9,17},{17,9},{25,1},{2,26},{10... | collective-permute-start | bytes 147464 | tf_op jit(solution)/shard_map/ppermute | solution.py:367
  16.1 5.1 %collective-permute-start.7 = (bf16[192,128]{1,0:T(8,128)(2,1)S(1)}, bf16[192,128]{1,0:T(8,128)(2,1)S(1)}, u32[]{:S(2)}, u32[]{:S(2)}) collective-permute-start(bf16[192,128]{1,0:T(8,128)(2,1)S(1)} %get-tuple-element.67), channel_id=1, source_target_pairs={{0,16},{8,24},{16,0},{24,8},{1,17},{9,25},{17,1},{25,9},{2,18},{10... | collective-permute-start | bytes 147464 | tf_op jit(solution)/shard_map/ppermute | solution.py:367
  16.1 2.8 %copy-start = (bf16[768,1024]{1,0:T(8,128)(2,1)S(1)}, bf16[768,1024]{1,0:T(8,128)(2,1)}, u32[]{:S(2)}) copy-start(bf16[768,1024]{1,0:T(8,128)(2,1)} %weight_ref.3) | copy-start | bytes 4718596
  16.1 5.2 %collective-permute-start.8 = (bf16[384,128]{1,0:T(8,128)(2,1)S(1)}, bf16[384,128]{1,0:T(8,128)(2,1)S(1)}, u32[]{:S(2)}, u32[]{:S(2)}) collective-permute-start(bf16[384,128]{1,0:T(8,128)(2,1)S(1)} %get-tuple-element.68), channel_id=1, source_target_pairs={{0,8},{8,0},{16,24},{24,16},{1,9},{9,1},{17,25},{25,17},{2,10},{10... | collective-permute-start | bytes 294920 | tf_op jit(solution)/shard_map/ppermute | solution.py:367
  18.8 2.4 %copy-start.1 = (bf16[1024,153]{0,1:T(8,128)(2,1)S(1)}, bf16[1024,153]{0,1:T(8,128)(2,1)}, u32[]{:S(2)}) copy-start(bf16[1024,153]{0,1:T(8,128)(2,1)} %param.21) | copy-start | bytes 940036
  21.3 13.4 %copy-start.2 = (bf16[1024,153]{0,1:T(8,128)(2,1)S(1)}, bf16[1024,153]{0,1:T(8,128)(2,1)}, u32[]{:S(2)}) copy-start(bf16[1024,153]{0,1:T(8,128)(2,1)} %param.20) | copy-start | bytes 940036
  21.9 5.9 %collective-permute-start.9 = (bf16[153,128]{1,0:T(8,128)(2,1)S(1)}, bf16[153,128]{1,0:T(8,128)(2,1)S(1)}, u32[]{:S(2)}, u32[]{:S(2)}) collective-permute-start(bf16[153,128]{1,0:T(8,128)(2,1)S(1)} %get-tuple-element.73), channel_id=1, source_target_pairs={{0,24},{8,16},{16,8},{24,0},{1,25},{9,17},{17,9},{25,1},{2,26},{10... | collective-permute-start | bytes 117512 | tf_op jit(solution)/shard_map/ppermute | solution.py:367
  24.4 5.2 %collective-permute-start.10 = (bf16[153,128]{1,0:T(8,128)(2,1)S(1)}, bf16[153,128]{1,0:T(8,128)(2,1)S(1)}, u32[]{:S(2)}, u32[]{:S(2)}) collective-permute-start(bf16[153,128]{1,0:T(8,128)(2,1)S(1)} %get-tuple-element.74), channel_id=1, source_target_pairs={{0,16},{8,24},{16,0},{24,8},{1,17},{9,25},{17,1},{25,9},{2,18},{10... | collective-permute-start | bytes 117512 | tf_op jit(solution)/shard_map/ppermute | solution.py:367
  24.4 5.2 %collective-permute-start.11 = (bf16[153,128]{1,0:T(8,128)(2,1)S(1)}, bf16[153,128]{1,0:T(8,128)(2,1)S(1)}, u32[]{:S(2)}, u32[]{:S(2)}) collective-permute-start(bf16[153,128]{1,0:T(8,128)(2,1)S(1)} %get-tuple-element.75), channel_id=1, source_target_pairs={{0,8},{8,0},{16,24},{24,16},{1,9},{9,1},{17,25},{25,17},{2,10},{10... | collective-permute-start | bytes 117512 | tf_op jit(solution)/shard_map/ppermute | solution.py:367
  29.9 1.3 %collective-permute-start.12 = (bf16[4,16,256]{2,1,0:T(8,128)(2,1)S(1)}, bf16[4,16,256]{2,1,0:T(8,128)(2,1)S(1)}, u32[]{:S(2)}, u32[]{:S(2)}) collective-permute-start(bf16[4,16,256]{2,1,0:T(8,128)(2,1)S(1)} %get-tuple-element.77), channel_id=1, source_target_pairs={{0,1},{1,0},{2,3},{3,2},{4,5},{5,4},{6,7},{7,6},{8,9},{9,8},{10,11... | collective-permute-start | bytes 98312 | tf_op jit(solution)/shard_map/ppermute | solution.py:372
  31.2 4.6 %collective-permute-start.13 = (bf16[2,16,256]{2,1,0:T(8,128)(2,1)S(1)}, bf16[2,16,256]{2,1,0:T(8,128)(2,1)S(1)}, u32[]{:S(2)}, u32[]{:S(2)}) collective-permute-start(bf16[2,16,256]{2,1,0:T(8,128)(2,1)S(1)} %get-tuple-element.79), channel_id=1, source_target_pairs={{0,6},{1,7},{2,4},{3,5},{4,2},{5,3},{6,0},{7,1},{8,14},{9,15},{10,... | collective-permute-start | bytes 49160 | tf_op jit(solution)/shard_map/ppermute | solution.py:376
  33.0 3.7 %collective-permute-start.14 = (bf16[2,16,256]{2,1,0:T(8,128)(2,1)S(1)}, bf16[2,16,256]{2,1,0:T(8,128)(2,1)S(1)}, u32[]{:S(2)}, u32[]{:S(2)}) collective-permute-start(bf16[2,16,256]{2,1,0:T(8,128)(2,1)S(1)} %get-tuple-element.80), channel_id=1, source_target_pairs={{0,4},{1,5},{2,6},{3,7},{4,0},{5,1},{6,2},{7,3},{8,12},{9,13},{10,... | collective-permute-start | bytes 49160 | tf_op jit(solution)/shard_map/ppermute | solution.py:376
  34.0 3.7 %collective-permute-start.15 = (bf16[2,16,256]{2,1,0:T(8,128)(2,1)S(1)}, bf16[2,16,256]{2,1,0:T(8,128)(2,1)S(1)}, u32[]{:S(2)}, u32[]{:S(2)}) collective-permute-start(bf16[2,16,256]{2,1,0:T(8,128)(2,1)S(1)} %get-tuple-element.81), channel_id=1, source_target_pairs={{0,2},{1,3},{2,0},{3,1},{4,6},{5,7},{6,4},{7,5},{8,10},{9,11},{10,... | collective-permute-start | bytes 49160 | tf_op jit(solution)/shard_map/ppermute | solution.py:376

commit v18 on v16

--- a/solution.py
+++ b/solution.py
@@ -217,17 +217,22 @@
         ).astype(bf16)
 
 
-def mean_kernel(me_ref, sums_ref, edges_ref, *rest):
+def mean_kernel(first, me_ref, sums_ref, edges_ref, *rest):
     groups, parts, slots, rows = edges_ref.shape
     arrived, outs = rest[: parts // 2], rest[parts // 2 :]
     width = outs[0].shape[0]
-    for k in range(groups):
+    for k, out in enumerate(outs, first):
         group = ahead(me_ref[0], groups, k)
         span = pl.ds(pl.multiple_of(group * slots, slots), slots)
         far = jnp.concatenate([x[:, span, :].reshape(2 * slots, -1) for x in arrived], axis=0)
         far = dot(far, edges_ref[group].reshape(parts * slots, rows), FIRST)
         total = sums_ref[group, :width, :] + far[:width]
-        outs[k][...] = (total / sums_ref[group, width : width + 1, :]).astype(bf16)
+        out[...] = (total / sums_ref[group, width : width + 1, :]).astype(bf16)
+
+
+def own_mean_kernel(after, *rest):
+    del after
+    mean_kernel(0, *rest)
 
 
 def rows_from(me, groups, k, width, near=False):
@@ -281,14 +286,23 @@
     copy.wait()
 
 
-def pick_kernel(me_ref, hits_ref, *rest):
+def pick_blocks(groups, first, me_ref, hits_ref, blocks):
+    rows = blocks[0].shape[1]
+    total = None
+    for k, block in enumerate(blocks, first):
+        at = pl.multiple_of(behind(me_ref[0], groups, k) * rows, rows)
+        term = dot(hits_ref[:, pl.ds(at, rows)], block[...], LAST)
+        total = term if total is None else total + term
+    return total
+
+
+def early_pick_kernel(groups, me_ref, hits_ref, *rest):
+    rest[-1][...] = pick_blocks(groups, 0, me_ref, hits_ref, rest[:-1])
+
+
+def pick_kernel(groups, me_ref, hits_ref, early_ref, *rest):
     projected, (mine_ref, mate_ref) = rest[:-2], rest[-2:]
-    groups, rows = len(projected), projected[0].shape[1]
-    total = None
-    for k in range(groups):
-        at = pl.multiple_of(behind(me_ref[0], groups, k) * rows, rows)
-        term = dot(hits_ref[:, pl.ds(at, rows)], projected[k][...], LAST)
-        total = term if total is None else total + term
+    total = early_ref[...] + pick_blocks(groups, 2, me_ref, hits_ref, projected)
     gap = mine_ref.shape[2] - total.shape[1]
     total = jnp.concatenate([total, jnp.zeros((total.shape[0], gap), f32)], axis=1).astype(bf16)
     half = total.shape[0] // 2
@@ -319,13 +333,14 @@
     out_ref[...] = own_ref[...] + total / sums_ref[me, width : width + 1, :]
 
 
-def last_kernel(me_ref, near_ref, edges_ref, sums_ref, *rest):
+def last_kernel(first, me_ref, near_ref, edges_ref, sums_ref, *rest):
     arrived, out_ref = rest[:-1], rest[-1]
-    groups, parts, slots, rows = edges_ref.shape
+    _, _, slots, rows = edges_ref.shape
     me, width = me_ref[0], sums_ref.shape[1] - EXTRA
+    count = 2 * len(arrived)
     arrived = jnp.concatenate([x[...].reshape(2 * slots, -1) for x in arrived], axis=0)
-    far = dot(arrived, edges_ref[me].reshape(parts * slots, rows), FIRST)
-    far = far[: near_ref.shape[0]]
+    edges = edges_ref[me, 2 * first : 2 * first + count].reshape(count * slots, rows)
+    far = dot(arrived, edges, FIRST)[: near_ref.shape[0]]
     total = near_ref[...] + far / sums_ref[me, width : width + 1, :]
     out_ref[...] = total.reshape(out_ref.shape)
 
@@ -429,14 +444,14 @@
     arrived = to_chips(paired[:chips])
     feature_blocks = shift(paired[chips:], near=True)
     means = call(
-        mean_kernel,
-        (shape(width, rows),) * groups,
+        functools.partial(mean_kernel, 1),
+        (shape(width, rows),) * (groups - 1),
         [SM] + [VM] * (2 + chips),
         (),
         2 * nodes * parts * slots * width,
         1 << 20,
     )(me, sums, edges, *arrived)
-    means = [means[0]] + shift(means[1:])
+    means = shift(means)
     own = call(
         self_kernel,
         shape(rows, hid, dtype=f32),
@@ -449,6 +464,15 @@
         2 * rows * hid * groups * width,
         2 << 20,
     )(me, feature_rows, self_one, *feature_blocks)
+    own_mean = call(
+        own_mean_kernel,
+        (shape(width, rows),),
+        [VM, SM] + [VM] * (2 + chips),
+        (),
+        2 * rows * parts * slots * width,
+        1 << 18,
+    )(own, me, sums, edges, *arrived)
+    means = [*own_mean, *means]
     early = call(
         functools.partial(early_kernel, groups),
         shape(rows, hid, dtype=f32),
@@ -474,14 +498,22 @@
         1 << 19,
     )(projected[0], me, part, sources[0])
     projected = projected[:1] + shift(projected[1:])
+    early = call(
+        functools.partial(early_pick_kernel, groups),
+        shape(parts * slots, classes, dtype=f32),
+        [SM] + [VM] * 3,
+        (),
+        parts * slots * nodes * classes,
+        1 << 18,
+    )(me, hits, *projected[:2])
     mine, mate = call(
-        pick_kernel,
+        functools.partial(pick_kernel, groups),
         (shape(chips, slots, whole_lanes(classes)),) * 2,
-        [SM] + [VM] * (1 + groups),
-        (),
-        2 * parts * slots * nodes * classes,
-        1 << 19,
-    )(me, hits, *projected)
+        [SM] + [VM] * groups,
+        (),
+        parts * slots * nodes * classes,
+        1 << 18,
+    )(me, hits, early, *projected[2:])
     mate = to_mate(mate)
     arrived = to_chips(
         call(pair_kernel, (shape(2, slots, whole_lanes(classes)),) * chips, [VM] * 3, (), 0, 1 << 19)(
@@ -505,14 +537,23 @@
         2 * rows * nodes * classes,
         1 << 19,
     )(me, own, sums, band, *projected)
+    half = chips // 2
+    near = call(
+        functools.partial(last_kernel, 0),
+        shape(classes, rows, dtype=f32),
+        [SM] + [VM] * (3 + half),
+        (),
+        rows * parts * slots * classes,
+        1 << 18,
+    )(me, near, edges, sums, *arrived[:half])
     logits = call(
-        last_kernel,
+        functools.partial(last_kernel, half),
         shape(classes, 1, rows, dtype=f32),
-        [SM] + [VM] * (3 + chips),
-        (),
-        2 * rows * parts * slots * classes,
+        [SM] + [VM] * (3 + chips - half),
+        (),
+        rows * parts * slots * classes,
         1 << 19,
-    )(me, near, edges, sums, *arrived)
+    )(me, near, edges, sums, *arrived[half:])
     return hidden[None], logits.transpose(1, 0, 2)
 
 

time: 38.2 us -> 38.2 us (level)
  waiting for transfers between devices: 6.93 us -> 6.37 us
  Pallas kernels: 8.39 us -> 8.89 us
    pallas_call x13 -> x16, Pallas kernels: 8.39 us -> 8.89 us  [placed(): run(*(pltpu.with_memory_space_constraint(value, pltpu.HBM) if spec is HB...]
  transfers between devices with their start and end apart: 17 -> 17, of which waited for: 8 -> 8; matrix products, arithmetic and copies ran while one was open for 0% -> 0% of each run, Pallas kernels for 14% -> 16%
where the time goes in v18:
time: 38.2 us; the launch traced here: 37.9 us
  starting transfers between devices  21.9 us (57%)
  Pallas kernels  8.89 us (23%)
  waiting for transfers between devices  6.37 us (17%)
  between operations  0.79 us (2%)
    ppermute x9, starting transfers between devices, shift(): lax.ppermute(block, 'feat', [(i, ahead(i, groups, k, near)) for i in rang...  13.5 us
    pallas_call x16, Pallas kernels, placed(): run(*(pltpu.with_memory_space_constraint(value, pltpu.HBM) if spec is HB...  8.89 us
    ppermute x6, starting transfers between devices, to_chips(): lax.ppermute(blocks[j], 'dom', [(d, next_to(d // 2, j, chips) * 2 + d % 2...  7.8 us
    ppermute x9, waiting for transfers between devices, shift(): lax.ppermute(block, 'feat', [(i, ahead(i, groups, k, near)) for i in rang...  3.25 us
    ppermute x6, waiting for transfers between devices, to_chips(): lax.ppermute(blocks[j], 'dom', [(d, next_to(d // 2, j, chips) * 2 + d % 2...  1.92 us
    ppermute x2, waiting for transfers between devices, to_mate(): return lax.ppermute(value, 'dom', [(d, d ^ 1) for d in range(parts)])  1.2 us
  transfers between devices with their start and end apart: 17, of which 8 were waited for; matrix products, arithmetic and copies ran while one was open for 0% of the time, Pallas kernels for 16%

profile of v18, /device:TPU:0, one launch (start us, length us, event | category | flops | bytes accessed | tf_op | source)
XLA Modules:
  0.0 37.9 jit_solution(8505817934944466706)
XLA Ops:
  0.6 1.3 %shard_map.122 = (bf16[4,64,256]{2,1,0:T(8,128)(2,1)S(1)}, bf16[256,512]{1,0:T(8,128)(2,1)S(1)}, s32[8,4,16]{2,1,0:T(4,128)S(1)}, bf16[12,128,128]{2,1,0:T(8,128...) custom-call(s32[1]{0:T(128)} %bitcast.4.part_ref, ...), custom_call_target="tpu_custom_call" | custom-call | flops 100663296 | bytes 1048576 | tf_op jit(solution)/shard_map/pallas_call | solution.py:33
  1.9 0.5 %collective-permute-start = (bf16[4,64,256]{2,1,0:T(8,128)(2,1)S(1)}, bf16[4,64,256]{2,1,0:T(8,128)(2,1)S(1)}, u32[]{:S(2)}, u32[]{:S(2)}) collective-permute-start(bf16[4,64,256]{2,1,0:T(8,128)(2,1)S(1)} %get-tuple-element.49), channel_id=1, source_target_pairs={{0,1},{1,0},{2,3},{3,2},{4,5},{5,4},{6,7},{7,6},{8,9},{9,8},{10,11... | collective-permute-start | bytes 393224 | tf_op jit(solution)/shard_map/ppermute | solution.py:381
  2.5 1.2 %shard_map.123 = (f32[4,208,128]{2,1,0:T(8,128)S(1)}, bf16[4,8,16,128]{3,2,1,0:T(8,128)(2,1)S(1)}, bf16[128,512]{1,0:T(8,128)(2,1)S(1)}, bf16[4,64,256]{2,1,0:T(...) custom-call(s32[1]{0:T(128)} %bitcast.me_ref.rest_0_, ...), custom_call_target="tpu_custom_call" | custom-call | flops 100663296 | bytes 1048576 | tf_op jit(solution)/shard_map/pallas_call | solution.py:33
  3.6 0.0 collective-permute-done.got_ref
  3.7 3.7 %collective-permute-start.4 = (bf16[2,64,256]{2,1,0:T(8,128)(2,1)S(1)}, bf16[2,64,256]{2,1,0:T(8,128)(2,1)S(1)}, u32[]{:S(2)}, u32[]{:S(2)}) collective-permute-start(bf16[2,64,256]{2,1,0:T(8,128)(2,1)S(1)} %get-tuple-element.59), channel_id=1, source_target_pairs={{0,6},{1,7},{2,4},{3,5},{4,2},{5,3},{6,0},{7,1},{8,14},{9,15},{10,... | collective-permute-start | bytes 196616 | tf_op jit(solution)/shard_map/ppermute | solution.py:385
  7.4 0.5 %collective-permute-start.5 = (bf16[2,64,256]{2,1,0:T(8,128)(2,1)S(1)}, bf16[2,64,256]{2,1,0:T(8,128)(2,1)S(1)}, u32[]{:S(2)}, u32[]{:S(2)}) collective-permute-start(bf16[2,64,256]{2,1,0:T(8,128)(2,1)S(1)} %get-tuple-element.60), channel_id=1, source_target_pairs={{0,4},{1,5},{2,6},{3,7},{4,0},{5,1},{6,2},{7,3},{8,12},{9,13},{10,... | collective-permute-start | bytes 196616 | tf_op jit(solution)/shard_map/ppermute | solution.py:385
  7.9 0.1 collective-permute-start.6
  8.0 3.0 %collective-permute-start.1 = (bf16[192,128]{1,0:T(8,128)(2,1)S(1)}, bf16[192,128]{1,0:T(8,128)(2,1)S(1)}, u32[]{:S(2)}, u32[]{:S(2)}) collective-permute-start(bf16[192,128]{1,0:T(8,128)(2,1)S(1)} %get-tuple-element.53), channel_id=1, source_target_pairs={{0,16},{8,24},{16,0},{24,8},{1,17},{9,25},{17,1},{25,9},{2,18},{10... | collective-permute-start | bytes 147464 | tf_op jit(solution)/shard_map/ppermute | solution.py:376
  11.0 1.3 %collective-permute-start.2 = (bf16[192,128]{1,0:T(8,128)(2,1)S(1)}, bf16[192,128]{1,0:T(8,128)(2,1)S(1)}, u32[]{:S(2)}, u32[]{:S(2)}) collective-permute-start(bf16[192,128]{1,0:T(8,128)(2,1)S(1)} %get-tuple-element.54), channel_id=1, source_target_pairs={{0,24},{8,16},{16,8},{24,0},{1,25},{9,17},{17,9},{25,1},{2,26},{10... | collective-permute-start | bytes 147464 | tf_op jit(solution)/shard_map/ppermute | solution.py:376
  12.3 0.0 collective-permute-done.4.rest_4_.rest_1_
  12.3 0.2 collective-permute-start.3
  12.6 0.0 collective-permute-done.5.rest_5_.rest_2_
  12.6 0.0 collective-permute-done.6.rest_6_.rest_3_
  12.6 0.2 shard_map.127
  12.8 3.2 %collective-permute-start.7 = (bf16[192,128]{1,0:T(8,128)(2,1)S(1)}, bf16[192,128]{1,0:T(8,128)(2,1)S(1)}, u32[]{:S(2)}, u32[]{:S(2)}) collective-permute-start(bf16[192,128]{1,0:T(8,128)(2,1)S(1)} %get-tuple-element.62), channel_id=1, source_target_pairs={{0,24},{8,16},{16,8},{24,0},{1,25},{9,17},{17,9},{25,1},{2,26},{10... | collective-permute-start | bytes 147464 | tf_op jit(solution)/shard_map/ppermute | solution.py:376
  16.0 0.1 collective-permute-start.8
  16.1 0.0 collective-permute-done.1.rest_0_
  16.1 1.1 %collective-permute-start.9 = (bf16[192,128]{1,0:T(8,128)(2,1)S(1)}, bf16[192,128]{1,0:T(8,128)(2,1)S(1)}, u32[]{:S(2)}, u32[]{:S(2)}) collective-permute-start(bf16[192,128]{1,0:T(8,128)(2,1)S(1)} %get-tuple-element.64), channel_id=1, source_target_pairs={{0,8},{8,0},{16,24},{24,16},{1,9},{9,1},{17,25},{25,17},{2,10},{10... | collective-permute-start | bytes 147464 | tf_op jit(solution)/shard_map/ppermute | solution.py:376
  17.3 0.2 collective-permute-done.2.rest_1_
  17.4 0.0 collective-permute-done.3.rest_2_
  17.5 1.8 %shard_map.125.after.own_ref = f32[128,1024]{1,0:T(8,128)S(1)} custom-call(s32[1]{0:T(128)} %bitcast.me_ref.rest_0_, bf16[192,512]{1,0:T(8,128)(2,1)} %bitcast.22, bf16[768,1024]{1,0:T(8,128)(2,1)} %weight_hbm.1, bf16[192,128]{1,0:T(8,128)(2,1)S(1)} %collective-permute-done.1.rest_0_, bf16[192,128]{1,0:T(8,128)(2,1)S(1)} %collective-permute-done.2.rest_1_, ...), custom_call_target="tpu_custom_call" | custom-call | flops 201326592 | bytes 2097152 | tf_op jit(solution)/shard_map/pallas_call | solution.py:33
  19.3 0.2 shard_map.126.rest_0_
  19.5 0.0 collective-permute-done.7.rest_1_
  19.5 0.3 shard_map.128.early_ref
  19.8 1.4 %collective-permute-done.8.rest_0_ = bf16[192,128]{1,0:T(8,128)(2,1)S(1)} collective-permute-done((bf16[192,128]{1,0:T(8,128)(2,1)S(1)}, bf16[192,128]{1,0:T(8,128)(2,1)S(1)}, u32[]{:S(2)}, u32[]{:S(2)}) %collective-permute-start.8) | collective-permute-done | bytes 49184 | tf_op jit(solution)/shard_map/ppermute | solution.py:376
  21.2 0.0 collective-permute-done.9.rest_1_
  21.2 0.5 %shard_map.129 = (bf16[128,1024]{1,0:T(8,128)(2,1)S(1)}, bf16[153,128]{1,0:T(8,128)(2,1)S(1)}, bf16[153,128]{1,0:T(8,128)(2,1)S(1)}, bf16[153,128]{1,0:T(8,128)(2,1)S(1)}, bf16[153,128]{1,0:T(8,128)(2,1)S(1)}) custom-call(s32[1]{0:T(128)} %bitcast.me_ref.rest_0_, bf16[768,1024]{1,0:T(8,128)(2,1)S(1)} %copy-done, bf16[153,1024]{1,0:T(8,128)(2,1)S(1)} %bitcast.20, ...), custom_call_target="tpu_custom_call" | custom-call | flops 100663296 | bytes 2097152 | tf_op jit(solution)/shard_map/pallas_call | solution.py:33
  21.8 2.3 %collective-permute-start.10 = (bf16[153,128]{1,0:T(8,128)(2,1)S(1)}, bf16[153,128]{1,0:T(8,128)(2,1)S(1)}, u32[]{:S(2)}, u32[]{:S(2)}) collective-permute-start(bf16[153,128]{1,0:T(8,128)(2,1)S(1)} %get-tuple-element.69), channel_id=1, source_target_pairs={{0,24},{8,16},{16,8},{24,0},{1,25},{9,17},{17,9},{25,1},{2,26},{10... | collective-permute-start | bytes 117512 | tf_op jit(solution)/shard_map/ppermute | solution.py:376
  24.0 0.0 collective-permute-start.11
  24.0 2.2 %collective-permute-start.12 = (bf16[153,128]{1,0:T(8,128)(2,1)S(1)}, bf16[153,128]{1,0:T(8,128)(2,1)S(1)}, u32[]{:S(2)}, u32[]{:S(2)}) collective-permute-start(bf16[153,128]{1,0:T(8,128)(2,1)S(1)} %get-tuple-element.71), channel_id=1, source_target_pairs={{0,8},{8,0},{16,24},{24,16},{1,9},{9,1},{17,25},{25,17},{2,10},{10... | collective-permute-start | bytes 117512 | tf_op jit(solution)/shard_map/ppermute | solution.py:376
  26.2 0.9 %shard_map.132.hits_ref.after = bf16[128,512]{1,0:T(8,128)(2,1)S(1)} custom-call(bf16[153,128]{1,0:T(8,128)(2,1)S(1)} %get-tuple-element.68.rest_0_.after, s32[1]{0:T(128)} %bitcast.me_ref.rest_0_, s32[1]{0:T(128)} %bitcast.4.part_ref, s32[8,4,16]{2,1,0:T(4,128)} %bitcast.26), custom_call_target="tpu_custom_call" | custom-call | bytes 524288 | tf_op jit(solution)/shard_map/pallas_call | solution.py:33
  27.1 0.7 %collective-permute-done.10.rest_1_ = bf16[153,128]{1,0:T(8,128)(2,1)S(1)} collective-permute-done((bf16[153,128]{1,0:T(8,128)(2,1)S(1)}, bf16[153,128]{1,0:T(8,128)(2,1)S(1)}, u32[]{:S(2)}, u32[]{:S(2)}) %collective-permute-start.10) | collective-permute-done | bytes 39200 | tf_op jit(solution)/shard_map/ppermute | solution.py:376
  27.8 0.2 shard_map.133.early_ref
  28.0 1.0 %collective-permute-done.11.rest_2_.rest_0_ = bf16[153,128]{1,0:T(8,128)(2,1)S(1)} collective-permute-done((bf16[153,128]{1,0:T(8,128)(2,1)S(1)}, bf16[153,128]{1,0:T(8,128)(2,1)S(1)}, u32[]{:S(2)}, u32[]{:S(2)}) %collective-permute-start.11) | collective-permute-done | bytes 39200 | tf_op jit(solution)/shard_map/ppermute | solution.py:376
  29.0 0.0 collective-permute-done.12.rest_3_.rest_1_
  29.0 0.2 shard_map.134
  29.2 0.1 collective-permute-start.13
  29.3 1.2 %collective-permute-done.13.got_ref = bf16[4,16,256]{2,1,0:T(8,128)(2,1)S(1)} collective-permute-done((bf16[4,16,256]{2,1,0:T(8,128)(2,1)S(1)}, bf16[4,16,256]{2,1,0:T(8,128)(2,1)S(1)}, u32[]{:S(2)}, u32[]{:S(2)}) %collective-permute-start.13) | collective-permute-done | bytes 32800 | tf_op jit(solution)/shard_map/ppermute | solution.py:381
  30.5 2.4 %collective-permute-start.14 = (bf16[2,16,256]{2,1,0:T(8,128)(2,1)S(1)}, bf16[2,16,256]{2,1,0:T(8,128)(2,1)S(1)}, u32[]{:S(2)}, u32[]{:S(2)}) collective-permute-start(bf16[2,16,256]{2,1,0:T(8,128)(2,1)S(1)} %get-tuple-element.75), channel_id=1, source_target_pairs={{0,6},{1,7},{2,4},{3,5},{4,2},{5,3},{6,0},{7,1},{8,14},{9,15},{10,... | collective-permute-start | bytes 49160 | tf_op jit(solution)/shard_map/ppermute | solution.py:385
  33.0 0.4 collective-permute-start.15
  33.3 0.7 %collective-permute-start.16 = (bf16[2,16,256]{2,1,0:T(8,128)(2,1)S(1)}, bf16[2,16,256]{2,1,0:T(8,128)(2,1)S(1)}, u32[]{:S(2)}, u32[]{:S(2)}) collective-permute-start(bf16[2,16,256]{2,1,0:T(8,128)(2,1)S(1)} %get-tuple-element.77), channel_id=1, source_target_pairs={{0,2},{1,3},{2,0},{3,1},{4,6},{5,7},{6,4},{7,5},{8,10},{9,11},{10,... | collective-permute-start | bytes 49160 | tf_op jit(solution)/shard_map/ppermute | solution.py:385
  34.0 0.7 %shard_map.130 = (f32[153,128]{1,0:T(8,128)S(1)}, bf16[128,1024]{1,0:T(8,128)(2,1)}) custom-call(bf16[128,1024]{1,0:T(8,128)(2,1)S(1)} %get-tuple-element.65.hidden_ref, bf16[153,1024]{1,0:T(8,128)(2,1)S(1)} %bitcast.19), custom_call_target="tpu_custom_call" | custom-call | flops 40108032 | bytes 1048576 | tf_op jit(solution)/shard_map/pallas_call | solution.py:33
  34.7 0.2 shard_map.131.near_ref
  35.0 0.2 collective-permute-done.14.rest_1_
  35.1 0.2 shard_map.136.near_ref
  35.3 1.3 %collective-permute-done.15.rest_0_ = bf16[2,16,256]{2,1,0:T(8,128)(2,1)S(1)} collective-permute-done((bf16[2,16,256]{2,1,0:T(8,128)(2,1)S(1)}, bf16[2,16,256]{2,1,0:T(8,128)(2,1)S(1)}, u32[]{:S(2)}, u32[]{:S(2)}) %collective-permute-start.15) | collective-permute-done | bytes 16416 | tf_op jit(solution)/shard_map/ppermute | solution.py:385
  36.7 0.4 collective-permute-done.16.rest_1_
  37.1 0.9 %shard_map.137 = f32[153,1,128]{2,1,0:T(1,128)} custom-call(s32[1]{0:T(128)} %bitcast.me_ref.rest_0_, f32[153,128]{1,0:T(8,128)S(1)} %shard_map.136.near_ref, bf16[4,8,16,128]{3,2,1,0:T(8,128)(2,1)S(1)} %get-tuple-element.57.rest_2_.edges_ref, f32[4,208,128]{2,1,0:T(8,128)S(1)} %get-tuple-element.56.rest_1_.sums_ref, ...), custom_call_target="tpu_custom_call" | custom-call | flops 2506752 | bytes 524288 | tf_op jit(solution)/shard_map/pallas_call | solution.py:33
  (8 shorter events, 0.0 us)
Async XLA Ops:
  1.9 1.7 %collective-permute-start = (bf16[4,64,256]{2,1,0:T(8,128)(2,1)S(1)}, bf16[4,64,256]{2,1,0:T(8,128)(2,1)S(1)}, u32[]{:S(2)}, u32[]{:S(2)}) collective-permute-start(bf16[4,64,256]{2,1,0:T(8,128)(2,1)S(1)} %get-tuple-element.49), channel_id=1, source_target_pairs={{0,1},{1,0},{2,3},{3,2},{4,5},{5,4},{6,7},{7,6},{8,9},{9,8},{10,11... | collective-permute-start | bytes 393224 | tf_op jit(solution)/shard_map/ppermute | solution.py:381
  3.7 8.7 %collective-permute-start.4 = (bf16[2,64,256]{2,1,0:T(8,128)(2,1)S(1)}, bf16[2,64,256]{2,1,0:T(8,128)(2,1)S(1)}, u32[]{:S(2)}, u32[]{:S(2)}) collective-permute-start(bf16[2,64,256]{2,1,0:T(8,128)(2,1)S(1)} %get-tuple-element.59), channel_id=1, source_target_pairs={{0,6},{1,7},{2,4},{3,5},{4,2},{5,3},{6,0},{7,1},{8,14},{9,15},{10,... | collective-permute-start | bytes 196616 | tf_op jit(solution)/shard_map/ppermute | solution.py:385
  7.4 5.2 %collective-permute-start.5 = (bf16[2,64,256]{2,1,0:T(8,128)(2,1)S(1)}, bf16[2,64,256]{2,1,0:T(8,128)(2,1)S(1)}, u32[]{:S(2)}, u32[]{:S(2)}) collective-permute-start(bf16[2,64,256]{2,1,0:T(8,128)(2,1)S(1)} %get-tuple-element.60), channel_id=1, source_target_pairs={{0,4},{1,5},{2,6},{3,7},{4,0},{5,1},{6,2},{7,3},{8,12},{9,13},{10,... | collective-permute-start | bytes 196616 | tf_op jit(solution)/shard_map/ppermute | solution.py:385
  7.9 4.7 %collective-permute-start.6 = (bf16[2,64,256]{2,1,0:T(8,128)(2,1)S(1)}, bf16[2,64,256]{2,1,0:T(8,128)(2,1)S(1)}, u32[]{:S(2)}, u32[]{:S(2)}) collective-permute-start(bf16[2,64,256]{2,1,0:T(8,128)(2,1)S(1)} %get-tuple-element.61), channel_id=1, source_target_pairs={{0,2},{1,3},{2,0},{3,1},{4,6},{5,7},{6,4},{7,5},{8,10},{9,11},{10,... | collective-permute-start | bytes 196616 | tf_op jit(solution)/shard_map/ppermute | solution.py:385
  8.0 8.1 %collective-permute-start.1 = (bf16[192,128]{1,0:T(8,128)(2,1)S(1)}, bf16[192,128]{1,0:T(8,128)(2,1)S(1)}, u32[]{:S(2)}, u32[]{:S(2)}) collective-permute-start(bf16[192,128]{1,0:T(8,128)(2,1)S(1)} %get-tuple-element.53), channel_id=1, source_target_pairs={{0,16},{8,24},{16,0},{24,8},{1,17},{9,25},{17,1},{25,9},{2,18},{10... | collective-permute-start | bytes 147464 | tf_op jit(solution)/shard_map/ppermute | solution.py:376
  11.0 6.5 %collective-permute-start.2 = (bf16[192,128]{1,0:T(8,128)(2,1)S(1)}, bf16[192,128]{1,0:T(8,128)(2,1)S(1)}, u32[]{:S(2)}, u32[]{:S(2)}) collective-permute-start(bf16[192,128]{1,0:T(8,128)(2,1)S(1)} %get-tuple-element.54), channel_id=1, source_target_pairs={{0,24},{8,16},{16,8},{24,0},{1,25},{9,17},{17,9},{25,1},{2,26},{10... | collective-permute-start | bytes 147464 | tf_op jit(solution)/shard_map/ppermute | solution.py:376
  12.3 5.1 %collective-permute-start.3 = (bf16[192,128]{1,0:T(8,128)(2,1)S(1)}, bf16[192,128]{1,0:T(8,128)(2,1)S(1)}, u32[]{:S(2)}, u32[]{:S(2)}) collective-permute-start(bf16[192,128]{1,0:T(8,128)(2,1)S(1)} %get-tuple-element.55), channel_id=1, source_target_pairs={{0,8},{8,0},{16,24},{24,16},{1,9},{9,1},{17,25},{25,17},{2,10},{10... | collective-permute-start | bytes 147464 | tf_op jit(solution)/shard_map/ppermute | solution.py:376
  12.8 6.7 %collective-permute-start.7 = (bf16[192,128]{1,0:T(8,128)(2,1)S(1)}, bf16[192,128]{1,0:T(8,128)(2,1)S(1)}, u32[]{:S(2)}, u32[]{:S(2)}) collective-permute-start(bf16[192,128]{1,0:T(8,128)(2,1)S(1)} %get-tuple-element.62), channel_id=1, source_target_pairs={{0,24},{8,16},{16,8},{24,0},{1,25},{9,17},{17,9},{25,1},{2,26},{10... | collective-permute-start | bytes 147464 | tf_op jit(solution)/shard_map/ppermute | solution.py:376
  16.0 5.2 %collective-permute-start.8 = (bf16[192,128]{1,0:T(8,128)(2,1)S(1)}, bf16[192,128]{1,0:T(8,128)(2,1)S(1)}, u32[]{:S(2)}, u32[]{:S(2)}) collective-permute-start(bf16[192,128]{1,0:T(8,128)(2,1)S(1)} %get-tuple-element.63), channel_id=1, source_target_pairs={{0,16},{8,24},{16,0},{24,8},{1,17},{9,25},{17,1},{25,9},{2,18},{10... | collective-permute-start | bytes 147464 | tf_op jit(solution)/shard_map/ppermute | solution.py:376
  16.1 3.4 %copy-start = (bf16[768,1024]{1,0:T(8,128)(2,1)S(1)}, bf16[768,1024]{1,0:T(8,128)(2,1)}, u32[]{:S(2)}) copy-start(bf16[768,1024]{1,0:T(8,128)(2,1)} %weight_ref.3) | copy-start | bytes 4718596
  16.1 5.1 %collective-permute-start.9 = (bf16[192,128]{1,0:T(8,128)(2,1)S(1)}, bf16[192,128]{1,0:T(8,128)(2,1)S(1)}, u32[]{:S(2)}, u32[]{:S(2)}) collective-permute-start(bf16[192,128]{1,0:T(8,128)(2,1)S(1)} %get-tuple-element.64), channel_id=1, source_target_pairs={{0,8},{8,0},{16,24},{24,16},{1,9},{9,1},{17,25},{25,17},{2,10},{10... | collective-permute-start | bytes 147464 | tf_op jit(solution)/shard_map/ppermute | solution.py:376
  19.5 1.7 %copy-start.2 = (bf16[1024,153]{0,1:T(8,128)(2,1)S(1)}, bf16[1024,153]{0,1:T(8,128)(2,1)}, u32[]{:S(2)}) copy-start(bf16[1024,153]{0,1:T(8,128)(2,1)} %param.21) | copy-start | bytes 940036
  21.2 12.8 %copy-start.1 = (bf16[1024,153]{0,1:T(8,128)(2,1)S(1)}, bf16[1024,153]{0,1:T(8,128)(2,1)}, u32[]{:S(2)}) copy-start(bf16[1024,153]{0,1:T(8,128)(2,1)} %param.20) | copy-start | bytes 940036
  21.8 6.0 %collective-permute-start.10 = (bf16[153,128]{1,0:T(8,128)(2,1)S(1)}, bf16[153,128]{1,0:T(8,128)(2,1)S(1)}, u32[]{:S(2)}, u32[]{:S(2)}) collective-permute-start(bf16[153,128]{1,0:T(8,128)(2,1)S(1)} %get-tuple-element.69), channel_id=1, source_target_pairs={{0,24},{8,16},{16,8},{24,0},{1,25},{9,17},{17,9},{25,1},{2,26},{10... | collective-permute-start | bytes 117512 | tf_op jit(solution)/shard_map/ppermute | solution.py:376
  24.0 5.0 %collective-permute-start.11 = (bf16[153,128]{1,0:T(8,128)(2,1)S(1)}, bf16[153,128]{1,0:T(8,128)(2,1)S(1)}, u32[]{:S(2)}, u32[]{:S(2)}) collective-permute-start(bf16[153,128]{1,0:T(8,128)(2,1)S(1)} %get-tuple-element.70), channel_id=1, source_target_pairs={{0,16},{8,24},{16,0},{24,8},{1,17},{9,25},{17,1},{25,9},{2,18},{10... | collective-permute-start | bytes 117512 | tf_op jit(solution)/shard_map/ppermute | solution.py:376
  24.0 5.0 %collective-permute-start.12 = (bf16[153,128]{1,0:T(8,128)(2,1)S(1)}, bf16[153,128]{1,0:T(8,128)(2,1)S(1)}, u32[]{:S(2)}, u32[]{:S(2)}) collective-permute-start(bf16[153,128]{1,0:T(8,128)(2,1)S(1)} %get-tuple-element.71), channel_id=1, source_target_pairs={{0,8},{8,0},{16,24},{24,16},{1,9},{9,1},{17,25},{25,17},{2,10},{10... | collective-permute-start | bytes 117512 | tf_op jit(solution)/shard_map/ppermute | solution.py:376
  29.2 1.3 %collective-permute-start.13 = (bf16[4,16,256]{2,1,0:T(8,128)(2,1)S(1)}, bf16[4,16,256]{2,1,0:T(8,128)(2,1)S(1)}, u32[]{:S(2)}, u32[]{:S(2)}) collective-permute-start(bf16[4,16,256]{2,1,0:T(8,128)(2,1)S(1)} %get-tuple-element.73), channel_id=1, source_target_pairs={{0,1},{1,0},{2,3},{3,2},{4,5},{5,4},{6,7},{7,6},{8,9},{9,8},{10,11... | collective-permute-start | bytes 98312 | tf_op jit(solution)/shard_map/ppermute | solution.py:381
  30.5 4.6 %collective-permute-start.14 = (bf16[2,16,256]{2,1,0:T(8,128)(2,1)S(1)}, bf16[2,16,256]{2,1,0:T(8,128)(2,1)S(1)}, u32[]{:S(2)}, u32[]{:S(2)}) collective-permute-start(bf16[2,16,256]{2,1,0:T(8,128)(2,1)S(1)} %get-tuple-element.75), channel_id=1, source_target_pairs={{0,6},{1,7},{2,4},{3,5},{4,2},{5,3},{6,0},{7,1},{8,14},{9,15},{10,... | collective-permute-start | bytes 49160 | tf_op jit(solution)/shard_map/ppermute | solution.py:385
  33.0 3.7 %collective-permute-start.15 = (bf16[2,16,256]{2,1,0:T(8,128)(2,1)S(1)}, bf16[2,16,256]{2,1,0:T(8,128)(2,1)S(1)}, u32[]{:S(2)}, u32[]{:S(2)}) collective-permute-start(bf16[2,16,256]{2,1,0:T(8,128)(2,1)S(1)} %get-tuple-element.76), channel_id=1, source_target_pairs={{0,4},{1,5},{2,6},{3,7},{4,0},{5,1},{6,2},{7,3},{8,12},{9,13},{10,... | collective-permute-start | bytes 49160 | tf_op jit(solution)/shard_map/ppermute | solution.py:385
  33.3 3.7 %collective-permute-start.16 = (bf16[2,16,256]{2,1,0:T(8,128)(2,1)S(1)}, bf16[2,16,256]{2,1,0:T(8,128)(2,1)S(1)}, u32[]{:S(2)}, u32[]{:S(2)}) collective-permute-start(bf16[2,16,256]{2,1,0:T(8,128)(2,1)S(1)} %get-tuple-element.77), channel_id=1, source_target_pairs={{0,2},{1,3},{2,0},{3,1},{4,6},{5,7},{6,4},{7,5},{8,10},{9,11},{10,... | collective-permute-start | bytes 49160 | tf_op jit(solution)/shard_map/ppermute | solution.py:385

commit v19 on v18

--- a/solution.py
+++ b/solution.py
@@ -341,8 +341,15 @@
     arrived = jnp.concatenate([x[...].reshape(2 * slots, -1) for x in arrived], axis=0)
     edges = edges_ref[me, 2 * first : 2 * first + count].reshape(count * slots, rows)
     far = dot(arrived, edges, FIRST)[: near_ref.shape[0]]
-    total = near_ref[...] + far / sums_ref[me, width : width + 1, :]
-    out_ref[...] = total.reshape(out_ref.shape)
+    out_ref[...] = near_ref[...] + far / sums_ref[me, width : width + 1, :]
+
+
+def scores_kernel(first, me_ref, *rest):
+    rest, (out_hbm, scores_ref, sem) = rest[:-3], rest[-3:]
+    last_kernel(first, me_ref, *rest, scores_ref)
+    copy = pltpu.make_async_copy(scores_ref, out_hbm.at[:, 0, :], sem)
+    copy.start()
+    copy.wait()
 
 
 def on_device(
@@ -547,12 +554,13 @@
         1 << 18,
     )(me, near, edges, sums, *arrived[:half])
     logits = call(
-        functools.partial(last_kernel, half),
+        functools.partial(scores_kernel, half),
         shape(classes, 1, rows, dtype=f32),
         [SM] + [VM] * (3 + chips - half),
-        (),
+        [pltpu.VMEM((classes, rows), f32), pltpu.SemaphoreType.DMA],
         rows * parts * slots * classes,
         1 << 19,
+        out_specs=HB,
     )(me, near, edges, sums, *arrived[half:])
     return hidden[None], logits.transpose(1, 0, 2)
 

time: 38.2 us -> 38.1 us (level)
  no operation moved by 1% of the time
where the time goes in v19:
time: 38.1 us; the launch traced here: 37.9 us
  starting transfers between devices  21.9 us (57%)
  Pallas kernels  8.87 us (23%)
  waiting for transfers between devices  6.37 us (17%)
  between operations  0.79 us (2%)
    ppermute x9, starting transfers between devices, shift(): lax.ppermute(block, 'feat', [(i, ahead(i, groups, k, near)) for i in rang...  13.5 us
    pallas_call x16, Pallas kernels, placed(): run(*(pltpu.with_memory_space_constraint(value, pltpu.HBM) if spec is HB...  8.87 us
    ppermute x6, starting transfers between devices, to_chips(): lax.ppermute(blocks[j], 'dom', [(d, next_to(d // 2, j, chips) * 2 + d % 2...  7.8 us
    ppermute x9, waiting for transfers between devices, shift(): lax.ppermute(block, 'feat', [(i, ahead(i, groups, k, near)) for i in rang...  3.25 us
    ppermute x6, waiting for transfers between devices, to_chips(): lax.ppermute(blocks[j], 'dom', [(d, next_to(d // 2, j, chips) * 2 + d % 2...  1.92 us
    ppermute x2, waiting for transfers between devices, to_mate(): return lax.ppermute(value, 'dom', [(d, d ^ 1) for d in range(parts)])  1.2 us
  transfers between devices with their start and end apart: 17, of which 8 were waited for; matrix products, arithmetic and copies ran while one was open for 0% of the time, Pallas kernels for 16%

profile of v19, /device:TPU:0, one launch (start us, length us, event | category | flops | bytes accessed | tf_op | source)
XLA Modules:
  0.0 37.9 jit_solution(2114286784625078281)
XLA Ops:
  0.6 1.3 %shard_map.122 = (bf16[4,64,256]{2,1,0:T(8,128)(2,1)S(1)}, bf16[256,512]{1,0:T(8,128)(2,1)S(1)}, s32[8,4,16]{2,1,0:T(4,128)S(1)}, bf16[12,128,128]{2,1,0:T(8,128...) custom-call(s32[1]{0:T(128)} %bitcast.4.part_ref, ...), custom_call_target="tpu_custom_call" | custom-call | flops 100663296 | bytes 1048576 | tf_op jit(solution)/shard_map/pallas_call | solution.py:33
  1.9 0.5 %collective-permute-start = (bf16[4,64,256]{2,1,0:T(8,128)(2,1)S(1)}, bf16[4,64,256]{2,1,0:T(8,128)(2,1)S(1)}, u32[]{:S(2)}, u32[]{:S(2)}) collective-permute-start(bf16[4,64,256]{2,1,0:T(8,128)(2,1)S(1)} %get-tuple-element.49), channel_id=1, source_target_pairs={{0,1},{1,0},{2,3},{3,2},{4,5},{5,4},{6,7},{7,6},{8,9},{9,8},{10,11... | collective-permute-start | bytes 393224 | tf_op jit(solution)/shard_map/ppermute | solution.py:388
  2.5 1.2 %shard_map.123 = (f32[4,208,128]{2,1,0:T(8,128)S(1)}, bf16[4,8,16,128]{3,2,1,0:T(8,128)(2,1)S(1)}, bf16[128,512]{1,0:T(8,128)(2,1)S(1)}, bf16[4,64,256]{2,1,0:T(...) custom-call(s32[1]{0:T(128)} %bitcast.me_ref.rest_0_, ...), custom_call_target="tpu_custom_call" | custom-call | flops 100663296 | bytes 1048576 | tf_op jit(solution)/shard_map/pallas_call | solution.py:33
  3.6 0.0 collective-permute-done.got_ref
  3.7 3.7 %collective-permute-start.4 = (bf16[2,64,256]{2,1,0:T(8,128)(2,1)S(1)}, bf16[2,64,256]{2,1,0:T(8,128)(2,1)S(1)}, u32[]{:S(2)}, u32[]{:S(2)}) collective-permute-start(bf16[2,64,256]{2,1,0:T(8,128)(2,1)S(1)} %get-tuple-element.59), channel_id=1, source_target_pairs={{0,6},{1,7},{2,4},{3,5},{4,2},{5,3},{6,0},{7,1},{8,14},{9,15},{10,... | collective-permute-start | bytes 196616 | tf_op jit(solution)/shard_map/ppermute | solution.py:392
  7.4 0.5 %collective-permute-start.5 = (bf16[2,64,256]{2,1,0:T(8,128)(2,1)S(1)}, bf16[2,64,256]{2,1,0:T(8,128)(2,1)S(1)}, u32[]{:S(2)}, u32[]{:S(2)}) collective-permute-start(bf16[2,64,256]{2,1,0:T(8,128)(2,1)S(1)} %get-tuple-element.60), channel_id=1, source_target_pairs={{0,4},{1,5},{2,6},{3,7},{4,0},{5,1},{6,2},{7,3},{8,12},{9,13},{10,... | collective-permute-start | bytes 196616 | tf_op jit(solution)/shard_map/ppermute | solution.py:392
  7.9 0.1 collective-permute-start.6
  8.0 3.0 %collective-permute-start.1 = (bf16[192,128]{1,0:T(8,128)(2,1)S(1)}, bf16[192,128]{1,0:T(8,128)(2,1)S(1)}, u32[]{:S(2)}, u32[]{:S(2)}) collective-permute-start(bf16[192,128]{1,0:T(8,128)(2,1)S(1)} %get-tuple-element.53), channel_id=1, source_target_pairs={{0,16},{8,24},{16,0},{24,8},{1,17},{9,25},{17,1},{25,9},{2,18},{10... | collective-permute-start | bytes 147464 | tf_op jit(solution)/shard_map/ppermute | solution.py:383
  11.0 1.3 %collective-permute-start.2 = (bf16[192,128]{1,0:T(8,128)(2,1)S(1)}, bf16[192,128]{1,0:T(8,128)(2,1)S(1)}, u32[]{:S(2)}, u32[]{:S(2)}) collective-permute-start(bf16[192,128]{1,0:T(8,128)(2,1)S(1)} %get-tuple-element.54), channel_id=1, source_target_pairs={{0,24},{8,16},{16,8},{24,0},{1,25},{9,17},{17,9},{25,1},{2,26},{10... | collective-permute-start | bytes 147464 | tf_op jit(solution)/shard_map/ppermute | solution.py:383
  12.3 0.0 collective-permute-done.4.rest_4_.rest_1_
  12.3 0.2 collective-permute-start.3
  12.6 0.0 collective-permute-done.5.rest_5_.rest_2_
  12.6 0.0 collective-permute-done.6.rest_6_.rest_3_
  12.6 0.2 shard_map.127
  12.8 3.2 %collective-permute-start.7 = (bf16[192,128]{1,0:T(8,128)(2,1)S(1)}, bf16[192,128]{1,0:T(8,128)(2,1)S(1)}, u32[]{:S(2)}, u32[]{:S(2)}) collective-permute-start(bf16[192,128]{1,0:T(8,128)(2,1)S(1)} %get-tuple-element.62), channel_id=1, source_target_pairs={{0,24},{8,16},{16,8},{24,0},{1,25},{9,17},{17,9},{25,1},{2,26},{10... | collective-permute-start | bytes 147464 | tf_op jit(solution)/shard_map/ppermute | solution.py:383
  16.0 0.1 collective-permute-start.8
  16.1 0.0 collective-permute-done.1.rest_0_
  16.1 1.1 %collective-permute-start.9 = (bf16[192,128]{1,0:T(8,128)(2,1)S(1)}, bf16[192,128]{1,0:T(8,128)(2,1)S(1)}, u32[]{:S(2)}, u32[]{:S(2)}) collective-permute-start(bf16[192,128]{1,0:T(8,128)(2,1)S(1)} %get-tuple-element.64), channel_id=1, source_target_pairs={{0,8},{8,0},{16,24},{24,16},{1,9},{9,1},{17,25},{25,17},{2,10},{10... | collective-permute-start | bytes 147464 | tf_op jit(solution)/shard_map/ppermute | solution.py:383
  17.3 0.2 collective-permute-done.2.rest_1_
  17.4 0.0 collective-permute-done.3.rest_2_
  17.5 1.8 %shard_map.125.after.own_ref = f32[128,1024]{1,0:T(8,128)S(1)} custom-call(s32[1]{0:T(128)} %bitcast.me_ref.rest_0_, bf16[192,512]{1,0:T(8,128)(2,1)} %bitcast.22, bf16[768,1024]{1,0:T(8,128)(2,1)} %weight_hbm.1, bf16[192,128]{1,0:T(8,128)(2,1)S(1)} %collective-permute-done.1.rest_0_, bf16[192,128]{1,0:T(8,128)(2,1)S(1)} %collective-permute-done.2.rest_1_, ...), custom_call_target="tpu_custom_call" | custom-call | flops 201326592 | bytes 2097152 | tf_op jit(solution)/shard_map/pallas_call | solution.py:33
  19.3 0.2 shard_map.126.rest_0_
  19.5 0.0 collective-permute-done.7.rest_1_
  19.5 0.3 shard_map.128.early_ref
  19.8 1.4 %collective-permute-done.8.rest_0_ = bf16[192,128]{1,0:T(8,128)(2,1)S(1)} collective-permute-done((bf16[192,128]{1,0:T(8,128)(2,1)S(1)}, bf16[192,128]{1,0:T(8,128)(2,1)S(1)}, u32[]{:S(2)}, u32[]{:S(2)}) %collective-permute-start.8) | collective-permute-done | bytes 49184 | tf_op jit(solution)/shard_map/ppermute | solution.py:383
  21.2 0.0 collective-permute-done.9.rest_1_
  21.2 0.5 %shard_map.129 = (bf16[128,1024]{1,0:T(8,128)(2,1)S(1)}, bf16[153,128]{1,0:T(8,128)(2,1)S(1)}, bf16[153,128]{1,0:T(8,128)(2,1)S(1)}, bf16[153,128]{1,0:T(8,128)(2,1)S(1)}, bf16[153,128]{1,0:T(8,128)(2,1)S(1)}) custom-call(s32[1]{0:T(128)} %bitcast.me_ref.rest_0_, bf16[768,1024]{1,0:T(8,128)(2,1)S(1)} %copy-done, bf16[153,1024]{1,0:T(8,128)(2,1)S(1)} %bitcast.20, ...), custom_call_target="tpu_custom_call" | custom-call | flops 100663296 | bytes 2097152 | tf_op jit(solution)/shard_map/pallas_call | solution.py:33
  21.8 2.3 %collective-permute-start.10 = (bf16[153,128]{1,0:T(8,128)(2,1)S(1)}, bf16[153,128]{1,0:T(8,128)(2,1)S(1)}, u32[]{:S(2)}, u32[]{:S(2)}) collective-permute-start(bf16[153,128]{1,0:T(8,128)(2,1)S(1)} %get-tuple-element.69), channel_id=1, source_target_pairs={{0,24},{8,16},{16,8},{24,0},{1,25},{9,17},{17,9},{25,1},{2,26},{10... | collective-permute-start | bytes 117512 | tf_op jit(solution)/shard_map/ppermute | solution.py:383
  24.0 0.0 collective-permute-start.11
  24.0 2.2 %collective-permute-start.12 = (bf16[153,128]{1,0:T(8,128)(2,1)S(1)}, bf16[153,128]{1,0:T(8,128)(2,1)S(1)}, u32[]{:S(2)}, u32[]{:S(2)}) collective-permute-start(bf16[153,128]{1,0:T(8,128)(2,1)S(1)} %get-tuple-element.71), channel_id=1, source_target_pairs={{0,8},{8,0},{16,24},{24,16},{1,9},{9,1},{17,25},{25,17},{2,10},{10... | collective-permute-start | bytes 117512 | tf_op jit(solution)/shard_map/ppermute | solution.py:383
  26.2 0.9 %shard_map.132.hits_ref.after = bf16[128,512]{1,0:T(8,128)(2,1)S(1)} custom-call(bf16[153,128]{1,0:T(8,128)(2,1)S(1)} %get-tuple-element.68.rest_0_.after, s32[1]{0:T(128)} %bitcast.me_ref.rest_0_, s32[1]{0:T(128)} %bitcast.4.part_ref, s32[8,4,16]{2,1,0:T(4,128)} %bitcast.26), custom_call_target="tpu_custom_call" | custom-call | bytes 524288 | tf_op jit(solution)/shard_map/pallas_call | solution.py:33
  27.1 0.7 %collective-permute-done.10.rest_1_ = bf16[153,128]{1,0:T(8,128)(2,1)S(1)} collective-permute-done((bf16[153,128]{1,0:T(8,128)(2,1)S(1)}, bf16[153,128]{1,0:T(8,128)(2,1)S(1)}, u32[]{:S(2)}, u32[]{:S(2)}) %collective-permute-start.10) | collective-permute-done | bytes 39200 | tf_op jit(solution)/shard_map/ppermute | solution.py:383
  27.8 0.2 shard_map.133.early_ref
  28.0 1.0 %collective-permute-done.11.rest_2_.rest_0_ = bf16[153,128]{1,0:T(8,128)(2,1)S(1)} collective-permute-done((bf16[153,128]{1,0:T(8,128)(2,1)S(1)}, bf16[153,128]{1,0:T(8,128)(2,1)S(1)}, u32[]{:S(2)}, u32[]{:S(2)}) %collective-permute-start.11) | collective-permute-done | bytes 39200 | tf_op jit(solution)/shard_map/ppermute | solution.py:383
  29.0 0.0 collective-permute-done.12.rest_3_.rest_1_
  29.0 0.2 shard_map.134
  29.2 0.1 collective-permute-start.13
  29.3 1.2 %collective-permute-done.13.got_ref = bf16[4,16,256]{2,1,0:T(8,128)(2,1)S(1)} collective-permute-done((bf16[4,16,256]{2,1,0:T(8,128)(2,1)S(1)}, bf16[4,16,256]{2,1,0:T(8,128)(2,1)S(1)}, u32[]{:S(2)}, u32[]{:S(2)}) %collective-permute-start.13) | collective-permute-done | bytes 32800 | tf_op jit(solution)/shard_map/ppermute | solution.py:388
  30.5 2.4 %collective-permute-start.14 = (bf16[2,16,256]{2,1,0:T(8,128)(2,1)S(1)}, bf16[2,16,256]{2,1,0:T(8,128)(2,1)S(1)}, u32[]{:S(2)}, u32[]{:S(2)}) collective-permute-start(bf16[2,16,256]{2,1,0:T(8,128)(2,1)S(1)} %get-tuple-element.75), channel_id=1, source_target_pairs={{0,6},{1,7},{2,4},{3,5},{4,2},{5,3},{6,0},{7,1},{8,14},{9,15},{10,... | collective-permute-start | bytes 49160 | tf_op jit(solution)/shard_map/ppermute | solution.py:392
  33.0 0.4 collective-permute-start.15
  33.3 0.7 %collective-permute-start.16 = (bf16[2,16,256]{2,1,0:T(8,128)(2,1)S(1)}, bf16[2,16,256]{2,1,0:T(8,128)(2,1)S(1)}, u32[]{:S(2)}, u32[]{:S(2)}) collective-permute-start(bf16[2,16,256]{2,1,0:T(8,128)(2,1)S(1)} %get-tuple-element.77), channel_id=1, source_target_pairs={{0,2},{1,3},{2,0},{3,1},{4,6},{5,7},{6,4},{7,5},{8,10},{9,11},{10,... | collective-permute-start | bytes 49160 | tf_op jit(solution)/shard_map/ppermute | solution.py:392
  34.0 0.7 %shard_map.130 = (f32[153,128]{1,0:T(8,128)S(1)}, bf16[128,1024]{1,0:T(8,128)(2,1)}) custom-call(bf16[128,1024]{1,0:T(8,128)(2,1)S(1)} %get-tuple-element.65.hidden_ref, bf16[153,1024]{1,0:T(8,128)(2,1)S(1)} %bitcast.19), custom_call_target="tpu_custom_call" | custom-call | flops 40108032 | bytes 1048576 | tf_op jit(solution)/shard_map/pallas_call | solution.py:33
  34.7 0.2 shard_map.131.near_ref
  35.0 0.2 collective-permute-done.14.rest_1_
  35.1 0.2 shard_map.136.rest_0_
  35.3 1.3 %collective-permute-done.15.rest_3_ = bf16[2,16,256]{2,1,0:T(8,128)(2,1)S(1)} collective-permute-done((bf16[2,16,256]{2,1,0:T(8,128)(2,1)S(1)}, bf16[2,16,256]{2,1,0:T(8,128)(2,1)S(1)}, u32[]{:S(2)}, u32[]{:S(2)}) %collective-permute-start.15) | collective-permute-done | bytes 16416 | tf_op jit(solution)/shard_map/ppermute | solution.py:392
  36.7 0.4 collective-permute-done.16.rest_4_
  37.1 0.8 %shard_map.137 = f32[153,1,128]{2,1,0:T(1,128)} custom-call(s32[1]{0:T(128)} %bitcast.me_ref.rest_0_, f32[153,128]{1,0:T(8,128)S(1)} %shard_map.136.rest_0_, bf16[4,8,16,128]{3,2,1,0:T(8,128)(2,1)S(1)} %get-tuple-element.57.rest_2_.edges_ref.rest_1_, f32[4,208,128]{2,1,0:T(8,128)S(1)} %get-tuple-element.56.rest_1_.sums_ref.rest_2_, ...), custom_call_target="tpu_custom_call" | custom-call | flops 2506752 | bytes 524288 | tf_op jit(solution)/shard_map/pallas_call | solution.py:33
  (8 shorter events, 0.0 us)
Async XLA Ops:
  1.9 1.7 %collective-permute-start = (bf16[4,64,256]{2,1,0:T(8,128)(2,1)S(1)}, bf16[4,64,256]{2,1,0:T(8,128)(2,1)S(1)}, u32[]{:S(2)}, u32[]{:S(2)}) collective-permute-start(bf16[4,64,256]{2,1,0:T(8,128)(2,1)S(1)} %get-tuple-element.49), channel_id=1, source_target_pairs={{0,1},{1,0},{2,3},{3,2},{4,5},{5,4},{6,7},{7,6},{8,9},{9,8},{10,11... | collective-permute-start | bytes 393224 | tf_op jit(solution)/shard_map/ppermute | solution.py:388
  3.7 8.7 %collective-permute-start.4 = (bf16[2,64,256]{2,1,0:T(8,128)(2,1)S(1)}, bf16[2,64,256]{2,1,0:T(8,128)(2,1)S(1)}, u32[]{:S(2)}, u32[]{:S(2)}) collective-permute-start(bf16[2,64,256]{2,1,0:T(8,128)(2,1)S(1)} %get-tuple-element.59), channel_id=1, source_target_pairs={{0,6},{1,7},{2,4},{3,5},{4,2},{5,3},{6,0},{7,1},{8,14},{9,15},{10,... | collective-permute-start | bytes 196616 | tf_op jit(solution)/shard_map/ppermute | solution.py:392
  7.4 5.2 %collective-permute-start.5 = (bf16[2,64,256]{2,1,0:T(8,128)(2,1)S(1)}, bf16[2,64,256]{2,1,0:T(8,128)(2,1)S(1)}, u32[]{:S(2)}, u32[]{:S(2)}) collective-permute-start(bf16[2,64,256]{2,1,0:T(8,128)(2,1)S(1)} %get-tuple-element.60), channel_id=1, source_target_pairs={{0,4},{1,5},{2,6},{3,7},{4,0},{5,1},{6,2},{7,3},{8,12},{9,13},{10,... | collective-permute-start | bytes 196616 | tf_op jit(solution)/shard_map/ppermute | solution.py:392
  7.9 4.7 %collective-permute-start.6 = (bf16[2,64,256]{2,1,0:T(8,128)(2,1)S(1)}, bf16[2,64,256]{2,1,0:T(8,128)(2,1)S(1)}, u32[]{:S(2)}, u32[]{:S(2)}) collective-permute-start(bf16[2,64,256]{2,1,0:T(8,128)(2,1)S(1)} %get-tuple-element.61), channel_id=1, source_target_pairs={{0,2},{1,3},{2,0},{3,1},{4,6},{5,7},{6,4},{7,5},{8,10},{9,11},{10,... | collective-permute-start | bytes 196616 | tf_op jit(solution)/shard_map/ppermute | solution.py:392
  8.0 8.1 %collective-permute-start.1 = (bf16[192,128]{1,0:T(8,128)(2,1)S(1)}, bf16[192,128]{1,0:T(8,128)(2,1)S(1)}, u32[]{:S(2)}, u32[]{:S(2)}) collective-permute-start(bf16[192,128]{1,0:T(8,128)(2,1)S(1)} %get-tuple-element.53), channel_id=1, source_target_pairs={{0,16},{8,24},{16,0},{24,8},{1,17},{9,25},{17,1},{25,9},{2,18},{10... | collective-permute-start | bytes 147464 | tf_op jit(solution)/shard_map/ppermute | solution.py:383
  11.0 6.5 %collective-permute-start.2 = (bf16[192,128]{1,0:T(8,128)(2,1)S(1)}, bf16[192,128]{1,0:T(8,128)(2,1)S(1)}, u32[]{:S(2)}, u32[]{:S(2)}) collective-permute-start(bf16[192,128]{1,0:T(8,128)(2,1)S(1)} %get-tuple-element.54), channel_id=1, source_target_pairs={{0,24},{8,16},{16,8},{24,0},{1,25},{9,17},{17,9},{25,1},{2,26},{10... | collective-permute-start | bytes 147464 | tf_op jit(solution)/shard_map/ppermute | solution.py:383
  12.3 5.1 %collective-permute-start.3 = (bf16[192,128]{1,0:T(8,128)(2,1)S(1)}, bf16[192,128]{1,0:T(8,128)(2,1)S(1)}, u32[]{:S(2)}, u32[]{:S(2)}) collective-permute-start(bf16[192,128]{1,0:T(8,128)(2,1)S(1)} %get-tuple-element.55), channel_id=1, source_target_pairs={{0,8},{8,0},{16,24},{24,16},{1,9},{9,1},{17,25},{25,17},{2,10},{10... | collective-permute-start | bytes 147464 | tf_op jit(solution)/shard_map/ppermute | solution.py:383
  12.8 6.7 %collective-permute-start.7 = (bf16[192,128]{1,0:T(8,128)(2,1)S(1)}, bf16[192,128]{1,0:T(8,128)(2,1)S(1)}, u32[]{:S(2)}, u32[]{:S(2)}) collective-permute-start(bf16[192,128]{1,0:T(8,128)(2,1)S(1)} %get-tuple-element.62), channel_id=1, source_target_pairs={{0,24},{8,16},{16,8},{24,0},{1,25},{9,17},{17,9},{25,1},{2,26},{10... | collective-permute-start | bytes 147464 | tf_op jit(solution)/shard_map/ppermute | solution.py:383
  16.0 5.2 %collective-permute-start.8 = (bf16[192,128]{1,0:T(8,128)(2,1)S(1)}, bf16[192,128]{1,0:T(8,128)(2,1)S(1)}, u32[]{:S(2)}, u32[]{:S(2)}) collective-permute-start(bf16[192,128]{1,0:T(8,128)(2,1)S(1)} %get-tuple-element.63), channel_id=1, source_target_pairs={{0,16},{8,24},{16,0},{24,8},{1,17},{9,25},{17,1},{25,9},{2,18},{10... | collective-permute-start | bytes 147464 | tf_op jit(solution)/shard_map/ppermute | solution.py:383
  16.1 3.4 %copy-start = (bf16[768,1024]{1,0:T(8,128)(2,1)S(1)}, bf16[768,1024]{1,0:T(8,128)(2,1)}, u32[]{:S(2)}) copy-start(bf16[768,1024]{1,0:T(8,128)(2,1)} %weight_ref.3) | copy-start | bytes 4718596
  16.1 5.1 %collective-permute-start.9 = (bf16[192,128]{1,0:T(8,128)(2,1)S(1)}, bf16[192,128]{1,0:T(8,128)(2,1)S(1)}, u32[]{:S(2)}, u32[]{:S(2)}) collective-permute-start(bf16[192,128]{1,0:T(8,128)(2,1)S(1)} %get-tuple-element.64), channel_id=1, source_target_pairs={{0,8},{8,0},{16,24},{24,16},{1,9},{9,1},{17,25},{25,17},{2,10},{10... | collective-permute-start | bytes 147464 | tf_op jit(solution)/shard_map/ppermute | solution.py:383
  19.5 1.7 %copy-start.2 = (bf16[1024,153]{0,1:T(8,128)(2,1)S(1)}, bf16[1024,153]{0,1:T(8,128)(2,1)}, u32[]{:S(2)}) copy-start(bf16[1024,153]{0,1:T(8,128)(2,1)} %param.21) | copy-start | bytes 940036
  21.2 12.8 %copy-start.1 = (bf16[1024,153]{0,1:T(8,128)(2,1)S(1)}, bf16[1024,153]{0,1:T(8,128)(2,1)}, u32[]{:S(2)}) copy-start(bf16[1024,153]{0,1:T(8,128)(2,1)} %param.20) | copy-start | bytes 940036
  21.8 6.0 %collective-permute-start.10 = (bf16[153,128]{1,0:T(8,128)(2,1)S(1)}, bf16[153,128]{1,0:T(8,128)(2,1)S(1)}, u32[]{:S(2)}, u32[]{:S(2)}) collective-permute-start(bf16[153,128]{1,0:T(8,128)(2,1)S(1)} %get-tuple-element.69), channel_id=1, source_target_pairs={{0,24},{8,16},{16,8},{24,0},{1,25},{9,17},{17,9},{25,1},{2,26},{10... | collective-permute-start | bytes 117512 | tf_op jit(solution)/shard_map/ppermute | solution.py:383
  24.0 5.0 %collective-permute-start.11 = (bf16[153,128]{1,0:T(8,128)(2,1)S(1)}, bf16[153,128]{1,0:T(8,128)(2,1)S(1)}, u32[]{:S(2)}, u32[]{:S(2)}) collective-permute-start(bf16[153,128]{1,0:T(8,128)(2,1)S(1)} %get-tuple-element.70), channel_id=1, source_target_pairs={{0,16},{8,24},{16,0},{24,8},{1,17},{9,25},{17,1},{25,9},{2,18},{10... | collective-permute-start | bytes 117512 | tf_op jit(solution)/shard_map/ppermute | solution.py:383
  24.0 5.0 %collective-permute-start.12 = (bf16[153,128]{1,0:T(8,128)(2,1)S(1)}, bf16[153,128]{1,0:T(8,128)(2,1)S(1)}, u32[]{:S(2)}, u32[]{:S(2)}) collective-permute-start(bf16[153,128]{1,0:T(8,128)(2,1)S(1)} %get-tuple-element.71), channel_id=1, source_target_pairs={{0,8},{8,0},{16,24},{24,16},{1,9},{9,1},{17,25},{25,17},{2,10},{10... | collective-permute-start | bytes 117512 | tf_op jit(solution)/shard_map/ppermute | solution.py:383
  29.2 1.3 %collective-permute-start.13 = (bf16[4,16,256]{2,1,0:T(8,128)(2,1)S(1)}, bf16[4,16,256]{2,1,0:T(8,128)(2,1)S(1)}, u32[]{:S(2)}, u32[]{:S(2)}) collective-permute-start(bf16[4,16,256]{2,1,0:T(8,128)(2,1)S(1)} %get-tuple-element.73), channel_id=1, source_target_pairs={{0,1},{1,0},{2,3},{3,2},{4,5},{5,4},{6,7},{7,6},{8,9},{9,8},{10,11... | collective-permute-start | bytes 98312 | tf_op jit(solution)/shard_map/ppermute | solution.py:388
  30.5 4.6 %collective-permute-start.14 = (bf16[2,16,256]{2,1,0:T(8,128)(2,1)S(1)}, bf16[2,16,256]{2,1,0:T(8,128)(2,1)S(1)}, u32[]{:S(2)}, u32[]{:S(2)}) collective-permute-start(bf16[2,16,256]{2,1,0:T(8,128)(2,1)S(1)} %get-tuple-element.75), channel_id=1, source_target_pairs={{0,6},{1,7},{2,4},{3,5},{4,2},{5,3},{6,0},{7,1},{8,14},{9,15},{10,... | collective-permute-start | bytes 49160 | tf_op jit(solution)/shard_map/ppermute | solution.py:392
  33.0 3.7 %collective-permute-start.15 = (bf16[2,16,256]{2,1,0:T(8,128)(2,1)S(1)}, bf16[2,16,256]{2,1,0:T(8,128)(2,1)S(1)}, u32[]{:S(2)}, u32[]{:S(2)}) collective-permute-start(bf16[2,16,256]{2,1,0:T(8,128)(2,1)S(1)} %get-tuple-element.76), channel_id=1, source_target_pairs={{0,4},{1,5},{2,6},{3,7},{4,0},{5,1},{6,2},{7,3},{8,12},{9,13},{10,... | collective-permute-start | bytes 49160 | tf_op jit(solution)/shard_map/ppermute | solution.py:392
  33.3 3.7 %collective-permute-start.16 = (bf16[2,16,256]{2,1,0:T(8,128)(2,1)S(1)}, bf16[2,16,256]{2,1,0:T(8,128)(2,1)S(1)}, u32[]{:S(2)}, u32[]{:S(2)}) collective-permute-start(bf16[2,16,256]{2,1,0:T(8,128)(2,1)S(1)} %get-tuple-element.77), channel_id=1, source_target_pairs={{0,2},{1,3},{2,0},{3,1},{4,6},{5,7},{6,4},{7,5},{8,10},{9,11},{10,... | collective-permute-start | bytes 49160 | tf_op jit(solution)/shard_map/ppermute | solution.py:392

commit v20 on v19

--- a/solution.py
+++ b/solution.py
@@ -18,24 +18,37 @@
 PASSED = 5
 
 
+class Place:
+    def __init__(self, axis):
+        self.axis = axis
+
+    def __getitem__(self, _):
+        return lax.axis_index(self.axis).astype(jnp.int32)
+
+
 def call(kernel, out_shape, in_specs, scratch=(), flops=0, size=0, limit=4, out_specs=None):
-    run = pl.pallas_call(
-        kernel,
-        out_shape=out_shape,
-        in_specs=in_specs,
-        out_specs=out_specs or jax.tree.map(lambda _: VM, out_shape),
-        scratch_shapes=list(scratch),
-        cost_estimate=pl.CostEstimate(flops=flops, bytes_accessed=size, transcendentals=0),
-        compiler_params=pltpu.CompilerParams(vmem_limit_bytes=limit << 20),
-    )
-
     def placed(*operands):
-        return run(
-            *(
-                pltpu.with_memory_space_constraint(value, pltpu.HBM) if spec is HB else value
-                for value, spec in zip(operands, in_specs)
-            )
-        )
+        places = [value if isinstance(value, Place) else None for value in operands]
+        arrays = [
+            pltpu.with_memory_space_constraint(value, pltpu.HBM) if spec is HB else value
+            for value, spec in zip(operands, in_specs)
+            if spec is not SM
+        ]
+
+        def body(*refs):
+            rest = iter(refs)
+            first = [place if place is not None else next(rest) for place in places]
+            kernel(*first, *rest)
+
+        return pl.pallas_call(
+            body,
+            out_shape=out_shape,
+            in_specs=[spec for spec in in_specs if spec is not SM],
+            out_specs=out_specs or jax.tree.map(lambda _: VM, out_shape),
+            scratch_shapes=list(scratch),
+            cost_estimate=pl.CostEstimate(flops=flops, bytes_accessed=size, transcendentals=0),
+            compiler_params=pltpu.CompilerParams(vmem_limit_bytes=limit << 20),
+        )(*arrays)
 
     return placed
 
@@ -367,8 +380,7 @@
 ):
     feature_rows, tile_contents = features[0].T, tiles[0]
     groups, parts = lax.axis_size("feat"), lax.axis_size("dom")
-    me = lax.axis_index("feat").astype(jnp.int32).reshape(1)
-    part = lax.axis_index("dom").astype(jnp.int32).reshape(1)
+    me, part = Place("feat"), Place("dom")
     width, nodes = feature_rows.shape
     rows, slots = nodes // groups, sources.shape[3]
     hid, classes = self_one.shape[1], self_out.shape[1]

time: 38.1 us -> 38.2 us (level)
  no operation moved by 1% of the time
where the time goes in v20:
time: 38.2 us; the launch traced here: 38 us
  starting transfers between devices  21.8 us (57%)
  Pallas kernels  8.94 us (23%)
  waiting for transfers between devices  6.42 us (17%)
  between operations  0.79 us (2%)
    ppermute x9, starting transfers between devices, shift(): lax.ppermute(block, 'feat', [(i, ahead(i, groups, k, near)) for i in rang...  13.5 us
    pallas_call x16, Pallas kernels, placed(): pl.pallas_call(body, out_shape=out_shape, in_specs=[spec for spec in in_s...  8.94 us
    ppermute x6, starting transfers between devices, to_chips(): lax.ppermute(blocks[j], 'dom', [(d, next_to(d // 2, j, chips) * 2 + d % 2...  7.74 us
    ppermute x9, waiting for transfers between devices, shift(): lax.ppermute(block, 'feat', [(i, ahead(i, groups, k, near)) for i in rang...  3.24 us
    ppermute x6, waiting for transfers between devices, to_chips(): lax.ppermute(blocks[j], 'dom', [(d, next_to(d // 2, j, chips) * 2 + d % 2...  1.99 us
    ppermute x2, waiting for transfers between devices, to_mate(): return lax.ppermute(value, 'dom', [(d, d ^ 1) for d in range(parts)])  1.2 us
  transfers between devices with their start and end apart: 17, of which 8 were waited for; matrix products, arithmetic and copies ran while one was open for 0% of the time, Pallas kernels for 16%

profile of v20, /device:TPU:0, one launch (start us, length us, event | category | flops | bytes accessed | tf_op | source)
XLA Modules:
  0.0 38.0 jit_solution(2848835938932923412)
XLA Ops:
  0.6 1.3 %shard_map.122 = (bf16[4,64,256]{2,1,0:T(8,128)(2,1)S(1)}, bf16[256,512]{1,0:T(8,128)(2,1)S(1)}, s32[8,4,16]{2,1,0:T(4,128)S(1)}, bf16[12,128,128]{2,1,0:T(8,128...) custom-call(s32[8,4,16]{2,1,0:T(4,128)} %bitcast.23, ...), custom_call_target="tpu_custom_call" | custom-call | flops 100663296 | bytes 1048576 | tf_op jit(solution)/shard_map/pallas_call | solution.py:43
  1.9 0.5 %collective-permute-start = (bf16[4,64,256]{2,1,0:T(8,128)(2,1)S(1)}, bf16[4,64,256]{2,1,0:T(8,128)(2,1)S(1)}, u32[]{:S(2)}, u32[]{:S(2)}) collective-permute-start(bf16[4,64,256]{2,1,0:T(8,128)(2,1)S(1)} %get-tuple-element.49), channel_id=1, source_target_pairs={{0,1},{1,0},{2,3},{3,2},{4,5},{5,4},{6,7},{7,6},{8,9},{9,8},{10,11... | collective-permute-start | bytes 393224 | tf_op jit(solution)/shard_map/ppermute | solution.py:400
  2.4 1.2 %shard_map.123 = (f32[4,208,128]{2,1,0:T(8,128)S(1)}, bf16[4,8,16,128]{3,2,1,0:T(8,128)(2,1)S(1)}, bf16[128,512]{1,0:T(8,128)(2,1)S(1)}, bf16[4,64,256]{2,1,0:T(...) custom-call(bf16[256,512]{1,0:T(8,128)(2,1)S(1)} %get-tuple-element.40.ref, ...), custom_call_target="tpu_custom_call" | custom-call | flops 100663296 | bytes 1048576 | tf_op jit(solution)/shard_map/pallas_call | solution.py:43
  3.7 0.0 collective-permute-done.refs_2_
  3.7 3.6 %collective-permute-start.4 = (bf16[2,64,256]{2,1,0:T(8,128)(2,1)S(1)}, bf16[2,64,256]{2,1,0:T(8,128)(2,1)S(1)}, u32[]{:S(2)}, u32[]{:S(2)}) collective-permute-start(bf16[2,64,256]{2,1,0:T(8,128)(2,1)S(1)} %get-tuple-element.59), channel_id=1, source_target_pairs={{0,6},{1,7},{2,4},{3,5},{4,2},{5,3},{6,0},{7,1},{8,14},{9,15},{10,... | collective-permute-start | bytes 196616 | tf_op jit(solution)/shard_map/ppermute | solution.py:404
  7.3 0.5 %collective-permute-start.5 = (bf16[2,64,256]{2,1,0:T(8,128)(2,1)S(1)}, bf16[2,64,256]{2,1,0:T(8,128)(2,1)S(1)}, u32[]{:S(2)}, u32[]{:S(2)}) collective-permute-start(bf16[2,64,256]{2,1,0:T(8,128)(2,1)S(1)} %get-tuple-element.60), channel_id=1, source_target_pairs={{0,4},{1,5},{2,6},{3,7},{4,0},{5,1},{6,2},{7,3},{8,12},{9,13},{10,... | collective-permute-start | bytes 196616 | tf_op jit(solution)/shard_map/ppermute | solution.py:404
  7.8 0.1 collective-permute-start.6
  8.0 3.0 %collective-permute-start.1 = (bf16[192,128]{1,0:T(8,128)(2,1)S(1)}, bf16[192,128]{1,0:T(8,128)(2,1)S(1)}, u32[]{:S(2)}, u32[]{:S(2)}) collective-permute-start(bf16[192,128]{1,0:T(8,128)(2,1)S(1)} %get-tuple-element.53), channel_id=1, source_target_pairs={{0,16},{8,24},{16,0},{24,8},{1,17},{9,25},{17,1},{25,9},{2,18},{10... | collective-permute-start | bytes 147464 | tf_op jit(solution)/shard_map/ppermute | solution.py:395
  11.0 1.3 %collective-permute-start.2 = (bf16[192,128]{1,0:T(8,128)(2,1)S(1)}, bf16[192,128]{1,0:T(8,128)(2,1)S(1)}, u32[]{:S(2)}, u32[]{:S(2)}) collective-permute-start(bf16[192,128]{1,0:T(8,128)(2,1)S(1)} %get-tuple-element.54), channel_id=1, source_target_pairs={{0,24},{8,16},{16,8},{24,0},{1,25},{9,17},{17,9},{25,1},{2,26},{10... | collective-permute-start | bytes 147464 | tf_op jit(solution)/shard_map/ppermute | solution.py:395
  12.3 0.0 collective-permute-done.4.refs_4_.refs_3_
  12.3 0.2 collective-permute-start.3
  12.5 0.0 collective-permute-done.5.refs_5_.refs_4_
  12.5 0.0 collective-permute-done.6.refs_6_.refs_5_
  12.6 0.2 shard_map.127
  12.8 3.2 %collective-permute-start.7 = (bf16[192,128]{1,0:T(8,128)(2,1)S(1)}, bf16[192,128]{1,0:T(8,128)(2,1)S(1)}, u32[]{:S(2)}, u32[]{:S(2)}) collective-permute-start(bf16[192,128]{1,0:T(8,128)(2,1)S(1)} %get-tuple-element.62), channel_id=1, source_target_pairs={{0,24},{8,16},{16,8},{24,0},{1,25},{9,17},{17,9},{25,1},{2,26},{10... | collective-permute-start | bytes 147464 | tf_op jit(solution)/shard_map/ppermute | solution.py:395
  16.0 0.1 collective-permute-start.8
  16.1 0.0 collective-permute-done.1.refs_2_
  16.1 1.1 %collective-permute-start.9 = (bf16[192,128]{1,0:T(8,128)(2,1)S(1)}, bf16[192,128]{1,0:T(8,128)(2,1)S(1)}, u32[]{:S(2)}, u32[]{:S(2)}) collective-permute-start(bf16[192,128]{1,0:T(8,128)(2,1)S(1)} %get-tuple-element.64), channel_id=1, source_target_pairs={{0,8},{8,0},{16,24},{24,16},{1,9},{9,1},{17,25},{25,17},{2,10},{10... | collective-permute-start | bytes 147464 | tf_op jit(solution)/shard_map/ppermute | solution.py:395
  17.3 0.2 collective-permute-done.2.refs_3_
  17.5 0.0 collective-permute-done.3.refs_4_
  17.5 1.8 %shard_map.125.refs_0_.refs_1_ = f32[128,1024]{1,0:T(8,128)S(1)} custom-call(bf16[192,512]{1,0:T(8,128)(2,1)} %bitcast.20, bf16[768,1024]{1,0:T(8,128)(2,1)} %refs_1_.1, bf16[192,128]{1,0:T(8,128)(2,1)S(1)} %collective-permute-done.1.refs_2_, bf16[192,128]{1,0:T(8,128)(2,1)S(1)} %collective-permute-done.2.refs_3_, ...), custom_call_target="tpu_custom_call" | custom-call | flops 201326592 | bytes 2097152 | tf_op jit(solution)/shard_map/pallas_call | solution.py:43
  19.3 0.2 shard_map.126.refs_2_
  19.5 0.0 collective-permute-done.7.refs_3_
  19.5 0.3 shard_map.128.refs_2_
  19.8 1.3 %collective-permute-done.8.refs_3_ = bf16[192,128]{1,0:T(8,128)(2,1)S(1)} collective-permute-done((bf16[192,128]{1,0:T(8,128)(2,1)S(1)}, bf16[192,128]{1,0:T(8,128)(2,1)S(1)}, u32[]{:S(2)}, u32[]{:S(2)}) %collective-permute-start.8) | collective-permute-done | bytes 49184 | tf_op jit(solution)/shard_map/ppermute | solution.py:395
  21.2 0.0 collective-permute-done.9.refs_4_
  21.2 0.5 %shard_map.129 = (bf16[128,1024]{1,0:T(8,128)(2,1)S(1)}, bf16[153,128]{1,0:T(8,128)(2,1)S(1)}, bf16[153,128]{1,0:T(8,128)(2,1)S(1)}, bf16[153,128]{1,0:T(8,128)(2,1)S(1)}, bf16[153,128]{1,0:T(8,128)(2,1)S(1)}) custom-call(bf16[768,1024]{1,0:T(8,128)(2,1)S(1)} %copy-done, bf16[153,1024]{1,0:T(8,128)(2,1)S(1)} %bitcast.17, ...), custom_call_target="tpu_custom_call" | custom-call | flops 100663296 | bytes 2097152 | tf_op jit(solution)/shard_map/pallas_call | solution.py:43
  21.7 2.4 %collective-permute-start.10 = (bf16[153,128]{1,0:T(8,128)(2,1)S(1)}, bf16[153,128]{1,0:T(8,128)(2,1)S(1)}, u32[]{:S(2)}, u32[]{:S(2)}) collective-permute-start(bf16[153,128]{1,0:T(8,128)(2,1)S(1)} %get-tuple-element.69), channel_id=1, source_target_pairs={{0,24},{8,16},{16,8},{24,0},{1,25},{9,17},{17,9},{25,1},{2,26},{10... | collective-permute-start | bytes 117512 | tf_op jit(solution)/shard_map/ppermute | solution.py:395
  24.1 0.0 collective-permute-start.11
  24.1 2.1 %collective-permute-start.12 = (bf16[153,128]{1,0:T(8,128)(2,1)S(1)}, bf16[153,128]{1,0:T(8,128)(2,1)S(1)}, u32[]{:S(2)}, u32[]{:S(2)}) collective-permute-start(bf16[153,128]{1,0:T(8,128)(2,1)S(1)} %get-tuple-element.71), channel_id=1, source_target_pairs={{0,8},{8,0},{16,24},{24,16},{1,9},{9,1},{17,25},{25,17},{2,10},{10... | collective-permute-start | bytes 117512 | tf_op jit(solution)/shard_map/ppermute | solution.py:395
  26.2 0.9 %shard_map.132.refs_0_ = bf16[128,512]{1,0:T(8,128)(2,1)S(1)} custom-call(bf16[153,128]{1,0:T(8,128)(2,1)S(1)} %get-tuple-element.68.refs_3_.refs_0_.refs_1_, s32[8,4,16]{2,1,0:T(4,128)} %bitcast.24), custom_call_target="tpu_custom_call" | custom-call | bytes 524288 | tf_op jit(solution)/shard_map/pallas_call | solution.py:43
  27.1 0.7 %collective-permute-done.10.refs_4_.refs_2_ = bf16[153,128]{1,0:T(8,128)(2,1)S(1)} collective-permute-done((bf16[153,128]{1,0:T(8,128)(2,1)S(1)}, bf16[153,128]{1,0:T(8,128)(2,1)S(1)}, u32[]{:S(2)}, u32[]{:S(2)}) %collective-permute-start.10) | collective-permute-done | bytes 39200 | tf_op jit(solution)/shard_map/ppermute | solution.py:395
  27.8 0.2 shard_map.133.refs_1_
  28.0 1.0 %collective-permute-done.11.refs_5_.refs_2_ = bf16[153,128]{1,0:T(8,128)(2,1)S(1)} collective-permute-done((bf16[153,128]{1,0:T(8,128)(2,1)S(1)}, bf16[153,128]{1,0:T(8,128)(2,1)S(1)}, u32[]{:S(2)}, u32[]{:S(2)}) %collective-permute-start.11) | collective-permute-done | bytes 39200 | tf_op jit(solution)/shard_map/ppermute | solution.py:395
  29.0 0.0 collective-permute-done.12.refs_6_.refs_3_
  29.0 0.2 shard_map.134
  29.2 0.1 collective-permute-start.13
  29.3 1.2 %collective-permute-done.13.refs_2_ = bf16[4,16,256]{2,1,0:T(8,128)(2,1)S(1)} collective-permute-done((bf16[4,16,256]{2,1,0:T(8,128)(2,1)S(1)}, bf16[4,16,256]{2,1,0:T(8,128)(2,1)S(1)}, u32[]{:S(2)}, u32[]{:S(2)}) %collective-permute-start.13) | collective-permute-done | bytes 32800 | tf_op jit(solution)/shard_map/ppermute | solution.py:400
  30.5 2.5 %collective-permute-start.14 = (bf16[2,16,256]{2,1,0:T(8,128)(2,1)S(1)}, bf16[2,16,256]{2,1,0:T(8,128)(2,1)S(1)}, u32[]{:S(2)}, u32[]{:S(2)}) collective-permute-start(bf16[2,16,256]{2,1,0:T(8,128)(2,1)S(1)} %get-tuple-element.75), channel_id=1, source_target_pairs={{0,6},{1,7},{2,4},{3,5},{4,2},{5,3},{6,0},{7,1},{8,14},{9,15},{10,... | collective-permute-start | bytes 49160 | tf_op jit(solution)/shard_map/ppermute | solution.py:404
  33.0 0.4 collective-permute-start.15
  33.4 0.6 %collective-permute-start.16 = (bf16[2,16,256]{2,1,0:T(8,128)(2,1)S(1)}, bf16[2,16,256]{2,1,0:T(8,128)(2,1)S(1)}, u32[]{:S(2)}, u32[]{:S(2)}) collective-permute-start(bf16[2,16,256]{2,1,0:T(8,128)(2,1)S(1)} %get-tuple-element.77), channel_id=1, source_target_pairs={{0,2},{1,3},{2,0},{3,1},{4,6},{5,7},{6,4},{7,5},{8,10},{9,11},{10,... | collective-permute-start | bytes 49160 | tf_op jit(solution)/shard_map/ppermute | solution.py:404
  34.0 0.7 %shard_map.130 = (f32[153,128]{1,0:T(8,128)S(1)}, bf16[128,1024]{1,0:T(8,128)(2,1)}) custom-call(bf16[128,1024]{1,0:T(8,128)(2,1)S(1)} %get-tuple-element.65.refs_0_, bf16[153,1024]{1,0:T(8,128)(2,1)S(1)} %bitcast.18), custom_call_target="tpu_custom_call" | custom-call | flops 40108032 | bytes 1048576 | tf_op jit(solution)/shard_map/pallas_call | solution.py:43
  34.7 0.2 shard_map.131.refs_0_
  34.9 0.2 collective-permute-done.14.refs_4_
  35.1 0.2 shard_map.136.refs_0_
  35.3 1.4 %collective-permute-done.15.refs_3_ = bf16[2,16,256]{2,1,0:T(8,128)(2,1)S(1)} collective-permute-done((bf16[2,16,256]{2,1,0:T(8,128)(2,1)S(1)}, bf16[2,16,256]{2,1,0:T(8,128)(2,1)S(1)}, u32[]{:S(2)}, u32[]{:S(2)}) %collective-permute-start.15) | collective-permute-done | bytes 16416 | tf_op jit(solution)/shard_map/ppermute | solution.py:404
  36.8 0.4 collective-permute-done.16.refs_4_
  37.1 0.8 %shard_map.137 = f32[153,1,128]{2,1,0:T(1,128)} custom-call(f32[153,128]{1,0:T(8,128)S(1)} %shard_map.136.refs_0_, bf16[4,8,16,128]{3,2,1,0:T(8,128)(2,1)S(1)} %get-tuple-element.57.refs_2_.refs_1_, f32[4,208,128]{2,1,0:T(8,128)S(1)} %get-tuple-element.56.refs_1_.refs_0_.refs_2_, bf16[2,16,256]{2,1,0:T(8,128)(2,1)S(1)} %collective-permute-done.15.refs_3_, ...), custom_call_target="tpu_custom_call" | custom-call | flops 2506752 | bytes 524288 | tf_op jit(solution)/shard_map/pallas_call | solution.py:43
  (8 shorter events, 0.0 us)
Async XLA Ops:
  1.9 1.8 %collective-permute-start = (bf16[4,64,256]{2,1,0:T(8,128)(2,1)S(1)}, bf16[4,64,256]{2,1,0:T(8,128)(2,1)S(1)}, u32[]{:S(2)}, u32[]{:S(2)}) collective-permute-start(bf16[4,64,256]{2,1,0:T(8,128)(2,1)S(1)} %get-tuple-element.49), channel_id=1, source_target_pairs={{0,1},{1,0},{2,3},{3,2},{4,5},{5,4},{6,7},{7,6},{8,9},{9,8},{10,11... | collective-permute-start | bytes 393224 | tf_op jit(solution)/shard_map/ppermute | solution.py:400
  3.7 8.6 %collective-permute-start.4 = (bf16[2,64,256]{2,1,0:T(8,128)(2,1)S(1)}, bf16[2,64,256]{2,1,0:T(8,128)(2,1)S(1)}, u32[]{:S(2)}, u32[]{:S(2)}) collective-permute-start(bf16[2,64,256]{2,1,0:T(8,128)(2,1)S(1)} %get-tuple-element.59), channel_id=1, source_target_pairs={{0,6},{1,7},{2,4},{3,5},{4,2},{5,3},{6,0},{7,1},{8,14},{9,15},{10,... | collective-permute-start | bytes 196616 | tf_op jit(solution)/shard_map/ppermute | solution.py:404
  7.3 5.2 %collective-permute-start.5 = (bf16[2,64,256]{2,1,0:T(8,128)(2,1)S(1)}, bf16[2,64,256]{2,1,0:T(8,128)(2,1)S(1)}, u32[]{:S(2)}, u32[]{:S(2)}) collective-permute-start(bf16[2,64,256]{2,1,0:T(8,128)(2,1)S(1)} %get-tuple-element.60), channel_id=1, source_target_pairs={{0,4},{1,5},{2,6},{3,7},{4,0},{5,1},{6,2},{7,3},{8,12},{9,13},{10,... | collective-permute-start | bytes 196616 | tf_op jit(solution)/shard_map/ppermute | solution.py:404
  7.8 4.7 %collective-permute-start.6 = (bf16[2,64,256]{2,1,0:T(8,128)(2,1)S(1)}, bf16[2,64,256]{2,1,0:T(8,128)(2,1)S(1)}, u32[]{:S(2)}, u32[]{:S(2)}) collective-permute-start(bf16[2,64,256]{2,1,0:T(8,128)(2,1)S(1)} %get-tuple-element.61), channel_id=1, source_target_pairs={{0,2},{1,3},{2,0},{3,1},{4,6},{5,7},{6,4},{7,5},{8,10},{9,11},{10,... | collective-permute-start | bytes 196616 | tf_op jit(solution)/shard_map/ppermute | solution.py:404
  8.0 8.1 %collective-permute-start.1 = (bf16[192,128]{1,0:T(8,128)(2,1)S(1)}, bf16[192,128]{1,0:T(8,128)(2,1)S(1)}, u32[]{:S(2)}, u32[]{:S(2)}) collective-permute-start(bf16[192,128]{1,0:T(8,128)(2,1)S(1)} %get-tuple-element.53), channel_id=1, source_target_pairs={{0,16},{8,24},{16,0},{24,8},{1,17},{9,25},{17,1},{25,9},{2,18},{10... | collective-permute-start | bytes 147464 | tf_op jit(solution)/shard_map/ppermute | solution.py:395
  11.0 6.5 %collective-permute-start.2 = (bf16[192,128]{1,0:T(8,128)(2,1)S(1)}, bf16[192,128]{1,0:T(8,128)(2,1)S(1)}, u32[]{:S(2)}, u32[]{:S(2)}) collective-permute-start(bf16[192,128]{1,0:T(8,128)(2,1)S(1)} %get-tuple-element.54), channel_id=1, source_target_pairs={{0,24},{8,16},{16,8},{24,0},{1,25},{9,17},{17,9},{25,1},{2,26},{10... | collective-permute-start | bytes 147464 | tf_op jit(solution)/shard_map/ppermute | solution.py:395
  12.3 5.1 %collective-permute-start.3 = (bf16[192,128]{1,0:T(8,128)(2,1)S(1)}, bf16[192,128]{1,0:T(8,128)(2,1)S(1)}, u32[]{:S(2)}, u32[]{:S(2)}) collective-permute-start(bf16[192,128]{1,0:T(8,128)(2,1)S(1)} %get-tuple-element.55), channel_id=1, source_target_pairs={{0,8},{8,0},{16,24},{24,16},{1,9},{9,1},{17,25},{25,17},{2,10},{10... | collective-permute-start | bytes 147464 | tf_op jit(solution)/shard_map/ppermute | solution.py:395
  12.8 6.7 %collective-permute-start.7 = (bf16[192,128]{1,0:T(8,128)(2,1)S(1)}, bf16[192,128]{1,0:T(8,128)(2,1)S(1)}, u32[]{:S(2)}, u32[]{:S(2)}) collective-permute-start(bf16[192,128]{1,0:T(8,128)(2,1)S(1)} %get-tuple-element.62), channel_id=1, source_target_pairs={{0,24},{8,16},{16,8},{24,0},{1,25},{9,17},{17,9},{25,1},{2,26},{10... | collective-permute-start | bytes 147464 | tf_op jit(solution)/shard_map/ppermute | solution.py:395
  16.0 5.2 %collective-permute-start.8 = (bf16[192,128]{1,0:T(8,128)(2,1)S(1)}, bf16[192,128]{1,0:T(8,128)(2,1)S(1)}, u32[]{:S(2)}, u32[]{:S(2)}) collective-permute-start(bf16[192,128]{1,0:T(8,128)(2,1)S(1)} %get-tuple-element.63), channel_id=1, source_target_pairs={{0,16},{8,24},{16,0},{24,8},{1,17},{9,25},{17,1},{25,9},{2,18},{10... | collective-permute-start | bytes 147464 | tf_op jit(solution)/shard_map/ppermute | solution.py:395
  16.1 3.4 %copy-start = (bf16[768,1024]{1,0:T(8,128)(2,1)S(1)}, bf16[768,1024]{1,0:T(8,128)(2,1)}, u32[]{:S(2)}) copy-start(bf16[768,1024]{1,0:T(8,128)(2,1)} %refs_0_.3) | copy-start | bytes 4718596
  16.1 5.1 %collective-permute-start.9 = (bf16[192,128]{1,0:T(8,128)(2,1)S(1)}, bf16[192,128]{1,0:T(8,128)(2,1)S(1)}, u32[]{:S(2)}, u32[]{:S(2)}) collective-permute-start(bf16[192,128]{1,0:T(8,128)(2,1)S(1)} %get-tuple-element.64), channel_id=1, source_target_pairs={{0,8},{8,0},{16,24},{24,16},{1,9},{9,1},{17,25},{25,17},{2,10},{10... | collective-permute-start | bytes 147464 | tf_op jit(solution)/shard_map/ppermute | solution.py:395
  19.5 1.7 %copy-start.1 = (bf16[1024,153]{0,1:T(8,128)(2,1)S(1)}, bf16[1024,153]{0,1:T(8,128)(2,1)}, u32[]{:S(2)}) copy-start(bf16[1024,153]{0,1:T(8,128)(2,1)} %param.21) | copy-start | bytes 940036
  21.2 12.8 %copy-start.2 = (bf16[1024,153]{0,1:T(8,128)(2,1)S(1)}, bf16[1024,153]{0,1:T(8,128)(2,1)}, u32[]{:S(2)}) copy-start(bf16[1024,153]{0,1:T(8,128)(2,1)} %param.20) | copy-start | bytes 940036
  21.7 6.0 %collective-permute-start.10 = (bf16[153,128]{1,0:T(8,128)(2,1)S(1)}, bf16[153,128]{1,0:T(8,128)(2,1)S(1)}, u32[]{:S(2)}, u32[]{:S(2)}) collective-permute-start(bf16[153,128]{1,0:T(8,128)(2,1)S(1)} %get-tuple-element.69), channel_id=1, source_target_pairs={{0,24},{8,16},{16,8},{24,0},{1,25},{9,17},{17,9},{25,1},{2,26},{10... | collective-permute-start | bytes 117512 | tf_op jit(solution)/shard_map/ppermute | solution.py:395
  24.1 4.9 %collective-permute-start.11 = (bf16[153,128]{1,0:T(8,128)(2,1)S(1)}, bf16[153,128]{1,0:T(8,128)(2,1)S(1)}, u32[]{:S(2)}, u32[]{:S(2)}) collective-permute-start(bf16[153,128]{1,0:T(8,128)(2,1)S(1)} %get-tuple-element.70), channel_id=1, source_target_pairs={{0,16},{8,24},{16,0},{24,8},{1,17},{9,25},{17,1},{25,9},{2,18},{10... | collective-permute-start | bytes 117512 | tf_op jit(solution)/shard_map/ppermute | solution.py:395
  24.1 4.9 %collective-permute-start.12 = (bf16[153,128]{1,0:T(8,128)(2,1)S(1)}, bf16[153,128]{1,0:T(8,128)(2,1)S(1)}, u32[]{:S(2)}, u32[]{:S(2)}) collective-permute-start(bf16[153,128]{1,0:T(8,128)(2,1)S(1)} %get-tuple-element.71), channel_id=1, source_target_pairs={{0,8},{8,0},{16,24},{24,16},{1,9},{9,1},{17,25},{25,17},{2,10},{10... | collective-permute-start | bytes 117512 | tf_op jit(solution)/shard_map/ppermute | solution.py:395
  29.2 1.3 %collective-permute-start.13 = (bf16[4,16,256]{2,1,0:T(8,128)(2,1)S(1)}, bf16[4,16,256]{2,1,0:T(8,128)(2,1)S(1)}, u32[]{:S(2)}, u32[]{:S(2)}) collective-permute-start(bf16[4,16,256]{2,1,0:T(8,128)(2,1)S(1)} %get-tuple-element.73), channel_id=1, source_target_pairs={{0,1},{1,0},{2,3},{3,2},{4,5},{5,4},{6,7},{7,6},{8,9},{9,8},{10,11... | collective-permute-start | bytes 98312 | tf_op jit(solution)/shard_map/ppermute | solution.py:400
  30.5 4.6 %collective-permute-start.14 = (bf16[2,16,256]{2,1,0:T(8,128)(2,1)S(1)}, bf16[2,16,256]{2,1,0:T(8,128)(2,1)S(1)}, u32[]{:S(2)}, u32[]{:S(2)}) collective-permute-start(bf16[2,16,256]{2,1,0:T(8,128)(2,1)S(1)} %get-tuple-element.75), channel_id=1, source_target_pairs={{0,6},{1,7},{2,4},{3,5},{4,2},{5,3},{6,0},{7,1},{8,14},{9,15},{10,... | collective-permute-start | bytes 49160 | tf_op jit(solution)/shard_map/ppermute | solution.py:404
  33.0 3.7 %collective-permute-start.15 = (bf16[2,16,256]{2,1,0:T(8,128)(2,1)S(1)}, bf16[2,16,256]{2,1,0:T(8,128)(2,1)S(1)}, u32[]{:S(2)}, u32[]{:S(2)}) collective-permute-start(bf16[2,16,256]{2,1,0:T(8,128)(2,1)S(1)} %get-tuple-element.76), channel_id=1, source_target_pairs={{0,4},{1,5},{2,6},{3,7},{4,0},{5,1},{6,2},{7,3},{8,12},{9,13},{10,... | collective-permute-start | bytes 49160 | tf_op jit(solution)/shard_map/ppermute | solution.py:404
  33.4 3.7 %collective-permute-start.16 = (bf16[2,16,256]{2,1,0:T(8,128)(2,1)S(1)}, bf16[2,16,256]{2,1,0:T(8,128)(2,1)S(1)}, u32[]{:S(2)}, u32[]{:S(2)}) collective-permute-start(bf16[2,16,256]{2,1,0:T(8,128)(2,1)S(1)} %get-tuple-element.77), channel_id=1, source_target_pairs={{0,2},{1,3},{2,0},{3,1},{4,6},{5,7},{6,4},{7,5},{8,10},{9,11},{10,... | collective-permute-start | bytes 49160 | tf_op jit(solution)/shard_map/ppermute | solution.py:404

commit v21 on v19

--- a/solution.py
+++ b/solution.py
@@ -44,23 +44,33 @@
     return lax.dot_general(left, right, dims, preferred_element_type=f32)
 
 
-def step_of(groups, k, near=False):
-    if near and groups > 2 and k in (1, 2):
-        return groups - 3 + k
-    return (groups - k) % groups
+MEANS, FEATURES, SCORES = range(3)
+
+
+def step_of(count, k):
+    return (count - k) % count
+
+
+def shift_of(groups, k, what):
+    if what == SCORES or k < 2:
+        return k
+    return groups - 1 if k == 2 else groups - k + 1
 
 
 def whole_lanes(count):
     return -(-count // 128) * 128
 
 
-def ahead(me, groups, k, near=False):
-    step = step_of(groups, k, near)
-    return me ^ step if groups & (groups - 1) == 0 else (me + step) % groups
-
-
-def behind(me, groups, k, near=False):
-    step = step_of(groups, k, near)
+def ahead(me, groups, k, what=MEANS):
+    if what != MEANS:
+        return (me + shift_of(groups, k, what)) % groups
+    return next_to(me, k, groups)
+
+
+def behind(me, groups, k, what=MEANS):
+    if what != MEANS:
+        return (me + groups - shift_of(groups, k, what)) % groups
+    step = step_of(groups, k)
     return me ^ step if groups & (groups - 1) == 0 else (me + groups - step) % groups
 
 
@@ -160,7 +170,7 @@
     picked = order.shape[0]
     pick_rows(picked, 0, part_ref, sources_ref, table_ref, mine_ref, order, hits, lambda: None)
     for k in range(1, groups):
-        group = ahead(me_ref[0], groups, k, True)
+        group = ahead(me_ref[0], groups, k, FEATURES)
         blocks[k - 1][...] = table_ref[:width, pl.ds(pl.multiple_of(group * rows, rows), rows)]
     for copy in copies:
         copy.wait()
@@ -235,15 +245,15 @@
     mean_kernel(0, *rest)
 
 
-def rows_from(me, groups, k, width, near=False):
-    return pl.ds(pl.multiple_of(behind(me, groups, k, near) * width, width), width)
+def rows_from(me, groups, k, width, what=MEANS):
+    return pl.ds(pl.multiple_of(behind(me, groups, k, what) * width, width), width)
 
 
 def self_kernel(me_ref, features_hbm, weight_hbm, *rest):
     blocks, (out_ref, own_ref, weight_ref, sems) = rest[:-4], rest[-4:]
     groups, (width, rows) = len(blocks) + 1, own_ref.shape
     me = me_ref[0]
-    spans = [rows_from(me, groups, k, width, True) for k in range(groups)]
+    spans = [rows_from(me, groups, k, width, FEATURES) for k in range(groups)]
     own, *weights = fetch(
         sems,
         (features_hbm.at[:, pl.ds(pl.multiple_of(me * rows, rows), rows)], own_ref),
@@ -290,7 +300,7 @@
     rows = blocks[0].shape[1]
     total = None
     for k, block in enumerate(blocks, first):
-        at = pl.multiple_of(behind(me_ref[0], groups, k) * rows, rows)
+        at = pl.multiple_of(behind(me_ref[0], groups, k, SCORES) * rows, rows)
         term = dot(hits_ref[:, pl.ds(at, rows)], block[...], LAST)
         total = term if total is None else total + term
     return total
@@ -327,7 +337,7 @@
     me, width = me_ref[0], sums_ref.shape[1] - EXTRA
     total = None
     for k in range(groups):
-        at = pl.multiple_of(behind(me, groups, k) * rows, rows)
+        at = pl.multiple_of(behind(me, groups, k, SCORES) * rows, rows)
         term = dot(projected[k][...], band_ref[:, pl.ds(at, rows)], LAST)
         total = term if total is None else total + term
     out_ref[...] = own_ref[...] + total / sums_ref[me, width : width + 1, :]
@@ -378,9 +388,9 @@
     def shape(*dims, dtype=bf16):
         return jax.ShapeDtypeStruct(dims, dtype)
 
-    def shift(blocks, near=False):
+    def shift(blocks, what=MEANS):
         return [
-            lax.ppermute(block, "feat", [(i, ahead(i, groups, k, near)) for i in range(groups)])
+            lax.ppermute(block, "feat", [(i, ahead(i, groups, k, what)) for i in range(groups)])
             for k, block in enumerate(blocks, 1)
         ]
 
@@ -449,7 +459,7 @@
         1 << 20,
     )(band, mine, mate, *feature_blocks)
     arrived = to_chips(paired[:chips])
-    feature_blocks = shift(paired[chips:], near=True)
+    feature_blocks = shift(paired[chips:], FEATURES)
     means = call(
         functools.partial(mean_kernel, 1),
         (shape(width, rows),) * (groups - 1),
@@ -504,7 +514,7 @@
         0,
         1 << 19,
     )(projected[0], me, part, sources[0])
-    projected = projected[:1] + shift(projected[1:])
+    projected = projected[:1] + shift(projected[1:], SCORES)
     early = call(
         functools.partial(early_pick_kernel, groups),
         shape(parts * slots, classes, dtype=f32),

time: 38.1 us -> 38.7 us (1.016)
  local copies, waits for them, and re-layouts: 0.01 us -> 0.59 us
    unnamed x6, local copies, waits for them, and re-layouts: 0.01 us -> 0.59 us
  transfers between devices with their start and end apart: 17 -> 17, of which waited for: 8 -> 7; matrix products, arithmetic and copies ran while one was open for 0% -> 0% of each run, Pallas kernels for 16% -> 16%
where the time goes in v21:
time: 38.7 us; the launch traced here: 38.4 us
  starting transfers between devices  21.8 us (56%)
  Pallas kernels  8.89 us (23%)
  waiting for transfers between devices  6.38 us (16%)
  between operations  0.82 us (2%)
  local copies, waits for them, and re-layouts  0.59 us (2%)
    ppermute x9, starting transfers between devices, shift(): lax.ppermute(block, 'feat', [(i, ahead(i, groups, k, what)) for i in rang...  13.3 us
    pallas_call x16, Pallas kernels, placed(): run(*(pltpu.with_memory_space_constraint(value, pltpu.HBM) if spec is HB...  8.89 us
    ppermute x6, starting transfers between devices, to_chips(): lax.ppermute(blocks[j], 'dom', [(d, next_to(d // 2, j, chips) * 2 + d % 2...  7.84 us
    ppermute x9, waiting for transfers between devices, shift(): lax.ppermute(block, 'feat', [(i, ahead(i, groups, k, what)) for i in rang...  3.1 us
    ppermute x6, waiting for transfers between devices, to_chips(): lax.ppermute(blocks[j], 'dom', [(d, next_to(d // 2, j, chips) * 2 + d % 2...  2.08 us
    ppermute x2, waiting for transfers between devices, to_mate(): return lax.ppermute(value, 'dom', [(d, d ^ 1) for d in range(parts)])  1.2 us
  transfers between devices with their start and end apart: 17, of which 7 were waited for; matrix products, arithmetic and copies ran while one was open for 0% of the time, Pallas kernels for 16%

profile of v21, /device:TPU:0, one launch (start us, length us, event | category | flops | bytes accessed | tf_op | source)
XLA Modules:
  0.0 38.4 jit_solution(9027175249691769024)
XLA Ops:
  0.6 1.3 %shard_map.122 = (bf16[4,64,256]{2,1,0:T(8,128)(2,1)S(1)}, bf16[256,512]{1,0:T(8,128)(2,1)S(1)}, s32[8,4,16]{2,1,0:T(4,128)S(1)}, bf16[12,128,128]{2,1,0:T(8,128...) custom-call(s32[1]{0:T(128)} %bitcast.4.part_ref, ...), custom_call_target="tpu_custom_call" | custom-call | flops 100663296 | bytes 1048576 | tf_op jit(solution)/shard_map/pallas_call | solution.py:33
  1.9 0.5 %collective-permute-start = (bf16[4,64,256]{2,1,0:T(8,128)(2,1)S(1)}, bf16[4,64,256]{2,1,0:T(8,128)(2,1)S(1)}, u32[]{:S(2)}, u32[]{:S(2)}) collective-permute-start(bf16[4,64,256]{2,1,0:T(8,128)(2,1)S(1)} %get-tuple-element.49), channel_id=1, source_target_pairs={{0,1},{1,0},{2,3},{3,2},{4,5},{5,4},{6,7},{7,6},{8,9},{9,8},{10,11... | collective-permute-start | bytes 393224 | tf_op jit(solution)/shard_map/ppermute | solution.py:398
  2.5 1.2 %shard_map.123 = (f32[4,208,128]{2,1,0:T(8,128)S(1)}, bf16[4,8,16,128]{3,2,1,0:T(8,128)(2,1)S(1)}, bf16[128,512]{1,0:T(8,128)(2,1)S(1)}, bf16[4,64,256]{2,1,0:T(...) custom-call(s32[1]{0:T(128)} %bitcast.me_ref.rest_0_, ...), custom_call_target="tpu_custom_call" | custom-call | flops 100663296 | bytes 1048576 | tf_op jit(solution)/shard_map/pallas_call | solution.py:33
  3.6 0.0 collective-permute-done.got_ref
  3.7 3.7 %collective-permute-start.4 = (bf16[2,64,256]{2,1,0:T(8,128)(2,1)S(1)}, bf16[2,64,256]{2,1,0:T(8,128)(2,1)S(1)}, u32[]{:S(2)}, u32[]{:S(2)}) collective-permute-start(bf16[2,64,256]{2,1,0:T(8,128)(2,1)S(1)} %get-tuple-element.59), channel_id=1, source_target_pairs={{0,6},{1,7},{2,4},{3,5},{4,2},{5,3},{6,0},{7,1},{8,14},{9,15},{10,... | collective-permute-start | bytes 196616 | tf_op jit(solution)/shard_map/ppermute | solution.py:402
  7.4 0.5 %collective-permute-start.5 = (bf16[2,64,256]{2,1,0:T(8,128)(2,1)S(1)}, bf16[2,64,256]{2,1,0:T(8,128)(2,1)S(1)}, u32[]{:S(2)}, u32[]{:S(2)}) collective-permute-start(bf16[2,64,256]{2,1,0:T(8,128)(2,1)S(1)} %get-tuple-element.60), channel_id=1, source_target_pairs={{0,4},{1,5},{2,6},{3,7},{4,0},{5,1},{6,2},{7,3},{8,12},{9,13},{10,... | collective-permute-start | bytes 196616 | tf_op jit(solution)/shard_map/ppermute | solution.py:402
  7.9 0.1 collective-permute-start.6
  8.0 2.0 %collective-permute-start.1 = (bf16[192,128]{1,0:T(8,128)(2,1)S(1)}, bf16[192,128]{1,0:T(8,128)(2,1)S(1)}, u32[]{:S(2)}, u32[]{:S(2)}) collective-permute-start(bf16[192,128]{1,0:T(8,128)(2,1)S(1)} %get-tuple-element.53), channel_id=1, source_target_pairs={{0,8},{8,16},{16,24},{24,0},{1,9},{9,17},{17,25},{25,1},{2,10},{10... | collective-permute-start | bytes 147464 | tf_op jit(solution)/shard_map/ppermute | solution.py:393
  10.0 2.0 %collective-permute-start.2 = (bf16[192,128]{1,0:T(8,128)(2,1)S(1)}, bf16[192,128]{1,0:T(8,128)(2,1)S(1)}, u32[]{:S(2)}, u32[]{:S(2)}) collective-permute-start(bf16[192,128]{1,0:T(8,128)(2,1)S(1)} %get-tuple-element.54), channel_id=1, source_target_pairs={{0,24},{8,0},{16,8},{24,16},{1,25},{9,1},{17,9},{25,17},{2,26},{10... | collective-permute-start | bytes 147464 | tf_op jit(solution)/shard_map/ppermute | solution.py:393
  12.0 0.0 collective-permute-done.4.rest_4_.rest_1_
  12.0 1.0 %collective-permute-start.3 = (bf16[192,128]{1,0:T(8,128)(2,1)S(1)}, bf16[192,128]{1,0:T(8,128)(2,1)S(1)}, u32[]{:S(2)}, u32[]{:S(2)}) collective-permute-start(bf16[192,128]{1,0:T(8,128)(2,1)S(1)} %get-tuple-element.55), channel_id=1, source_target_pairs={{0,16},{8,24},{16,0},{24,8},{1,17},{9,25},{17,1},{25,9},{2,18},{10... | collective-permute-start | bytes 147464 | tf_op jit(solution)/shard_map/ppermute | solution.py:393
  13.0 0.0 collective-permute-done.5.rest_5_.rest_2_
  13.0 0.0 collective-permute-done.6.rest_6_.rest_3_
  13.0 0.2 shard_map.127
  13.3 2.8 %collective-permute-start.7 = (bf16[192,128]{1,0:T(8,128)(2,1)S(1)}, bf16[192,128]{1,0:T(8,128)(2,1)S(1)}, u32[]{:S(2)}, u32[]{:S(2)}) collective-permute-start(bf16[192,128]{1,0:T(8,128)(2,1)S(1)} %get-tuple-element.62), channel_id=1, source_target_pairs={{0,24},{8,16},{16,8},{24,0},{1,25},{9,17},{17,9},{25,1},{2,26},{10... | collective-permute-start | bytes 147464 | tf_op jit(solution)/shard_map/ppermute | solution.py:393
  16.0 0.3 collective-permute-start.8
  16.4 0.0 collective-permute-done.1.rest_0_
  16.4 1.4 %collective-permute-start.9 = (bf16[192,128]{1,0:T(8,128)(2,1)S(1)}, bf16[192,128]{1,0:T(8,128)(2,1)S(1)}, u32[]{:S(2)}, u32[]{:S(2)}) collective-permute-start(bf16[192,128]{1,0:T(8,128)(2,1)S(1)} %get-tuple-element.64), channel_id=1, source_target_pairs={{0,8},{8,0},{16,24},{24,16},{1,9},{9,1},{17,25},{25,17},{2,10},{10... | collective-permute-start | bytes 147464 | tf_op jit(solution)/shard_map/ppermute | solution.py:393
  17.7 0.0 collective-permute-done.2.rest_1_
  17.7 1.7 %collective-permute-done.3.rest_2_ = bf16[192,128]{1,0:T(8,128)(2,1)S(1)} collective-permute-done((bf16[192,128]{1,0:T(8,128)(2,1)S(1)}, bf16[192,128]{1,0:T(8,128)(2,1)S(1)}, u32[]{:S(2)}, u32[]{:S(2)}) %collective-permute-start.3) | collective-permute-done | bytes 49184 | tf_op jit(solution)/shard_map/ppermute | solution.py:393
  19.4 1.8 %shard_map.125.after.own_ref = f32[128,1024]{1,0:T(8,128)S(1)} custom-call(s32[1]{0:T(128)} %bitcast.me_ref.rest_0_, bf16[192,512]{1,0:T(8,128)(2,1)} %bitcast.22, bf16[768,1024]{1,0:T(8,128)(2,1)} %weight_hbm.1, bf16[192,128]{1,0:T(8,128)(2,1)S(1)} %collective-permute-done.1.rest_0_, bf16[192,128]{1,0:T(8,128)(2,1)S(1)} %collective-permute-done.2.rest_1_, ...), custom_call_target="tpu_custom_call" | custom-call | flops 201326592 | bytes 2097152 | tf_op jit(solution)/shard_map/pallas_call | solution.py:33
  21.2 0.2 shard_map.126.rest_0_
  21.4 0.0 collective-permute-done.7.rest_1_
  21.4 0.3 shard_map.128.early_ref
  21.8 0.0 collective-permute-done.9.rest_1_
  21.8 0.6 %copy-done.2 = bf16[1024,153]{0,1:T(8,128)(2,1)S(1)} copy-done((bf16[1024,153]{0,1:T(8,128)(2,1)S(1)}, bf16[1024,153]{0,1:T(8,128)(2,1)}, u32[]{:S(2)}) %copy-start.2) | copy-done | bytes 313368
  22.4 0.5 %shard_map.129 = (bf16[128,1024]{1,0:T(8,128)(2,1)S(1)}, bf16[153,128]{1,0:T(8,128)(2,1)S(1)}, bf16[153,128]{1,0:T(8,128)(2,1)S(1)}, bf16[153,128]{1,0:T(8,128)(2,1)S(1)}, bf16[153,128]{1,0:T(8,128)(2,1)S(1)}) custom-call(s32[1]{0:T(128)} %bitcast.me_ref.rest_0_, bf16[768,1024]{1,0:T(8,128)(2,1)S(1)} %copy-done, bf16[153,1024]{1,0:T(8,128)(2,1)S(1)} %bitcast.20, ...), custom_call_target="tpu_custom_call" | custom-call | flops 100663296 | bytes 2097152 | tf_op jit(solution)/shard_map/pallas_call | solution.py:33
  22.9 0.1 collective-permute-start.10
  23.0 2.3 %collective-permute-start.11 = (bf16[153,128]{1,0:T(8,128)(2,1)S(1)}, bf16[153,128]{1,0:T(8,128)(2,1)S(1)}, u32[]{:S(2)}, u32[]{:S(2)}) collective-permute-start(bf16[153,128]{1,0:T(8,128)(2,1)S(1)} %get-tuple-element.70), channel_id=1, source_target_pairs={{0,16},{8,24},{16,0},{24,8},{1,17},{9,25},{17,1},{25,9},{2,18},{10... | collective-permute-start | bytes 117512 | tf_op jit(solution)/shard_map/ppermute | solution.py:393
  25.3 1.5 %collective-permute-start.12 = (bf16[153,128]{1,0:T(8,128)(2,1)S(1)}, bf16[153,128]{1,0:T(8,128)(2,1)S(1)}, u32[]{:S(2)}, u32[]{:S(2)}) collective-permute-start(bf16[153,128]{1,0:T(8,128)(2,1)S(1)} %get-tuple-element.71), channel_id=1, source_target_pairs={{0,24},{8,0},{16,8},{24,16},{1,25},{9,1},{17,9},{25,17},{2,26},{10... | collective-permute-start | bytes 117512 | tf_op jit(solution)/shard_map/ppermute | solution.py:393
  26.8 0.9 %shard_map.132.hits_ref.after = bf16[128,512]{1,0:T(8,128)(2,1)S(1)} custom-call(bf16[153,128]{1,0:T(8,128)(2,1)S(1)} %get-tuple-element.68.rest_0_.after, s32[1]{0:T(128)} %bitcast.me_ref.rest_0_, s32[1]{0:T(128)} %bitcast.4.part_ref, s32[8,4,16]{2,1,0:T(4,128)} %bitcast.26), custom_call_target="tpu_custom_call" | custom-call | bytes 524288 | tf_op jit(solution)/shard_map/pallas_call | solution.py:33
  27.7 1.1 %collective-permute-done.10.rest_1_ = bf16[153,128]{1,0:T(8,128)(2,1)S(1)} collective-permute-done((bf16[153,128]{1,0:T(8,128)(2,1)S(1)}, bf16[153,128]{1,0:T(8,128)(2,1)S(1)}, u32[]{:S(2)}, u32[]{:S(2)}) %collective-permute-start.10) | collective-permute-done | bytes 39200 | tf_op jit(solution)/shard_map/ppermute | solution.py:393
  28.8 0.2 shard_map.133.early_ref
  29.0 0.0 collective-permute-done.11.rest_2_.rest_0_
  29.0 0.4 collective-permute-done.12.rest_3_.rest_1_
  29.4 0.2 shard_map.134
  29.6 0.1 collective-permute-start.13
  29.6 1.2 %collective-permute-done.13.got_ref = bf16[4,16,256]{2,1,0:T(8,128)(2,1)S(1)} collective-permute-done((bf16[4,16,256]{2,1,0:T(8,128)(2,1)S(1)}, bf16[4,16,256]{2,1,0:T(8,128)(2,1)S(1)}, u32[]{:S(2)}, u32[]{:S(2)}) %collective-permute-start.13) | collective-permute-done | bytes 32800 | tf_op jit(solution)/shard_map/ppermute | solution.py:398
  30.8 2.9 %collective-permute-start.14 = (bf16[2,16,256]{2,1,0:T(8,128)(2,1)S(1)}, bf16[2,16,256]{2,1,0:T(8,128)(2,1)S(1)}, u32[]{:S(2)}, u32[]{:S(2)}) collective-permute-start(bf16[2,16,256]{2,1,0:T(8,128)(2,1)S(1)} %get-tuple-element.75), channel_id=1, source_target_pairs={{0,6},{1,7},{2,4},{3,5},{4,2},{5,3},{6,0},{7,1},{8,14},{9,15},{10,... | collective-permute-start | bytes 49160 | tf_op jit(solution)/shard_map/ppermute | solution.py:402
  33.7 0.1 collective-permute-start.15
  33.9 0.5 %collective-permute-start.16 = (bf16[2,16,256]{2,1,0:T(8,128)(2,1)S(1)}, bf16[2,16,256]{2,1,0:T(8,128)(2,1)S(1)}, u32[]{:S(2)}, u32[]{:S(2)}) collective-permute-start(bf16[2,16,256]{2,1,0:T(8,128)(2,1)S(1)} %get-tuple-element.77), channel_id=1, source_target_pairs={{0,2},{1,3},{2,0},{3,1},{4,6},{5,7},{6,4},{7,5},{8,10},{9,11},{10,... | collective-permute-start | bytes 49160 | tf_op jit(solution)/shard_map/ppermute | solution.py:402
  34.4 0.7 %shard_map.130 = (f32[153,128]{1,0:T(8,128)S(1)}, bf16[128,1024]{1,0:T(8,128)(2,1)}) custom-call(bf16[128,1024]{1,0:T(8,128)(2,1)S(1)} %get-tuple-element.65.hidden_ref, bf16[153,1024]{1,0:T(8,128)(2,1)S(1)} %bitcast.19), custom_call_target="tpu_custom_call" | custom-call | flops 40108032 | bytes 1048576 | tf_op jit(solution)/shard_map/pallas_call | solution.py:33
  35.1 0.2 shard_map.131.near_ref
  35.3 0.1 collective-permute-done.14.rest_1_
  35.5 0.2 shard_map.136.rest_0_
  35.7 1.8 %collective-permute-done.15.rest_3_ = bf16[2,16,256]{2,1,0:T(8,128)(2,1)S(1)} collective-permute-done((bf16[2,16,256]{2,1,0:T(8,128)(2,1)S(1)}, bf16[2,16,256]{2,1,0:T(8,128)(2,1)S(1)}, u32[]{:S(2)}, u32[]{:S(2)}) %collective-permute-start.15) | collective-permute-done | bytes 16416 | tf_op jit(solution)/shard_map/ppermute | solution.py:402
  37.5 0.1 collective-permute-done.16.rest_4_
  37.6 0.8 %shard_map.137 = f32[153,1,128]{2,1,0:T(1,128)} custom-call(s32[1]{0:T(128)} %bitcast.me_ref.rest_0_, f32[153,128]{1,0:T(8,128)S(1)} %shard_map.136.rest_0_, bf16[4,8,16,128]{3,2,1,0:T(8,128)(2,1)S(1)} %get-tuple-element.57.rest_2_.edges_ref.rest_1_, f32[4,208,128]{2,1,0:T(8,128)S(1)} %get-tuple-element.56.rest_1_.sums_ref.rest_2_, ...), custom_call_target="tpu_custom_call" | custom-call | flops 2506752 | bytes 524288 | tf_op jit(solution)/shard_map/pallas_call | solution.py:33
  (8 shorter events, 0.0 us)
Async XLA Ops:
  1.9 1.7 %collective-permute-start = (bf16[4,64,256]{2,1,0:T(8,128)(2,1)S(1)}, bf16[4,64,256]{2,1,0:T(8,128)(2,1)S(1)}, u32[]{:S(2)}, u32[]{:S(2)}) collective-permute-start(bf16[4,64,256]{2,1,0:T(8,128)(2,1)S(1)} %get-tuple-element.49), channel_id=1, source_target_pairs={{0,1},{1,0},{2,3},{3,2},{4,5},{5,4},{6,7},{7,6},{8,9},{9,8},{10,11... | collective-permute-start | bytes 393224 | tf_op jit(solution)/shard_map/ppermute | solution.py:398
  3.7 8.3 %collective-permute-start.4 = (bf16[2,64,256]{2,1,0:T(8,128)(2,1)S(1)}, bf16[2,64,256]{2,1,0:T(8,128)(2,1)S(1)}, u32[]{:S(2)}, u32[]{:S(2)}) collective-permute-start(bf16[2,64,256]{2,1,0:T(8,128)(2,1)S(1)} %get-tuple-element.59), channel_id=1, source_target_pairs={{0,6},{1,7},{2,4},{3,5},{4,2},{5,3},{6,0},{7,1},{8,14},{9,15},{10,... | collective-permute-start | bytes 196616 | tf_op jit(solution)/shard_map/ppermute | solution.py:402
  7.4 5.7 %collective-permute-start.5 = (bf16[2,64,256]{2,1,0:T(8,128)(2,1)S(1)}, bf16[2,64,256]{2,1,0:T(8,128)(2,1)S(1)}, u32[]{:S(2)}, u32[]{:S(2)}) collective-permute-start(bf16[2,64,256]{2,1,0:T(8,128)(2,1)S(1)} %get-tuple-element.60), channel_id=1, source_target_pairs={{0,4},{1,5},{2,6},{3,7},{4,0},{5,1},{6,2},{7,3},{8,12},{9,13},{10,... | collective-permute-start | bytes 196616 | tf_op jit(solution)/shard_map/ppermute | solution.py:402
  7.9 5.2 %collective-permute-start.6 = (bf16[2,64,256]{2,1,0:T(8,128)(2,1)S(1)}, bf16[2,64,256]{2,1,0:T(8,128)(2,1)S(1)}, u32[]{:S(2)}, u32[]{:S(2)}) collective-permute-start(bf16[2,64,256]{2,1,0:T(8,128)(2,1)S(1)} %get-tuple-element.61), channel_id=1, source_target_pairs={{0,2},{1,3},{2,0},{3,1},{4,6},{5,7},{6,4},{7,5},{8,10},{9,11},{10,... | collective-permute-start | bytes 196616 | tf_op jit(solution)/shard_map/ppermute | solution.py:402
  8.0 8.4 %collective-permute-start.1 = (bf16[192,128]{1,0:T(8,128)(2,1)S(1)}, bf16[192,128]{1,0:T(8,128)(2,1)S(1)}, u32[]{:S(2)}, u32[]{:S(2)}) collective-permute-start(bf16[192,128]{1,0:T(8,128)(2,1)S(1)} %get-tuple-element.53), channel_id=1, source_target_pairs={{0,8},{8,16},{16,24},{24,0},{1,9},{9,17},{17,25},{25,1},{2,10},{10... | collective-permute-start | bytes 147464 | tf_op jit(solution)/shard_map/ppermute | solution.py:393
  10.0 7.8 %collective-permute-start.2 = (bf16[192,128]{1,0:T(8,128)(2,1)S(1)}, bf16[192,128]{1,0:T(8,128)(2,1)S(1)}, u32[]{:S(2)}, u32[]{:S(2)}) collective-permute-start(bf16[192,128]{1,0:T(8,128)(2,1)S(1)} %get-tuple-element.54), channel_id=1, source_target_pairs={{0,24},{8,0},{16,8},{24,16},{1,25},{9,1},{17,9},{25,17},{2,26},{10... | collective-permute-start | bytes 147464 | tf_op jit(solution)/shard_map/ppermute | solution.py:393
  12.0 7.4 %collective-permute-start.3 = (bf16[192,128]{1,0:T(8,128)(2,1)S(1)}, bf16[192,128]{1,0:T(8,128)(2,1)S(1)}, u32[]{:S(2)}, u32[]{:S(2)}) collective-permute-start(bf16[192,128]{1,0:T(8,128)(2,1)S(1)} %get-tuple-element.55), channel_id=1, source_target_pairs={{0,16},{8,24},{16,0},{24,8},{1,17},{9,25},{17,1},{25,9},{2,18},{10... | collective-permute-start | bytes 147464 | tf_op jit(solution)/shard_map/ppermute | solution.py:393
  13.3 8.2 %collective-permute-start.7 = (bf16[192,128]{1,0:T(8,128)(2,1)S(1)}, bf16[192,128]{1,0:T(8,128)(2,1)S(1)}, u32[]{:S(2)}, u32[]{:S(2)}) collective-permute-start(bf16[192,128]{1,0:T(8,128)(2,1)S(1)} %get-tuple-element.62), channel_id=1, source_target_pairs={{0,24},{8,16},{16,8},{24,0},{1,25},{9,17},{17,9},{25,1},{2,26},{10... | collective-permute-start | bytes 147464 | tf_op jit(solution)/shard_map/ppermute | solution.py:393
  16.0 5.8 %collective-permute-start.8 = (bf16[192,128]{1,0:T(8,128)(2,1)S(1)}, bf16[192,128]{1,0:T(8,128)(2,1)S(1)}, u32[]{:S(2)}, u32[]{:S(2)}) collective-permute-start(bf16[192,128]{1,0:T(8,128)(2,1)S(1)} %get-tuple-element.63), channel_id=1, source_target_pairs={{0,16},{8,24},{16,0},{24,8},{1,17},{9,25},{17,1},{25,9},{2,18},{10... | collective-permute-start | bytes 147464 | tf_op jit(solution)/shard_map/ppermute | solution.py:393
  16.4 5.1 %copy-start = (bf16[768,1024]{1,0:T(8,128)(2,1)S(1)}, bf16[768,1024]{1,0:T(8,128)(2,1)}, u32[]{:S(2)}) copy-start(bf16[768,1024]{1,0:T(8,128)(2,1)} %weight_ref.3) | copy-start | bytes 4718596
  16.4 5.4 %collective-permute-start.9 = (bf16[192,128]{1,0:T(8,128)(2,1)S(1)}, bf16[192,128]{1,0:T(8,128)(2,1)S(1)}, u32[]{:S(2)}, u32[]{:S(2)}) collective-permute-start(bf16[192,128]{1,0:T(8,128)(2,1)S(1)} %get-tuple-element.64), channel_id=1, source_target_pairs={{0,8},{8,0},{16,24},{24,16},{1,9},{9,1},{17,25},{25,17},{2,10},{10... | collective-permute-start | bytes 147464 | tf_op jit(solution)/shard_map/ppermute | solution.py:393
  21.4 1.0 %copy-start.2 = (bf16[1024,153]{0,1:T(8,128)(2,1)S(1)}, bf16[1024,153]{0,1:T(8,128)(2,1)}, u32[]{:S(2)}) copy-start(bf16[1024,153]{0,1:T(8,128)(2,1)} %param.21) | copy-start | bytes 940036
  22.4 12.0 %copy-start.1 = (bf16[1024,153]{0,1:T(8,128)(2,1)S(1)}, bf16[1024,153]{0,1:T(8,128)(2,1)}, u32[]{:S(2)}) copy-start(bf16[1024,153]{0,1:T(8,128)(2,1)} %param.20) | copy-start | bytes 940036
  22.9 5.9 %collective-permute-start.10 = (bf16[153,128]{1,0:T(8,128)(2,1)S(1)}, bf16[153,128]{1,0:T(8,128)(2,1)S(1)}, u32[]{:S(2)}, u32[]{:S(2)}) collective-permute-start(bf16[153,128]{1,0:T(8,128)(2,1)S(1)} %get-tuple-element.69), channel_id=1, source_target_pairs={{0,8},{8,16},{16,24},{24,0},{1,9},{9,17},{17,25},{25,1},{2,10},{10... | collective-permute-start | bytes 117512 | tf_op jit(solution)/shard_map/ppermute | solution.py:393
  23.0 6.0 %collective-permute-start.11 = (bf16[153,128]{1,0:T(8,128)(2,1)S(1)}, bf16[153,128]{1,0:T(8,128)(2,1)S(1)}, u32[]{:S(2)}, u32[]{:S(2)}) collective-permute-start(bf16[153,128]{1,0:T(8,128)(2,1)S(1)} %get-tuple-element.70), channel_id=1, source_target_pairs={{0,16},{8,24},{16,0},{24,8},{1,17},{9,25},{17,1},{25,9},{2,18},{10... | collective-permute-start | bytes 117512 | tf_op jit(solution)/shard_map/ppermute | solution.py:393
  25.3 4.0 %collective-permute-start.12 = (bf16[153,128]{1,0:T(8,128)(2,1)S(1)}, bf16[153,128]{1,0:T(8,128)(2,1)S(1)}, u32[]{:S(2)}, u32[]{:S(2)}) collective-permute-start(bf16[153,128]{1,0:T(8,128)(2,1)S(1)} %get-tuple-element.71), channel_id=1, source_target_pairs={{0,24},{8,0},{16,8},{24,16},{1,25},{9,1},{17,9},{25,17},{2,26},{10... | collective-permute-start | bytes 117512 | tf_op jit(solution)/shard_map/ppermute | solution.py:393
  29.6 1.3 %collective-permute-start.13 = (bf16[4,16,256]{2,1,0:T(8,128)(2,1)S(1)}, bf16[4,16,256]{2,1,0:T(8,128)(2,1)S(1)}, u32[]{:S(2)}, u32[]{:S(2)}) collective-permute-start(bf16[4,16,256]{2,1,0:T(8,128)(2,1)S(1)} %get-tuple-element.73), channel_id=1, source_target_pairs={{0,1},{1,0},{2,3},{3,2},{4,5},{5,4},{6,7},{7,6},{8,9},{9,8},{10,11... | collective-permute-start | bytes 98312 | tf_op jit(solution)/shard_map/ppermute | solution.py:398
  30.8 4.6 %collective-permute-start.14 = (bf16[2,16,256]{2,1,0:T(8,128)(2,1)S(1)}, bf16[2,16,256]{2,1,0:T(8,128)(2,1)S(1)}, u32[]{:S(2)}, u32[]{:S(2)}) collective-permute-start(bf16[2,16,256]{2,1,0:T(8,128)(2,1)S(1)} %get-tuple-element.75), channel_id=1, source_target_pairs={{0,6},{1,7},{2,4},{3,5},{4,2},{5,3},{6,0},{7,1},{8,14},{9,15},{10,... | collective-permute-start | bytes 49160 | tf_op jit(solution)/shard_map/ppermute | solution.py:402
  33.7 3.7 %collective-permute-start.15 = (bf16[2,16,256]{2,1,0:T(8,128)(2,1)S(1)}, bf16[2,16,256]{2,1,0:T(8,128)(2,1)S(1)}, u32[]{:S(2)}, u32[]{:S(2)}) collective-permute-start(bf16[2,16,256]{2,1,0:T(8,128)(2,1)S(1)} %get-tuple-element.76), channel_id=1, source_target_pairs={{0,4},{1,5},{2,6},{3,7},{4,0},{5,1},{6,2},{7,3},{8,12},{9,13},{10,... | collective-permute-start | bytes 49160 | tf_op jit(solution)/shard_map/ppermute | solution.py:402
  33.9 3.7 %collective-permute-start.16 = (bf16[2,16,256]{2,1,0:T(8,128)(2,1)S(1)}, bf16[2,16,256]{2,1,0:T(8,128)(2,1)S(1)}, u32[]{:S(2)}, u32[]{:S(2)}) collective-permute-start(bf16[2,16,256]{2,1,0:T(8,128)(2,1)S(1)} %get-tuple-element.77), channel_id=1, source_target_pairs={{0,2},{1,3},{2,0},{3,1},{4,6},{5,7},{6,4},{7,5},{8,10},{9,11},{10,... | collective-permute-start | bytes 49160 | tf_op jit(solution)/shard_map/ppermute | solution.py:402

commit v22 on v19

--- a/solution.py
+++ b/solution.py
@@ -264,14 +264,14 @@
     return total
 
 
-def early_kernel(groups, me_ref, weight_ref, own_ref, *rest):
+def early_kernel(groups, first, me_ref, weight_ref, own_ref, *rest):
     blocks, out_ref = rest[:-1], rest[-1]
-    out_ref[...] = add_blocks(own_ref[...], me_ref[0], groups, 0, blocks, weight_ref)
+    out_ref[...] = add_blocks(own_ref[...], me_ref[0], groups, first, blocks, weight_ref)
 
 
 def hidden_kernel(groups, me_ref, weight_ref, out_weight_ref, early_ref, *rest):
-    blocks, (hidden_ref, *copies) = rest[: groups - 2], rest[groups - 2 :]
-    total = add_blocks(early_ref[...], me_ref[0], groups, 2, blocks, weight_ref)
+    last_ref, hidden_ref, *copies = rest
+    total = add_blocks(early_ref[...], me_ref[0], groups, groups - 1, [last_ref], weight_ref)
     hidden = jnp.maximum(total, 0.0).astype(bf16)
     hidden_ref[...] = hidden
     projected = dot(out_weight_ref[...], hidden, LAST).astype(bf16)
@@ -300,9 +300,13 @@
     rest[-1][...] = pick_blocks(groups, 0, me_ref, hits_ref, rest[:-1])
 
 
+def more_pick_kernel(groups, me_ref, hits_ref, early_ref, *rest):
+    rest[-1][...] = early_ref[...] + pick_blocks(groups, 2, me_ref, hits_ref, rest[:-1])
+
+
 def pick_kernel(groups, me_ref, hits_ref, early_ref, *rest):
-    projected, (mine_ref, mate_ref) = rest[:-2], rest[-2:]
-    total = early_ref[...] + pick_blocks(groups, 2, me_ref, hits_ref, projected)
+    last_ref, mine_ref, mate_ref = rest
+    total = early_ref[...] + pick_blocks(groups, groups - 1, me_ref, hits_ref, [last_ref])
     gap = mine_ref.shape[2] - total.shape[1]
     total = jnp.concatenate([total, jnp.zeros((total.shape[0], gap), f32)], axis=1).astype(bf16)
     half = total.shape[0] // 2
@@ -480,22 +484,24 @@
         1 << 18,
     )(own, me, sums, edges, *arrived)
     means = [*own_mean, *means]
-    early = call(
-        functools.partial(early_kernel, groups),
-        shape(rows, hid, dtype=f32),
-        [SM] + [VM] * 4,
-        (),
-        rows * hid * groups * width,
-        2 << 20,
-    )(me, neigh_one, own, *means[:2])
+    early = own
+    for first, last in ((0, 2), (2, groups - 1)):
+        early = call(
+            functools.partial(early_kernel, groups, first),
+            shape(rows, hid, dtype=f32),
+            [SM] + [VM] * (2 + last - first),
+            (),
+            rows * hid * groups * width,
+            2 << 20,
+        )(me, neigh_one, early, *means[first:last])
     hidden, *projected = call(
         functools.partial(hidden_kernel, groups),
         (shape(rows, hid),) + (shape(classes, rows),) * groups,
-        [SM] + [VM] * (1 + groups),
+        [SM] + [VM] * 4,
         (),
         rows * hid * groups * width,
         2 << 20,
-    )(me, neigh_one, neigh_out.T, early, *means[2:])
+    )(me, neigh_one, neigh_out.T, early, means[-1])
     hits = call(
         hits_kernel,
         shape(parts * slots, nodes),
@@ -513,14 +519,22 @@
         parts * slots * nodes * classes,
         1 << 18,
     )(me, hits, *projected[:2])
+    early = call(
+        functools.partial(more_pick_kernel, groups),
+        shape(parts * slots, classes, dtype=f32),
+        [SM] + [VM] * (groups - 1),
+        (),
+        parts * slots * nodes * classes,
+        1 << 18,
+    )(me, hits, early, *projected[2:-1])
     mine, mate = call(
         functools.partial(pick_kernel, groups),
         (shape(chips, slots, whole_lanes(classes)),) * 2,
-        [SM] + [VM] * groups,
+        [SM] + [VM] * 3,
         (),
         parts * slots * nodes * classes,
         1 << 18,
-    )(me, hits, early, *projected[2:])
+    )(me, hits, early, projected[-1])
     mate = to_mate(mate)
     arrived = to_chips(
         call(pair_kernel, (shape(2, slots, whole_lanes(classes)),) * chips, [VM] * 3, (), 0, 1 << 19)(

time: 38.1 us -> 38.5 us (1.010)
    pallas_call x16 -> x18, Pallas kernels: 8.87 us -> 9.18 us  [placed(): run(*(pltpu.with_memory_space_constraint(value, pltpu.HBM) if spec is HB...]
  transfers between devices with their start and end apart: 17 -> 17, of which waited for: 8 -> 8; matrix products, arithmetic and copies ran while one was open for 0% -> 0% of each run, Pallas kernels for 16% -> 17%
where the time goes in v22:
time: 38.5 us; the launch traced here: 38.3 us
  starting transfers between devices  21.9 us (57%)
  Pallas kernels  9.18 us (24%)
  waiting for transfers between devices  6.37 us (17%)
  between operations  0.82 us (2%)
    ppermute x9, starting transfers between devices, shift(): lax.ppermute(block, 'feat', [(i, ahead(i, groups, k, near)) for i in rang...  13.5 us
    pallas_call x18, Pallas kernels, placed(): run(*(pltpu.with_memory_space_constraint(value, pltpu.HBM) if spec is HB...  9.18 us
    ppermute x6, starting transfers between devices, to_chips(): lax.ppermute(blocks[j], 'dom', [(d, next_to(d // 2, j, chips) * 2 + d % 2...  7.8 us
    ppermute x9, waiting for transfers between devices, shift(): lax.ppermute(block, 'feat', [(i, ahead(i, groups, k, near)) for i in rang...  3.22 us
    ppermute x6, waiting for transfers between devices, to_chips(): lax.ppermute(blocks[j], 'dom', [(d, next_to(d // 2, j, chips) * 2 + d % 2...  1.95 us
    ppermute x2, waiting for transfers between devices, to_mate(): return lax.ppermute(value, 'dom', [(d, d ^ 1) for d in range(parts)])  1.2 us
  transfers between devices with their start and end apart: 17, of which 8 were waited for; matrix products, arithmetic and copies ran while one was open for 0% of the time, Pallas kernels for 17%

profile of v22, /device:TPU:0, one launch (start us, length us, event | category | flops | bytes accessed | tf_op | source)
XLA Modules:
  0.0 38.3 jit_solution(2600908405671168755)
XLA Ops:
  0.6 1.3 %shard_map.122 = (bf16[4,64,256]{2,1,0:T(8,128)(2,1)S(1)}, bf16[256,512]{1,0:T(8,128)(2,1)S(1)}, s32[8,4,16]{2,1,0:T(4,128)S(1)}, bf16[12,128,128]{2,1,0:T(8,128...) custom-call(s32[1]{0:T(128)} %bitcast.4.part_ref, ...), custom_call_target="tpu_custom_call" | custom-call | flops 100663296 | bytes 1048576 | tf_op jit(solution)/shard_map/pallas_call | solution.py:33
  1.9 0.5 %collective-permute-start = (bf16[4,64,256]{2,1,0:T(8,128)(2,1)S(1)}, bf16[4,64,256]{2,1,0:T(8,128)(2,1)S(1)}, u32[]{:S(2)}, u32[]{:S(2)}) collective-permute-start(bf16[4,64,256]{2,1,0:T(8,128)(2,1)S(1)} %get-tuple-element.49), channel_id=1, source_target_pairs={{0,1},{1,0},{2,3},{3,2},{4,5},{5,4},{6,7},{7,6},{8,9},{9,8},{10,11... | collective-permute-start | bytes 393224 | tf_op jit(solution)/shard_map/ppermute | solution.py:392
  2.5 1.2 %shard_map.123 = (f32[4,208,128]{2,1,0:T(8,128)S(1)}, bf16[4,8,16,128]{3,2,1,0:T(8,128)(2,1)S(1)}, bf16[128,512]{1,0:T(8,128)(2,1)S(1)}, bf16[4,64,256]{2,1,0:T(...) custom-call(s32[1]{0:T(128)} %bitcast.me_ref.rest_0_, ...), custom_call_target="tpu_custom_call" | custom-call | flops 100663296 | bytes 1048576 | tf_op jit(solution)/shard_map/pallas_call | solution.py:33
  3.7 3.7 %collective-permute-start.4 = (bf16[2,64,256]{2,1,0:T(8,128)(2,1)S(1)}, bf16[2,64,256]{2,1,0:T(8,128)(2,1)S(1)}, u32[]{:S(2)}, u32[]{:S(2)}) collective-permute-start(bf16[2,64,256]{2,1,0:T(8,128)(2,1)S(1)} %get-tuple-element.59), channel_id=1, source_target_pairs={{0,6},{1,7},{2,4},{3,5},{4,2},{5,3},{6,0},{7,1},{8,14},{9,15},{10,... | collective-permute-start | bytes 196616 | tf_op jit(solution)/shard_map/ppermute | solution.py:396
  7.4 0.5 %collective-permute-start.5 = (bf16[2,64,256]{2,1,0:T(8,128)(2,1)S(1)}, bf16[2,64,256]{2,1,0:T(8,128)(2,1)S(1)}, u32[]{:S(2)}, u32[]{:S(2)}) collective-permute-start(bf16[2,64,256]{2,1,0:T(8,128)(2,1)S(1)} %get-tuple-element.60), channel_id=1, source_target_pairs={{0,4},{1,5},{2,6},{3,7},{4,0},{5,1},{6,2},{7,3},{8,12},{9,13},{10,... | collective-permute-start | bytes 196616 | tf_op jit(solution)/shard_map/ppermute | solution.py:396
  7.9 0.1 collective-permute-start.6
  8.0 3.0 %collective-permute-start.1 = (bf16[192,128]{1,0:T(8,128)(2,1)S(1)}, bf16[192,128]{1,0:T(8,128)(2,1)S(1)}, u32[]{:S(2)}, u32[]{:S(2)}) collective-permute-start(bf16[192,128]{1,0:T(8,128)(2,1)S(1)} %get-tuple-element.53), channel_id=1, source_target_pairs={{0,16},{8,24},{16,0},{24,8},{1,17},{9,25},{17,1},{25,9},{2,18},{10... | collective-permute-start | bytes 147464 | tf_op jit(solution)/shard_map/ppermute | solution.py:387
  11.0 1.3 %collective-permute-start.2 = (bf16[192,128]{1,0:T(8,128)(2,1)S(1)}, bf16[192,128]{1,0:T(8,128)(2,1)S(1)}, u32[]{:S(2)}, u32[]{:S(2)}) collective-permute-start(bf16[192,128]{1,0:T(8,128)(2,1)S(1)} %get-tuple-element.54), channel_id=1, source_target_pairs={{0,24},{8,16},{16,8},{24,0},{1,25},{9,17},{17,9},{25,1},{2,26},{10... | collective-permute-start | bytes 147464 | tf_op jit(solution)/shard_map/ppermute | solution.py:387
  12.3 0.0 collective-permute-done.4.rest_4_.rest_1_
  12.3 0.2 collective-permute-start.3
  12.6 0.0 collective-permute-done.5.rest_5_.rest_2_
  12.6 0.0 collective-permute-done.6.rest_6_.rest_3_
  12.6 0.2 shard_map.127
  12.8 3.2 %collective-permute-start.7 = (bf16[192,128]{1,0:T(8,128)(2,1)S(1)}, bf16[192,128]{1,0:T(8,128)(2,1)S(1)}, u32[]{:S(2)}, u32[]{:S(2)}) collective-permute-start(bf16[192,128]{1,0:T(8,128)(2,1)S(1)} %get-tuple-element.62), channel_id=1, source_target_pairs={{0,24},{8,16},{16,8},{24,0},{1,25},{9,17},{17,9},{25,1},{2,26},{10... | collective-permute-start | bytes 147464 | tf_op jit(solution)/shard_map/ppermute | solution.py:387
  16.0 0.1 collective-permute-start.8
  16.1 0.0 collective-permute-done.1.rest_0_
  16.1 1.1 %collective-permute-start.9 = (bf16[192,128]{1,0:T(8,128)(2,1)S(1)}, bf16[192,128]{1,0:T(8,128)(2,1)S(1)}, u32[]{:S(2)}, u32[]{:S(2)}) collective-permute-start(bf16[192,128]{1,0:T(8,128)(2,1)S(1)} %get-tuple-element.64), channel_id=1, source_target_pairs={{0,8},{8,0},{16,24},{24,16},{1,9},{9,1},{17,25},{25,17},{2,10},{10... | collective-permute-start | bytes 147464 | tf_op jit(solution)/shard_map/ppermute | solution.py:387
  17.3 0.2 collective-permute-done.2.rest_1_
  17.4 0.0 collective-permute-done.3.rest_2_
  17.5 1.8 %shard_map.125.after.own_ref = f32[128,1024]{1,0:T(8,128)S(1)} custom-call(s32[1]{0:T(128)} %bitcast.me_ref.rest_0_, bf16[192,512]{1,0:T(8,128)(2,1)} %bitcast.22, bf16[768,1024]{1,0:T(8,128)(2,1)} %weight_hbm.1, bf16[192,128]{1,0:T(8,128)(2,1)S(1)} %collective-permute-done.1.rest_0_, bf16[192,128]{1,0:T(8,128)(2,1)S(1)} %collective-permute-done.2.rest_1_, ...), custom_call_target="tpu_custom_call" | custom-call | flops 201326592 | bytes 2097152 | tf_op jit(solution)/shard_map/pallas_call | solution.py:33
  19.3 0.2 shard_map.126.rest_0_
  19.5 0.0 collective-permute-done.7.rest_1_
  19.5 0.3 shard_map.128.own_ref
  19.8 0.0 copy-start.2
  19.8 1.4 %collective-permute-done.8.rest_0_ = bf16[192,128]{1,0:T(8,128)(2,1)S(1)} collective-permute-done((bf16[192,128]{1,0:T(8,128)(2,1)S(1)}, bf16[192,128]{1,0:T(8,128)(2,1)S(1)}, u32[]{:S(2)}, u32[]{:S(2)}) %collective-permute-start.8) | collective-permute-done | bytes 49184 | tf_op jit(solution)/shard_map/ppermute | solution.py:387
  21.2 0.2 shard_map.129.early_ref
  21.5 0.0 copy-start.1
  21.5 0.5 %shard_map.130 = (bf16[128,1024]{1,0:T(8,128)(2,1)S(1)}, bf16[153,128]{1,0:T(8,128)(2,1)S(1)}, bf16[153,128]{1,0:T(8,128)(2,1)S(1)}, bf16[153,128]{1,0:T(8,128)(2,1)S(1)}, bf16[153,128]{1,0:T(8,128)(2,1)S(1)}) custom-call(s32[1]{0:T(128)} %bitcast.me_ref.rest_0_, bf16[768,1024]{1,0:T(8,128)(2,1)S(1)} %copy-done, bf16[153,1024]{1,0:T(8,128)(2,1)S(1)} %bitcast.20, ...), custom_call_target="tpu_custom_call" | custom-call | flops 100663296 | bytes 2097152 | tf_op jit(solution)/shard_map/pallas_call | solution.py:33
  22.0 2.3 %collective-permute-start.10 = (bf16[153,128]{1,0:T(8,128)(2,1)S(1)}, bf16[153,128]{1,0:T(8,128)(2,1)S(1)}, u32[]{:S(2)}, u32[]{:S(2)}) collective-permute-start(bf16[153,128]{1,0:T(8,128)(2,1)S(1)} %get-tuple-element.69), channel_id=1, source_target_pairs={{0,24},{8,16},{16,8},{24,0},{1,25},{9,17},{17,9},{25,1},{2,26},{10... | collective-permute-start | bytes 117512 | tf_op jit(solution)/shard_map/ppermute | solution.py:387
  24.3 2.1 %collective-permute-start.12 = (bf16[153,128]{1,0:T(8,128)(2,1)S(1)}, bf16[153,128]{1,0:T(8,128)(2,1)S(1)}, u32[]{:S(2)}, u32[]{:S(2)}) collective-permute-start(bf16[153,128]{1,0:T(8,128)(2,1)S(1)} %get-tuple-element.71), channel_id=1, source_target_pairs={{0,8},{8,0},{16,24},{24,16},{1,9},{9,1},{17,25},{25,17},{2,10},{10... | collective-permute-start | bytes 117512 | tf_op jit(solution)/shard_map/ppermute | solution.py:387
  26.4 0.9 %shard_map.133.hits_ref.after = bf16[128,512]{1,0:T(8,128)(2,1)S(1)} custom-call(bf16[153,128]{1,0:T(8,128)(2,1)S(1)} %get-tuple-element.68.rest_0_.after, s32[1]{0:T(128)} %bitcast.me_ref.rest_0_, s32[1]{0:T(128)} %bitcast.4.part_ref, s32[8,4,16]{2,1,0:T(4,128)} %bitcast.26), custom_call_target="tpu_custom_call" | custom-call | bytes 524288 | tf_op jit(solution)/shard_map/pallas_call | solution.py:33
  27.3 0.7 %collective-permute-done.10.rest_1_ = bf16[153,128]{1,0:T(8,128)(2,1)S(1)} collective-permute-done((bf16[153,128]{1,0:T(8,128)(2,1)S(1)}, bf16[153,128]{1,0:T(8,128)(2,1)S(1)}, u32[]{:S(2)}, u32[]{:S(2)}) %collective-permute-start.10) | collective-permute-done | bytes 39200 | tf_op jit(solution)/shard_map/ppermute | solution.py:387
  28.0 0.2 shard_map.134.early_ref
  28.2 1.0 %collective-permute-done.11.rest_2_.rest_0_ = bf16[153,128]{1,0:T(8,128)(2,1)S(1)} collective-permute-done((bf16[153,128]{1,0:T(8,128)(2,1)S(1)}, bf16[153,128]{1,0:T(8,128)(2,1)S(1)}, u32[]{:S(2)}, u32[]{:S(2)}) %collective-permute-start.11) | collective-permute-done | bytes 39200 | tf_op jit(solution)/shard_map/ppermute | solution.py:387
  29.2 0.2 shard_map.135.early_ref
  29.4 0.2 shard_map.136
  29.6 0.1 collective-permute-start.13
  29.6 1.2 %collective-permute-done.13.got_ref = bf16[4,16,256]{2,1,0:T(8,128)(2,1)S(1)} collective-permute-done((bf16[4,16,256]{2,1,0:T(8,128)(2,1)S(1)}, bf16[4,16,256]{2,1,0:T(8,128)(2,1)S(1)}, u32[]{:S(2)}, u32[]{:S(2)}) %collective-permute-start.13) | collective-permute-done | bytes 32800 | tf_op jit(solution)/shard_map/ppermute | solution.py:392
  30.8 2.4 %collective-permute-start.14 = (bf16[2,16,256]{2,1,0:T(8,128)(2,1)S(1)}, bf16[2,16,256]{2,1,0:T(8,128)(2,1)S(1)}, u32[]{:S(2)}, u32[]{:S(2)}) collective-permute-start(bf16[2,16,256]{2,1,0:T(8,128)(2,1)S(1)} %get-tuple-element.75), channel_id=1, source_target_pairs={{0,6},{1,7},{2,4},{3,5},{4,2},{5,3},{6,0},{7,1},{8,14},{9,15},{10,... | collective-permute-start | bytes 49160 | tf_op jit(solution)/shard_map/ppermute | solution.py:396
  33.2 0.4 %collective-permute-start.15 = (bf16[2,16,256]{2,1,0:T(8,128)(2,1)S(1)}, bf16[2,16,256]{2,1,0:T(8,128)(2,1)S(1)}, u32[]{:S(2)}, u32[]{:S(2)}) collective-permute-start(bf16[2,16,256]{2,1,0:T(8,128)(2,1)S(1)} %get-tuple-element.76), channel_id=1, source_target_pairs={{0,4},{1,5},{2,6},{3,7},{4,0},{5,1},{6,2},{7,3},{8,12},{9,13},{10,... | collective-permute-start | bytes 49160 | tf_op jit(solution)/shard_map/ppermute | solution.py:396
  33.7 0.6 %collective-permute-start.16 = (bf16[2,16,256]{2,1,0:T(8,128)(2,1)S(1)}, bf16[2,16,256]{2,1,0:T(8,128)(2,1)S(1)}, u32[]{:S(2)}, u32[]{:S(2)}) collective-permute-start(bf16[2,16,256]{2,1,0:T(8,128)(2,1)S(1)} %get-tuple-element.77), channel_id=1, source_target_pairs={{0,2},{1,3},{2,0},{3,1},{4,6},{5,7},{6,4},{7,5},{8,10},{9,11},{10,... | collective-permute-start | bytes 49160 | tf_op jit(solution)/shard_map/ppermute | solution.py:396
  34.3 0.7 %shard_map.131 = (f32[153,128]{1,0:T(8,128)S(1)}, bf16[128,1024]{1,0:T(8,128)(2,1)}) custom-call(bf16[128,1024]{1,0:T(8,128)(2,1)S(1)} %get-tuple-element.65.hidden_ref, bf16[153,1024]{1,0:T(8,128)(2,1)S(1)} %bitcast.19), custom_call_target="tpu_custom_call" | custom-call | flops 40108032 | bytes 1048576 | tf_op jit(solution)/shard_map/pallas_call | solution.py:33
  35.0 0.2 shard_map.132.near_ref
  35.3 0.2 collective-permute-done.14.rest_1_
  35.5 0.2 shard_map.138.rest_0_
  35.7 1.3 %collective-permute-done.15.rest_3_ = bf16[2,16,256]{2,1,0:T(8,128)(2,1)S(1)} collective-permute-done((bf16[2,16,256]{2,1,0:T(8,128)(2,1)S(1)}, bf16[2,16,256]{2,1,0:T(8,128)(2,1)S(1)}, u32[]{:S(2)}, u32[]{:S(2)}) %collective-permute-start.15) | collective-permute-done | bytes 16416 | tf_op jit(solution)/shard_map/ppermute | solution.py:396
  37.0 0.4 %collective-permute-done.16.rest_4_ = bf16[2,16,256]{2,1,0:T(8,128)(2,1)S(1)} collective-permute-done((bf16[2,16,256]{2,1,0:T(8,128)(2,1)S(1)}, bf16[2,16,256]{2,1,0:T(8,128)(2,1)S(1)}, u32[]{:S(2)}, u32[]{:S(2)}) %collective-permute-start.16) | collective-permute-done | bytes 16416 | tf_op jit(solution)/shard_map/ppermute | solution.py:396
  37.4 0.8 %shard_map.139 = f32[153,1,128]{2,1,0:T(1,128)} custom-call(s32[1]{0:T(128)} %bitcast.me_ref.rest_0_, f32[153,128]{1,0:T(8,128)S(1)} %shard_map.138.rest_0_, bf16[4,8,16,128]{3,2,1,0:T(8,128)(2,1)S(1)} %get-tuple-element.57.rest_2_.edges_ref.rest_1_, f32[4,208,128]{2,1,0:T(8,128)S(1)} %get-tuple-element.56.rest_1_.sums_ref.rest_2_, ...), custom_call_target="tpu_custom_call" | custom-call | flops 2506752 | bytes 524288 | tf_op jit(solution)/shard_map/pallas_call | solution.py:33
  (10 shorter events, 0.1 us)
Async XLA Ops:
  1.9 1.7 %collective-permute-start = (bf16[4,64,256]{2,1,0:T(8,128)(2,1)S(1)}, bf16[4,64,256]{2,1,0:T(8,128)(2,1)S(1)}, u32[]{:S(2)}, u32[]{:S(2)}) collective-permute-start(bf16[4,64,256]{2,1,0:T(8,128)(2,1)S(1)} %get-tuple-element.49), channel_id=1, source_target_pairs={{0,1},{1,0},{2,3},{3,2},{4,5},{5,4},{6,7},{7,6},{8,9},{9,8},{10,11... | collective-permute-start | bytes 393224 | tf_op jit(solution)/shard_map/ppermute | solution.py:392
  3.7 8.7 %collective-permute-start.4 = (bf16[2,64,256]{2,1,0:T(8,128)(2,1)S(1)}, bf16[2,64,256]{2,1,0:T(8,128)(2,1)S(1)}, u32[]{:S(2)}, u32[]{:S(2)}) collective-permute-start(bf16[2,64,256]{2,1,0:T(8,128)(2,1)S(1)} %get-tuple-element.59), channel_id=1, source_target_pairs={{0,6},{1,7},{2,4},{3,5},{4,2},{5,3},{6,0},{7,1},{8,14},{9,15},{10,... | collective-permute-start | bytes 196616 | tf_op jit(solution)/shard_map/ppermute | solution.py:396
  7.4 5.2 %collective-permute-start.5 = (bf16[2,64,256]{2,1,0:T(8,128)(2,1)S(1)}, bf16[2,64,256]{2,1,0:T(8,128)(2,1)S(1)}, u32[]{:S(2)}, u32[]{:S(2)}) collective-permute-start(bf16[2,64,256]{2,1,0:T(8,128)(2,1)S(1)} %get-tuple-element.60), channel_id=1, source_target_pairs={{0,4},{1,5},{2,6},{3,7},{4,0},{5,1},{6,2},{7,3},{8,12},{9,13},{10,... | collective-permute-start | bytes 196616 | tf_op jit(solution)/shard_map/ppermute | solution.py:396
  7.9 4.7 %collective-permute-start.6 = (bf16[2,64,256]{2,1,0:T(8,128)(2,1)S(1)}, bf16[2,64,256]{2,1,0:T(8,128)(2,1)S(1)}, u32[]{:S(2)}, u32[]{:S(2)}) collective-permute-start(bf16[2,64,256]{2,1,0:T(8,128)(2,1)S(1)} %get-tuple-element.61), channel_id=1, source_target_pairs={{0,2},{1,3},{2,0},{3,1},{4,6},{5,7},{6,4},{7,5},{8,10},{9,11},{10,... | collective-permute-start | bytes 196616 | tf_op jit(solution)/shard_map/ppermute | solution.py:396
  8.0 8.1 %collective-permute-start.1 = (bf16[192,128]{1,0:T(8,128)(2,1)S(1)}, bf16[192,128]{1,0:T(8,128)(2,1)S(1)}, u32[]{:S(2)}, u32[]{:S(2)}) collective-permute-start(bf16[192,128]{1,0:T(8,128)(2,1)S(1)} %get-tuple-element.53), channel_id=1, source_target_pairs={{0,16},{8,24},{16,0},{24,8},{1,17},{9,25},{17,1},{25,9},{2,18},{10... | collective-permute-start | bytes 147464 | tf_op jit(solution)/shard_map/ppermute | solution.py:387
  11.0 6.5 %collective-permute-start.2 = (bf16[192,128]{1,0:T(8,128)(2,1)S(1)}, bf16[192,128]{1,0:T(8,128)(2,1)S(1)}, u32[]{:S(2)}, u32[]{:S(2)}) collective-permute-start(bf16[192,128]{1,0:T(8,128)(2,1)S(1)} %get-tuple-element.54), channel_id=1, source_target_pairs={{0,24},{8,16},{16,8},{24,0},{1,25},{9,17},{17,9},{25,1},{2,26},{10... | collective-permute-start | bytes 147464 | tf_op jit(solution)/shard_map/ppermute | solution.py:387
  12.3 5.1 %collective-permute-start.3 = (bf16[192,128]{1,0:T(8,128)(2,1)S(1)}, bf16[192,128]{1,0:T(8,128)(2,1)S(1)}, u32[]{:S(2)}, u32[]{:S(2)}) collective-permute-start(bf16[192,128]{1,0:T(8,128)(2,1)S(1)} %get-tuple-element.55), channel_id=1, source_target_pairs={{0,8},{8,0},{16,24},{24,16},{1,9},{9,1},{17,25},{25,17},{2,10},{10... | collective-permute-start | bytes 147464 | tf_op jit(solution)/shard_map/ppermute | solution.py:387
  12.8 6.7 %collective-permute-start.7 = (bf16[192,128]{1,0:T(8,128)(2,1)S(1)}, bf16[192,128]{1,0:T(8,128)(2,1)S(1)}, u32[]{:S(2)}, u32[]{:S(2)}) collective-permute-start(bf16[192,128]{1,0:T(8,128)(2,1)S(1)} %get-tuple-element.62), channel_id=1, source_target_pairs={{0,24},{8,16},{16,8},{24,0},{1,25},{9,17},{17,9},{25,1},{2,26},{10... | collective-permute-start | bytes 147464 | tf_op jit(solution)/shard_map/ppermute | solution.py:387
  16.0 5.2 %collective-permute-start.8 = (bf16[192,128]{1,0:T(8,128)(2,1)S(1)}, bf16[192,128]{1,0:T(8,128)(2,1)S(1)}, u32[]{:S(2)}, u32[]{:S(2)}) collective-permute-start(bf16[192,128]{1,0:T(8,128)(2,1)S(1)} %get-tuple-element.63), channel_id=1, source_target_pairs={{0,16},{8,24},{16,0},{24,8},{1,17},{9,25},{17,1},{25,9},{2,18},{10... | collective-permute-start | bytes 147464 | tf_op jit(solution)/shard_map/ppermute | solution.py:387
  16.1 3.4 %copy-start = (bf16[768,1024]{1,0:T(8,128)(2,1)S(1)}, bf16[768,1024]{1,0:T(8,128)(2,1)}, u32[]{:S(2)}) copy-start(bf16[768,1024]{1,0:T(8,128)(2,1)} %weight_ref.5) | copy-start | bytes 4718596
  16.1 5.3 %collective-permute-start.9 = (bf16[192,128]{1,0:T(8,128)(2,1)S(1)}, bf16[192,128]{1,0:T(8,128)(2,1)S(1)}, u32[]{:S(2)}, u32[]{:S(2)}) collective-permute-start(bf16[192,128]{1,0:T(8,128)(2,1)S(1)} %get-tuple-element.64), channel_id=1, source_target_pairs={{0,8},{8,0},{16,24},{24,16},{1,9},{9,1},{17,25},{25,17},{2,10},{10... | collective-permute-start | bytes 147464 | tf_op jit(solution)/shard_map/ppermute | solution.py:387
  19.8 1.6 %copy-start.2 = (bf16[1024,153]{0,1:T(8,128)(2,1)S(1)}, bf16[1024,153]{0,1:T(8,128)(2,1)}, u32[]{:S(2)}) copy-start(bf16[1024,153]{0,1:T(8,128)(2,1)} %param.21) | copy-start | bytes 940036
  21.5 12.8 %copy-start.1 = (bf16[1024,153]{0,1:T(8,128)(2,1)S(1)}, bf16[1024,153]{0,1:T(8,128)(2,1)}, u32[]{:S(2)}) copy-start(bf16[1024,153]{0,1:T(8,128)(2,1)} %param.20) | copy-start | bytes 940036
  22.0 6.1 %collective-permute-start.10 = (bf16[153,128]{1,0:T(8,128)(2,1)S(1)}, bf16[153,128]{1,0:T(8,128)(2,1)S(1)}, u32[]{:S(2)}, u32[]{:S(2)}) collective-permute-start(bf16[153,128]{1,0:T(8,128)(2,1)S(1)} %get-tuple-element.69), channel_id=1, source_target_pairs={{0,24},{8,16},{16,8},{24,0},{1,25},{9,17},{17,9},{25,1},{2,26},{10... | collective-permute-start | bytes 117512 | tf_op jit(solution)/shard_map/ppermute | solution.py:387
  24.3 4.9 %collective-permute-start.11 = (bf16[153,128]{1,0:T(8,128)(2,1)S(1)}, bf16[153,128]{1,0:T(8,128)(2,1)S(1)}, u32[]{:S(2)}, u32[]{:S(2)}) collective-permute-start(bf16[153,128]{1,0:T(8,128)(2,1)S(1)} %get-tuple-element.70), channel_id=1, source_target_pairs={{0,16},{8,24},{16,0},{24,8},{1,17},{9,25},{17,1},{25,9},{2,18},{10... | collective-permute-start | bytes 117512 | tf_op jit(solution)/shard_map/ppermute | solution.py:387
  24.3 5.1 %collective-permute-start.12 = (bf16[153,128]{1,0:T(8,128)(2,1)S(1)}, bf16[153,128]{1,0:T(8,128)(2,1)S(1)}, u32[]{:S(2)}, u32[]{:S(2)}) collective-permute-start(bf16[153,128]{1,0:T(8,128)(2,1)S(1)} %get-tuple-element.71), channel_id=1, source_target_pairs={{0,8},{8,0},{16,24},{24,16},{1,9},{9,1},{17,25},{25,17},{2,10},{10... | collective-permute-start | bytes 117512 | tf_op jit(solution)/shard_map/ppermute | solution.py:387
  29.6 1.3 %collective-permute-start.13 = (bf16[4,16,256]{2,1,0:T(8,128)(2,1)S(1)}, bf16[4,16,256]{2,1,0:T(8,128)(2,1)S(1)}, u32[]{:S(2)}, u32[]{:S(2)}) collective-permute-start(bf16[4,16,256]{2,1,0:T(8,128)(2,1)S(1)} %get-tuple-element.73), channel_id=1, source_target_pairs={{0,1},{1,0},{2,3},{3,2},{4,5},{5,4},{6,7},{7,6},{8,9},{9,8},{10,11... | collective-permute-start | bytes 98312 | tf_op jit(solution)/shard_map/ppermute | solution.py:392
  30.8 4.6 %collective-permute-start.14 = (bf16[2,16,256]{2,1,0:T(8,128)(2,1)S(1)}, bf16[2,16,256]{2,1,0:T(8,128)(2,1)S(1)}, u32[]{:S(2)}, u32[]{:S(2)}) collective-permute-start(bf16[2,16,256]{2,1,0:T(8,128)(2,1)S(1)} %get-tuple-element.75), channel_id=1, source_target_pairs={{0,6},{1,7},{2,4},{3,5},{4,2},{5,3},{6,0},{7,1},{8,14},{9,15},{10,... | collective-permute-start | bytes 49160 | tf_op jit(solution)/shard_map/ppermute | solution.py:396
  33.2 3.7 %collective-permute-start.15 = (bf16[2,16,256]{2,1,0:T(8,128)(2,1)S(1)}, bf16[2,16,256]{2,1,0:T(8,128)(2,1)S(1)}, u32[]{:S(2)}, u32[]{:S(2)}) collective-permute-start(bf16[2,16,256]{2,1,0:T(8,128)(2,1)S(1)} %get-tuple-element.76), channel_id=1, source_target_pairs={{0,4},{1,5},{2,6},{3,7},{4,0},{5,1},{6,2},{7,3},{8,12},{9,13},{10,... | collective-permute-start | bytes 49160 | tf_op jit(solution)/shard_map/ppermute | solution.py:396
  33.7 3.7 %collective-permute-start.16 = (bf16[2,16,256]{2,1,0:T(8,128)(2,1)S(1)}, bf16[2,16,256]{2,1,0:T(8,128)(2,1)S(1)}, u32[]{:S(2)}, u32[]{:S(2)}) collective-permute-start(bf16[2,16,256]{2,1,0:T(8,128)(2,1)S(1)} %get-tuple-element.77), channel_id=1, source_target_pairs={{0,2},{1,3},{2,0},{3,1},{4,6},{5,7},{6,4},{7,5},{8,10},{9,11},{10,... | collective-permute-start | bytes 49160 | tf_op jit(solution)/shard_map/ppermute | solution.py:396

commit v23 on v19

--- a/solution.py
+++ b/solution.py
@@ -86,9 +86,10 @@
 
 
 def pick_rows(chunk, other, part_ref, sources_ref, table_ref, out_ref, order, hits, ready):
-    chips, lanes = out_ref.shape[0], out_ref.shape[2]
+    chips = out_ref.shape[0]
     _, groups, slots = sources_ref.shape
-    nodes = table_ref.shape[1]
+    lanes, nodes = table_ref.shape[0] - EXTRA, table_ref.shape[1]
+    half = groups * slots // 2
     chip, core = part_ref[0] // 2, part_ref[0] % 2
     lane = lax.broadcasted_iota(jnp.int32, (slots, nodes), 1)
 
@@ -102,8 +103,15 @@
             ).astype(bf16)
         if last:
             ready()
-        picked = dot(hits[...], table_ref[:lanes, :], LAST).astype(bf16)
-        out_ref[pl.ds(i * chunk, chunk)] = picked.reshape(chunk, groups * slots, -1)
+        picked = dot(hits[...], table_ref[:lanes, :], LAST)
+        picked = picked.reshape(chunk, groups * slots, lanes)
+        tail = picked[:, :, lanes - 128 :]
+        left = lax.broadcasted_iota(jnp.int32, (chunk, half, 128), 2) < 64
+        tail = jnp.where(left, tail[:, :half], tail[:, half:]).astype(bf16)
+        out_ref[pl.ds(i * chunk, chunk), out_ref.shape[1] - half :, :] = tail
+        if lanes > 128:
+            body = picked[:, :, :128].astype(bf16)
+            out_ref[pl.ds(i * chunk, chunk), : 2 * half, :] = body
 
     if chips == chunk:
         step(0, True)
@@ -116,19 +124,21 @@
     extras, (mate_ref, table_ref, sources_ref, *rest) = rest[:PASSED], rest[PASSED:]
     passed, (order, hits, sems) = rest[:PASSED], rest[PASSED:]
     width, nodes = features_hbm.shape
-    indices, table, *others = fetch(
+    indices, table, tail, *others = fetch(
         sems,
         (sources_hbm, sources_ref),
         (features_hbm, table_ref.at[pl.ds(0, width), :]),
+        (features_hbm.at[pl.ds(width - 64, 64), :], table_ref.at[pl.ds(width, 64), :]),
         *zip(extras, passed),
     )
-    table_ref[width : width + EXTRA, :] = jnp.ones((EXTRA, nodes), bf16)
-    if table_ref.shape[0] > width + EXTRA:
-        table_ref[width + EXTRA :, :] = jnp.zeros(
-            (table_ref.shape[0] - width - EXTRA, nodes), bf16
-        )
+    table_ref[width + 64 :, :] = jnp.ones((EXTRA, nodes), bf16)
+
+    def ready():
+        table.wait()
+        tail.wait()
+
     indices.wait()
-    pick_rows(chunk, 1, part_ref, sources_ref, table_ref, mate_ref, order, hits, table.wait)
+    pick_rows(chunk, 1, part_ref, sources_ref, table_ref, mate_ref, order, hits, ready)
     for copy in others:
         copy.wait()
 
@@ -154,7 +164,7 @@
     parts, groups, slots = targets_ref.shape
     rows = edges_ref.shape[3]
     high = sums_ref.shape[1]
-    width = high - EXTRA
+    width = high - EXTRA - 64
     copies = fetch(sems, (ids_vmem, ids_ref), (counts_vmem, counts_ref))
     bands_ref[...] = jnp.zeros_like(bands_ref)
     picked = order.shape[0]
@@ -191,7 +201,7 @@
                 values = jnp.where(hit, weight[:, n : n + 1], 0.0)
                 edges_ref[g, at] = values.astype(bf16)
                 degree = degree + jnp.sum(values, axis=0, keepdims=True)
-            sums_ref[g, width : width + 1, :] += degree
+            sums_ref[g, high - EXTRA : high - EXTRA + 1, :] += degree
         return 0
 
     if parts == chunk:
@@ -220,14 +230,24 @@
 def mean_kernel(first, me_ref, sums_ref, edges_ref, *rest):
     groups, parts, slots, rows = edges_ref.shape
     arrived, outs = rest[: parts // 2], rest[parts // 2 :]
-    width = outs[0].shape[0]
+    width, high = outs[0].shape[0], sums_ref.shape[1] - EXTRA
+    body, half = width - 64, groups // 2
     for k, out in enumerate(outs, first):
         group = ahead(me_ref[0], groups, k)
-        span = pl.ds(pl.multiple_of(group * slots, slots), slots)
-        far = jnp.concatenate([x[:, span, :].reshape(2 * slots, -1) for x in arrived], axis=0)
-        far = dot(far, edges_ref[group].reshape(parts * slots, rows), FIRST)
-        total = sums_ref[group, :width, :] + far[:width]
-        out[...] = (total / sums_ref[group, width : width + 1, :]).astype(bf16)
+        edges = edges_ref[group].reshape(parts * slots, rows)
+
+        def boundary(row):
+            span = pl.ds(pl.multiple_of(row * slots, slots), slots)
+            far = [x[:, span, :].reshape(2 * slots, 128) for x in arrived]
+            return dot(jnp.concatenate(far, axis=0), edges, FIRST)
+
+        tail = boundary((groups if body else 0) + group % half)
+        tail = jnp.where(group < half, tail[:64], tail[64:])
+        degree = sums_ref[group, high : high + 1, :]
+        out[body:, :] = ((sums_ref[group, body:width, :] + tail) / degree).astype(bf16)
+        if body:
+            total = sums_ref[group, :body, :] + boundary(group)
+            out[:body, :] = (total / degree).astype(bf16)
 
 
 def own_mean_kernel(after, *rest):
@@ -399,7 +419,7 @@
 
     picked = min(chips, chunk)
     lanes = whole_lanes(width)
-    table_rows = max(lanes, width + EXTRA)
+    folded = groups * slots // 2 * (3 if width > 64 else 1)
     extras = (tile_contents, targets[0], edge_weight[0], tile_ids[0].T, counts[0].T)
     picking = [
         pltpu.VMEM((picked, groups, slots), jnp.int32),
@@ -408,13 +428,13 @@
     mate, table, *passed = call(
         functools.partial(gather_kernel, picked),
         (
-            shape(chips, groups * slots, lanes),
-            shape(table_rows, nodes),
+            shape(chips, folded, 128),
+            shape(lanes + EXTRA, nodes),
             shape(parts, groups, slots, dtype=jnp.int32),
         )
         + tuple(shape(*value.shape, dtype=value.dtype) for value in extras),
         [SM, HB, HB] + [HB] * PASSED,
-        picking + [pltpu.SemaphoreType.DMA((2 + PASSED,))],
+        picking + [pltpu.SemaphoreType.DMA((3 + PASSED,))],
         2 * nodes * nodes * width,
         1 << 20,
     )(part, sources[0], feature_rows, *extras)
@@ -422,10 +442,10 @@
     sums, edges, band, mine, *feature_blocks = call(
         functools.partial(local_kernel, chunk),
         (
-            shape(groups, width + EXTRA, rows, dtype=f32),
+            shape(groups, lanes + EXTRA, rows, dtype=f32),
             shape(groups, parts, slots, rows),
             shape(rows, nodes),
-            shape(chips, groups * slots, lanes),
+            shape(chips, folded, 128),
         )
         + (shape(width, rows),) * (groups - 1),
         [SM, SM, VM, VM] + [VM] * PASSED,
@@ -442,7 +462,7 @@
     )(me, part, table, *passed)
     paired = call(
         pair_kernel,
-        (shape(2, groups * slots, lanes),) * chips + (shape(width, rows),) * (groups - 1),
+        (shape(2, folded, 128),) * chips + (shape(width, rows),) * (groups - 1),
         [VM] * (2 + groups),
         (),
         0,

time: 38.1 us -> 38.4 us (level)
  no operation moved by 1% of the time
where the time goes in v23:
time: 38.4 us; the launch traced here: 38.1 us
  starting transfers between devices  21.7 us (57%)
  Pallas kernels  8.97 us (23%)
  waiting for transfers between devices  6.64 us (17%)
  between operations  0.79 us (2%)
    ppermute x9, starting transfers between devices, shift(): lax.ppermute(block, 'feat', [(i, ahead(i, groups, k, near)) for i in rang...  13.5 us
    pallas_call x16, Pallas kernels, placed(): run(*(pltpu.with_memory_space_constraint(value, pltpu.HBM) if spec is HB...  8.97 us
    ppermute x6, starting transfers between devices, to_chips(): lax.ppermute(blocks[j], 'dom', [(d, next_to(d // 2, j, chips) * 2 + d % 2...  7.67 us
    ppermute x9, waiting for transfers between devices, shift(): lax.ppermute(block, 'feat', [(i, ahead(i, groups, k, near)) for i in rang...  3.37 us
    ppermute x6, waiting for transfers between devices, to_chips(): lax.ppermute(blocks[j], 'dom', [(d, next_to(d // 2, j, chips) * 2 + d % 2...  2.08 us
    ppermute x2, waiting for transfers between devices, to_mate(): return lax.ppermute(value, 'dom', [(d, d ^ 1) for d in range(parts)])  1.2 us
  transfers between devices with their start and end apart: 17, of which 8 were waited for; matrix products, arithmetic and copies ran while one was open for 0% of the time, Pallas kernels for 16%

profile of v23, /device:TPU:0, one launch (start us, length us, event | category | flops | bytes accessed | tf_op | source)
XLA Modules:
  0.0 38.1 jit_solution(16844530896740438473)
XLA Ops:
  0.6 1.3 %shard_map.122 = (bf16[4,96,128]{2,1,0:T(8,128)(2,1)S(1)}, bf16[272,512]{1,0:T(8,128)(2,1)S(1)}, s32[8,4,16]{2,1,0:T(4,128)S(1)}, bf16[12,128,128]{2,1,0:T(8,128...) custom-call(s32[1]{0:T(128)} %bitcast.4.part_ref, ...), custom_call_target="tpu_custom_call" | custom-call | flops 100663296 | bytes 1048576 | tf_op jit(solution)/shard_map/pallas_call | solution.py:33
  1.9 0.5 %collective-permute-start = (bf16[4,96,128]{2,1,0:T(8,128)(2,1)S(1)}, bf16[4,96,128]{2,1,0:T(8,128)(2,1)S(1)}, u32[]{:S(2)}, u32[]{:S(2)}) collective-permute-start(bf16[4,96,128]{2,1,0:T(8,128)(2,1)S(1)} %get-tuple-element.49), channel_id=1, source_target_pairs={{0,1},{1,0},{2,3},{3,2},{4,5},{5,4},{6,7},{7,6},{8,9},{9,8},{10,11... | collective-permute-start | bytes 294920 | tf_op jit(solution)/shard_map/ppermute | solution.py:408
  2.5 1.2 %shard_map.123 = (f32[4,272,128]{2,1,0:T(8,128)S(1)}, bf16[4,8,16,128]{3,2,1,0:T(8,128)(2,1)S(1)}, bf16[128,512]{1,0:T(8,128)(2,1)S(1)}, bf16[4,96,128]{2,1,0:T(...) custom-call(s32[1]{0:T(128)} %bitcast.me_ref.rest_0_, ...), custom_call_target="tpu_custom_call" | custom-call | flops 100663296 | bytes 1048576 | tf_op jit(solution)/shard_map/pallas_call | solution.py:33
  3.7 0.0 collective-permute-done.got_ref
  3.8 3.5 %collective-permute-start.4 = (bf16[2,96,128]{2,1,0:T(8,128)(2,1)S(1)}, bf16[2,96,128]{2,1,0:T(8,128)(2,1)S(1)}, u32[]{:S(2)}, u32[]{:S(2)}) collective-permute-start(bf16[2,96,128]{2,1,0:T(8,128)(2,1)S(1)} %get-tuple-element.59), channel_id=1, source_target_pairs={{0,6},{1,7},{2,4},{3,5},{4,2},{5,3},{6,0},{7,1},{8,14},{9,15},{10,... | collective-permute-start | bytes 147464 | tf_op jit(solution)/shard_map/ppermute | solution.py:412
  7.3 0.5 %collective-permute-start.5 = (bf16[2,96,128]{2,1,0:T(8,128)(2,1)S(1)}, bf16[2,96,128]{2,1,0:T(8,128)(2,1)S(1)}, u32[]{:S(2)}, u32[]{:S(2)}) collective-permute-start(bf16[2,96,128]{2,1,0:T(8,128)(2,1)S(1)} %get-tuple-element.60), channel_id=1, source_target_pairs={{0,4},{1,5},{2,6},{3,7},{4,0},{5,1},{6,2},{7,3},{8,12},{9,13},{10,... | collective-permute-start | bytes 147464 | tf_op jit(solution)/shard_map/ppermute | solution.py:412
  7.8 0.1 collective-permute-start.6
  7.9 3.0 %collective-permute-start.1 = (bf16[192,128]{1,0:T(8,128)(2,1)S(1)}, bf16[192,128]{1,0:T(8,128)(2,1)S(1)}, u32[]{:S(2)}, u32[]{:S(2)}) collective-permute-start(bf16[192,128]{1,0:T(8,128)(2,1)S(1)} %get-tuple-element.53), channel_id=1, source_target_pairs={{0,16},{8,24},{16,0},{24,8},{1,17},{9,25},{17,1},{25,9},{2,18},{10... | collective-permute-start | bytes 147464 | tf_op jit(solution)/shard_map/ppermute | solution.py:403
  10.9 1.3 %collective-permute-start.2 = (bf16[192,128]{1,0:T(8,128)(2,1)S(1)}, bf16[192,128]{1,0:T(8,128)(2,1)S(1)}, u32[]{:S(2)}, u32[]{:S(2)}) collective-permute-start(bf16[192,128]{1,0:T(8,128)(2,1)S(1)} %get-tuple-element.54), channel_id=1, source_target_pairs={{0,24},{8,16},{16,8},{24,0},{1,25},{9,17},{17,9},{25,1},{2,26},{10... | collective-permute-start | bytes 147464 | tf_op jit(solution)/shard_map/ppermute | solution.py:403
  12.3 0.0 collective-permute-done.4.rest_4_.rest_1_
  12.3 0.2 collective-permute-start.3
  12.5 0.0 collective-permute-done.5.rest_5_.rest_2_
  12.5 0.0 collective-permute-done.6.rest_6_.rest_3_
  12.5 0.2 shard_map.127
  12.8 3.0 %collective-permute-start.7 = (bf16[192,128]{1,0:T(8,128)(2,1)S(1)}, bf16[192,128]{1,0:T(8,128)(2,1)S(1)}, u32[]{:S(2)}, u32[]{:S(2)}) collective-permute-start(bf16[192,128]{1,0:T(8,128)(2,1)S(1)} %get-tuple-element.62), channel_id=1, source_target_pairs={{0,24},{8,16},{16,8},{24,0},{1,25},{9,17},{17,9},{25,1},{2,26},{10... | collective-permute-start | bytes 147464 | tf_op jit(solution)/shard_map/ppermute | solution.py:403
  15.8 0.3 collective-permute-start.8
  16.1 0.0 collective-permute-done.1.rest_0_
  16.1 1.1 %collective-permute-start.9 = (bf16[192,128]{1,0:T(8,128)(2,1)S(1)}, bf16[192,128]{1,0:T(8,128)(2,1)S(1)}, u32[]{:S(2)}, u32[]{:S(2)}) collective-permute-start(bf16[192,128]{1,0:T(8,128)(2,1)S(1)} %get-tuple-element.64), channel_id=1, source_target_pairs={{0,8},{8,0},{16,24},{24,16},{1,9},{9,1},{17,25},{25,17},{2,10},{10... | collective-permute-start | bytes 147464 | tf_op jit(solution)/shard_map/ppermute | solution.py:403
  17.2 0.2 collective-permute-done.2.rest_1_
  17.5 0.0 collective-permute-done.3.rest_2_
  17.5 1.8 %shard_map.125.after.own_ref = f32[128,1024]{1,0:T(8,128)S(1)} custom-call(s32[1]{0:T(128)} %bitcast.me_ref.rest_0_, bf16[192,512]{1,0:T(8,128)(2,1)} %bitcast.22, bf16[768,1024]{1,0:T(8,128)(2,1)} %weight_hbm.1, bf16[192,128]{1,0:T(8,128)(2,1)S(1)} %collective-permute-done.1.rest_0_, bf16[192,128]{1,0:T(8,128)(2,1)S(1)} %collective-permute-done.2.rest_1_, ...), custom_call_target="tpu_custom_call" | custom-call | flops 201326592 | bytes 2097152 | tf_op jit(solution)/shard_map/pallas_call | solution.py:33
  19.3 0.2 shard_map.126.rest_0_
  19.5 0.0 collective-permute-done.7.rest_1_
  19.5 0.3 shard_map.128.early_ref
  19.8 1.3 %collective-permute-done.8.rest_0_ = bf16[192,128]{1,0:T(8,128)(2,1)S(1)} collective-permute-done((bf16[192,128]{1,0:T(8,128)(2,1)S(1)}, bf16[192,128]{1,0:T(8,128)(2,1)S(1)}, u32[]{:S(2)}, u32[]{:S(2)}) %collective-permute-start.8) | collective-permute-done | bytes 49184 | tf_op jit(solution)/shard_map/ppermute | solution.py:403
  21.2 0.0 collective-permute-done.9.rest_1_
  21.2 0.5 %shard_map.129 = (bf16[128,1024]{1,0:T(8,128)(2,1)S(1)}, bf16[153,128]{1,0:T(8,128)(2,1)S(1)}, bf16[153,128]{1,0:T(8,128)(2,1)S(1)}, bf16[153,128]{1,0:T(8,128)(2,1)S(1)}, bf16[153,128]{1,0:T(8,128)(2,1)S(1)}) custom-call(s32[1]{0:T(128)} %bitcast.me_ref.rest_0_, bf16[768,1024]{1,0:T(8,128)(2,1)S(1)} %copy-done, bf16[153,1024]{1,0:T(8,128)(2,1)S(1)} %bitcast.20, ...), custom_call_target="tpu_custom_call" | custom-call | flops 100663296 | bytes 2097152 | tf_op jit(solution)/shard_map/pallas_call | solution.py:33
  21.7 2.5 %collective-permute-start.10 = (bf16[153,128]{1,0:T(8,128)(2,1)S(1)}, bf16[153,128]{1,0:T(8,128)(2,1)S(1)}, u32[]{:S(2)}, u32[]{:S(2)}) collective-permute-start(bf16[153,128]{1,0:T(8,128)(2,1)S(1)} %get-tuple-element.69), channel_id=1, source_target_pairs={{0,24},{8,16},{16,8},{24,0},{1,25},{9,17},{17,9},{25,1},{2,26},{10... | collective-permute-start | bytes 117512 | tf_op jit(solution)/shard_map/ppermute | solution.py:403
  24.2 0.0 collective-permute-start.11
  24.2 2.0 %collective-permute-start.12 = (bf16[153,128]{1,0:T(8,128)(2,1)S(1)}, bf16[153,128]{1,0:T(8,128)(2,1)S(1)}, u32[]{:S(2)}, u32[]{:S(2)}) collective-permute-start(bf16[153,128]{1,0:T(8,128)(2,1)S(1)} %get-tuple-element.71), channel_id=1, source_target_pairs={{0,8},{8,0},{16,24},{24,16},{1,9},{9,1},{17,25},{25,17},{2,10},{10... | collective-permute-start | bytes 117512 | tf_op jit(solution)/shard_map/ppermute | solution.py:403
  26.2 0.9 %shard_map.132.hits_ref.after = bf16[128,512]{1,0:T(8,128)(2,1)S(1)} custom-call(bf16[153,128]{1,0:T(8,128)(2,1)S(1)} %get-tuple-element.68.rest_0_.after, s32[1]{0:T(128)} %bitcast.me_ref.rest_0_, s32[1]{0:T(128)} %bitcast.4.part_ref, s32[8,4,16]{2,1,0:T(4,128)} %bitcast.26), custom_call_target="tpu_custom_call" | custom-call | bytes 524288 | tf_op jit(solution)/shard_map/pallas_call | solution.py:33
  27.1 0.6 %collective-permute-done.10.rest_1_ = bf16[153,128]{1,0:T(8,128)(2,1)S(1)} collective-permute-done((bf16[153,128]{1,0:T(8,128)(2,1)S(1)}, bf16[153,128]{1,0:T(8,128)(2,1)S(1)}, u32[]{:S(2)}, u32[]{:S(2)}) %collective-permute-start.10) | collective-permute-done | bytes 39200 | tf_op jit(solution)/shard_map/ppermute | solution.py:403
  27.7 0.2 shard_map.133.early_ref
  27.9 1.2 %collective-permute-done.11.rest_2_.rest_0_ = bf16[153,128]{1,0:T(8,128)(2,1)S(1)} collective-permute-done((bf16[153,128]{1,0:T(8,128)(2,1)S(1)}, bf16[153,128]{1,0:T(8,128)(2,1)S(1)}, u32[]{:S(2)}, u32[]{:S(2)}) %collective-permute-start.11) | collective-permute-done | bytes 39200 | tf_op jit(solution)/shard_map/ppermute | solution.py:403
  29.1 0.0 collective-permute-done.12.rest_3_.rest_1_
  29.1 0.2 shard_map.134
  29.3 0.1 collective-permute-start.13
  29.4 1.2 %collective-permute-done.13.got_ref = bf16[4,16,256]{2,1,0:T(8,128)(2,1)S(1)} collective-permute-done((bf16[4,16,256]{2,1,0:T(8,128)(2,1)S(1)}, bf16[4,16,256]{2,1,0:T(8,128)(2,1)S(1)}, u32[]{:S(2)}, u32[]{:S(2)}) %collective-permute-start.13) | collective-permute-done | bytes 32800 | tf_op jit(solution)/shard_map/ppermute | solution.py:408
  30.6 2.5 %collective-permute-start.14 = (bf16[2,16,256]{2,1,0:T(8,128)(2,1)S(1)}, bf16[2,16,256]{2,1,0:T(8,128)(2,1)S(1)}, u32[]{:S(2)}, u32[]{:S(2)}) collective-permute-start(bf16[2,16,256]{2,1,0:T(8,128)(2,1)S(1)} %get-tuple-element.75), channel_id=1, source_target_pairs={{0,6},{1,7},{2,4},{3,5},{4,2},{5,3},{6,0},{7,1},{8,14},{9,15},{10,... | collective-permute-start | bytes 49160 | tf_op jit(solution)/shard_map/ppermute | solution.py:412
  33.1 0.5 %collective-permute-start.15 = (bf16[2,16,256]{2,1,0:T(8,128)(2,1)S(1)}, bf16[2,16,256]{2,1,0:T(8,128)(2,1)S(1)}, u32[]{:S(2)}, u32[]{:S(2)}) collective-permute-start(bf16[2,16,256]{2,1,0:T(8,128)(2,1)S(1)} %get-tuple-element.76), channel_id=1, source_target_pairs={{0,4},{1,5},{2,6},{3,7},{4,0},{5,1},{6,2},{7,3},{8,12},{9,13},{10,... | collective-permute-start | bytes 49160 | tf_op jit(solution)/shard_map/ppermute | solution.py:412
  33.6 0.5 %collective-permute-start.16 = (bf16[2,16,256]{2,1,0:T(8,128)(2,1)S(1)}, bf16[2,16,256]{2,1,0:T(8,128)(2,1)S(1)}, u32[]{:S(2)}, u32[]{:S(2)}) collective-permute-start(bf16[2,16,256]{2,1,0:T(8,128)(2,1)S(1)} %get-tuple-element.77), channel_id=1, source_target_pairs={{0,2},{1,3},{2,0},{3,1},{4,6},{5,7},{6,4},{7,5},{8,10},{9,11},{10,... | collective-permute-start | bytes 49160 | tf_op jit(solution)/shard_map/ppermute | solution.py:412
  34.1 0.7 %shard_map.130 = (f32[153,128]{1,0:T(8,128)S(1)}, bf16[128,1024]{1,0:T(8,128)(2,1)}) custom-call(bf16[128,1024]{1,0:T(8,128)(2,1)S(1)} %get-tuple-element.65.hidden_ref, bf16[153,1024]{1,0:T(8,128)(2,1)S(1)} %bitcast.19), custom_call_target="tpu_custom_call" | custom-call | flops 40108032 | bytes 1048576 | tf_op jit(solution)/shard_map/pallas_call | solution.py:33
  34.8 0.2 shard_map.131.near_ref
  35.0 0.2 collective-permute-done.14.rest_1_
  35.2 0.2 shard_map.136.rest_0_
  35.4 1.4 %collective-permute-done.15.rest_3_ = bf16[2,16,256]{2,1,0:T(8,128)(2,1)S(1)} collective-permute-done((bf16[2,16,256]{2,1,0:T(8,128)(2,1)S(1)}, bf16[2,16,256]{2,1,0:T(8,128)(2,1)S(1)}, u32[]{:S(2)}, u32[]{:S(2)}) %collective-permute-start.15) | collective-permute-done | bytes 16416 | tf_op jit(solution)/shard_map/ppermute | solution.py:412
  36.8 0.5 %collective-permute-done.16.rest_4_ = bf16[2,16,256]{2,1,0:T(8,128)(2,1)S(1)} collective-permute-done((bf16[2,16,256]{2,1,0:T(8,128)(2,1)S(1)}, bf16[2,16,256]{2,1,0:T(8,128)(2,1)S(1)}, u32[]{:S(2)}, u32[]{:S(2)}) %collective-permute-start.16) | collective-permute-done | bytes 16416 | tf_op jit(solution)/shard_map/ppermute | solution.py:412
  37.3 0.8 %shard_map.137 = f32[153,1,128]{2,1,0:T(1,128)} custom-call(s32[1]{0:T(128)} %bitcast.me_ref.rest_0_, f32[153,128]{1,0:T(8,128)S(1)} %shard_map.136.rest_0_, bf16[4,8,16,128]{3,2,1,0:T(8,128)(2,1)S(1)} %get-tuple-element.57.rest_2_.edges_ref.rest_1_, f32[4,272,128]{2,1,0:T(8,128)S(1)} %get-tuple-element.56.rest_1_.sums_ref.rest_2_, ...), custom_call_target="tpu_custom_call" | custom-call | flops 2506752 | bytes 524288 | tf_op jit(solution)/shard_map/pallas_call | solution.py:33
  (8 shorter events, 0.0 us)
Async XLA Ops:
  1.9 1.8 %collective-permute-start = (bf16[4,96,128]{2,1,0:T(8,128)(2,1)S(1)}, bf16[4,96,128]{2,1,0:T(8,128)(2,1)S(1)}, u32[]{:S(2)}, u32[]{:S(2)}) collective-permute-start(bf16[4,96,128]{2,1,0:T(8,128)(2,1)S(1)} %get-tuple-element.49), channel_id=1, source_target_pairs={{0,1},{1,0},{2,3},{3,2},{4,5},{5,4},{6,7},{7,6},{8,9},{9,8},{10,11... | collective-permute-start | bytes 294920 | tf_op jit(solution)/shard_map/ppermute | solution.py:408
  3.8 8.5 %collective-permute-start.4 = (bf16[2,96,128]{2,1,0:T(8,128)(2,1)S(1)}, bf16[2,96,128]{2,1,0:T(8,128)(2,1)S(1)}, u32[]{:S(2)}, u32[]{:S(2)}) collective-permute-start(bf16[2,96,128]{2,1,0:T(8,128)(2,1)S(1)} %get-tuple-element.59), channel_id=1, source_target_pairs={{0,6},{1,7},{2,4},{3,5},{4,2},{5,3},{6,0},{7,1},{8,14},{9,15},{10,... | collective-permute-start | bytes 147464 | tf_op jit(solution)/shard_map/ppermute | solution.py:412
  7.3 5.2 %collective-permute-start.5 = (bf16[2,96,128]{2,1,0:T(8,128)(2,1)S(1)}, bf16[2,96,128]{2,1,0:T(8,128)(2,1)S(1)}, u32[]{:S(2)}, u32[]{:S(2)}) collective-permute-start(bf16[2,96,128]{2,1,0:T(8,128)(2,1)S(1)} %get-tuple-element.60), channel_id=1, source_target_pairs={{0,4},{1,5},{2,6},{3,7},{4,0},{5,1},{6,2},{7,3},{8,12},{9,13},{10,... | collective-permute-start | bytes 147464 | tf_op jit(solution)/shard_map/ppermute | solution.py:412
  7.8 4.7 %collective-permute-start.6 = (bf16[2,96,128]{2,1,0:T(8,128)(2,1)S(1)}, bf16[2,96,128]{2,1,0:T(8,128)(2,1)S(1)}, u32[]{:S(2)}, u32[]{:S(2)}) collective-permute-start(bf16[2,96,128]{2,1,0:T(8,128)(2,1)S(1)} %get-tuple-element.61), channel_id=1, source_target_pairs={{0,2},{1,3},{2,0},{3,1},{4,6},{5,7},{6,4},{7,5},{8,10},{9,11},{10,... | collective-permute-start | bytes 147464 | tf_op jit(solution)/shard_map/ppermute | solution.py:412
  7.9 8.2 %collective-permute-start.1 = (bf16[192,128]{1,0:T(8,128)(2,1)S(1)}, bf16[192,128]{1,0:T(8,128)(2,1)S(1)}, u32[]{:S(2)}, u32[]{:S(2)}) collective-permute-start(bf16[192,128]{1,0:T(8,128)(2,1)S(1)} %get-tuple-element.53), channel_id=1, source_target_pairs={{0,16},{8,24},{16,0},{24,8},{1,17},{9,25},{17,1},{25,9},{2,18},{10... | collective-permute-start | bytes 147464 | tf_op jit(solution)/shard_map/ppermute | solution.py:403
  10.9 6.5 %collective-permute-start.2 = (bf16[192,128]{1,0:T(8,128)(2,1)S(1)}, bf16[192,128]{1,0:T(8,128)(2,1)S(1)}, u32[]{:S(2)}, u32[]{:S(2)}) collective-permute-start(bf16[192,128]{1,0:T(8,128)(2,1)S(1)} %get-tuple-element.54), channel_id=1, source_target_pairs={{0,24},{8,16},{16,8},{24,0},{1,25},{9,17},{17,9},{25,1},{2,26},{10... | collective-permute-start | bytes 147464 | tf_op jit(solution)/shard_map/ppermute | solution.py:403
  12.3 5.2 %collective-permute-start.3 = (bf16[192,128]{1,0:T(8,128)(2,1)S(1)}, bf16[192,128]{1,0:T(8,128)(2,1)S(1)}, u32[]{:S(2)}, u32[]{:S(2)}) collective-permute-start(bf16[192,128]{1,0:T(8,128)(2,1)S(1)} %get-tuple-element.55), channel_id=1, source_target_pairs={{0,8},{8,0},{16,24},{24,16},{1,9},{9,1},{17,25},{25,17},{2,10},{10... | collective-permute-start | bytes 147464 | tf_op jit(solution)/shard_map/ppermute | solution.py:403
  12.8 6.7 %collective-permute-start.7 = (bf16[192,128]{1,0:T(8,128)(2,1)S(1)}, bf16[192,128]{1,0:T(8,128)(2,1)S(1)}, u32[]{:S(2)}, u32[]{:S(2)}) collective-permute-start(bf16[192,128]{1,0:T(8,128)(2,1)S(1)} %get-tuple-element.62), channel_id=1, source_target_pairs={{0,24},{8,16},{16,8},{24,0},{1,25},{9,17},{17,9},{25,1},{2,26},{10... | collective-permute-start | bytes 147464 | tf_op jit(solution)/shard_map/ppermute | solution.py:403
  15.8 5.3 %collective-permute-start.8 = (bf16[192,128]{1,0:T(8,128)(2,1)S(1)}, bf16[192,128]{1,0:T(8,128)(2,1)S(1)}, u32[]{:S(2)}, u32[]{:S(2)}) collective-permute-start(bf16[192,128]{1,0:T(8,128)(2,1)S(1)} %get-tuple-element.63), channel_id=1, source_target_pairs={{0,16},{8,24},{16,0},{24,8},{1,17},{9,25},{17,1},{25,9},{2,18},{10... | collective-permute-start | bytes 147464 | tf_op jit(solution)/shard_map/ppermute | solution.py:403
  16.1 3.4 %copy-start = (bf16[768,1024]{1,0:T(8,128)(2,1)S(1)}, bf16[768,1024]{1,0:T(8,128)(2,1)}, u32[]{:S(2)}) copy-start(bf16[768,1024]{1,0:T(8,128)(2,1)} %weight_ref.3) | copy-start | bytes 4718596
  16.1 5.1 %collective-permute-start.9 = (bf16[192,128]{1,0:T(8,128)(2,1)S(1)}, bf16[192,128]{1,0:T(8,128)(2,1)S(1)}, u32[]{:S(2)}, u32[]{:S(2)}) collective-permute-start(bf16[192,128]{1,0:T(8,128)(2,1)S(1)} %get-tuple-element.64), channel_id=1, source_target_pairs={{0,8},{8,0},{16,24},{24,16},{1,9},{9,1},{17,25},{25,17},{2,10},{10... | collective-permute-start | bytes 147464 | tf_op jit(solution)/shard_map/ppermute | solution.py:403
  19.5 1.7 %copy-start.2 = (bf16[1024,153]{0,1:T(8,128)(2,1)S(1)}, bf16[1024,153]{0,1:T(8,128)(2,1)}, u32[]{:S(2)}) copy-start(bf16[1024,153]{0,1:T(8,128)(2,1)} %param.21) | copy-start | bytes 940036
  21.2 12.9 %copy-start.1 = (bf16[1024,153]{0,1:T(8,128)(2,1)S(1)}, bf16[1024,153]{0,1:T(8,128)(2,1)}, u32[]{:S(2)}) copy-start(bf16[1024,153]{0,1:T(8,128)(2,1)} %param.20) | copy-start | bytes 940036
  21.7 6.0 %collective-permute-start.10 = (bf16[153,128]{1,0:T(8,128)(2,1)S(1)}, bf16[153,128]{1,0:T(8,128)(2,1)S(1)}, u32[]{:S(2)}, u32[]{:S(2)}) collective-permute-start(bf16[153,128]{1,0:T(8,128)(2,1)S(1)} %get-tuple-element.69), channel_id=1, source_target_pairs={{0,24},{8,16},{16,8},{24,0},{1,25},{9,17},{17,9},{25,1},{2,26},{10... | collective-permute-start | bytes 117512 | tf_op jit(solution)/shard_map/ppermute | solution.py:403
  24.2 4.9 %collective-permute-start.11 = (bf16[153,128]{1,0:T(8,128)(2,1)S(1)}, bf16[153,128]{1,0:T(8,128)(2,1)S(1)}, u32[]{:S(2)}, u32[]{:S(2)}) collective-permute-start(bf16[153,128]{1,0:T(8,128)(2,1)S(1)} %get-tuple-element.70), channel_id=1, source_target_pairs={{0,16},{8,24},{16,0},{24,8},{1,17},{9,25},{17,1},{25,9},{2,18},{10... | collective-permute-start | bytes 117512 | tf_op jit(solution)/shard_map/ppermute | solution.py:403
  24.2 4.9 %collective-permute-start.12 = (bf16[153,128]{1,0:T(8,128)(2,1)S(1)}, bf16[153,128]{1,0:T(8,128)(2,1)S(1)}, u32[]{:S(2)}, u32[]{:S(2)}) collective-permute-start(bf16[153,128]{1,0:T(8,128)(2,1)S(1)} %get-tuple-element.71), channel_id=1, source_target_pairs={{0,8},{8,0},{16,24},{24,16},{1,9},{9,1},{17,25},{25,17},{2,10},{10... | collective-permute-start | bytes 117512 | tf_op jit(solution)/shard_map/ppermute | solution.py:403
  29.3 1.3 %collective-permute-start.13 = (bf16[4,16,256]{2,1,0:T(8,128)(2,1)S(1)}, bf16[4,16,256]{2,1,0:T(8,128)(2,1)S(1)}, u32[]{:S(2)}, u32[]{:S(2)}) collective-permute-start(bf16[4,16,256]{2,1,0:T(8,128)(2,1)S(1)} %get-tuple-element.73), channel_id=1, source_target_pairs={{0,1},{1,0},{2,3},{3,2},{4,5},{5,4},{6,7},{7,6},{8,9},{9,8},{10,11... | collective-permute-start | bytes 98312 | tf_op jit(solution)/shard_map/ppermute | solution.py:408
  30.6 4.6 %collective-permute-start.14 = (bf16[2,16,256]{2,1,0:T(8,128)(2,1)S(1)}, bf16[2,16,256]{2,1,0:T(8,128)(2,1)S(1)}, u32[]{:S(2)}, u32[]{:S(2)}) collective-permute-start(bf16[2,16,256]{2,1,0:T(8,128)(2,1)S(1)} %get-tuple-element.75), channel_id=1, source_target_pairs={{0,6},{1,7},{2,4},{3,5},{4,2},{5,3},{6,0},{7,1},{8,14},{9,15},{10,... | collective-permute-start | bytes 49160 | tf_op jit(solution)/shard_map/ppermute | solution.py:412
  33.1 3.7 %collective-permute-start.15 = (bf16[2,16,256]{2,1,0:T(8,128)(2,1)S(1)}, bf16[2,16,256]{2,1,0:T(8,128)(2,1)S(1)}, u32[]{:S(2)}, u32[]{:S(2)}) collective-permute-start(bf16[2,16,256]{2,1,0:T(8,128)(2,1)S(1)} %get-tuple-element.76), channel_id=1, source_target_pairs={{0,4},{1,5},{2,6},{3,7},{4,0},{5,1},{6,2},{7,3},{8,12},{9,13},{10,... | collective-permute-start | bytes 49160 | tf_op jit(solution)/shard_map/ppermute | solution.py:412
  33.6 3.7 %collective-permute-start.16 = (bf16[2,16,256]{2,1,0:T(8,128)(2,1)S(1)}, bf16[2,16,256]{2,1,0:T(8,128)(2,1)S(1)}, u32[]{:S(2)}, u32[]{:S(2)}) collective-permute-start(bf16[2,16,256]{2,1,0:T(8,128)(2,1)S(1)} %get-tuple-element.77), channel_id=1, source_target_pairs={{0,2},{1,3},{2,0},{3,1},{4,6},{5,7},{6,4},{7,5},{8,10},{9,11},{10,... | collective-permute-start | bytes 49160 | tf_op jit(solution)/shard_map/ppermute | solution.py:412

commit v24 on v19

--- a/solution.py
+++ b/solution.py
@@ -64,12 +64,24 @@
     return me ^ step if groups & (groups - 1) == 0 else (me + groups - step) % groups
 
 
+def gray(a):
+    return a ^ (a >> 1)
+
+
+def swapped(j):
+    return (j >> 1) | ((j & 1) << 1)
+
+
 def step_to(a, b, count):
+    if count == 4:
+        return swapped((gray(b) + count - gray(a)) % count)
     step = a ^ b if count & (count - 1) == 0 else (b + count - a) % count
     return (count - step) % count
 
 
 def next_to(a, j, count):
+    if count == 4:
+        return gray((gray(a) + swapped(j)) % count)
     step = step_of(count, j)
     return a ^ step if count & (count - 1) == 0 else (a + step) % count
 

time: 38.1 us -> 38.3 us (level)
    ppermute x6, starting transfers between devices: 7.8 us -> 8.39 us  [to_chips(): lax.ppermute(blocks[j], 'dom', [(d, next_to(d // 2, j, chips) * 2 + d % 2...]
    ppermute x9, starting transfers between devices: 13.5 us -> 13.1 us  [shift(): lax.ppermute(block, 'feat', [(i, ahead(i, groups, k, near)) for i in rang...]
where the time goes in v24:
time: 38.3 us; the launch traced here: 38.1 us
  starting transfers between devices  22.1 us (58%)
  Pallas kernels  8.89 us (23%)
  waiting for transfers between devices  6.32 us (17%)
  between operations  0.8 us (2%)
    ppermute x9, starting transfers between devices, shift(): lax.ppermute(block, 'feat', [(i, ahead(i, groups, k, near)) for i in rang...  13.1 us
    pallas_call x16, Pallas kernels, placed(): run(*(pltpu.with_memory_space_constraint(value, pltpu.HBM) if spec is HB...  8.89 us
    ppermute x6, starting transfers between devices, to_chips(): lax.ppermute(blocks[j], 'dom', [(d, next_to(d // 2, j, chips) * 2 + d % 2...  8.39 us
    ppermute x9, waiting for transfers between devices, shift(): lax.ppermute(block, 'feat', [(i, ahead(i, groups, k, near)) for i in rang...  3.27 us
    ppermute x6, waiting for transfers between devices, to_chips(): lax.ppermute(blocks[j], 'dom', [(d, next_to(d // 2, j, chips) * 2 + d % 2...  1.85 us
    ppermute x2, waiting for transfers between devices, to_mate(): return lax.ppermute(value, 'dom', [(d, d ^ 1) for d in range(parts)])  1.2 us
  transfers between devices with their start and end apart: 17, of which 8 were waited for; matrix products, arithmetic and copies ran while one was open for 0% of the time, Pallas kernels for 16%

profile of v24, /device:TPU:0, one launch (start us, length us, event | category | flops | bytes accessed | tf_op | source)
XLA Modules:
  0.0 38.1 jit_solution(6216777314375003397)
XLA Ops:
  0.6 1.3 %shard_map.122 = (bf16[4,64,256]{2,1,0:T(8,128)(2,1)S(1)}, bf16[256,512]{1,0:T(8,128)(2,1)S(1)}, s32[8,4,16]{2,1,0:T(4,128)S(1)}, bf16[12,128,128]{2,1,0:T(8,128...) custom-call(s32[1]{0:T(128)} %bitcast.4.part_ref, ...), custom_call_target="tpu_custom_call" | custom-call | flops 100663296 | bytes 1048576 | tf_op jit(solution)/shard_map/pallas_call | solution.py:33
  1.9 0.5 %collective-permute-start = (bf16[4,64,256]{2,1,0:T(8,128)(2,1)S(1)}, bf16[4,64,256]{2,1,0:T(8,128)(2,1)S(1)}, u32[]{:S(2)}, u32[]{:S(2)}) collective-permute-start(bf16[4,64,256]{2,1,0:T(8,128)(2,1)S(1)} %get-tuple-element.49), channel_id=1, source_target_pairs={{0,1},{1,0},{2,3},{3,2},{4,5},{5,4},{6,7},{7,6},{8,9},{9,8},{10,11... | collective-permute-start | bytes 393224 | tf_op jit(solution)/shard_map/ppermute | solution.py:400
  2.5 1.2 %shard_map.123 = (f32[4,208,128]{2,1,0:T(8,128)S(1)}, bf16[4,8,16,128]{3,2,1,0:T(8,128)(2,1)S(1)}, bf16[128,512]{1,0:T(8,128)(2,1)S(1)}, bf16[4,64,256]{2,1,0:T(...) custom-call(s32[1]{0:T(128)} %bitcast.me_ref.rest_0_, ...), custom_call_target="tpu_custom_call" | custom-call | flops 100663296 | bytes 1048576 | tf_op jit(solution)/shard_map/pallas_call | solution.py:33
  3.6 0.0 collective-permute-done.got_ref
  3.7 3.7 %collective-permute-start.4 = (bf16[2,64,256]{2,1,0:T(8,128)(2,1)S(1)}, bf16[2,64,256]{2,1,0:T(8,128)(2,1)S(1)}, u32[]{:S(2)}, u32[]{:S(2)}) collective-permute-start(bf16[2,64,256]{2,1,0:T(8,128)(2,1)S(1)} %get-tuple-element.59), channel_id=1, source_target_pairs={{0,6},{1,7},{2,4},{3,5},{4,2},{5,3},{6,0},{7,1},{8,14},{9,15},{10,... | collective-permute-start | bytes 196616 | tf_op jit(solution)/shard_map/ppermute | solution.py:404
  7.4 0.5 %collective-permute-start.5 = (bf16[2,64,256]{2,1,0:T(8,128)(2,1)S(1)}, bf16[2,64,256]{2,1,0:T(8,128)(2,1)S(1)}, u32[]{:S(2)}, u32[]{:S(2)}) collective-permute-start(bf16[2,64,256]{2,1,0:T(8,128)(2,1)S(1)} %get-tuple-element.60), channel_id=1, source_target_pairs={{0,2},{1,3},{2,6},{3,7},{4,0},{5,1},{6,4},{7,5},{8,10},{9,11},{10,... | collective-permute-start | bytes 196616 | tf_op jit(solution)/shard_map/ppermute | solution.py:404
  7.9 1.5 %collective-permute-start.6 = (bf16[2,64,256]{2,1,0:T(8,128)(2,1)S(1)}, bf16[2,64,256]{2,1,0:T(8,128)(2,1)S(1)}, u32[]{:S(2)}, u32[]{:S(2)}) collective-permute-start(bf16[2,64,256]{2,1,0:T(8,128)(2,1)S(1)} %get-tuple-element.61), channel_id=1, source_target_pairs={{0,4},{1,5},{2,0},{3,1},{4,6},{5,7},{6,2},{7,3},{8,12},{9,13},{10,... | collective-permute-start | bytes 196616 | tf_op jit(solution)/shard_map/ppermute | solution.py:404
  9.4 2.6 %collective-permute-start.1 = (bf16[192,128]{1,0:T(8,128)(2,1)S(1)}, bf16[192,128]{1,0:T(8,128)(2,1)S(1)}, u32[]{:S(2)}, u32[]{:S(2)}) collective-permute-start(bf16[192,128]{1,0:T(8,128)(2,1)S(1)} %get-tuple-element.53), channel_id=1, source_target_pairs={{0,16},{8,24},{16,0},{24,8},{1,17},{9,25},{17,1},{25,9},{2,18},{10... | collective-permute-start | bytes 147464 | tf_op jit(solution)/shard_map/ppermute | solution.py:395
  12.0 1.4 %collective-permute-start.2 = (bf16[192,128]{1,0:T(8,128)(2,1)S(1)}, bf16[192,128]{1,0:T(8,128)(2,1)S(1)}, u32[]{:S(2)}, u32[]{:S(2)}) collective-permute-start(bf16[192,128]{1,0:T(8,128)(2,1)S(1)} %get-tuple-element.54), channel_id=1, source_target_pairs={{0,24},{8,16},{16,8},{24,0},{1,25},{9,17},{17,9},{25,1},{2,26},{10... | collective-permute-start | bytes 147464 | tf_op jit(solution)/shard_map/ppermute | solution.py:395
  13.3 0.0 collective-permute-done.4.rest_4_.rest_1_
  13.3 0.2 collective-permute-start.3
  13.5 0.0 collective-permute-done.5.rest_5_.rest_2_
  13.6 0.0 collective-permute-done.6.rest_6_.rest_3_
  13.6 0.2 shard_map.127
  13.8 3.0 %collective-permute-start.7 = (bf16[192,128]{1,0:T(8,128)(2,1)S(1)}, bf16[192,128]{1,0:T(8,128)(2,1)S(1)}, u32[]{:S(2)}, u32[]{:S(2)}) collective-permute-start(bf16[192,128]{1,0:T(8,128)(2,1)S(1)} %get-tuple-element.62), channel_id=1, source_target_pairs={{0,24},{8,16},{16,8},{24,0},{1,25},{9,17},{17,9},{25,1},{2,26},{10... | collective-permute-start | bytes 147464 | tf_op jit(solution)/shard_map/ppermute | solution.py:395
  16.8 0.3 collective-permute-start.8
  17.1 0.0 collective-permute-done.1.rest_0_
  17.1 1.1 %collective-permute-start.9 = (bf16[192,128]{1,0:T(8,128)(2,1)S(1)}, bf16[192,128]{1,0:T(8,128)(2,1)S(1)}, u32[]{:S(2)}, u32[]{:S(2)}) collective-permute-start(bf16[192,128]{1,0:T(8,128)(2,1)S(1)} %get-tuple-element.64), channel_id=1, source_target_pairs={{0,8},{8,0},{16,24},{24,16},{1,9},{9,1},{17,25},{25,17},{2,10},{10... | collective-permute-start | bytes 147464 | tf_op jit(solution)/shard_map/ppermute | solution.py:395
  18.3 0.2 collective-permute-done.2.rest_1_
  18.4 0.1 collective-permute-done.3.rest_2_
  18.5 1.8 %shard_map.125.after.own_ref = f32[128,1024]{1,0:T(8,128)S(1)} custom-call(s32[1]{0:T(128)} %bitcast.me_ref.rest_0_, bf16[192,512]{1,0:T(8,128)(2,1)} %bitcast.22, bf16[768,1024]{1,0:T(8,128)(2,1)} %weight_hbm.1, bf16[192,128]{1,0:T(8,128)(2,1)S(1)} %collective-permute-done.1.rest_0_, bf16[192,128]{1,0:T(8,128)(2,1)S(1)} %collective-permute-done.2.rest_1_, ...), custom_call_target="tpu_custom_call" | custom-call | flops 201326592 | bytes 2097152 | tf_op jit(solution)/shard_map/pallas_call | solution.py:33
  20.3 0.2 shard_map.126.rest_0_
  20.5 0.0 collective-permute-done.7.rest_1_
  20.5 0.3 shard_map.128.early_ref
  20.9 1.3 %collective-permute-done.8.rest_0_ = bf16[192,128]{1,0:T(8,128)(2,1)S(1)} collective-permute-done((bf16[192,128]{1,0:T(8,128)(2,1)S(1)}, bf16[192,128]{1,0:T(8,128)(2,1)S(1)}, u32[]{:S(2)}, u32[]{:S(2)}) %collective-permute-start.8) | collective-permute-done | bytes 49184 | tf_op jit(solution)/shard_map/ppermute | solution.py:395
  22.2 0.0 collective-permute-done.9.rest_1_
  22.2 0.5 %shard_map.129 = (bf16[128,1024]{1,0:T(8,128)(2,1)S(1)}, bf16[153,128]{1,0:T(8,128)(2,1)S(1)}, bf16[153,128]{1,0:T(8,128)(2,1)S(1)}, bf16[153,128]{1,0:T(8,128)(2,1)S(1)}, bf16[153,128]{1,0:T(8,128)(2,1)S(1)}) custom-call(s32[1]{0:T(128)} %bitcast.me_ref.rest_0_, bf16[768,1024]{1,0:T(8,128)(2,1)S(1)} %copy-done, bf16[153,1024]{1,0:T(8,128)(2,1)S(1)} %bitcast.20, ...), custom_call_target="tpu_custom_call" | custom-call | flops 100663296 | bytes 2097152 | tf_op jit(solution)/shard_map/pallas_call | solution.py:33
  22.8 2.4 %collective-permute-start.10 = (bf16[153,128]{1,0:T(8,128)(2,1)S(1)}, bf16[153,128]{1,0:T(8,128)(2,1)S(1)}, u32[]{:S(2)}, u32[]{:S(2)}) collective-permute-start(bf16[153,128]{1,0:T(8,128)(2,1)S(1)} %get-tuple-element.69), channel_id=1, source_target_pairs={{0,24},{8,16},{16,8},{24,0},{1,25},{9,17},{17,9},{25,1},{2,26},{10... | collective-permute-start | bytes 117512 | tf_op jit(solution)/shard_map/ppermute | solution.py:395
  25.1 0.0 collective-permute-start.11
  25.1 2.1 %collective-permute-start.12 = (bf16[153,128]{1,0:T(8,128)(2,1)S(1)}, bf16[153,128]{1,0:T(8,128)(2,1)S(1)}, u32[]{:S(2)}, u32[]{:S(2)}) collective-permute-start(bf16[153,128]{1,0:T(8,128)(2,1)S(1)} %get-tuple-element.71), channel_id=1, source_target_pairs={{0,8},{8,0},{16,24},{24,16},{1,9},{9,1},{17,25},{25,17},{2,10},{10... | collective-permute-start | bytes 117512 | tf_op jit(solution)/shard_map/ppermute | solution.py:395
  27.2 0.9 %shard_map.132.hits_ref.after = bf16[128,512]{1,0:T(8,128)(2,1)S(1)} custom-call(bf16[153,128]{1,0:T(8,128)(2,1)S(1)} %get-tuple-element.68.rest_0_.after, s32[1]{0:T(128)} %bitcast.me_ref.rest_0_, s32[1]{0:T(128)} %bitcast.4.part_ref, s32[8,4,16]{2,1,0:T(4,128)} %bitcast.26), custom_call_target="tpu_custom_call" | custom-call | bytes 524288 | tf_op jit(solution)/shard_map/pallas_call | solution.py:33
  28.1 0.7 %collective-permute-done.10.rest_1_ = bf16[153,128]{1,0:T(8,128)(2,1)S(1)} collective-permute-done((bf16[153,128]{1,0:T(8,128)(2,1)S(1)}, bf16[153,128]{1,0:T(8,128)(2,1)S(1)}, u32[]{:S(2)}, u32[]{:S(2)}) %collective-permute-start.10) | collective-permute-done | bytes 39200 | tf_op jit(solution)/shard_map/ppermute | solution.py:395
  28.8 0.2 shard_map.133.early_ref
  29.0 1.0 %collective-permute-done.11.rest_2_.rest_0_ = bf16[153,128]{1,0:T(8,128)(2,1)S(1)} collective-permute-done((bf16[153,128]{1,0:T(8,128)(2,1)S(1)}, bf16[153,128]{1,0:T(8,128)(2,1)S(1)}, u32[]{:S(2)}, u32[]{:S(2)}) %collective-permute-start.11) | collective-permute-done | bytes 39200 | tf_op jit(solution)/shard_map/ppermute | solution.py:395
  30.0 0.0 collective-permute-done.12.rest_3_.rest_1_
  30.0 0.2 shard_map.134
  30.2 0.1 collective-permute-start.13
  30.3 1.2 %collective-permute-done.13.got_ref = bf16[4,16,256]{2,1,0:T(8,128)(2,1)S(1)} collective-permute-done((bf16[4,16,256]{2,1,0:T(8,128)(2,1)S(1)}, bf16[4,16,256]{2,1,0:T(8,128)(2,1)S(1)}, u32[]{:S(2)}, u32[]{:S(2)}) %collective-permute-start.13) | collective-permute-done | bytes 32800 | tf_op jit(solution)/shard_map/ppermute | solution.py:400
  31.5 0.7 %collective-permute-start.14 = (bf16[2,16,256]{2,1,0:T(8,128)(2,1)S(1)}, bf16[2,16,256]{2,1,0:T(8,128)(2,1)S(1)}, u32[]{:S(2)}, u32[]{:S(2)}) collective-permute-start(bf16[2,16,256]{2,1,0:T(8,128)(2,1)S(1)} %get-tuple-element.75), channel_id=1, source_target_pairs={{0,6},{1,7},{2,4},{3,5},{4,2},{5,3},{6,0},{7,1},{8,14},{9,15},{10,... | collective-permute-start | bytes 49160 | tf_op jit(solution)/shard_map/ppermute | solution.py:404
  32.2 1.3 %collective-permute-start.15 = (bf16[2,16,256]{2,1,0:T(8,128)(2,1)S(1)}, bf16[2,16,256]{2,1,0:T(8,128)(2,1)S(1)}, u32[]{:S(2)}, u32[]{:S(2)}) collective-permute-start(bf16[2,16,256]{2,1,0:T(8,128)(2,1)S(1)} %get-tuple-element.76), channel_id=1, source_target_pairs={{0,2},{1,3},{2,6},{3,7},{4,0},{5,1},{6,4},{7,5},{8,10},{9,11},{10,... | collective-permute-start | bytes 49160 | tf_op jit(solution)/shard_map/ppermute | solution.py:404
  33.5 0.7 %collective-permute-start.16 = (bf16[2,16,256]{2,1,0:T(8,128)(2,1)S(1)}, bf16[2,16,256]{2,1,0:T(8,128)(2,1)S(1)}, u32[]{:S(2)}, u32[]{:S(2)}) collective-permute-start(bf16[2,16,256]{2,1,0:T(8,128)(2,1)S(1)} %get-tuple-element.77), channel_id=1, source_target_pairs={{0,4},{1,5},{2,0},{3,1},{4,6},{5,7},{6,2},{7,3},{8,12},{9,13},{10,... | collective-permute-start | bytes 49160 | tf_op jit(solution)/shard_map/ppermute | solution.py:404
  34.2 0.7 %shard_map.130 = (f32[153,128]{1,0:T(8,128)S(1)}, bf16[128,1024]{1,0:T(8,128)(2,1)}) custom-call(bf16[128,1024]{1,0:T(8,128)(2,1)S(1)} %get-tuple-element.65.hidden_ref, bf16[153,1024]{1,0:T(8,128)(2,1)S(1)} %bitcast.19), custom_call_target="tpu_custom_call" | custom-call | flops 40108032 | bytes 1048576 | tf_op jit(solution)/shard_map/pallas_call | solution.py:33
  34.9 0.2 shard_map.131.near_ref
  35.2 1.0 %collective-permute-done.14.rest_1_ = bf16[2,16,256]{2,1,0:T(8,128)(2,1)S(1)} collective-permute-done((bf16[2,16,256]{2,1,0:T(8,128)(2,1)S(1)}, bf16[2,16,256]{2,1,0:T(8,128)(2,1)S(1)}, u32[]{:S(2)}, u32[]{:S(2)}) %collective-permute-start.14) | collective-permute-done | bytes 16416 | tf_op jit(solution)/shard_map/ppermute | solution.py:404
  36.2 0.2 shard_map.136.rest_0_
  36.4 0.0 collective-permute-done.15.rest_3_
  36.4 0.9 %collective-permute-done.16.rest_4_ = bf16[2,16,256]{2,1,0:T(8,128)(2,1)S(1)} collective-permute-done((bf16[2,16,256]{2,1,0:T(8,128)(2,1)S(1)}, bf16[2,16,256]{2,1,0:T(8,128)(2,1)S(1)}, u32[]{:S(2)}, u32[]{:S(2)}) %collective-permute-start.16) | collective-permute-done | bytes 16416 | tf_op jit(solution)/shard_map/ppermute | solution.py:404
  37.2 0.8 %shard_map.137 = f32[153,1,128]{2,1,0:T(1,128)} custom-call(s32[1]{0:T(128)} %bitcast.me_ref.rest_0_, f32[153,128]{1,0:T(8,128)S(1)} %shard_map.136.rest_0_, bf16[4,8,16,128]{3,2,1,0:T(8,128)(2,1)S(1)} %get-tuple-element.57.rest_2_.edges_ref.rest_1_, f32[4,208,128]{2,1,0:T(8,128)S(1)} %get-tuple-element.56.rest_1_.sums_ref.rest_2_, ...), custom_call_target="tpu_custom_call" | custom-call | flops 2506752 | bytes 524288 | tf_op jit(solution)/shard_map/pallas_call | solution.py:33
  (8 shorter events, 0.0 us)
Async XLA Ops:
  1.9 1.7 %collective-permute-start = (bf16[4,64,256]{2,1,0:T(8,128)(2,1)S(1)}, bf16[4,64,256]{2,1,0:T(8,128)(2,1)S(1)}, u32[]{:S(2)}, u32[]{:S(2)}) collective-permute-start(bf16[4,64,256]{2,1,0:T(8,128)(2,1)S(1)} %get-tuple-element.49), channel_id=1, source_target_pairs={{0,1},{1,0},{2,3},{3,2},{4,5},{5,4},{6,7},{7,6},{8,9},{9,8},{10,11... | collective-permute-start | bytes 393224 | tf_op jit(solution)/shard_map/ppermute | solution.py:400
  3.7 9.6 %collective-permute-start.4 = (bf16[2,64,256]{2,1,0:T(8,128)(2,1)S(1)}, bf16[2,64,256]{2,1,0:T(8,128)(2,1)S(1)}, u32[]{:S(2)}, u32[]{:S(2)}) collective-permute-start(bf16[2,64,256]{2,1,0:T(8,128)(2,1)S(1)} %get-tuple-element.59), channel_id=1, source_target_pairs={{0,6},{1,7},{2,4},{3,5},{4,2},{5,3},{6,0},{7,1},{8,14},{9,15},{10,... | collective-permute-start | bytes 196616 | tf_op jit(solution)/shard_map/ppermute | solution.py:404
  7.4 6.2 %collective-permute-start.5 = (bf16[2,64,256]{2,1,0:T(8,128)(2,1)S(1)}, bf16[2,64,256]{2,1,0:T(8,128)(2,1)S(1)}, u32[]{:S(2)}, u32[]{:S(2)}) collective-permute-start(bf16[2,64,256]{2,1,0:T(8,128)(2,1)S(1)} %get-tuple-element.60), channel_id=1, source_target_pairs={{0,2},{1,3},{2,6},{3,7},{4,0},{5,1},{6,4},{7,5},{8,10},{9,11},{10,... | collective-permute-start | bytes 196616 | tf_op jit(solution)/shard_map/ppermute | solution.py:404
  7.9 5.7 %collective-permute-start.6 = (bf16[2,64,256]{2,1,0:T(8,128)(2,1)S(1)}, bf16[2,64,256]{2,1,0:T(8,128)(2,1)S(1)}, u32[]{:S(2)}, u32[]{:S(2)}) collective-permute-start(bf16[2,64,256]{2,1,0:T(8,128)(2,1)S(1)} %get-tuple-element.61), channel_id=1, source_target_pairs={{0,4},{1,5},{2,0},{3,1},{4,6},{5,7},{6,2},{7,3},{8,12},{9,13},{10,... | collective-permute-start | bytes 196616 | tf_op jit(solution)/shard_map/ppermute | solution.py:404
  9.4 7.8 %collective-permute-start.1 = (bf16[192,128]{1,0:T(8,128)(2,1)S(1)}, bf16[192,128]{1,0:T(8,128)(2,1)S(1)}, u32[]{:S(2)}, u32[]{:S(2)}) collective-permute-start(bf16[192,128]{1,0:T(8,128)(2,1)S(1)} %get-tuple-element.53), channel_id=1, source_target_pairs={{0,16},{8,24},{16,0},{24,8},{1,17},{9,25},{17,1},{25,9},{2,18},{10... | collective-permute-start | bytes 147464 | tf_op jit(solution)/shard_map/ppermute | solution.py:395
  12.0 6.5 %collective-permute-start.2 = (bf16[192,128]{1,0:T(8,128)(2,1)S(1)}, bf16[192,128]{1,0:T(8,128)(2,1)S(1)}, u32[]{:S(2)}, u32[]{:S(2)}) collective-permute-start(bf16[192,128]{1,0:T(8,128)(2,1)S(1)} %get-tuple-element.54), channel_id=1, source_target_pairs={{0,24},{8,16},{16,8},{24,0},{1,25},{9,17},{17,9},{25,1},{2,26},{10... | collective-permute-start | bytes 147464 | tf_op jit(solution)/shard_map/ppermute | solution.py:395
  13.3 5.2 %collective-permute-start.3 = (bf16[192,128]{1,0:T(8,128)(2,1)S(1)}, bf16[192,128]{1,0:T(8,128)(2,1)S(1)}, u32[]{:S(2)}, u32[]{:S(2)}) collective-permute-start(bf16[192,128]{1,0:T(8,128)(2,1)S(1)} %get-tuple-element.55), channel_id=1, source_target_pairs={{0,8},{8,0},{16,24},{24,16},{1,9},{9,1},{17,25},{25,17},{2,10},{10... | collective-permute-start | bytes 147464 | tf_op jit(solution)/shard_map/ppermute | solution.py:395
  13.8 6.7 %collective-permute-start.7 = (bf16[192,128]{1,0:T(8,128)(2,1)S(1)}, bf16[192,128]{1,0:T(8,128)(2,1)S(1)}, u32[]{:S(2)}, u32[]{:S(2)}) collective-permute-start(bf16[192,128]{1,0:T(8,128)(2,1)S(1)} %get-tuple-element.62), channel_id=1, source_target_pairs={{0,24},{8,16},{16,8},{24,0},{1,25},{9,17},{17,9},{25,1},{2,26},{10... | collective-permute-start | bytes 147464 | tf_op jit(solution)/shard_map/ppermute | solution.py:395
  16.8 5.4 %collective-permute-start.8 = (bf16[192,128]{1,0:T(8,128)(2,1)S(1)}, bf16[192,128]{1,0:T(8,128)(2,1)S(1)}, u32[]{:S(2)}, u32[]{:S(2)}) collective-permute-start(bf16[192,128]{1,0:T(8,128)(2,1)S(1)} %get-tuple-element.63), channel_id=1, source_target_pairs={{0,16},{8,24},{16,0},{24,8},{1,17},{9,25},{17,1},{25,9},{2,18},{10... | collective-permute-start | bytes 147464 | tf_op jit(solution)/shard_map/ppermute | solution.py:395
  17.1 3.4 %copy-start = (bf16[768,1024]{1,0:T(8,128)(2,1)S(1)}, bf16[768,1024]{1,0:T(8,128)(2,1)}, u32[]{:S(2)}) copy-start(bf16[768,1024]{1,0:T(8,128)(2,1)} %weight_ref.3) | copy-start | bytes 4718596
  17.1 5.1 %collective-permute-start.9 = (bf16[192,128]{1,0:T(8,128)(2,1)S(1)}, bf16[192,128]{1,0:T(8,128)(2,1)S(1)}, u32[]{:S(2)}, u32[]{:S(2)}) collective-permute-start(bf16[192,128]{1,0:T(8,128)(2,1)S(1)} %get-tuple-element.64), channel_id=1, source_target_pairs={{0,8},{8,0},{16,24},{24,16},{1,9},{9,1},{17,25},{25,17},{2,10},{10... | collective-permute-start | bytes 147464 | tf_op jit(solution)/shard_map/ppermute | solution.py:395
  20.5 1.7 %copy-start.2 = (bf16[1024,153]{0,1:T(8,128)(2,1)S(1)}, bf16[1024,153]{0,1:T(8,128)(2,1)}, u32[]{:S(2)}) copy-start(bf16[1024,153]{0,1:T(8,128)(2,1)} %param.21) | copy-start | bytes 940036
  22.2 12.0 %copy-start.1 = (bf16[1024,153]{0,1:T(8,128)(2,1)S(1)}, bf16[1024,153]{0,1:T(8,128)(2,1)}, u32[]{:S(2)}) copy-start(bf16[1024,153]{0,1:T(8,128)(2,1)} %param.20) | copy-start | bytes 940036
  22.8 6.1 %collective-permute-start.10 = (bf16[153,128]{1,0:T(8,128)(2,1)S(1)}, bf16[153,128]{1,0:T(8,128)(2,1)S(1)}, u32[]{:S(2)}, u32[]{:S(2)}) collective-permute-start(bf16[153,128]{1,0:T(8,128)(2,1)S(1)} %get-tuple-element.69), channel_id=1, source_target_pairs={{0,24},{8,16},{16,8},{24,0},{1,25},{9,17},{17,9},{25,1},{2,26},{10... | collective-permute-start | bytes 117512 | tf_op jit(solution)/shard_map/ppermute | solution.py:395
  25.1 4.9 %collective-permute-start.11 = (bf16[153,128]{1,0:T(8,128)(2,1)S(1)}, bf16[153,128]{1,0:T(8,128)(2,1)S(1)}, u32[]{:S(2)}, u32[]{:S(2)}) collective-permute-start(bf16[153,128]{1,0:T(8,128)(2,1)S(1)} %get-tuple-element.70), channel_id=1, source_target_pairs={{0,16},{8,24},{16,0},{24,8},{1,17},{9,25},{17,1},{25,9},{2,18},{10... | collective-permute-start | bytes 117512 | tf_op jit(solution)/shard_map/ppermute | solution.py:395
  25.1 4.9 %collective-permute-start.12 = (bf16[153,128]{1,0:T(8,128)(2,1)S(1)}, bf16[153,128]{1,0:T(8,128)(2,1)S(1)}, u32[]{:S(2)}, u32[]{:S(2)}) collective-permute-start(bf16[153,128]{1,0:T(8,128)(2,1)S(1)} %get-tuple-element.71), channel_id=1, source_target_pairs={{0,8},{8,0},{16,24},{24,16},{1,9},{9,1},{17,25},{25,17},{2,10},{10... | collective-permute-start | bytes 117512 | tf_op jit(solution)/shard_map/ppermute | solution.py:395
  30.2 1.3 %collective-permute-start.13 = (bf16[4,16,256]{2,1,0:T(8,128)(2,1)S(1)}, bf16[4,16,256]{2,1,0:T(8,128)(2,1)S(1)}, u32[]{:S(2)}, u32[]{:S(2)}) collective-permute-start(bf16[4,16,256]{2,1,0:T(8,128)(2,1)S(1)} %get-tuple-element.73), channel_id=1, source_target_pairs={{0,1},{1,0},{2,3},{3,2},{4,5},{5,4},{6,7},{7,6},{8,9},{9,8},{10,11... | collective-permute-start | bytes 98312 | tf_op jit(solution)/shard_map/ppermute | solution.py:400
  31.5 4.6 %collective-permute-start.14 = (bf16[2,16,256]{2,1,0:T(8,128)(2,1)S(1)}, bf16[2,16,256]{2,1,0:T(8,128)(2,1)S(1)}, u32[]{:S(2)}, u32[]{:S(2)}) collective-permute-start(bf16[2,16,256]{2,1,0:T(8,128)(2,1)S(1)} %get-tuple-element.75), channel_id=1, source_target_pairs={{0,6},{1,7},{2,4},{3,5},{4,2},{5,3},{6,0},{7,1},{8,14},{9,15},{10,... | collective-permute-start | bytes 49160 | tf_op jit(solution)/shard_map/ppermute | solution.py:404
  32.2 4.2 %collective-permute-start.15 = (bf16[2,16,256]{2,1,0:T(8,128)(2,1)S(1)}, bf16[2,16,256]{2,1,0:T(8,128)(2,1)S(1)}, u32[]{:S(2)}, u32[]{:S(2)}) collective-permute-start(bf16[2,16,256]{2,1,0:T(8,128)(2,1)S(1)} %get-tuple-element.76), channel_id=1, source_target_pairs={{0,2},{1,3},{2,6},{3,7},{4,0},{5,1},{6,4},{7,5},{8,10},{9,11},{10,... | collective-permute-start | bytes 49160 | tf_op jit(solution)/shard_map/ppermute | solution.py:404
  33.5 3.7 %collective-permute-start.16 = (bf16[2,16,256]{2,1,0:T(8,128)(2,1)S(1)}, bf16[2,16,256]{2,1,0:T(8,128)(2,1)S(1)}, u32[]{:S(2)}, u32[]{:S(2)}) collective-permute-start(bf16[2,16,256]{2,1,0:T(8,128)(2,1)S(1)} %get-tuple-element.77), channel_id=1, source_target_pairs={{0,4},{1,5},{2,0},{3,1},{4,6},{5,7},{6,2},{7,3},{8,12},{9,13},{10,... | collective-permute-start | bytes 49160 | tf_op jit(solution)/shard_map/ppermute | solution.py:404

commit v25 on v24

--- a/solution.py
+++ b/solution.py
@@ -72,18 +72,24 @@
     return (j >> 1) | ((j & 1) << 1)
 
 
-def step_to(a, b, count):
-    if count == 4:
+def step_to(a, b, count, square=False):
+    if square and count == 4:
         return swapped((gray(b) + count - gray(a)) % count)
     step = a ^ b if count & (count - 1) == 0 else (b + count - a) % count
     return (count - step) % count
 
 
-def next_to(a, j, count):
-    if count == 4:
+def next_to(a, j, count, square=False):
+    if square and count == 4:
         return gray((gray(a) + swapped(j)) % count)
     step = step_of(count, j)
     return a ^ step if count & (count - 1) == 0 else (a + step) % count
+
+
+def pair_at(chip, j, count):
+    if count == 4:
+        return step_to(gray((gray(chip) + count - swapped(j)) % count), chip, count)
+    return j
 
 
 def fetch(sems, *pairs):
@@ -223,7 +229,7 @@
     picks = jnp.sum(jnp.where(mine, sources_ref[...], 0), axis=1).T
     lane = lax.broadcasted_iota(jnp.int32, (slots, hits_ref.shape[1]), 1)
     for d in range(parts):
-        to = ((d % 2) ^ core) * chips + step_to(chip, d // 2, chips)
+        to = ((d % 2) ^ core) * chips + step_to(chip, d // 2, chips, True)
         hits_ref[pl.ds(pl.multiple_of(to * slots, slots), slots), :] = jnp.where(
             picks[:, d : d + 1] == lane, 1.0, 0.0
         ).astype(bf16)
@@ -345,20 +351,22 @@
     out_ref[...] = own_ref[...] + total / sums_ref[me, width : width + 1, :]
 
 
-def last_kernel(first, me_ref, near_ref, edges_ref, sums_ref, *rest):
+def last_kernel(first, part_ref, me_ref, near_ref, edges_ref, sums_ref, *rest):
     arrived, out_ref = rest[:-1], rest[-1]
-    _, _, slots, rows = edges_ref.shape
+    _, parts, slots, rows = edges_ref.shape
+    chip = part_ref[0] // 2
     me, width = me_ref[0], sums_ref.shape[1] - EXTRA
     count = 2 * len(arrived)
     arrived = jnp.concatenate([x[...].reshape(2 * slots, -1) for x in arrived], axis=0)
-    edges = edges_ref[me, 2 * first : 2 * first + count].reshape(count * slots, rows)
+    spans = [pl.ds(2 * pair_at(chip, first + i, parts // 2), 2) for i in range(count // 2)]
+    edges = jnp.concatenate([edges_ref[me, x].reshape(2 * slots, rows) for x in spans], axis=0)
     far = dot(arrived, edges, FIRST)[: near_ref.shape[0]]
     out_ref[...] = near_ref[...] + far / sums_ref[me, width : width + 1, :]
 
 
-def scores_kernel(first, me_ref, *rest):
+def scores_kernel(first, part_ref, me_ref, *rest):
     rest, (out_hbm, scores_ref, sem) = rest[:-3], rest[-3:]
-    last_kernel(first, me_ref, *rest, scores_ref)
+    last_kernel(first, part_ref, me_ref, *rest, scores_ref)
     copy = pltpu.make_async_copy(scores_ref, out_hbm.at[:, 0, :], sem)
     copy.start()
     copy.wait()
@@ -399,12 +407,12 @@
     def to_mate(value):
         return lax.ppermute(value, "dom", [(d, d ^ 1) for d in range(parts)])
 
-    def to_chips(blocks):
+    def to_chips(blocks, square=False):
         return [blocks[0]] + [
             lax.ppermute(
                 blocks[j],
                 "dom",
-                [(d, next_to(d // 2, j, chips) * 2 + d % 2) for d in range(parts)],
+                [(d, next_to(d // 2, j, chips, square) * 2 + d % 2) for d in range(parts)],
             )
             for j in range(1, chips)
         ]
@@ -537,7 +545,8 @@
     arrived = to_chips(
         call(pair_kernel, (shape(2, slots, whole_lanes(classes)),) * chips, [VM] * 3, (), 0, 1 << 19)(
             hits, mine, mate
-        )
+        ),
+        True,
     )
     own, hidden = call(
         own_kernel,
@@ -560,20 +569,20 @@
     near = call(
         functools.partial(last_kernel, 0),
         shape(classes, rows, dtype=f32),
-        [SM] + [VM] * (3 + half),
+        [SM, SM] + [VM] * (3 + half),
         (),
         rows * parts * slots * classes,
         1 << 18,
-    )(me, near, edges, sums, *arrived[:half])
+    )(part, me, near, edges, sums, *arrived[:half])
     logits = call(
         functools.partial(scores_kernel, half),
         shape(classes, 1, rows, dtype=f32),
-        [SM] + [VM] * (3 + chips - half),
+        [SM, SM] + [VM] * (3 + chips - half),
         [pltpu.VMEM((classes, rows), f32), pltpu.SemaphoreType.DMA],
         rows * parts * slots * classes,
         1 << 19,
         out_specs=HB,
-    )(me, near, edges, sums, *arrived[half:])
+    )(part, me, near, edges, sums, *arrived[half:])
     return hidden[None], logits.transpose(1, 0, 2)
 
 

time: 38.3 us -> 38.3 us (level)
  waiting for transfers between devices: 6.32 us -> 5.54 us
  starting transfers between devices: 22.1 us -> 22.8 us
    ppermute x6, waiting for transfers between devices: 1.85 us -> 1.1 us  [to_chips(): lax.ppermute(blocks[j], 'dom', [(d, next_to(d // 2, j, chips, square) * 2...]
    ppermute x9, starting transfers between devices: 13.1 us -> 13.5 us  [shift(): lax.ppermute(block, 'feat', [(i, ahead(i, groups, k, near)) for i in rang...]
    ppermute x6, starting transfers between devices: 8.39 us -> 8.78 us  [to_chips(): lax.ppermute(blocks[j], 'dom', [(d, next_to(d // 2, j, chips, square) * 2...]
  transfers between devices with their start and end apart: 17 -> 17, of which waited for: 8 -> 7; matrix products, arithmetic and copies ran while one was open for 0% -> 0% of each run, Pallas kernels for 16% -> 16%
where the time goes in v25:
time: 38.3 us; the launch traced here: 38.1 us
  starting transfers between devices  22.8 us (60%)
  Pallas kernels  8.87 us (23%)
  waiting for transfers between devices  5.54 us (14%)
  between operations  0.8 us (2%)
    ppermute x9, starting transfers between devices, shift(): lax.ppermute(block, 'feat', [(i, ahead(i, groups, k, near)) for i in rang...  13.5 us
    pallas_call x16, Pallas kernels, placed(): run(*(pltpu.with_memory_space_constraint(value, pltpu.HBM) if spec is HB...  8.87 us
    ppermute x6, starting transfers between devices, to_chips(): lax.ppermute(blocks[j], 'dom', [(d, next_to(d // 2, j, chips, square) * 2...  8.78 us
    ppermute x9, waiting for transfers between devices, shift(): lax.ppermute(block, 'feat', [(i, ahead(i, groups, k, near)) for i in rang...  3.25 us
    ppermute x2, waiting for transfers between devices, to_mate(): return lax.ppermute(value, 'dom', [(d, d ^ 1) for d in range(parts)])  1.2 us
    ppermute x6, waiting for transfers between devices, to_chips(): lax.ppermute(blocks[j], 'dom', [(d, next_to(d // 2, j, chips, square) * 2...  1.1 us
  transfers between devices with their start and end apart: 17, of which 7 were waited for; matrix products, arithmetic and copies ran while one was open for 0% of the time, Pallas kernels for 16%

profile of v25, /device:TPU:0, one launch (start us, length us, event | category | flops | bytes accessed | tf_op | source)
XLA Modules:
  0.0 38.1 jit_solution(970362824240875935)
XLA Ops:
  0.6 1.3 %shard_map.122 = (bf16[4,64,256]{2,1,0:T(8,128)(2,1)S(1)}, bf16[256,512]{1,0:T(8,128)(2,1)S(1)}, s32[8,4,16]{2,1,0:T(4,128)S(1)}, bf16[12,128,128]{2,1,0:T(8,128...) custom-call(s32[1]{0:T(128)} %bitcast.4.part_ref, ...), custom_call_target="tpu_custom_call" | custom-call | flops 100663296 | bytes 1048576 | tf_op jit(solution)/shard_map/pallas_call | solution.py:33
  1.9 0.5 %collective-permute-start = (bf16[4,64,256]{2,1,0:T(8,128)(2,1)S(1)}, bf16[4,64,256]{2,1,0:T(8,128)(2,1)S(1)}, u32[]{:S(2)}, u32[]{:S(2)}) collective-permute-start(bf16[4,64,256]{2,1,0:T(8,128)(2,1)S(1)} %get-tuple-element.49), channel_id=1, source_target_pairs={{0,1},{1,0},{2,3},{3,2},{4,5},{5,4},{6,7},{7,6},{8,9},{9,8},{10,11... | collective-permute-start | bytes 393224 | tf_op jit(solution)/shard_map/ppermute | solution.py:408
  2.5 1.2 %shard_map.123 = (f32[4,208,128]{2,1,0:T(8,128)S(1)}, bf16[4,8,16,128]{3,2,1,0:T(8,128)(2,1)S(1)}, bf16[128,512]{1,0:T(8,128)(2,1)S(1)}, bf16[4,64,256]{2,1,0:T(...) custom-call(s32[1]{0:T(128)} %bitcast.me_ref.rest_0_, ...), custom_call_target="tpu_custom_call" | custom-call | flops 100663296 | bytes 1048576 | tf_op jit(solution)/shard_map/pallas_call | solution.py:33
  3.6 0.0 collective-permute-done.got_ref
  3.7 3.7 %collective-permute-start.4 = (bf16[2,64,256]{2,1,0:T(8,128)(2,1)S(1)}, bf16[2,64,256]{2,1,0:T(8,128)(2,1)S(1)}, u32[]{:S(2)}, u32[]{:S(2)}) collective-permute-start(bf16[2,64,256]{2,1,0:T(8,128)(2,1)S(1)} %get-tuple-element.59), channel_id=1, source_target_pairs={{0,6},{1,7},{2,4},{3,5},{4,2},{5,3},{6,0},{7,1},{8,14},{9,15},{10,... | collective-permute-start | bytes 196616 | tf_op jit(solution)/shard_map/ppermute | solution.py:412
  7.4 0.5 %collective-permute-start.5 = (bf16[2,64,256]{2,1,0:T(8,128)(2,1)S(1)}, bf16[2,64,256]{2,1,0:T(8,128)(2,1)S(1)}, u32[]{:S(2)}, u32[]{:S(2)}) collective-permute-start(bf16[2,64,256]{2,1,0:T(8,128)(2,1)S(1)} %get-tuple-element.60), channel_id=1, source_target_pairs={{0,4},{1,5},{2,6},{3,7},{4,0},{5,1},{6,2},{7,3},{8,12},{9,13},{10,... | collective-permute-start | bytes 196616 | tf_op jit(solution)/shard_map/ppermute | solution.py:412
  7.9 0.1 collective-permute-start.6
  8.0 3.0 %collective-permute-start.1 = (bf16[192,128]{1,0:T(8,128)(2,1)S(1)}, bf16[192,128]{1,0:T(8,128)(2,1)S(1)}, u32[]{:S(2)}, u32[]{:S(2)}) collective-permute-start(bf16[192,128]{1,0:T(8,128)(2,1)S(1)} %get-tuple-element.53), channel_id=1, source_target_pairs={{0,16},{8,24},{16,0},{24,8},{1,17},{9,25},{17,1},{25,9},{2,18},{10... | collective-permute-start | bytes 147464 | tf_op jit(solution)/shard_map/ppermute | solution.py:403
  11.0 1.3 %collective-permute-start.2 = (bf16[192,128]{1,0:T(8,128)(2,1)S(1)}, bf16[192,128]{1,0:T(8,128)(2,1)S(1)}, u32[]{:S(2)}, u32[]{:S(2)}) collective-permute-start(bf16[192,128]{1,0:T(8,128)(2,1)S(1)} %get-tuple-element.54), channel_id=1, source_target_pairs={{0,24},{8,16},{16,8},{24,0},{1,25},{9,17},{17,9},{25,1},{2,26},{10... | collective-permute-start | bytes 147464 | tf_op jit(solution)/shard_map/ppermute | solution.py:403
  12.3 0.0 collective-permute-done.4.rest_4_.rest_1_
  12.3 0.2 collective-permute-start.3
  12.6 0.0 collective-permute-done.5.rest_5_.rest_2_
  12.6 0.0 collective-permute-done.6.rest_6_.rest_3_
  12.6 0.2 shard_map.127
  12.8 3.2 %collective-permute-start.7 = (bf16[192,128]{1,0:T(8,128)(2,1)S(1)}, bf16[192,128]{1,0:T(8,128)(2,1)S(1)}, u32[]{:S(2)}, u32[]{:S(2)}) collective-permute-start(bf16[192,128]{1,0:T(8,128)(2,1)S(1)} %get-tuple-element.62), channel_id=1, source_target_pairs={{0,24},{8,16},{16,8},{24,0},{1,25},{9,17},{17,9},{25,1},{2,26},{10... | collective-permute-start | bytes 147464 | tf_op jit(solution)/shard_map/ppermute | solution.py:403
  16.0 0.1 collective-permute-start.8
  16.1 0.0 collective-permute-done.1.rest_0_
  16.1 1.1 %collective-permute-start.9 = (bf16[192,128]{1,0:T(8,128)(2,1)S(1)}, bf16[192,128]{1,0:T(8,128)(2,1)S(1)}, u32[]{:S(2)}, u32[]{:S(2)}) collective-permute-start(bf16[192,128]{1,0:T(8,128)(2,1)S(1)} %get-tuple-element.64), channel_id=1, source_target_pairs={{0,8},{8,0},{16,24},{24,16},{1,9},{9,1},{17,25},{25,17},{2,10},{10... | collective-permute-start | bytes 147464 | tf_op jit(solution)/shard_map/ppermute | solution.py:403
  17.3 0.2 collective-permute-done.2.rest_1_
  17.4 0.0 collective-permute-done.3.rest_2_
  17.5 1.8 %shard_map.125.after.own_ref = f32[128,1024]{1,0:T(8,128)S(1)} custom-call(s32[1]{0:T(128)} %bitcast.me_ref.rest_0_, bf16[192,512]{1,0:T(8,128)(2,1)} %bitcast.22, bf16[768,1024]{1,0:T(8,128)(2,1)} %weight_hbm.1, bf16[192,128]{1,0:T(8,128)(2,1)S(1)} %collective-permute-done.1.rest_0_, bf16[192,128]{1,0:T(8,128)(2,1)S(1)} %collective-permute-done.2.rest_1_, ...), custom_call_target="tpu_custom_call" | custom-call | flops 201326592 | bytes 2097152 | tf_op jit(solution)/shard_map/pallas_call | solution.py:33
  19.3 0.2 shard_map.126.rest_0_
  19.5 0.0 collective-permute-done.7.rest_1_
  19.5 0.3 shard_map.128.early_ref
  19.8 1.4 %collective-permute-done.8.rest_0_ = bf16[192,128]{1,0:T(8,128)(2,1)S(1)} collective-permute-done((bf16[192,128]{1,0:T(8,128)(2,1)S(1)}, bf16[192,128]{1,0:T(8,128)(2,1)S(1)}, u32[]{:S(2)}, u32[]{:S(2)}) %collective-permute-start.8) | collective-permute-done | bytes 49184 | tf_op jit(solution)/shard_map/ppermute | solution.py:403
  21.2 0.0 collective-permute-done.9.rest_1_
  21.2 0.5 %shard_map.129 = (bf16[128,1024]{1,0:T(8,128)(2,1)S(1)}, bf16[153,128]{1,0:T(8,128)(2,1)S(1)}, bf16[153,128]{1,0:T(8,128)(2,1)S(1)}, bf16[153,128]{1,0:T(8,128)(2,1)S(1)}, bf16[153,128]{1,0:T(8,128)(2,1)S(1)}) custom-call(s32[1]{0:T(128)} %bitcast.me_ref.rest_0_, bf16[768,1024]{1,0:T(8,128)(2,1)S(1)} %copy-done, bf16[153,1024]{1,0:T(8,128)(2,1)S(1)} %bitcast.20, ...), custom_call_target="tpu_custom_call" | custom-call | flops 100663296 | bytes 2097152 | tf_op jit(solution)/shard_map/pallas_call | solution.py:33
  21.8 2.3 %collective-permute-start.10 = (bf16[153,128]{1,0:T(8,128)(2,1)S(1)}, bf16[153,128]{1,0:T(8,128)(2,1)S(1)}, u32[]{:S(2)}, u32[]{:S(2)}) collective-permute-start(bf16[153,128]{1,0:T(8,128)(2,1)S(1)} %get-tuple-element.69), channel_id=1, source_target_pairs={{0,24},{8,16},{16,8},{24,0},{1,25},{9,17},{17,9},{25,1},{2,26},{10... | collective-permute-start | bytes 117512 | tf_op jit(solution)/shard_map/ppermute | solution.py:403
  24.0 0.0 collective-permute-start.11
  24.0 2.2 %collective-permute-start.12 = (bf16[153,128]{1,0:T(8,128)(2,1)S(1)}, bf16[153,128]{1,0:T(8,128)(2,1)S(1)}, u32[]{:S(2)}, u32[]{:S(2)}) collective-permute-start(bf16[153,128]{1,0:T(8,128)(2,1)S(1)} %get-tuple-element.71), channel_id=1, source_target_pairs={{0,8},{8,0},{16,24},{24,16},{1,9},{9,1},{17,25},{25,17},{2,10},{10... | collective-permute-start | bytes 117512 | tf_op jit(solution)/shard_map/ppermute | solution.py:403
  26.2 0.9 %shard_map.132.hits_ref.after = bf16[128,512]{1,0:T(8,128)(2,1)S(1)} custom-call(bf16[153,128]{1,0:T(8,128)(2,1)S(1)} %get-tuple-element.68.rest_0_.after, s32[1]{0:T(128)} %bitcast.me_ref.rest_0_, s32[1]{0:T(128)} %bitcast.4.part_ref, s32[8,4,16]{2,1,0:T(4,128)} %bitcast.26), custom_call_target="tpu_custom_call" | custom-call | bytes 524288 | tf_op jit(solution)/shard_map/pallas_call | solution.py:33
  27.1 0.7 %collective-permute-done.10.rest_1_ = bf16[153,128]{1,0:T(8,128)(2,1)S(1)} collective-permute-done((bf16[153,128]{1,0:T(8,128)(2,1)S(1)}, bf16[153,128]{1,0:T(8,128)(2,1)S(1)}, u32[]{:S(2)}, u32[]{:S(2)}) %collective-permute-start.10) | collective-permute-done | bytes 39200 | tf_op jit(solution)/shard_map/ppermute | solution.py:403
  27.8 0.2 shard_map.133.early_ref
  28.0 1.0 %collective-permute-done.11.rest_2_.rest_0_ = bf16[153,128]{1,0:T(8,128)(2,1)S(1)} collective-permute-done((bf16[153,128]{1,0:T(8,128)(2,1)S(1)}, bf16[153,128]{1,0:T(8,128)(2,1)S(1)}, u32[]{:S(2)}, u32[]{:S(2)}) %collective-permute-start.11) | collective-permute-done | bytes 39200 | tf_op jit(solution)/shard_map/ppermute | solution.py:403
  29.0 0.0 collective-permute-done.12.rest_3_.rest_1_
  29.0 0.2 shard_map.134
  29.2 0.1 collective-permute-start.13
  29.3 1.2 %collective-permute-done.13.got_ref = bf16[4,16,256]{2,1,0:T(8,128)(2,1)S(1)} collective-permute-done((bf16[4,16,256]{2,1,0:T(8,128)(2,1)S(1)}, bf16[4,16,256]{2,1,0:T(8,128)(2,1)S(1)}, u32[]{:S(2)}, u32[]{:S(2)}) %collective-permute-start.13) | collective-permute-done | bytes 32800 | tf_op jit(solution)/shard_map/ppermute | solution.py:408
  30.5 2.4 %collective-permute-start.14 = (bf16[2,16,256]{2,1,0:T(8,128)(2,1)S(1)}, bf16[2,16,256]{2,1,0:T(8,128)(2,1)S(1)}, u32[]{:S(2)}, u32[]{:S(2)}) collective-permute-start(bf16[2,16,256]{2,1,0:T(8,128)(2,1)S(1)} %get-tuple-element.75), channel_id=1, source_target_pairs={{0,6},{1,7},{2,4},{3,5},{4,2},{5,3},{6,0},{7,1},{8,14},{9,15},{10,... | collective-permute-start | bytes 49160 | tf_op jit(solution)/shard_map/ppermute | solution.py:412
  33.0 0.5 %collective-permute-start.15 = (bf16[2,16,256]{2,1,0:T(8,128)(2,1)S(1)}, bf16[2,16,256]{2,1,0:T(8,128)(2,1)S(1)}, u32[]{:S(2)}, u32[]{:S(2)}) collective-permute-start(bf16[2,16,256]{2,1,0:T(8,128)(2,1)S(1)} %get-tuple-element.76), channel_id=1, source_target_pairs={{0,2},{1,3},{2,6},{3,7},{4,0},{5,1},{6,4},{7,5},{8,10},{9,11},{10,... | collective-permute-start | bytes 49160 | tf_op jit(solution)/shard_map/ppermute | solution.py:412
  33.5 1.5 %collective-permute-start.16 = (bf16[2,16,256]{2,1,0:T(8,128)(2,1)S(1)}, bf16[2,16,256]{2,1,0:T(8,128)(2,1)S(1)}, u32[]{:S(2)}, u32[]{:S(2)}) collective-permute-start(bf16[2,16,256]{2,1,0:T(8,128)(2,1)S(1)} %get-tuple-element.77), channel_id=1, source_target_pairs={{0,4},{1,5},{2,0},{3,1},{4,6},{5,7},{6,2},{7,3},{8,12},{9,13},{10,... | collective-permute-start | bytes 49160 | tf_op jit(solution)/shard_map/ppermute | solution.py:412
  35.0 0.7 %shard_map.130 = (f32[153,128]{1,0:T(8,128)S(1)}, bf16[128,1024]{1,0:T(8,128)(2,1)}) custom-call(bf16[128,1024]{1,0:T(8,128)(2,1)S(1)} %get-tuple-element.65.hidden_ref, bf16[153,1024]{1,0:T(8,128)(2,1)S(1)} %bitcast.19), custom_call_target="tpu_custom_call" | custom-call | flops 40108032 | bytes 1048576 | tf_op jit(solution)/shard_map/pallas_call | solution.py:33
  35.7 0.2 shard_map.131.near_ref
  35.9 0.0 collective-permute-done.14.rest_1_
  35.9 0.2 shard_map.136.rest_0_
  36.1 0.5 %collective-permute-done.15.rest_3_ = bf16[2,16,256]{2,1,0:T(8,128)(2,1)S(1)} collective-permute-done((bf16[2,16,256]{2,1,0:T(8,128)(2,1)S(1)}, bf16[2,16,256]{2,1,0:T(8,128)(2,1)S(1)}, u32[]{:S(2)}, u32[]{:S(2)}) %collective-permute-start.15) | collective-permute-done | bytes 16416 | tf_op jit(solution)/shard_map/ppermute | solution.py:412
  36.7 0.5 %collective-permute-done.16.rest_4_ = bf16[2,16,256]{2,1,0:T(8,128)(2,1)S(1)} collective-permute-done((bf16[2,16,256]{2,1,0:T(8,128)(2,1)S(1)}, bf16[2,16,256]{2,1,0:T(8,128)(2,1)S(1)}, u32[]{:S(2)}, u32[]{:S(2)}) %collective-permute-start.16) | collective-permute-done | bytes 16416 | tf_op jit(solution)/shard_map/ppermute | solution.py:412
  37.2 0.8 %shard_map.137 = f32[153,1,128]{2,1,0:T(1,128)} custom-call(s32[1]{0:T(128)} %bitcast.4.part_ref, s32[1]{0:T(128)} %bitcast.me_ref.rest_0_, f32[153,128]{1,0:T(8,128)S(1)} %shard_map.136.rest_0_, bf16[4,8,16,128]{3,2,1,0:T(8,128)(2,1)S(1)} %get-tuple-element.57.rest_2_.edges_ref.rest_1_, f32[4,208,128]{2,1,0:T(8,128)S(1)} %get-tuple-element.56.rest_1_.sums_ref.rest_2_, ...), custom_call_target="tpu_custom_call" | custom-call | flops 2506752 | bytes 524288 | tf_op jit(solution)/shard_map/pallas_call | solution.py:33
  (8 shorter events, 0.0 us)
Async XLA Ops:
  1.9 1.7 %collective-permute-start = (bf16[4,64,256]{2,1,0:T(8,128)(2,1)S(1)}, bf16[4,64,256]{2,1,0:T(8,128)(2,1)S(1)}, u32[]{:S(2)}, u32[]{:S(2)}) collective-permute-start(bf16[4,64,256]{2,1,0:T(8,128)(2,1)S(1)} %get-tuple-element.49), channel_id=1, source_target_pairs={{0,1},{1,0},{2,3},{3,2},{4,5},{5,4},{6,7},{7,6},{8,9},{9,8},{10,11... | collective-permute-start | bytes 393224 | tf_op jit(solution)/shard_map/ppermute | solution.py:408
  3.7 8.7 %collective-permute-start.4 = (bf16[2,64,256]{2,1,0:T(8,128)(2,1)S(1)}, bf16[2,64,256]{2,1,0:T(8,128)(2,1)S(1)}, u32[]{:S(2)}, u32[]{:S(2)}) collective-permute-start(bf16[2,64,256]{2,1,0:T(8,128)(2,1)S(1)} %get-tuple-element.59), channel_id=1, source_target_pairs={{0,6},{1,7},{2,4},{3,5},{4,2},{5,3},{6,0},{7,1},{8,14},{9,15},{10,... | collective-permute-start | bytes 196616 | tf_op jit(solution)/shard_map/ppermute | solution.py:412
  7.4 5.2 %collective-permute-start.5 = (bf16[2,64,256]{2,1,0:T(8,128)(2,1)S(1)}, bf16[2,64,256]{2,1,0:T(8,128)(2,1)S(1)}, u32[]{:S(2)}, u32[]{:S(2)}) collective-permute-start(bf16[2,64,256]{2,1,0:T(8,128)(2,1)S(1)} %get-tuple-element.60), channel_id=1, source_target_pairs={{0,4},{1,5},{2,6},{3,7},{4,0},{5,1},{6,2},{7,3},{8,12},{9,13},{10,... | collective-permute-start | bytes 196616 | tf_op jit(solution)/shard_map/ppermute | solution.py:412
  7.9 4.7 %collective-permute-start.6 = (bf16[2,64,256]{2,1,0:T(8,128)(2,1)S(1)}, bf16[2,64,256]{2,1,0:T(8,128)(2,1)S(1)}, u32[]{:S(2)}, u32[]{:S(2)}) collective-permute-start(bf16[2,64,256]{2,1,0:T(8,128)(2,1)S(1)} %get-tuple-element.61), channel_id=1, source_target_pairs={{0,2},{1,3},{2,0},{3,1},{4,6},{5,7},{6,4},{7,5},{8,10},{9,11},{10,... | collective-permute-start | bytes 196616 | tf_op jit(solution)/shard_map/ppermute | solution.py:412
  8.0 8.1 %collective-permute-start.1 = (bf16[192,128]{1,0:T(8,128)(2,1)S(1)}, bf16[192,128]{1,0:T(8,128)(2,1)S(1)}, u32[]{:S(2)}, u32[]{:S(2)}) collective-permute-start(bf16[192,128]{1,0:T(8,128)(2,1)S(1)} %get-tuple-element.53), channel_id=1, source_target_pairs={{0,16},{8,24},{16,0},{24,8},{1,17},{9,25},{17,1},{25,9},{2,18},{10... | collective-permute-start | bytes 147464 | tf_op jit(solution)/shard_map/ppermute | solution.py:403
  11.0 6.5 %collective-permute-start.2 = (bf16[192,128]{1,0:T(8,128)(2,1)S(1)}, bf16[192,128]{1,0:T(8,128)(2,1)S(1)}, u32[]{:S(2)}, u32[]{:S(2)}) collective-permute-start(bf16[192,128]{1,0:T(8,128)(2,1)S(1)} %get-tuple-element.54), channel_id=1, source_target_pairs={{0,24},{8,16},{16,8},{24,0},{1,25},{9,17},{17,9},{25,1},{2,26},{10... | collective-permute-start | bytes 147464 | tf_op jit(solution)/shard_map/ppermute | solution.py:403
  12.3 5.1 %collective-permute-start.3 = (bf16[192,128]{1,0:T(8,128)(2,1)S(1)}, bf16[192,128]{1,0:T(8,128)(2,1)S(1)}, u32[]{:S(2)}, u32[]{:S(2)}) collective-permute-start(bf16[192,128]{1,0:T(8,128)(2,1)S(1)} %get-tuple-element.55), channel_id=1, source_target_pairs={{0,8},{8,0},{16,24},{24,16},{1,9},{9,1},{17,25},{25,17},{2,10},{10... | collective-permute-start | bytes 147464 | tf_op jit(solution)/shard_map/ppermute | solution.py:403
  12.8 6.7 %collective-permute-start.7 = (bf16[192,128]{1,0:T(8,128)(2,1)S(1)}, bf16[192,128]{1,0:T(8,128)(2,1)S(1)}, u32[]{:S(2)}, u32[]{:S(2)}) collective-permute-start(bf16[192,128]{1,0:T(8,128)(2,1)S(1)} %get-tuple-element.62), channel_id=1, source_target_pairs={{0,24},{8,16},{16,8},{24,0},{1,25},{9,17},{17,9},{25,1},{2,26},{10... | collective-permute-start | bytes 147464 | tf_op jit(solution)/shard_map/ppermute | solution.py:403
  16.0 5.2 %collective-permute-start.8 = (bf16[192,128]{1,0:T(8,128)(2,1)S(1)}, bf16[192,128]{1,0:T(8,128)(2,1)S(1)}, u32[]{:S(2)}, u32[]{:S(2)}) collective-permute-start(bf16[192,128]{1,0:T(8,128)(2,1)S(1)} %get-tuple-element.63), channel_id=1, source_target_pairs={{0,16},{8,24},{16,0},{24,8},{1,17},{9,25},{17,1},{25,9},{2,18},{10... | collective-permute-start | bytes 147464 | tf_op jit(solution)/shard_map/ppermute | solution.py:403
  16.1 3.4 %copy-start = (bf16[768,1024]{1,0:T(8,128)(2,1)S(1)}, bf16[768,1024]{1,0:T(8,128)(2,1)}, u32[]{:S(2)}) copy-start(bf16[768,1024]{1,0:T(8,128)(2,1)} %weight_ref.3) | copy-start | bytes 4718596
  16.1 5.1 %collective-permute-start.9 = (bf16[192,128]{1,0:T(8,128)(2,1)S(1)}, bf16[192,128]{1,0:T(8,128)(2,1)S(1)}, u32[]{:S(2)}, u32[]{:S(2)}) collective-permute-start(bf16[192,128]{1,0:T(8,128)(2,1)S(1)} %get-tuple-element.64), channel_id=1, source_target_pairs={{0,8},{8,0},{16,24},{24,16},{1,9},{9,1},{17,25},{25,17},{2,10},{10... | collective-permute-start | bytes 147464 | tf_op jit(solution)/shard_map/ppermute | solution.py:403
  19.5 1.7 %copy-start.2 = (bf16[1024,153]{0,1:T(8,128)(2,1)S(1)}, bf16[1024,153]{0,1:T(8,128)(2,1)}, u32[]{:S(2)}) copy-start(bf16[1024,153]{0,1:T(8,128)(2,1)} %param.21) | copy-start | bytes 940036
  21.2 13.8 %copy-start.1 = (bf16[1024,153]{0,1:T(8,128)(2,1)S(1)}, bf16[1024,153]{0,1:T(8,128)(2,1)}, u32[]{:S(2)}) copy-start(bf16[1024,153]{0,1:T(8,128)(2,1)} %param.20) | copy-start | bytes 940036
  21.8 6.0 %collective-permute-start.10 = (bf16[153,128]{1,0:T(8,128)(2,1)S(1)}, bf16[153,128]{1,0:T(8,128)(2,1)S(1)}, u32[]{:S(2)}, u32[]{:S(2)}) collective-permute-start(bf16[153,128]{1,0:T(8,128)(2,1)S(1)} %get-tuple-element.69), channel_id=1, source_target_pairs={{0,24},{8,16},{16,8},{24,0},{1,25},{9,17},{17,9},{25,1},{2,26},{10... | collective-permute-start | bytes 117512 | tf_op jit(solution)/shard_map/ppermute | solution.py:403
  24.0 5.0 %collective-permute-start.11 = (bf16[153,128]{1,0:T(8,128)(2,1)S(1)}, bf16[153,128]{1,0:T(8,128)(2,1)S(1)}, u32[]{:S(2)}, u32[]{:S(2)}) collective-permute-start(bf16[153,128]{1,0:T(8,128)(2,1)S(1)} %get-tuple-element.70), channel_id=1, source_target_pairs={{0,16},{8,24},{16,0},{24,8},{1,17},{9,25},{17,1},{25,9},{2,18},{10... | collective-permute-start | bytes 117512 | tf_op jit(solution)/shard_map/ppermute | solution.py:403
  24.0 5.0 %collective-permute-start.12 = (bf16[153,128]{1,0:T(8,128)(2,1)S(1)}, bf16[153,128]{1,0:T(8,128)(2,1)S(1)}, u32[]{:S(2)}, u32[]{:S(2)}) collective-permute-start(bf16[153,128]{1,0:T(8,128)(2,1)S(1)} %get-tuple-element.71), channel_id=1, source_target_pairs={{0,8},{8,0},{16,24},{24,16},{1,9},{9,1},{17,25},{25,17},{2,10},{10... | collective-permute-start | bytes 117512 | tf_op jit(solution)/shard_map/ppermute | solution.py:403
  29.2 1.3 %collective-permute-start.13 = (bf16[4,16,256]{2,1,0:T(8,128)(2,1)S(1)}, bf16[4,16,256]{2,1,0:T(8,128)(2,1)S(1)}, u32[]{:S(2)}, u32[]{:S(2)}) collective-permute-start(bf16[4,16,256]{2,1,0:T(8,128)(2,1)S(1)} %get-tuple-element.73), channel_id=1, source_target_pairs={{0,1},{1,0},{2,3},{3,2},{4,5},{5,4},{6,7},{7,6},{8,9},{9,8},{10,11... | collective-permute-start | bytes 98312 | tf_op jit(solution)/shard_map/ppermute | solution.py:408
  30.5 5.4 %collective-permute-start.14 = (bf16[2,16,256]{2,1,0:T(8,128)(2,1)S(1)}, bf16[2,16,256]{2,1,0:T(8,128)(2,1)S(1)}, u32[]{:S(2)}, u32[]{:S(2)}) collective-permute-start(bf16[2,16,256]{2,1,0:T(8,128)(2,1)S(1)} %get-tuple-element.75), channel_id=1, source_target_pairs={{0,6},{1,7},{2,4},{3,5},{4,2},{5,3},{6,0},{7,1},{8,14},{9,15},{10,... | collective-permute-start | bytes 49160 | tf_op jit(solution)/shard_map/ppermute | solution.py:412
  33.0 3.7 %collective-permute-start.15 = (bf16[2,16,256]{2,1,0:T(8,128)(2,1)S(1)}, bf16[2,16,256]{2,1,0:T(8,128)(2,1)S(1)}, u32[]{:S(2)}, u32[]{:S(2)}) collective-permute-start(bf16[2,16,256]{2,1,0:T(8,128)(2,1)S(1)} %get-tuple-element.76), channel_id=1, source_target_pairs={{0,2},{1,3},{2,6},{3,7},{4,0},{5,1},{6,4},{7,5},{8,10},{9,11},{10,... | collective-permute-start | bytes 49160 | tf_op jit(solution)/shard_map/ppermute | solution.py:412
  33.5 3.7 %collective-permute-start.16 = (bf16[2,16,256]{2,1,0:T(8,128)(2,1)S(1)}, bf16[2,16,256]{2,1,0:T(8,128)(2,1)S(1)}, u32[]{:S(2)}, u32[]{:S(2)}) collective-permute-start(bf16[2,16,256]{2,1,0:T(8,128)(2,1)S(1)} %get-tuple-element.77), channel_id=1, source_target_pairs={{0,4},{1,5},{2,0},{3,1},{4,6},{5,7},{6,2},{7,3},{8,12},{9,13},{10,... | collective-permute-start | bytes 49160 | tf_op jit(solution)/shard_map/ppermute | solution.py:412
